TPU v7x, 32 devices: a whole 2x2x4 slice. The times are simulated.
32 devices in a mesh: strip: 8 (over z, y), chan: 4 (over x, core).
Axes of the slice: x: 2, y: 2, z: 4, core: 2. Of those that a mesh axis runs over, the one named last changes fastest.
Arguments:
- grid: bfloat16 [2, 64, 1024, 1024], P(None, 'chan', 'strip'), may hold values from -6 to 6
- model_image: float32 [64, 1024, 1024], P('chan', 'strip'), may hold values from -160 to 160
- step_size: float32 [64], P('chan'), may hold values from 0.5 to 1.5
- highpass: float32 [3, 4], replicated, may hold values from -1.4 to 1.4
- shrinkage: float32 [8], P('strip'), may hold values from 0.1 to 0.5
Outputs:
- updated: float32 [64, 1024, 1024], P('chan', 'strip')
All inputs are finite; a program needn't handle non-finite values.
Results may differ from a plain program's by a relative error of at most 0.0019.
Values may be sent and summed in bfloat16 or wider, within the bound.
No kernel may reach another device: no remote copies, remote signals or barrier semaphores. Data moves between devices by JAX's collectives and lax.ppermute only.
A program may use at most 128 MiB of HBM per device.

v0:
```python
import jax
import jax.numpy as jnp
from jax import lax
from jax.sharding import PartitionSpec as P

NS_ITERS = 5


def extended(cells, sides, width):
    for axis, dim in sides:
        count = lax.axis_size(axis)
        ends = count - 1
        head = lax.slice_in_dim(cells, 0, width, axis=dim)
        tail = lax.slice_in_dim(cells, cells.shape[dim] - width, cells.shape[dim], axis=dim)
        cells = jnp.concatenate(
            [
                lax.ppermute(tail, axis, [(i, (i + 1) % count) for i in range(ends)]),
                cells,
                lax.ppermute(head, axis, [((i + 1) % count, i) for i in range(ends)]),
            ],
            axis=dim,
        )
    return cells


def make_tables(side_len):
    indices = jnp.arange(side_len, dtype=jnp.int32)
    products = indices[:, None] * indices[None, :] % side_len
    phases = products.astype(jnp.float32) * (2.0 * 3.141592653589793 / side_len)
    unit_scale = float(side_len) ** (-0.5)
    cosine = (jnp.cos(phases) * unit_scale).astype(jnp.bfloat16)
    sine_table = (jnp.sin(phases) * unit_scale).astype(jnp.bfloat16)
    return (cosine, sine_table)


def filter_rows(source, filter_taps, first_row, row_total, dilation, direction):
    half_taps = filter_taps.shape[0] // 2
    running = jnp.zeros((source.shape[0], row_total, source.shape[2]), jnp.float32)
    for tap_index in range(filter_taps.shape[0]):
        offset = direction * (tap_index - half_taps) * dilation
        running = (
            running
            + filter_taps[tap_index]
            * source[:, first_row + offset : first_row + offset + row_total, :]
        )
    return running


def newton_schulz(gram_sum):
    frob_norm = jnp.sqrt(jnp.sum(gram_sum * gram_sum))
    identity = jnp.eye(gram_sum.shape[0], dtype=jnp.float32)
    current = gram_sum / frob_norm
    inverse = identity
    for iteration in range(NS_ITERS):
        middle = 0.5 * (3.0 * identity - jnp.dot(inverse, current, precision=lax.Precision.HIGHEST))
        current = jnp.dot(current, middle, precision=lax.Precision.HIGHEST)
        inverse = jnp.dot(middle, inverse, precision=lax.Precision.HIGHEST)
    return (inverse, frob_norm)


def local(grid, model_image, step_size, highpass, shrinkage):
    local_chans, local_rows, side_len = model_image.shape
    cosine, sine_table = make_tables(side_len)
    real_part = grid[0]
    imag_part = grid[1]
    half_real = jnp.einsum(
        "cuv,vm->cum", real_part, cosine, preferred_element_type=jnp.float32
    ) - jnp.einsum("cuv,vm->cum", imag_part, sine_table, preferred_element_type=jnp.float32)
    half_imag = jnp.einsum(
        "cuv,vm->cum", real_part, sine_table, preferred_element_type=jnp.float32
    ) + jnp.einsum("cuv,vm->cum", imag_part, cosine, preferred_element_type=jnp.float32)
    half_grid = jnp.stack((half_real.astype(jnp.bfloat16), half_imag.astype(jnp.bfloat16)))
    grid_block = lax.all_to_all(half_grid, "strip", split_axis=3, concat_axis=2, tiled=True)
    dirty_image = jnp.einsum(
        "cum,ul->cml", grid_block[0], cosine, preferred_element_type=jnp.float32
    ) - jnp.einsum("cum,ul->cml", grid_block[1], sine_table, preferred_element_type=jnp.float32)
    half_taps = highpass.shape[1] // 2
    levels = highpass.shape[0]
    gradient = jnp.zeros(model_image.shape, jnp.float32)
    for level_idx in range(levels):
        dilation = 2**level_idx
        reach_rows = half_taps * dilation
        padded = extended(model_image, (("strip", 1),), reach_rows)
        detail = filter_rows(padded, highpass[level_idx], reach_rows, local_rows, dilation, 1)
        widened = extended(detail, (("strip", 1),), reach_rows)
        gradient = gradient + filter_rows(
            widened, highpass[level_idx], reach_rows, local_rows, dilation, -1
        )
    moved = model_image + step_size[:, None, None] * (dirty_image - gradient)
    facet = lax.all_to_all(moved, "chan", split_axis=1, concat_axis=0, tiled=True)
    pixels = facet.reshape(facet.shape[0], -1)
    gram_part = jnp.dot(pixels, pixels.T, precision=lax.Precision.HIGHEST)
    gram_sum = lax.psum(gram_part, "chan")
    inverse, frob_norm = newton_schulz(gram_sum)
    polar = jnp.sqrt(local_rows * side_len / frob_norm) * jnp.dot(
        inverse.T, pixels, precision=lax.Precision.HIGHEST
    )
    result = (pixels - shrinkage[0] * polar).reshape(facet.shape)
    updated = lax.all_to_all(result, "chan", split_axis=0, concat_axis=1, tiled=True)
    return updated


def solution(mesh):
    return jax.shard_map(
        local,
        mesh=mesh,
        in_specs=(
            P(None, "chan", "strip", None),
            P("chan", "strip", None),
            P("chan"),
            P(),
            P("strip"),
        ),
        out_specs=P("chan", "strip", None),
        check_vma=False,
    )
```

profile of v0, /device:TPU:12, one launch (start us, length us, event | category | flops | bytes accessed | tf_op | source)
XLA Modules:
  0.0 760.2 jit_solution(16960938376810770823)
XLA Ops:
  0.0 24.0 %fusion.53 = f32[1024,16,128]{2,0,1:T(8,128)} fusion(bf16[2,16,128,1024]{3,2,1,0:T(8,128)(2,1)} %param.5), kind=kOutput, calls=%fused_computation.84 | convolution fusion | flops 4311744512 | bytes 12582912 | tf_op jit(solution)/shard_map/cuv,vm->cum/dot_general | solution.py:68
  24.0 19.4 %fusion.51 = f32[1024,16,128]{2,0,1:T(8,128)S(1)} fusion(bf16[2,16,128,1024]{3,2,1,0:T(8,128)(2,1)S(1)} %copy-done.4), kind=kOutput, calls=%fused_computation.82 | convolution fusion | flops 4311744512 | bytes 12582912 | tf_op jit(solution)/shard_map/cuv,vm->cum/dot_general | solution.py:71
  43.5 21.7 %fusion.49 = bf16[1,16,128,1024]{2,3,1,0:T(8,128)(2,1)S(1)} fusion(f32[1024,16,128]{2,0,1:T(8,128)} %fusion.53, bf16[2,16,128,1024]{3,2,1,0:T(8,128)(2,1)S(1)} %copy-done.4), kind=kOutput, calls=%fused_computation.80 | convolution fusion | flops 4315938816 | bytes 16777216 | tf_op jit(solution)/shard_map/cuv,vm->cum/dot_general | solution.py:66
  65.2 21.5 %fusion.50 = bf16[1,16,128,1024]{2,3,1,0:T(8,128)(2,1)} fusion(f32[1024,16,128]{2,0,1:T(8,128)S(1)} %fusion.51, bf16[2,16,128,1024]{3,2,1,0:T(8,128)(2,1)S(1)} %copy-done.4), kind=kOutput, calls=%fused_computation.81 | convolution fusion | flops 4315938816 | bytes 16777216 | tf_op jit(solution)/shard_map/cuv,vm->cum/dot_general | solution.py:69
  86.7 6.4 pad_maximum_fusion.11
  93.1 12.0 %copy.18 = bf16[2,16,128,1024]{2,1,0,3:T(8,128)(2,1)} copy(bf16[2,16,128,1024]{2,3,1,0:T(8,128)(2,1)} %pad_maximum_fusion.11) | data formatting | bytes 16777216 | tf_op jit(solution)/shard_map/stack | solution.py:72
  105.1 6.4 all-to-all-start
  111.5 1.3 fusion.122
  112.8 3.4 collective-permute-start.8
  116.1 1.3 fusion.121
  117.5 3.4 collective-permute-start.4
  120.8 2.5 collective-permute-start.5
  123.3 3.4 collective-permute-start.9
  126.7 1.3 fusion.120
  128.0 3.4 collective-permute-start
  132.1 170.4 %collective-permute-done.8 = f32[16,8,1024]{2,1,0:T(8,128)S(1)} collective-permute-done((f32[16,8,1024]{2,1,0:T(8,128)S(1)}, f32[16,8,1024]{2,1,0:T(8,128)S(1)}, u32[]{:S(2)}, u32[]{:S(2)}) %collective-permute-start.8) | collective-permute-done | bytes 524320 | tf_op jit(solution)/shard_map/ppermute | solution.py:17
  302.5 1.9 collective-permute-start.1
  304.4 0.8 constant_dynamic-update-slice_fusion.1
  305.2 2.9 collective-permute-done.4
  308.1 24.0 %fusion.21 = (f32[16,128,1024]{2,1,0:T(8,128)}, f32[16,136,1024]{2,1,0:T(8,128)}) fusion(f32[16,4,1024]{2,1,0:T(4,128)S(1)} %collective-permute-done.4, f32[16,128,1024]{2,1,0:T(8,128)} %param.6, f32[16,4,1024]{2,1,0:T(4,128)S(1)} %collective-permute-done.5, f32[]{:T(128)} %bitcast.21, f32[]{:T(128)} %bitcast.20, f32[]{:T(128)} %bitcast.19, f32[]{:T(128)} %bitcast.18, ...), kind=kLoop, calls=%fused_computation.32 | loop fusion | flops 20971520 | bytes 25692160 | tf_op jit(solution)/shard_map/add | solution.py:42
  332.1 29.2 %fusion.31 = (f32[16,128,1024]{2,1,0:T(8,128)S(1)}, f32[16,128,1024]{2,1,0:T(8,128)S(1)}) fusion(f32[16,2,1024]{2,1,0:T(2,128)S(1)} %collective-permute-done, f32[16,128,1024]{2,1,0:T(8,128)} %param.6, f32[16,2,1024]{2,1,0:T(2,128)S(1)} %collective-permute-done.1, f32[]{:T(128)} %bitcast.17, f32[]{:T(128)} %bitcast.16, f32[]{:T(128)} %bitcast.15, ...), kind=kLoop, calls=%fused_computation.42 | loop fusion | flops 37748736 | bytes 42729504 | tf_op jit(solution)/shard_map/add | solution.py:42
  361.3 3.3 copy-done.1
  364.6 1.9 collective-permute-start.10
  366.6 5.4 collective-permute-start.11
  372.0 0.8 fusion.117
  372.8 1.9 collective-permute-start.2
  374.7 4.8 collective-permute-start.3
  379.5 1.3 fusion.118
  380.8 1.9 collective-permute-start.6
  382.8 12.0 %copy.34 = bf16[2,16,128,8,128]{2,3,4,1,0:T(8,128)(2,1)} copy(bf16[2,16,128,8,128]{2,1,0,4,3:T(8,128)(2,1)} %bitcast.10) | data formatting | bytes 16777216 | tf_op jit(solution)/shard_map/all_to_all | solution.py:73
  394.8 6.0 fusion.116
  400.8 7.3 squeeze.71
  408.1 4.8 collective-permute-start.7
  412.9 22.7 %fusion.75 = f32[16,128,1024]{2,1,0:T(8,128)} fusion(bf16[16,1024,128]{1,2,0:T(8,128)(2,1)} %squeeze.71), kind=kOutput, calls=%fused_computation.101 | convolution fusion | flops 4311744512 | bytes 12582912 | tf_op jit(solution)/shard_map/cum,ul->cml/dot_general | solution.py:74
  435.6 7.3 squeeze.72
  443.0 55.1 %fusion.10 = f32[16,128,1024]{2,1,0:T(8,128)S(1)} fusion(f32[16,128,1024]{2,1,0:T(8,128)} %param.6, f32[16,128,1024]{2,1,0:T(8,128)} %copy-done.1, f32[16,8,1024]{2,1,0:T(8,128)} %collective-permute-done.10, f32[16,128,1024]{2,1,0:T(8,128)} %get-tuple-element.17, f32[16,4,1024]{2,1,0:T(4,128)S(1)} %collective-permute-done.6, ...), kind=kOutput, calls=%fused_computation.21 | convolution fusion | flops 4387241984 | bytes 56361072 | tf_op jit(solution)/shard_map/cum,ul->cml/dot_general | solution.py:76
  498.1 8.3 %copy.20 = f32[16,128,1024]{2,0,1:T(8,128)} copy(f32[16,128,1024]{2,1,0:T(8,128)S(1)} %fusion.10) | data formatting | bytes 16777216 | tf_op jit(solution)/shard_map/add | solution.py:89
  506.3 5.8 all-to-all-start.1
  512.8 92.4 %all-to-all-done.1 = f32[16,128,1024]{2,0,1:T(8,128)} async-done(((f32[16,128,1024]{2,0,1:T(8,128)}), f32[16,128,1024]{2,0,1:T(8,128)}, u32[]{:S(2)}, u32[]{:S(2)}) %all-to-all-start.1) | async-done | bytes 8388640 | tf_op jit(solution)/shard_map/all_to_all | solution.py:90
  605.2 8.2 %copy.21 = f32[16,4,32,1024]{3,2,0,1:T(8,128)S(1)} copy(f32[16,4,32,1024]{3,0,2,1:T(8,128)} %bitcast.26) | data formatting | bytes 16777216 | tf_op jit(solution)/shard_map/all_to_all | solution.py:90
  613.4 5.0 copy.31
  618.5 3.4 copy-done
  621.8 6.9 fusion.124
  628.7 10.3 %psum.7 = f32[64,64]{1,0:T(8,128)S(1)} all-reduce(f32[64,64]{1,0:T(8,128)S(1)} %fusion.124), channel_id=1, replica_groups=mesh['strip'=8,'chan'=4] {'chan'}, use_global_device_ids=true, to_apply=%region_0.1 | all-reduce | flops 4096 | bytes 32768 | tf_op jit(solution)/shard_map/psum | solution.py:93
  642.7 12.0 %fusion.1 = f32[64,32768]{1,0:T(8,128)S(1)} fusion(f32[64,32768]{1,0:T(8,128)} %bitcast.107, f32[64,64]{1,0:T(8,128)S(1)} %fusion.131, f32[]{:T(128)S(6)} %sqrt.7, f32[]{:T(128)} %bitcast.105), kind=kOutput, calls=%fused_computation.2 | convolution fusion | flops 1616904192 | bytes 16793608 | tf_op jit(solution)/shard_map/dot_general | solution.py:95
  654.7 5.0 copy.32
  659.7 95.9 %all_to_all.48 = f32[64,32,1024]{2,1,0:T(8,128)S(1)} all-to-all(f32[64,32,1024]{2,1,0:T(8,128)S(1)} %bitcast.111), channel_id=1, replica_groups=mesh['strip'=8,'chan'=4] {'chan'}, dimensions={0} | all-to-all | bytes 16777216 | tf_op jit(solution)/shard_map/all_to_all | solution.py:99
  755.6 4.2 copy.22
  (38 shorter events, 3.7 us)
Async XLA Ops:
  0.0 24.0 %copy-start.4 = (bf16[2,16,128,1024]{3,2,1,0:T(8,128)(2,1)S(1)}, bf16[2,16,128,1024]{3,2,1,0:T(8,128)(2,1)}, u32[]{:S(2)}) copy-start(bf16[2,16,128,1024]{3,2,1,0:T(8,128)(2,1)} %param.5) | copy-start | bytes 25165828
  105.1 26.3 %copy-start.3 = (f32[3,4]{1,0:T(4,128)S(1)}, f32[3,4]{1,0:T(4,128)}, u32[]{:S(2)}) copy-start(f32[3,4]{1,0:T(4,128)} %param.8) | copy-start | bytes 148
  105.1 277.7 %all-to-all-start = ((bf16[2,16,128,1024]{2,1,0,3:T(8,128)(2,1)}), bf16[2,16,128,1024]{2,1,0,3:T(8,128)(2,1)}, u32[]{:S(2)}, u32[]{:S(2)}) async-start(bf16[2,16,128,1024]{2,1,0,3:T(8,128)(2,1)} %copy.18), calls=%async_computation | async-start | bytes 16777216 | tf_op jit(solution)/shard_map/all_to_all | solution.py:73
  112.8 189.7 %collective-permute-start.8 = (f32[16,8,1024]{2,1,0:T(8,128)S(1)}, f32[16,8,1024]{2,1,0:T(8,128)S(1)}, u32[]{:S(2)}, u32[]{:S(2)}) collective-permute-start(f32[16,8,1024]{2,1,0:T(8,128)S(1)} %get-tuple-element.21), channel_id=1, source_target_pairs={{0,4},{4,8},{8,12},{12,16},{16,20},{20,24},{24,28},{1,5},{5,9},{9,... | collective-permute-start | bytes 1572872 | tf_op jit(solution)/shard_map/ppermute | solution.py:17
  117.5 190.6 %collective-permute-start.4 = (f32[16,4,1024]{2,1,0:T(4,128)S(1)}, f32[16,4,1024]{2,1,0:T(4,128)S(1)}, u32[]{:S(2)}, u32[]{:S(2)}) collective-permute-start(f32[16,4,1024]{2,1,0:T(4,128)S(1)} %get-tuple-element.20), channel_id=1, source_target_pairs={{0,4},{4,8},{8,12},{12,16},{16,20},{20,24},{24,28},{1,5},{5,9},{9,... | collective-permute-start | bytes 786440 | tf_op jit(solution)/shard_map/ppermute | solution.py:17
  120.8 187.2 %collective-permute-start.5 = (f32[16,4,1024]{2,1,0:T(4,128)S(1)}, f32[16,4,1024]{2,1,0:T(4,128)S(1)}, u32[]{:S(2)}, u32[]{:S(2)}) collective-permute-start(f32[16,4,1024]{2,1,0:T(4,128)S(1)} %get-tuple-element.19), channel_id=1, source_target_pairs={{4,0},{8,4},{12,8},{16,12},{20,16},{24,20},{28,24},{5,1},{9,5},{13... | collective-permute-start | bytes 786440 | tf_op jit(solution)/shard_map/ppermute | solution.py:19
  123.3 208.7 %collective-permute-start.9 = (f32[16,8,1024]{2,1,0:T(8,128)S(1)}, f32[16,8,1024]{2,1,0:T(8,128)S(1)}, u32[]{:S(2)}, u32[]{:S(2)}) collective-permute-start(f32[16,8,1024]{2,1,0:T(8,128)S(1)} %get-tuple-element.22), channel_id=1, source_target_pairs={{4,0},{8,4},{12,8},{16,12},{20,16},{24,20},{28,24},{5,1},{9,5},{13... | collective-permute-start | bytes 1572872 | tf_op jit(solution)/shard_map/ppermute | solution.py:19
  128.0 204.1 %collective-permute-start = (f32[16,2,1024]{2,1,0:T(2,128)S(1)}, f32[16,2,1024]{2,1,0:T(2,128)S(1)}, u32[]{:S(2)}, u32[]{:S(2)}) collective-permute-start(f32[16,2,1024]{2,1,0:T(2,128)S(1)} %get-tuple-element.16), channel_id=1, source_target_pairs={{0,4},{4,8},{8,12},{12,16},{16,20},{20,24},{24,28},{1,5},{5,9},{9,... | collective-permute-start | bytes 393224 | tf_op jit(solution)/shard_map/ppermute | solution.py:17
  302.5 29.6 %collective-permute-start.1 = (f32[16,2,1024]{2,1,0:T(2,128)S(1)}, f32[16,2,1024]{2,1,0:T(2,128)S(1)}, u32[]{:S(2)}, u32[]{:S(2)}) collective-permute-start(f32[16,2,1024]{2,1,0:T(2,128)S(1)} %get-tuple-element.15), channel_id=1, source_target_pairs={{4,0},{8,4},{12,8},{16,12},{20,16},{24,20},{28,24},{5,1},{9,5},{13... | collective-permute-start | bytes 393224 | tf_op jit(solution)/shard_map/ppermute | solution.py:19
  361.2 3.3 copy-start.1
  361.3 10.7 %copy-start.2 = (f32[16,128,1024]{2,1,0:T(8,128)}, f32[16,128,1024]{2,1,0:T(8,128)S(1)}, u32[]{:S(2)}) copy-start(f32[16,128,1024]{2,1,0:T(8,128)S(1)} %get-tuple-element.13) | copy-start | bytes 25165828
  364.6 78.3 %collective-permute-start.10 = (f32[16,8,1024]{2,1,0:T(8,128)S(1)}, f32[16,8,1024]{2,1,0:T(8,128)}, u32[]{:S(2)}, u32[]{:S(2)}) collective-permute-start(f32[16,8,1024]{2,1,0:T(8,128)S(1)} %get-tuple-element.12), channel_id=1, source_target_pairs={{4,0},{8,4},{12,8},{16,12},{20,16},{24,20},{28,24},{5,1},{9,5},{13... | collective-permute-start | bytes 1572872 | tf_op jit(solution)/shard_map/ppermute | solution.py:19
  366.6 76.4 %collective-permute-start.11 = (f32[16,8,1024]{2,1,0:T(8,128)S(1)}, f32[16,8,1024]{2,1,0:T(8,128)}, u32[]{:S(2)}, u32[]{:S(2)}) collective-permute-start(f32[16,8,1024]{2,1,0:T(8,128)S(1)} %get-tuple-element.11), channel_id=1, source_target_pairs={{0,4},{4,8},{8,12},{12,16},{16,20},{20,24},{24,28},{1,5},{5,9},{9,... | collective-permute-start | bytes 1572872 | tf_op jit(solution)/shard_map/ppermute | solution.py:17
  372.8 35.3 %collective-permute-start.2 = (f32[16,2,1024]{2,1,0:T(2,128)}, f32[16,2,1024]{2,1,0:T(2,128)S(1)}, u32[]{:S(2)}, u32[]{:S(2)}) collective-permute-start(f32[16,2,1024]{2,1,0:T(2,128)} %get-tuple-element.8), channel_id=1, source_target_pairs={{4,0},{8,4},{12,8},{16,12},{20,16},{24,20},{28,24},{5,1},{9,5},{13... | collective-permute-start | bytes 393224 | tf_op jit(solution)/shard_map/ppermute | solution.py:19
  374.7 68.3 %collective-permute-start.3 = (f32[16,2,1024]{2,1,0:T(2,128)}, f32[16,2,1024]{2,1,0:T(2,128)S(1)}, u32[]{:S(2)}, u32[]{:S(2)}) collective-permute-start(f32[16,2,1024]{2,1,0:T(2,128)} %get-tuple-element.7), channel_id=1, source_target_pairs={{0,4},{4,8},{8,12},{12,16},{16,20},{20,24},{24,28},{1,5},{5,9},{9,... | collective-permute-start | bytes 393224 | tf_op jit(solution)/shard_map/ppermute | solution.py:17
  380.8 62.1 %collective-permute-start.6 = (f32[16,4,1024]{2,1,0:T(4,128)S(1)}, f32[16,4,1024]{2,1,0:T(4,128)S(1)}, u32[]{:S(2)}, u32[]{:S(2)}) collective-permute-start(f32[16,4,1024]{2,1,0:T(4,128)S(1)} %get-tuple-element.10), channel_id=1, source_target_pairs={{4,0},{8,4},{12,8},{16,12},{20,16},{24,20},{28,24},{5,1},{9,5},{13... | collective-permute-start | bytes 786440 | tf_op jit(solution)/shard_map/ppermute | solution.py:19
  408.1 34.9 %collective-permute-start.7 = (f32[16,4,1024]{2,1,0:T(4,128)S(1)}, f32[16,4,1024]{2,1,0:T(4,128)S(1)}, u32[]{:S(2)}, u32[]{:S(2)}) collective-permute-start(f32[16,4,1024]{2,1,0:T(4,128)S(1)} %get-tuple-element.9), channel_id=1, source_target_pairs={{0,4},{4,8},{8,12},{12,16},{16,20},{20,24},{24,28},{1,5},{5,9},{9,... | collective-permute-start | bytes 786440 | tf_op jit(solution)/shard_map/ppermute | solution.py:17
  435.6 7.4 copy-start.5
  506.3 98.8 %all-to-all-start.1 = ((f32[16,128,1024]{2,0,1:T(8,128)}), f32[16,128,1024]{2,0,1:T(8,128)}, u32[]{:S(2)}, u32[]{:S(2)}) async-start(f32[16,128,1024]{2,0,1:T(8,128)} %copy.20), calls=%async_computation.1 | async-start | bytes 16777216 | tf_op jit(solution)/shard_map/all_to_all | solution.py:90
  618.4 3.4 copy-start
where the time goes:
time: 769 us; the launch traced here: 760 us
  waiting for transfers between devices  266 us (35%)
  matrix products  186 us (24%)
  blocking collectives  106 us (14%)
  local copies, waits for them, and re-layouts  89.8 us (12%)
  other arithmetic  60.1 us (8%)
  starting transfers between devices  50.8 us (7%)
    ppermute x6, waiting for transfers between devices, extended(): lax.ppermute(tail, axis, [(i, (i + 1) % count) for i in range(ends)])  173 us
    all_to_all x1, blocking collectives, local(): lax.all_to_all(result, 'chan', split_axis=0, concat_axis=1, tiled=True)  95.9 us
    all_to_all x1, waiting for transfers between devices, local(): lax.all_to_all(moved, 'chan', split_axis=1, concat_axis=0, tiled=True)  92.4 us
    dot_general x1, matrix products, local(): jnp.einsum('cum,ul->cml', grid_block[1], sine_table, preferred_element_ty...  55.1 us
    add x2, other arithmetic, filter_rows(): running + filter_taps[tap_index] * source[:, first_row + offset:first_row...  53.1 us
    ppermute x6, starting transfers between devices, extended(): lax.ppermute(tail, axis, [(i, (i + 1) % count) for i in range(ends)])  25.1 us
    dot_general x1, matrix products, local(): jnp.einsum('cuv,vm->cum', imag_part, sine_table, preferred_element_type=j...  24 us
    dot_general x1, matrix products, local(): jnp.einsum('cum,ul->cml', grid_block[0], cosine, preferred_element_type=j...  22.7 us
  transfers between devices with their start and end apart: 14, of which 3 were waited for; matrix products, arithmetic and copies ran while one was open for 15% of the time, Pallas kernels for 0%

commit v1 on v0

v1 whole, which is shorter than its diff:
```python
import functools

import jax
import jax.numpy as jnp
import ml_dtypes
import numpy as np
from jax import lax
from jax.experimental import pallas as pl
from jax.experimental.pallas import tpu as pltpu
from jax.sharding import PartitionSpec as P

NS_ITERS = 5
CHUNK_ROWS = 16
HIGHEST = lax.Precision.HIGHEST
F32 = jnp.float32
BF16 = jnp.bfloat16
MIB = 1 << 20


def make_tables(side_len):
    indices = np.arange(side_len, dtype=np.int64)
    phases = (np.outer(indices, indices) % side_len).astype(np.float32) * np.float32(
        2.0 * 3.141592653589793 / side_len
    )
    unit_scale = np.float32(float(side_len) ** (-0.5))
    cosine = (np.cos(phases) * unit_scale).astype(ml_dtypes.bfloat16)
    sine_table = (np.sin(phases) * unit_scale).astype(ml_dtypes.bfloat16)
    return cosine, sine_table


def dot_nt(a, b, precision=None):
    return lax.dot_general(
        a, b, (((1,), (1,)), ((), ())), precision=precision, preferred_element_type=F32
    )


def dot_nn(a, b, precision=None):
    return lax.dot_general(
        a, b, (((1,), (0,)), ((), ())), precision=precision, preferred_element_type=F32
    )


def first_body(table_ref, grid_ref, out_ref):
    strips, _, chans, rows, width = out_ref.shape
    side_len = table_ref.shape[-1]
    table = table_ref[0]
    middle = strips * rows
    turned = jnp.concatenate([-table[middle:], table[:middle]], axis=0)
    total = dot_nt(table, grid_ref[0].reshape(chans * width, side_len))
    total = total + dot_nt(turned, grid_ref[1].reshape(chans * width, side_len))
    total = total.astype(BF16)
    for part in range(2):
        for strip in range(strips):
            first = (part * strips + strip) * rows
            for chan in range(chans):
                out_ref[strip, part, chan] = total[
                    first : first + rows, chan * width : (chan + 1) * width
                ]


def first_transform(tables, grid, chunk, strips):
    _, chans, width, side_len = grid.shape
    rows = tables.shape[1] // (2 * strips)
    shape = (strips, 2, chans, rows, width)
    if width % 128 or rows % 16:
        middle = strips * rows
        table = tables[chunk]
        turned = jnp.concatenate([-table[middle:], table[:middle]], axis=0)
        total = jnp.einsum("mv,cuv->mcu", table, grid[0], preferred_element_type=F32)
        total = total + jnp.einsum("mv,cuv->mcu", turned, grid[1], preferred_element_type=F32)
        total = total.astype(BF16).reshape(2, strips, rows, chans, width)
        return total.transpose(1, 0, 3, 2, 4)
    block = 4 if chans % 4 == 0 else 1
    return pl.pallas_call(
        first_body,
        grid=(chans // block,),
        in_specs=[
            pl.BlockSpec((1,) + tables.shape[1:], lambda i: (chunk, 0, 0)),
            pl.BlockSpec((2, block, width, side_len), lambda i: (0, i, 0, 0)),
        ],
        out_specs=pl.BlockSpec((strips, 2, block, rows, width), lambda i: (0, 0, i, 0, 0)),
        out_shape=jax.ShapeDtypeStruct(shape, BF16),
        compiler_params=pltpu.CompilerParams(vmem_limit_bytes=48 * MIB),
        cost_estimate=pl.CostEstimate(
            flops=4 * 2 * strips * rows * chans * width * side_len // 2,
            bytes_accessed=2 * grid.size,
            transcendentals=0,
        ),
        name="first_transform",
    )(tables, grid)


def band_matrix(highpass, own_rows, reach, first_row, image_rows):
    levels, taps = highpass.shape
    half_taps = taps // 2
    row = lax.broadcasted_iota(jnp.int32, (own_rows, own_rows + 2 * reach), 0)
    column = lax.broadcasted_iota(jnp.int32, (own_rows, own_rows + 2 * reach), 1) - reach
    total = jnp.zeros(row.shape, F32)
    for level in range(levels):
        dilation = 2**level
        for outer in range(taps):
            detail_row = row - (outer - half_taps) * dilation
            inside = (detail_row + first_row >= 0) & (detail_row + first_row < image_rows)
            for inner in range(taps):
                hit = inside & (column == detail_row + (inner - half_taps) * dilation)
                total = total + jnp.where(hit, highpass[level, outer] * highpass[level, inner], 0.0)
    return total


def base_body(step_ref, own_ref, side_ref, model_ref, edge_ref, out_ref):
    first = pl.program_id(0) * model_ref.shape[0]
    for chan in range(model_ref.shape[0]):
        model = model_ref[chan]
        gradient = dot_nn(own_ref[...], model, HIGHEST)
        gradient = gradient + dot_nn(side_ref[...], edge_ref[chan].astype(F32), HIGHEST)
        out_ref[chan] = model - step_ref[first + chan] * gradient


def base_step(step_size, own_band, side_band, model_image, edges):
    chans, rows, side_len = model_image.shape
    block = 2 if chans % 2 == 0 else 1
    return pl.pallas_call(
        base_body,
        grid=(chans // block,),
        in_specs=[
            pl.BlockSpec(memory_space=pltpu.SMEM),
            pl.BlockSpec(own_band.shape, lambda i: (0, 0)),
            pl.BlockSpec(side_band.shape, lambda i: (0, 0)),
            pl.BlockSpec((block, rows, side_len), lambda i: (i, 0, 0)),
            pl.BlockSpec((block, edges.shape[1], side_len), lambda i: (i, 0, 0)),
        ],
        out_specs=pl.BlockSpec((block, rows, side_len), lambda i: (i, 0, 0)),
        out_shape=jax.ShapeDtypeStruct(model_image.shape, F32),
        compiler_params=pltpu.CompilerParams(vmem_limit_bytes=32 * MIB),
        cost_estimate=pl.CostEstimate(
            flops=12 * rows * rows * chans * side_len, bytes_accessed=8 * model_image.size, transcendentals=0
        ),
        name="base_step",
    )(step_size, own_band, side_band, model_image, edges)


def second_body(step_ref, half_ref, cosine_ref, sine_ref, base_ref, moved_ref, pixels_ref):
    strips, _, chans, rows, width = half_ref.shape
    real = jnp.concatenate([half_ref[s, 0].reshape(chans * rows, width) for s in range(strips)], axis=1)
    imag = jnp.concatenate([half_ref[s, 1].reshape(chans * rows, width) for s in range(strips)], axis=1)
    dirty = dot_nn(real, cosine_ref[...]) - dot_nn(imag, sine_ref[...])
    pieces = []
    for chan in range(chans):
        moved = base_ref[chan] + step_ref[chan] * dirty[chan * rows : (chan + 1) * rows]
        moved_ref[chan] = moved
        pieces.append(moved)
    pixels_ref[...] = jnp.swapaxes(jnp.stack(pieces), 0, 1).astype(BF16)


def second_transform(step_size, half, cosine, sine_table, base, chunk):
    strips, _, chans, rows, width = half.shape
    side_len = cosine.shape[0]
    if width % 128 or rows % 16 or chans % 16:
        dirty = jnp.einsum("scmu,sul->cml", half[:, 0], cosine.reshape(strips, width, side_len), preferred_element_type=F32)
        dirty = dirty - jnp.einsum(
            "scmu,sul->cml", half[:, 1], sine_table.reshape(strips, width, side_len), preferred_element_type=F32
        )
        moved = base[:, chunk * rows : (chunk + 1) * rows] + step_size[:, None, None] * dirty
        pixels = moved.astype(BF16).transpose(1, 0, 2)
        return lax.dynamic_update_slice(base, moved, (0, chunk * rows, 0)), pixels
    block = min(256, side_len)
    return pl.pallas_call(
        second_body,
        grid=(side_len // block,),
        in_specs=[
            pl.BlockSpec(memory_space=pltpu.SMEM),
            pl.BlockSpec(half.shape, lambda i: (0, 0, 0, 0, 0)),
            pl.BlockSpec((side_len, block), lambda i: (0, i)),
            pl.BlockSpec((side_len, block), lambda i: (0, i)),
            pl.BlockSpec((chans, rows, block), lambda i: (0, chunk, i)),
        ],
        out_specs=[
            pl.BlockSpec((chans, rows, block), lambda i: (0, chunk, i)),
            pl.BlockSpec((rows, chans, block), lambda i: (0, 0, i)),
        ],
        out_shape=[
            jax.ShapeDtypeStruct(base.shape, F32),
            jax.ShapeDtypeStruct((rows, chans, side_len), BF16),
        ],
        input_output_aliases={4: 0},
        compiler_params=pltpu.CompilerParams(vmem_limit_bytes=32 * MIB),
        cost_estimate=pl.CostEstimate(
            flops=4 * chans * rows * side_len * side_len,
            bytes_accessed=4 * side_len * side_len + 10 * chans * rows * side_len,
            transcendentals=0,
        ),
        name="second_transform",
    )(step_size, half, cosine, sine_table, base)


GRAM_ROWS = 4
POLAR_ROWS = 8


def stacked(pixels_ref, first, count):
    groups = pixels_ref.shape[0]
    pieces = [pixels_ref[g, first + i] for i in range(count) for g in range(groups)]
    return jnp.concatenate(pieces, axis=0)


def gram_body(pixels_ref, before_ref, total_ref):
    @pl.when(pl.program_id(0) == 0)
    def _():
        total_ref[...] = before_ref[...]

    pixels = stacked(pixels_ref, 0, GRAM_ROWS)
    total_ref[...] += dot_nt(pixels, pixels)


def gram_step(pixels, before):
    groups, rows, chans, side_len = pixels.shape
    return pl.pallas_call(
        gram_body,
        grid=(rows // GRAM_ROWS,),
        in_specs=[
            pl.BlockSpec((groups, GRAM_ROWS, chans, side_len), lambda i: (0, i, 0, 0)),
            pl.BlockSpec(before.shape, lambda i: (0, 0)),
        ],
        out_specs=pl.BlockSpec(before.shape, lambda i: (0, 0)),
        out_shape=jax.ShapeDtypeStruct(before.shape, F32),
        compiler_params=pltpu.CompilerParams(vmem_limit_bytes=32 * MIB),
        cost_estimate=pl.CostEstimate(
            flops=2 * before.size * side_len * rows // GRAM_ROWS, bytes_accessed=2 * pixels.size, transcendentals=0
        ),
        name="gram_step",
    )(pixels, before)


def iota(shape, dim):
    return lax.broadcasted_iota(jnp.int32, shape, dim)


def newton_schulz(gram):
    size = gram.shape[0]
    frob_norm = jnp.sqrt(jnp.sum(gram * gram))
    identity = (iota((size, size), 0) == iota((size, size), 1)).astype(F32)
    current = gram / frob_norm
    inverse = identity
    for iteration in range(NS_ITERS):
        middle = 0.5 * (3.0 * identity - dot_nn(inverse, current, HIGHEST))
        if iteration + 1 < NS_ITERS:
            current = dot_nn(current, middle, HIGHEST)
        inverse = dot_nn(middle, inverse, HIGHEST)
    return inverse, frob_norm


def polar_body(chunks, shrink_ref, select_ref, gram_ref, moved_hbm, *refs):
    pixels_hbm = refs[:chunks]
    out_hbm, pixels, moved, in_sems, moved_sems, out_sems = refs[chunks:]
    own, all_rows, side_len = moved.shape
    rows = all_rows // chunks
    size = select_ref.shape[1]
    moved_copies = []
    pixel_copies = []
    for chunk in range(chunks):
        copy = pltpu.make_async_copy(pixels_hbm[chunk], pixels.at[chunk], in_sems.at[chunk])
        copy.start()
        pixel_copies.append(copy)
        part = pl.ds(chunk * rows, rows)
        copy = pltpu.make_async_copy(moved_hbm.at[:, part], moved.at[:, part], moved_sems.at[chunk])
        copy.start()
        moved_copies.append(copy)
    gram = jnp.zeros((size, size), F32)
    for i in range(GRAM_ROWS):
        gram = gram + gram_ref[i * size : (i + 1) * size, i * size : (i + 1) * size]
    inverse, frob_norm = newton_schulz(gram)
    factor = shrink_ref[0] * jnp.sqrt(all_rows * side_len / frob_norm)
    weights = dot_nt(select_ref[...], inverse, HIGHEST) * factor
    spread = POLAR_ROWS * own
    wide = POLAR_ROWS * size
    repeat = (iota((spread, own), 0) // POLAR_ROWS == iota((spread, own), 1)).astype(BF16)
    weights = dot_nn(repeat, weights.astype(BF16)).astype(BF16)
    repeat = (iota((size, wide), 1) % size == iota((size, wide), 0)).astype(BF16)
    weights = dot_nn(weights, repeat)
    keep = iota((spread, wide), 0) % POLAR_ROWS == iota((spread, wide), 1) // size
    weights = jnp.where(keep, weights, 0.0).astype(BF16)
    out_copies = []
    for chunk in range(chunks):
        pixel_copies[chunk].wait()
        moved_copies[chunk].wait()
        for group in range(rows // POLAR_ROWS):
            data = stacked(pixels.at[chunk], group * POLAR_ROWS, POLAR_ROWS)
            polar = dot_nn(weights, data).reshape(own, POLAR_ROWS, side_len)
            first = chunk * rows + group * POLAR_ROWS
            moved[:, first : first + POLAR_ROWS] -= polar
        part = pl.ds(chunk * rows, rows)
        copy = pltpu.make_async_copy(moved.at[:, part], out_hbm.at[:, part], out_sems.at[chunk])
        copy.start()
        out_copies.append(copy)
    for copy in out_copies:
        copy.wait()


def polar_step(shrinkage, select, gram, moved, pixels):
    chunks = len(pixels)
    hbm = pl.BlockSpec(memory_space=pl.ANY)
    return pl.pallas_call(
        functools.partial(polar_body, chunks),
        in_specs=[
            pl.BlockSpec(memory_space=pltpu.SMEM),
            pl.BlockSpec(memory_space=pltpu.VMEM),
            pl.BlockSpec(memory_space=pltpu.VMEM),
            hbm,
        ]
        + [hbm] * chunks,
        out_specs=hbm,
        out_shape=jax.ShapeDtypeStruct(moved.shape, F32),
        scratch_shapes=[
            pltpu.VMEM((chunks,) + pixels[0].shape, BF16),
            pltpu.VMEM(moved.shape, F32),
            pltpu.SemaphoreType.DMA((chunks,)),
            pltpu.SemaphoreType.DMA((chunks,)),
            pltpu.SemaphoreType.DMA((chunks,)),
        ],
        compiler_params=pltpu.CompilerParams(vmem_limit_bytes=48 * MIB),
        name="polar_step",
    )(shrinkage, select, gram, moved, *pixels)


def neighbour_rows(model_image, reach):
    count = lax.axis_size("strip")
    ends = count - 1
    head = model_image[:, :reach].astype(BF16)
    tail = model_image[:, model_image.shape[1] - reach :].astype(BF16)
    before = lax.ppermute(tail, "strip", [(i, i + 1) for i in range(ends)])
    after = lax.ppermute(head, "strip", [(i + 1, i) for i in range(ends)])
    return jnp.concatenate([before, after], axis=1)


def local(grid, model_image, step_size, highpass, shrinkage):
    chans, own_rows, side_len = model_image.shape
    strips = lax.axis_size("strip")
    chan_devices = lax.axis_size("chan")
    size = chans * chan_devices
    rows = CHUNK_ROWS
    chunks = own_rows // rows

    cosine, sine_table = make_tables(side_len)
    split = (strips, chunks, rows, side_len)
    tables = np.stack([cosine.reshape(split), sine_table.reshape(split)])
    tables = tables.transpose(2, 0, 1, 3, 4).reshape(chunks, 2 * strips * rows, side_len)

    levels, taps = highpass.shape
    reach = (taps - 1) * 2 ** (levels - 1)
    edges = neighbour_rows(model_image, reach)

    halves = []
    for chunk in range(chunks):
        sent = first_transform(tables, grid, chunk, strips)
        halves.append(lax.all_to_all(sent, "strip", split_axis=0, concat_axis=0, tiled=True))

    first_row = lax.axis_index("strip") * own_rows
    band = band_matrix(highpass, own_rows, reach, first_row, strips * own_rows)
    own_band = band[:, reach : reach + own_rows]
    side_band = jnp.concatenate([band[:, :reach], band[:, reach + own_rows :]], axis=1)
    moved = base_step(step_size, own_band, side_band, model_image, edges)

    gram = jnp.zeros((GRAM_ROWS * size, GRAM_ROWS * size), F32)
    gathered = []
    for chunk in range(chunks):
        moved, pixels = second_transform(step_size, halves[chunk], cosine, sine_table, moved, chunk)
        pixels = lax.all_gather(pixels, "chan", axis=0, tiled=False)
        if chans % 16:
            pixels = pixels.transpose(1, 0, 2, 3).reshape(1, rows, size, side_len)
        gram = gram_step(pixels, gram)
        gathered.append(pixels)

    own = lax.axis_index("chan") * chans + jnp.arange(chans, dtype=jnp.int32)
    select = (own[:, None] == jnp.arange(size, dtype=jnp.int32)[None, :]).astype(F32)
    return polar_step(shrinkage, select, gram, moved, gathered)


def solution(mesh):
    return jax.shard_map(
        local,
        mesh=mesh,
        in_specs=(
            P(None, "chan", "strip", None),
            P("chan", "strip", None),
            P("chan"),
            P(),
            P("strip"),
        ),
        out_specs=P("chan", "strip", None),
        check_vma=False,
    )
```

time: 769 us -> 475 us (0.62)
  waiting for transfers between devices: 266 us -> 0.29 us
  matrix products: 186 us -> 0 us
  Pallas kernels: 0 us -> 116 us
  blocking collectives: 106 us -> 200 us
  other arithmetic: 60.1 us -> 5.62 us
  between operations: 2.16 us -> 51.9 us
  starting transfers between devices: 50.8 us -> 12.5 us
    dot_general x22 -> x0, matrix products: 186 us -> none  [the longest x1 55.1 us: local(): jnp.einsum('cum,ul->cml', grid_block[1], sine_table, preferred_element_ty...]
    ppermute x12 -> x2, waiting for transfers between devices: 173 us -> 0.01 us  [the longest x1 0.01 us: neighbour_rows(): before = lax.ppermute(tail, 'strip', [(i, i + 1) for i in range(ends)])]
    pallas_call x0 -> x26, Pallas kernels: none -> 116 us  [the longest x8 48.1 us: first_transform(): pl.pallas_call(first_body, grid=(chans // block,), in_specs=[pl.BlockSpec...]
    all_to_all x1 -> x7, blocking collectives: 95.9 us -> 200 us  [local(): lax.all_to_all(sent, 'strip', split_axis=0, concat_axis=0, tiled=True)]
    all_to_all x2 -> x1, waiting for transfers between devices: 92.4 us -> 0.01 us  [local(): lax.all_to_all(sent, 'strip', split_axis=0, concat_axis=0, tiled=True)]
    unnamed x15 -> x96, local copies, waits for them, and re-layouts: 17.6 us -> 82.9 us
    add x2 -> x9, other arithmetic: 53.1 us -> 1.13 us  [the longest x1 1.1 us: band_matrix(): total + jnp.where(hit, highpass[level, outer] * highpass[level, inner], 0.0)]
    ppermute x12 -> x2, starting transfers between devices: 38.6 us -> 5.84 us  [the longest x1 3.37 us: neighbour_rows(): before = lax.ppermute(tail, 'strip', [(i, i + 1) for i in range(ends)])]
  transfers between devices with their start and end apart: 14 -> 11, of which waited for: 3 -> 0; matrix products, arithmetic and copies ran while one was open for 15% -> 1% of each run, Pallas kernels for 0% -> 20%
where the time goes in v1:
time: 475 us; the launch traced here: 470 us
  blocking collectives  200 us (42%)
  Pallas kernels  116 us (24%)
  local copies, waits for them, and re-layouts  84 us (18%)
  between operations  51.9 us (11%)
  starting transfers between devices  12.5 us (3%)
  other arithmetic  5.62 us (1%)
    all_to_all x7, blocking collectives, local(): lax.all_to_all(sent, 'strip', split_axis=0, concat_axis=0, tiled=True)  200 us
    unnamed x96, local copies, waits for them, and re-layouts  82.9 us
    pallas_call x8, Pallas kernels, first_transform(): pl.pallas_call(first_body, grid=(chans // block,), in_specs=[pl.BlockSpec...  48.1 us
    pallas_call x8, Pallas kernels, second_transform(): pl.pallas_call(second_body, grid=(side_len // block,), in_specs=[pl.Block...  28.7 us
    pallas_call x1, Pallas kernels, base_step(): pl.pallas_call(base_body, grid=(chans // block,), in_specs=[pl.BlockSpec(...  14.8 us
    pallas_call x8, Pallas kernels, gram_step(): pl.pallas_call(gram_body, grid=(rows // GRAM_ROWS,), in_specs=[pl.BlockSp...  12.6 us
    pallas_call x1, Pallas kernels, polar_step(): pl.pallas_call(functools.partial(polar_body, chunks), in_specs=[pl.BlockS...  11.6 us
  transfers between devices with their start and end apart: 11, of which 0 were waited for; matrix products, arithmetic and copies ran while one was open for 1% of the time, Pallas kernels for 20%

profile of v1, /device:TPU:12, one launch (start us, length us, event | category | flops | bytes accessed | tf_op | source)
XLA Modules:
  0.0 470.2 jit_solution(3021274446204007413)
XLA Ops:
  6.5 2.2 copy-done.17
  8.7 6.4 %first_transform.15 = bf16[8,2,16,16,128]{4,3,2,1,0:T(8,128)(2,1)} custom-call(bf16[8,256,1024]{2,1,0:T(8,128)(2,1)S(1)} %copy-done.17, bf16[2,16,128,1024]{3,2,1,0:T(8,128)(2,1)} %grid_ref.15), custom_call_target="tpu_custom_call" | custom-call | flops 1073741824 | bytes 8388608 | tf_op jit(solution)/shard_map/first_transform/pallas_call | solution.py:74
  15.1 6.2 %all-to-all-start.7 = ((bf16[8,2,16,16,128]{4,3,2,1,0:T(8,128)(2,1)}), bf16[8,2,16,16,128]{4,3,2,1,0:T(8,128)(2,1)S(1)}, u32[]{:S(2)}, u32[]{:S(2)}) async-start(bf16[8,2,16,16,128]{4,3,2,1,0:T(8,128)(2,1)} %first_transform.15), calls=%async_computation.7 | async-start | bytes 2097152 | tf_op jit(solution)/shard_map/all_to_all | solution.py:355
  21.4 4.1 convert.4
  25.6 3.4 collective-permute-start
  29.0 2.5 collective-permute-start.1
  71.2 3.4 copy-done.34
  74.6 14.8 %base_step.1.base_ref = f32[16,128,1024]{2,1,0:T(8,128)S(1)} custom-call(f32[16]{0:T(128)S(1)} %copy-done.46, f32[128,128]{1,0:T(8,128)S(1)} %slice.53.own_ref, f32[128,24]{1,0:T(8,128)S(1)} %pad_maximum_fusion.1.side_ref, f32[16,128,1024]{2,1,0:T(8,128)S(1)} %copy-done.34, bf16[16,24,1024]{2,1,0:T(8,128)(2,1)S(1)} %pad_maximum_fusion.edge_ref), custom_call_target="tpu_custom_call" | custom-call | flops 3221225472 | bytes 16777216 | tf_op jit(solution)/shard_map/base_step/pallas_call | solution.py:122
  89.4 3.4 copy-done
  92.8 3.4 copy-done.1
  97.7 3.0 second_transform.8
  100.8 3.4 copy-done.2
  105.1 2.2 copy-done.18
  107.2 5.9 %first_transform.14 = bf16[8,2,16,16,128]{4,3,2,1,0:T(8,128)(2,1)S(1)} custom-call(bf16[8,256,1024]{2,1,0:T(8,128)(2,1)S(1)} %copy-done.18, bf16[2,16,128,1024]{3,2,1,0:T(8,128)(2,1)} %grid_ref.15), custom_call_target="tpu_custom_call" | custom-call | flops 1073741824 | bytes 8388608 | tf_op jit(solution)/shard_map/first_transform/pallas_call | solution.py:74
  113.2 28.3 %all_to_all.40.half_ref = bf16[8,2,16,16,128]{4,3,2,1,0:T(8,128)(2,1)S(1)} all-to-all(bf16[8,2,16,16,128]{4,3,2,1,0:T(8,128)(2,1)S(1)} %first_transform.14), channel_id=1, replica_groups=mesh['strip'=8,'chan'=4] {'strip'}, dimensions={0} | all-to-all | bytes 2097152 | tf_op jit(solution)/shard_map/all_to_all | solution.py:355
  143.1 3.7 second_transform.9
  146.7 3.4 copy-done.4
  150.2 2.2 copy-done.19
  152.4 6.0 %first_transform.13 = bf16[8,2,16,16,128]{4,3,2,1,0:T(8,128)(2,1)S(1)} custom-call(bf16[8,256,1024]{2,1,0:T(8,128)(2,1)S(1)} %copy-done.19, bf16[2,16,128,1024]{3,2,1,0:T(8,128)(2,1)} %grid_ref.15), custom_call_target="tpu_custom_call" | custom-call | flops 1073741824 | bytes 8388608 | tf_op jit(solution)/shard_map/first_transform/pallas_call | solution.py:74
  158.4 28.6 %all_to_all.41.half_ref = bf16[8,2,16,16,128]{4,3,2,1,0:T(8,128)(2,1)S(1)} all-to-all(bf16[8,2,16,16,128]{4,3,2,1,0:T(8,128)(2,1)S(1)} %first_transform.13), channel_id=1, replica_groups=mesh['strip'=8,'chan'=4] {'strip'}, dimensions={0} | all-to-all | bytes 2097152 | tf_op jit(solution)/shard_map/all_to_all | solution.py:355
  188.6 3.7 second_transform.10
  192.2 3.4 copy-done.6
  195.7 2.2 copy-done.20
  197.9 6.0 %first_transform.12 = bf16[8,2,16,16,128]{4,3,2,1,0:T(8,128)(2,1)S(1)} custom-call(bf16[8,256,1024]{2,1,0:T(8,128)(2,1)S(1)} %copy-done.20, bf16[2,16,128,1024]{3,2,1,0:T(8,128)(2,1)} %grid_ref.15), custom_call_target="tpu_custom_call" | custom-call | flops 1073741824 | bytes 8388608 | tf_op jit(solution)/shard_map/first_transform/pallas_call | solution.py:74
  203.9 28.6 %all_to_all.42.half_ref = bf16[8,2,16,16,128]{4,3,2,1,0:T(8,128)(2,1)S(1)} all-to-all(bf16[8,2,16,16,128]{4,3,2,1,0:T(8,128)(2,1)S(1)} %first_transform.12), channel_id=1, replica_groups=mesh['strip'=8,'chan'=4] {'strip'}, dimensions={0} | all-to-all | bytes 2097152 | tf_op jit(solution)/shard_map/all_to_all | solution.py:355
  234.1 3.7 second_transform.11
  237.7 3.4 copy-done.8
  241.2 2.2 copy-done.21
  243.4 6.0 %first_transform.11 = bf16[8,2,16,16,128]{4,3,2,1,0:T(8,128)(2,1)S(1)} custom-call(bf16[8,256,1024]{2,1,0:T(8,128)(2,1)S(1)} %copy-done.21, bf16[2,16,128,1024]{3,2,1,0:T(8,128)(2,1)} %grid_ref.15), custom_call_target="tpu_custom_call" | custom-call | flops 1073741824 | bytes 8388608 | tf_op jit(solution)/shard_map/first_transform/pallas_call | solution.py:74
  249.4 28.6 %all_to_all.43.half_ref = bf16[8,2,16,16,128]{4,3,2,1,0:T(8,128)(2,1)S(1)} all-to-all(bf16[8,2,16,16,128]{4,3,2,1,0:T(8,128)(2,1)S(1)} %first_transform.11), channel_id=1, replica_groups=mesh['strip'=8,'chan'=4] {'strip'}, dimensions={0} | all-to-all | bytes 2097152 | tf_op jit(solution)/shard_map/all_to_all | solution.py:355
  279.6 3.7 second_transform.12
  283.3 3.4 copy-done.10
  286.9 2.2 copy-done.22
  289.1 6.0 %first_transform.10 = bf16[8,2,16,16,128]{4,3,2,1,0:T(8,128)(2,1)S(1)} custom-call(bf16[8,256,1024]{2,1,0:T(8,128)(2,1)S(1)} %copy-done.22, bf16[2,16,128,1024]{3,2,1,0:T(8,128)(2,1)} %grid_ref.15), custom_call_target="tpu_custom_call" | custom-call | flops 1073741824 | bytes 8388608 | tf_op jit(solution)/shard_map/first_transform/pallas_call | solution.py:74
  295.1 28.6 %all_to_all.44.half_ref = bf16[8,2,16,16,128]{4,3,2,1,0:T(8,128)(2,1)S(1)} all-to-all(bf16[8,2,16,16,128]{4,3,2,1,0:T(8,128)(2,1)S(1)} %first_transform.10), channel_id=1, replica_groups=mesh['strip'=8,'chan'=4] {'strip'}, dimensions={0} | all-to-all | bytes 2097152 | tf_op jit(solution)/shard_map/all_to_all | solution.py:355
  325.3 3.7 second_transform.13
  329.0 3.4 copy-done.12
  332.5 2.2 copy-done.23
  334.6 6.0 %first_transform.9 = bf16[8,2,16,16,128]{4,3,2,1,0:T(8,128)(2,1)S(1)} custom-call(bf16[8,256,1024]{2,1,0:T(8,128)(2,1)S(1)} %copy-done.23, bf16[2,16,128,1024]{3,2,1,0:T(8,128)(2,1)} %grid_ref.15), custom_call_target="tpu_custom_call" | custom-call | flops 1073741824 | bytes 8388608 | tf_op jit(solution)/shard_map/first_transform/pallas_call | solution.py:74
  340.6 28.6 %all_to_all.45.half_ref = bf16[8,2,16,16,128]{4,3,2,1,0:T(8,128)(2,1)S(1)} all-to-all(bf16[8,2,16,16,128]{4,3,2,1,0:T(8,128)(2,1)S(1)} %first_transform.9), channel_id=1, replica_groups=mesh['strip'=8,'chan'=4] {'strip'}, dimensions={0} | all-to-all | bytes 2097152 | tf_op jit(solution)/shard_map/all_to_all | solution.py:355
  370.8 3.7 second_transform.14
  374.5 3.4 copy-done.14
  378.0 2.2 copy-done.24
  380.2 6.0 %first_transform.8 = bf16[8,2,16,16,128]{4,3,2,1,0:T(8,128)(2,1)S(1)} custom-call(bf16[8,256,1024]{2,1,0:T(8,128)(2,1)S(1)} %copy-done.24, bf16[2,16,128,1024]{3,2,1,0:T(8,128)(2,1)} %grid_ref.15), custom_call_target="tpu_custom_call" | custom-call | flops 1073741824 | bytes 8388608 | tf_op jit(solution)/shard_map/first_transform/pallas_call | solution.py:74
  386.1 28.6 %all_to_all.46.half_ref = bf16[8,2,16,16,128]{4,3,2,1,0:T(8,128)(2,1)S(1)} all-to-all(bf16[8,2,16,16,128]{4,3,2,1,0:T(8,128)(2,1)S(1)} %first_transform.8), channel_id=1, replica_groups=mesh['strip'=8,'chan'=4] {'strip'}, dimensions={0} | all-to-all | bytes 2097152 | tf_op jit(solution)/shard_map/all_to_all | solution.py:355
  416.4 3.7 second_transform.15
  420.0 3.3 copy-done.16
  451.7 11.6 %polar_step.1 = f32[16,128,1024]{2,1,0:T(8,128)} custom-call(f32[1]{0:T(128)S(6)} %copy.28.shrink_ref, f32[16,64]{1,0:T(8,128)S(1)} %fusion.61.select_ref, f32[256,256]{1,0:T(8,128)S(1)} %gram_step.15.gram_ref, f32[16,128,1024]{2,1,0:T(8,128)} %copy-done.16, bf16[4,16,16,1024]{3,2,1,0:T(8,128)(2,1)S(1)} %bitcast.39, bf16[4,16,16,1024]{3,2,1,0:T(8,128)(2,1)S(1)} %bitcast.41, ...), custom_call_target="tpu_custom_call" | custom-call | tf_op jit(solution)/shard_map/polar_step/pallas_call | solution.py:302
  (134 shorter events, 44.2 us)
Async XLA Ops:
  6.5 2.2 copy-start.17
  15.1 77.6 %all-to-all-start.7 = ((bf16[8,2,16,16,128]{4,3,2,1,0:T(8,128)(2,1)}), bf16[8,2,16,16,128]{4,3,2,1,0:T(8,128)(2,1)S(1)}, u32[]{:S(2)}, u32[]{:S(2)}) async-start(bf16[8,2,16,16,128]{4,3,2,1,0:T(8,128)(2,1)} %first_transform.15), calls=%async_computation.7 | async-start | bytes 2097152 | tf_op jit(solution)/shard_map/all_to_all | solution.py:355
  21.4 10.2 %copy-start.47 = (f32[3,4]{1,0:T(4,128)S(1)}, f32[3,4]{1,0:T(4,128)}, u32[]{:S(2)}) copy-start(f32[3,4]{1,0:T(4,128)} %param.11) | copy-start | bytes 148
  21.4 402.7 %all-gather.31.cloned.1.call-start = ((), (), s32[]{:S(2)}) async-start(), calls=%async_computation.15 | async-start | bytes 2621440 | tf_op jit(solution)/shard_map/all_gather | solution.py:367
  25.4 45.7 %copy-start.46 = (f32[16]{0:T(128)S(1)}, f32[16]{0:T(128)}, u32[]{:S(2)}) copy-start(f32[16]{0:T(128)} %step_ref.17) | copy-start | bytes 196
  25.6 45.3 %collective-permute-start = (bf16[16,12,1024]{2,1,0:T(8,128)(2,1)S(1)}, bf16[16,12,1024]{2,1,0:T(8,128)(2,1)S(1)}, u32[]{:S(2)}, u32[]{:S(2)}) collective-permute-start(bf16[16,12,1024]{2,1,0:T(8,128)(2,1)S(1)} %get-tuple-element.37), channel_id=1, source_target_pairs={{0,4},{4,8},{8,12},{12,16},{16,20},{20,24},{24,28},{1,5},{5,9},{9,... | collective-permute-start | bytes 1179656 | tf_op jit(solution)/shard_map/ppermute | solution.py:330
  29.0 41.9 %collective-permute-start.1 = (bf16[16,12,1024]{2,1,0:T(8,128)(2,1)S(1)}, bf16[16,12,1024]{2,1,0:T(8,128)(2,1)S(1)}, u32[]{:S(2)}, u32[]{:S(2)}) collective-permute-start(bf16[16,12,1024]{2,1,0:T(8,128)(2,1)S(1)} %get-tuple-element.38), channel_id=1, source_target_pairs={{4,0},{8,4},{12,8},{16,12},{20,16},{24,20},{28,24},{5,1},{9,5},{13... | collective-permute-start | bytes 1179656 | tf_op jit(solution)/shard_map/ppermute | solution.py:331
  71.2 3.4 copy-start.34
  74.6 18.2 %copy-start.25 = (bf16[1024,1024]{1,0:T(8,128)(2,1)S(1)}, bf16[1024,1024]{1,0:T(8,128)(2,1)}, u32[]{:S(2)}) copy-start(bf16[1024,1024]{1,0:T(8,128)(2,1)} %constant.83.clone.sine_ref) | copy-start | bytes 6291460
  89.4 3.4 copy-start
  92.8 3.4 copy-start.1
  100.8 3.4 copy-start.2
  105.0 322.3 %all-gather.29.cloned.1.call-start = ((), (), s32[]{:S(2)}) async-start(), calls=%async_computation.14 | async-start | bytes 2621440 | tf_op jit(solution)/shard_map/all_gather | solution.py:367
  105.0 2.2 copy-start.18
  107.2 34.2 %copy-start.3 = (f32[16,128,1024]{2,1,0:T(8,128)S(1)}, f32[16,128,1024]{2,1,0:T(8,128)}, u32[]{:S(2)}) copy-start(f32[16,128,1024]{2,1,0:T(8,128)} %copy-done.2) | copy-start | bytes 25165828
  146.7 3.4 copy-start.4
  150.2 280.4 %all-gather.27.cloned.1.call-start = ((), (), s32[]{:S(2)}) async-start(), calls=%async_computation.13 | async-start | bytes 2621440 | tf_op jit(solution)/shard_map/all_gather | solution.py:367
  150.2 2.2 copy-start.19
  152.4 34.6 %copy-start.5 = (f32[16,128,1024]{2,1,0:T(8,128)S(1)}, f32[16,128,1024]{2,1,0:T(8,128)}, u32[]{:S(2)}) copy-start(f32[16,128,1024]{2,1,0:T(8,128)} %copy-done.4) | copy-start | bytes 25165828
  192.2 3.4 copy-start.6
  195.7 238.2 %all-gather.25.cloned.1.call-start = ((), (), s32[]{:S(2)}) async-start(), calls=%async_computation.12 | async-start | bytes 2621440 | tf_op jit(solution)/shard_map/all_gather | solution.py:367
  195.7 2.2 copy-start.20
  197.9 34.6 %copy-start.7 = (f32[16,128,1024]{2,1,0:T(8,128)S(1)}, f32[16,128,1024]{2,1,0:T(8,128)}, u32[]{:S(2)}) copy-start(f32[16,128,1024]{2,1,0:T(8,128)} %copy-done.6) | copy-start | bytes 25165828
  237.7 3.4 copy-start.8
  241.2 195.9 %all-gather.23.cloned.1.call-start = ((), (), s32[]{:S(2)}) async-start(), calls=%async_computation.11 | async-start | bytes 2621440 | tf_op jit(solution)/shard_map/all_gather | solution.py:367
  241.2 2.2 copy-start.21
  243.4 34.6 %copy-start.9 = (f32[16,128,1024]{2,1,0:T(8,128)S(1)}, f32[16,128,1024]{2,1,0:T(8,128)}, u32[]{:S(2)}) copy-start(f32[16,128,1024]{2,1,0:T(8,128)} %copy-done.8) | copy-start | bytes 25165828
  283.3 3.4 copy-start.10
  286.7 153.7 %all-gather.21.cloned.1.call-start = ((), (), s32[]{:S(2)}) async-start(), calls=%async_computation.10 | async-start | bytes 2621440 | tf_op jit(solution)/shard_map/all_gather | solution.py:367
  286.9 2.2 copy-start.22
  289.1 34.6 %copy-start.11 = (f32[16,128,1024]{2,1,0:T(8,128)S(1)}, f32[16,128,1024]{2,1,0:T(8,128)}, u32[]{:S(2)}) copy-start(f32[16,128,1024]{2,1,0:T(8,128)} %copy-done.10) | copy-start | bytes 25165828
  329.0 3.4 copy-start.12
  332.4 111.3 %all-gather.19.cloned.1.call-start = ((), (), s32[]{:S(2)}) async-start(), calls=%async_computation.9 | async-start | bytes 2621440 | tf_op jit(solution)/shard_map/all_gather | solution.py:367
  332.4 2.2 copy-start.23
  334.6 34.6 %copy-start.13 = (f32[16,128,1024]{2,1,0:T(8,128)S(1)}, f32[16,128,1024]{2,1,0:T(8,128)}, u32[]{:S(2)}) copy-start(f32[16,128,1024]{2,1,0:T(8,128)} %copy-done.12) | copy-start | bytes 25165828
  374.5 3.4 copy-start.14
  377.9 69.0 %all-gather.17.cloned.1.call-start = ((), (), s32[]{:S(2)}) async-start(), calls=%async_computation.8 | async-start | bytes 2621440 | tf_op jit(solution)/shard_map/all_gather | solution.py:367
  378.0 2.2 copy-start.24
  380.2 34.6 %copy-start.15 = (f32[16,128,1024]{2,1,0:T(8,128)S(1)}, f32[16,128,1024]{2,1,0:T(8,128)}, u32[]{:S(2)}) copy-start(f32[16,128,1024]{2,1,0:T(8,128)} %copy-done.14) | copy-start | bytes 25165828
  414.8 1.6 copy-start.33
  420.0 3.3 copy-start.16
  430.5 1.7 copy-start.39
  433.9 1.6 copy-start.40
  437.1 1.6 copy-start.41
  440.3 9.8 %copy-start.36 = (bf16[64,16,1024]{2,1,0:T(8,128)(2,1)S(1)}, bf16[64,16,1024]{2,1,0:T(8,128)(2,1)}, u32[]{:S(2)}) copy-start(bf16[64,16,1024]{2,1,0:T(8,128)(2,1)} %all-gather.31.cloned.1.call-done) | copy-start | bytes 6291460
  440.3 1.7 copy-start.42
  446.9 1.6 copy-start.44
  450.1 1.6 copy-start.38
  (11 other events, 16.7 us)
Sparse Core Ops, SparseCore 0:
  105.1 23.4 all-gather.30
  150.3 23.2 all-gather.28
  195.8 23.2 all-gather.26
  241.3 23.2 all-gather.24
  286.8 23.2 all-gather.22
  332.5 23.2 all-gather.20
  378.0 23.2 all-gather.18
  423.5 23.2 all-gather.16

commit v2 on v1

v2 whole, which is shorter than its diff:
```python
import functools

import jax
import jax.numpy as jnp
import ml_dtypes
import numpy as np
from jax import lax
from jax.experimental import pallas as pl
from jax.experimental.pallas import tpu as pltpu
from jax.sharding import PartitionSpec as P

NS_ITERS = 5
SMALL_ROWS = 16
LARGE_ROWS = 32
GRAM_ROWS = 4
POLAR_ROWS = 8
HIGHEST = lax.Precision.HIGHEST
F32 = jnp.float32
BF16 = jnp.bfloat16
VMEM_LIMIT = 60 << 20
BYTES_PER_US = 3690000

ANY = pl.BlockSpec(memory_space=pl.ANY)
SMEM = pl.BlockSpec(memory_space=pltpu.SMEM)


def kernel_params():
    return pltpu.CompilerParams(vmem_limit_bytes=VMEM_LIMIT)


def cost(micros):
    return pl.CostEstimate(flops=0, bytes_accessed=int(micros * BYTES_PER_US), transcendentals=0)


def dot_nt(a, b, precision=None):
    return lax.dot_general(
        a, b, (((1,), (1,)), ((), ())), precision=precision, preferred_element_type=F32
    )


def dot_nn(a, b, precision=None):
    return lax.dot_general(
        a, b, (((1,), (0,)), ((), ())), precision=precision, preferred_element_type=F32
    )


def iota(shape, dim):
    return lax.broadcasted_iota(jnp.int32, shape, dim)


def make_tables(side_len):
    indices = np.arange(side_len, dtype=np.int64)
    phases = (np.outer(indices, indices) % side_len).astype(np.float32) * np.float32(
        2.0 * 3.141592653589793 / side_len
    )
    unit_scale = np.float32(float(side_len) ** (-0.5))
    cosine = (np.cos(phases) * unit_scale).astype(ml_dtypes.bfloat16)
    sine_table = (np.sin(phases) * unit_scale).astype(ml_dtypes.bfloat16)
    return cosine, sine_table


def chunk_rows(own_rows):
    large = [(first, LARGE_ROWS) for first in range(2 * SMALL_ROWS, own_rows - LARGE_ROWS + 1, LARGE_ROWS)]
    covered = 2 * SMALL_ROWS + LARGE_ROWS * len(large)
    rest = [(first, SMALL_ROWS) for first in range(covered, own_rows, SMALL_ROWS)]
    return [(0, SMALL_ROWS)] + large + rest + [(SMALL_ROWS, SMALL_ROWS)]


def first_body(strips, strip_ref, table_ref, grid_ref, after_ref, *out_refs):
    _, chans, rows, width = out_refs[0].shape
    side_len = table_ref.shape[-1]
    cosine = jnp.concatenate([table_ref[strip_ref[0] ^ k, 0] for k in range(strips)], axis=0)
    sine_table = jnp.concatenate([table_ref[strip_ref[0] ^ k, 1] for k in range(strips)], axis=0)
    total = dot_nt(jnp.concatenate([cosine, sine_table], axis=0), grid_ref[0].reshape(chans * width, side_len))
    total = total + dot_nt(
        jnp.concatenate([-sine_table, cosine], axis=0), grid_ref[1].reshape(chans * width, side_len)
    )
    total = total.astype(BF16)
    for part in range(2):
        for k in range(strips):
            first = (part * strips + k) * rows
            for chan in range(chans):
                out_refs[k][part, chan] = total[first : first + rows, chan * width : (chan + 1) * width]


def first_transform(strip, tables, grid, after):
    strips, _, rows, side_len = tables.shape
    _, chans, width, _ = grid.shape
    if width % 128 or rows % 16:
        order = strip[0] ^ jnp.arange(strips, dtype=jnp.int32)
        cosine = jnp.take(tables[:, 0], order, axis=0)
        sine_table = jnp.take(tables[:, 1], order, axis=0)

        def product(table, part):
            return jnp.einsum("kmv,cuv->kcmu", table, part, preferred_element_type=F32)

        real = product(cosine, grid[0]) - product(sine_table, grid[1])
        imag = product(sine_table, grid[0]) + product(cosine, grid[1])
        both = jnp.stack([real, imag], axis=1).astype(BF16)
        return [both[k] for k in range(strips)]
    block = 4 if chans % 4 == 0 else 1
    return pl.pallas_call(
        functools.partial(first_body, strips),
        grid=(chans // block,),
        in_specs=[
            SMEM,
            pl.BlockSpec(tables.shape, lambda i: (0, 0, 0, 0)),
            pl.BlockSpec((2, block, width, side_len), lambda i: (0, i, 0, 0)),
            ANY,
        ],
        out_specs=[pl.BlockSpec((2, block, rows, width), lambda i: (0, i, 0, 0))] * strips,
        out_shape=[jax.ShapeDtypeStruct((2, chans, rows, width), BF16)] * strips,
        compiler_params=kernel_params(),
        cost_estimate=cost(4 + rows // 6),
        name="first_transform",
    )(strip, tables, grid, after)


def band_matrix(taps_of, levels, taps, own_rows, reach, first_row, image_rows):
    half_taps = taps // 2
    shape = (own_rows, own_rows + 2 * reach)
    row = iota(shape, 0)
    column = iota(shape, 1)
    place = jnp.where(
        column < own_rows, column, jnp.where(column < own_rows + reach, column - own_rows - reach, column - reach)
    )
    total = jnp.zeros(shape, F32)
    for level in range(levels):
        dilation = 2**level
        for outer in range(taps):
            detail_row = row - (outer - half_taps) * dilation
            inside = (detail_row + first_row >= 0) & (detail_row + first_row < image_rows)
            for inner in range(taps):
                hit = inside & (place == detail_row + (inner - half_taps) * dilation)
                total = total + jnp.where(hit, taps_of(level, outer) * taps_of(level, inner), 0.0)
    return total


def base_body(levels, taps, reach, strips, strip_ref, step_ref, highpass_ref, model_ref, edge_ref, after_ref, out_ref, high, low):
    block, own_rows, side_len = model_ref.shape

    @pl.when(pl.program_id(0) == 0)
    def _():
        band = band_matrix(
            lambda level, tap: highpass_ref[level, tap],
            levels,
            taps,
            own_rows,
            reach,
            strip_ref[0] * own_rows,
            strips * own_rows,
        )
        top = band.astype(BF16)
        high[...] = top
        low[...] = (band - top.astype(F32)).astype(BF16)

    first = pl.program_id(0) * block
    for chan in range(block):
        model = model_ref[chan]
        top = model.astype(BF16)
        rest = (model - top.astype(F32)).astype(BF16)
        edge = edge_ref[chan].astype(F32)
        whole = jnp.concatenate([top.astype(F32), edge], axis=0).astype(BF16)
        gradient = dot_nn(high[...], whole)
        gradient = gradient + dot_nn(low[...], whole)
        gradient = gradient + dot_nn(high[:, :own_rows], rest)
        out_ref[chan] = model - step_ref[first + chan] * gradient


def base_step(strip, strips, step_size, highpass, model_image, edges, after):
    chans, rows, side_len = model_image.shape
    levels, taps = highpass.shape
    reach = edges.shape[1] // 2
    block = 2 if chans % 2 == 0 else 1
    wide = rows + 2 * reach
    return pl.pallas_call(
        functools.partial(base_body, levels, taps, reach, strips),
        grid=(chans // block,),
        in_specs=[
            SMEM,
            SMEM,
            SMEM,
            pl.BlockSpec((block, rows, side_len), lambda i: (i, 0, 0)),
            pl.BlockSpec((block, 2 * reach, side_len), lambda i: (i, 0, 0)),
            ANY,
        ],
        out_specs=pl.BlockSpec((block, rows, side_len), lambda i: (i, 0, 0)),
        out_shape=jax.ShapeDtypeStruct(model_image.shape, F32),
        scratch_shapes=[pltpu.VMEM((rows, wide), BF16), pltpu.VMEM((rows, wide), BF16)],
        compiler_params=kernel_params(),
        cost_estimate=cost(9),
        name="base_step",
    )(strip, step_size, highpass, model_image, edges, after)


def second_body(strips, strip_ref, step_ref, cosine_ref, sine_ref, base_ref, after_ref, *refs):
    halves = refs[:strips]
    moved_ref, pixels_ref = refs[strips:]
    _, chans, rows, width = halves[0].shape
    real = jnp.concatenate([half[0].reshape(chans * rows, width) for half in halves], axis=1)
    imag = jnp.concatenate([half[1].reshape(chans * rows, width) for half in halves], axis=1)

    def ordered(table_ref):
        parts = [table_ref[pl.ds(pl.multiple_of((strip_ref[0] ^ k) * width, width), width), :] for k in range(strips)]
        return jnp.concatenate(parts, axis=0)

    dirty = dot_nn(real, ordered(cosine_ref)) - dot_nn(imag, ordered(sine_ref))
    pieces = []
    for chan in range(chans):
        moved = base_ref[chan] + step_ref[chan] * dirty[chan * rows : (chan + 1) * rows]
        moved_ref[chan] = moved
        pieces.append(moved)
    pixels_ref[...] = jnp.swapaxes(jnp.stack(pieces), 0, 1).astype(BF16)


def second_transform(strip, step_size, halves, cosine, sine_table, base, first_row, after):
    strips = len(halves)
    _, chans, rows, width = halves[0].shape
    side_len = cosine.shape[0]
    if width % 128 or rows % 16 or chans % 16:
        order = strip[0] ^ jnp.arange(strips, dtype=jnp.int32)
        both = jnp.stack(halves)

        def product(part, table):
            parts = jnp.take(table.reshape(strips, width, side_len), order, axis=0)
            return jnp.einsum("kcmu,kul->cml", part, parts, preferred_element_type=F32)

        dirty = product(both[:, 0], jnp.asarray(cosine)) - product(both[:, 1], jnp.asarray(sine_table))
        moved = base[:, first_row : first_row + rows] + step_size[:, None, None] * dirty
        pixels = moved.astype(BF16).transpose(1, 0, 2)
        return lax.dynamic_update_slice(base, moved, (0, first_row, 0)), pixels
    block = min(256, side_len)
    place = first_row // rows
    halves_spec = pl.BlockSpec(halves[0].shape, lambda i: (0, 0, 0, 0))
    return pl.pallas_call(
        functools.partial(second_body, strips),
        grid=(side_len // block,),
        in_specs=[
            SMEM,
            SMEM,
            pl.BlockSpec((side_len, block), lambda i: (0, i)),
            pl.BlockSpec((side_len, block), lambda i: (0, i)),
            pl.BlockSpec((chans, rows, block), lambda i: (0, place, i)),
            ANY,
        ]
        + [halves_spec] * strips,
        out_specs=[
            pl.BlockSpec((chans, rows, block), lambda i: (0, place, i)),
            pl.BlockSpec((rows, chans, block), lambda i: (0, 0, i)),
        ],
        out_shape=[
            jax.ShapeDtypeStruct(base.shape, F32),
            jax.ShapeDtypeStruct((rows, chans, side_len), BF16),
        ],
        input_output_aliases={4: 0},
        compiler_params=kernel_params(),
        cost_estimate=cost(2 + rows // 10),
        name="second_transform",
    )(strip, step_size, cosine, sine_table, base, after, *halves)


def stacked(group_refs, first, count):
    return jnp.concatenate([ref[first + i] for i in range(count) for ref in group_refs], axis=0)


def gram_body(groups, before_ref, after_ref, *refs):
    total_ref = refs[groups]

    @pl.when(pl.program_id(0) == 0)
    def _():
        total_ref[...] = before_ref[...]

    pixels = stacked(refs[:groups], 0, GRAM_ROWS)
    total_ref[...] += dot_nt(pixels, pixels)


def gram_step(groups, before, after):
    rows, chans, side_len = groups[0].shape
    spec = pl.BlockSpec((GRAM_ROWS, chans, side_len), lambda i: (i, 0, 0))
    return pl.pallas_call(
        functools.partial(gram_body, len(groups)),
        grid=(rows // GRAM_ROWS,),
        in_specs=[pl.BlockSpec(before.shape, lambda i: (0, 0)), ANY] + [spec] * len(groups),
        out_specs=pl.BlockSpec(before.shape, lambda i: (0, 0)),
        out_shape=jax.ShapeDtypeStruct(before.shape, F32),
        compiler_params=kernel_params(),
        cost_estimate=cost(1 + rows // 16),
        name="gram_step",
    )(before, after, *groups)


def newton_schulz(gram):
    size = gram.shape[0]
    frob_norm = jnp.sqrt(jnp.sum(gram * gram))
    identity = (iota((size, size), 0) == iota((size, size), 1)).astype(F32)
    current = gram / frob_norm
    inverse = identity
    for iteration in range(NS_ITERS):
        middle = 0.5 * (3.0 * identity - dot_nn(inverse, current, HIGHEST))
        if iteration + 1 < NS_ITERS:
            current = dot_nn(current, middle, HIGHEST)
        inverse = dot_nn(middle, inverse, HIGHEST)
    return inverse, frob_norm


def polar_body(starts, sizes, groups, shrink_ref, gram_ref, moved_hbm, *refs):
    chunks = len(sizes)
    pixels_hbm = refs[: chunks * groups]
    out_hbm, moved, in_sems, moved_sems, out_sems = refs[chunks * groups : chunks * groups + 5]
    pixels = refs[chunks * groups + 5 :]
    own, all_rows, side_len = moved.shape
    size = pixels[0].shape[2] * groups
    moved_copies = []
    pixel_copies = []
    for chunk in range(chunks):
        copies = []
        for group in range(groups):
            place = chunk * groups + group
            copy = pltpu.make_async_copy(pixels_hbm[place], pixels[chunk].at[group], in_sems.at[place])
            copy.start()
            copies.append(copy)
        pixel_copies.append(copies)
        part = pl.ds(starts[chunk], sizes[chunk])
        copy = pltpu.make_async_copy(moved_hbm.at[:, part], moved.at[:, part], moved_sems.at[chunk])
        copy.start()
        moved_copies.append(copy)
    gram = jnp.zeros((size, size), F32)
    for i in range(GRAM_ROWS):
        gram = gram + gram_ref[i * size : (i + 1) * size, i * size : (i + 1) * size]
    inverse, frob_norm = newton_schulz(gram)
    factor = shrink_ref[0] * jnp.sqrt(all_rows * side_len / frob_norm)
    select = (iota((own, size), 0) == iota((own, size), 1)).astype(F32)
    weights = dot_nt(select, inverse, HIGHEST) * factor
    spread = POLAR_ROWS * own
    wide = POLAR_ROWS * size
    repeat = (iota((spread, own), 0) // POLAR_ROWS == iota((spread, own), 1)).astype(BF16)
    weights = dot_nn(repeat, weights.astype(BF16)).astype(BF16)
    repeat = (iota((size, wide), 1) % size == iota((size, wide), 0)).astype(BF16)
    weights = dot_nn(weights, repeat)
    keep = iota((spread, wide), 0) % POLAR_ROWS == iota((spread, wide), 1) // size
    weights = jnp.where(keep, weights, 0.0).astype(BF16)
    out_copies = []
    for chunk in range(chunks):
        for copy in pixel_copies[chunk]:
            copy.wait()
        moved_copies[chunk].wait()
        for step in range(sizes[chunk] // POLAR_ROWS):
            data = stacked([pixels[chunk].at[group] for group in range(groups)], step * POLAR_ROWS, POLAR_ROWS)
            polar = dot_nn(weights, data).reshape(own, POLAR_ROWS, side_len)
            first = starts[chunk] + step * POLAR_ROWS
            moved[:, first : first + POLAR_ROWS] -= polar
        part = pl.ds(starts[chunk], sizes[chunk])
        copy = pltpu.make_async_copy(moved.at[:, part], out_hbm.at[:, part], out_sems.at[chunk])
        copy.start()
        out_copies.append(copy)
    for copy in out_copies:
        copy.wait()


def polar_step(shrinkage, gram, moved, gathered, starts):
    chunks = len(gathered)
    groups = len(gathered[0])
    sizes = [pieces[0].shape[0] for pieces in gathered]
    flat = [piece for pieces in gathered for piece in pieces]
    return pl.pallas_call(
        functools.partial(polar_body, starts, sizes, groups),
        in_specs=[SMEM, pl.BlockSpec(memory_space=pltpu.VMEM), ANY] + [ANY] * len(flat),
        out_specs=ANY,
        out_shape=jax.ShapeDtypeStruct(moved.shape, F32),
        scratch_shapes=[
            pltpu.VMEM(moved.shape, F32),
            pltpu.SemaphoreType.DMA((chunks * groups,)),
            pltpu.SemaphoreType.DMA((chunks,)),
            pltpu.SemaphoreType.DMA((chunks,)),
        ]
        + [pltpu.VMEM((groups,) + pieces[0].shape, BF16) for pieces in gathered],
        compiler_params=kernel_params(),
        cost_estimate=cost(11),
        name="polar_step",
    )(shrinkage, gram, moved, *flat)


def swap(value, axis, bits):
    count = lax.axis_size(axis)
    return lax.ppermute(value, axis, [(i, i ^ bits) for i in range(count)])


def neighbour_rows(model_image, reach):
    ends = lax.axis_size("strip") - 1
    head = model_image[:, :reach].astype(BF16)
    tail = model_image[:, model_image.shape[1] - reach :].astype(BF16)
    before = lax.ppermute(tail, "strip", [(i, i + 1) for i in range(ends)])
    after = lax.ppermute(head, "strip", [(i + 1, i) for i in range(ends)])
    return jnp.concatenate([before, after], axis=1)


def exchange(pieces):
    order = sorted(range(1, len(pieces)), reverse=True)
    arrived = {k: swap(pieces[k], "strip", k) for k in order}
    return [pieces[0]] + [arrived[k] for k in range(1, len(pieces))]


def gather_channels(pixels):
    devices = lax.axis_size("chan")
    far = [swap(pixels, "chan", bits) for bits in range(2, devices, 2)]
    kept = [pixels] + far
    if devices == 1:
        return kept
    return kept + [swap(piece, "chan", 1) for piece in kept]


def local(grid, model_image, step_size, highpass, shrinkage):
    chans, own_rows, side_len = model_image.shape
    strips = lax.axis_size("strip")
    size = chans * lax.axis_size("chan")
    starts, sizes = zip(*chunk_rows(own_rows))
    chunks = len(sizes)
    strip = lax.axis_index("strip").astype(jnp.int32).reshape(1)

    cosine, sine_table = make_tables(side_len)
    split = np.stack([cosine.reshape(strips, own_rows, side_len), sine_table.reshape(strips, own_rows, side_len)], axis=1)
    tables = [np.ascontiguousarray(split[:, :, start : start + rows]) for start, rows in zip(starts, sizes)]

    levels, taps = highpass.shape
    reach = (taps - 1) * 2 ** (levels - 1)
    edges = neighbour_rows(model_image, reach)

    ahead = 2
    halves = {}
    moved = None
    gathered = []
    gram = jnp.zeros((GRAM_ROWS * size, GRAM_ROWS * size), F32)
    last = strip
    for chunk in range(chunks + ahead):
        if chunk < chunks:
            pieces = first_transform(strip, tables[chunk], grid, last)
            last = pieces[0]
            halves[chunk] = exchange(pieces)
        if chunk == ahead - 1:
            moved = base_step(strip, strips, step_size, highpass, model_image, edges, last)
            last = moved
        if chunk >= ahead:
            done = chunk - ahead
            moved, pixels = second_transform(
                strip, step_size, halves[done], cosine, sine_table, moved, starts[done], last
            )
            last = pixels
            groups = gather_channels(pixels)
            if chans % 16:
                groups = [jnp.concatenate(groups, axis=1)]
            gathered.append(groups)
            if done > 0:
                gram = gram_step(gathered[done - 1], gram, last)
                last = gram
    gram = gram_step(gathered[-1], gram, last)
    return polar_step(shrinkage, gram, moved, gathered, starts)


def solution(mesh):
    return jax.shard_map(
        local,
        mesh=mesh,
        in_specs=(
            P(None, "chan", "strip", None),
            P("chan", "strip", None),
            P("chan"),
            P(),
            P("strip"),
        ),
        out_specs=P("chan", "strip", None),
        check_vma=False,
    )
```

time: 475 us -> 331 us (0.70)
  blocking collectives: 200 us -> 0 us
  waiting for transfers between devices: 0.29 us -> 121 us
  local copies, waits for them, and re-layouts: 84 us -> 6.7 us
  starting transfers between devices: 12.5 us -> 67.7 us
  between operations: 51.9 us -> 1.32 us
  Pallas kernels: 116 us -> 126 us
    all_to_all x7 -> x0, blocking collectives: 200 us -> none  [local(): lax.all_to_all(sent, 'strip', split_axis=0, concat_axis=0, tiled=True)]
    ppermute x0 -> x50, waiting for transfers between devices: none -> 121 us  [swap(): return lax.ppermute(value, axis, [(i, i ^ bits) for i in range(count)])]
    unnamed x96 -> x92, local copies, waits for them, and re-layouts: 82.9 us -> 5.79 us
    ppermute x0 -> x50, starting transfers between devices: none -> 61.4 us  [swap(): return lax.ppermute(value, axis, [(i, i ^ bits) for i in range(count)])]
    pallas_call x26 -> x17, Pallas kernels: 116 us -> 126 us  [the longest x5 38.6 us: first_transform(): pl.pallas_call(functools.partial(first_body, strips), grid=(chans // bloc...]
    all_to_all x1 -> x0, starting transfers between devices: 6.22 us -> none  [local(): lax.all_to_all(sent, 'strip', split_axis=0, concat_axis=0, tiled=True)]
  transfers between devices with their start and end apart: 11 -> 52, of which waited for: 0 -> 24; matrix products, arithmetic and copies ran while one was open for 1% -> 2% of each run, Pallas kernels for 20% -> 31%
where the time goes in v2:
time: 331 us; the launch traced here: 328 us
  Pallas kernels  126 us (38%)
  waiting for transfers between devices  121 us (37%)
  starting transfers between devices  67.7 us (20%)
  local copies, waits for them, and re-layouts  6.7 us (2%)
  other arithmetic  5.15 us (2%)
    ppermute x50, waiting for transfers between devices, swap(): return lax.ppermute(value, axis, [(i, i ^ bits) for i in range(count)])  121 us
    ppermute x50, starting transfers between devices, swap(): return lax.ppermute(value, axis, [(i, i ^ bits) for i in range(count)])  61.4 us
    pallas_call x5, Pallas kernels, first_transform(): pl.pallas_call(functools.partial(first_body, strips), grid=(chans // bloc...  38.6 us
    pallas_call x5, Pallas kernels, second_transform(): pl.pallas_call(functools.partial(second_body, strips), grid=(side_len //...  32.4 us
    pallas_call x5, Pallas kernels, gram_step(): pl.pallas_call(functools.partial(gram_body, len(groups)), grid=(rows // G...  29.3 us
    pallas_call x1, Pallas kernels, polar_step(): pl.pallas_call(functools.partial(polar_body, starts, sizes, groups), in_s...  14.5 us
    pallas_call x1, Pallas kernels, base_step(): pl.pallas_call(functools.partial(base_body, levels, taps, reach, strips),...  11.3 us
  transfers between devices with their start and end apart: 52, of which 24 were waited for; matrix products, arithmetic and copies ran while one was open for 2% of the time, Pallas kernels for 31%

profile of v2, /device:TPU:12, one launch (start us, length us, event | category | flops | bytes accessed | tf_op | source)
XLA Modules:
  0.0 327.9 jit_solution(16987260452479492871)
XLA Ops:
  0.0 6.5 %first_transform.5 = (bf16[2,16,16,128]{3,2,1,0:T(8,128)(2,1)}, bf16[2,16,16,128]{3,2,1,0:T(8,128)(2,1)}, bf16[2,16,16,128]{3,2,1,0:T(8,128)(2,1)}, bf16[2,16,16...) custom-call(s32[1]{0:T(128)} %bitcast.strip_ref.after_ref, ...), custom_call_target="tpu_custom_call" | custom-call | bytes 22140000 | tf_op jit(solution)/shard_map/first_transform/pallas_call | solution.py:102
  7.1 3.0 collective-permute-start.4
  10.1 2.6 collective-permute-start.5
  13.0 4.0 %convert.4 = bf16[16,128,1024]{2,1,0:T(8,128)(2,1)S(1)} convert(f32[16,128,1024]{2,1,0:T(8,128)} %model_ref.1) | non-fusion elementwise | flops 2097152 | bytes 12582912 | tf_op jit(solution)/shard_map/convert.1
  17.2 4.4 %collective-permute-start = (bf16[16,12,1024]{2,1,0:T(8,128)(2,1)S(1)}, bf16[16,12,1024]{2,1,0:T(8,128)(2,1)S(1)}, u32[]{:S(2)}, u32[]{:S(2)}) collective-permute-start(bf16[16,12,1024]{2,1,0:T(8,128)(2,1)S(1)} %get-tuple-element.105), channel_id=1, source_target_pairs={{0,4},{4,8},{8,12},{12,16},{16,20},{20,24},{24,28},{1,5},{5,9},{9,... | collective-permute-start | bytes 1179656 | tf_op jit(solution)/shard_map/ppermute | solution.py:392
  25.3 8.4 %first_transform.6 = (bf16[2,16,32,128]{3,2,1,0:T(8,128)(2,1)}, bf16[2,16,32,128]{3,2,1,0:T(8,128)(2,1)}, bf16[2,16,32,128]{3,2,1,0:T(8,128)(2,1)}, bf16[2,16,32...) custom-call(s32[1]{0:T(128)} %bitcast.strip_ref.after_ref, ...), custom_call_target="tpu_custom_call" | custom-call | bytes 33210000 | tf_op jit(solution)/shard_map/first_transform/pallas_call | solution.py:102
  35.7 2.5 collective-permute-start.10
  38.2 4.5 %collective-permute-done.7.refs_6_ = bf16[2,16,16,128]{3,2,1,0:T(8,128)(2,1)S(1)} collective-permute-done((bf16[2,16,16,128]{3,2,1,0:T(8,128)(2,1)S(1)}, bf16[2,16,16,128]{3,2,1,0:T(8,128)(2,1)S(1)}, u32[]{:S(2)}, u32[]{:S(2)}) %collective-permute-start.7) | collective-permute-done | bytes 131104 | tf_op jit(solution)/shard_map/ppermute | solution.py:385
  42.8 7.4 %collective-permute-done.8.refs_7_ = bf16[2,16,16,128]{3,2,1,0:T(8,128)(2,1)S(1)} collective-permute-done((bf16[2,16,16,128]{3,2,1,0:T(8,128)(2,1)S(1)}, bf16[2,16,16,128]{3,2,1,0:T(8,128)(2,1)S(1)}, u32[]{:S(2)}, u32[]{:S(2)}) %collective-permute-start.8) | collective-permute-done | bytes 131104 | tf_op jit(solution)/shard_map/ppermute | solution.py:385
  50.8 3.2 collective-permute-start.11
  54.0 3.4 %collective-permute-done.9.refs_1_ = bf16[2,16,32,128]{3,2,1,0:T(8,128)(2,1)S(1)} collective-permute-done((bf16[2,16,32,128]{3,2,1,0:T(8,128)(2,1)}, bf16[2,16,32,128]{3,2,1,0:T(8,128)(2,1)S(1)}, u32[]{:S(2)}, u32[]{:S(2)}) %collective-permute-start.9) | collective-permute-done | bytes 262176 | tf_op jit(solution)/shard_map/ppermute | solution.py:385
  57.4 4.6 %collective-permute-start.12 = (bf16[2,16,32,128]{3,2,1,0:T(8,128)(2,1)}, bf16[2,16,32,128]{3,2,1,0:T(8,128)(2,1)S(1)}, u32[]{:S(2)}, u32[]{:S(2)}) collective-permute-start(bf16[2,16,32,128]{3,2,1,0:T(8,128)(2,1)} %get-tuple-element.71), channel_id=1, source_target_pairs={{0,16},{4,20},{8,24},{12,28},{16,0},{20,4},{24,8},{28,12},{1,17},{... | collective-permute-start | bytes 786440 | tf_op jit(solution)/shard_map/ppermute | solution.py:385
  67.1 11.3 %base_step.1.after_ref.base_ref = f32[16,128,1024]{2,1,0:T(8,128)} custom-call(s32[1]{0:T(128)} %bitcast.strip_ref.after_ref, f32[16]{0:T(128)} %step_ref.11, f32[3,4]{1,0:T(4,128)} %highpass_ref.1, f32[16,128,1024]{2,1,0:T(8,128)} %model_ref.1, bf16[16,24,1024]{2,1,0:T(8,128)(2,1)} %pad_maximum_fusion.edge_ref, ...), custom_call_target="tpu_custom_call" | custom-call | bytes 33210000 | tf_op jit(solution)/shard_map/base_step/pallas_call | solution.py:176
  78.5 8.5 %first_transform.7 = (bf16[2,16,32,128]{3,2,1,0:T(8,128)(2,1)}, bf16[2,16,32,128]{3,2,1,0:T(8,128)(2,1)}, bf16[2,16,32,128]{3,2,1,0:T(8,128)(2,1)}, bf16[2,16,32...) custom-call(s32[1]{0:T(128)} %bitcast.strip_ref.after_ref, ...), custom_call_target="tpu_custom_call" | custom-call | bytes 33210000 | tf_op jit(solution)/shard_map/first_transform/pallas_call | solution.py:102
  87.0 5.5 %second_transform.5 = (f32[16,128,1024]{2,1,0:T(8,128)}, bf16[16,16,1024]{2,1,0:T(8,128)(2,1)}) custom-call(s32[1]{0:T(128)} %bitcast.strip_ref.after_ref, f32[16]{0:T(128)} %step_ref.11, bf16[1024,1024]{1,0:T(8,128)(2,1)} %constant.25.clone.cosine_ref, bf16[1024,1024]{1,0:T(8,128)(2,1)} %constant.26.clone.sine_ref, ...), custom_call_target="tpu_custom_call", output_to_operand_aliasing={{0}: (4, {})} | custom-call | bytes 11070000 | tf_op jit(solution)/shard_map/second_transform/pallas_call | solution.py:235
  94.1 8.5 %first_transform.8 = (bf16[2,16,32,128]{3,2,1,0:T(8,128)(2,1)}, bf16[2,16,32,128]{3,2,1,0:T(8,128)(2,1)}, bf16[2,16,32,128]{3,2,1,0:T(8,128)(2,1)}, bf16[2,16,32...) custom-call(s32[1]{0:T(128)} %bitcast.strip_ref.after_ref, ...), custom_call_target="tpu_custom_call" | custom-call | bytes 33210000 | tf_op jit(solution)/shard_map/first_transform/pallas_call | solution.py:102
  102.7 4.1 %collective-permute-done.15.refs_7_ = bf16[2,16,32,128]{3,2,1,0:T(8,128)(2,1)S(1)} collective-permute-done((bf16[2,16,32,128]{3,2,1,0:T(8,128)(2,1)}, bf16[2,16,32,128]{3,2,1,0:T(8,128)(2,1)S(1)}, u32[]{:S(2)}, u32[]{:S(2)}) %collective-permute-start.15) | collective-permute-done | bytes 262176 | tf_op jit(solution)/shard_map/ppermute | solution.py:385
  107.5 7.1 %second_transform.6 = (f32[16,128,1024]{2,1,0:T(8,128)}, bf16[32,16,1024]{2,1,0:T(8,128)(2,1)}) custom-call(s32[1]{0:T(128)} %bitcast.strip_ref.after_ref, f32[16]{0:T(128)} %step_ref.11, bf16[1024,1024]{1,0:T(8,128)(2,1)} %constant.25.clone.cosine_ref, bf16[1024,1024]{1,0:T(8,128)(2,1)} %constant.26.clone.sine_ref, ...), custom_call_target="tpu_custom_call", output_to_operand_aliasing={{0}: (4, {})} | custom-call | bytes 18450000 | tf_op jit(solution)/shard_map/second_transform/pallas_call | solution.py:235
  117.5 5.8 %collective-permute-done.19.refs_1_ = bf16[2,16,32,128]{3,2,1,0:T(8,128)(2,1)S(1)} collective-permute-done((bf16[2,16,32,128]{3,2,1,0:T(8,128)(2,1)}, bf16[2,16,32,128]{3,2,1,0:T(8,128)(2,1)S(1)}, u32[]{:S(2)}, u32[]{:S(2)}) %collective-permute-start.19) | collective-permute-done | bytes 262176 | tf_op jit(solution)/shard_map/ppermute | solution.py:385
  124.6 3.5 %collective-permute-start.22 = (bf16[2,16,32,128]{3,2,1,0:T(8,128)(2,1)S(1)}, bf16[2,16,32,128]{3,2,1,0:T(8,128)(2,1)S(1)}, u32[]{:S(2)}, u32[]{:S(2)}) collective-permute-start(bf16[2,16,32,128]{3,2,1,0:T(8,128)(2,1)S(1)} %copy-done.38), channel_id=1, source_target_pairs={{0,16},{4,20},{8,24},{12,28},{16,0},{20,4},{24,8},{28,12},{1,17},{... | collective-permute-start | bytes 786440 | tf_op jit(solution)/shard_map/ppermute | solution.py:385
  128.2 6.1 %collective-permute-done.21.refs_3_ = bf16[2,16,32,128]{3,2,1,0:T(8,128)(2,1)S(1)} collective-permute-done((bf16[2,16,32,128]{3,2,1,0:T(8,128)(2,1)}, bf16[2,16,32,128]{3,2,1,0:T(8,128)(2,1)S(1)}, u32[]{:S(2)}, u32[]{:S(2)}) %collective-permute-start.21) | collective-permute-done | bytes 262176 | tf_op jit(solution)/shard_map/ppermute | solution.py:385
  134.2 4.3 %collective-permute-start.23 = (bf16[2,16,32,128]{3,2,1,0:T(8,128)(2,1)}, bf16[2,16,32,128]{3,2,1,0:T(8,128)(2,1)}, u32[]{:S(2)}, u32[]{:S(2)}) collective-permute-start(bf16[2,16,32,128]{3,2,1,0:T(8,128)(2,1)} %get-tuple-element.82), channel_id=1, source_target_pairs={{0,20},{4,16},{8,28},{12,24},{16,4},{20,0},{24,12},{28,8},{1,21},{... | collective-permute-start | bytes 786440 | tf_op jit(solution)/shard_map/ppermute | solution.py:385
  138.5 7.4 %collective-permute-done.22.refs_4_ = bf16[2,16,32,128]{3,2,1,0:T(8,128)(2,1)S(1)} collective-permute-done((bf16[2,16,32,128]{3,2,1,0:T(8,128)(2,1)S(1)}, bf16[2,16,32,128]{3,2,1,0:T(8,128)(2,1)S(1)}, u32[]{:S(2)}, u32[]{:S(2)}) %collective-permute-start.22) | collective-permute-done | bytes 262176 | tf_op jit(solution)/shard_map/ppermute | solution.py:385
  145.9 7.5 %collective-permute-start.25 = (bf16[2,16,32,128]{3,2,1,0:T(8,128)(2,1)}, bf16[2,16,32,128]{3,2,1,0:T(8,128)(2,1)S(1)}, u32[]{:S(2)}, u32[]{:S(2)}) collective-permute-start(bf16[2,16,32,128]{3,2,1,0:T(8,128)(2,1)} %get-tuple-element.84), channel_id=1, source_target_pairs={{0,28},{4,24},{8,20},{12,16},{16,12},{20,8},{24,4},{28,0},{1,29},{... | collective-permute-start | bytes 786440 | tf_op jit(solution)/shard_map/ppermute | solution.py:385
  154.1 4.2 %gram_step.5.after_ref.before_ref = f32[256,256]{1,0:T(8,128)} custom-call(f32[256,256]{1,0:T(8,128)} %broadcast_in_dim.3.before_ref, bf16[32,16,1024]{2,1,0:T(8,128)(2,1)} %get-tuple-element.75.after_ref.refs_0_.refs_4_, bf16[16,16,1024]{2,1,0:T(8,128)(2,1)} %get-tuple-element.66.after_ref.refs_0_, bf16[16,16,1024]{2,1,0:T(8,128)(2,1)} %copy-done.8, ...), custom_call_target="tpu_custom_call" | custom-call | bytes 7380000 | tf_op jit(solution)/shard_map/gram_step/pallas_call | solution.py:280
  158.3 6.6 %first_transform.9 = (bf16[2,16,16,128]{3,2,1,0:T(8,128)(2,1)}, bf16[2,16,16,128]{3,2,1,0:T(8,128)(2,1)}, bf16[2,16,16,128]{3,2,1,0:T(8,128)(2,1)}, bf16[2,16,16...) custom-call(s32[1]{0:T(128)} %bitcast.strip_ref.after_ref, ...), custom_call_target="tpu_custom_call" | custom-call | bytes 22140000 | tf_op jit(solution)/shard_map/first_transform/pallas_call | solution.py:102
  164.9 3.5 %collective-permute-done.24.refs_6_ = bf16[2,16,32,128]{3,2,1,0:T(8,128)(2,1)} collective-permute-done((bf16[2,16,32,128]{3,2,1,0:T(8,128)(2,1)}, bf16[2,16,32,128]{3,2,1,0:T(8,128)(2,1)}, u32[]{:S(2)}, u32[]{:S(2)}) %collective-permute-start.24) | collective-permute-done | bytes 262176 | tf_op jit(solution)/shard_map/ppermute | solution.py:385
  168.4 5.4 %collective-permute-done.25.refs_7_ = bf16[2,16,32,128]{3,2,1,0:T(8,128)(2,1)S(1)} collective-permute-done((bf16[2,16,32,128]{3,2,1,0:T(8,128)(2,1)}, bf16[2,16,32,128]{3,2,1,0:T(8,128)(2,1)S(1)}, u32[]{:S(2)}, u32[]{:S(2)}) %collective-permute-start.25) | collective-permute-done | bytes 262176 | tf_op jit(solution)/shard_map/ppermute | solution.py:385
  174.5 7.1 %second_transform.7 = (f32[16,128,1024]{2,1,0:T(8,128)}, bf16[32,16,1024]{2,1,0:T(8,128)(2,1)}) custom-call(s32[1]{0:T(128)} %bitcast.strip_ref.after_ref, f32[16]{0:T(128)} %step_ref.11, bf16[1024,1024]{1,0:T(8,128)(2,1)} %constant.25.clone.cosine_ref, bf16[1024,1024]{1,0:T(8,128)(2,1)} %constant.26.clone.sine_ref, ...), custom_call_target="tpu_custom_call", output_to_operand_aliasing={{0}: (4, {})} | custom-call | bytes 18450000 | tf_op jit(solution)/shard_map/second_transform/pallas_call | solution.py:235
  182.4 8.8 %collective-permute-done.29.refs_1_ = bf16[2,16,32,128]{3,2,1,0:T(8,128)(2,1)S(1)} collective-permute-done((bf16[2,16,32,128]{3,2,1,0:T(8,128)(2,1)}, bf16[2,16,32,128]{3,2,1,0:T(8,128)(2,1)S(1)}, u32[]{:S(2)}, u32[]{:S(2)}) %collective-permute-start.29) | collective-permute-done | bytes 262176 | tf_op jit(solution)/shard_map/ppermute | solution.py:385
  191.1 3.1 collective-permute-start.32
  194.3 8.4 %collective-permute-done.31.refs_3_ = bf16[2,16,32,128]{3,2,1,0:T(8,128)(2,1)S(1)} collective-permute-done((bf16[2,16,32,128]{3,2,1,0:T(8,128)(2,1)}, bf16[2,16,32,128]{3,2,1,0:T(8,128)(2,1)S(1)}, u32[]{:S(2)}, u32[]{:S(2)}) %collective-permute-start.31) | collective-permute-done | bytes 262176 | tf_op jit(solution)/shard_map/ppermute | solution.py:385
  202.7 2.5 collective-permute-start.33
  205.3 12.6 %collective-permute-done.32.refs_4_ = bf16[2,16,32,128]{3,2,1,0:T(8,128)(2,1)S(1)} collective-permute-done((bf16[2,16,32,128]{3,2,1,0:T(8,128)(2,1)}, bf16[2,16,32,128]{3,2,1,0:T(8,128)(2,1)S(1)}, u32[]{:S(2)}, u32[]{:S(2)}) %collective-permute-start.32) | collective-permute-done | bytes 262176 | tf_op jit(solution)/shard_map/ppermute | solution.py:385
  221.2 7.0 %gram_step.6.after_ref.before_ref = f32[256,256]{1,0:T(8,128)} custom-call(f32[256,256]{1,0:T(8,128)} %gram_step.5.after_ref.before_ref, bf16[32,16,1024]{2,1,0:T(8,128)(2,1)} %get-tuple-element.85.after_ref.refs_0_.refs_8_, bf16[32,16,1024]{2,1,0:T(8,128)(2,1)} %get-tuple-element.75.after_ref.refs_0_.refs_4_, bf16[32,16,1024]{2,1,0:T(8,128)(2,1)} %copy-done.4, ...), custom_call_target="tpu_custom_call" | custom-call | bytes 11070000 | tf_op jit(solution)/shard_map/gram_step/pallas_call | solution.py:280
  228.2 6.5 %collective-permute-done.34.refs_6_ = bf16[2,16,32,128]{3,2,1,0:T(8,128)(2,1)} collective-permute-done((bf16[2,16,32,128]{3,2,1,0:T(8,128)(2,1)}, bf16[2,16,32,128]{3,2,1,0:T(8,128)(2,1)}, u32[]{:S(2)}, u32[]{:S(2)}) %collective-permute-start.34) | collective-permute-done | bytes 262176 | tf_op jit(solution)/shard_map/ppermute | solution.py:385
  234.7 6.1 %collective-permute-done.35.refs_7_ = bf16[2,16,32,128]{3,2,1,0:T(8,128)(2,1)} collective-permute-done((bf16[2,16,32,128]{3,2,1,0:T(8,128)(2,1)}, bf16[2,16,32,128]{3,2,1,0:T(8,128)(2,1)}, u32[]{:S(2)}, u32[]{:S(2)}) %collective-permute-start.35) | collective-permute-done | bytes 262176 | tf_op jit(solution)/shard_map/ppermute | solution.py:385
  240.8 7.1 %second_transform.8 = (f32[16,128,1024]{2,1,0:T(8,128)}, bf16[32,16,1024]{2,1,0:T(8,128)(2,1)}) custom-call(s32[1]{0:T(128)} %bitcast.strip_ref.after_ref, f32[16]{0:T(128)} %step_ref.11, bf16[1024,1024]{1,0:T(8,128)(2,1)} %constant.25.clone.cosine_ref, bf16[1024,1024]{1,0:T(8,128)(2,1)} %constant.26.clone.sine_ref, ...), custom_call_target="tpu_custom_call", output_to_operand_aliasing={{0}: (4, {})} | custom-call | bytes 18450000 | tf_op jit(solution)/shard_map/second_transform/pallas_call | solution.py:235
  250.0 4.5 %collective-permute-done.39.refs_1_ = bf16[2,16,16,128]{3,2,1,0:T(8,128)(2,1)S(1)} collective-permute-done((bf16[2,16,16,128]{3,2,1,0:T(8,128)(2,1)S(1)}, bf16[2,16,16,128]{3,2,1,0:T(8,128)(2,1)S(1)}, u32[]{:S(2)}, u32[]{:S(2)}) %collective-permute-start.39) | collective-permute-done | bytes 131104 | tf_op jit(solution)/shard_map/ppermute | solution.py:385
  254.9 2.7 collective-permute-start.42
  257.7 3.1 collective-permute-done.41.refs_3_
  264.1 7.0 %gram_step.7.after_ref.before_ref = f32[256,256]{1,0:T(8,128)} custom-call(f32[256,256]{1,0:T(8,128)} %gram_step.6.after_ref.before_ref, bf16[32,16,1024]{2,1,0:T(8,128)(2,1)} %get-tuple-element.94.after_ref.refs_0_.refs_12_, bf16[32,16,1024]{2,1,0:T(8,128)(2,1)} %get-tuple-element.85.after_ref.refs_0_.refs_8_, bf16[32,16,1024]{2,1,0:T(8,128)(2,1)} %copy-done.6, ...), custom_call_target="tpu_custom_call" | custom-call | bytes 11070000 | tf_op jit(solution)/shard_map/gram_step/pallas_call | solution.py:280
  274.2 3.9 %collective-permute-done.44.refs_6_ = bf16[2,16,16,128]{3,2,1,0:T(8,128)(2,1)} collective-permute-done((bf16[2,16,16,128]{3,2,1,0:T(8,128)(2,1)}, bf16[2,16,16,128]{3,2,1,0:T(8,128)(2,1)}, u32[]{:S(2)}, u32[]{:S(2)}) %collective-permute-start.44) | collective-permute-done | bytes 131104 | tf_op jit(solution)/shard_map/ppermute | solution.py:385
  280.9 5.6 %second_transform.9 = (f32[16,128,1024]{2,1,0:T(8,128)}, bf16[16,16,1024]{2,1,0:T(8,128)(2,1)}) custom-call(s32[1]{0:T(128)} %bitcast.strip_ref.after_ref, f32[16]{0:T(128)} %step_ref.11, bf16[1024,1024]{1,0:T(8,128)(2,1)} %constant.25.clone.cosine_ref, bf16[1024,1024]{1,0:T(8,128)(2,1)} %constant.26.clone.sine_ref, ...), custom_call_target="tpu_custom_call", output_to_operand_aliasing={{0}: (4, {})} | custom-call | bytes 11070000 | tf_op jit(solution)/shard_map/second_transform/pallas_call | solution.py:235
  287.1 12.3 %collective-permute-done.49.refs_1_.refs_17_ = bf16[16,16,1024]{2,1,0:T(8,128)(2,1)S(1)} collective-permute-done((bf16[16,16,1024]{2,1,0:T(8,128)(2,1)}, bf16[16,16,1024]{2,1,0:T(8,128)(2,1)S(1)}, u32[]{:S(2)}, u32[]{:S(2)}) %collective-permute-start.49) | collective-permute-done | bytes 524320 | tf_op jit(solution)/shard_map/ppermute | solution.py:385
  302.0 7.0 %gram_step.8.before_ref.after_ref = f32[256,256]{1,0:T(8,128)} custom-call(f32[256,256]{1,0:T(8,128)} %gram_step.7.after_ref.before_ref, bf16[16,16,1024]{2,1,0:T(8,128)(2,1)} %get-tuple-element.103.after_ref.refs_0_.refs_16_, bf16[32,16,1024]{2,1,0:T(8,128)(2,1)} %get-tuple-element.94.after_ref.refs_0_.refs_12_, bf16[32,16,1024]{2,1,0:T(8,128)(2,1)} %copy-done.1, ...), custom_call_target="tpu_custom_call" | custom-call | bytes 11070000 | tf_op jit(solution)/shard_map/gram_step/pallas_call | solution.py:280
  309.1 4.1 %gram_step.9.gram_ref = f32[256,256]{1,0:T(8,128)} custom-call(f32[256,256]{1,0:T(8,128)} %gram_step.8.before_ref.after_ref, f32[256,256]{1,0:T(8,128)} %gram_step.8.before_ref.after_ref, bf16[16,16,1024]{2,1,0:T(8,128)(2,1)} %get-tuple-element.103.after_ref.refs_0_.refs_16_, bf16[16,16,1024]{2,1,0:T(8,128)(2,1)} %copy-done.10, ...), custom_call_target="tpu_custom_call" | custom-call | bytes 7380000 | tf_op jit(solution)/shard_map/gram_step/pallas_call | solution.py:280
  313.2 14.5 %polar_step.1 = f32[16,128,1024]{2,1,0:T(8,128)} custom-call(f32[1]{0:T(128)S(6)} %copy.23.shrink_ref, f32[256,256]{1,0:T(8,128)} %gram_step.9.gram_ref, f32[16,128,1024]{2,1,0:T(8,128)} %get-tuple-element.104.moved_hbm, bf16[16,16,1024]{2,1,0:T(8,128)(2,1)} %get-tuple-element.66.after_ref.refs_0_, bf16[16,16,1024]{2,1,0:T(8,128)(2,1)} %copy-done.8, ...), custom_call_target="tpu_custom_call" | custom-call | bytes 40590000 | tf_op jit(solution)/shard_map/polar_step/pallas_call | solution.py:365
  (169 shorter events, 38.5 us)
Async XLA Ops:
  6.5 10.7 %collective-permute-start.2 = (bf16[2,16,16,128]{3,2,1,0:T(8,128)(2,1)}, bf16[2,16,16,128]{3,2,1,0:T(8,128)(2,1)S(1)}, u32[]{:S(2)}, u32[]{:S(2)}) collective-permute-start(bf16[2,16,16,128]{3,2,1,0:T(8,128)(2,1)} %get-tuple-element.58), channel_id=1, source_target_pairs={{0,4},{4,0},{8,12},{12,8},{16,20},{20,16},{24,28},{28,24},{1,5},{5... | collective-permute-start | bytes 393224 | tf_op jit(solution)/shard_map/ppermute | solution.py:385
  7.1 14.6 %collective-permute-start.3 = (bf16[2,16,16,128]{3,2,1,0:T(8,128)(2,1)}, bf16[2,16,16,128]{3,2,1,0:T(8,128)(2,1)S(1)}, u32[]{:S(2)}, u32[]{:S(2)}) collective-permute-start(bf16[2,16,16,128]{3,2,1,0:T(8,128)(2,1)} %get-tuple-element.59), channel_id=1, source_target_pairs={{0,8},{4,12},{8,0},{12,4},{16,24},{20,28},{24,16},{28,20},{1,9},{5... | collective-permute-start | bytes 393224 | tf_op jit(solution)/shard_map/ppermute | solution.py:385
  7.1 16.5 %collective-permute-start.4 = (bf16[2,16,16,128]{3,2,1,0:T(8,128)(2,1)}, bf16[2,16,16,128]{3,2,1,0:T(8,128)(2,1)S(1)}, u32[]{:S(2)}, u32[]{:S(2)}) collective-permute-start(bf16[2,16,16,128]{3,2,1,0:T(8,128)(2,1)} %get-tuple-element.60), channel_id=1, source_target_pairs={{0,12},{4,8},{8,4},{12,0},{16,28},{20,24},{24,20},{28,16},{1,13},{... | collective-permute-start | bytes 393224 | tf_op jit(solution)/shard_map/ppermute | solution.py:385
  10.1 23.7 %collective-permute-start.5 = (bf16[2,16,16,128]{3,2,1,0:T(8,128)(2,1)}, bf16[2,16,16,128]{3,2,1,0:T(8,128)(2,1)S(1)}, u32[]{:S(2)}, u32[]{:S(2)}) collective-permute-start(bf16[2,16,16,128]{3,2,1,0:T(8,128)(2,1)} %get-tuple-element.61), channel_id=1, source_target_pairs={{0,16},{4,20},{8,24},{12,28},{16,0},{20,4},{24,8},{28,12},{1,17},{... | collective-permute-start | bytes 393224 | tf_op jit(solution)/shard_map/ppermute | solution.py:385
  12.7 23.1 %collective-permute-start.6 = (bf16[2,16,16,128]{3,2,1,0:T(8,128)(2,1)}, bf16[2,16,16,128]{3,2,1,0:T(8,128)(2,1)S(1)}, u32[]{:S(2)}, u32[]{:S(2)}) collective-permute-start(bf16[2,16,16,128]{3,2,1,0:T(8,128)(2,1)} %get-tuple-element.62), channel_id=1, source_target_pairs={{0,20},{4,16},{8,28},{12,24},{16,4},{20,0},{24,12},{28,8},{1,21},{... | collective-permute-start | bytes 393224 | tf_op jit(solution)/shard_map/ppermute | solution.py:385
  17.2 46.7 %collective-permute-start = (bf16[16,12,1024]{2,1,0:T(8,128)(2,1)S(1)}, bf16[16,12,1024]{2,1,0:T(8,128)(2,1)S(1)}, u32[]{:S(2)}, u32[]{:S(2)}) collective-permute-start(bf16[16,12,1024]{2,1,0:T(8,128)(2,1)S(1)} %get-tuple-element.105), channel_id=1, source_target_pairs={{0,4},{4,8},{8,12},{12,16},{16,20},{20,24},{24,28},{1,5},{5,9},{9,... | collective-permute-start | bytes 1179656 | tf_op jit(solution)/shard_map/ppermute | solution.py:392
  21.7 43.2 %collective-permute-start.1 = (bf16[16,12,1024]{2,1,0:T(8,128)(2,1)S(1)}, bf16[16,12,1024]{2,1,0:T(8,128)(2,1)S(1)}, u32[]{:S(2)}, u32[]{:S(2)}) collective-permute-start(bf16[16,12,1024]{2,1,0:T(8,128)(2,1)S(1)} %get-tuple-element.106), channel_id=1, source_target_pairs={{4,0},{8,4},{12,8},{16,12},{20,16},{24,20},{28,24},{5,1},{9,5},{13... | collective-permute-start | bytes 1179656 | tf_op jit(solution)/shard_map/ppermute | solution.py:393
  23.7 19.1 %collective-permute-start.7 = (bf16[2,16,16,128]{3,2,1,0:T(8,128)(2,1)S(1)}, bf16[2,16,16,128]{3,2,1,0:T(8,128)(2,1)S(1)}, u32[]{:S(2)}, u32[]{:S(2)}) collective-permute-start(bf16[2,16,16,128]{3,2,1,0:T(8,128)(2,1)S(1)} %copy-done.45), channel_id=1, source_target_pairs={{0,24},{4,28},{8,16},{12,20},{16,8},{20,12},{24,0},{28,4},{1,25},{... | collective-permute-start | bytes 393224 | tf_op jit(solution)/shard_map/ppermute | solution.py:385
  33.8 23.7 %collective-permute-start.9 = (bf16[2,16,32,128]{3,2,1,0:T(8,128)(2,1)}, bf16[2,16,32,128]{3,2,1,0:T(8,128)(2,1)S(1)}, u32[]{:S(2)}, u32[]{:S(2)}) collective-permute-start(bf16[2,16,32,128]{3,2,1,0:T(8,128)(2,1)} %get-tuple-element.68), channel_id=1, source_target_pairs={{0,4},{4,0},{8,12},{12,8},{16,20},{20,16},{24,28},{28,24},{1,5},{5... | collective-permute-start | bytes 786440 | tf_op jit(solution)/shard_map/ppermute | solution.py:385
  35.7 26.3 %collective-permute-start.10 = (bf16[2,16,32,128]{3,2,1,0:T(8,128)(2,1)}, bf16[2,16,32,128]{3,2,1,0:T(8,128)(2,1)S(1)}, u32[]{:S(2)}, u32[]{:S(2)}) collective-permute-start(bf16[2,16,32,128]{3,2,1,0:T(8,128)(2,1)} %get-tuple-element.69), channel_id=1, source_target_pairs={{0,8},{4,12},{8,0},{12,4},{16,24},{20,28},{24,16},{28,20},{1,9},{5... | collective-permute-start | bytes 786440 | tf_op jit(solution)/shard_map/ppermute | solution.py:385
  42.8 7.4 %collective-permute-start.8 = (bf16[2,16,16,128]{3,2,1,0:T(8,128)(2,1)S(1)}, bf16[2,16,16,128]{3,2,1,0:T(8,128)(2,1)S(1)}, u32[]{:S(2)}, u32[]{:S(2)}) collective-permute-start(bf16[2,16,16,128]{3,2,1,0:T(8,128)(2,1)S(1)} %copy-done.44), channel_id=1, source_target_pairs={{0,28},{4,24},{8,20},{12,16},{16,12},{20,8},{24,4},{28,0},{1,29},{... | collective-permute-start | bytes 393224 | tf_op jit(solution)/shard_map/ppermute | solution.py:385
  50.8 41.8 %collective-permute-start.11 = (bf16[2,16,32,128]{3,2,1,0:T(8,128)(2,1)}, bf16[2,16,32,128]{3,2,1,0:T(8,128)(2,1)S(1)}, u32[]{:S(2)}, u32[]{:S(2)}) collective-permute-start(bf16[2,16,32,128]{3,2,1,0:T(8,128)(2,1)} %get-tuple-element.70), channel_id=1, source_target_pairs={{0,12},{4,8},{8,4},{12,0},{16,28},{20,24},{24,20},{28,16},{1,13},{... | collective-permute-start | bytes 786440 | tf_op jit(solution)/shard_map/ppermute | solution.py:385
  57.4 45.2 %collective-permute-start.12 = (bf16[2,16,32,128]{3,2,1,0:T(8,128)(2,1)}, bf16[2,16,32,128]{3,2,1,0:T(8,128)(2,1)S(1)}, u32[]{:S(2)}, u32[]{:S(2)}) collective-permute-start(bf16[2,16,32,128]{3,2,1,0:T(8,128)(2,1)} %get-tuple-element.71), channel_id=1, source_target_pairs={{0,16},{4,20},{8,24},{12,28},{16,0},{20,4},{24,8},{28,12},{1,17},{... | collective-permute-start | bytes 786440 | tf_op jit(solution)/shard_map/ppermute | solution.py:385
  62.1 40.6 %collective-permute-start.13 = (bf16[2,16,32,128]{3,2,1,0:T(8,128)(2,1)}, bf16[2,16,32,128]{3,2,1,0:T(8,128)(2,1)S(1)}, u32[]{:S(2)}, u32[]{:S(2)}) collective-permute-start(bf16[2,16,32,128]{3,2,1,0:T(8,128)(2,1)} %get-tuple-element.72), channel_id=1, source_target_pairs={{0,20},{4,16},{8,28},{12,24},{16,4},{20,0},{24,12},{28,8},{1,21},{... | collective-permute-start | bytes 786440 | tf_op jit(solution)/shard_map/ppermute | solution.py:385
  64.0 38.7 %collective-permute-start.14 = (bf16[2,16,32,128]{3,2,1,0:T(8,128)(2,1)}, bf16[2,16,32,128]{3,2,1,0:T(8,128)(2,1)S(1)}, u32[]{:S(2)}, u32[]{:S(2)}) collective-permute-start(bf16[2,16,32,128]{3,2,1,0:T(8,128)(2,1)} %get-tuple-element.73), channel_id=1, source_target_pairs={{0,24},{4,28},{8,16},{12,20},{16,8},{20,12},{24,0},{28,4},{1,25},{... | collective-permute-start | bytes 786440 | tf_op jit(solution)/shard_map/ppermute | solution.py:385
  64.9 41.9 %collective-permute-start.15 = (bf16[2,16,32,128]{3,2,1,0:T(8,128)(2,1)}, bf16[2,16,32,128]{3,2,1,0:T(8,128)(2,1)S(1)}, u32[]{:S(2)}, u32[]{:S(2)}) collective-permute-start(bf16[2,16,32,128]{3,2,1,0:T(8,128)(2,1)} %get-tuple-element.74), channel_id=1, source_target_pairs={{0,28},{4,24},{8,20},{12,16},{16,12},{20,8},{24,4},{28,0},{1,29},{... | collective-permute-start | bytes 786440 | tf_op jit(solution)/shard_map/ppermute | solution.py:385
  92.6 24.5 %collective-permute-start.16 = (bf16[16,16,1024]{2,1,0:T(8,128)(2,1)}, bf16[16,16,1024]{2,1,0:T(8,128)(2,1)S(1)}, u32[]{:S(2)}, u32[]{:S(2)}) collective-permute-start(bf16[16,16,1024]{2,1,0:T(8,128)(2,1)} %get-tuple-element.66.after_ref.refs_0_), channel_id=1, source_target_pairs={{0,2},{1,3},{2,0},{3,1},{4,6},{5,7},{6,4},{7,5},{8,10},{9,11},{10,... | collective-permute-start | bytes 1572872 | tf_op jit(solution)/shard_map/ppermute | solution.py:385
  114.6 67.6 %collective-permute-start.26 = (bf16[32,16,1024]{2,1,0:T(8,128)(2,1)}, bf16[32,16,1024]{2,1,0:T(8,128)(2,1)S(1)}, u32[]{:S(2)}, u32[]{:S(2)}) collective-permute-start(bf16[32,16,1024]{2,1,0:T(8,128)(2,1)} %get-tuple-element.75.after_ref.refs_0_.refs_4_), channel_id=1, source_target_pairs={{0,2},{1,3},{2,0},{3,1},{4,6},{5,7},{6,4},{7,5},{8,10},{9,11},{10,... | collective-permute-start | bytes 3145736 | tf_op jit(solution)/shard_map/ppermute | solution.py:385
  116.9 7.7 %collective-permute-start.20 = (bf16[2,16,32,128]{3,2,1,0:T(8,128)(2,1)S(1)}, bf16[2,16,32,128]{3,2,1,0:T(8,128)(2,1)S(1)}, u32[]{:S(2)}, u32[]{:S(2)}) collective-permute-start(bf16[2,16,32,128]{3,2,1,0:T(8,128)(2,1)S(1)} %copy-done.39), channel_id=1, source_target_pairs={{0,8},{4,12},{8,0},{12,4},{16,24},{20,28},{24,16},{28,20},{1,9},{5... | collective-permute-start | bytes 786440 | tf_op jit(solution)/shard_map/ppermute | solution.py:385
  117.0 28.9 %collective-permute-start.17 = (bf16[16,16,1024]{2,1,0:T(8,128)(2,1)S(1)}, bf16[16,16,1024]{2,1,0:T(8,128)(2,1)S(1)}, u32[]{:S(2)}, u32[]{:S(2)}) collective-permute-start(bf16[16,16,1024]{2,1,0:T(8,128)(2,1)S(1)} %copy-done), channel_id=1, source_target_pairs={{0,1},{1,0},{2,3},{3,2},{4,5},{5,4},{6,7},{7,6},{8,9},{9,8},{10,11... | collective-permute-start | bytes 1572872 | tf_op jit(solution)/shard_map/ppermute | solution.py:385
  117.1 36.3 %collective-permute-start.18 = (bf16[16,16,1024]{2,1,0:T(8,128)(2,1)S(1)}, bf16[16,16,1024]{2,1,0:T(8,128)(2,1)}, u32[]{:S(2)}, u32[]{:S(2)}) collective-permute-start(bf16[16,16,1024]{2,1,0:T(8,128)(2,1)S(1)} %collective-permute-done.16.refs_1_), channel_id=1, source_target_pairs={{0,1},{1,0},{2,3},{3,2},{4,5},{5,4},{6,7},{7,6},{8,9},{9,8},{10,11... | collective-permute-start | bytes 1572872 | tf_op jit(solution)/shard_map/ppermute | solution.py:385
  123.4 10.9 %collective-permute-start.21 = (bf16[2,16,32,128]{3,2,1,0:T(8,128)(2,1)}, bf16[2,16,32,128]{3,2,1,0:T(8,128)(2,1)S(1)}, u32[]{:S(2)}, u32[]{:S(2)}) collective-permute-start(bf16[2,16,32,128]{3,2,1,0:T(8,128)(2,1)} %get-tuple-element.80), channel_id=1, source_target_pairs={{0,12},{4,8},{8,4},{12,0},{16,28},{20,24},{24,20},{28,16},{1,13},{... | collective-permute-start | bytes 786440 | tf_op jit(solution)/shard_map/ppermute | solution.py:385
  124.6 21.2 %collective-permute-start.22 = (bf16[2,16,32,128]{3,2,1,0:T(8,128)(2,1)S(1)}, bf16[2,16,32,128]{3,2,1,0:T(8,128)(2,1)S(1)}, u32[]{:S(2)}, u32[]{:S(2)}) collective-permute-start(bf16[2,16,32,128]{3,2,1,0:T(8,128)(2,1)S(1)} %copy-done.38), channel_id=1, source_target_pairs={{0,16},{4,20},{8,24},{12,28},{16,0},{20,4},{24,8},{28,12},{1,17},{... | collective-permute-start | bytes 786440 | tf_op jit(solution)/shard_map/ppermute | solution.py:385
  134.2 30.7 %collective-permute-start.23 = (bf16[2,16,32,128]{3,2,1,0:T(8,128)(2,1)}, bf16[2,16,32,128]{3,2,1,0:T(8,128)(2,1)}, u32[]{:S(2)}, u32[]{:S(2)}) collective-permute-start(bf16[2,16,32,128]{3,2,1,0:T(8,128)(2,1)} %get-tuple-element.82), channel_id=1, source_target_pairs={{0,20},{4,16},{8,28},{12,24},{16,4},{20,0},{24,12},{28,8},{1,21},{... | collective-permute-start | bytes 786440 | tf_op jit(solution)/shard_map/ppermute | solution.py:385
  145.8 22.6 %collective-permute-start.24 = (bf16[2,16,32,128]{3,2,1,0:T(8,128)(2,1)}, bf16[2,16,32,128]{3,2,1,0:T(8,128)(2,1)}, u32[]{:S(2)}, u32[]{:S(2)}) collective-permute-start(bf16[2,16,32,128]{3,2,1,0:T(8,128)(2,1)} %get-tuple-element.83), channel_id=1, source_target_pairs={{0,24},{4,28},{8,16},{12,20},{16,8},{20,12},{24,0},{28,4},{1,25},{... | collective-permute-start | bytes 786440 | tf_op jit(solution)/shard_map/ppermute | solution.py:385
  145.9 28.0 %collective-permute-start.25 = (bf16[2,16,32,128]{3,2,1,0:T(8,128)(2,1)}, bf16[2,16,32,128]{3,2,1,0:T(8,128)(2,1)S(1)}, u32[]{:S(2)}, u32[]{:S(2)}) collective-permute-start(bf16[2,16,32,128]{3,2,1,0:T(8,128)(2,1)} %get-tuple-element.84), channel_id=1, source_target_pairs={{0,28},{4,24},{8,20},{12,16},{16,12},{20,8},{24,4},{28,0},{1,29},{... | collective-permute-start | bytes 786440 | tf_op jit(solution)/shard_map/ppermute | solution.py:385
  153.3 64.5 %collective-permute-start.27 = (bf16[32,16,1024]{2,1,0:T(8,128)(2,1)}, bf16[32,16,1024]{2,1,0:T(8,128)(2,1)S(1)}, u32[]{:S(2)}, u32[]{:S(2)}) collective-permute-start(bf16[32,16,1024]{2,1,0:T(8,128)(2,1)} %get-tuple-element.75.after_ref.refs_0_.refs_4_), channel_id=1, source_target_pairs={{0,1},{1,0},{2,3},{3,2},{4,5},{5,4},{6,7},{7,6},{8,9},{9,8},{10,11... | collective-permute-start | bytes 3145736 | tf_op jit(solution)/shard_map/ppermute | solution.py:385
  181.6 38.0 %collective-permute-start.36 = (bf16[32,16,1024]{2,1,0:T(8,128)(2,1)}, bf16[32,16,1024]{2,1,0:T(8,128)(2,1)S(1)}, u32[]{:S(2)}, u32[]{:S(2)}) collective-permute-start(bf16[32,16,1024]{2,1,0:T(8,128)(2,1)} %get-tuple-element.85.after_ref.refs_0_.refs_8_), channel_id=1, source_target_pairs={{0,2},{1,3},{2,0},{3,1},{4,6},{5,7},{6,4},{7,5},{8,10},{9,11},{10,... | collective-permute-start | bytes 3145736 | tf_op jit(solution)/shard_map/ppermute | solution.py:385
  182.2 37.5 %collective-permute-start.28 = (bf16[32,16,1024]{2,1,0:T(8,128)(2,1)S(1)}, bf16[32,16,1024]{2,1,0:T(8,128)(2,1)S(1)}, u32[]{:S(2)}, u32[]{:S(2)}) collective-permute-start(bf16[32,16,1024]{2,1,0:T(8,128)(2,1)S(1)} %collective-permute-done.26.refs_1_.refs_5_), channel_id=1, source_target_pairs={{0,1},{1,0},{2,3},{3,2},{4,5},{5,4},{6,7},{7,6},{8,9},{9,8},{10,11... | collective-permute-start | bytes 3145736 | tf_op jit(solution)/shard_map/ppermute | solution.py:385
  182.2 8.9 %collective-permute-start.29 = (bf16[2,16,32,128]{3,2,1,0:T(8,128)(2,1)}, bf16[2,16,32,128]{3,2,1,0:T(8,128)(2,1)S(1)}, u32[]{:S(2)}, u32[]{:S(2)}) collective-permute-start(bf16[2,16,32,128]{3,2,1,0:T(8,128)(2,1)} %get-tuple-element.87), channel_id=1, source_target_pairs={{0,4},{4,0},{8,12},{12,8},{16,20},{20,16},{24,28},{28,24},{1,5},{5... | collective-permute-start | bytes 786440 | tf_op jit(solution)/shard_map/ppermute | solution.py:385
  182.3 8.9 %collective-permute-start.30 = (bf16[2,16,32,128]{3,2,1,0:T(8,128)(2,1)}, bf16[2,16,32,128]{3,2,1,0:T(8,128)(2,1)S(1)}, u32[]{:S(2)}, u32[]{:S(2)}) collective-permute-start(bf16[2,16,32,128]{3,2,1,0:T(8,128)(2,1)} %get-tuple-element.88), channel_id=1, source_target_pairs={{0,8},{4,12},{8,0},{12,4},{16,24},{20,28},{24,16},{28,20},{1,9},{5... | collective-permute-start | bytes 786440 | tf_op jit(solution)/shard_map/ppermute | solution.py:385
  191.1 11.6 %collective-permute-start.31 = (bf16[2,16,32,128]{3,2,1,0:T(8,128)(2,1)}, bf16[2,16,32,128]{3,2,1,0:T(8,128)(2,1)S(1)}, u32[]{:S(2)}, u32[]{:S(2)}) collective-permute-start(bf16[2,16,32,128]{3,2,1,0:T(8,128)(2,1)} %get-tuple-element.89), channel_id=1, source_target_pairs={{0,12},{4,8},{8,4},{12,0},{16,28},{20,24},{24,20},{28,16},{1,13},{... | collective-permute-start | bytes 786440 | tf_op jit(solution)/shard_map/ppermute | solution.py:385
  191.1 26.7 %collective-permute-start.32 = (bf16[2,16,32,128]{3,2,1,0:T(8,128)(2,1)}, bf16[2,16,32,128]{3,2,1,0:T(8,128)(2,1)S(1)}, u32[]{:S(2)}, u32[]{:S(2)}) collective-permute-start(bf16[2,16,32,128]{3,2,1,0:T(8,128)(2,1)} %get-tuple-element.90), channel_id=1, source_target_pairs={{0,16},{4,20},{8,24},{12,28},{16,0},{20,4},{24,8},{28,12},{1,17},{... | collective-permute-start | bytes 786440 | tf_op jit(solution)/shard_map/ppermute | solution.py:385
  202.7 25.5 %collective-permute-start.33 = (bf16[2,16,32,128]{3,2,1,0:T(8,128)(2,1)}, bf16[2,16,32,128]{3,2,1,0:T(8,128)(2,1)}, u32[]{:S(2)}, u32[]{:S(2)}) collective-permute-start(bf16[2,16,32,128]{3,2,1,0:T(8,128)(2,1)} %get-tuple-element.91), channel_id=1, source_target_pairs={{0,20},{4,16},{8,28},{12,24},{16,4},{20,0},{24,12},{28,8},{1,21},{... | collective-permute-start | bytes 786440 | tf_op jit(solution)/shard_map/ppermute | solution.py:385
  217.8 16.9 %collective-permute-start.34 = (bf16[2,16,32,128]{3,2,1,0:T(8,128)(2,1)}, bf16[2,16,32,128]{3,2,1,0:T(8,128)(2,1)}, u32[]{:S(2)}, u32[]{:S(2)}) collective-permute-start(bf16[2,16,32,128]{3,2,1,0:T(8,128)(2,1)} %get-tuple-element.92), channel_id=1, source_target_pairs={{0,24},{4,28},{8,16},{12,20},{16,8},{20,12},{24,0},{28,4},{1,25},{... | collective-permute-start | bytes 786440 | tf_op jit(solution)/shard_map/ppermute | solution.py:385
  217.9 22.9 %collective-permute-start.35 = (bf16[2,16,32,128]{3,2,1,0:T(8,128)(2,1)}, bf16[2,16,32,128]{3,2,1,0:T(8,128)(2,1)}, u32[]{:S(2)}, u32[]{:S(2)}) collective-permute-start(bf16[2,16,32,128]{3,2,1,0:T(8,128)(2,1)} %get-tuple-element.93), channel_id=1, source_target_pairs={{0,28},{4,24},{8,20},{12,16},{16,12},{20,8},{24,4},{28,0},{1,29},{... | collective-permute-start | bytes 786440 | tf_op jit(solution)/shard_map/ppermute | solution.py:385
  219.7 42.7 %collective-permute-start.37 = (bf16[32,16,1024]{2,1,0:T(8,128)(2,1)}, bf16[32,16,1024]{2,1,0:T(8,128)(2,1)}, u32[]{:S(2)}, u32[]{:S(2)}) collective-permute-start(bf16[32,16,1024]{2,1,0:T(8,128)(2,1)} %get-tuple-element.85.after_ref.refs_0_.refs_8_), channel_id=1, source_target_pairs={{0,1},{1,0},{2,3},{3,2},{4,5},{5,4},{6,7},{7,6},{8,9},{9,8},{10,11... | collective-permute-start | bytes 3145736 | tf_op jit(solution)/shard_map/ppermute | solution.py:385
  220.7 41.6 %collective-permute-start.38 = (bf16[32,16,1024]{2,1,0:T(8,128)(2,1)S(1)}, bf16[32,16,1024]{2,1,0:T(8,128)(2,1)}, u32[]{:S(2)}, u32[]{:S(2)}) collective-permute-start(bf16[32,16,1024]{2,1,0:T(8,128)(2,1)S(1)} %collective-permute-done.36.refs_1_.refs_9_), channel_id=1, source_target_pairs={{0,1},{1,0},{2,3},{3,2},{4,5},{5,4},{6,7},{7,6},{8,9},{9,8},{10,11... | collective-permute-start | bytes 3145736 | tf_op jit(solution)/shard_map/ppermute | solution.py:385
  247.9 25.1 %collective-permute-start.46 = (bf16[32,16,1024]{2,1,0:T(8,128)(2,1)}, bf16[32,16,1024]{2,1,0:T(8,128)(2,1)S(1)}, u32[]{:S(2)}, u32[]{:S(2)}) collective-permute-start(bf16[32,16,1024]{2,1,0:T(8,128)(2,1)} %get-tuple-element.94.after_ref.refs_0_.refs_12_), channel_id=1, source_target_pairs={{0,2},{1,3},{2,0},{3,1},{4,6},{5,7},{6,4},{7,5},{8,10},{9,11},{10,... | collective-permute-start | bytes 3145736 | tf_op jit(solution)/shard_map/ppermute | solution.py:385
  254.9 16.3 %collective-permute-start.42 = (bf16[2,16,16,128]{3,2,1,0:T(8,128)(2,1)S(1)}, bf16[2,16,16,128]{3,2,1,0:T(8,128)(2,1)}, u32[]{:S(2)}, u32[]{:S(2)}) collective-permute-start(bf16[2,16,16,128]{3,2,1,0:T(8,128)(2,1)S(1)} %copy-done.40), channel_id=1, source_target_pairs={{0,16},{4,20},{8,24},{12,28},{16,0},{20,4},{24,8},{28,12},{1,17},{... | collective-permute-start | bytes 393224 | tf_op jit(solution)/shard_map/ppermute | solution.py:385
  260.8 13.3 %collective-permute-start.43 = (bf16[2,16,16,128]{3,2,1,0:T(8,128)(2,1)}, bf16[2,16,16,128]{3,2,1,0:T(8,128)(2,1)}, u32[]{:S(2)}, u32[]{:S(2)}) collective-permute-start(bf16[2,16,16,128]{3,2,1,0:T(8,128)(2,1)} %get-tuple-element.100), channel_id=1, source_target_pairs={{0,20},{4,16},{8,28},{12,24},{16,4},{20,0},{24,12},{28,8},{1,21},{... | collective-permute-start | bytes 393224 | tf_op jit(solution)/shard_map/ppermute | solution.py:385
  262.3 15.8 %collective-permute-start.44 = (bf16[2,16,16,128]{3,2,1,0:T(8,128)(2,1)}, bf16[2,16,16,128]{3,2,1,0:T(8,128)(2,1)}, u32[]{:S(2)}, u32[]{:S(2)}) collective-permute-start(bf16[2,16,16,128]{3,2,1,0:T(8,128)(2,1)} %get-tuple-element.101), channel_id=1, source_target_pairs={{0,24},{4,28},{8,16},{12,20},{16,8},{20,12},{24,0},{28,4},{1,25},{... | collective-permute-start | bytes 393224 | tf_op jit(solution)/shard_map/ppermute | solution.py:385
  262.3 17.9 %collective-permute-start.45 = (bf16[2,16,16,128]{3,2,1,0:T(8,128)(2,1)}, bf16[2,16,16,128]{3,2,1,0:T(8,128)(2,1)S(1)}, u32[]{:S(2)}, u32[]{:S(2)}) collective-permute-start(bf16[2,16,16,128]{3,2,1,0:T(8,128)(2,1)} %get-tuple-element.102), channel_id=1, source_target_pairs={{0,28},{4,24},{8,20},{12,16},{16,12},{20,8},{24,4},{28,0},{1,29},{... | collective-permute-start | bytes 393224 | tf_op jit(solution)/shard_map/ppermute | solution.py:385
  271.2 28.8 %collective-permute-start.47 = (bf16[32,16,1024]{2,1,0:T(8,128)(2,1)}, bf16[32,16,1024]{2,1,0:T(8,128)(2,1)S(1)}, u32[]{:S(2)}, u32[]{:S(2)}) collective-permute-start(bf16[32,16,1024]{2,1,0:T(8,128)(2,1)} %get-tuple-element.94.after_ref.refs_0_.refs_12_), channel_id=1, source_target_pairs={{0,1},{1,0},{2,3},{3,2},{4,5},{5,4},{6,7},{7,6},{8,9},{9,8},{10,11... | collective-permute-start | bytes 3145736 | tf_op jit(solution)/shard_map/ppermute | solution.py:385
  273.0 27.0 %collective-permute-start.48 = (bf16[32,16,1024]{2,1,0:T(8,128)(2,1)S(1)}, bf16[32,16,1024]{2,1,0:T(8,128)(2,1)S(1)}, u32[]{:S(2)}, u32[]{:S(2)}) collective-permute-start(bf16[32,16,1024]{2,1,0:T(8,128)(2,1)S(1)} %collective-permute-done.46.refs_1_.refs_13_), channel_id=1, source_target_pairs={{0,1},{1,0},{2,3},{3,2},{4,5},{5,4},{6,7},{7,6},{8,9},{9,8},{10,11... | collective-permute-start | bytes 3145736 | tf_op jit(solution)/shard_map/ppermute | solution.py:385
  286.5 12.9 %collective-permute-start.49 = (bf16[16,16,1024]{2,1,0:T(8,128)(2,1)}, bf16[16,16,1024]{2,1,0:T(8,128)(2,1)S(1)}, u32[]{:S(2)}, u32[]{:S(2)}) collective-permute-start(bf16[16,16,1024]{2,1,0:T(8,128)(2,1)} %get-tuple-element.103.after_ref.refs_0_.refs_16_), channel_id=1, source_target_pairs={{0,2},{1,3},{2,0},{3,1},{4,6},{5,7},{6,4},{7,5},{8,10},{9,11},{10,... | collective-permute-start | bytes 1572872 | tf_op jit(solution)/shard_map/ppermute | solution.py:385
  287.1 22.0 %collective-permute-start.50 = (bf16[16,16,1024]{2,1,0:T(8,128)(2,1)}, bf16[16,16,1024]{2,1,0:T(8,128)(2,1)}, u32[]{:S(2)}, u32[]{:S(2)}) collective-permute-start(bf16[16,16,1024]{2,1,0:T(8,128)(2,1)} %get-tuple-element.103.after_ref.refs_0_.refs_16_), channel_id=1, source_target_pairs={{0,1},{1,0},{2,3},{3,2},{4,5},{5,4},{6,7},{7,6},{8,9},{9,8},{10,11... | collective-permute-start | bytes 1572872 | tf_op jit(solution)/shard_map/ppermute | solution.py:385
  299.4 9.7 %collective-permute-start.51 = (bf16[16,16,1024]{2,1,0:T(8,128)(2,1)S(1)}, bf16[16,16,1024]{2,1,0:T(8,128)(2,1)}, u32[]{:S(2)}, u32[]{:S(2)}) collective-permute-start(bf16[16,16,1024]{2,1,0:T(8,128)(2,1)S(1)} %collective-permute-done.49.refs_1_.refs_17_), channel_id=1, source_target_pairs={{0,1},{1,0},{2,3},{3,2},{4,5},{5,4},{6,7},{7,6},{8,9},{9,8},{10,11... | collective-permute-start | bytes 1572872 | tf_op jit(solution)/shard_map/ppermute | solution.py:385
  (50 other events, 1019.0 us)

commit v3 on v2

v3 whole, which is shorter than its diff:
```python
import functools

import jax
import jax.numpy as jnp
import ml_dtypes
import numpy as np
from jax import lax
from jax.experimental import pallas as pl
from jax.experimental.pallas import tpu as pltpu
from jax.sharding import PartitionSpec as P

NS_ITERS = 5
SMALL_ROWS = 16
LARGE_ROWS = 32
GRAM_ROWS = 4
POLAR_ROWS = 8
HIGHEST = lax.Precision.HIGHEST
F32 = jnp.float32
BF16 = jnp.bfloat16
VMEM_LIMIT = 60 << 20
BYTES_PER_US = 3690000

ANY = pl.BlockSpec(memory_space=pl.ANY)
SMEM = pl.BlockSpec(memory_space=pltpu.SMEM)


def kernel_params():
    return pltpu.CompilerParams(vmem_limit_bytes=VMEM_LIMIT)


def cost(micros):
    return pl.CostEstimate(flops=0, bytes_accessed=int(micros * BYTES_PER_US), transcendentals=0)


def dot_nt(a, b, precision=None):
    return lax.dot_general(
        a, b, (((1,), (1,)), ((), ())), precision=precision, preferred_element_type=F32
    )


def dot_nn(a, b, precision=None):
    return lax.dot_general(
        a, b, (((1,), (0,)), ((), ())), precision=precision, preferred_element_type=F32
    )


def iota(shape, dim):
    return lax.broadcasted_iota(jnp.int32, shape, dim)


def make_tables(side_len):
    indices = np.arange(side_len, dtype=np.int64)
    phases = (np.outer(indices, indices) % side_len).astype(np.float32) * np.float32(
        2.0 * 3.141592653589793 / side_len
    )
    unit_scale = np.float32(float(side_len) ** (-0.5))
    cosine = (np.cos(phases) * unit_scale).astype(ml_dtypes.bfloat16)
    sine_table = (np.sin(phases) * unit_scale).astype(ml_dtypes.bfloat16)
    return cosine, sine_table


def chunk_rows(own_rows):
    large = [(first, LARGE_ROWS) for first in range(2 * SMALL_ROWS, own_rows - LARGE_ROWS + 1, LARGE_ROWS)]
    covered = 2 * SMALL_ROWS + LARGE_ROWS * len(large)
    rest = [(first, SMALL_ROWS) for first in range(covered, own_rows, SMALL_ROWS)]
    return [(0, SMALL_ROWS)] + large + rest + [(SMALL_ROWS, SMALL_ROWS)]


def first_body(table_ref, grid_ref, after_ref, out_ref):
    strips, _, chans, rows, width = out_ref.shape
    side_len = table_ref.shape[-1]
    table = table_ref[...]
    middle = strips * rows
    turned = jnp.concatenate([-table[middle:], table[:middle]], axis=0)
    total = dot_nt(table, grid_ref[0].reshape(chans * width, side_len))
    total = total + dot_nt(turned, grid_ref[1].reshape(chans * width, side_len))
    total = total.astype(BF16)
    for part in range(2):
        for strip in range(strips):
            first = (part * strips + strip) * rows
            for chan in range(chans):
                out_ref[strip, part, chan] = total[first : first + rows, chan * width : (chan + 1) * width]


def first_transform(table, grid, strips, after):
    _, chans, width, side_len = grid.shape
    rows = table.shape[0] // (2 * strips)
    shape = (strips, 2, chans, rows, width)
    if width % 128 or rows % 16:
        middle = strips * rows
        turned = jnp.concatenate([-table[middle:], table[:middle]], axis=0)
        total = jnp.einsum("mv,cuv->mcu", table, grid[0], preferred_element_type=F32)
        total = total + jnp.einsum("mv,cuv->mcu", turned, grid[1], preferred_element_type=F32)
        total = total.astype(BF16).reshape(2, strips, rows, chans, width)
        return total.transpose(1, 0, 3, 2, 4)
    block = 4 if chans % 4 == 0 else 1
    return pl.pallas_call(
        first_body,
        grid=(chans // block,),
        in_specs=[
            pl.BlockSpec(table.shape, lambda i: (0, 0)),
            pl.BlockSpec((2, block, width, side_len), lambda i: (0, i, 0, 0)),
            ANY,
        ],
        out_specs=pl.BlockSpec((strips, 2, block, rows, width), lambda i: (0, 0, i, 0, 0)),
        out_shape=jax.ShapeDtypeStruct(shape, BF16),
        compiler_params=kernel_params(),
        cost_estimate=cost(4 + rows // 6),
        name="first_transform",
    )(table, grid, after)


def band_matrix(taps_of, levels, taps, own_rows, reach, first_row, image_rows):
    half_taps = taps // 2
    shape = (own_rows, own_rows + 2 * reach)
    row = iota(shape, 0)
    column = iota(shape, 1)
    place = jnp.where(
        column < own_rows, column, jnp.where(column < own_rows + reach, column - own_rows - reach, column - reach)
    )
    total = jnp.zeros(shape, F32)
    for level in range(levels):
        dilation = 2**level
        for outer in range(taps):
            detail_row = row - (outer - half_taps) * dilation
            inside = (detail_row + first_row >= 0) & (detail_row + first_row < image_rows)
            for inner in range(taps):
                hit = inside & (place == detail_row + (inner - half_taps) * dilation)
                total = total + jnp.where(hit, taps_of(level, outer) * taps_of(level, inner), 0.0)
    return total


def base_body(levels, taps, reach, strips, strip_ref, step_ref, highpass_ref, model_ref, edge_ref, after_ref, out_ref, high, low):
    block, own_rows, side_len = model_ref.shape

    @pl.when(pl.program_id(0) == 0)
    def _():
        band = band_matrix(
            lambda level, tap: highpass_ref[level, tap],
            levels,
            taps,
            own_rows,
            reach,
            strip_ref[0] * own_rows,
            strips * own_rows,
        )
        top = band.astype(BF16)
        high[...] = top
        low[...] = (band - top.astype(F32)).astype(BF16)

    first = pl.program_id(0) * block
    for chan in range(block):
        model = model_ref[chan]
        top = model.astype(BF16)
        rest = (model - top.astype(F32)).astype(BF16)
        edge = edge_ref[chan].astype(F32)
        whole = jnp.concatenate([top.astype(F32), edge], axis=0).astype(BF16)
        gradient = dot_nn(high[...], whole)
        gradient = gradient + dot_nn(low[...], whole)
        gradient = gradient + dot_nn(high[:, :own_rows], rest)
        out_ref[chan] = model - step_ref[first + chan] * gradient


def base_step(strip, strips, step_size, highpass, model_image, edges, after):
    chans, rows, side_len = model_image.shape
    levels, taps = highpass.shape
    reach = edges.shape[1] // 2
    block = 2 if chans % 2 == 0 else 1
    wide = rows + 2 * reach
    return pl.pallas_call(
        functools.partial(base_body, levels, taps, reach, strips),
        grid=(chans // block,),
        in_specs=[
            SMEM,
            SMEM,
            SMEM,
            pl.BlockSpec((block, rows, side_len), lambda i: (i, 0, 0)),
            pl.BlockSpec((block, 2 * reach, side_len), lambda i: (i, 0, 0)),
            ANY,
        ],
        out_specs=pl.BlockSpec((block, rows, side_len), lambda i: (i, 0, 0)),
        out_shape=jax.ShapeDtypeStruct(model_image.shape, F32),
        scratch_shapes=[pltpu.VMEM((rows, wide), BF16), pltpu.VMEM((rows, wide), BF16)],
        compiler_params=kernel_params(),
        cost_estimate=cost(9),
        name="base_step",
    )(strip, step_size, highpass, model_image, edges, after)


def second_body(step_ref, half_ref, cosine_ref, sine_ref, base_ref, after_ref, moved_ref, pixels_ref):
    strips, _, chans, rows, width = half_ref.shape
    real = jnp.concatenate([half_ref[s, 0].reshape(chans * rows, width) for s in range(strips)], axis=1)
    imag = jnp.concatenate([half_ref[s, 1].reshape(chans * rows, width) for s in range(strips)], axis=1)
    dirty = dot_nn(real, cosine_ref[...]) - dot_nn(imag, sine_ref[...])
    pieces = []
    for chan in range(chans):
        moved = base_ref[chan] + step_ref[chan] * dirty[chan * rows : (chan + 1) * rows]
        moved_ref[chan] = moved
        pieces.append(moved)
    pixels_ref[...] = jnp.swapaxes(jnp.stack(pieces), 0, 1).astype(BF16)


def second_transform(step_size, half, cosine, sine_table, base, first_row, after):
    strips, _, chans, rows, width = half.shape
    side_len = cosine.shape[0]
    if width % 128 or rows % 16 or chans % 16:
        split = (strips, width, side_len)
        dirty = jnp.einsum("scmu,sul->cml", half[:, 0], cosine.reshape(split), preferred_element_type=F32)
        dirty = dirty - jnp.einsum("scmu,sul->cml", half[:, 1], sine_table.reshape(split), preferred_element_type=F32)
        moved = base[:, first_row : first_row + rows] + step_size[:, None, None] * dirty
        pixels = moved.astype(BF16).transpose(1, 0, 2)
        return lax.dynamic_update_slice(base, moved, (0, first_row, 0)), pixels
    block = min(256, side_len)
    place = first_row // rows
    return pl.pallas_call(
        second_body,
        grid=(side_len // block,),
        in_specs=[
            SMEM,
            pl.BlockSpec(half.shape, lambda i: (0, 0, 0, 0, 0)),
            pl.BlockSpec((side_len, block), lambda i: (0, i)),
            pl.BlockSpec((side_len, block), lambda i: (0, i)),
            pl.BlockSpec((chans, rows, block), lambda i: (0, place, i)),
            ANY,
        ],
        out_specs=[
            pl.BlockSpec((chans, rows, block), lambda i: (0, place, i)),
            pl.BlockSpec((rows, chans, block), lambda i: (0, 0, i)),
        ],
        out_shape=[
            jax.ShapeDtypeStruct(base.shape, F32),
            jax.ShapeDtypeStruct((rows, chans, side_len), BF16),
        ],
        input_output_aliases={4: 0},
        compiler_params=kernel_params(),
        cost_estimate=cost(2 + rows // 10),
        name="second_transform",
    )(step_size, half, cosine, sine_table, base, after)


def stacked(group_refs, first, count):
    return jnp.concatenate([ref[first + i] for i in range(count) for ref in group_refs], axis=0)


def gram_body(before_ref, after_ref, pixels_ref, total_ref):
    groups, rows, _, _ = pixels_ref.shape

    @pl.when(pl.program_id(0) == 0)
    def _():
        total_ref[...] = before_ref[...]

    total = total_ref[...]
    for first in range(0, rows, GRAM_ROWS):
        pixels = stacked([pixels_ref.at[group] for group in range(groups)], first, GRAM_ROWS)
        total = total + dot_nt(pixels, pixels)
    total_ref[...] = total


def gram_step(pixels, before, after):
    groups, rows, chans, side_len = pixels.shape
    block = 8
    return pl.pallas_call(
        gram_body,
        grid=(rows // block,),
        in_specs=[
            pl.BlockSpec(before.shape, lambda i: (0, 0)),
            ANY,
            pl.BlockSpec((groups, block, chans, side_len), lambda i: (0, i, 0, 0)),
        ],
        out_specs=pl.BlockSpec(before.shape, lambda i: (0, 0)),
        out_shape=jax.ShapeDtypeStruct(before.shape, F32),
        compiler_params=kernel_params(),
        cost_estimate=cost(1 + rows // 16),
        name="gram_step",
    )(before, after, pixels)


def newton_schulz(gram):
    size = gram.shape[0]
    frob_norm = jnp.sqrt(jnp.sum(gram * gram))
    identity = (iota((size, size), 0) == iota((size, size), 1)).astype(F32)
    current = gram / frob_norm
    inverse = identity
    for iteration in range(NS_ITERS):
        middle = 0.5 * (3.0 * identity - dot_nn(inverse, current, HIGHEST))
        if iteration + 1 < NS_ITERS:
            current = dot_nn(current, middle, HIGHEST)
        inverse = dot_nn(middle, inverse, HIGHEST)
    return inverse, frob_norm


def polar_body(starts, sizes, shrink_ref, select_ref, gram_ref, moved_hbm, *refs):
    chunks = len(sizes)
    pixels_hbm = refs[:chunks]
    out_hbm, moved, in_sems, moved_sems, out_sems = refs[chunks : chunks + 5]
    pixels = refs[chunks + 5 :]
    own, all_rows, side_len = moved.shape
    groups = pixels[0].shape[0]
    size = pixels[0].shape[2] * groups
    moved_copies = []
    pixel_copies = []
    for chunk in range(chunks):
        copy = pltpu.make_async_copy(pixels_hbm[chunk], pixels[chunk], in_sems.at[chunk])
        copy.start()
        pixel_copies.append(copy)
        part = pl.ds(starts[chunk], sizes[chunk])
        copy = pltpu.make_async_copy(moved_hbm.at[:, part], moved.at[:, part], moved_sems.at[chunk])
        copy.start()
        moved_copies.append(copy)
    gram = jnp.zeros((size, size), F32)
    for i in range(GRAM_ROWS):
        gram = gram + gram_ref[i * size : (i + 1) * size, i * size : (i + 1) * size]
    inverse, frob_norm = newton_schulz(gram)
    factor = shrink_ref[0] * jnp.sqrt(all_rows * side_len / frob_norm)
    weights = dot_nt(select_ref[...], inverse, HIGHEST) * factor
    spread = POLAR_ROWS * own
    wide = POLAR_ROWS * size
    repeat = (iota((spread, own), 0) // POLAR_ROWS == iota((spread, own), 1)).astype(BF16)
    weights = dot_nn(repeat, weights.astype(BF16)).astype(BF16)
    repeat = (iota((size, wide), 1) % size == iota((size, wide), 0)).astype(BF16)
    weights = dot_nn(weights, repeat)
    keep = iota((spread, wide), 0) % POLAR_ROWS == iota((spread, wide), 1) // size
    weights = jnp.where(keep, weights, 0.0).astype(BF16)
    out_copies = []
    for chunk in range(chunks):
        pixel_copies[chunk].wait()
        moved_copies[chunk].wait()
        for step in range(sizes[chunk] // POLAR_ROWS):
            data = stacked([pixels[chunk].at[group] for group in range(groups)], step * POLAR_ROWS, POLAR_ROWS)
            polar = dot_nn(weights, data).reshape(own, POLAR_ROWS, side_len)
            first = starts[chunk] + step * POLAR_ROWS
            moved[:, first : first + POLAR_ROWS] -= polar
        part = pl.ds(starts[chunk], sizes[chunk])
        copy = pltpu.make_async_copy(moved.at[:, part], out_hbm.at[:, part], out_sems.at[chunk])
        copy.start()
        out_copies.append(copy)
    for copy in out_copies:
        copy.wait()


def polar_step(shrinkage, select, gram, moved, gathered, starts):
    chunks = len(gathered)
    sizes = [pieces.shape[1] for pieces in gathered]
    return pl.pallas_call(
        functools.partial(polar_body, starts, sizes),
        in_specs=[SMEM, pl.BlockSpec(memory_space=pltpu.VMEM), pl.BlockSpec(memory_space=pltpu.VMEM), ANY] + [ANY] * chunks,
        out_specs=ANY,
        out_shape=jax.ShapeDtypeStruct(moved.shape, F32),
        scratch_shapes=[
            pltpu.VMEM(moved.shape, F32),
            pltpu.SemaphoreType.DMA((chunks,)),
            pltpu.SemaphoreType.DMA((chunks,)),
            pltpu.SemaphoreType.DMA((chunks,)),
        ]
        + [pltpu.VMEM(pieces.shape, BF16) for pieces in gathered],
        compiler_params=kernel_params(),
        cost_estimate=cost(11),
        name="polar_step",
    )(shrinkage, select, gram, moved, *gathered)


def neighbour_rows(model_image, reach):
    ends = lax.axis_size("strip") - 1
    head, tail = lax.optimization_barrier((model_image[:, :reach], model_image[:, model_image.shape[1] - reach :]))
    before = lax.ppermute(tail.astype(BF16), "strip", [(i, i + 1) for i in range(ends)])
    after = lax.ppermute(head.astype(BF16), "strip", [(i + 1, i) for i in range(ends)])
    return jnp.concatenate([before, after], axis=1)


def local(grid, model_image, step_size, highpass, shrinkage):
    chans, own_rows, side_len = model_image.shape
    strips = lax.axis_size("strip")
    size = chans * lax.axis_size("chan")
    starts, sizes = zip(*chunk_rows(own_rows))
    chunks = len(sizes)
    strip = lax.axis_index("strip").astype(jnp.int32).reshape(1)

    cosine, sine_table = make_tables(side_len)
    split = np.stack([cosine.reshape(strips, own_rows, side_len), sine_table.reshape(strips, own_rows, side_len)])
    tables = [
        np.ascontiguousarray(split[:, :, start : start + rows]).reshape(2 * strips * rows, side_len)
        for start, rows in zip(starts, sizes)
    ]

    levels, taps = highpass.shape
    reach = (taps - 1) * 2 ** (levels - 1)

    halves = {}
    gathered = []
    gram = jnp.zeros((GRAM_ROWS * size, GRAM_ROWS * size), F32)
    last = strip
    moved = None
    for chunk in range(chunks + 1):
        if chunk < chunks:
            sent = first_transform(tables[chunk], grid, strips, last)
            last = sent
            halves[chunk] = lax.all_to_all(sent, "strip", split_axis=0, concat_axis=0, tiled=True)
        if chunk == 0:
            edges = neighbour_rows(model_image, reach)
            moved = base_step(strip, strips, step_size, highpass, model_image, edges, last)
            last = moved
        else:
            done = chunk - 1
            moved, pixels = second_transform(step_size, halves[done], cosine, sine_table, moved, starts[done], last)
            last = pixels
            pixels = lax.all_gather(pixels, "chan", axis=0, tiled=False)
            if chans % 16:
                pixels = pixels.transpose(1, 0, 2, 3).reshape(1, sizes[done], size, side_len)
            gathered.append(pixels)
        if chunk > 1:
            gram = gram_step(gathered[chunk - 2], gram, last)
            last = gram
    gram = gram_step(gathered[-1], gram, last)

    own = lax.axis_index("chan") * chans + jnp.arange(chans, dtype=jnp.int32)
    select = (own[:, None] == jnp.arange(size, dtype=jnp.int32)[None, :]).astype(F32)
    return polar_step(shrinkage, select, gram, moved, gathered, starts)


def solution(mesh):
    return jax.shard_map(
        local,
        mesh=mesh,
        in_specs=(
            P(None, "chan", "strip", None),
            P("chan", "strip", None),
            P("chan"),
            P(),
            P("strip"),
        ),
        out_specs=P("chan", "strip", None),
        check_vma=False,
    )
```

time: 331 us -> 344 us (1.039)
  waiting for transfers between devices: 121 us -> 161 us
  starting transfers between devices: 67.7 us -> 39.8 us
  between operations: 1.32 us -> 13.8 us
  Pallas kernels: 126 us -> 116 us
    all_to_all x0 -> x5, waiting for transfers between devices: none -> 115 us  [local(): lax.all_to_all(sent, 'strip', split_axis=0, concat_axis=0, tiled=True)]
    ppermute x52 -> x2, waiting for transfers between devices: 121 us -> 28 us  [the longest x1 26.1 us: neighbour_rows(): lax.ppermute(tail.astype(BF16), 'strip', [(i, i + 1) for i in range(ends)])]
    ppermute x52 -> x2, starting transfers between devices: 67.7 us -> 5.84 us  [the longest x1 3.37 us: neighbour_rows(): lax.ppermute(tail.astype(BF16), 'strip', [(i, i + 1) for i in range(ends)])]
    all_to_all x0 -> x5, starting transfers between devices: none -> 34 us  [local(): lax.all_to_all(sent, 'strip', split_axis=0, concat_axis=0, tiled=True)]
    all_gather x0 -> x5, waiting for transfers between devices: none -> 18.5 us  [local(): pixels = lax.all_gather(pixels, 'chan', axis=0, tiled=False)]
    pallas_call x16, Pallas kernels: 115 us -> 105 us  [the longest x5 38.9 us: first_transform(): pl.pallas_call(first_body, grid=(chans // block,), in_specs=[pl.BlockSpec...]
    another operation x1 -> x0, other arithmetic: 4.04 us -> none
  transfers between devices with their start and end apart: 52 -> 12, of which waited for: 24 -> 7; matrix products, arithmetic and copies ran while one was open for 2% -> 1% of each run, Pallas kernels for 31% -> 28%
where the time goes in v3:
time: 344 us; the launch traced here: 341 us
  waiting for transfers between devices  161 us (47%)
  Pallas kernels  116 us (34%)
  starting transfers between devices  39.8 us (12%)
  between operations  13.8 us (4%)
  local copies, waits for them, and re-layouts  7.38 us (2%)
    all_to_all x5, waiting for transfers between devices, local(): lax.all_to_all(sent, 'strip', split_axis=0, concat_axis=0, tiled=True)  115 us
    pallas_call x5, Pallas kernels, first_transform(): pl.pallas_call(first_body, grid=(chans // block,), in_specs=[pl.BlockSpec...  38.9 us
    all_to_all x5, starting transfers between devices, local(): lax.all_to_all(sent, 'strip', split_axis=0, concat_axis=0, tiled=True)  34 us
    pallas_call x5, Pallas kernels, second_transform(): pl.pallas_call(second_body, grid=(side_len // block,), in_specs=[SMEM, pl...  32.6 us
    ppermute x1, waiting for transfers between devices, neighbour_rows(): lax.ppermute(tail.astype(BF16), 'strip', [(i, i + 1) for i in range(ends)])  26.1 us
    pallas_call x5, Pallas kernels, gram_step(): pl.pallas_call(gram_body, grid=(rows // block,), in_specs=[pl.BlockSpec(b...  20.7 us
    all_gather x5, waiting for transfers between devices, local(): pixels = lax.all_gather(pixels, 'chan', axis=0, tiled=False)  18.5 us
    pallas_call x1, Pallas kernels, polar_step(): pl.pallas_call(functools.partial(polar_body, starts, sizes), in_specs=[SM...  12.9 us
  transfers between devices with their start and end apart: 12, of which 7 were waited for; matrix products, arithmetic and copies ran while one was open for 1% of the time, Pallas kernels for 28%

profile of v3, /device:TPU:12, one launch (start us, length us, event | category | flops | bytes accessed | tf_op | source)
XLA Modules:
  0.0 340.6 jit_solution(2129779553349707136)
XLA Ops:
  6.5 6.5 %first_transform.5.after_ref = bf16[8,2,16,16,128]{4,3,2,1,0:T(8,128)(2,1)} custom-call(bf16[256,1024]{1,0:T(8,128)(2,1)} %constant.27.clone.table_ref, bf16[2,16,128,1024]{3,2,1,0:T(8,128)(2,1)} %grid_ref.9, s32[1]{0:T(128)} %bitcast.after_ref.strip_ref), custom_call_target="tpu_custom_call" | custom-call | bytes 22140000 | tf_op jit(solution)/shard_map/first_transform/pallas_call | solution.py:97
  13.0 6.2 %all-to-all-start.1 = ((bf16[8,2,16,16,128]{4,3,2,1,0:T(8,128)(2,1)}), bf16[8,2,16,16,128]{4,3,2,1,0:T(8,128)(2,1)S(1)}, u32[]{:S(2)}, u32[]{:S(2)}) async-start(bf16[8,2,16,16,128]{4,3,2,1,0:T(8,128)(2,1)} %first_transform.5.after_ref), calls=%async_computation.1 | async-start | bytes 2097152 | tf_op jit(solution)/shard_map/all_to_all | solution.py:397
  19.3 1.7 fusion.1
  21.0 3.4 collective-permute-start
  24.4 2.5 collective-permute-start.1
  26.9 26.1 %collective-permute-done = bf16[16,12,1024]{2,1,0:T(8,128)(2,1)S(1)} collective-permute-done((bf16[16,12,1024]{2,1,0:T(8,128)(2,1)S(1)}, bf16[16,12,1024]{2,1,0:T(8,128)(2,1)S(1)}, u32[]{:S(2)}, u32[]{:S(2)}) %collective-permute-start) | collective-permute-done | bytes 393248 | tf_op jit(solution)/shard_map/ppermute | solution.py:365
  52.9 1.9 collective-permute-done.1
  54.9 1.1 pad_maximum_fusion.edge_ref
  56.0 11.4 %base_step.1.after_ref.base_ref = f32[16,128,1024]{2,1,0:T(8,128)} custom-call(s32[1]{0:T(128)} %bitcast.after_ref.strip_ref, f32[16]{0:T(128)} %step_ref.11, f32[3,4]{1,0:T(4,128)} %highpass_ref.1, f32[16,128,1024]{2,1,0:T(8,128)} %model_ref.1, bf16[16,24,1024]{2,1,0:T(8,128)(2,1)} %pad_maximum_fusion.edge_ref, ...), custom_call_target="tpu_custom_call" | custom-call | bytes 33210000 | tf_op jit(solution)/shard_map/base_step/pallas_call | solution.py:170
  67.4 8.5 %first_transform.6.after_ref = bf16[8,2,16,32,128]{4,3,2,1,0:T(8,128)(2,1)} custom-call(bf16[512,1024]{1,0:T(8,128)(2,1)} %constant.28.clone.table_ref, bf16[2,16,128,1024]{3,2,1,0:T(8,128)(2,1)} %grid_ref.9, f32[16,128,1024]{2,1,0:T(8,128)} %base_step.1.after_ref.base_ref), custom_call_target="tpu_custom_call" | custom-call | bytes 33210000 | tf_op jit(solution)/shard_map/first_transform/pallas_call | solution.py:97
  75.9 0.0 all-to-all-done.1.half_ref
  75.9 7.0 %all-to-all-start = ((bf16[8,2,16,32,128]{4,3,2,1,0:T(8,128)(2,1)}), bf16[8,2,16,32,128]{4,3,2,1,0:T(8,128)(2,1)S(1)}, u32[]{:S(2)}, u32[]{:S(2)}) async-start(bf16[8,2,16,32,128]{4,3,2,1,0:T(8,128)(2,1)} %first_transform.6.after_ref), calls=%async_computation | async-start | bytes 4194304 | tf_op jit(solution)/shard_map/all_to_all | solution.py:397
  82.8 0.0 copy-done.3
  82.8 5.6 %second_transform.5 = (f32[16,128,1024]{2,1,0:T(8,128)}, bf16[16,16,1024]{2,1,0:T(8,128)(2,1)}) custom-call(f32[16]{0:T(128)} %step_ref.11, bf16[8,2,16,16,128]{4,3,2,1,0:T(8,128)(2,1)} %copy-done.3, bf16[1024,1024]{1,0:T(8,128)(2,1)} %constant.29.clone.cosine_ref, bf16[1024,1024]{1,0:T(8,128)(2,1)} %constant.30.clone.sine_ref, ...), custom_call_target="tpu_custom_call", output_to_operand_aliasing={{0}: (4, {})} | custom-call | bytes 11070000 | tf_op jit(solution)/shard_map/second_transform/pallas_call | solution.py:215
  88.4 0.0 all-gather.11.cloned.1.call-update
  88.4 0.0 all-gather.13.cloned.1.call-start
  88.5 8.5 %first_transform.7.after_ref = bf16[8,2,16,32,128]{4,3,2,1,0:T(8,128)(2,1)} custom-call(bf16[512,1024]{1,0:T(8,128)(2,1)} %constant.31.clone.table_ref, bf16[2,16,128,1024]{3,2,1,0:T(8,128)(2,1)} %grid_ref.9, bf16[16,16,1024]{2,1,0:T(8,128)(2,1)} %get-tuple-element.20.after_ref), custom_call_target="tpu_custom_call" | custom-call | bytes 33210000 | tf_op jit(solution)/shard_map/first_transform/pallas_call | solution.py:97
  97.0 30.8 %all-to-all-done.half_ref = bf16[8,2,16,32,128]{4,3,2,1,0:T(8,128)(2,1)S(1)} async-done(((bf16[8,2,16,32,128]{4,3,2,1,0:T(8,128)(2,1)}), bf16[8,2,16,32,128]{4,3,2,1,0:T(8,128)(2,1)S(1)}, u32[]{:S(2)}, u32[]{:S(2)}) %all-to-all-start) | async-done | bytes 2097184 | tf_op jit(solution)/shard_map/all_to_all | solution.py:397
  127.8 1.3 copy-done
  129.1 7.2 %second_transform.6 = (f32[16,128,1024]{2,1,0:T(8,128)}, bf16[32,16,1024]{2,1,0:T(8,128)(2,1)}) custom-call(f32[16]{0:T(128)} %step_ref.11, bf16[8,2,16,32,128]{4,3,2,1,0:T(8,128)(2,1)} %copy-done, bf16[1024,1024]{1,0:T(8,128)(2,1)} %constant.29.clone.cosine_ref, bf16[1024,1024]{1,0:T(8,128)(2,1)} %constant.30.clone.sine_ref, ...), custom_call_target="tpu_custom_call", output_to_operand_aliasing={{0}: (4, {})} | custom-call | bytes 18450000 | tf_op jit(solution)/shard_map/second_transform/pallas_call | solution.py:215
  136.3 0.0 all-gather.13.cloned.1.call-update
  136.3 6.9 %all-to-all-start.2 = ((bf16[8,2,16,32,128]{4,3,2,1,0:T(8,128)(2,1)}), bf16[8,2,16,32,128]{4,3,2,1,0:T(8,128)(2,1)S(1)}, u32[]{:S(2)}, u32[]{:S(2)}) async-start(bf16[8,2,16,32,128]{4,3,2,1,0:T(8,128)(2,1)} %first_transform.7.after_ref), calls=%async_computation.2 | async-start | bytes 4194304 | tf_op jit(solution)/shard_map/all_to_all | solution.py:397
  143.3 0.7 broadcast_in_dim.2.before_ref
  144.0 3.1 gram_step.5.after_ref.before_ref
  147.1 8.9 %first_transform.8.after_ref = bf16[8,2,16,32,128]{4,3,2,1,0:T(8,128)(2,1)} custom-call(bf16[512,1024]{1,0:T(8,128)(2,1)} %constant.32.clone.table_ref, bf16[2,16,128,1024]{3,2,1,0:T(8,128)(2,1)} %grid_ref.9, f32[256,256]{1,0:T(8,128)} %gram_step.5.after_ref.before_ref), custom_call_target="tpu_custom_call" | custom-call | bytes 33210000 | tf_op jit(solution)/shard_map/first_transform/pallas_call | solution.py:97
  155.9 32.5 %all-to-all-done.2.half_ref = bf16[8,2,16,32,128]{4,3,2,1,0:T(8,128)(2,1)S(1)} async-done(((bf16[8,2,16,32,128]{4,3,2,1,0:T(8,128)(2,1)}), bf16[8,2,16,32,128]{4,3,2,1,0:T(8,128)(2,1)S(1)}, u32[]{:S(2)}, u32[]{:S(2)}) %all-to-all-start.2) | async-done | bytes 2097184 | tf_op jit(solution)/shard_map/all_to_all | solution.py:397
  188.4 1.3 copy-done.1
  189.7 7.1 %second_transform.7 = (f32[16,128,1024]{2,1,0:T(8,128)}, bf16[32,16,1024]{2,1,0:T(8,128)(2,1)}) custom-call(f32[16]{0:T(128)} %step_ref.11, bf16[8,2,16,32,128]{4,3,2,1,0:T(8,128)(2,1)} %copy-done.1, bf16[1024,1024]{1,0:T(8,128)(2,1)} %constant.29.clone.cosine_ref, bf16[1024,1024]{1,0:T(8,128)(2,1)} %constant.30.clone.sine_ref, ...), custom_call_target="tpu_custom_call", output_to_operand_aliasing={{0}: (4, {})} | custom-call | bytes 18450000 | tf_op jit(solution)/shard_map/second_transform/pallas_call | solution.py:215
  196.8 0.0 all-gather.15.cloned.1.call-update
  196.9 6.9 %all-to-all-start.3 = ((bf16[8,2,16,32,128]{4,3,2,1,0:T(8,128)(2,1)}), bf16[8,2,16,32,128]{4,3,2,1,0:T(8,128)(2,1)S(1)}, u32[]{:S(2)}, u32[]{:S(2)}) async-start(bf16[8,2,16,32,128]{4,3,2,1,0:T(8,128)(2,1)} %first_transform.8.after_ref), calls=%async_computation.3 | async-start | bytes 4194304 | tf_op jit(solution)/shard_map/all_to_all | solution.py:397
  203.8 4.9 %gram_step.6.after_ref.before_ref = f32[256,256]{1,0:T(8,128)} custom-call(f32[256,256]{1,0:T(8,128)} %gram_step.5.after_ref.before_ref, bf16[32,16,1024]{2,1,0:T(8,128)(2,1)} %get-tuple-element.23.after_ref, bf16[4,32,16,1024]{3,2,1,0:T(8,128)(2,1)} %bitcast.8), custom_call_target="tpu_custom_call" | custom-call | bytes 11070000 | tf_op jit(solution)/shard_map/gram_step/pallas_call | solution.py:262
  208.7 6.5 %first_transform.9.after_ref = bf16[8,2,16,16,128]{4,3,2,1,0:T(8,128)(2,1)} custom-call(bf16[256,1024]{1,0:T(8,128)(2,1)} %constant.33.clone.table_ref, bf16[2,16,128,1024]{3,2,1,0:T(8,128)(2,1)} %grid_ref.9, f32[256,256]{1,0:T(8,128)} %gram_step.6.after_ref.before_ref), custom_call_target="tpu_custom_call" | custom-call | bytes 22140000 | tf_op jit(solution)/shard_map/first_transform/pallas_call | solution.py:97
  215.2 33.7 %all-to-all-done.3.half_ref = bf16[8,2,16,32,128]{4,3,2,1,0:T(8,128)(2,1)S(1)} async-done(((bf16[8,2,16,32,128]{4,3,2,1,0:T(8,128)(2,1)}), bf16[8,2,16,32,128]{4,3,2,1,0:T(8,128)(2,1)S(1)}, u32[]{:S(2)}, u32[]{:S(2)}) %all-to-all-start.3) | async-done | bytes 2097184 | tf_op jit(solution)/shard_map/all_to_all | solution.py:397
  248.9 1.3 copy-done.2
  250.2 7.2 %second_transform.8 = (f32[16,128,1024]{2,1,0:T(8,128)}, bf16[32,16,1024]{2,1,0:T(8,128)(2,1)}) custom-call(f32[16]{0:T(128)} %step_ref.11, bf16[8,2,16,32,128]{4,3,2,1,0:T(8,128)(2,1)} %copy-done.2, bf16[1024,1024]{1,0:T(8,128)(2,1)} %constant.29.clone.cosine_ref, bf16[1024,1024]{1,0:T(8,128)(2,1)} %constant.30.clone.sine_ref, ...), custom_call_target="tpu_custom_call", output_to_operand_aliasing={{0}: (4, {})} | custom-call | bytes 18450000 | tf_op jit(solution)/shard_map/second_transform/pallas_call | solution.py:215
  257.4 0.0 all-gather.17.cloned.1.call-update
  257.5 6.9 %all-to-all-start.4 = ((bf16[8,2,16,16,128]{4,3,2,1,0:T(8,128)(2,1)}), bf16[8,2,16,16,128]{4,3,2,1,0:T(8,128)(2,1)S(1)}, u32[]{:S(2)}, u32[]{:S(2)}) async-start(bf16[8,2,16,16,128]{4,3,2,1,0:T(8,128)(2,1)} %first_transform.9.after_ref), calls=%async_computation.4 | async-start | bytes 2097152 | tf_op jit(solution)/shard_map/all_to_all | solution.py:397
  264.4 0.0 all-gather.19.cloned.1.call-start
  264.4 4.9 %gram_step.7.after_ref.before_ref = f32[256,256]{1,0:T(8,128)} custom-call(f32[256,256]{1,0:T(8,128)} %gram_step.6.after_ref.before_ref, bf16[32,16,1024]{2,1,0:T(8,128)(2,1)} %get-tuple-element.25.after_ref, bf16[4,32,16,1024]{3,2,1,0:T(8,128)(2,1)} %bitcast.10), custom_call_target="tpu_custom_call" | custom-call | bytes 11070000 | tf_op jit(solution)/shard_map/gram_step/pallas_call | solution.py:262
  269.3 17.7 %all-to-all-done.4.half_ref = bf16[8,2,16,16,128]{4,3,2,1,0:T(8,128)(2,1)S(1)} async-done(((bf16[8,2,16,16,128]{4,3,2,1,0:T(8,128)(2,1)}), bf16[8,2,16,16,128]{4,3,2,1,0:T(8,128)(2,1)S(1)}, u32[]{:S(2)}, u32[]{:S(2)}) %all-to-all-start.4) | async-done | bytes 1048608 | tf_op jit(solution)/shard_map/all_to_all | solution.py:397
  287.1 1.0 copy-done.4
  288.0 5.5 %second_transform.9 = (f32[16,128,1024]{2,1,0:T(8,128)}, bf16[16,16,1024]{2,1,0:T(8,128)(2,1)}) custom-call(f32[16]{0:T(128)} %step_ref.11, bf16[8,2,16,16,128]{4,3,2,1,0:T(8,128)(2,1)} %copy-done.4, bf16[1024,1024]{1,0:T(8,128)(2,1)} %constant.29.clone.cosine_ref, bf16[1024,1024]{1,0:T(8,128)(2,1)} %constant.30.clone.sine_ref, ...), custom_call_target="tpu_custom_call", output_to_operand_aliasing={{0}: (4, {})} | custom-call | bytes 11070000 | tf_op jit(solution)/shard_map/second_transform/pallas_call | solution.py:215
  293.6 0.0 all-gather.19.cloned.1.call-update
  294.3 0.7 fusion.select_ref
  294.9 4.7 %gram_step.8.before_ref.after_ref = f32[256,256]{1,0:T(8,128)} custom-call(f32[256,256]{1,0:T(8,128)} %gram_step.7.after_ref.before_ref, bf16[16,16,1024]{2,1,0:T(8,128)(2,1)} %get-tuple-element.27.after_ref, bf16[4,32,16,1024]{3,2,1,0:T(8,128)(2,1)} %bitcast.6), custom_call_target="tpu_custom_call" | custom-call | bytes 11070000 | tf_op jit(solution)/shard_map/gram_step/pallas_call | solution.py:262
  299.7 18.5 %all-gather.19.cloned.1.call-done = bf16[64,16,1024]{2,1,0:T(8,128)(2,1)} async-done(((bf16[16,16,1024]{2,1,0:T(8,128)(2,1)}), bf16[64,16,1024]{2,1,0:T(8,128)(2,1)}) %all-gather.19.cloned.1.call-update) | async-done | bytes 2097168 | tf_op jit(solution)/shard_map/all_gather | solution.py:406
  318.2 3.0 gram_step.9.gram_ref
  321.2 12.9 %polar_step.1 = f32[16,128,1024]{2,1,0:T(8,128)} custom-call(f32[1]{0:T(128)S(6)} %copy.23.shrink_ref, f32[16,64]{1,0:T(8,128)} %fusion.select_ref, f32[256,256]{1,0:T(8,128)} %gram_step.9.gram_ref, f32[16,128,1024]{2,1,0:T(8,128)} %get-tuple-element.28.moved_hbm, bf16[4,16,16,1024]{3,2,1,0:T(8,128)(2,1)} %bitcast.13, bf16[4,32,16,1024]{3,2,1,0:T(8,128)(2,1)} %bitcast.9, ...), custom_call_target="tpu_custom_call" | custom-call | bytes 40590000 | tf_op jit(solution)/shard_map/polar_step/pallas_call | solution.py:344
  (13 shorter events, 0.0 us)
Async XLA Ops:
  13.0 62.8 %all-to-all-start.1 = ((bf16[8,2,16,16,128]{4,3,2,1,0:T(8,128)(2,1)}), bf16[8,2,16,16,128]{4,3,2,1,0:T(8,128)(2,1)S(1)}, u32[]{:S(2)}, u32[]{:S(2)}) async-start(bf16[8,2,16,16,128]{4,3,2,1,0:T(8,128)(2,1)} %first_transform.5.after_ref), calls=%async_computation.1 | async-start | bytes 2097152 | tf_op jit(solution)/shard_map/all_to_all | solution.py:397
  21.0 31.9 %collective-permute-start = (bf16[16,12,1024]{2,1,0:T(8,128)(2,1)S(1)}, bf16[16,12,1024]{2,1,0:T(8,128)(2,1)S(1)}, u32[]{:S(2)}, u32[]{:S(2)}) collective-permute-start(bf16[16,12,1024]{2,1,0:T(8,128)(2,1)S(1)} %get-tuple-element.17), channel_id=1, source_target_pairs={{0,4},{4,8},{8,12},{12,16},{16,20},{20,24},{24,28},{1,5},{5,9},{9,... | collective-permute-start | bytes 1179656 | tf_op jit(solution)/shard_map/ppermute | solution.py:365
  24.4 30.5 %collective-permute-start.1 = (bf16[16,12,1024]{2,1,0:T(8,128)(2,1)S(1)}, bf16[16,12,1024]{2,1,0:T(8,128)(2,1)S(1)}, u32[]{:S(2)}, u32[]{:S(2)}) collective-permute-start(bf16[16,12,1024]{2,1,0:T(8,128)(2,1)S(1)} %get-tuple-element.18), channel_id=1, source_target_pairs={{4,0},{8,4},{12,8},{16,12},{20,16},{24,20},{28,24},{5,1},{9,5},{13... | collective-permute-start | bytes 1179656 | tf_op jit(solution)/shard_map/ppermute | solution.py:366
  75.9 7.0 %copy-start.3 = (bf16[8,2,16,16,128]{4,3,2,1,0:T(8,128)(2,1)}, bf16[8,2,16,16,128]{4,3,2,1,0:T(8,128)(2,1)S(1)}, u32[]{:S(2)}) copy-start(bf16[8,2,16,16,128]{4,3,2,1,0:T(8,128)(2,1)S(1)} %all-to-all-done.1.half_ref) | copy-start | bytes 3145732
  75.9 52.0 %all-to-all-start = ((bf16[8,2,16,32,128]{4,3,2,1,0:T(8,128)(2,1)}), bf16[8,2,16,32,128]{4,3,2,1,0:T(8,128)(2,1)S(1)}, u32[]{:S(2)}, u32[]{:S(2)}) async-start(bf16[8,2,16,32,128]{4,3,2,1,0:T(8,128)(2,1)} %first_transform.6.after_ref), calls=%async_computation | async-start | bytes 4194304 | tf_op jit(solution)/shard_map/all_to_all | solution.py:397
  82.8 60.4 %all-gather.11.cloned.1.call-start = ((), (), s32[]{:S(2)}) async-start(), calls=%async_computation.5 | async-start | bytes 2621440 | tf_op jit(solution)/shard_map/all_gather | solution.py:406
  88.4 115.4 %all-gather.13.cloned.1.call-start = ((), (), s32[]{:S(2)}) async-start(), calls=%async_computation.6 | async-start | bytes 5242880 | tf_op jit(solution)/shard_map/all_gather | solution.py:406
  127.8 1.3 copy-start
  136.3 52.1 %all-to-all-start.2 = ((bf16[8,2,16,32,128]{4,3,2,1,0:T(8,128)(2,1)}), bf16[8,2,16,32,128]{4,3,2,1,0:T(8,128)(2,1)S(1)}, u32[]{:S(2)}, u32[]{:S(2)}) async-start(bf16[8,2,16,32,128]{4,3,2,1,0:T(8,128)(2,1)} %first_transform.7.after_ref), calls=%async_computation.2 | async-start | bytes 4194304 | tf_op jit(solution)/shard_map/all_to_all | solution.py:397
  143.2 121.1 %all-gather.15.cloned.1.call-start = ((), (), s32[]{:S(2)}) async-start(), calls=%async_computation.7 | async-start | bytes 5242880 | tf_op jit(solution)/shard_map/all_gather | solution.py:406
  188.4 1.3 copy-start.1
  196.9 52.1 %all-to-all-start.3 = ((bf16[8,2,16,32,128]{4,3,2,1,0:T(8,128)(2,1)}), bf16[8,2,16,32,128]{4,3,2,1,0:T(8,128)(2,1)S(1)}, u32[]{:S(2)}, u32[]{:S(2)}) async-start(bf16[8,2,16,32,128]{4,3,2,1,0:T(8,128)(2,1)} %first_transform.8.after_ref), calls=%async_computation.3 | async-start | bytes 4194304 | tf_op jit(solution)/shard_map/all_to_all | solution.py:397
  203.8 91.1 %all-gather.17.cloned.1.call-start = ((), (), s32[]{:S(2)}) async-start(), calls=%async_computation.8 | async-start | bytes 5242880 | tf_op jit(solution)/shard_map/all_gather | solution.py:406
  248.9 1.3 copy-start.2
  257.5 29.6 %all-to-all-start.4 = ((bf16[8,2,16,16,128]{4,3,2,1,0:T(8,128)(2,1)}), bf16[8,2,16,16,128]{4,3,2,1,0:T(8,128)(2,1)S(1)}, u32[]{:S(2)}, u32[]{:S(2)}) async-start(bf16[8,2,16,16,128]{4,3,2,1,0:T(8,128)(2,1)} %first_transform.9.after_ref), calls=%async_computation.4 | async-start | bytes 2097152 | tf_op jit(solution)/shard_map/all_to_all | solution.py:397
  264.4 53.8 %all-gather.19.cloned.1.call-start = ((), (), s32[]{:S(2)}) async-start(), calls=%async_computation.9 | async-start | bytes 2621440 | tf_op jit(solution)/shard_map/all_gather | solution.py:406
  287.1 1.0 copy-start.4
Sparse Core Ops, SparseCore 0:
  88.5 23.4 all-gather.10
  136.4 36.2 all-gather.12
  197.0 36.2 all-gather.14
  257.6 36.2 all-gather.16
  295.3 22.8 all-gather.18

commit v4 on v3

--- a/solution.py
+++ b/solution.py
@@ -10,26 +10,23 @@
 from jax.sharding import PartitionSpec as P
 
 NS_ITERS = 5
-SMALL_ROWS = 16
-LARGE_ROWS = 32
+EDGE_ROWS = 16
 GRAM_ROWS = 4
 POLAR_ROWS = 8
 HIGHEST = lax.Precision.HIGHEST
 F32 = jnp.float32
 BF16 = jnp.bfloat16
-VMEM_LIMIT = 60 << 20
-BYTES_PER_US = 3690000
+MIB = 1 << 20
 
 ANY = pl.BlockSpec(memory_space=pl.ANY)
 SMEM = pl.BlockSpec(memory_space=pltpu.SMEM)
 
 
-def kernel_params():
-    return pltpu.CompilerParams(vmem_limit_bytes=VMEM_LIMIT)
-
-
-def cost(micros):
-    return pl.CostEstimate(flops=0, bytes_accessed=int(micros * BYTES_PER_US), transcendentals=0)
+def kernel_params(mebibytes):
+    return pltpu.CompilerParams(vmem_limit_bytes=mebibytes * MIB)
+
+
+COST = pl.CostEstimate(flops=0, bytes_accessed=1 << 16, transcendentals=0)
 
 
 def dot_nt(a, b, precision=None):
@@ -60,10 +57,10 @@
 
 
 def chunk_rows(own_rows):
-    large = [(first, LARGE_ROWS) for first in range(2 * SMALL_ROWS, own_rows - LARGE_ROWS + 1, LARGE_ROWS)]
-    covered = 2 * SMALL_ROWS + LARGE_ROWS * len(large)
-    rest = [(first, SMALL_ROWS) for first in range(covered, own_rows, SMALL_ROWS)]
-    return [(0, SMALL_ROWS)] + large + rest + [(SMALL_ROWS, SMALL_ROWS)]
+    inner = own_rows - 2 * EDGE_ROWS
+    pieces = 2 if inner >= 4 * EDGE_ROWS and inner % (2 * EDGE_ROWS) == 0 else 1
+    sizes = [EDGE_ROWS] + [inner // pieces] * pieces + [EDGE_ROWS]
+    return [sum(sizes[:place]) for place in range(len(sizes))], sizes
 
 
 def first_body(table_ref, grid_ref, after_ref, out_ref):
@@ -104,8 +101,8 @@
         ],
         out_specs=pl.BlockSpec((strips, 2, block, rows, width), lambda i: (0, 0, i, 0, 0)),
         out_shape=jax.ShapeDtypeStruct(shape, BF16),
-        compiler_params=kernel_params(),
-        cost_estimate=cost(4 + rows // 6),
+        compiler_params=kernel_params(28),
+        cost_estimate=COST,
         name="first_transform",
     )(table, grid, after)
 
@@ -130,8 +127,11 @@
     return total
 
 
-def base_body(levels, taps, reach, strips, strip_ref, step_ref, highpass_ref, model_ref, edge_ref, after_ref, out_ref, high, low):
+def base_body(levels, taps, starts, strips, strip_ref, step_ref, highpass_ref, model_ref, edge_ref, after_ref, *refs):
+    high, low = refs[-2:]
+    out_refs = refs[:-2]
     block, own_rows, side_len = model_ref.shape
+    reach = edge_ref.shape[1] // 2
 
     @pl.when(pl.program_id(0) == 0)
     def _():
@@ -158,17 +158,19 @@
         gradient = dot_nn(high[...], whole)
         gradient = gradient + dot_nn(low[...], whole)
         gradient = gradient + dot_nn(high[:, :own_rows], rest)
-        out_ref[chan] = model - step_ref[first + chan] * gradient
-
-
-def base_step(strip, strips, step_size, highpass, model_image, edges, after):
+        base = model - step_ref[first + chan] * gradient
+        for start, out_ref in zip(starts, out_refs):
+            out_ref[chan] = base[start : start + out_ref.shape[1]]
+
+
+def base_step(strip, strips, step_size, highpass, model_image, edges, starts, sizes, after):
     chans, rows, side_len = model_image.shape
     levels, taps = highpass.shape
     reach = edges.shape[1] // 2
     block = 2 if chans % 2 == 0 else 1
     wide = rows + 2 * reach
     return pl.pallas_call(
-        functools.partial(base_body, levels, taps, reach, strips),
+        functools.partial(base_body, levels, taps, starts, strips),
         grid=(chans // block,),
         in_specs=[
             SMEM,
@@ -178,11 +180,11 @@
             pl.BlockSpec((block, 2 * reach, side_len), lambda i: (i, 0, 0)),
             ANY,
         ],
-        out_specs=pl.BlockSpec((block, rows, side_len), lambda i: (i, 0, 0)),
-        out_shape=jax.ShapeDtypeStruct(model_image.shape, F32),
+        out_specs=[pl.BlockSpec((block, part, side_len), lambda i: (i, 0, 0)) for part in sizes],
+        out_shape=[jax.ShapeDtypeStruct((chans, part, side_len), F32) for part in sizes],
         scratch_shapes=[pltpu.VMEM((rows, wide), BF16), pltpu.VMEM((rows, wide), BF16)],
-        compiler_params=kernel_params(),
-        cost_estimate=cost(9),
+        compiler_params=kernel_params(20),
+        cost_estimate=COST,
         name="base_step",
     )(strip, step_size, highpass, model_image, edges, after)
 
@@ -200,18 +202,16 @@
     pixels_ref[...] = jnp.swapaxes(jnp.stack(pieces), 0, 1).astype(BF16)
 
 
-def second_transform(step_size, half, cosine, sine_table, base, first_row, after):
+def second_transform(step_size, half, cosine, sine_table, base, after):
     strips, _, chans, rows, width = half.shape
     side_len = cosine.shape[0]
     if width % 128 or rows % 16 or chans % 16:
         split = (strips, width, side_len)
         dirty = jnp.einsum("scmu,sul->cml", half[:, 0], cosine.reshape(split), preferred_element_type=F32)
         dirty = dirty - jnp.einsum("scmu,sul->cml", half[:, 1], sine_table.reshape(split), preferred_element_type=F32)
-        moved = base[:, first_row : first_row + rows] + step_size[:, None, None] * dirty
-        pixels = moved.astype(BF16).transpose(1, 0, 2)
-        return lax.dynamic_update_slice(base, moved, (0, first_row, 0)), pixels
+        moved = base + step_size[:, None, None] * dirty
+        return moved, moved.astype(BF16).transpose(1, 0, 2)
     block = min(256, side_len)
-    place = first_row // rows
     return pl.pallas_call(
         second_body,
         grid=(side_len // block,),
@@ -220,20 +220,19 @@
             pl.BlockSpec(half.shape, lambda i: (0, 0, 0, 0, 0)),
             pl.BlockSpec((side_len, block), lambda i: (0, i)),
             pl.BlockSpec((side_len, block), lambda i: (0, i)),
-            pl.BlockSpec((chans, rows, block), lambda i: (0, place, i)),
+            pl.BlockSpec((chans, rows, block), lambda i: (0, 0, i)),
             ANY,
         ],
         out_specs=[
-            pl.BlockSpec((chans, rows, block), lambda i: (0, place, i)),
+            pl.BlockSpec((chans, rows, block), lambda i: (0, 0, i)),
             pl.BlockSpec((rows, chans, block), lambda i: (0, 0, i)),
         ],
         out_shape=[
             jax.ShapeDtypeStruct(base.shape, F32),
             jax.ShapeDtypeStruct((rows, chans, side_len), BF16),
         ],
-        input_output_aliases={4: 0},
-        compiler_params=kernel_params(),
-        cost_estimate=cost(2 + rows // 10),
+        compiler_params=kernel_params(24),
+        cost_estimate=COST,
         name="second_transform",
     )(step_size, half, cosine, sine_table, base, after)
 
@@ -242,37 +241,34 @@
     return jnp.concatenate([ref[first + i] for i in range(count) for ref in group_refs], axis=0)
 
 
-def gram_body(before_ref, after_ref, pixels_ref, total_ref):
-    groups, rows, _, _ = pixels_ref.shape
+def gram_body(groups, before_ref, after_ref, *refs):
+    total_ref = refs[groups]
 
     @pl.when(pl.program_id(0) == 0)
     def _():
         total_ref[...] = before_ref[...]
 
     total = total_ref[...]
-    for first in range(0, rows, GRAM_ROWS):
-        pixels = stacked([pixels_ref.at[group] for group in range(groups)], first, GRAM_ROWS)
+    for first in range(0, refs[0].shape[0], GRAM_ROWS):
+        pixels = stacked(refs[:groups], first, GRAM_ROWS)
         total = total + dot_nt(pixels, pixels)
     total_ref[...] = total
 
 
-def gram_step(pixels, before, after):
-    groups, rows, chans, side_len = pixels.shape
-    block = 8
+def gram_step(pieces, before, after):
+    rows, chans, side_len = pieces[0].shape
+    block = EDGE_ROWS // 2
+    spec = pl.BlockSpec((block, chans, side_len), lambda i: (i, 0, 0))
     return pl.pallas_call(
-        gram_body,
+        functools.partial(gram_body, len(pieces)),
         grid=(rows // block,),
-        in_specs=[
-            pl.BlockSpec(before.shape, lambda i: (0, 0)),
-            ANY,
-            pl.BlockSpec((groups, block, chans, side_len), lambda i: (0, i, 0, 0)),
-        ],
+        in_specs=[pl.BlockSpec(before.shape, lambda i: (0, 0)), ANY] + [spec] * len(pieces),
         out_specs=pl.BlockSpec(before.shape, lambda i: (0, 0)),
         out_shape=jax.ShapeDtypeStruct(before.shape, F32),
-        compiler_params=kernel_params(),
-        cost_estimate=cost(1 + rows // 16),
+        compiler_params=kernel_params(16),
+        cost_estimate=COST,
         name="gram_step",
-    )(before, after, pixels)
+    )(before, after, *pieces)
 
 
 def newton_schulz(gram):
@@ -289,30 +285,33 @@
     return inverse, frob_norm
 
 
-def polar_body(starts, sizes, shrink_ref, select_ref, gram_ref, moved_hbm, *refs):
+def polar_body(starts, sizes, groups, shrink_ref, gram_ref, *refs):
     chunks = len(sizes)
-    pixels_hbm = refs[:chunks]
-    out_hbm, moved, in_sems, moved_sems, out_sems = refs[chunks : chunks + 5]
-    pixels = refs[chunks + 5 :]
+    moved_hbm = refs[:chunks]
+    pixels_hbm = refs[chunks : chunks * (groups + 1)]
+    out_hbm, moved, pixel_sems, moved_sems, out_sems = refs[chunks * (groups + 1) : chunks * (groups + 1) + 5]
+    pixels = refs[chunks * (groups + 1) + 5 :]
     own, all_rows, side_len = moved.shape
-    groups = pixels[0].shape[0]
     size = pixels[0].shape[2] * groups
     moved_copies = []
     pixel_copies = []
     for chunk in range(chunks):
-        copy = pltpu.make_async_copy(pixels_hbm[chunk], pixels[chunk], in_sems.at[chunk])
-        copy.start()
-        pixel_copies.append(copy)
         part = pl.ds(starts[chunk], sizes[chunk])
-        copy = pltpu.make_async_copy(moved_hbm.at[:, part], moved.at[:, part], moved_sems.at[chunk])
-        copy.start()
-        moved_copies.append(copy)
+        copies = []
+        for group in range(groups):
+            place = chunk * groups + group
+            copies.append(pltpu.make_async_copy(pixels_hbm[place], pixels[chunk].at[group], pixel_sems.at[place]))
+        pixel_copies.append(copies)
+        moved_copies.append(pltpu.make_async_copy(moved_hbm[chunk], moved.at[:, part], moved_sems.at[chunk]))
+        for copy in copies + moved_copies[-1:]:
+            copy.start()
     gram = jnp.zeros((size, size), F32)
     for i in range(GRAM_ROWS):
         gram = gram + gram_ref[i * size : (i + 1) * size, i * size : (i + 1) * size]
     inverse, frob_norm = newton_schulz(gram)
     factor = shrink_ref[0] * jnp.sqrt(all_rows * side_len / frob_norm)
-    weights = dot_nt(select_ref[...], inverse, HIGHEST) * factor
+    select = (iota((own, size), 0) == iota((own, size), 1)).astype(F32)
+    weights = dot_nt(select, inverse, HIGHEST) * factor
     spread = POLAR_ROWS * own
     wide = POLAR_ROWS * size
     repeat = (iota((spread, own), 0) // POLAR_ROWS == iota((spread, own), 1)).astype(BF16)
@@ -323,7 +322,8 @@
     weights = jnp.where(keep, weights, 0.0).astype(BF16)
     out_copies = []
     for chunk in range(chunks):
-        pixel_copies[chunk].wait()
+        for copy in pixel_copies[chunk]:
+            copy.wait()
         moved_copies[chunk].wait()
         for step in range(sizes[chunk] // POLAR_ROWS):
             data = stacked([pixels[chunk].at[group] for group in range(groups)], step * POLAR_ROWS, POLAR_ROWS)
@@ -338,25 +338,28 @@
         copy.wait()
 
 
-def polar_step(shrinkage, select, gram, moved, gathered, starts):
+def polar_step(shrinkage, gram, moved, gathered, starts, sizes):
     chunks = len(gathered)
-    sizes = [pieces.shape[1] for pieces in gathered]
+    groups = len(gathered[0])
+    chans, _, side_len = moved[0].shape
+    shape = (chans, sum(sizes), side_len)
+    flat = [piece for pieces in gathered for piece in pieces]
     return pl.pallas_call(
-        functools.partial(polar_body, starts, sizes),
-        in_specs=[SMEM, pl.BlockSpec(memory_space=pltpu.VMEM), pl.BlockSpec(memory_space=pltpu.VMEM), ANY] + [ANY] * chunks,
+        functools.partial(polar_body, starts, sizes, groups),
+        in_specs=[SMEM, pl.BlockSpec(memory_space=pltpu.VMEM)] + [ANY] * (chunks + len(flat)),
         out_specs=ANY,
-        out_shape=jax.ShapeDtypeStruct(moved.shape, F32),
+        out_shape=jax.ShapeDtypeStruct(shape, F32),
         scratch_shapes=[
-            pltpu.VMEM(moved.shape, F32),
-            pltpu.SemaphoreType.DMA((chunks,)),
+            pltpu.VMEM(shape, F32),
+            pltpu.SemaphoreType.DMA((chunks * groups,)),
             pltpu.SemaphoreType.DMA((chunks,)),
             pltpu.SemaphoreType.DMA((chunks,)),
         ]
-        + [pltpu.VMEM(pieces.shape, BF16) for pieces in gathered],
-        compiler_params=kernel_params(),
-        cost_estimate=cost(11),
+        + [pltpu.VMEM((groups,) + pieces[0].shape, BF16) for pieces in gathered],
+        compiler_params=kernel_params(40),
+        cost_estimate=COST,
         name="polar_step",
-    )(shrinkage, select, gram, moved, *gathered)
+    )(shrinkage, gram, *moved, *flat)
 
 
 def neighbour_rows(model_image, reach):
@@ -367,11 +370,24 @@
     return jnp.concatenate([before, after], axis=1)
 
 
+def swap(value, axis, bits):
+    count = lax.axis_size(axis)
+    return lax.ppermute(value, axis, [(i, i ^ bits) for i in range(count)])
+
+
+def gather_channels(pixels):
+    devices = lax.axis_size("chan")
+    kept = [pixels] + [swap(pixels, "chan", bits) for bits in range(2, devices, 2)]
+    if devices == 1:
+        return kept
+    return kept + [swap(piece, "chan", 1) for piece in kept]
+
+
 def local(grid, model_image, step_size, highpass, shrinkage):
     chans, own_rows, side_len = model_image.shape
     strips = lax.axis_size("strip")
     size = chans * lax.axis_size("chan")
-    starts, sizes = zip(*chunk_rows(own_rows))
+    starts, sizes = chunk_rows(own_rows)
     chunks = len(sizes)
     strip = lax.axis_index("strip").astype(jnp.int32).reshape(1)
 
@@ -384,37 +400,35 @@
 
     levels, taps = highpass.shape
     reach = (taps - 1) * 2 ** (levels - 1)
-
-    halves = {}
+    edges = neighbour_rows(model_image, reach)
+
+    halves = []
+    moved = []
     gathered = []
     gram = jnp.zeros((GRAM_ROWS * size, GRAM_ROWS * size), F32)
     last = strip
-    moved = None
     for chunk in range(chunks + 1):
         if chunk < chunks:
             sent = first_transform(tables[chunk], grid, strips, last)
             last = sent
-            halves[chunk] = lax.all_to_all(sent, "strip", split_axis=0, concat_axis=0, tiled=True)
-        if chunk == 0:
-            edges = neighbour_rows(model_image, reach)
-            moved = base_step(strip, strips, step_size, highpass, model_image, edges, last)
-            last = moved
-        else:
+            halves.append(lax.all_to_all(sent, "strip", split_axis=0, concat_axis=0, tiled=True))
+        if chunk == 1:
+            bases = base_step(strip, strips, step_size, highpass, model_image, edges, starts, sizes, last)
+            last = bases[0]
+        if chunk >= 1:
             done = chunk - 1
-            moved, pixels = second_transform(step_size, halves[done], cosine, sine_table, moved, starts[done], last)
+            result, pixels = second_transform(step_size, halves[done], cosine, sine_table, bases[done], last)
             last = pixels
-            pixels = lax.all_gather(pixels, "chan", axis=0, tiled=False)
+            moved.append(result)
+            pieces = gather_channels(pixels)
             if chans % 16:
-                pixels = pixels.transpose(1, 0, 2, 3).reshape(1, sizes[done], size, side_len)
-            gathered.append(pixels)
-        if chunk > 1:
+                pieces = [jnp.concatenate(pieces, axis=1)]
+            gathered.append(pieces)
+        if chunk >= 2:
             gram = gram_step(gathered[chunk - 2], gram, last)
             last = gram
     gram = gram_step(gathered[-1], gram, last)
-
-    own = lax.axis_index("chan") * chans + jnp.arange(chans, dtype=jnp.int32)
-    select = (own[:, None] == jnp.arange(size, dtype=jnp.int32)[None, :]).astype(F32)
-    return polar_step(shrinkage, select, gram, moved, gathered, starts)
+    return polar_step(shrinkage, gram, moved, gathered, starts, sizes)
 
 
 def solution(mesh):

time: 344 us -> 326 us (0.948)
  Pallas kernels: 116 us -> 76.2 us
  local copies, waits for them, and re-layouts: 7.38 us -> 42.3 us
  between operations: 13.8 us -> 1.18 us
    all_to_all x5 -> x4, waiting for transfers between devices: 115 us -> 47.8 us  [local(): lax.all_to_all(sent, 'strip', split_axis=0, concat_axis=0, tiled=True)]
    ppermute x1, waiting for transfers between devices: 26.1 us -> 70.4 us  [neighbour_rows(): lax.ppermute(tail.astype(BF16), 'strip', [(i, i + 1) for i in range(ends)])]
    ppermute x0 -> x12, waiting for transfers between devices: none -> 40.8 us  [swap(): return lax.ppermute(value, axis, [(i, i ^ bits) for i in range(count)])]
    unnamed x10 -> x82, local copies, waits for them, and re-layouts: 4.93 us -> 40.5 us
    all_gather x5 -> x0, waiting for transfers between devices: 18.5 us -> none  [local(): pixels = lax.all_gather(pixels, 'chan', axis=0, tiled=False)]
    pallas_call x7 -> x6, Pallas kernels: 45 us -> 28.4 us  [the longest x4 13 us: gram_step(): pl.pallas_call(functools.partial(gram_body, len(pieces)), grid=(rows // b...]
    pallas_call x5 -> x4, Pallas kernels: 38.9 us -> 25.4 us  [first_transform(): pl.pallas_call(first_body, grid=(chans // block,), in_specs=[pl.BlockSpec...]
    pallas_call x5 -> x4, Pallas kernels: 32.6 us -> 22.4 us  [second_transform(): pl.pallas_call(second_body, grid=(side_len // block,), in_specs=[SMEM, pl...]
  transfers between devices with their start and end apart: 12 -> 18, of which waited for: 7 -> 8; matrix products, arithmetic and copies ran while one was open for 1% -> 1% of each run, Pallas kernels for 28% -> 19%
where the time goes in v4:
time: 326 us; the launch traced here: 320 us
  waiting for transfers between devices  161 us (49%)
  Pallas kernels  76.2 us (23%)
  local copies, waits for them, and re-layouts  42.3 us (13%)
  starting transfers between devices  39.3 us (12%)
    ppermute x1, waiting for transfers between devices, neighbour_rows(): lax.ppermute(tail.astype(BF16), 'strip', [(i, i + 1) for i in range(ends)])  70.4 us
    all_to_all x4, waiting for transfers between devices, local(): lax.all_to_all(sent, 'strip', split_axis=0, concat_axis=0, tiled=True)  47.8 us
    ppermute x12, waiting for transfers between devices, swap(): return lax.ppermute(value, axis, [(i, i ^ bits) for i in range(count)])  40.8 us
    unnamed x82, local copies, waits for them, and re-layouts  40.5 us
    all_to_all x4, starting transfers between devices, local(): lax.all_to_all(sent, 'strip', split_axis=0, concat_axis=0, tiled=True)  27 us
    pallas_call x4, Pallas kernels, first_transform(): pl.pallas_call(first_body, grid=(chans // block,), in_specs=[pl.BlockSpec...  25.4 us
    pallas_call x4, Pallas kernels, second_transform(): pl.pallas_call(second_body, grid=(side_len // block,), in_specs=[SMEM, pl...  22.4 us
    pallas_call x4, Pallas kernels, gram_step(): pl.pallas_call(functools.partial(gram_body, len(pieces)), grid=(rows // b...  13 us
  transfers between devices with their start and end apart: 18, of which 8 were waited for; matrix products, arithmetic and copies ran while one was open for 1% of the time, Pallas kernels for 19%

profile of v4, /device:TPU:12, one launch (start us, length us, event | category | flops | bytes accessed | tf_op | source)
XLA Modules:
  0.0 320.1 jit_solution(3301265712503032355)
XLA Ops:
  0.0 3.4 %copy-done = bf16[2,16,128,1024]{3,2,1,0:T(8,128)(2,1)S(1)} copy-done((bf16[2,16,128,1024]{3,2,1,0:T(8,128)(2,1)S(1)}, bf16[2,16,128,1024]{3,2,1,0:T(8,128)(2,1)}, u32[]{:S(2)}) %copy-start) | copy-done | bytes 8388632
  3.4 1.0 copy-done.36
  4.4 4.3 %first_transform.4.after_ref = bf16[8,2,16,16,128]{4,3,2,1,0:T(8,128)(2,1)} custom-call(bf16[256,1024]{1,0:T(8,128)(2,1)S(1)} %copy-done.36, bf16[2,16,128,1024]{3,2,1,0:T(8,128)(2,1)S(1)} %copy-done, s32[1]{0:T(128)} %bitcast.after_ref.strip_ref), custom_call_target="tpu_custom_call" | custom-call | bytes 65536 | tf_op jit(solution)/shard_map/first_transform/pallas_call | solution.py:94
  8.7 6.4 %all-to-all-start.1 = ((bf16[8,2,16,16,128]{4,3,2,1,0:T(8,128)(2,1)}), bf16[8,2,16,16,128]{4,3,2,1,0:T(8,128)(2,1)S(1)}, u32[]{:S(2)}, u32[]{:S(2)}) async-start(bf16[8,2,16,16,128]{4,3,2,1,0:T(8,128)(2,1)} %first_transform.4.after_ref), calls=%async_computation.1 | async-start | bytes 2097152 | tf_op jit(solution)/shard_map/all_to_all | solution.py:414
  15.1 3.4 %copy-done.1 = bf16[2,16,128,1024]{3,2,1,0:T(8,128)(2,1)S(1)} copy-done((bf16[2,16,128,1024]{3,2,1,0:T(8,128)(2,1)S(1)}, bf16[2,16,128,1024]{3,2,1,0:T(8,128)(2,1)}, u32[]{:S(2)}) %copy-start.1) | copy-done | bytes 8388632
  18.5 8.8 %first_transform.5.after_ref = bf16[8,2,16,48,128]{4,3,2,1,0:T(8,128)(2,1)} custom-call(bf16[768,1024]{1,0:T(8,128)(2,1)S(1)} %copy-done.29, bf16[2,16,128,1024]{3,2,1,0:T(8,128)(2,1)S(1)} %copy-done.1, bf16[8,2,16,16,128]{4,3,2,1,0:T(8,128)(2,1)} %first_transform.4.after_ref), custom_call_target="tpu_custom_call" | custom-call | bytes 65536 | tf_op jit(solution)/shard_map/first_transform/pallas_call | solution.py:94
  27.3 10.3 %all-to-all-done.1.half_ref = bf16[8,2,16,16,128]{4,3,2,1,0:T(8,128)(2,1)S(1)} async-done(((bf16[8,2,16,16,128]{4,3,2,1,0:T(8,128)(2,1)}), bf16[8,2,16,16,128]{4,3,2,1,0:T(8,128)(2,1)S(1)}, u32[]{:S(2)}, u32[]{:S(2)}) %all-to-all-start.1) | async-done | bytes 1048608 | tf_op jit(solution)/shard_map/all_to_all | solution.py:414
  38.5 7.7 %all-to-all-start = ((bf16[8,2,16,48,128]{4,3,2,1,0:T(8,128)(2,1)}), bf16[8,2,16,48,128]{4,3,2,1,0:T(8,128)(2,1)}, u32[]{:S(2)}, u32[]{:S(2)}) async-start(bf16[8,2,16,48,128]{4,3,2,1,0:T(8,128)(2,1)} %first_transform.5.after_ref), calls=%async_computation | async-start | bytes 6291456 | tf_op jit(solution)/shard_map/all_to_all | solution.py:414
  46.2 1.8 fusion
  48.0 3.4 %collective-permute-start = (bf16[16,12,1024]{2,1,0:T(8,128)(2,1)S(1)}, bf16[16,12,1024]{2,1,0:T(8,128)(2,1)S(1)}, u32[]{:S(2)}, u32[]{:S(2)}) collective-permute-start(bf16[16,12,1024]{2,1,0:T(8,128)(2,1)S(1)} %get-tuple-element.19), channel_id=1, source_target_pairs={{0,4},{4,8},{8,12},{12,16},{16,20},{20,24},{24,28},{1,5},{5,9},{9,... | collective-permute-start | bytes 1179656 | tf_op jit(solution)/shard_map/ppermute | solution.py:368
  51.3 2.5 collective-permute-start.1
  53.8 70.4 %collective-permute-done = bf16[16,12,1024]{2,1,0:T(8,128)(2,1)S(1)} collective-permute-done((bf16[16,12,1024]{2,1,0:T(8,128)(2,1)S(1)}, bf16[16,12,1024]{2,1,0:T(8,128)(2,1)S(1)}, u32[]{:S(2)}, u32[]{:S(2)}) %collective-permute-start) | collective-permute-done | bytes 393248 | tf_op jit(solution)/shard_map/ppermute | solution.py:368
  124.2 1.9 collective-permute-done.1
  126.4 3.5 %copy-done.10 = f32[16,128,1024]{2,1,0:T(8,128)S(1)} copy-done((f32[16,128,1024]{2,1,0:T(8,128)S(1)}, f32[16,128,1024]{2,1,0:T(8,128)}, u32[]{:S(2)}) %copy-start.10) | copy-done | bytes 8388632
  129.9 5.8 %base_step.1 = (f32[16,16,1024]{2,1,0:T(8,128)S(1)}, f32[16,48,1024]{2,1,0:T(8,128)S(1)}, f32[16,48,1024]{2,1,0:T(8,128)S(1)}, f32[16,16,1024]{2,1,0:T(8,128)S(1)}) custom-call(s32[1]{0:T(128)} %bitcast.after_ref.strip_ref, f32[16]{0:T(128)S(1)} %copy-done.37, f32[3,4]{1,0:T(4,128)S(1)} %copy-done.38, f32[16,128,1024]{2,1,0:T(8,128)S(1)} %copy-done.10, ...), custom_call_target="tpu_custom_call" | custom-call | bytes 65536 | tf_op jit(solution)/shard_map/base_step/pallas_call | solution.py:172
  135.8 1.6 copy-done.21
  138.4 3.1 second_transform.4
  142.5 8.0 %first_transform.6.after_ref = bf16[8,2,16,48,128]{4,3,2,1,0:T(8,128)(2,1)S(1)} custom-call(bf16[768,1024]{1,0:T(8,128)(2,1)S(1)} %copy-done.30, bf16[2,16,128,1024]{3,2,1,0:T(8,128)(2,1)S(1)} %bitcast.2, bf16[16,16,1024]{2,1,0:T(8,128)(2,1)S(1)} %get-tuple-element.23.after_ref.refs_0_.refs_4_), custom_call_target="tpu_custom_call" | custom-call | bytes 65536 | tf_op jit(solution)/shard_map/first_transform/pallas_call | solution.py:94
  150.5 1.7 copy-done.8
  152.3 4.4 %all-to-all-start.2 = ((bf16[8,2,16,48,128]{4,3,2,1,0:T(8,128)(2,1)}), bf16[8,2,16,48,128]{4,3,2,1,0:T(8,128)(2,1)}, u32[]{:S(2)}, u32[]{:S(2)}) async-start(bf16[8,2,16,48,128]{4,3,2,1,0:T(8,128)(2,1)} %copy-done.8), calls=%async_computation.2 | async-start | bytes 6291456 | tf_op jit(solution)/shard_map/all_to_all | solution.py:414
  156.7 1.6 collective-permute-start.2
  158.3 1.6 copy-done.5
  159.8 1.9 copy-done.9
  161.7 1.9 copy-done.22
  163.6 7.8 %second_transform.5 = (f32[16,48,1024]{2,1,0:T(8,128)S(1)}, bf16[48,16,1024]{2,1,0:T(8,128)(2,1)}) custom-call(f32[16]{0:T(128)S(1)} %copy-done.37, bf16[8,2,16,48,128]{4,3,2,1,0:T(8,128)(2,1)} %all-to-all-done.half_ref, bf16[1024,1024]{1,0:T(8,128)(2,1)S(1)} %copy-done.5, bf16[1024,1024]{1,0:T(8,128)(2,1)S(1)} %copy-done.3, f32[16,48,1024]{2,1,0:T(8,128)S(1)} %copy-done.22, ...), custom_call_target="tpu_custom_call" | custom-call | bytes 65536 | tf_op jit(solution)/shard_map/second_transform/pallas_call | solution.py:215
  171.4 1.6 copy-done.17
  174.1 1.4 collective-permute-done.3.refs_2_.refs_6_
  176.3 1.0 gram_step.4.after_ref.before_ref
  178.9 3.4 %copy-done.2 = bf16[2,16,128,1024]{3,2,1,0:T(8,128)(2,1)S(1)} copy-done((bf16[2,16,128,1024]{3,2,1,0:T(8,128)(2,1)S(1)}, bf16[2,16,128,1024]{3,2,1,0:T(8,128)(2,1)}, u32[]{:S(2)}) %copy-start.2) | copy-done | bytes 8388632
  182.3 4.3 %first_transform.7.after_ref = bf16[8,2,16,16,128]{4,3,2,1,0:T(8,128)(2,1)} custom-call(bf16[256,1024]{1,0:T(8,128)(2,1)S(1)} %copy-done.35, bf16[2,16,128,1024]{3,2,1,0:T(8,128)(2,1)S(1)} %copy-done.2, f32[256,256]{1,0:T(8,128)S(1)} %gram_step.4.after_ref.before_ref), custom_call_target="tpu_custom_call" | custom-call | bytes 65536 | tf_op jit(solution)/shard_map/first_transform/pallas_call | solution.py:94
  186.6 37.5 %all-to-all-done.2.half_ref = bf16[8,2,16,48,128]{4,3,2,1,0:T(8,128)(2,1)} async-done(((bf16[8,2,16,48,128]{4,3,2,1,0:T(8,128)(2,1)}), bf16[8,2,16,48,128]{4,3,2,1,0:T(8,128)(2,1)}, u32[]{:S(2)}, u32[]{:S(2)}) %all-to-all-start.2) | async-done | bytes 3145760 | tf_op jit(solution)/shard_map/all_to_all | solution.py:414
  224.1 1.6 copy-done.6
  225.7 1.9 copy-done.20
  227.6 7.8 %second_transform.6 = (f32[16,48,1024]{2,1,0:T(8,128)S(1)}, bf16[48,16,1024]{2,1,0:T(8,128)(2,1)}) custom-call(f32[16]{0:T(128)S(1)} %copy-done.37, bf16[8,2,16,48,128]{4,3,2,1,0:T(8,128)(2,1)} %all-to-all-done.2.half_ref, bf16[1024,1024]{1,0:T(8,128)(2,1)S(1)} %copy-done.6, bf16[1024,1024]{1,0:T(8,128)(2,1)S(1)} %copy-done.3, ...), custom_call_target="tpu_custom_call" | custom-call | bytes 65536 | tf_op jit(solution)/shard_map/second_transform/pallas_call | solution.py:215
  235.4 1.7 copy-done.18
  237.1 1.5 collective-permute-start.8
  238.6 8.5 %all-to-all-start.3 = ((bf16[8,2,16,16,128]{4,3,2,1,0:T(8,128)(2,1)}), bf16[8,2,16,16,128]{4,3,2,1,0:T(8,128)(2,1)}, u32[]{:S(2)}, u32[]{:S(2)}) async-start(bf16[8,2,16,16,128]{4,3,2,1,0:T(8,128)(2,1)} %first_transform.7.after_ref), calls=%async_computation.3 | async-start | bytes 2097152 | tf_op jit(solution)/shard_map/all_to_all | solution.py:414
  247.7 26.0 %collective-permute-done.8.refs_1_.refs_13_ = bf16[48,16,1024]{2,1,0:T(8,128)(2,1)} collective-permute-done((bf16[48,16,1024]{2,1,0:T(8,128)(2,1)}, bf16[48,16,1024]{2,1,0:T(8,128)(2,1)}, u32[]{:S(2)}, u32[]{:S(2)}) %collective-permute-start.8) | collective-permute-done | bytes 1572896 | tf_op jit(solution)/shard_map/ppermute | solution.py:375
  273.7 5.1 %gram_step.5.after_ref.before_ref = f32[256,256]{1,0:T(8,128)S(1)} custom-call(f32[256,256]{1,0:T(8,128)S(1)} %gram_step.4.after_ref.before_ref, bf16[48,16,1024]{2,1,0:T(8,128)(2,1)} %get-tuple-element.26.after_ref.refs_0_.refs_12_, bf16[48,16,1024]{2,1,0:T(8,128)(2,1)} %get-tuple-element.24.after_ref.refs_0_.refs_8_, ...), custom_call_target="tpu_custom_call" | custom-call | bytes 65536 | tf_op jit(solution)/shard_map/gram_step/pallas_call | solution.py:262
  278.9 1.1 copy-done.11
  280.0 1.2 copy-done.13
  281.2 1.6 copy-done.7
  282.8 1.2 copy-done.34
  284.0 3.7 %second_transform.7 = (f32[16,16,1024]{2,1,0:T(8,128)S(1)}, bf16[16,16,1024]{2,1,0:T(8,128)(2,1)S(1)}) custom-call(f32[16]{0:T(128)S(1)} %copy-done.37, bf16[8,2,16,16,128]{4,3,2,1,0:T(8,128)(2,1)} %all-to-all-done.3.half_ref, bf16[1024,1024]{1,0:T(8,128)(2,1)S(1)} %copy-done.7, bf16[1024,1024]{1,0:T(8,128)(2,1)S(1)} %copy-done.3, ...), custom_call_target="tpu_custom_call" | custom-call | bytes 65536 | tf_op jit(solution)/shard_map/second_transform/pallas_call | solution.py:215
  287.7 1.6 collective-permute-start.11
  289.5 12.6 %collective-permute-done.11.refs_1_.refs_17_ = bf16[16,16,1024]{2,1,0:T(8,128)(2,1)S(1)} collective-permute-done((bf16[16,16,1024]{2,1,0:T(8,128)(2,1)S(1)}, bf16[16,16,1024]{2,1,0:T(8,128)(2,1)S(1)}, u32[]{:S(2)}, u32[]{:S(2)}) %collective-permute-start.11) | collective-permute-done | bytes 524320 | tf_op jit(solution)/shard_map/ppermute | solution.py:375
  302.8 5.8 %gram_step.6.before_ref.after_ref = f32[256,256]{1,0:T(8,128)S(1)} custom-call(f32[256,256]{1,0:T(8,128)S(1)} %gram_step.5.after_ref.before_ref, bf16[16,16,1024]{2,1,0:T(8,128)(2,1)S(1)} %get-tuple-element.28.after_ref.refs_0_.refs_16_, bf16[48,16,1024]{2,1,0:T(8,128)(2,1)} %get-tuple-element.26.after_ref.refs_0_.refs_12_, ...), custom_call_target="tpu_custom_call" | custom-call | bytes 65536 | tf_op jit(solution)/shard_map/gram_step/pallas_call | solution.py:262
  310.3 9.6 %polar_step.1 = f32[16,128,1024]{2,1,0:T(8,128)} custom-call(f32[1]{0:T(128)S(6)} %copy.12.shrink_ref, f32[256,256]{1,0:T(8,128)S(1)} %gram_step.7.gram_ref, f32[16,16,1024]{2,1,0:T(8,128)S(1)} %copy-done.32, f32[16,48,1024]{2,1,0:T(8,128)} %copy-done.17, f32[16,48,1024]{2,1,0:T(8,128)} %copy-done.18, f32[16,16,1024]{2,1,0:T(8,128)S(1)} %get-tuple-element.32.refs_3_, ...), custom_call_target="tpu_custom_call" | custom-call | bytes 65536 | tf_op jit(solution)/shard_map/polar_step/pallas_call | solution.py:347
  (88 shorter events, 9.1 us)
Async XLA Ops:
  0.0 3.4 %copy-start = (bf16[2,16,128,1024]{3,2,1,0:T(8,128)(2,1)S(1)}, bf16[2,16,128,1024]{3,2,1,0:T(8,128)(2,1)}, u32[]{:S(2)}) copy-start(bf16[2,16,128,1024]{3,2,1,0:T(8,128)(2,1)} %grid_ref.7) | copy-start | bytes 25165828
  8.7 6.4 %copy-start.29 = (bf16[768,1024]{1,0:T(8,128)(2,1)S(1)}, bf16[768,1024]{1,0:T(8,128)(2,1)}, u32[]{:S(2)}) copy-start(bf16[768,1024]{1,0:T(8,128)(2,1)} %constant.21.clone.table_ref) | copy-start | bytes 4718596
  8.7 28.8 %all-to-all-start.1 = ((bf16[8,2,16,16,128]{4,3,2,1,0:T(8,128)(2,1)}), bf16[8,2,16,16,128]{4,3,2,1,0:T(8,128)(2,1)S(1)}, u32[]{:S(2)}, u32[]{:S(2)}) async-start(bf16[8,2,16,16,128]{4,3,2,1,0:T(8,128)(2,1)} %first_transform.4.after_ref), calls=%async_computation.1 | async-start | bytes 2097152 | tf_op jit(solution)/shard_map/all_to_all | solution.py:414
  15.1 3.4 %copy-start.1 = (bf16[2,16,128,1024]{3,2,1,0:T(8,128)(2,1)S(1)}, bf16[2,16,128,1024]{3,2,1,0:T(8,128)(2,1)}, u32[]{:S(2)}) copy-start(bf16[2,16,128,1024]{3,2,1,0:T(8,128)(2,1)} %grid_ref.7) | copy-start | bytes 25165828
  38.5 113.8 %all-to-all-start = ((bf16[8,2,16,48,128]{4,3,2,1,0:T(8,128)(2,1)}), bf16[8,2,16,48,128]{4,3,2,1,0:T(8,128)(2,1)}, u32[]{:S(2)}, u32[]{:S(2)}) async-start(bf16[8,2,16,48,128]{4,3,2,1,0:T(8,128)(2,1)} %first_transform.5.after_ref), calls=%async_computation | async-start | bytes 6291456 | tf_op jit(solution)/shard_map/all_to_all | solution.py:414
  46.2 80.2 %copy-start.37 = (f32[16]{0:T(128)S(1)}, f32[16]{0:T(128)}, u32[]{:S(2)}) copy-start(f32[16]{0:T(128)} %step_ref.9) | copy-start | bytes 196
  46.2 80.2 %copy-start.38 = (f32[3,4]{1,0:T(4,128)S(1)}, f32[3,4]{1,0:T(4,128)}, u32[]{:S(2)}) copy-start(f32[3,4]{1,0:T(4,128)} %highpass_ref.1) | copy-start | bytes 148
  48.0 76.3 %collective-permute-start = (bf16[16,12,1024]{2,1,0:T(8,128)(2,1)S(1)}, bf16[16,12,1024]{2,1,0:T(8,128)(2,1)S(1)}, u32[]{:S(2)}, u32[]{:S(2)}) collective-permute-start(bf16[16,12,1024]{2,1,0:T(8,128)(2,1)S(1)} %get-tuple-element.19), channel_id=1, source_target_pairs={{0,4},{4,8},{8,12},{12,16},{16,20},{20,24},{24,28},{1,5},{5,9},{9,... | collective-permute-start | bytes 1179656 | tf_op jit(solution)/shard_map/ppermute | solution.py:368
  51.3 74.8 %collective-permute-start.1 = (bf16[16,12,1024]{2,1,0:T(8,128)(2,1)S(1)}, bf16[16,12,1024]{2,1,0:T(8,128)(2,1)S(1)}, u32[]{:S(2)}, u32[]{:S(2)}) collective-permute-start(bf16[16,12,1024]{2,1,0:T(8,128)(2,1)S(1)} %get-tuple-element.20), channel_id=1, source_target_pairs={{4,0},{8,4},{12,8},{16,12},{20,16},{24,20},{28,24},{5,1},{9,5},{13... | collective-permute-start | bytes 1179656 | tf_op jit(solution)/shard_map/ppermute | solution.py:369
  126.1 16.4 %slice-start = ((s8[8388608]{0:T(1024)(128)(4,1)}), s8[4194304]{0:T(1024)(128)(4,1)S(1)}, s32[]{:S(2)}) async-start(s8[8388608]{0:T(1024)(128)(4,1)} %bitcast.1), calls=%async_computation.4 | async-start | bytes 8388608
  126.4 3.5 %copy-start.10 = (f32[16,128,1024]{2,1,0:T(8,128)S(1)}, f32[16,128,1024]{2,1,0:T(8,128)}, u32[]{:S(2)}) copy-start(f32[16,128,1024]{2,1,0:T(8,128)} %model_ref.1) | copy-start | bytes 25165828
  129.9 8.5 %copy-start.3 = (bf16[1024,1024]{1,0:T(8,128)(2,1)S(1)}, bf16[1024,1024]{1,0:T(8,128)(2,1)}, u32[]{:S(2)}) copy-start(bf16[1024,1024]{1,0:T(8,128)(2,1)} %constant.23.clone.sine_ref) | copy-start | bytes 6291460
  129.9 8.5 %copy-start.4 = (bf16[1024,1024]{1,0:T(8,128)(2,1)S(1)}, bf16[1024,1024]{1,0:T(8,128)(2,1)}, u32[]{:S(2)}) copy-start(bf16[1024,1024]{1,0:T(8,128)(2,1)} %constant.22.clone.cosine_ref) | copy-start | bytes 6291460
  129.9 8.5 %copy-start.16 = (bf16[8,2,16,16,128]{4,3,2,1,0:T(8,128)(2,1)S(1)}, bf16[8,2,16,16,128]{4,3,2,1,0:T(8,128)(2,1)}, u32[]{:S(2)}) copy-start(bf16[8,2,16,16,128]{4,3,2,1,0:T(8,128)(2,1)} %copy-done.15) | copy-start | bytes 3145732
  129.9 12.6 %slice-start.1 = ((s8[8388608]{0:T(1024)(128)(4,1)}), s8[4194304]{0:T(1024)(128)(4,1)S(1)}, s32[]{:S(2)}) async-start(s8[8388608]{0:T(1024)(128)(4,1)} %bitcast.1), calls=%async_computation.5 | async-start | bytes 8388608
  135.8 1.6 copy-start.21
  138.4 3.1 copy-start.19
  138.4 4.1 %copy-start.30 = (bf16[768,1024]{1,0:T(8,128)(2,1)S(1)}, bf16[768,1024]{1,0:T(8,128)(2,1)}, u32[]{:S(2)}) copy-start(bf16[768,1024]{1,0:T(8,128)(2,1)} %constant.24.clone.table_ref) | copy-start | bytes 4718596
  150.5 1.7 copy-start.8
  152.3 71.9 %all-to-all-start.2 = ((bf16[8,2,16,48,128]{4,3,2,1,0:T(8,128)(2,1)}), bf16[8,2,16,48,128]{4,3,2,1,0:T(8,128)(2,1)}, u32[]{:S(2)}, u32[]{:S(2)}) async-start(bf16[8,2,16,48,128]{4,3,2,1,0:T(8,128)(2,1)} %copy-done.8), calls=%async_computation.2 | async-start | bytes 6291456 | tf_op jit(solution)/shard_map/all_to_all | solution.py:414
  156.7 16.9 %collective-permute-start.2 = (bf16[16,16,1024]{2,1,0:T(8,128)(2,1)S(1)}, bf16[16,16,1024]{2,1,0:T(8,128)(2,1)S(1)}, u32[]{:S(2)}, u32[]{:S(2)}) collective-permute-start(bf16[16,16,1024]{2,1,0:T(8,128)(2,1)S(1)} %get-tuple-element.23.after_ref.refs_0_.refs_4_), channel_id=1, source_target_pairs={{0,2},{1,3},{2,0},{3,1},{4,6},{5,7},{6,4},{7,5},{8,10},{9,11},{10,... | collective-permute-start | bytes 1572872 | tf_op jit(solution)/shard_map/ppermute | solution.py:375
  158.3 1.6 copy-start.5
  159.8 1.9 copy-start.9
  161.7 1.9 copy-start.22
  171.4 1.6 copy-start.17
  173.1 74.0 %collective-permute-start.5 = (bf16[48,16,1024]{2,1,0:T(8,128)(2,1)}, bf16[48,16,1024]{2,1,0:T(8,128)(2,1)}, u32[]{:S(2)}, u32[]{:S(2)}) collective-permute-start(bf16[48,16,1024]{2,1,0:T(8,128)(2,1)} %get-tuple-element.24.after_ref.refs_0_.refs_8_), channel_id=1, source_target_pairs={{0,2},{1,3},{2,0},{3,1},{4,6},{5,7},{6,4},{7,5},{8,10},{9,11},{10,... | collective-permute-start | bytes 4718600 | tf_op jit(solution)/shard_map/ppermute | solution.py:375
  173.6 1.9 collective-permute-start.3
  173.6 3.7 %copy-start.23 = (bf16[16,16,1024]{2,1,0:T(8,128)(2,1)}, bf16[16,16,1024]{2,1,0:T(8,128)(2,1)S(1)}, u32[]{:S(2)}) copy-start(bf16[16,16,1024]{2,1,0:T(8,128)(2,1)S(1)} %collective-permute-done.2.refs_1_.refs_5_) | copy-start | bytes 1572868
  173.6 2.6 collective-permute-start.4
  176.3 2.7 copy-start.35
  178.9 3.4 %copy-start.2 = (bf16[2,16,128,1024]{3,2,1,0:T(8,128)(2,1)S(1)}, bf16[2,16,128,1024]{3,2,1,0:T(8,128)(2,1)}, u32[]{:S(2)}) copy-start(bf16[2,16,128,1024]{3,2,1,0:T(8,128)(2,1)} %grid_ref.7) | copy-start | bytes 25165828
  224.1 1.6 copy-start.6
  225.7 1.9 copy-start.20
  235.4 1.7 copy-start.18
  237.1 36.6 %collective-permute-start.8 = (bf16[48,16,1024]{2,1,0:T(8,128)(2,1)}, bf16[48,16,1024]{2,1,0:T(8,128)(2,1)}, u32[]{:S(2)}, u32[]{:S(2)}) collective-permute-start(bf16[48,16,1024]{2,1,0:T(8,128)(2,1)} %get-tuple-element.26.after_ref.refs_0_.refs_12_), channel_id=1, source_target_pairs={{0,2},{1,3},{2,0},{3,1},{4,6},{5,7},{6,4},{7,5},{8,10},{9,11},{10,... | collective-permute-start | bytes 4718600 | tf_op jit(solution)/shard_map/ppermute | solution.py:375
  238.6 42.6 %all-to-all-start.3 = ((bf16[8,2,16,16,128]{4,3,2,1,0:T(8,128)(2,1)}), bf16[8,2,16,16,128]{4,3,2,1,0:T(8,128)(2,1)}, u32[]{:S(2)}, u32[]{:S(2)}) async-start(bf16[8,2,16,16,128]{4,3,2,1,0:T(8,128)(2,1)} %first_transform.7.after_ref), calls=%async_computation.3 | async-start | bytes 2097152 | tf_op jit(solution)/shard_map/all_to_all | solution.py:414
  247.1 26.6 %collective-permute-start.6 = (bf16[48,16,1024]{2,1,0:T(8,128)(2,1)}, bf16[48,16,1024]{2,1,0:T(8,128)(2,1)S(1)}, u32[]{:S(2)}, u32[]{:S(2)}) collective-permute-start(bf16[48,16,1024]{2,1,0:T(8,128)(2,1)} %get-tuple-element.24.after_ref.refs_0_.refs_8_), channel_id=1, source_target_pairs={{0,1},{1,0},{2,3},{3,2},{4,5},{5,4},{6,7},{7,6},{8,9},{9,8},{10,11... | collective-permute-start | bytes 4718600 | tf_op jit(solution)/shard_map/ppermute | solution.py:375
  247.1 26.6 %collective-permute-start.7 = (bf16[48,16,1024]{2,1,0:T(8,128)(2,1)}, bf16[48,16,1024]{2,1,0:T(8,128)(2,1)S(1)}, u32[]{:S(2)}, u32[]{:S(2)}) collective-permute-start(bf16[48,16,1024]{2,1,0:T(8,128)(2,1)} %collective-permute-done.5.refs_1_.refs_9_), channel_id=1, source_target_pairs={{0,1},{1,0},{2,3},{3,2},{4,5},{5,4},{6,7},{7,6},{8,9},{9,8},{10,11... | collective-permute-start | bytes 4718600 | tf_op jit(solution)/shard_map/ppermute | solution.py:375
  247.6 55.2 %collective-permute-start.9 = (bf16[48,16,1024]{2,1,0:T(8,128)(2,1)}, bf16[48,16,1024]{2,1,0:T(8,128)(2,1)}, u32[]{:S(2)}, u32[]{:S(2)}) collective-permute-start(bf16[48,16,1024]{2,1,0:T(8,128)(2,1)} %get-tuple-element.26.after_ref.refs_0_.refs_12_), channel_id=1, source_target_pairs={{0,1},{1,0},{2,3},{3,2},{4,5},{5,4},{6,7},{7,6},{8,9},{9,8},{10,11... | collective-permute-start | bytes 4718600 | tf_op jit(solution)/shard_map/ppermute | solution.py:375
  273.7 29.1 %collective-permute-start.10 = (bf16[48,16,1024]{2,1,0:T(8,128)(2,1)}, bf16[48,16,1024]{2,1,0:T(8,128)(2,1)}, u32[]{:S(2)}, u32[]{:S(2)}) collective-permute-start(bf16[48,16,1024]{2,1,0:T(8,128)(2,1)} %collective-permute-done.8.refs_1_.refs_13_), channel_id=1, source_target_pairs={{0,1},{1,0},{2,3},{3,2},{4,5},{5,4},{6,7},{7,6},{8,9},{9,8},{10,11... | collective-permute-start | bytes 4718600 | tf_op jit(solution)/shard_map/ppermute | solution.py:375
  281.2 1.6 copy-start.7
  287.7 14.4 %collective-permute-start.11 = (bf16[16,16,1024]{2,1,0:T(8,128)(2,1)S(1)}, bf16[16,16,1024]{2,1,0:T(8,128)(2,1)S(1)}, u32[]{:S(2)}, u32[]{:S(2)}) collective-permute-start(bf16[16,16,1024]{2,1,0:T(8,128)(2,1)S(1)} %get-tuple-element.28.after_ref.refs_0_.refs_16_), channel_id=1, source_target_pairs={{0,2},{1,3},{2,0},{3,1},{4,6},{5,7},{6,4},{7,5},{8,10},{9,11},{10,... | collective-permute-start | bytes 1572872 | tf_op jit(solution)/shard_map/ppermute | solution.py:375
  289.3 19.4 %collective-permute-start.12 = (bf16[16,16,1024]{2,1,0:T(8,128)(2,1)S(1)}, bf16[16,16,1024]{2,1,0:T(8,128)(2,1)S(1)}, u32[]{:S(2)}, u32[]{:S(2)}) collective-permute-start(bf16[16,16,1024]{2,1,0:T(8,128)(2,1)S(1)} %get-tuple-element.28.after_ref.refs_0_.refs_16_), channel_id=1, source_target_pairs={{0,1},{1,0},{2,3},{3,2},{4,5},{5,4},{6,7},{7,6},{8,9},{9,8},{10,11... | collective-permute-start | bytes 1572872 | tf_op jit(solution)/shard_map/ppermute | solution.py:375
  302.1 6.6 %collective-permute-start.13 = (bf16[16,16,1024]{2,1,0:T(8,128)(2,1)S(1)}, bf16[16,16,1024]{2,1,0:T(8,128)(2,1)S(1)}, u32[]{:S(2)}, u32[]{:S(2)}) collective-permute-start(bf16[16,16,1024]{2,1,0:T(8,128)(2,1)S(1)} %collective-permute-done.11.refs_1_.refs_17_), channel_id=1, source_target_pairs={{0,1},{1,0},{2,3},{3,2},{4,5},{5,4},{6,7},{7,6},{8,9},{9,8},{10,11... | collective-permute-start | bytes 1572872 | tf_op jit(solution)/shard_map/ppermute | solution.py:375
  302.8 6.9 %copy-start.14 = (bf16[48,16,1024]{2,1,0:T(8,128)(2,1)S(1)}, bf16[48,16,1024]{2,1,0:T(8,128)(2,1)}, u32[]{:S(2)}) copy-start(bf16[48,16,1024]{2,1,0:T(8,128)(2,1)} %copy-done.13) | copy-start | bytes 4718596
  302.8 6.9 %copy-start.28 = (bf16[16,16,1024]{2,1,0:T(8,128)(2,1)S(1)}, bf16[16,16,1024]{2,1,0:T(8,128)(2,1)}, u32[]{:S(2)}) copy-start(bf16[16,16,1024]{2,1,0:T(8,128)(2,1)} %copy-done.27) | copy-start | bytes 1572868
  302.8 6.9 %copy-start.32 = (f32[16,16,1024]{2,1,0:T(8,128)S(1)}, f32[16,16,1024]{2,1,0:T(8,128)}, u32[]{:S(2)}) copy-start(f32[16,16,1024]{2,1,0:T(8,128)} %copy-done.31) | copy-start | bytes 3145732
  308.7 1.7 copy-start.26
  (11 other events, 12.1 us)

commit v5 on v4

--- a/solution.py
+++ b/solution.py
@@ -57,10 +57,25 @@
 
 
 def chunk_rows(own_rows):
-    inner = own_rows - 2 * EDGE_ROWS
-    pieces = 2 if inner >= 4 * EDGE_ROWS and inner % (2 * EDGE_ROWS) == 0 else 1
-    sizes = [EDGE_ROWS] + [inner // pieces] * pieces + [EDGE_ROWS]
+    sizes = [EDGE_ROWS, own_rows // 2, own_rows // 2 - 2 * EDGE_ROWS, EDGE_ROWS]
+    sizes = [size for size in sizes if size > 0]
     return [sum(sizes[:place]) for place in range(len(sizes))], sizes
+
+
+def gate_body(value_ref, after_ref, out_ref):
+    pass
+
+
+def gate(value, after):
+    return pl.pallas_call(
+        gate_body,
+        in_specs=[ANY, ANY],
+        out_specs=ANY,
+        out_shape=jax.ShapeDtypeStruct(value.shape, value.dtype),
+        input_output_aliases={0: 0},
+        cost_estimate=COST,
+        name="gate",
+    )(value, after)
 
 
 def first_body(table_ref, grid_ref, after_ref, out_ref):
@@ -101,7 +116,7 @@
         ],
         out_specs=pl.BlockSpec((strips, 2, block, rows, width), lambda i: (0, 0, i, 0, 0)),
         out_shape=jax.ShapeDtypeStruct(shape, BF16),
-        compiler_params=kernel_params(28),
+        compiler_params=kernel_params(60),
         cost_estimate=COST,
         name="first_transform",
     )(table, grid, after)
@@ -183,7 +198,7 @@
         out_specs=[pl.BlockSpec((block, part, side_len), lambda i: (i, 0, 0)) for part in sizes],
         out_shape=[jax.ShapeDtypeStruct((chans, part, side_len), F32) for part in sizes],
         scratch_shapes=[pltpu.VMEM((rows, wide), BF16), pltpu.VMEM((rows, wide), BF16)],
-        compiler_params=kernel_params(20),
+        compiler_params=kernel_params(60),
         cost_estimate=COST,
         name="base_step",
     )(strip, step_size, highpass, model_image, edges, after)
@@ -231,7 +246,7 @@
             jax.ShapeDtypeStruct(base.shape, F32),
             jax.ShapeDtypeStruct((rows, chans, side_len), BF16),
         ],
-        compiler_params=kernel_params(24),
+        compiler_params=kernel_params(60),
         cost_estimate=COST,
         name="second_transform",
     )(step_size, half, cosine, sine_table, base, after)
@@ -276,11 +291,11 @@
     frob_norm = jnp.sqrt(jnp.sum(gram * gram))
     identity = (iota((size, size), 0) == iota((size, size), 1)).astype(F32)
     current = gram / frob_norm
-    inverse = identity
-    for iteration in range(NS_ITERS):
+    middle = 0.5 * (3.0 * identity - current)
+    inverse = middle
+    for iteration in range(1, NS_ITERS):
+        current = dot_nn(current, middle, HIGHEST)
         middle = 0.5 * (3.0 * identity - dot_nn(inverse, current, HIGHEST))
-        if iteration + 1 < NS_ITERS:
-            current = dot_nn(current, middle, HIGHEST)
         inverse = dot_nn(middle, inverse, HIGHEST)
     return inverse, frob_norm
 
@@ -375,9 +390,11 @@
     return lax.ppermute(value, axis, [(i, i ^ bits) for i in range(count)])
 
 
-def gather_channels(pixels):
+def gather_channels(pixels, after=None):
     devices = lax.axis_size("chan")
     kept = [pixels] + [swap(pixels, "chan", bits) for bits in range(2, devices, 2)]
+    if after is not None:
+        kept = [pixels] + [gate(piece, after) for piece in kept[1:]]
     if devices == 1:
         return kept
     return kept + [swap(piece, "chan", 1) for piece in kept]
@@ -410,6 +427,8 @@
     for chunk in range(chunks + 1):
         if chunk < chunks:
             sent = first_transform(tables[chunk], grid, strips, last)
+            if chunk == 1:
+                sent = gate(sent, edges)
             last = sent
             halves.append(lax.all_to_all(sent, "strip", split_axis=0, concat_axis=0, tiled=True))
         if chunk == 1:
@@ -420,13 +439,13 @@
             result, pixels = second_transform(step_size, halves[done], cosine, sine_table, bases[done], last)
             last = pixels
             moved.append(result)
-            pieces = gather_channels(pixels)
+            if done >= 1:
+                gram = gram_step(gathered[done - 1], gram, last)
+                last = gram
+            pieces = gather_channels(pixels, gram if chunk == chunks else None)
             if chans % 16:
                 pieces = [jnp.concatenate(pieces, axis=1)]
             gathered.append(pieces)
-        if chunk >= 2:
-            gram = gram_step(gathered[chunk - 2], gram, last)
-            last = gram
     gram = gram_step(gathered[-1], gram, last)
     return polar_step(shrinkage, gram, moved, gathered, starts, sizes)
 

time: 326 us -> 328 us (level)
  local copies, waits for them, and re-layouts: 42.3 us -> 16 us
  Pallas kernels: 76.2 us -> 98.7 us
  waiting for transfers between devices: 161 us -> 170 us
    ppermute x1, waiting for transfers between devices: 70.4 us -> 13.3 us  [neighbour_rows(): lax.ppermute(tail.astype(BF16), 'strip', [(i, i + 1) for i in range(ends)])]
    ppermute x12, waiting for transfers between devices: 40.8 us -> 90.7 us  [swap(): return lax.ppermute(value, axis, [(i, i ^ bits) for i in range(count)])]
    unnamed x82 -> x50, local copies, waits for them, and re-layouts: 40.5 us -> 14.2 us
    all_to_all x4, waiting for transfers between devices: 47.8 us -> 64.6 us  [local(): lax.all_to_all(sent, 'strip', split_axis=0, concat_axis=0, tiled=True)]
    pallas_call x4, Pallas kernels: 25.4 us -> 34.2 us  [first_transform(): pl.pallas_call(first_body, grid=(chans // block,), in_specs=[pl.BlockSpec...]
    pallas_call x4, Pallas kernels: 22.4 us -> 29.6 us  [second_transform(): pl.pallas_call(second_body, grid=(side_len // block,), in_specs=[SMEM, pl...]
    pallas_call x1, Pallas kernels: 5.85 us -> 11.2 us  [base_step(): pl.pallas_call(functools.partial(base_body, levels, taps, starts, strips)...]
  transfers between devices with their start and end apart: 18 -> 18, of which waited for: 8 -> 8; matrix products, arithmetic and copies ran while one was open for 1% -> 1% of each run, Pallas kernels for 19% -> 25%
where the time goes in v5:
time: 328 us; the launch traced here: 325 us
  waiting for transfers between devices  170 us (52%)
  Pallas kernels  98.7 us (30%)
  starting transfers between devices  37.8 us (12%)
  local copies, waits for them, and re-layouts  16 us (5%)
    ppermute x12, waiting for transfers between devices, swap(): return lax.ppermute(value, axis, [(i, i ^ bits) for i in range(count)])  90.7 us
    all_to_all x4, waiting for transfers between devices, local(): lax.all_to_all(sent, 'strip', split_axis=0, concat_axis=0, tiled=True)  64.6 us
    pallas_call x4, Pallas kernels, first_transform(): pl.pallas_call(first_body, grid=(chans // block,), in_specs=[pl.BlockSpec...  34.2 us
    pallas_call x4, Pallas kernels, second_transform(): pl.pallas_call(second_body, grid=(side_len // block,), in_specs=[SMEM, pl...  29.6 us
    all_to_all x4, starting transfers between devices, local(): lax.all_to_all(sent, 'strip', split_axis=0, concat_axis=0, tiled=True)  26.2 us
    unnamed x50, local copies, waits for them, and re-layouts  14.2 us
    pallas_call x4, Pallas kernels, gram_step(): pl.pallas_call(functools.partial(gram_body, len(pieces)), grid=(rows // b...  13.9 us
    ppermute x1, waiting for transfers between devices, neighbour_rows(): lax.ppermute(tail.astype(BF16), 'strip', [(i, i + 1) for i in range(ends)])  13.3 us
  transfers between devices with their start and end apart: 18, of which 8 were waited for; matrix products, arithmetic and copies ran while one was open for 1% of the time, Pallas kernels for 25%

profile of v5, /device:TPU:12, one launch (start us, length us, event | category | flops | bytes accessed | tf_op | source)
XLA Modules:
  0.0 325.1 jit_solution(16804825010931106608)
XLA Ops:
  0.0 6.5 %first_transform.4.after_ref = bf16[8,2,16,16,128]{4,3,2,1,0:T(8,128)(2,1)} custom-call(bf16[256,1024]{1,0:T(8,128)(2,1)} %constant.20.clone.table_ref, bf16[2,16,128,1024]{3,2,1,0:T(8,128)(2,1)} %grid_ref.7, s32[1]{0:T(128)} %bitcast.after_ref.strip_ref), custom_call_target="tpu_custom_call" | custom-call | bytes 65536 | tf_op jit(solution)/shard_map/first_transform/pallas_call | solution.py:109
  6.5 6.2 %all-to-all-start.1 = ((bf16[8,2,16,16,128]{4,3,2,1,0:T(8,128)(2,1)}), bf16[8,2,16,16,128]{4,3,2,1,0:T(8,128)(2,1)S(1)}, u32[]{:S(2)}, u32[]{:S(2)}) async-start(bf16[8,2,16,16,128]{4,3,2,1,0:T(8,128)(2,1)} %first_transform.4.after_ref), calls=%async_computation.1 | async-start | bytes 2097152 | tf_op jit(solution)/shard_map/all_to_all | solution.py:433
  12.7 1.7 fusion
  14.5 3.4 %collective-permute-start = (bf16[16,12,1024]{2,1,0:T(8,128)(2,1)S(1)}, bf16[16,12,1024]{2,1,0:T(8,128)(2,1)S(1)}, u32[]{:S(2)}, u32[]{:S(2)}) collective-permute-start(bf16[16,12,1024]{2,1,0:T(8,128)(2,1)S(1)} %get-tuple-element.19), channel_id=1, source_target_pairs={{0,4},{4,8},{8,12},{12,16},{16,20},{20,24},{24,28},{1,5},{5,9},{9,... | collective-permute-start | bytes 1179656 | tf_op jit(solution)/shard_map/ppermute | solution.py:383
  17.9 2.5 collective-permute-start.1
  20.3 12.7 %first_transform.5.value_ref = bf16[8,2,16,64,128]{4,3,2,1,0:T(8,128)(2,1)} custom-call(bf16[1024,1024]{1,0:T(8,128)(2,1)} %constant.21.clone.table_ref, bf16[2,16,128,1024]{3,2,1,0:T(8,128)(2,1)} %grid_ref.7, bf16[8,2,16,16,128]{4,3,2,1,0:T(8,128)(2,1)} %first_transform.4.after_ref), custom_call_target="tpu_custom_call" | custom-call | bytes 65536 | tf_op jit(solution)/shard_map/first_transform/pallas_call | solution.py:109
  33.1 13.3 %collective-permute-done = bf16[16,12,1024]{2,1,0:T(8,128)(2,1)S(1)} collective-permute-done((bf16[16,12,1024]{2,1,0:T(8,128)(2,1)S(1)}, bf16[16,12,1024]{2,1,0:T(8,128)(2,1)S(1)}, u32[]{:S(2)}, u32[]{:S(2)}) %collective-permute-start) | collective-permute-done | bytes 393248 | tf_op jit(solution)/shard_map/ppermute | solution.py:383
  46.4 1.9 collective-permute-done.1
  48.3 1.1 pad_maximum_fusion.after_ref.edge_ref
  49.4 1.0 copy-done.24
  50.4 7.0 %all-to-all-start = ((bf16[8,2,16,64,128]{4,3,2,1,0:T(8,128)(2,1)}), bf16[8,2,16,64,128]{4,3,2,1,0:T(8,128)(2,1)}, u32[]{:S(2)}, u32[]{:S(2)}) async-start(bf16[8,2,16,64,128]{4,3,2,1,0:T(8,128)(2,1)} %gate.2.after_ref), calls=%async_computation | async-start | bytes 8388608 | tf_op jit(solution)/shard_map/all_to_all | solution.py:433
  57.4 11.2 %base_step.1 = (f32[16,16,1024]{2,1,0:T(8,128)}, f32[16,64,1024]{2,1,0:T(8,128)}, f32[16,32,1024]{2,1,0:T(8,128)}, f32[16,16,1024]{2,1,0:T(8,128)}) custom-call(s32[1]{0:T(128)} %bitcast.after_ref.strip_ref, f32[16]{0:T(128)} %step_ref.9, f32[3,4]{1,0:T(4,128)} %highpass_ref.1, f32[16,128,1024]{2,1,0:T(8,128)} %model_ref.1, ...), custom_call_target="tpu_custom_call" | custom-call | bytes 65536 | tf_op jit(solution)/shard_map/base_step/pallas_call | solution.py:187
  68.6 5.7 %second_transform.4 = (f32[16,16,1024]{2,1,0:T(8,128)}, bf16[16,16,1024]{2,1,0:T(8,128)(2,1)}) custom-call(f32[16]{0:T(128)} %step_ref.9, bf16[8,2,16,16,128]{4,3,2,1,0:T(8,128)(2,1)} %copy-done.24, bf16[1024,1024]{1,0:T(8,128)(2,1)} %constant.22.clone.cosine_ref, bf16[1024,1024]{1,0:T(8,128)(2,1)} %constant.23.clone.sine_ref, ...), custom_call_target="tpu_custom_call" | custom-call | bytes 65536 | tf_op jit(solution)/shard_map/second_transform/pallas_call | solution.py:230
  74.3 8.5 %first_transform.6.after_ref = bf16[8,2,16,32,128]{4,3,2,1,0:T(8,128)(2,1)} custom-call(bf16[512,1024]{1,0:T(8,128)(2,1)} %constant.24.clone.table_ref, bf16[2,16,128,1024]{3,2,1,0:T(8,128)(2,1)} %grid_ref.7, bf16[16,16,1024]{2,1,0:T(8,128)(2,1)} %get-tuple-element.23.after_ref.refs_0_.refs_4_), custom_call_target="tpu_custom_call" | custom-call | bytes 65536 | tf_op jit(solution)/shard_map/first_transform/pallas_call | solution.py:109
  82.8 64.6 %all-to-all-done.half_ref = bf16[8,2,16,64,128]{4,3,2,1,0:T(8,128)(2,1)} async-done(((bf16[8,2,16,64,128]{4,3,2,1,0:T(8,128)(2,1)}), bf16[8,2,16,64,128]{4,3,2,1,0:T(8,128)(2,1)}, u32[]{:S(2)}, u32[]{:S(2)}) %all-to-all-start) | async-done | bytes 4194336 | tf_op jit(solution)/shard_map/all_to_all | solution.py:433
  147.3 7.0 %all-to-all-start.2 = ((bf16[8,2,16,32,128]{4,3,2,1,0:T(8,128)(2,1)}), bf16[8,2,16,32,128]{4,3,2,1,0:T(8,128)(2,1)S(1)}, u32[]{:S(2)}, u32[]{:S(2)}) async-start(bf16[8,2,16,32,128]{4,3,2,1,0:T(8,128)(2,1)} %first_transform.6.after_ref), calls=%async_computation.2 | async-start | bytes 4194304 | tf_op jit(solution)/shard_map/all_to_all | solution.py:433
  154.3 10.7 %second_transform.5 = (f32[16,64,1024]{2,1,0:T(8,128)}, bf16[64,16,1024]{2,1,0:T(8,128)(2,1)}) custom-call(f32[16]{0:T(128)} %step_ref.9, bf16[8,2,16,64,128]{4,3,2,1,0:T(8,128)(2,1)} %all-to-all-done.half_ref, bf16[1024,1024]{1,0:T(8,128)(2,1)} %constant.22.clone.cosine_ref, bf16[1024,1024]{1,0:T(8,128)(2,1)} %constant.23.clone.sine_ref, ...), custom_call_target="tpu_custom_call" | custom-call | bytes 65536 | tf_op jit(solution)/shard_map/second_transform/pallas_call | solution.py:230
  165.0 1.5 collective-permute-start.5
  166.5 0.5 collective-permute-start.2
  167.1 56.4 %collective-permute-done.2.refs_1_.refs_5_ = bf16[16,16,1024]{2,1,0:T(8,128)(2,1)S(1)} collective-permute-done((bf16[16,16,1024]{2,1,0:T(8,128)(2,1)S(1)}, bf16[16,16,1024]{2,1,0:T(8,128)(2,1)S(1)}, u32[]{:S(2)}, u32[]{:S(2)}) %collective-permute-start.2) | collective-permute-done | bytes 524320 | tf_op jit(solution)/shard_map/ppermute | solution.py:390
  224.0 2.1 collective-permute-done.4.refs_3_.refs_7_
  226.1 1.6 copy-done
  227.7 1.0 gram_step.4.after_ref.before_ref
  228.7 0.7 copy-done.12
  229.4 0.8 copy-done.16
  230.2 0.8 copy-done.18
  231.0 6.5 %first_transform.7.after_ref = bf16[8,2,16,16,128]{4,3,2,1,0:T(8,128)(2,1)} custom-call(bf16[256,1024]{1,0:T(8,128)(2,1)} %constant.25.clone.table_ref, bf16[2,16,128,1024]{3,2,1,0:T(8,128)(2,1)} %grid_ref.7, f32[256,256]{1,0:T(8,128)} %copy-done.12), custom_call_target="tpu_custom_call" | custom-call | bytes 65536 | tf_op jit(solution)/shard_map/first_transform/pallas_call | solution.py:109
  237.6 6.0 %all-to-all-start.3 = ((bf16[8,2,16,16,128]{4,3,2,1,0:T(8,128)(2,1)}), bf16[8,2,16,16,128]{4,3,2,1,0:T(8,128)(2,1)}, u32[]{:S(2)}, u32[]{:S(2)}) async-start(bf16[8,2,16,16,128]{4,3,2,1,0:T(8,128)(2,1)} %first_transform.7.after_ref), calls=%async_computation.3 | async-start | bytes 2097152 | tf_op jit(solution)/shard_map/all_to_all | solution.py:433
  243.6 7.5 %second_transform.6 = (f32[16,32,1024]{2,1,0:T(8,128)}, bf16[32,16,1024]{2,1,0:T(8,128)(2,1)}) custom-call(f32[16]{0:T(128)} %step_ref.9, bf16[8,2,16,32,128]{4,3,2,1,0:T(8,128)(2,1)} %copy-done.23, bf16[1024,1024]{1,0:T(8,128)(2,1)} %constant.22.clone.cosine_ref, bf16[1024,1024]{1,0:T(8,128)(2,1)} %constant.23.clone.sine_ref, ...), custom_call_target="tpu_custom_call" | custom-call | bytes 65536 | tf_op jit(solution)/shard_map/second_transform/pallas_call | solution.py:230
  251.0 1.5 collective-permute-start.8
  252.5 23.5 %collective-permute-done.8.refs_1_.refs_13_ = bf16[32,16,1024]{2,1,0:T(8,128)(2,1)} collective-permute-done((bf16[32,16,1024]{2,1,0:T(8,128)(2,1)}, bf16[32,16,1024]{2,1,0:T(8,128)(2,1)}, u32[]{:S(2)}, u32[]{:S(2)}) %collective-permute-start.8) | collective-permute-done | bytes 1048608 | tf_op jit(solution)/shard_map/ppermute | solution.py:390
  276.0 1.2 copy-done.2
  277.2 7.0 %gram_step.5.after_ref.before_ref = f32[256,256]{1,0:T(8,128)S(1)} custom-call(f32[256,256]{1,0:T(8,128)S(1)} %copy-done.13, bf16[32,16,1024]{2,1,0:T(8,128)(2,1)S(1)} %copy-done.2, bf16[64,16,1024]{2,1,0:T(8,128)(2,1)S(1)} %copy-done.1, bf16[64,16,1024]{2,1,0:T(8,128)(2,1)} %collective-permute-done.5.refs_1_.refs_9_, ...), custom_call_target="tpu_custom_call" | custom-call | bytes 65536 | tf_op jit(solution)/shard_map/gram_step/pallas_call | solution.py:277
  284.3 0.7 copy-done.14
  285.0 5.8 %second_transform.7 = (f32[16,16,1024]{2,1,0:T(8,128)}, bf16[16,16,1024]{2,1,0:T(8,128)(2,1)}) custom-call(f32[16]{0:T(128)} %step_ref.9, bf16[8,2,16,16,128]{4,3,2,1,0:T(8,128)(2,1)} %all-to-all-done.3.half_ref, bf16[1024,1024]{1,0:T(8,128)(2,1)} %constant.22.clone.cosine_ref, bf16[1024,1024]{1,0:T(8,128)(2,1)} %constant.23.clone.sine_ref, ...), custom_call_target="tpu_custom_call" | custom-call | bytes 65536 | tf_op jit(solution)/shard_map/second_transform/pallas_call | solution.py:230
  290.8 1.5 collective-permute-start.11
  292.5 1.0 copy-done.5
  293.6 3.8 %gram_step.6.after_ref.before_ref = f32[256,256]{1,0:T(8,128)S(1)} custom-call(f32[256,256]{1,0:T(8,128)S(1)} %copy-done.15, bf16[16,16,1024]{2,1,0:T(8,128)(2,1)S(1)} %copy-done.5, bf16[32,16,1024]{2,1,0:T(8,128)(2,1)S(1)} %copy-done.3, bf16[32,16,1024]{2,1,0:T(8,128)(2,1)} %collective-permute-done.8.refs_1_.refs_13_, ...), custom_call_target="tpu_custom_call" | custom-call | bytes 65536 | tf_op jit(solution)/shard_map/gram_step/pallas_call | solution.py:277
  297.4 0.7 copy-done.10
  298.1 7.2 %collective-permute-done.11.value_ref = bf16[16,16,1024]{2,1,0:T(8,128)(2,1)S(1)} collective-permute-done((bf16[16,16,1024]{2,1,0:T(8,128)(2,1)}, bf16[16,16,1024]{2,1,0:T(8,128)(2,1)S(1)}, u32[]{:S(2)}, u32[]{:S(2)}) %collective-permute-start.11) | collective-permute-done | bytes 524320 | tf_op jit(solution)/shard_map/ppermute | solution.py:390
  305.3 0.8 copy-done.7
  306.8 1.5 collective-permute-done.13.refs_3_.refs_19_
  308.3 1.0 copy-done.8
  309.3 0.9 copy-done.11
  310.3 2.1 gram_step.7.gram_ref
  312.4 1.6 copy-done.20
  314.0 1.2 copy-done.22
  315.2 9.7 %polar_step.1 = f32[16,128,1024]{2,1,0:T(8,128)} custom-call(f32[1]{0:T(128)S(6)} %copy.16.shrink_ref, f32[256,256]{1,0:T(8,128)S(1)} %gram_step.7.gram_ref, f32[16,16,1024]{2,1,0:T(8,128)S(1)} %copy-done.21, f32[16,64,1024]{2,1,0:T(8,128)} %get-tuple-element.30.refs_1_, f32[16,32,1024]{2,1,0:T(8,128)S(1)} %copy-done.20, f32[16,16,1024]{2,1,0:T(8,128)S(1)} %copy-done.22, ...), custom_call_target="tpu_custom_call" | custom-call | bytes 65536 | tf_op jit(solution)/shard_map/polar_step/pallas_call | solution.py:362
  (57 shorter events, 0.9 us)
Async XLA Ops:
  6.5 42.9 %all-to-all-start.1 = ((bf16[8,2,16,16,128]{4,3,2,1,0:T(8,128)(2,1)}), bf16[8,2,16,16,128]{4,3,2,1,0:T(8,128)(2,1)S(1)}, u32[]{:S(2)}, u32[]{:S(2)}) async-start(bf16[8,2,16,16,128]{4,3,2,1,0:T(8,128)(2,1)} %first_transform.4.after_ref), calls=%async_computation.1 | async-start | bytes 2097152 | tf_op jit(solution)/shard_map/all_to_all | solution.py:433
  14.5 31.9 %collective-permute-start = (bf16[16,12,1024]{2,1,0:T(8,128)(2,1)S(1)}, bf16[16,12,1024]{2,1,0:T(8,128)(2,1)S(1)}, u32[]{:S(2)}, u32[]{:S(2)}) collective-permute-start(bf16[16,12,1024]{2,1,0:T(8,128)(2,1)S(1)} %get-tuple-element.19), channel_id=1, source_target_pairs={{0,4},{4,8},{8,12},{12,16},{16,20},{20,24},{24,28},{1,5},{5,9},{9,... | collective-permute-start | bytes 1179656 | tf_op jit(solution)/shard_map/ppermute | solution.py:383
  17.9 30.5 %collective-permute-start.1 = (bf16[16,12,1024]{2,1,0:T(8,128)(2,1)S(1)}, bf16[16,12,1024]{2,1,0:T(8,128)(2,1)S(1)}, u32[]{:S(2)}, u32[]{:S(2)}) collective-permute-start(bf16[16,12,1024]{2,1,0:T(8,128)(2,1)S(1)} %get-tuple-element.20), channel_id=1, source_target_pairs={{4,0},{8,4},{12,8},{16,12},{20,16},{24,20},{28,24},{5,1},{9,5},{13... | collective-permute-start | bytes 1179656 | tf_op jit(solution)/shard_map/ppermute | solution.py:384
  49.4 1.0 copy-start.24
  50.4 96.9 %all-to-all-start = ((bf16[8,2,16,64,128]{4,3,2,1,0:T(8,128)(2,1)}), bf16[8,2,16,64,128]{4,3,2,1,0:T(8,128)(2,1)}, u32[]{:S(2)}, u32[]{:S(2)}) async-start(bf16[8,2,16,64,128]{4,3,2,1,0:T(8,128)(2,1)} %gate.2.after_ref), calls=%async_computation | async-start | bytes 8388608 | tf_op jit(solution)/shard_map/all_to_all | solution.py:433
  147.3 90.2 %all-to-all-start.2 = ((bf16[8,2,16,32,128]{4,3,2,1,0:T(8,128)(2,1)}), bf16[8,2,16,32,128]{4,3,2,1,0:T(8,128)(2,1)S(1)}, u32[]{:S(2)}, u32[]{:S(2)}) async-start(bf16[8,2,16,32,128]{4,3,2,1,0:T(8,128)(2,1)} %first_transform.6.after_ref), calls=%async_computation.2 | async-start | bytes 4194304 | tf_op jit(solution)/shard_map/all_to_all | solution.py:433
  154.3 12.2 %copy-start.4 = (bf16[16,16,1024]{2,1,0:T(8,128)(2,1)S(1)}, bf16[16,16,1024]{2,1,0:T(8,128)(2,1)}, u32[]{:S(2)}) copy-start(bf16[16,16,1024]{2,1,0:T(8,128)(2,1)} %get-tuple-element.23.after_ref.refs_0_.refs_4_) | copy-start | bytes 1572868
  165.0 59.0 %collective-permute-start.5 = (bf16[64,16,1024]{2,1,0:T(8,128)(2,1)}, bf16[64,16,1024]{2,1,0:T(8,128)(2,1)}, u32[]{:S(2)}, u32[]{:S(2)}) collective-permute-start(bf16[64,16,1024]{2,1,0:T(8,128)(2,1)} %get-tuple-element.24.after_ref.refs_0_.refs_8_), channel_id=1, source_target_pairs={{0,2},{1,3},{2,0},{3,1},{4,6},{5,7},{6,4},{7,5},{8,10},{9,11},{10,... | collective-permute-start | bytes 6291464 | tf_op jit(solution)/shard_map/ppermute | solution.py:390
  166.5 56.9 %collective-permute-start.2 = (bf16[16,16,1024]{2,1,0:T(8,128)(2,1)S(1)}, bf16[16,16,1024]{2,1,0:T(8,128)(2,1)S(1)}, u32[]{:S(2)}, u32[]{:S(2)}) collective-permute-start(bf16[16,16,1024]{2,1,0:T(8,128)(2,1)S(1)} %copy-done.4), channel_id=1, source_target_pairs={{0,2},{1,3},{2,0},{3,1},{4,6},{5,7},{6,4},{7,5},{8,10},{9,11},{10,... | collective-permute-start | bytes 1572872 | tf_op jit(solution)/shard_map/ppermute | solution.py:390
  167.1 56.9 %collective-permute-start.3 = (bf16[16,16,1024]{2,1,0:T(8,128)(2,1)S(1)}, bf16[16,16,1024]{2,1,0:T(8,128)(2,1)S(1)}, u32[]{:S(2)}, u32[]{:S(2)}) collective-permute-start(bf16[16,16,1024]{2,1,0:T(8,128)(2,1)S(1)} %copy-done.4), channel_id=1, source_target_pairs={{0,1},{1,0},{2,3},{3,2},{4,5},{5,4},{6,7},{7,6},{8,9},{9,8},{10,11... | collective-permute-start | bytes 1572872 | tf_op jit(solution)/shard_map/ppermute | solution.py:390
  223.5 2.6 collective-permute-start.4
  223.5 52.5 %collective-permute-start.6 = (bf16[64,16,1024]{2,1,0:T(8,128)(2,1)}, bf16[64,16,1024]{2,1,0:T(8,128)(2,1)}, u32[]{:S(2)}, u32[]{:S(2)}) collective-permute-start(bf16[64,16,1024]{2,1,0:T(8,128)(2,1)} %get-tuple-element.24.after_ref.refs_0_.refs_8_), channel_id=1, source_target_pairs={{0,1},{1,0},{2,3},{3,2},{4,5},{5,4},{6,7},{7,6},{8,9},{9,8},{10,11... | collective-permute-start | bytes 6291464 | tf_op jit(solution)/shard_map/ppermute | solution.py:390
  224.0 52.0 %collective-permute-start.7 = (bf16[64,16,1024]{2,1,0:T(8,128)(2,1)}, bf16[64,16,1024]{2,1,0:T(8,128)(2,1)}, u32[]{:S(2)}, u32[]{:S(2)}) collective-permute-start(bf16[64,16,1024]{2,1,0:T(8,128)(2,1)} %collective-permute-done.5.refs_1_.refs_9_), channel_id=1, source_target_pairs={{0,1},{1,0},{2,3},{3,2},{4,5},{5,4},{6,7},{7,6},{8,9},{9,8},{10,11... | collective-permute-start | bytes 6291464 | tf_op jit(solution)/shard_map/ppermute | solution.py:390
  226.1 1.6 copy-start
  228.7 0.7 copy-start.12
  229.4 0.8 copy-start.16
  230.2 0.8 copy-start.18
  237.6 6.0 %copy-start.23 = (bf16[8,2,16,32,128]{4,3,2,1,0:T(8,128)(2,1)}, bf16[8,2,16,32,128]{4,3,2,1,0:T(8,128)(2,1)S(1)}, u32[]{:S(2)}) copy-start(bf16[8,2,16,32,128]{4,3,2,1,0:T(8,128)(2,1)S(1)} %all-to-all-done.2.half_ref) | copy-start | bytes 6291460
  237.6 47.5 %all-to-all-start.3 = ((bf16[8,2,16,16,128]{4,3,2,1,0:T(8,128)(2,1)}), bf16[8,2,16,16,128]{4,3,2,1,0:T(8,128)(2,1)}, u32[]{:S(2)}, u32[]{:S(2)}) async-start(bf16[8,2,16,16,128]{4,3,2,1,0:T(8,128)(2,1)} %first_transform.7.after_ref), calls=%async_computation.3 | async-start | bytes 2097152 | tf_op jit(solution)/shard_map/all_to_all | solution.py:433
  243.6 32.4 %copy-start.1 = (bf16[64,16,1024]{2,1,0:T(8,128)(2,1)S(1)}, bf16[64,16,1024]{2,1,0:T(8,128)(2,1)}, u32[]{:S(2)}) copy-start(bf16[64,16,1024]{2,1,0:T(8,128)(2,1)} %get-tuple-element.24.after_ref.refs_0_.refs_8_) | copy-start | bytes 6291460
  243.6 32.5 %copy-start.13 = (f32[256,256]{1,0:T(8,128)S(1)}, f32[256,256]{1,0:T(8,128)}, u32[]{:S(2)}) copy-start(f32[256,256]{1,0:T(8,128)} %copy-done.12) | copy-start | bytes 786436
  251.0 25.0 %collective-permute-start.8 = (bf16[32,16,1024]{2,1,0:T(8,128)(2,1)}, bf16[32,16,1024]{2,1,0:T(8,128)(2,1)}, u32[]{:S(2)}, u32[]{:S(2)}) collective-permute-start(bf16[32,16,1024]{2,1,0:T(8,128)(2,1)} %get-tuple-element.26.after_ref.refs_0_.refs_12_), channel_id=1, source_target_pairs={{0,2},{1,3},{2,0},{3,1},{4,6},{5,7},{6,4},{7,5},{8,10},{9,11},{10,... | collective-permute-start | bytes 3145736 | tf_op jit(solution)/shard_map/ppermute | solution.py:390
  252.5 40.0 %collective-permute-start.9 = (bf16[32,16,1024]{2,1,0:T(8,128)(2,1)}, bf16[32,16,1024]{2,1,0:T(8,128)(2,1)}, u32[]{:S(2)}, u32[]{:S(2)}) collective-permute-start(bf16[32,16,1024]{2,1,0:T(8,128)(2,1)} %get-tuple-element.26.after_ref.refs_0_.refs_12_), channel_id=1, source_target_pairs={{0,1},{1,0},{2,3},{3,2},{4,5},{5,4},{6,7},{7,6},{8,9},{9,8},{10,11... | collective-permute-start | bytes 3145736 | tf_op jit(solution)/shard_map/ppermute | solution.py:390
  276.0 16.5 %collective-permute-start.10 = (bf16[32,16,1024]{2,1,0:T(8,128)(2,1)}, bf16[32,16,1024]{2,1,0:T(8,128)(2,1)}, u32[]{:S(2)}, u32[]{:S(2)}) collective-permute-start(bf16[32,16,1024]{2,1,0:T(8,128)(2,1)} %collective-permute-done.8.refs_1_.refs_13_), channel_id=1, source_target_pairs={{0,1},{1,0},{2,3},{3,2},{4,5},{5,4},{6,7},{7,6},{8,9},{9,8},{10,11... | collective-permute-start | bytes 3145736 | tf_op jit(solution)/shard_map/ppermute | solution.py:390
  276.0 1.2 copy-start.2
  284.3 0.7 copy-start.14
  285.0 7.5 %copy-start.3 = (bf16[32,16,1024]{2,1,0:T(8,128)(2,1)S(1)}, bf16[32,16,1024]{2,1,0:T(8,128)(2,1)}, u32[]{:S(2)}) copy-start(bf16[32,16,1024]{2,1,0:T(8,128)(2,1)} %get-tuple-element.26.after_ref.refs_0_.refs_12_) | copy-start | bytes 3145732
  285.0 7.5 %copy-start.15 = (f32[256,256]{1,0:T(8,128)S(1)}, f32[256,256]{1,0:T(8,128)}, u32[]{:S(2)}) copy-start(f32[256,256]{1,0:T(8,128)} %copy-done.14) | copy-start | bytes 786436
  290.8 14.5 %collective-permute-start.11 = (bf16[16,16,1024]{2,1,0:T(8,128)(2,1)}, bf16[16,16,1024]{2,1,0:T(8,128)(2,1)S(1)}, u32[]{:S(2)}, u32[]{:S(2)}) collective-permute-start(bf16[16,16,1024]{2,1,0:T(8,128)(2,1)} %get-tuple-element.28.after_ref.refs_0_.refs_16_), channel_id=1, source_target_pairs={{0,2},{1,3},{2,0},{3,1},{4,6},{5,7},{6,4},{7,5},{8,10},{9,11},{10,... | collective-permute-start | bytes 1572872 | tf_op jit(solution)/shard_map/ppermute | solution.py:390
  292.3 14.5 %collective-permute-start.12 = (bf16[16,16,1024]{2,1,0:T(8,128)(2,1)}, bf16[16,16,1024]{2,1,0:T(8,128)(2,1)}, u32[]{:S(2)}, u32[]{:S(2)}) collective-permute-start(bf16[16,16,1024]{2,1,0:T(8,128)(2,1)} %get-tuple-element.28.after_ref.refs_0_.refs_16_), channel_id=1, source_target_pairs={{0,1},{1,0},{2,3},{3,2},{4,5},{5,4},{6,7},{7,6},{8,9},{9,8},{10,11... | collective-permute-start | bytes 1572872 | tf_op jit(solution)/shard_map/ppermute | solution.py:390
  292.5 1.0 copy-start.5
  293.6 14.7 %copy-start.6 = (bf16[16,16,1024]{2,1,0:T(8,128)(2,1)S(1)}, bf16[16,16,1024]{2,1,0:T(8,128)(2,1)}, u32[]{:S(2)}) copy-start(bf16[16,16,1024]{2,1,0:T(8,128)(2,1)} %get-tuple-element.28.after_ref.refs_0_.refs_16_) | copy-start | bytes 1572868
  297.4 0.7 copy-start.10
  305.3 0.8 copy-start.7
  306.1 2.1 collective-permute-start.13
  308.3 1.0 copy-start.8
  309.3 0.9 copy-start.11
  310.3 2.1 copy-start.9
  310.3 2.1 copy-start.17
  310.3 2.1 copy-start.19
  310.3 2.1 copy-start.21
  312.4 1.6 copy-start.20
  314.0 1.2 copy-start.22

commit v6 on v5

--- a/solution.py
+++ b/solution.py
@@ -419,35 +419,59 @@
     reach = (taps - 1) * 2 ** (levels - 1)
     edges = neighbour_rows(model_image, reach)
 
-    halves = []
-    moved = []
-    gathered = []
-    gram = jnp.zeros((GRAM_ROWS * size, GRAM_ROWS * size), F32)
-    last = strip
-    for chunk in range(chunks + 1):
-        if chunk < chunks:
-            sent = first_transform(tables[chunk], grid, strips, last)
-            if chunk == 1:
-                sent = gate(sent, edges)
-            last = sent
-            halves.append(lax.all_to_all(sent, "strip", split_axis=0, concat_axis=0, tiled=True))
+    halves = {}
+    moved = {}
+    gathered = {}
+    state = dict(last=strip, gram=jnp.zeros((GRAM_ROWS * size, GRAM_ROWS * size), F32), bases=None)
+
+    def first(chunk):
+        sent = first_transform(tables[chunk], grid, strips, state["last"])
         if chunk == 1:
-            bases = base_step(strip, strips, step_size, highpass, model_image, edges, starts, sizes, last)
-            last = bases[0]
-        if chunk >= 1:
-            done = chunk - 1
-            result, pixels = second_transform(step_size, halves[done], cosine, sine_table, bases[done], last)
-            last = pixels
-            moved.append(result)
-            if done >= 1:
-                gram = gram_step(gathered[done - 1], gram, last)
-                last = gram
-            pieces = gather_channels(pixels, gram if chunk == chunks else None)
-            if chans % 16:
-                pieces = [jnp.concatenate(pieces, axis=1)]
-            gathered.append(pieces)
-    gram = gram_step(gathered[-1], gram, last)
-    return polar_step(shrinkage, gram, moved, gathered, starts, sizes)
+            sent = gate(sent, edges)
+        state["last"] = sent
+        halves[chunk] = lax.all_to_all(sent, "strip", split_axis=0, concat_axis=0, tiled=True)
+
+    def base():
+        state["bases"] = base_step(
+            strip, strips, step_size, highpass, model_image, edges, starts, sizes, state["last"]
+        )
+        state["last"] = state["bases"][0]
+
+    def second(chunk):
+        moved[chunk], pixels = second_transform(
+            step_size, halves[chunk], cosine, sine_table, state["bases"][chunk], state["last"]
+        )
+        state["last"] = pixels
+        return pixels
+
+    def gather(chunk, pixels, after=None):
+        pieces = gather_channels(pixels, after)
+        if chans % 16:
+            pieces = [jnp.concatenate(pieces, axis=1)]
+        gathered[chunk] = pieces
+
+    def gram(chunk):
+        state["gram"] = gram_step(gathered[chunk], state["gram"], state["last"])
+        state["last"] = state["gram"]
+
+    first(0)
+    if chunks > 1:
+        first(1)
+    base()
+    for chunk in range(chunks):
+        pixels = second(chunk)
+        if chunk + 2 < chunks:
+            first(chunk + 2)
+        if chunk > 1 or (chunk == 1 and chunks < 4):
+            gram(chunk - 1)
+        gather(chunk, pixels, state["gram"] if chunk + 1 == chunks else None)
+        if chunk == 0 and chunks >= 4:
+            gram(0)
+    gram(chunks - 1)
+    order = range(chunks)
+    return polar_step(
+        shrinkage, state["gram"], [moved[k] for k in order], [gathered[k] for k in order], starts, sizes
+    )
 
 
 def solution(mesh):

time: 328 us -> 327 us (level)
  local copies, waits for them, and re-layouts: 16 us -> 12.7 us
    unnamed x50 -> x48, local copies, waits for them, and re-layouts: 14.2 us -> 11 us
  transfers between devices with their start and end apart: 18 -> 18, of which waited for: 8 -> 9; matrix products, arithmetic and copies ran while one was open for 1% -> 1% of each run, Pallas kernels for 25% -> 25%
where the time goes in v6:
time: 327 us; the launch traced here: 324 us
  waiting for transfers between devices  172 us (53%)
  Pallas kernels  98.6 us (30%)
  starting transfers between devices  38.8 us (12%)
  local copies, waits for them, and re-layouts  12.7 us (4%)
    ppermute x12, waiting for transfers between devices, swap(): return lax.ppermute(value, axis, [(i, i ^ bits) for i in range(count)])  92.2 us
    all_to_all x4, waiting for transfers between devices, first(): lax.all_to_all(sent, 'strip', split_axis=0, concat_axis=0, tiled=True)  64.6 us
    pallas_call x4, Pallas kernels, first_transform(): pl.pallas_call(first_body, grid=(chans // block,), in_specs=[pl.BlockSpec...  34.2 us
    pallas_call x4, Pallas kernels, second_transform(): pl.pallas_call(second_body, grid=(side_len // block,), in_specs=[SMEM, pl...  29.5 us
    all_to_all x4, starting transfers between devices, first(): lax.all_to_all(sent, 'strip', split_axis=0, concat_axis=0, tiled=True)  26.8 us
    pallas_call x4, Pallas kernels, gram_step(): pl.pallas_call(functools.partial(gram_body, len(pieces)), grid=(rows // b...  13.9 us
    ppermute x1, waiting for transfers between devices, neighbour_rows(): lax.ppermute(tail.astype(BF16), 'strip', [(i, i + 1) for i in range(ends)])  13.3 us
    pallas_call x1, Pallas kernels, base_step(): pl.pallas_call(functools.partial(base_body, levels, taps, starts, strips)...  11.2 us
  transfers between devices with their start and end apart: 18, of which 9 were waited for; matrix products, arithmetic and copies ran while one was open for 1% of the time, Pallas kernels for 25%

profile of v6, /device:TPU:12, one launch (start us, length us, event | category | flops | bytes accessed | tf_op | source)
XLA Modules:
  0.0 324.3 jit_solution(2732809798112117002)
XLA Ops:
  0.0 6.5 %first_transform.4.after_ref = bf16[8,2,16,16,128]{4,3,2,1,0:T(8,128)(2,1)} custom-call(bf16[256,1024]{1,0:T(8,128)(2,1)} %constant.20.clone.table_ref, bf16[2,16,128,1024]{3,2,1,0:T(8,128)(2,1)} %grid_ref.7, s32[1]{0:T(128)} %bitcast.after_ref.strip_ref), custom_call_target="tpu_custom_call" | custom-call | bytes 65536 | tf_op jit(solution)/shard_map/first_transform/pallas_call | solution.py:109
  6.5 6.2 %all-to-all-start = ((bf16[8,2,16,16,128]{4,3,2,1,0:T(8,128)(2,1)}), bf16[8,2,16,16,128]{4,3,2,1,0:T(8,128)(2,1)S(1)}, u32[]{:S(2)}, u32[]{:S(2)}) async-start(bf16[8,2,16,16,128]{4,3,2,1,0:T(8,128)(2,1)} %first_transform.4.after_ref), calls=%async_computation | async-start | bytes 2097152 | tf_op jit(solution)/shard_map/all_to_all | solution.py:432
  12.7 1.7 fusion
  14.5 3.4 %collective-permute-start = (bf16[16,12,1024]{2,1,0:T(8,128)(2,1)S(1)}, bf16[16,12,1024]{2,1,0:T(8,128)(2,1)S(1)}, u32[]{:S(2)}, u32[]{:S(2)}) collective-permute-start(bf16[16,12,1024]{2,1,0:T(8,128)(2,1)S(1)} %get-tuple-element.19), channel_id=1, source_target_pairs={{0,4},{4,8},{8,12},{12,16},{16,20},{20,24},{24,28},{1,5},{5,9},{9,... | collective-permute-start | bytes 1179656 | tf_op jit(solution)/shard_map/ppermute | solution.py:383
  17.9 2.5 collective-permute-start.1
  20.3 12.7 %first_transform.5.value_ref = bf16[8,2,16,64,128]{4,3,2,1,0:T(8,128)(2,1)} custom-call(bf16[1024,1024]{1,0:T(8,128)(2,1)} %constant.21.clone.table_ref, bf16[2,16,128,1024]{3,2,1,0:T(8,128)(2,1)} %grid_ref.7, bf16[8,2,16,16,128]{4,3,2,1,0:T(8,128)(2,1)} %first_transform.4.after_ref), custom_call_target="tpu_custom_call" | custom-call | bytes 65536 | tf_op jit(solution)/shard_map/first_transform/pallas_call | solution.py:109
  33.1 13.3 %collective-permute-done = bf16[16,12,1024]{2,1,0:T(8,128)(2,1)S(1)} collective-permute-done((bf16[16,12,1024]{2,1,0:T(8,128)(2,1)S(1)}, bf16[16,12,1024]{2,1,0:T(8,128)(2,1)S(1)}, u32[]{:S(2)}, u32[]{:S(2)}) %collective-permute-start) | collective-permute-done | bytes 393248 | tf_op jit(solution)/shard_map/ppermute | solution.py:383
  46.4 1.9 collective-permute-done.1
  48.3 1.1 pad_maximum_fusion.after_ref.edge_ref
  49.4 1.0 copy-done.23
  50.4 7.0 %all-to-all-start.2 = ((bf16[8,2,16,64,128]{4,3,2,1,0:T(8,128)(2,1)}), bf16[8,2,16,64,128]{4,3,2,1,0:T(8,128)(2,1)}, u32[]{:S(2)}, u32[]{:S(2)}) async-start(bf16[8,2,16,64,128]{4,3,2,1,0:T(8,128)(2,1)} %gate.2.after_ref), calls=%async_computation.2 | async-start | bytes 8388608 | tf_op jit(solution)/shard_map/all_to_all | solution.py:432
  57.4 11.2 %base_step.1 = (f32[16,16,1024]{2,1,0:T(8,128)}, f32[16,64,1024]{2,1,0:T(8,128)}, f32[16,32,1024]{2,1,0:T(8,128)}, f32[16,16,1024]{2,1,0:T(8,128)}) custom-call(s32[1]{0:T(128)} %bitcast.after_ref.strip_ref, f32[16]{0:T(128)} %step_ref.9, f32[3,4]{1,0:T(4,128)} %highpass_ref.1, f32[16,128,1024]{2,1,0:T(8,128)} %model_ref.1, ...), custom_call_target="tpu_custom_call" | custom-call | bytes 65536 | tf_op jit(solution)/shard_map/base_step/pallas_call | solution.py:187
  68.6 5.7 %second_transform.4 = (f32[16,16,1024]{2,1,0:T(8,128)}, bf16[16,16,1024]{2,1,0:T(8,128)(2,1)}) custom-call(f32[16]{0:T(128)} %step_ref.9, bf16[8,2,16,16,128]{4,3,2,1,0:T(8,128)(2,1)} %copy-done.23, bf16[1024,1024]{1,0:T(8,128)(2,1)} %constant.22.clone.cosine_ref, bf16[1024,1024]{1,0:T(8,128)(2,1)} %constant.23.clone.sine_ref, ...), custom_call_target="tpu_custom_call" | custom-call | bytes 65536 | tf_op jit(solution)/shard_map/second_transform/pallas_call | solution.py:230
  74.3 8.4 %first_transform.6.after_ref = bf16[8,2,16,32,128]{4,3,2,1,0:T(8,128)(2,1)} custom-call(bf16[512,1024]{1,0:T(8,128)(2,1)} %constant.24.clone.table_ref, bf16[2,16,128,1024]{3,2,1,0:T(8,128)(2,1)} %grid_ref.7, bf16[16,16,1024]{2,1,0:T(8,128)(2,1)} %get-tuple-element.22.after_ref.refs_0_.refs_4_), custom_call_target="tpu_custom_call" | custom-call | bytes 65536 | tf_op jit(solution)/shard_map/first_transform/pallas_call | solution.py:109
  82.8 64.6 %all-to-all-done.2.half_ref = bf16[8,2,16,64,128]{4,3,2,1,0:T(8,128)(2,1)} async-done(((bf16[8,2,16,64,128]{4,3,2,1,0:T(8,128)(2,1)}), bf16[8,2,16,64,128]{4,3,2,1,0:T(8,128)(2,1)}, u32[]{:S(2)}, u32[]{:S(2)}) %all-to-all-start.2) | async-done | bytes 4194336 | tf_op jit(solution)/shard_map/all_to_all | solution.py:432
  147.3 7.6 %all-to-all-start.1 = ((bf16[8,2,16,32,128]{4,3,2,1,0:T(8,128)(2,1)}), bf16[8,2,16,32,128]{4,3,2,1,0:T(8,128)(2,1)}, u32[]{:S(2)}, u32[]{:S(2)}) async-start(bf16[8,2,16,32,128]{4,3,2,1,0:T(8,128)(2,1)} %first_transform.6.after_ref), calls=%async_computation.1 | async-start | bytes 4194304 | tf_op jit(solution)/shard_map/all_to_all | solution.py:432
  154.9 1.5 collective-permute-start.2
  156.4 11.2 %collective-permute-done.2.refs_1_.refs_5_ = bf16[16,16,1024]{2,1,0:T(8,128)(2,1)S(1)} collective-permute-done((bf16[16,16,1024]{2,1,0:T(8,128)(2,1)S(1)}, bf16[16,16,1024]{2,1,0:T(8,128)(2,1)S(1)}, u32[]{:S(2)}, u32[]{:S(2)}) %collective-permute-start.2) | collective-permute-done | bytes 524320 | tf_op jit(solution)/shard_map/ppermute | solution.py:390
  167.6 1.9 collective-permute-done.4.refs_3_.refs_7_
  169.6 1.0 gram_step.4.after_ref.before_ref
  170.6 0.7 copy-done.12
  171.3 10.6 %second_transform.5 = (f32[16,64,1024]{2,1,0:T(8,128)}, bf16[64,16,1024]{2,1,0:T(8,128)(2,1)}) custom-call(f32[16]{0:T(128)} %step_ref.9, bf16[8,2,16,64,128]{4,3,2,1,0:T(8,128)(2,1)} %all-to-all-done.2.half_ref, bf16[1024,1024]{1,0:T(8,128)(2,1)} %constant.22.clone.cosine_ref, bf16[1024,1024]{1,0:T(8,128)(2,1)} %constant.23.clone.sine_ref, ...), custom_call_target="tpu_custom_call" | custom-call | bytes 65536 | tf_op jit(solution)/shard_map/second_transform/pallas_call | solution.py:230
  181.9 1.5 collective-permute-start.5
  183.4 46.5 %collective-permute-done.5.refs_1_.refs_9_ = bf16[64,16,1024]{2,1,0:T(8,128)(2,1)} collective-permute-done((bf16[64,16,1024]{2,1,0:T(8,128)(2,1)}, bf16[64,16,1024]{2,1,0:T(8,128)(2,1)}, u32[]{:S(2)}, u32[]{:S(2)}) %collective-permute-start.5) | collective-permute-done | bytes 2097184 | tf_op jit(solution)/shard_map/ppermute | solution.py:390
  229.9 6.5 %first_transform.7.after_ref = bf16[8,2,16,16,128]{4,3,2,1,0:T(8,128)(2,1)} custom-call(bf16[256,1024]{1,0:T(8,128)(2,1)} %constant.25.clone.table_ref, bf16[2,16,128,1024]{3,2,1,0:T(8,128)(2,1)} %grid_ref.7, bf16[64,16,1024]{2,1,0:T(8,128)(2,1)} %get-tuple-element.25.after_ref.refs_0_.refs_8_), custom_call_target="tpu_custom_call" | custom-call | bytes 65536 | tf_op jit(solution)/shard_map/first_transform/pallas_call | solution.py:109
  236.4 6.0 %all-to-all-start.3 = ((bf16[8,2,16,16,128]{4,3,2,1,0:T(8,128)(2,1)}), bf16[8,2,16,16,128]{4,3,2,1,0:T(8,128)(2,1)}, u32[]{:S(2)}, u32[]{:S(2)}) async-start(bf16[8,2,16,16,128]{4,3,2,1,0:T(8,128)(2,1)} %first_transform.7.after_ref), calls=%async_computation.3 | async-start | bytes 2097152 | tf_op jit(solution)/shard_map/all_to_all | solution.py:432
  242.4 7.4 %second_transform.6 = (f32[16,32,1024]{2,1,0:T(8,128)}, bf16[32,16,1024]{2,1,0:T(8,128)(2,1)}) custom-call(f32[16]{0:T(128)} %step_ref.9, bf16[8,2,16,32,128]{4,3,2,1,0:T(8,128)(2,1)} %all-to-all-done.1.half_ref, bf16[1024,1024]{1,0:T(8,128)(2,1)} %constant.22.clone.cosine_ref, bf16[1024,1024]{1,0:T(8,128)(2,1)} %constant.23.clone.sine_ref, ...), custom_call_target="tpu_custom_call" | custom-call | bytes 65536 | tf_op jit(solution)/shard_map/second_transform/pallas_call | solution.py:230
  249.8 1.5 collective-permute-start.8
  251.3 23.8 %collective-permute-done.8.refs_1_.refs_13_ = bf16[32,16,1024]{2,1,0:T(8,128)(2,1)} collective-permute-done((bf16[32,16,1024]{2,1,0:T(8,128)(2,1)}, bf16[32,16,1024]{2,1,0:T(8,128)(2,1)}, u32[]{:S(2)}, u32[]{:S(2)}) %collective-permute-start.8) | collective-permute-done | bytes 1048608 | tf_op jit(solution)/shard_map/ppermute | solution.py:390
  275.2 1.2 copy-done.2
  276.4 7.0 %gram_step.5.after_ref.before_ref = f32[256,256]{1,0:T(8,128)S(1)} custom-call(f32[256,256]{1,0:T(8,128)S(1)} %copy-done.13, bf16[32,16,1024]{2,1,0:T(8,128)(2,1)S(1)} %copy-done.2, bf16[64,16,1024]{2,1,0:T(8,128)(2,1)S(1)} %copy-done, bf16[64,16,1024]{2,1,0:T(8,128)(2,1)} %collective-permute-done.5.refs_1_.refs_9_, ...), custom_call_target="tpu_custom_call" | custom-call | bytes 65536 | tf_op jit(solution)/shard_map/gram_step/pallas_call | solution.py:277
  283.5 0.7 copy-done.14
  284.1 5.8 %second_transform.7 = (f32[16,16,1024]{2,1,0:T(8,128)}, bf16[16,16,1024]{2,1,0:T(8,128)(2,1)}) custom-call(f32[16]{0:T(128)} %step_ref.9, bf16[8,2,16,16,128]{4,3,2,1,0:T(8,128)(2,1)} %all-to-all-done.3.half_ref, bf16[1024,1024]{1,0:T(8,128)(2,1)} %constant.22.clone.cosine_ref, bf16[1024,1024]{1,0:T(8,128)(2,1)} %constant.23.clone.sine_ref, ...), custom_call_target="tpu_custom_call" | custom-call | bytes 65536 | tf_op jit(solution)/shard_map/second_transform/pallas_call | solution.py:230
  290.0 1.5 collective-permute-start.11
  291.5 0.2 collective-permute-start.12
  291.7 1.0 copy-done.5
  292.8 3.8 %gram_step.6.after_ref.before_ref = f32[256,256]{1,0:T(8,128)S(1)} custom-call(f32[256,256]{1,0:T(8,128)S(1)} %copy-done.15, bf16[16,16,1024]{2,1,0:T(8,128)(2,1)S(1)} %copy-done.5, bf16[32,16,1024]{2,1,0:T(8,128)(2,1)S(1)} %copy-done.3, bf16[32,16,1024]{2,1,0:T(8,128)(2,1)} %collective-permute-done.8.refs_1_.refs_13_, ...), custom_call_target="tpu_custom_call" | custom-call | bytes 65536 | tf_op jit(solution)/shard_map/gram_step/pallas_call | solution.py:277
  296.6 0.7 copy-done.10
  297.3 7.3 %collective-permute-done.11.value_ref = bf16[16,16,1024]{2,1,0:T(8,128)(2,1)S(1)} collective-permute-done((bf16[16,16,1024]{2,1,0:T(8,128)(2,1)}, bf16[16,16,1024]{2,1,0:T(8,128)(2,1)S(1)}, u32[]{:S(2)}, u32[]{:S(2)}) %collective-permute-start.11) | collective-permute-done | bytes 524320 | tf_op jit(solution)/shard_map/ppermute | solution.py:390
  304.5 0.8 copy-done.7
  306.0 1.5 collective-permute-done.13.refs_3_.refs_19_
  307.4 1.0 copy-done.8
  308.5 0.9 copy-done.11
  309.5 2.1 gram_step.7.gram_ref
  311.6 0.0 copy-start.20
  311.6 1.6 copy-done.20
  313.2 1.2 copy-done.22
  314.4 9.7 %polar_step.1 = f32[16,128,1024]{2,1,0:T(8,128)} custom-call(f32[1]{0:T(128)S(6)} %copy.16.shrink_ref, f32[256,256]{1,0:T(8,128)S(1)} %gram_step.7.gram_ref, f32[16,16,1024]{2,1,0:T(8,128)S(1)} %copy-done.21, f32[16,64,1024]{2,1,0:T(8,128)} %get-tuple-element.30.refs_1_, f32[16,32,1024]{2,1,0:T(8,128)S(1)} %copy-done.20, f32[16,16,1024]{2,1,0:T(8,128)S(1)} %copy-done.22, ...), custom_call_target="tpu_custom_call" | custom-call | bytes 65536 | tf_op jit(solution)/shard_map/polar_step/pallas_call | solution.py:362
  (55 shorter events, 0.1 us)
Async XLA Ops:
  6.5 42.9 %all-to-all-start = ((bf16[8,2,16,16,128]{4,3,2,1,0:T(8,128)(2,1)}), bf16[8,2,16,16,128]{4,3,2,1,0:T(8,128)(2,1)S(1)}, u32[]{:S(2)}, u32[]{:S(2)}) async-start(bf16[8,2,16,16,128]{4,3,2,1,0:T(8,128)(2,1)} %first_transform.4.after_ref), calls=%async_computation | async-start | bytes 2097152 | tf_op jit(solution)/shard_map/all_to_all | solution.py:432
  14.5 31.9 %collective-permute-start = (bf16[16,12,1024]{2,1,0:T(8,128)(2,1)S(1)}, bf16[16,12,1024]{2,1,0:T(8,128)(2,1)S(1)}, u32[]{:S(2)}, u32[]{:S(2)}) collective-permute-start(bf16[16,12,1024]{2,1,0:T(8,128)(2,1)S(1)} %get-tuple-element.19), channel_id=1, source_target_pairs={{0,4},{4,8},{8,12},{12,16},{16,20},{20,24},{24,28},{1,5},{5,9},{9,... | collective-permute-start | bytes 1179656 | tf_op jit(solution)/shard_map/ppermute | solution.py:383
  17.9 30.5 %collective-permute-start.1 = (bf16[16,12,1024]{2,1,0:T(8,128)(2,1)S(1)}, bf16[16,12,1024]{2,1,0:T(8,128)(2,1)S(1)}, u32[]{:S(2)}, u32[]{:S(2)}) collective-permute-start(bf16[16,12,1024]{2,1,0:T(8,128)(2,1)S(1)} %get-tuple-element.20), channel_id=1, source_target_pairs={{4,0},{8,4},{12,8},{16,12},{20,16},{24,20},{28,24},{5,1},{9,5},{13... | collective-permute-start | bytes 1179656 | tf_op jit(solution)/shard_map/ppermute | solution.py:384
  49.4 1.0 copy-start.23
  50.4 96.9 %all-to-all-start.2 = ((bf16[8,2,16,64,128]{4,3,2,1,0:T(8,128)(2,1)}), bf16[8,2,16,64,128]{4,3,2,1,0:T(8,128)(2,1)}, u32[]{:S(2)}, u32[]{:S(2)}) async-start(bf16[8,2,16,64,128]{4,3,2,1,0:T(8,128)(2,1)} %gate.2.after_ref), calls=%async_computation.2 | async-start | bytes 8388608 | tf_op jit(solution)/shard_map/all_to_all | solution.py:432
  82.8 72.2 %copy-start.4 = (bf16[16,16,1024]{2,1,0:T(8,128)(2,1)S(1)}, bf16[16,16,1024]{2,1,0:T(8,128)(2,1)}, u32[]{:S(2)}) copy-start(bf16[16,16,1024]{2,1,0:T(8,128)(2,1)} %get-tuple-element.22.after_ref.refs_0_.refs_4_) | copy-start | bytes 1572868
  82.8 86.8 %copy-start.1 = (bf16[8,2,16,32,128]{4,3,2,1,0:T(8,128)(2,1)S(1)}, bf16[8,2,16,32,128]{4,3,2,1,0:T(8,128)(2,1)}, u32[]{:S(2)}) copy-start(bf16[8,2,16,32,128]{4,3,2,1,0:T(8,128)(2,1)} %first_transform.6.after_ref) | copy-start | bytes 6291460
  147.3 89.1 %all-to-all-start.1 = ((bf16[8,2,16,32,128]{4,3,2,1,0:T(8,128)(2,1)}), bf16[8,2,16,32,128]{4,3,2,1,0:T(8,128)(2,1)}, u32[]{:S(2)}, u32[]{:S(2)}) async-start(bf16[8,2,16,32,128]{4,3,2,1,0:T(8,128)(2,1)} %first_transform.6.after_ref), calls=%async_computation.1 | async-start | bytes 4194304 | tf_op jit(solution)/shard_map/all_to_all | solution.py:432
  154.9 12.7 %collective-permute-start.2 = (bf16[16,16,1024]{2,1,0:T(8,128)(2,1)S(1)}, bf16[16,16,1024]{2,1,0:T(8,128)(2,1)S(1)}, u32[]{:S(2)}, u32[]{:S(2)}) collective-permute-start(bf16[16,16,1024]{2,1,0:T(8,128)(2,1)S(1)} %copy-done.4), channel_id=1, source_target_pairs={{0,2},{1,3},{2,0},{3,1},{4,6},{5,7},{6,4},{7,5},{8,10},{9,11},{10,... | collective-permute-start | bytes 1572872 | tf_op jit(solution)/shard_map/ppermute | solution.py:390
  156.4 11.2 %collective-permute-start.3 = (bf16[16,16,1024]{2,1,0:T(8,128)(2,1)S(1)}, bf16[16,16,1024]{2,1,0:T(8,128)(2,1)S(1)}, u32[]{:S(2)}, u32[]{:S(2)}) collective-permute-start(bf16[16,16,1024]{2,1,0:T(8,128)(2,1)S(1)} %copy-done.4), channel_id=1, source_target_pairs={{0,1},{1,0},{2,3},{3,2},{4,5},{5,4},{6,7},{7,6},{8,9},{9,8},{10,11... | collective-permute-start | bytes 1572872 | tf_op jit(solution)/shard_map/ppermute | solution.py:390
  167.6 1.9 collective-permute-start.4
  167.6 2.9 copy-start.16
  169.5 1.1 copy-start.18
  170.6 0.7 copy-start.12
  181.9 48.0 %collective-permute-start.5 = (bf16[64,16,1024]{2,1,0:T(8,128)(2,1)}, bf16[64,16,1024]{2,1,0:T(8,128)(2,1)}, u32[]{:S(2)}, u32[]{:S(2)}) collective-permute-start(bf16[64,16,1024]{2,1,0:T(8,128)(2,1)} %get-tuple-element.25.after_ref.refs_0_.refs_8_), channel_id=1, source_target_pairs={{0,2},{1,3},{2,0},{3,1},{4,6},{5,7},{6,4},{7,5},{8,10},{9,11},{10,... | collective-permute-start | bytes 6291464 | tf_op jit(solution)/shard_map/ppermute | solution.py:390
  183.4 91.7 %collective-permute-start.6 = (bf16[64,16,1024]{2,1,0:T(8,128)(2,1)}, bf16[64,16,1024]{2,1,0:T(8,128)(2,1)}, u32[]{:S(2)}, u32[]{:S(2)}) collective-permute-start(bf16[64,16,1024]{2,1,0:T(8,128)(2,1)} %get-tuple-element.25.after_ref.refs_0_.refs_8_), channel_id=1, source_target_pairs={{0,1},{1,0},{2,3},{3,2},{4,5},{5,4},{6,7},{7,6},{8,9},{9,8},{10,11... | collective-permute-start | bytes 6291464 | tf_op jit(solution)/shard_map/ppermute | solution.py:390
  229.9 45.2 %collective-permute-start.7 = (bf16[64,16,1024]{2,1,0:T(8,128)(2,1)}, bf16[64,16,1024]{2,1,0:T(8,128)(2,1)}, u32[]{:S(2)}, u32[]{:S(2)}) collective-permute-start(bf16[64,16,1024]{2,1,0:T(8,128)(2,1)} %collective-permute-done.5.refs_1_.refs_9_), channel_id=1, source_target_pairs={{0,1},{1,0},{2,3},{3,2},{4,5},{5,4},{6,7},{7,6},{8,9},{9,8},{10,11... | collective-permute-start | bytes 6291464 | tf_op jit(solution)/shard_map/ppermute | solution.py:390
  236.4 47.7 %all-to-all-start.3 = ((bf16[8,2,16,16,128]{4,3,2,1,0:T(8,128)(2,1)}), bf16[8,2,16,16,128]{4,3,2,1,0:T(8,128)(2,1)}, u32[]{:S(2)}, u32[]{:S(2)}) async-start(bf16[8,2,16,16,128]{4,3,2,1,0:T(8,128)(2,1)} %first_transform.7.after_ref), calls=%async_computation.3 | async-start | bytes 2097152 | tf_op jit(solution)/shard_map/all_to_all | solution.py:432
  242.4 32.7 %copy-start = (bf16[64,16,1024]{2,1,0:T(8,128)(2,1)S(1)}, bf16[64,16,1024]{2,1,0:T(8,128)(2,1)}, u32[]{:S(2)}) copy-start(bf16[64,16,1024]{2,1,0:T(8,128)(2,1)} %get-tuple-element.25.after_ref.refs_0_.refs_8_) | copy-start | bytes 6291460
  242.4 32.7 %copy-start.13 = (f32[256,256]{1,0:T(8,128)S(1)}, f32[256,256]{1,0:T(8,128)}, u32[]{:S(2)}) copy-start(f32[256,256]{1,0:T(8,128)} %copy-done.12) | copy-start | bytes 786436
  249.8 25.3 %collective-permute-start.8 = (bf16[32,16,1024]{2,1,0:T(8,128)(2,1)}, bf16[32,16,1024]{2,1,0:T(8,128)(2,1)}, u32[]{:S(2)}, u32[]{:S(2)}) collective-permute-start(bf16[32,16,1024]{2,1,0:T(8,128)(2,1)} %get-tuple-element.26.after_ref.refs_0_.refs_12_), channel_id=1, source_target_pairs={{0,2},{1,3},{2,0},{3,1},{4,6},{5,7},{6,4},{7,5},{8,10},{9,11},{10,... | collective-permute-start | bytes 3145736 | tf_op jit(solution)/shard_map/ppermute | solution.py:390
  251.3 40.4 %collective-permute-start.9 = (bf16[32,16,1024]{2,1,0:T(8,128)(2,1)}, bf16[32,16,1024]{2,1,0:T(8,128)(2,1)}, u32[]{:S(2)}, u32[]{:S(2)}) collective-permute-start(bf16[32,16,1024]{2,1,0:T(8,128)(2,1)} %get-tuple-element.26.after_ref.refs_0_.refs_12_), channel_id=1, source_target_pairs={{0,1},{1,0},{2,3},{3,2},{4,5},{5,4},{6,7},{7,6},{8,9},{9,8},{10,11... | collective-permute-start | bytes 3145736 | tf_op jit(solution)/shard_map/ppermute | solution.py:390
  275.1 16.6 %collective-permute-start.10 = (bf16[32,16,1024]{2,1,0:T(8,128)(2,1)}, bf16[32,16,1024]{2,1,0:T(8,128)(2,1)}, u32[]{:S(2)}, u32[]{:S(2)}) collective-permute-start(bf16[32,16,1024]{2,1,0:T(8,128)(2,1)} %collective-permute-done.8.refs_1_.refs_13_), channel_id=1, source_target_pairs={{0,1},{1,0},{2,3},{3,2},{4,5},{5,4},{6,7},{7,6},{8,9},{9,8},{10,11... | collective-permute-start | bytes 3145736 | tf_op jit(solution)/shard_map/ppermute | solution.py:390
  275.2 1.2 copy-start.2
  283.4 0.7 copy-start.14
  284.1 7.6 %copy-start.3 = (bf16[32,16,1024]{2,1,0:T(8,128)(2,1)S(1)}, bf16[32,16,1024]{2,1,0:T(8,128)(2,1)}, u32[]{:S(2)}) copy-start(bf16[32,16,1024]{2,1,0:T(8,128)(2,1)} %get-tuple-element.26.after_ref.refs_0_.refs_12_) | copy-start | bytes 3145732
  284.1 7.6 %copy-start.15 = (f32[256,256]{1,0:T(8,128)S(1)}, f32[256,256]{1,0:T(8,128)}, u32[]{:S(2)}) copy-start(f32[256,256]{1,0:T(8,128)} %copy-done.14) | copy-start | bytes 786436
  290.0 14.5 %collective-permute-start.11 = (bf16[16,16,1024]{2,1,0:T(8,128)(2,1)}, bf16[16,16,1024]{2,1,0:T(8,128)(2,1)S(1)}, u32[]{:S(2)}, u32[]{:S(2)}) collective-permute-start(bf16[16,16,1024]{2,1,0:T(8,128)(2,1)} %get-tuple-element.28.after_ref.refs_0_.refs_16_), channel_id=1, source_target_pairs={{0,2},{1,3},{2,0},{3,1},{4,6},{5,7},{6,4},{7,5},{8,10},{9,11},{10,... | collective-permute-start | bytes 1572872 | tf_op jit(solution)/shard_map/ppermute | solution.py:390
  291.5 14.5 %collective-permute-start.12 = (bf16[16,16,1024]{2,1,0:T(8,128)(2,1)}, bf16[16,16,1024]{2,1,0:T(8,128)(2,1)}, u32[]{:S(2)}, u32[]{:S(2)}) collective-permute-start(bf16[16,16,1024]{2,1,0:T(8,128)(2,1)} %get-tuple-element.28.after_ref.refs_0_.refs_16_), channel_id=1, source_target_pairs={{0,1},{1,0},{2,3},{3,2},{4,5},{5,4},{6,7},{7,6},{8,9},{9,8},{10,11... | collective-permute-start | bytes 1572872 | tf_op jit(solution)/shard_map/ppermute | solution.py:390
  291.7 1.0 copy-start.5
  292.8 14.7 %copy-start.6 = (bf16[16,16,1024]{2,1,0:T(8,128)(2,1)S(1)}, bf16[16,16,1024]{2,1,0:T(8,128)(2,1)}, u32[]{:S(2)}) copy-start(bf16[16,16,1024]{2,1,0:T(8,128)(2,1)} %get-tuple-element.28.after_ref.refs_0_.refs_16_) | copy-start | bytes 1572868
  296.6 0.7 copy-start.10
  304.5 0.8 copy-start.7
  305.3 2.1 collective-permute-start.13
  307.4 1.0 copy-start.8
  308.5 0.9 copy-start.11
  309.4 2.1 copy-start.9
  309.4 2.1 copy-start.17
  309.4 2.1 copy-start.19
  309.4 2.1 copy-start.21
  311.6 1.6 copy-start.20
  313.2 1.2 copy-start.22

commit v7 on v6

--- a/solution.py
+++ b/solution.py
@@ -78,7 +78,8 @@
     )(value, after)
 
 
-def first_body(table_ref, grid_ref, after_ref, out_ref):
+def first_body(table_ref, grid_ref, after_ref, out_ref, token_ref):
+    token_ref[...] = jnp.zeros(token_ref.shape, F32)
     strips, _, chans, rows, width = out_ref.shape
     side_len = table_ref.shape[-1]
     table = table_ref[...]
@@ -104,7 +105,7 @@
         total = jnp.einsum("mv,cuv->mcu", table, grid[0], preferred_element_type=F32)
         total = total + jnp.einsum("mv,cuv->mcu", turned, grid[1], preferred_element_type=F32)
         total = total.astype(BF16).reshape(2, strips, rows, chans, width)
-        return total.transpose(1, 0, 3, 2, 4)
+        return total.transpose(1, 0, 3, 2, 4), jnp.zeros((8, 128), F32)
     block = 4 if chans % 4 == 0 else 1
     return pl.pallas_call(
         first_body,
@@ -114,8 +115,11 @@
             pl.BlockSpec((2, block, width, side_len), lambda i: (0, i, 0, 0)),
             ANY,
         ],
-        out_specs=pl.BlockSpec((strips, 2, block, rows, width), lambda i: (0, 0, i, 0, 0)),
-        out_shape=jax.ShapeDtypeStruct(shape, BF16),
+        out_specs=[
+            pl.BlockSpec((strips, 2, block, rows, width), lambda i: (0, 0, i, 0, 0)),
+            pl.BlockSpec((8, 128), lambda i: (0, 0)),
+        ],
+        out_shape=[jax.ShapeDtypeStruct(shape, BF16), jax.ShapeDtypeStruct((8, 128), F32)],
         compiler_params=kernel_params(60),
         cost_estimate=COST,
         name="first_transform",
@@ -422,13 +426,16 @@
     halves = {}
     moved = {}
     gathered = {}
+    pixels = {}
     state = dict(last=strip, gram=jnp.zeros((GRAM_ROWS * size, GRAM_ROWS * size), F32), bases=None)
 
     def first(chunk):
-        sent = first_transform(tables[chunk], grid, strips, state["last"])
+        sent, state["last"] = first_transform(tables[chunk], grid, strips, state["last"])
         if chunk == 1:
             sent = gate(sent, edges)
-        state["last"] = sent
+        if chunk == 2:
+            gather(0, gram_after=True)
+            sent = gate(sent, state["gram"])
         halves[chunk] = lax.all_to_all(sent, "strip", split_axis=0, concat_axis=0, tiled=True)
 
     def base():
@@ -438,36 +445,31 @@
         state["last"] = state["bases"][0]
 
     def second(chunk):
-        moved[chunk], pixels = second_transform(
+        moved[chunk], pixels[chunk] = second_transform(
             step_size, halves[chunk], cosine, sine_table, state["bases"][chunk], state["last"]
         )
-        state["last"] = pixels
-        return pixels
-
-    def gather(chunk, pixels, after=None):
-        pieces = gather_channels(pixels, after)
+        state["last"] = pixels[chunk]
+
+    def gather(chunk, gram_after):
+        pieces = gather_channels(pixels[chunk], state["last"])
         if chans % 16:
             pieces = [jnp.concatenate(pieces, axis=1)]
         gathered[chunk] = pieces
-
-    def gram(chunk):
-        state["gram"] = gram_step(gathered[chunk], state["gram"], state["last"])
-        state["last"] = state["gram"]
+        if gram_after:
+            state["gram"] = gram_step(pieces, state["gram"], state["last"])
+            state["last"] = state["gram"]
 
     first(0)
     if chunks > 1:
         first(1)
     base()
     for chunk in range(chunks):
-        pixels = second(chunk)
+        second(chunk)
         if chunk + 2 < chunks:
             first(chunk + 2)
-        if chunk > 1 or (chunk == 1 and chunks < 4):
-            gram(chunk - 1)
-        gather(chunk, pixels, state["gram"] if chunk + 1 == chunks else None)
-        if chunk == 0 and chunks >= 4:
-            gram(0)
-    gram(chunks - 1)
+        if chunk >= 1 and chunk - 1 not in gathered:
+            gather(chunk - 1, gram_after=True)
+    gather(chunks - 1, gram_after=True)
     order = range(chunks)
     return polar_step(
         shrinkage, state["gram"], [moved[k] for k in order], [gathered[k] for k in order], starts, sizes

time: 327 us -> 290 us (0.89)
  waiting for transfers between devices: 172 us -> 126 us
  local copies, waits for them, and re-layouts: 12.7 us -> 19.3 us
    ppermute x12, waiting for transfers between devices: 92.2 us -> 19.4 us  [swap(): return lax.ppermute(value, axis, [(i, i ^ bits) for i in range(count)])]
    all_to_all x4, waiting for transfers between devices: 64.6 us -> 91.2 us  [first(): lax.all_to_all(sent, 'strip', split_axis=0, concat_axis=0, tiled=True)]
    unnamed x48 -> x60, local copies, waits for them, and re-layouts: 11 us -> 17.5 us
  transfers between devices with their start and end apart: 18 -> 18, of which waited for: 9 -> 11; matrix products, arithmetic and copies ran while one was open for 1% -> 1% of each run, Pallas kernels for 25% -> 28%
where the time goes in v7:
time: 290 us; the launch traced here: 284 us
  waiting for transfers between devices  126 us (43%)
  Pallas kernels  97.7 us (34%)
  starting transfers between devices  39.1 us (13%)
  local copies, waits for them, and re-layouts  19.3 us (7%)
    all_to_all x4, waiting for transfers between devices, first(): lax.all_to_all(sent, 'strip', split_axis=0, concat_axis=0, tiled=True)  91.2 us
    pallas_call x4, Pallas kernels, first_transform(): pl.pallas_call(first_body, grid=(chans // block,), in_specs=[pl.BlockSpec...  34.2 us
    pallas_call x4, Pallas kernels, second_transform(): pl.pallas_call(second_body, grid=(side_len // block,), in_specs=[SMEM, pl...  29.2 us
    all_to_all x4, starting transfers between devices, first(): lax.all_to_all(sent, 'strip', split_axis=0, concat_axis=0, tiled=True)  27.1 us
    ppermute x12, waiting for transfers between devices, swap(): return lax.ppermute(value, axis, [(i, i ^ bits) for i in range(count)])  19.4 us
    unnamed x60, local copies, waits for them, and re-layouts  17.5 us
    ppermute x1, waiting for transfers between devices, neighbour_rows(): lax.ppermute(tail.astype(BF16), 'strip', [(i, i + 1) for i in range(ends)])  13.3 us
    pallas_call x4, Pallas kernels, gram_step(): pl.pallas_call(functools.partial(gram_body, len(pieces)), grid=(rows // b...  13.3 us
  transfers between devices with their start and end apart: 18, of which 11 were waited for; matrix products, arithmetic and copies ran while one was open for 1% of the time, Pallas kernels for 28%

profile of v7, /device:TPU:12, one launch (start us, length us, event | category | flops | bytes accessed | tf_op | source)
XLA Modules:
  0.0 284.2 jit_solution(8509853674603071064)
XLA Ops:
  0.0 6.5 %first_transform.4 = (bf16[8,2,16,16,128]{4,3,2,1,0:T(8,128)(2,1)}, f32[8,128]{1,0:T(8,128)}) custom-call(bf16[256,1024]{1,0:T(8,128)(2,1)} %constant.20.clone.table_ref, bf16[2,16,128,1024]{3,2,1,0:T(8,128)(2,1)} %grid_ref.7, s32[1]{0:T(128)} %bitcast.after_ref.strip_ref), custom_call_target="tpu_custom_call" | custom-call | bytes 65536 | tf_op jit(solution)/shard_map/first_transform/pallas_call | solution.py:110
  6.5 6.2 %all-to-all-start = ((bf16[8,2,16,16,128]{4,3,2,1,0:T(8,128)(2,1)}), bf16[8,2,16,16,128]{4,3,2,1,0:T(8,128)(2,1)S(1)}, u32[]{:S(2)}, u32[]{:S(2)}) async-start(bf16[8,2,16,16,128]{4,3,2,1,0:T(8,128)(2,1)} %get-tuple-element.27), calls=%async_computation | async-start | bytes 2097152 | tf_op jit(solution)/shard_map/all_to_all | solution.py:439
  12.7 1.7 fusion
  14.5 3.4 %collective-permute-start = (bf16[16,12,1024]{2,1,0:T(8,128)(2,1)S(1)}, bf16[16,12,1024]{2,1,0:T(8,128)(2,1)S(1)}, u32[]{:S(2)}, u32[]{:S(2)}) collective-permute-start(bf16[16,12,1024]{2,1,0:T(8,128)(2,1)S(1)} %get-tuple-element.28), channel_id=1, source_target_pairs={{0,4},{4,8},{8,12},{12,16},{16,20},{20,24},{24,28},{1,5},{5,9},{9,... | collective-permute-start | bytes 1179656 | tf_op jit(solution)/shard_map/ppermute | solution.py:387
  17.9 2.5 collective-permute-start.1
  20.3 12.8 %first_transform.5 = (bf16[8,2,16,64,128]{4,3,2,1,0:T(8,128)(2,1)}, f32[8,128]{1,0:T(8,128)}) custom-call(bf16[1024,1024]{1,0:T(8,128)(2,1)} %constant.21.clone.table_ref, bf16[2,16,128,1024]{3,2,1,0:T(8,128)(2,1)} %grid_ref.7, f32[8,128]{1,0:T(8,128)} %get-tuple-element.30.after_ref), custom_call_target="tpu_custom_call" | custom-call | bytes 65536 | tf_op jit(solution)/shard_map/first_transform/pallas_call | solution.py:110
  33.1 13.3 %collective-permute-done = bf16[16,12,1024]{2,1,0:T(8,128)(2,1)S(1)} collective-permute-done((bf16[16,12,1024]{2,1,0:T(8,128)(2,1)S(1)}, bf16[16,12,1024]{2,1,0:T(8,128)(2,1)S(1)}, u32[]{:S(2)}, u32[]{:S(2)}) %collective-permute-start) | collective-permute-done | bytes 393248 | tf_op jit(solution)/shard_map/ppermute | solution.py:387
  46.4 1.9 collective-permute-done.1
  48.3 1.1 pad_maximum_fusion.edge_ref.after_ref
  49.5 1.0 copy-done.29
  50.4 7.0 %all-to-all-start.2 = ((bf16[8,2,16,64,128]{4,3,2,1,0:T(8,128)(2,1)}), bf16[8,2,16,64,128]{4,3,2,1,0:T(8,128)(2,1)}, u32[]{:S(2)}, u32[]{:S(2)}) async-start(bf16[8,2,16,64,128]{4,3,2,1,0:T(8,128)(2,1)} %gate.8), calls=%async_computation.2 | async-start | bytes 8388608 | tf_op jit(solution)/shard_map/all_to_all | solution.py:439
  57.4 11.2 %base_step.1 = (f32[16,16,1024]{2,1,0:T(8,128)}, f32[16,64,1024]{2,1,0:T(8,128)}, f32[16,32,1024]{2,1,0:T(8,128)}, f32[16,16,1024]{2,1,0:T(8,128)}) custom-call(s32[1]{0:T(128)} %bitcast.after_ref.strip_ref, f32[16]{0:T(128)} %step_ref.9, f32[3,4]{1,0:T(4,128)} %highpass_ref.1, f32[16,128,1024]{2,1,0:T(8,128)} %model_ref.1, ...), custom_call_target="tpu_custom_call" | custom-call | bytes 65536 | tf_op jit(solution)/shard_map/base_step/pallas_call | solution.py:191
  68.6 5.7 %second_transform.4 = (f32[16,16,1024]{2,1,0:T(8,128)}, bf16[16,16,1024]{2,1,0:T(8,128)(2,1)}) custom-call(f32[16]{0:T(128)} %step_ref.9, bf16[8,2,16,16,128]{4,3,2,1,0:T(8,128)(2,1)} %copy-done.29, bf16[1024,1024]{1,0:T(8,128)(2,1)} %constant.22.clone.cosine_ref, bf16[1024,1024]{1,0:T(8,128)(2,1)} %constant.23.clone.sine_ref, ...), custom_call_target="tpu_custom_call" | custom-call | bytes 65536 | tf_op jit(solution)/shard_map/second_transform/pallas_call | solution.py:234
  74.3 1.5 collective-permute-start.2
  75.9 8.5 %first_transform.6 = (bf16[8,2,16,32,128]{4,3,2,1,0:T(8,128)(2,1)}, f32[8,128]{1,0:T(8,128)}) custom-call(bf16[512,1024]{1,0:T(8,128)(2,1)} %constant.24.clone.table_ref, bf16[2,16,128,1024]{3,2,1,0:T(8,128)(2,1)} %grid_ref.7, bf16[16,16,1024]{2,1,0:T(8,128)(2,1)} %get-tuple-element.33.after_ref.refs_0_.refs_4_), custom_call_target="tpu_custom_call" | custom-call | bytes 65536 | tf_op jit(solution)/shard_map/first_transform/pallas_call | solution.py:110
  84.4 3.4 %collective-permute-done.2.value_ref = bf16[16,16,1024]{2,1,0:T(8,128)(2,1)S(1)} collective-permute-done((bf16[16,16,1024]{2,1,0:T(8,128)(2,1)}, bf16[16,16,1024]{2,1,0:T(8,128)(2,1)S(1)}, u32[]{:S(2)}, u32[]{:S(2)}) %collective-permute-start.2) | collective-permute-done | bytes 524320 | tf_op jit(solution)/shard_map/ppermute | solution.py:394
  87.7 0.9 copy-done.7
  88.6 2.1 collective-permute-done.4.refs_3_.refs_7_
  90.8 1.2 copy-done.8
  92.6 1.0 gram_step.4.after_ref.before_ref
  94.4 53.0 %all-to-all-done.2.half_ref = bf16[8,2,16,64,128]{4,3,2,1,0:T(8,128)(2,1)} async-done(((bf16[8,2,16,64,128]{4,3,2,1,0:T(8,128)(2,1)}), bf16[8,2,16,64,128]{4,3,2,1,0:T(8,128)(2,1)}, u32[]{:S(2)}, u32[]{:S(2)}) %all-to-all-start.2) | async-done | bytes 4194336 | tf_op jit(solution)/shard_map/all_to_all | solution.py:439
  147.3 7.6 %all-to-all-start.1 = ((bf16[8,2,16,32,128]{4,3,2,1,0:T(8,128)(2,1)}), bf16[8,2,16,32,128]{4,3,2,1,0:T(8,128)(2,1)}, u32[]{:S(2)}, u32[]{:S(2)}) async-start(bf16[8,2,16,32,128]{4,3,2,1,0:T(8,128)(2,1)} %gate.7), calls=%async_computation.1 | async-start | bytes 4194304 | tf_op jit(solution)/shard_map/all_to_all | solution.py:439
  154.9 10.6 %second_transform.5 = (f32[16,64,1024]{2,1,0:T(8,128)}, bf16[64,16,1024]{2,1,0:T(8,128)(2,1)}) custom-call(f32[16]{0:T(128)} %step_ref.9, bf16[8,2,16,64,128]{4,3,2,1,0:T(8,128)(2,1)} %all-to-all-done.2.half_ref, bf16[1024,1024]{1,0:T(8,128)(2,1)} %constant.22.clone.cosine_ref, bf16[1024,1024]{1,0:T(8,128)(2,1)} %constant.23.clone.sine_ref, ...), custom_call_target="tpu_custom_call" | custom-call | bytes 65536 | tf_op jit(solution)/shard_map/second_transform/pallas_call | solution.py:234
  165.6 1.5 collective-permute-start.5
  167.1 6.5 %first_transform.7 = (bf16[8,2,16,16,128]{4,3,2,1,0:T(8,128)(2,1)}, f32[8,128]{1,0:T(8,128)}) custom-call(bf16[256,1024]{1,0:T(8,128)(2,1)} %constant.25.clone.table_ref, bf16[2,16,128,1024]{3,2,1,0:T(8,128)(2,1)} %grid_ref.7, bf16[64,16,1024]{2,1,0:T(8,128)(2,1)} %get-tuple-element.39.after_ref.refs_0_.refs_8_), custom_call_target="tpu_custom_call" | custom-call | bytes 65536 | tf_op jit(solution)/shard_map/first_transform/pallas_call | solution.py:110
  173.6 25.9 %all-to-all-done.1.half_ref = bf16[8,2,16,32,128]{4,3,2,1,0:T(8,128)(2,1)} async-done(((bf16[8,2,16,32,128]{4,3,2,1,0:T(8,128)(2,1)}), bf16[8,2,16,32,128]{4,3,2,1,0:T(8,128)(2,1)}, u32[]{:S(2)}, u32[]{:S(2)}) %all-to-all-start.1) | async-done | bytes 2097184 | tf_op jit(solution)/shard_map/all_to_all | solution.py:439
  199.5 7.2 %second_transform.6 = (f32[16,32,1024]{2,1,0:T(8,128)}, bf16[32,16,1024]{2,1,0:T(8,128)(2,1)}) custom-call(f32[16]{0:T(128)} %step_ref.9, bf16[8,2,16,32,128]{4,3,2,1,0:T(8,128)(2,1)} %all-to-all-done.1.half_ref, bf16[1024,1024]{1,0:T(8,128)(2,1)} %constant.22.clone.cosine_ref, bf16[1024,1024]{1,0:T(8,128)(2,1)} %constant.23.clone.sine_ref, ...), custom_call_target="tpu_custom_call" | custom-call | bytes 65536 | tf_op jit(solution)/shard_map/second_transform/pallas_call | solution.py:234
  206.7 5.4 %collective-permute-done.5.value_ref = bf16[64,16,1024]{2,1,0:T(8,128)(2,1)S(1)} collective-permute-done((bf16[64,16,1024]{2,1,0:T(8,128)(2,1)}, bf16[64,16,1024]{2,1,0:T(8,128)(2,1)S(1)}, u32[]{:S(2)}, u32[]{:S(2)}) %collective-permute-start.5) | collective-permute-done | bytes 2097184 | tf_op jit(solution)/shard_map/ppermute | solution.py:394
  212.1 1.3 copy-done
  213.5 6.3 %all-to-all-start.3 = ((bf16[8,2,16,16,128]{4,3,2,1,0:T(8,128)(2,1)}), bf16[8,2,16,16,128]{4,3,2,1,0:T(8,128)(2,1)}, u32[]{:S(2)}, u32[]{:S(2)}) async-start(bf16[8,2,16,16,128]{4,3,2,1,0:T(8,128)(2,1)} %get-tuple-element.42), calls=%async_computation.3 | async-start | bytes 2097152 | tf_op jit(solution)/shard_map/all_to_all | solution.py:439
  219.7 1.5 collective-permute-start.8
  221.3 1.6 copy-done.2
  222.9 6.7 %gram_step.5.after_ref.before_ref = f32[256,256]{1,0:T(8,128)S(1)} custom-call(f32[256,256]{1,0:T(8,128)S(1)} %copy-done.16, bf16[32,16,1024]{2,1,0:T(8,128)(2,1)S(1)} %copy-done.3, bf16[64,16,1024]{2,1,0:T(8,128)(2,1)S(1)} %copy-done.2, bf16[64,16,1024]{2,1,0:T(8,128)(2,1)S(1)} %copy-done.1, bf16[64,16,1024]{2,1,0:T(8,128)(2,1)} %collective-permute-done.6.refs_2_.refs_10_, ...), custom_call_target="tpu_custom_call" | custom-call | bytes 65536 | tf_op jit(solution)/shard_map/gram_step/pallas_call | solution.py:281
  230.2 12.4 %all-to-all-done.3.half_ref = bf16[8,2,16,16,128]{4,3,2,1,0:T(8,128)(2,1)} async-done(((bf16[8,2,16,16,128]{4,3,2,1,0:T(8,128)(2,1)}), bf16[8,2,16,16,128]{4,3,2,1,0:T(8,128)(2,1)}, u32[]{:S(2)}, u32[]{:S(2)}) %all-to-all-start.3) | async-done | bytes 1048608 | tf_op jit(solution)/shard_map/all_to_all | solution.py:439
  242.6 5.7 %second_transform.7 = (f32[16,16,1024]{2,1,0:T(8,128)}, bf16[16,16,1024]{2,1,0:T(8,128)(2,1)}) custom-call(f32[16]{0:T(128)} %step_ref.9, bf16[8,2,16,16,128]{4,3,2,1,0:T(8,128)(2,1)} %all-to-all-done.3.half_ref, bf16[1024,1024]{1,0:T(8,128)(2,1)} %constant.22.clone.cosine_ref, bf16[1024,1024]{1,0:T(8,128)(2,1)} %constant.23.clone.sine_ref, ...), custom_call_target="tpu_custom_call" | custom-call | bytes 65536 | tf_op jit(solution)/shard_map/second_transform/pallas_call | solution.py:234
  248.4 0.9 copy-done.4
  249.3 1.5 collective-permute-start.11
  251.2 3.6 %gram_step.6.after_ref.before_ref = f32[256,256]{1,0:T(8,128)S(1)} custom-call(f32[256,256]{1,0:T(8,128)S(1)} %copy-done.20, bf16[16,16,1024]{2,1,0:T(8,128)(2,1)S(1)} %copy-done.4, bf16[32,16,1024]{2,1,0:T(8,128)(2,1)S(1)} %copy-done.3, bf16[32,16,1024]{2,1,0:T(8,128)(2,1)} %gate.10.refs_1_.refs_13_, ...), custom_call_target="tpu_custom_call" | custom-call | bytes 65536 | tf_op jit(solution)/shard_map/gram_step/pallas_call | solution.py:281
  254.8 1.0 copy-done.13
  256.5 6.6 %collective-permute-done.11.value_ref = bf16[16,16,1024]{2,1,0:T(8,128)(2,1)S(1)} collective-permute-done((bf16[16,16,1024]{2,1,0:T(8,128)(2,1)S(1)}, bf16[16,16,1024]{2,1,0:T(8,128)(2,1)S(1)}, u32[]{:S(2)}, u32[]{:S(2)}) %collective-permute-start.11) | collective-permute-done | bytes 524320 | tf_op jit(solution)/shard_map/ppermute | solution.py:394
  264.7 1.5 collective-permute-done.13.refs_3_.refs_19_
  266.1 1.0 copy-done.11
  267.2 0.9 copy-done.18
  268.1 2.1 gram_step.7.gram_ref
  270.3 1.6 copy-done.25
  271.9 1.2 copy-done.26
  273.1 1.2 copy-done.27
  274.3 9.7 %polar_step.1 = f32[16,128,1024]{2,1,0:T(8,128)} custom-call(f32[1]{0:T(128)S(6)} %copy.24.shrink_ref, f32[256,256]{1,0:T(8,128)S(1)} %gram_step.7.gram_ref, f32[16,16,1024]{2,1,0:T(8,128)S(1)} %copy-done.26, f32[16,64,1024]{2,1,0:T(8,128)} %get-tuple-element.46.refs_1_, f32[16,32,1024]{2,1,0:T(8,128)S(1)} %copy-done.25, f32[16,16,1024]{2,1,0:T(8,128)S(1)} %copy-done.27, ...), custom_call_target="tpu_custom_call" | custom-call | bytes 65536 | tf_op jit(solution)/shard_map/polar_step/pallas_call | solution.py:366
  (71 shorter events, 4.2 us)
Async XLA Ops:
  6.5 43.0 %all-to-all-start = ((bf16[8,2,16,16,128]{4,3,2,1,0:T(8,128)(2,1)}), bf16[8,2,16,16,128]{4,3,2,1,0:T(8,128)(2,1)S(1)}, u32[]{:S(2)}, u32[]{:S(2)}) async-start(bf16[8,2,16,16,128]{4,3,2,1,0:T(8,128)(2,1)} %get-tuple-element.27), calls=%async_computation | async-start | bytes 2097152 | tf_op jit(solution)/shard_map/all_to_all | solution.py:439
  14.5 31.9 %collective-permute-start = (bf16[16,12,1024]{2,1,0:T(8,128)(2,1)S(1)}, bf16[16,12,1024]{2,1,0:T(8,128)(2,1)S(1)}, u32[]{:S(2)}, u32[]{:S(2)}) collective-permute-start(bf16[16,12,1024]{2,1,0:T(8,128)(2,1)S(1)} %get-tuple-element.28), channel_id=1, source_target_pairs={{0,4},{4,8},{8,12},{12,16},{16,20},{20,24},{24,28},{1,5},{5,9},{9,... | collective-permute-start | bytes 1179656 | tf_op jit(solution)/shard_map/ppermute | solution.py:387
  17.9 30.5 %collective-permute-start.1 = (bf16[16,12,1024]{2,1,0:T(8,128)(2,1)S(1)}, bf16[16,12,1024]{2,1,0:T(8,128)(2,1)S(1)}, u32[]{:S(2)}, u32[]{:S(2)}) collective-permute-start(bf16[16,12,1024]{2,1,0:T(8,128)(2,1)S(1)} %get-tuple-element.29), channel_id=1, source_target_pairs={{4,0},{8,4},{12,8},{16,12},{20,16},{24,20},{28,24},{5,1},{9,5},{13... | collective-permute-start | bytes 1179656 | tf_op jit(solution)/shard_map/ppermute | solution.py:388
  49.5 1.0 copy-start.29
  50.4 96.9 %all-to-all-start.2 = ((bf16[8,2,16,64,128]{4,3,2,1,0:T(8,128)(2,1)}), bf16[8,2,16,64,128]{4,3,2,1,0:T(8,128)(2,1)}, u32[]{:S(2)}, u32[]{:S(2)}) async-start(bf16[8,2,16,64,128]{4,3,2,1,0:T(8,128)(2,1)} %gate.8), calls=%async_computation.2 | async-start | bytes 8388608 | tf_op jit(solution)/shard_map/all_to_all | solution.py:439
  74.3 16.4 %copy-start.5 = (bf16[16,16,1024]{2,1,0:T(8,128)(2,1)S(1)}, bf16[16,16,1024]{2,1,0:T(8,128)(2,1)}, u32[]{:S(2)}) copy-start(bf16[16,16,1024]{2,1,0:T(8,128)(2,1)} %get-tuple-element.33.after_ref.refs_0_.refs_4_) | copy-start | bytes 1572868
  74.3 13.4 %collective-permute-start.2 = (bf16[16,16,1024]{2,1,0:T(8,128)(2,1)}, bf16[16,16,1024]{2,1,0:T(8,128)(2,1)S(1)}, u32[]{:S(2)}, u32[]{:S(2)}) collective-permute-start(bf16[16,16,1024]{2,1,0:T(8,128)(2,1)} %get-tuple-element.33.after_ref.refs_0_.refs_4_), channel_id=1, source_target_pairs={{0,2},{1,3},{2,0},{3,1},{4,6},{5,7},{6,4},{7,5},{8,10},{9,11},{10,... | collective-permute-start | bytes 1572872 | tf_op jit(solution)/shard_map/ppermute | solution.py:394
  75.9 12.7 %collective-permute-start.3 = (bf16[16,16,1024]{2,1,0:T(8,128)(2,1)}, bf16[16,16,1024]{2,1,0:T(8,128)(2,1)S(1)}, u32[]{:S(2)}, u32[]{:S(2)}) collective-permute-start(bf16[16,16,1024]{2,1,0:T(8,128)(2,1)} %get-tuple-element.33.after_ref.refs_0_.refs_4_), channel_id=1, source_target_pairs={{0,1},{1,0},{2,3},{3,2},{4,5},{5,4},{6,7},{7,6},{8,9},{9,8},{10,11... | collective-permute-start | bytes 1572872 | tf_op jit(solution)/shard_map/ppermute | solution.py:394
  87.7 0.9 copy-start.7
  88.6 2.1 collective-permute-start.4
  88.6 5.8 %copy-start.21 = (bf16[16,16,1024]{2,1,0:T(8,128)(2,1)}, bf16[16,16,1024]{2,1,0:T(8,128)(2,1)S(1)}, u32[]{:S(2)}) copy-start(bf16[16,16,1024]{2,1,0:T(8,128)(2,1)S(1)} %collective-permute-done.3.refs_2_.refs_6_) | copy-start | bytes 1572868
  90.7 2.9 %copy-start.23 = (bf16[16,16,1024]{2,1,0:T(8,128)(2,1)}, bf16[16,16,1024]{2,1,0:T(8,128)(2,1)S(1)}, u32[]{:S(2)}) copy-start(bf16[16,16,1024]{2,1,0:T(8,128)(2,1)S(1)} %collective-permute-done.4.refs_3_.refs_7_) | copy-start | bytes 1572868
  90.7 1.2 copy-start.8
  92.0 0.7 copy-start.28
  93.6 0.7 copy-start.15
  147.3 52.2 %all-to-all-start.1 = ((bf16[8,2,16,32,128]{4,3,2,1,0:T(8,128)(2,1)}), bf16[8,2,16,32,128]{4,3,2,1,0:T(8,128)(2,1)}, u32[]{:S(2)}, u32[]{:S(2)}) async-start(bf16[8,2,16,32,128]{4,3,2,1,0:T(8,128)(2,1)} %gate.7), calls=%async_computation.1 | async-start | bytes 4194304 | tf_op jit(solution)/shard_map/all_to_all | solution.py:439
  165.6 46.6 %collective-permute-start.5 = (bf16[64,16,1024]{2,1,0:T(8,128)(2,1)}, bf16[64,16,1024]{2,1,0:T(8,128)(2,1)S(1)}, u32[]{:S(2)}, u32[]{:S(2)}) collective-permute-start(bf16[64,16,1024]{2,1,0:T(8,128)(2,1)} %get-tuple-element.39.after_ref.refs_0_.refs_8_), channel_id=1, source_target_pairs={{0,2},{1,3},{2,0},{3,1},{4,6},{5,7},{6,4},{7,5},{8,10},{9,11},{10,... | collective-permute-start | bytes 6291464 | tf_op jit(solution)/shard_map/ppermute | solution.py:394
  167.1 54.2 %collective-permute-start.6 = (bf16[64,16,1024]{2,1,0:T(8,128)(2,1)}, bf16[64,16,1024]{2,1,0:T(8,128)(2,1)}, u32[]{:S(2)}, u32[]{:S(2)}) collective-permute-start(bf16[64,16,1024]{2,1,0:T(8,128)(2,1)} %get-tuple-element.39.after_ref.refs_0_.refs_8_), channel_id=1, source_target_pairs={{0,1},{1,0},{2,3},{3,2},{4,5},{5,4},{6,7},{7,6},{8,9},{9,8},{10,11... | collective-permute-start | bytes 6291464 | tf_op jit(solution)/shard_map/ppermute | solution.py:394
  212.1 1.3 copy-start
  213.4 6.3 %copy-start.3 = (bf16[32,16,1024]{2,1,0:T(8,128)(2,1)S(1)}, bf16[32,16,1024]{2,1,0:T(8,128)(2,1)}, u32[]{:S(2)}) copy-start(bf16[32,16,1024]{2,1,0:T(8,128)(2,1)} %get-tuple-element.41.after_ref.refs_0_.refs_12_) | copy-start | bytes 3145732
  213.5 7.8 %copy-start.16 = (f32[256,256]{1,0:T(8,128)S(1)}, f32[256,256]{1,0:T(8,128)}, u32[]{:S(2)}) copy-start(f32[256,256]{1,0:T(8,128)} %copy-done.15) | copy-start | bytes 786436
  213.5 7.8 %copy-start.1 = (bf16[64,16,1024]{2,1,0:T(8,128)(2,1)S(1)}, bf16[64,16,1024]{2,1,0:T(8,128)(2,1)}, u32[]{:S(2)}) copy-start(bf16[64,16,1024]{2,1,0:T(8,128)(2,1)} %gate.9.refs_1_.refs_9_) | copy-start | bytes 6291460
  213.5 7.8 %collective-permute-start.7 = (bf16[64,16,1024]{2,1,0:T(8,128)(2,1)}, bf16[64,16,1024]{2,1,0:T(8,128)(2,1)}, u32[]{:S(2)}, u32[]{:S(2)}) collective-permute-start(bf16[64,16,1024]{2,1,0:T(8,128)(2,1)} %gate.9.refs_1_.refs_9_), channel_id=1, source_target_pairs={{0,1},{1,0},{2,3},{3,2},{4,5},{5,4},{6,7},{7,6},{8,9},{9,8},{10,11... | collective-permute-start | bytes 6291464 | tf_op jit(solution)/shard_map/ppermute | solution.py:394
  213.5 29.2 %all-to-all-start.3 = ((bf16[8,2,16,16,128]{4,3,2,1,0:T(8,128)(2,1)}), bf16[8,2,16,16,128]{4,3,2,1,0:T(8,128)(2,1)}, u32[]{:S(2)}, u32[]{:S(2)}) async-start(bf16[8,2,16,16,128]{4,3,2,1,0:T(8,128)(2,1)} %get-tuple-element.42), calls=%async_computation.3 | async-start | bytes 2097152 | tf_op jit(solution)/shard_map/all_to_all | solution.py:439
  219.7 28.5 %collective-permute-start.8 = (bf16[32,16,1024]{2,1,0:T(8,128)(2,1)S(1)}, bf16[32,16,1024]{2,1,0:T(8,128)(2,1)}, u32[]{:S(2)}, u32[]{:S(2)}) collective-permute-start(bf16[32,16,1024]{2,1,0:T(8,128)(2,1)S(1)} %copy-done.3), channel_id=1, source_target_pairs={{0,2},{1,3},{2,0},{3,1},{4,6},{5,7},{6,4},{7,5},{8,10},{9,11},{10,... | collective-permute-start | bytes 3145736 | tf_op jit(solution)/shard_map/ppermute | solution.py:394
  221.3 29.6 %collective-permute-start.9 = (bf16[32,16,1024]{2,1,0:T(8,128)(2,1)S(1)}, bf16[32,16,1024]{2,1,0:T(8,128)(2,1)}, u32[]{:S(2)}, u32[]{:S(2)}) collective-permute-start(bf16[32,16,1024]{2,1,0:T(8,128)(2,1)S(1)} %copy-done.3), channel_id=1, source_target_pairs={{0,1},{1,0},{2,3},{3,2},{4,5},{5,4},{6,7},{7,6},{8,9},{9,8},{10,11... | collective-permute-start | bytes 3145736 | tf_op jit(solution)/shard_map/ppermute | solution.py:394
  221.3 1.6 copy-start.2
  229.5 0.7 copy-start.19
  248.3 1.0 copy-start.4
  248.3 3.0 %copy-start.20 = (f32[256,256]{1,0:T(8,128)S(1)}, f32[256,256]{1,0:T(8,128)}, u32[]{:S(2)}) copy-start(f32[256,256]{1,0:T(8,128)} %copy-done.19) | copy-start | bytes 786436
  248.3 2.9 %collective-permute-start.10 = (bf16[32,16,1024]{2,1,0:T(8,128)(2,1)}, bf16[32,16,1024]{2,1,0:T(8,128)(2,1)S(1)}, u32[]{:S(2)}, u32[]{:S(2)}) collective-permute-start(bf16[32,16,1024]{2,1,0:T(8,128)(2,1)} %gate.10.refs_1_.refs_13_), channel_id=1, source_target_pairs={{0,1},{1,0},{2,3},{3,2},{4,5},{5,4},{6,7},{7,6},{8,9},{9,8},{10,11... | collective-permute-start | bytes 3145736 | tf_op jit(solution)/shard_map/ppermute | solution.py:394
  249.3 13.8 %collective-permute-start.11 = (bf16[16,16,1024]{2,1,0:T(8,128)(2,1)S(1)}, bf16[16,16,1024]{2,1,0:T(8,128)(2,1)S(1)}, u32[]{:S(2)}, u32[]{:S(2)}) collective-permute-start(bf16[16,16,1024]{2,1,0:T(8,128)(2,1)S(1)} %copy-done.4), channel_id=1, source_target_pairs={{0,2},{1,3},{2,0},{3,1},{4,6},{5,7},{6,4},{7,5},{8,10},{9,11},{10,... | collective-permute-start | bytes 1572872 | tf_op jit(solution)/shard_map/ppermute | solution.py:394
  250.8 13.8 %collective-permute-start.12 = (bf16[16,16,1024]{2,1,0:T(8,128)(2,1)S(1)}, bf16[16,16,1024]{2,1,0:T(8,128)(2,1)}, u32[]{:S(2)}, u32[]{:S(2)}) collective-permute-start(bf16[16,16,1024]{2,1,0:T(8,128)(2,1)S(1)} %copy-done.4), channel_id=1, source_target_pairs={{0,1},{1,0},{2,3},{3,2},{4,5},{5,4},{6,7},{7,6},{8,9},{9,8},{10,11... | collective-permute-start | bytes 1572872 | tf_op jit(solution)/shard_map/ppermute | solution.py:394
  254.8 1.0 copy-start.13
  255.8 0.7 copy-start.17
  256.5 13.7 %copy-start.6 = (bf16[16,16,1024]{2,1,0:T(8,128)(2,1)S(1)}, bf16[16,16,1024]{2,1,0:T(8,128)(2,1)}, u32[]{:S(2)}) copy-start(bf16[16,16,1024]{2,1,0:T(8,128)(2,1)} %get-tuple-element.33.after_ref.refs_0_.refs_4_) | copy-start | bytes 1572868
  256.5 13.7 %copy-start.9 = (bf16[16,16,1024]{2,1,0:T(8,128)(2,1)S(1)}, bf16[16,16,1024]{2,1,0:T(8,128)(2,1)}, u32[]{:S(2)}) copy-start(bf16[16,16,1024]{2,1,0:T(8,128)(2,1)} %gate.6.refs_1_.refs_5_) | copy-start | bytes 1572868
  263.2 0.8 copy-start.10
  264.0 2.1 collective-permute-start.13
  266.1 1.0 copy-start.11
  267.1 0.9 copy-start.18
  268.1 2.1 copy-start.12
  268.1 2.2 copy-start.14
  268.1 2.2 copy-start.22
  268.1 2.2 copy-start.24
  270.3 1.6 copy-start.25
  271.9 1.2 copy-start.26
  273.1 1.2 copy-start.27

commit v8 on v7

--- a/solution.py
+++ b/solution.py
@@ -57,7 +57,8 @@
 
 
 def chunk_rows(own_rows):
-    sizes = [EDGE_ROWS, own_rows // 2, own_rows // 2 - 2 * EDGE_ROWS, EDGE_ROWS]
+    quarter = own_rows // 4
+    sizes = [quarter, own_rows - 2 * quarter - EDGE_ROWS, quarter, EDGE_ROWS]
     sizes = [size for size in sizes if size > 0]
     return [sum(sizes[:place]) for place in range(len(sizes))], sizes
 
@@ -284,7 +285,7 @@
         in_specs=[pl.BlockSpec(before.shape, lambda i: (0, 0)), ANY] + [spec] * len(pieces),
         out_specs=pl.BlockSpec(before.shape, lambda i: (0, 0)),
         out_shape=jax.ShapeDtypeStruct(before.shape, F32),
-        compiler_params=kernel_params(16),
+        compiler_params=kernel_params(60),
         cost_estimate=COST,
         name="gram_step",
     )(before, after, *pieces)
@@ -312,21 +313,39 @@
     pixels = refs[chunks * (groups + 1) + 5 :]
     own, all_rows, side_len = moved.shape
     size = pixels[0].shape[2] * groups
+
+    blocks = [
+        (chunk, row) for chunk in [chunks - 1] + list(range(chunks - 1)) for row in range(0, sizes[chunk], EDGE_ROWS)
+    ]
+    pixel_copies = []
     moved_copies = []
-    pixel_copies = []
-    for chunk in range(chunks):
-        part = pl.ds(starts[chunk], sizes[chunk])
-        copies = []
-        for group in range(groups):
-            place = chunk * groups + group
-            copies.append(pltpu.make_async_copy(pixels_hbm[place], pixels[chunk].at[group], pixel_sems.at[place]))
+    for place, (chunk, row) in enumerate(blocks):
+        part = pl.ds(row, EDGE_ROWS)
+        into = pl.ds(starts[chunk] + row, EDGE_ROWS)
+        copies = [
+            pltpu.make_async_copy(
+                pixels_hbm[chunk * groups + group].at[part], pixels[chunk].at[group, part], pixel_sems.at[place, group]
+            )
+            for group in range(groups)
+        ]
         pixel_copies.append(copies)
-        moved_copies.append(pltpu.make_async_copy(moved_hbm[chunk], moved.at[:, part], moved_sems.at[chunk]))
+        moved_copies.append(
+            pltpu.make_async_copy(moved_hbm[chunk].at[:, part], moved.at[:, into], moved_sems.at[place])
+        )
         for copy in copies + moved_copies[-1:]:
             copy.start()
+
+    last_blocks = sizes[-1] // EDGE_ROWS
+    for copies in pixel_copies[:last_blocks]:
+        for copy in copies:
+            copy.wait()
+    total = gram_ref[...]
+    for first in range(0, sizes[-1], GRAM_ROWS):
+        data = stacked([pixels[-1].at[group] for group in range(groups)], first, GRAM_ROWS)
+        total = total + dot_nt(data, data)
     gram = jnp.zeros((size, size), F32)
     for i in range(GRAM_ROWS):
-        gram = gram + gram_ref[i * size : (i + 1) * size, i * size : (i + 1) * size]
+        gram = gram + total[i * size : (i + 1) * size, i * size : (i + 1) * size]
     inverse, frob_norm = newton_schulz(gram)
     factor = shrink_ref[0] * jnp.sqrt(all_rows * side_len / frob_norm)
     select = (iota((own, size), 0) == iota((own, size), 1)).astype(F32)
@@ -339,18 +358,20 @@
     weights = dot_nn(weights, repeat)
     keep = iota((spread, wide), 0) % POLAR_ROWS == iota((spread, wide), 1) // size
     weights = jnp.where(keep, weights, 0.0).astype(BF16)
+
     out_copies = []
-    for chunk in range(chunks):
-        for copy in pixel_copies[chunk]:
-            copy.wait()
-        moved_copies[chunk].wait()
-        for step in range(sizes[chunk] // POLAR_ROWS):
-            data = stacked([pixels[chunk].at[group] for group in range(groups)], step * POLAR_ROWS, POLAR_ROWS)
+    for place, (chunk, row) in enumerate(blocks):
+        if place >= last_blocks:
+            for copy in pixel_copies[place]:
+                copy.wait()
+        moved_copies[place].wait()
+        for first in range(row, row + EDGE_ROWS, POLAR_ROWS):
+            data = stacked([pixels[chunk].at[group] for group in range(groups)], first, POLAR_ROWS)
             polar = dot_nn(weights, data).reshape(own, POLAR_ROWS, side_len)
-            first = starts[chunk] + step * POLAR_ROWS
-            moved[:, first : first + POLAR_ROWS] -= polar
-        part = pl.ds(starts[chunk], sizes[chunk])
-        copy = pltpu.make_async_copy(moved.at[:, part], out_hbm.at[:, part], out_sems.at[chunk])
+            into = starts[chunk] + first
+            moved[:, into : into + POLAR_ROWS] -= polar
+        part = pl.ds(starts[chunk] + row, EDGE_ROWS)
+        copy = pltpu.make_async_copy(moved.at[:, part], out_hbm.at[:, part], out_sems.at[place])
         copy.start()
         out_copies.append(copy)
     for copy in out_copies:
@@ -362,6 +383,7 @@
     groups = len(gathered[0])
     chans, _, side_len = moved[0].shape
     shape = (chans, sum(sizes), side_len)
+    blocks = sum(sizes) // EDGE_ROWS
     flat = [piece for pieces in gathered for piece in pieces]
     return pl.pallas_call(
         functools.partial(polar_body, starts, sizes, groups),
@@ -370,12 +392,12 @@
         out_shape=jax.ShapeDtypeStruct(shape, F32),
         scratch_shapes=[
             pltpu.VMEM(shape, F32),
-            pltpu.SemaphoreType.DMA((chunks * groups,)),
-            pltpu.SemaphoreType.DMA((chunks,)),
-            pltpu.SemaphoreType.DMA((chunks,)),
+            pltpu.SemaphoreType.DMA((blocks, groups)),
+            pltpu.SemaphoreType.DMA((blocks,)),
+            pltpu.SemaphoreType.DMA((blocks,)),
         ]
         + [pltpu.VMEM((groups,) + pieces[0].shape, BF16) for pieces in gathered],
-        compiler_params=kernel_params(40),
+        compiler_params=kernel_params(60),
         cost_estimate=COST,
         name="polar_step",
     )(shrinkage, gram, *moved, *flat)
@@ -427,6 +449,7 @@
     moved = {}
     gathered = {}
     pixels = {}
+    done = set()
     state = dict(last=strip, gram=jnp.zeros((GRAM_ROWS * size, GRAM_ROWS * size), F32), bases=None)
 
     def first(chunk):
@@ -434,7 +457,9 @@
         if chunk == 1:
             sent = gate(sent, edges)
         if chunk == 2:
-            gather(0, gram_after=True)
+            gather(0)
+            gram(0)
+            done.add(0)
             sent = gate(sent, state["gram"])
         halves[chunk] = lax.all_to_all(sent, "strip", split_axis=0, concat_axis=0, tiled=True)
 
@@ -450,14 +475,15 @@
         )
         state["last"] = pixels[chunk]
 
-    def gather(chunk, gram_after):
+    def gather(chunk):
         pieces = gather_channels(pixels[chunk], state["last"])
         if chans % 16:
             pieces = [jnp.concatenate(pieces, axis=1)]
         gathered[chunk] = pieces
-        if gram_after:
-            state["gram"] = gram_step(pieces, state["gram"], state["last"])
-            state["last"] = state["gram"]
+
+    def gram(chunk):
+        state["gram"] = gram_step(gathered[chunk], state["gram"], state["last"])
+        state["last"] = state["gram"]
 
     first(0)
     if chunks > 1:
@@ -467,9 +493,14 @@
         second(chunk)
         if chunk + 2 < chunks:
             first(chunk + 2)
-        if chunk >= 1 and chunk - 1 not in gathered:
-            gather(chunk - 1, gram_after=True)
-    gather(chunks - 1, gram_after=True)
+        if chunk == 1:
+            gather(1)
+        if chunk >= 1 and chunk - 1 not in done:
+            if chunk - 1 not in gathered:
+                gather(chunk - 1)
+            gram(chunk - 1)
+    if chunks - 1 not in gathered:
+        gather(chunks - 1)
     order = range(chunks)
     return polar_step(
         shrinkage, state["gram"], [moved[k] for k in order], [gathered[k] for k in order], starts, sizes

time: 290 us -> 278 us (0.959); the launches traced: 284 us -> 275 us
  local copies, waits for them, and re-layouts: 19.3 us -> 11 us
  Pallas kernels: 97.7 us -> 104 us
  waiting for transfers between devices: 126 us -> 120 us
    all_to_all x4, waiting for transfers between devices: 91.2 us -> 48.5 us  [first(): lax.all_to_all(sent, 'strip', split_axis=0, concat_axis=0, tiled=True)]
    ppermute x1, waiting for transfers between devices: 13.3 us -> 37.5 us  [neighbour_rows(): lax.ppermute(tail.astype(BF16), 'strip', [(i, i + 1) for i in range(ends)])]
    ppermute x12, waiting for transfers between devices: 19.4 us -> 32.7 us  [swap(): return lax.ppermute(value, axis, [(i, i ^ bits) for i in range(count)])]
    unnamed x60 -> x20, local copies, waits for them, and re-layouts: 17.5 us -> 7.77 us
    pallas_call x1, Pallas kernels: 9.7 us -> 13.4 us  [polar_step(): pl.pallas_call(functools.partial(polar_body, starts, sizes, groups), in_s...]
    pallas_call x4 -> x3, Pallas kernels: 13.3 us -> 16.1 us  [gram_step(): pl.pallas_call(functools.partial(gram_body, len(pieces)), grid=(rows // b...]
  transfers between devices with their start and end apart: 18 -> 18, of which waited for: 11 -> 11; matrix products, arithmetic and copies ran while one was open for 1% -> 2% of each run, Pallas kernels for 28% -> 30%
where the time goes in v8:
time: 278 us; the launch traced here: 275 us
  waiting for transfers between devices  120 us (43%)
  Pallas kernels  104 us (37%)
  starting transfers between devices  38.1 us (14%)
  local copies, waits for them, and re-layouts  11 us (4%)
    all_to_all x4, waiting for transfers between devices, first(): lax.all_to_all(sent, 'strip', split_axis=0, concat_axis=0, tiled=True)  48.5 us
    ppermute x1, waiting for transfers between devices, neighbour_rows(): lax.ppermute(tail.astype(BF16), 'strip', [(i, i + 1) for i in range(ends)])  37.5 us
    pallas_call x4, Pallas kernels, first_transform(): pl.pallas_call(first_body, grid=(chans // block,), in_specs=[pl.BlockSpec...  33.7 us
    ppermute x12, waiting for transfers between devices, swap(): return lax.ppermute(value, axis, [(i, i ^ bits) for i in range(count)])  32.7 us
    pallas_call x4, Pallas kernels, second_transform(): pl.pallas_call(second_body, grid=(side_len // block,), in_specs=[SMEM, pl...  29.2 us
    all_to_all x4, starting transfers between devices, first(): lax.all_to_all(sent, 'strip', split_axis=0, concat_axis=0, tiled=True)  25.5 us
    pallas_call x3, Pallas kernels, gram_step(): pl.pallas_call(functools.partial(gram_body, len(pieces)), grid=(rows // b...  16.1 us
    pallas_call x1, Pallas kernels, polar_step(): pl.pallas_call(functools.partial(polar_body, starts, sizes, groups), in_s...  13.4 us
  transfers between devices with their start and end apart: 18, of which 11 were waited for; matrix products, arithmetic and copies ran while one was open for 2% of the time, Pallas kernels for 30%

profile of v8, /device:TPU:12, one launch (start us, length us, event | category | flops | bytes accessed | tf_op | source)
XLA Modules:
  0.0 275.2 jit_solution(2751693595238147848)
XLA Ops:
  0.0 8.4 %first_transform.4 = (bf16[8,2,16,32,128]{4,3,2,1,0:T(8,128)(2,1)}, f32[8,128]{1,0:T(8,128)}) custom-call(bf16[512,1024]{1,0:T(8,128)(2,1)} %constant.20.clone.table_ref, bf16[2,16,128,1024]{3,2,1,0:T(8,128)(2,1)} %grid_ref.7, s32[1]{0:T(128)} %bitcast.after_ref.strip_ref), custom_call_target="tpu_custom_call" | custom-call | bytes 65536 | tf_op jit(solution)/shard_map/first_transform/pallas_call | solution.py:111
  8.4 6.2 %all-to-all-start = ((bf16[8,2,16,32,128]{4,3,2,1,0:T(8,128)(2,1)}), bf16[8,2,16,32,128]{4,3,2,1,0:T(8,128)(2,1)S(1)}, u32[]{:S(2)}, u32[]{:S(2)}) async-start(bf16[8,2,16,32,128]{4,3,2,1,0:T(8,128)(2,1)} %get-tuple-element.27), calls=%async_computation | async-start | bytes 4194304 | tf_op jit(solution)/shard_map/all_to_all | solution.py:464
  14.7 2.5 fusion
  17.2 3.4 %collective-permute-start = (bf16[16,12,1024]{2,1,0:T(8,128)(2,1)}, bf16[16,12,1024]{2,1,0:T(8,128)(2,1)S(1)}, u32[]{:S(2)}, u32[]{:S(2)}) collective-permute-start(bf16[16,12,1024]{2,1,0:T(8,128)(2,1)} %get-tuple-element.28), channel_id=1, source_target_pairs={{0,4},{4,8},{8,12},{12,16},{16,20},{20,24},{24,28},{1,5},{5,9},{9,... | collective-permute-start | bytes 1179656 | tf_op jit(solution)/shard_map/ppermute | solution.py:409
  20.6 2.5 collective-permute-start.1
  23.1 10.3 %first_transform.5 = (bf16[8,2,16,48,128]{4,3,2,1,0:T(8,128)(2,1)}, f32[8,128]{1,0:T(8,128)}) custom-call(bf16[768,1024]{1,0:T(8,128)(2,1)} %constant.21.clone.table_ref, bf16[2,16,128,1024]{3,2,1,0:T(8,128)(2,1)} %grid_ref.7, f32[8,128]{1,0:T(8,128)} %get-tuple-element.30.after_ref), custom_call_target="tpu_custom_call" | custom-call | bytes 65536 | tf_op jit(solution)/shard_map/first_transform/pallas_call | solution.py:111
  33.4 37.5 %collective-permute-done = bf16[16,12,1024]{2,1,0:T(8,128)(2,1)S(1)} collective-permute-done((bf16[16,12,1024]{2,1,0:T(8,128)(2,1)}, bf16[16,12,1024]{2,1,0:T(8,128)(2,1)S(1)}, u32[]{:S(2)}, u32[]{:S(2)}) %collective-permute-start) | collective-permute-done | bytes 393248 | tf_op jit(solution)/shard_map/ppermute | solution.py:409
  70.9 1.8 collective-permute-done.1
  72.7 1.1 pad_maximum_fusion.edge_ref.after_ref
  73.8 1.3 copy-done.4
  75.2 4.2 %all-to-all-start.2 = ((bf16[8,2,16,48,128]{4,3,2,1,0:T(8,128)(2,1)}), bf16[8,2,16,48,128]{4,3,2,1,0:T(8,128)(2,1)S(1)}, u32[]{:S(2)}, u32[]{:S(2)}) async-start(bf16[8,2,16,48,128]{4,3,2,1,0:T(8,128)(2,1)} %gate.8), calls=%async_computation.2 | async-start | bytes 6291456 | tf_op jit(solution)/shard_map/all_to_all | solution.py:464
  79.4 11.2 %base_step.1 = (f32[16,32,1024]{2,1,0:T(8,128)}, f32[16,48,1024]{2,1,0:T(8,128)}, f32[16,32,1024]{2,1,0:T(8,128)}, f32[16,16,1024]{2,1,0:T(8,128)}) custom-call(s32[1]{0:T(128)} %bitcast.after_ref.strip_ref, f32[16]{0:T(128)} %step_ref.9, f32[3,4]{1,0:T(4,128)} %highpass_ref.1, f32[16,128,1024]{2,1,0:T(8,128)} %model_ref.1, ...), custom_call_target="tpu_custom_call" | custom-call | bytes 65536 | tf_op jit(solution)/shard_map/base_step/pallas_call | solution.py:192
  90.6 7.3 %second_transform.4 = (f32[16,32,1024]{2,1,0:T(8,128)}, bf16[32,16,1024]{2,1,0:T(8,128)(2,1)}) custom-call(f32[16]{0:T(128)} %step_ref.9, bf16[8,2,16,32,128]{4,3,2,1,0:T(8,128)(2,1)} %copy-done.4, bf16[1024,1024]{1,0:T(8,128)(2,1)} %constant.22.clone.cosine_ref, bf16[1024,1024]{1,0:T(8,128)(2,1)} %constant.23.clone.sine_ref, ...), custom_call_target="tpu_custom_call" | custom-call | bytes 65536 | tf_op jit(solution)/shard_map/second_transform/pallas_call | solution.py:235
  97.9 1.5 collective-permute-start.2
  99.4 8.4 %first_transform.6 = (bf16[8,2,16,32,128]{4,3,2,1,0:T(8,128)(2,1)}, f32[8,128]{1,0:T(8,128)}) custom-call(bf16[512,1024]{1,0:T(8,128)(2,1)} %constant.24.clone.table_ref, bf16[2,16,128,1024]{3,2,1,0:T(8,128)(2,1)} %grid_ref.7, bf16[32,16,1024]{2,1,0:T(8,128)(2,1)} %get-tuple-element.33.after_ref.refs_0_.refs_4_), custom_call_target="tpu_custom_call" | custom-call | bytes 65536 | tf_op jit(solution)/shard_map/first_transform/pallas_call | solution.py:111
  107.8 14.9 %collective-permute-done.2.value_ref = bf16[32,16,1024]{2,1,0:T(8,128)(2,1)} collective-permute-done((bf16[32,16,1024]{2,1,0:T(8,128)(2,1)}, bf16[32,16,1024]{2,1,0:T(8,128)(2,1)}, u32[]{:S(2)}, u32[]{:S(2)}) %collective-permute-start.2) | collective-permute-done | bytes 1048608 | tf_op jit(solution)/shard_map/ppermute | solution.py:416
  122.7 0.0 collective-permute-start.4
  122.7 0.0 collective-permute-done.3.refs_2_.refs_6_
  122.7 3.0 %collective-permute-done.4.refs_3_.refs_7_ = bf16[32,16,1024]{2,1,0:T(8,128)(2,1)} collective-permute-done((bf16[32,16,1024]{2,1,0:T(8,128)(2,1)}, bf16[32,16,1024]{2,1,0:T(8,128)(2,1)}, u32[]{:S(2)}, u32[]{:S(2)}) %collective-permute-start.4) | collective-permute-done | bytes 1048608 | tf_op jit(solution)/shard_map/ppermute | solution.py:416
  125.7 0.7 broadcast_in_dim.3.before_ref
  126.4 4.8 %gram_step.3.after_ref.before_ref = f32[256,256]{1,0:T(8,128)} custom-call(f32[256,256]{1,0:T(8,128)} %broadcast_in_dim.3.before_ref, f32[8,128]{1,0:T(8,128)} %get-tuple-element.34.after_ref, bf16[32,16,1024]{2,1,0:T(8,128)(2,1)} %get-tuple-element.33.after_ref.refs_0_.refs_4_, bf16[32,16,1024]{2,1,0:T(8,128)(2,1)} %gate.6.refs_1_.refs_5_, ...), custom_call_target="tpu_custom_call" | custom-call | bytes 65536 | tf_op jit(solution)/shard_map/gram_step/pallas_call | solution.py:282
  131.2 15.8 %all-to-all-done.2.half_ref = bf16[8,2,16,48,128]{4,3,2,1,0:T(8,128)(2,1)S(1)} async-done(((bf16[8,2,16,48,128]{4,3,2,1,0:T(8,128)(2,1)}), bf16[8,2,16,48,128]{4,3,2,1,0:T(8,128)(2,1)S(1)}, u32[]{:S(2)}, u32[]{:S(2)}) %all-to-all-start.2) | async-done | bytes 3145760 | tf_op jit(solution)/shard_map/all_to_all | solution.py:464
  147.0 1.7 copy-done.2
  148.7 7.5 %all-to-all-start.1 = ((bf16[8,2,16,32,128]{4,3,2,1,0:T(8,128)(2,1)}), bf16[8,2,16,32,128]{4,3,2,1,0:T(8,128)(2,1)}, u32[]{:S(2)}, u32[]{:S(2)}) async-start(bf16[8,2,16,32,128]{4,3,2,1,0:T(8,128)(2,1)} %gate.7), calls=%async_computation.1 | async-start | bytes 4194304 | tf_op jit(solution)/shard_map/all_to_all | solution.py:464
  156.2 9.0 %second_transform.5 = (f32[16,48,1024]{2,1,0:T(8,128)}, bf16[48,16,1024]{2,1,0:T(8,128)(2,1)}) custom-call(f32[16]{0:T(128)} %step_ref.9, bf16[8,2,16,48,128]{4,3,2,1,0:T(8,128)(2,1)} %copy-done.2, bf16[1024,1024]{1,0:T(8,128)(2,1)} %constant.22.clone.cosine_ref, bf16[1024,1024]{1,0:T(8,128)(2,1)} %constant.23.clone.sine_ref, ...), custom_call_target="tpu_custom_call" | custom-call | bytes 65536 | tf_op jit(solution)/shard_map/second_transform/pallas_call | solution.py:235
  165.2 1.5 collective-permute-start.5
  166.7 6.5 %first_transform.7 = (bf16[8,2,16,16,128]{4,3,2,1,0:T(8,128)(2,1)}, f32[8,128]{1,0:T(8,128)}) custom-call(bf16[256,1024]{1,0:T(8,128)(2,1)} %constant.25.clone.table_ref, bf16[2,16,128,1024]{3,2,1,0:T(8,128)(2,1)} %grid_ref.7, bf16[48,16,1024]{2,1,0:T(8,128)(2,1)} %get-tuple-element.39.after_ref.refs_0_.refs_8_), custom_call_target="tpu_custom_call" | custom-call | bytes 65536 | tf_op jit(solution)/shard_map/first_transform/pallas_call | solution.py:111
  173.2 27.6 %all-to-all-done.1.half_ref = bf16[8,2,16,32,128]{4,3,2,1,0:T(8,128)(2,1)} async-done(((bf16[8,2,16,32,128]{4,3,2,1,0:T(8,128)(2,1)}), bf16[8,2,16,32,128]{4,3,2,1,0:T(8,128)(2,1)}, u32[]{:S(2)}, u32[]{:S(2)}) %all-to-all-start.1) | async-done | bytes 2097184 | tf_op jit(solution)/shard_map/all_to_all | solution.py:464
  200.7 7.5 %all-to-all-start.3 = ((bf16[8,2,16,16,128]{4,3,2,1,0:T(8,128)(2,1)}), bf16[8,2,16,16,128]{4,3,2,1,0:T(8,128)(2,1)}, u32[]{:S(2)}, u32[]{:S(2)}) async-start(bf16[8,2,16,16,128]{4,3,2,1,0:T(8,128)(2,1)} %get-tuple-element.42), calls=%async_computation.3 | async-start | bytes 2097152 | tf_op jit(solution)/shard_map/all_to_all | solution.py:464
  208.3 1.2 copy-done.1
  209.5 0.5 collective-permute-start.7
  210.0 7.3 %second_transform.6 = (f32[16,32,1024]{2,1,0:T(8,128)}, bf16[32,16,1024]{2,1,0:T(8,128)(2,1)}) custom-call(f32[16]{0:T(128)} %step_ref.9, bf16[8,2,16,32,128]{4,3,2,1,0:T(8,128)(2,1)} %all-to-all-done.1.half_ref, bf16[1024,1024]{1,0:T(8,128)(2,1)} %constant.22.clone.cosine_ref, bf16[1024,1024]{1,0:T(8,128)(2,1)} %constant.23.clone.sine_ref, ...), custom_call_target="tpu_custom_call" | custom-call | bytes 65536 | tf_op jit(solution)/shard_map/second_transform/pallas_call | solution.py:235
  217.2 1.5 collective-permute-start.8
  218.7 6.5 %gram_step.4.after_ref.before_ref = f32[256,256]{1,0:T(8,128)} custom-call(f32[256,256]{1,0:T(8,128)} %gram_step.3.after_ref.before_ref, bf16[32,16,1024]{2,1,0:T(8,128)(2,1)} %get-tuple-element.41.after_ref.refs_0_.refs_12_, bf16[48,16,1024]{2,1,0:T(8,128)(2,1)} %get-tuple-element.39.after_ref.refs_0_.refs_8_, bf16[48,16,1024]{2,1,0:T(8,128)(2,1)} %gate.9.refs_1_.refs_9_, ...), custom_call_target="tpu_custom_call" | custom-call | bytes 65536 | tf_op jit(solution)/shard_map/gram_step/pallas_call | solution.py:282
  225.3 5.1 %all-to-all-done.3.half_ref = bf16[8,2,16,16,128]{4,3,2,1,0:T(8,128)(2,1)} async-done(((bf16[8,2,16,16,128]{4,3,2,1,0:T(8,128)(2,1)}), bf16[8,2,16,16,128]{4,3,2,1,0:T(8,128)(2,1)}, u32[]{:S(2)}, u32[]{:S(2)}) %all-to-all-start.3) | async-done | bytes 1048608 | tf_op jit(solution)/shard_map/all_to_all | solution.py:464
  230.4 5.7 %second_transform.7 = (f32[16,16,1024]{2,1,0:T(8,128)}, bf16[16,16,1024]{2,1,0:T(8,128)(2,1)}) custom-call(f32[16]{0:T(128)} %step_ref.9, bf16[8,2,16,16,128]{4,3,2,1,0:T(8,128)(2,1)} %all-to-all-done.3.half_ref, bf16[1024,1024]{1,0:T(8,128)(2,1)} %constant.22.clone.cosine_ref, bf16[1024,1024]{1,0:T(8,128)(2,1)} %constant.23.clone.sine_ref, ...), custom_call_target="tpu_custom_call" | custom-call | bytes 65536 | tf_op jit(solution)/shard_map/second_transform/pallas_call | solution.py:235
  236.1 6.5 %collective-permute-done.8.value_ref = bf16[32,16,1024]{2,1,0:T(8,128)(2,1)S(1)} collective-permute-done((bf16[32,16,1024]{2,1,0:T(8,128)(2,1)}, bf16[32,16,1024]{2,1,0:T(8,128)(2,1)S(1)}, u32[]{:S(2)}, u32[]{:S(2)}) %collective-permute-start.8) | collective-permute-done | bytes 1048608 | tf_op jit(solution)/shard_map/ppermute | solution.py:416
  242.5 1.0 copy-done.3
  243.5 1.5 collective-permute-start.11
  245.0 0.2 collective-permute-start.12
  245.2 1.1 collective-permute-done.10.refs_3_.refs_15_
  246.4 1.0 copy-done.6
  247.4 4.8 %gram_step.5.after_ref.gram_ref = f32[256,256]{1,0:T(8,128)} custom-call(f32[256,256]{1,0:T(8,128)} %gram_step.4.after_ref.before_ref, bf16[16,16,1024]{2,1,0:T(8,128)(2,1)} %get-tuple-element.44.after_ref.refs_16_, bf16[32,16,1024]{2,1,0:T(8,128)(2,1)} %get-tuple-element.41.after_ref.refs_0_.refs_12_, bf16[32,16,1024]{2,1,0:T(8,128)(2,1)} %gate.10.refs_1_.refs_13_, ...), custom_call_target="tpu_custom_call" | custom-call | bytes 65536 | tf_op jit(solution)/shard_map/gram_step/pallas_call | solution.py:282
  252.1 5.7 %collective-permute-done.11.value_ref = bf16[16,16,1024]{2,1,0:T(8,128)(2,1)S(1)} collective-permute-done((bf16[16,16,1024]{2,1,0:T(8,128)(2,1)S(1)}, bf16[16,16,1024]{2,1,0:T(8,128)(2,1)S(1)}, u32[]{:S(2)}, u32[]{:S(2)}) %collective-permute-start.11) | collective-permute-done | bytes 524320 | tf_op jit(solution)/shard_map/ppermute | solution.py:416
  257.9 0.8 copy-done.7
  259.3 1.4 collective-permute-done.13.refs_19_
  260.8 0.9 copy-done.9
  261.6 13.4 %polar_step.1 = f32[16,128,1024]{2,1,0:T(8,128)} custom-call(f32[1]{0:T(128)S(6)} %copy.24.shrink_ref, f32[256,256]{1,0:T(8,128)} %gram_step.5.after_ref.gram_ref, f32[16,32,1024]{2,1,0:T(8,128)} %get-tuple-element.45.refs_0_, f32[16,48,1024]{2,1,0:T(8,128)} %get-tuple-element.46.refs_1_, f32[16,32,1024]{2,1,0:T(8,128)} %get-tuple-element.47.refs_2_, ...), custom_call_target="tpu_custom_call" | custom-call | bytes 65536 | tf_op jit(solution)/shard_map/polar_step/pallas_call | solution.py:388
  (30 shorter events, 0.1 us)
Async XLA Ops:
  8.4 65.4 %all-to-all-start = ((bf16[8,2,16,32,128]{4,3,2,1,0:T(8,128)(2,1)}), bf16[8,2,16,32,128]{4,3,2,1,0:T(8,128)(2,1)S(1)}, u32[]{:S(2)}, u32[]{:S(2)}) async-start(bf16[8,2,16,32,128]{4,3,2,1,0:T(8,128)(2,1)} %get-tuple-element.27), calls=%async_computation | async-start | bytes 4194304 | tf_op jit(solution)/shard_map/all_to_all | solution.py:464
  17.2 53.7 %collective-permute-start = (bf16[16,12,1024]{2,1,0:T(8,128)(2,1)}, bf16[16,12,1024]{2,1,0:T(8,128)(2,1)S(1)}, u32[]{:S(2)}, u32[]{:S(2)}) collective-permute-start(bf16[16,12,1024]{2,1,0:T(8,128)(2,1)} %get-tuple-element.28), channel_id=1, source_target_pairs={{0,4},{4,8},{8,12},{12,16},{16,20},{20,24},{24,28},{1,5},{5,9},{9,... | collective-permute-start | bytes 1179656 | tf_op jit(solution)/shard_map/ppermute | solution.py:409
  20.6 52.1 %collective-permute-start.1 = (bf16[16,12,1024]{2,1,0:T(8,128)(2,1)S(1)}, bf16[16,12,1024]{2,1,0:T(8,128)(2,1)S(1)}, u32[]{:S(2)}, u32[]{:S(2)}) collective-permute-start(bf16[16,12,1024]{2,1,0:T(8,128)(2,1)S(1)} %get-tuple-element.29), channel_id=1, source_target_pairs={{4,0},{8,4},{12,8},{16,12},{20,16},{24,20},{28,24},{5,1},{9,5},{13... | collective-permute-start | bytes 1179656 | tf_op jit(solution)/shard_map/ppermute | solution.py:410
  73.8 1.3 copy-start.4
  75.2 71.9 %all-to-all-start.2 = ((bf16[8,2,16,48,128]{4,3,2,1,0:T(8,128)(2,1)}), bf16[8,2,16,48,128]{4,3,2,1,0:T(8,128)(2,1)S(1)}, u32[]{:S(2)}, u32[]{:S(2)}) async-start(bf16[8,2,16,48,128]{4,3,2,1,0:T(8,128)(2,1)} %gate.8), calls=%async_computation.2 | async-start | bytes 6291456 | tf_op jit(solution)/shard_map/all_to_all | solution.py:464
  97.9 24.8 %collective-permute-start.2 = (bf16[32,16,1024]{2,1,0:T(8,128)(2,1)}, bf16[32,16,1024]{2,1,0:T(8,128)(2,1)}, u32[]{:S(2)}, u32[]{:S(2)}) collective-permute-start(bf16[32,16,1024]{2,1,0:T(8,128)(2,1)} %get-tuple-element.33.after_ref.refs_0_.refs_4_), channel_id=1, source_target_pairs={{0,2},{1,3},{2,0},{3,1},{4,6},{5,7},{6,4},{7,5},{8,10},{9,11},{10,... | collective-permute-start | bytes 3145736 | tf_op jit(solution)/shard_map/ppermute | solution.py:416
  99.4 23.3 %collective-permute-start.3 = (bf16[32,16,1024]{2,1,0:T(8,128)(2,1)}, bf16[32,16,1024]{2,1,0:T(8,128)(2,1)}, u32[]{:S(2)}, u32[]{:S(2)}) collective-permute-start(bf16[32,16,1024]{2,1,0:T(8,128)(2,1)} %get-tuple-element.33.after_ref.refs_0_.refs_4_), channel_id=1, source_target_pairs={{0,1},{1,0},{2,3},{3,2},{4,5},{5,4},{6,7},{7,6},{8,9},{9,8},{10,11... | collective-permute-start | bytes 3145736 | tf_op jit(solution)/shard_map/ppermute | solution.py:416
  122.7 3.0 %collective-permute-start.4 = (bf16[32,16,1024]{2,1,0:T(8,128)(2,1)}, bf16[32,16,1024]{2,1,0:T(8,128)(2,1)}, u32[]{:S(2)}, u32[]{:S(2)}) collective-permute-start(bf16[32,16,1024]{2,1,0:T(8,128)(2,1)} %gate.6.refs_1_.refs_5_), channel_id=1, source_target_pairs={{0,1},{1,0},{2,3},{3,2},{4,5},{5,4},{6,7},{7,6},{8,9},{9,8},{10,11... | collective-permute-start | bytes 3145736 | tf_op jit(solution)/shard_map/ppermute | solution.py:416
  147.0 1.7 copy-start.2
  148.7 52.1 %all-to-all-start.1 = ((bf16[8,2,16,32,128]{4,3,2,1,0:T(8,128)(2,1)}), bf16[8,2,16,32,128]{4,3,2,1,0:T(8,128)(2,1)}, u32[]{:S(2)}, u32[]{:S(2)}) async-start(bf16[8,2,16,32,128]{4,3,2,1,0:T(8,128)(2,1)} %gate.7), calls=%async_computation.1 | async-start | bytes 4194304 | tf_op jit(solution)/shard_map/all_to_all | solution.py:464
  165.2 43.1 %collective-permute-start.5 = (bf16[48,16,1024]{2,1,0:T(8,128)(2,1)}, bf16[48,16,1024]{2,1,0:T(8,128)(2,1)S(1)}, u32[]{:S(2)}, u32[]{:S(2)}) collective-permute-start(bf16[48,16,1024]{2,1,0:T(8,128)(2,1)} %get-tuple-element.39.after_ref.refs_0_.refs_8_), channel_id=1, source_target_pairs={{0,2},{1,3},{2,0},{3,1},{4,6},{5,7},{6,4},{7,5},{8,10},{9,11},{10,... | collective-permute-start | bytes 4718600 | tf_op jit(solution)/shard_map/ppermute | solution.py:416
  173.1 35.1 %copy-start = (bf16[48,16,1024]{2,1,0:T(8,128)(2,1)S(1)}, bf16[48,16,1024]{2,1,0:T(8,128)(2,1)}, u32[]{:S(2)}) copy-start(bf16[48,16,1024]{2,1,0:T(8,128)(2,1)} %get-tuple-element.39.after_ref.refs_0_.refs_8_) | copy-start | bytes 4718596
  200.7 29.6 %all-to-all-start.3 = ((bf16[8,2,16,16,128]{4,3,2,1,0:T(8,128)(2,1)}), bf16[8,2,16,16,128]{4,3,2,1,0:T(8,128)(2,1)}, u32[]{:S(2)}, u32[]{:S(2)}) async-start(bf16[8,2,16,16,128]{4,3,2,1,0:T(8,128)(2,1)} %get-tuple-element.42), calls=%async_computation.3 | async-start | bytes 2097152 | tf_op jit(solution)/shard_map/all_to_all | solution.py:464
  208.3 10.5 %collective-permute-start.6 = (bf16[48,16,1024]{2,1,0:T(8,128)(2,1)S(1)}, bf16[48,16,1024]{2,1,0:T(8,128)(2,1)}, u32[]{:S(2)}, u32[]{:S(2)}) collective-permute-start(bf16[48,16,1024]{2,1,0:T(8,128)(2,1)S(1)} %copy-done), channel_id=1, source_target_pairs={{0,1},{1,0},{2,3},{3,2},{4,5},{5,4},{6,7},{7,6},{8,9},{9,8},{10,11... | collective-permute-start | bytes 4718600 | tf_op jit(solution)/shard_map/ppermute | solution.py:416
  208.3 1.2 copy-start.1
  209.5 9.3 %collective-permute-start.7 = (bf16[48,16,1024]{2,1,0:T(8,128)(2,1)}, bf16[48,16,1024]{2,1,0:T(8,128)(2,1)}, u32[]{:S(2)}, u32[]{:S(2)}) collective-permute-start(bf16[48,16,1024]{2,1,0:T(8,128)(2,1)} %gate.9.refs_1_.refs_9_), channel_id=1, source_target_pairs={{0,1},{1,0},{2,3},{3,2},{4,5},{5,4},{6,7},{7,6},{8,9},{9,8},{10,11... | collective-permute-start | bytes 4718600 | tf_op jit(solution)/shard_map/ppermute | solution.py:416
  217.2 25.3 %collective-permute-start.8 = (bf16[32,16,1024]{2,1,0:T(8,128)(2,1)}, bf16[32,16,1024]{2,1,0:T(8,128)(2,1)S(1)}, u32[]{:S(2)}, u32[]{:S(2)}) collective-permute-start(bf16[32,16,1024]{2,1,0:T(8,128)(2,1)} %get-tuple-element.41.after_ref.refs_0_.refs_12_), channel_id=1, source_target_pairs={{0,2},{1,3},{2,0},{3,1},{4,6},{5,7},{6,4},{7,5},{8,10},{9,11},{10,... | collective-permute-start | bytes 3145736 | tf_op jit(solution)/shard_map/ppermute | solution.py:416
  218.7 26.5 %collective-permute-start.9 = (bf16[32,16,1024]{2,1,0:T(8,128)(2,1)}, bf16[32,16,1024]{2,1,0:T(8,128)(2,1)}, u32[]{:S(2)}, u32[]{:S(2)}) collective-permute-start(bf16[32,16,1024]{2,1,0:T(8,128)(2,1)} %get-tuple-element.41.after_ref.refs_0_.refs_12_), channel_id=1, source_target_pairs={{0,1},{1,0},{2,3},{3,2},{4,5},{5,4},{6,7},{7,6},{8,9},{9,8},{10,11... | collective-permute-start | bytes 3145736 | tf_op jit(solution)/shard_map/ppermute | solution.py:416
  236.1 7.4 %copy-start.5 = (bf16[16,16,1024]{2,1,0:T(8,128)(2,1)S(1)}, bf16[16,16,1024]{2,1,0:T(8,128)(2,1)}, u32[]{:S(2)}) copy-start(bf16[16,16,1024]{2,1,0:T(8,128)(2,1)} %get-tuple-element.44.after_ref.refs_16_) | copy-start | bytes 1572868
  242.5 1.0 copy-start.3
  243.5 2.9 %collective-permute-start.10 = (bf16[32,16,1024]{2,1,0:T(8,128)(2,1)}, bf16[32,16,1024]{2,1,0:T(8,128)(2,1)S(1)}, u32[]{:S(2)}, u32[]{:S(2)}) collective-permute-start(bf16[32,16,1024]{2,1,0:T(8,128)(2,1)} %gate.10.refs_1_.refs_13_), channel_id=1, source_target_pairs={{0,1},{1,0},{2,3},{3,2},{4,5},{5,4},{6,7},{7,6},{8,9},{9,8},{10,11... | collective-permute-start | bytes 3145736 | tf_op jit(solution)/shard_map/ppermute | solution.py:416
  243.5 14.3 %collective-permute-start.11 = (bf16[16,16,1024]{2,1,0:T(8,128)(2,1)S(1)}, bf16[16,16,1024]{2,1,0:T(8,128)(2,1)S(1)}, u32[]{:S(2)}, u32[]{:S(2)}) collective-permute-start(bf16[16,16,1024]{2,1,0:T(8,128)(2,1)S(1)} %copy-done.5), channel_id=1, source_target_pairs={{0,2},{1,3},{2,0},{3,1},{4,6},{5,7},{6,4},{7,5},{8,10},{9,11},{10,... | collective-permute-start | bytes 1572872 | tf_op jit(solution)/shard_map/ppermute | solution.py:416
  245.0 14.3 %collective-permute-start.12 = (bf16[16,16,1024]{2,1,0:T(8,128)(2,1)S(1)}, bf16[16,16,1024]{2,1,0:T(8,128)(2,1)S(1)}, u32[]{:S(2)}, u32[]{:S(2)}) collective-permute-start(bf16[16,16,1024]{2,1,0:T(8,128)(2,1)S(1)} %copy-done.5), channel_id=1, source_target_pairs={{0,1},{1,0},{2,3},{3,2},{4,5},{5,4},{6,7},{7,6},{8,9},{9,8},{10,11... | collective-permute-start | bytes 1572872 | tf_op jit(solution)/shard_map/ppermute | solution.py:416
  246.4 1.0 copy-start.6
  257.8 0.8 copy-start.7
  258.6 2.1 collective-permute-start.13
  259.3 1.5 copy-start.8
  260.8 0.9 copy-start.9

commit v9 on v8

--- a/solution.py
+++ b/solution.py
@@ -57,8 +57,7 @@
 
 
 def chunk_rows(own_rows):
-    quarter = own_rows // 4
-    sizes = [quarter, own_rows - 2 * quarter - EDGE_ROWS, quarter, EDGE_ROWS]
+    sizes = [EDGE_ROWS, own_rows // 2, own_rows // 2 - 2 * EDGE_ROWS, EDGE_ROWS]
     sizes = [size for size in sizes if size > 0]
     return [sum(sizes[:place]) for place in range(len(sizes))], sizes
 
@@ -125,6 +124,61 @@
         cost_estimate=COST,
         name="first_transform",
     )(table, grid, after)
+
+
+def pieces_body(strips, strip_ref, table_ref, grid_ref, after_ref, *refs):
+    out_refs = refs[:strips]
+    refs[strips][...] = jnp.zeros(refs[strips].shape, F32)
+    _, chans, rows, width = out_refs[0].shape
+    side_len = table_ref.shape[-1]
+    cosine = jnp.concatenate([table_ref[0, strip_ref[0] ^ k] for k in range(strips)], axis=0)
+    sine_table = jnp.concatenate([table_ref[1, strip_ref[0] ^ k] for k in range(strips)], axis=0)
+    total = dot_nt(jnp.concatenate([cosine, sine_table], axis=0), grid_ref[0].reshape(chans * width, side_len))
+    total = total + dot_nt(
+        jnp.concatenate([-sine_table, cosine], axis=0), grid_ref[1].reshape(chans * width, side_len)
+    )
+    total = total.astype(BF16)
+    for part in range(2):
+        for k in range(strips):
+            first = (part * strips + k) * rows
+            for chan in range(chans):
+                out_refs[k][part, chan] = total[first : first + rows, chan * width : (chan + 1) * width]
+
+
+def first_pieces(strip, table, grid, strips, after):
+    _, chans, width, side_len = grid.shape
+    rows = table.shape[0] // (2 * strips)
+    table = table.reshape(2, strips, rows, side_len)
+    if width % 128 or rows % 16:
+        order = strip[0] ^ jnp.arange(strips, dtype=jnp.int32)
+        cosine, sine_table = (jnp.take(table[part], order, axis=0) for part in range(2))
+
+        def product(table, part):
+            return jnp.einsum("kmv,cuv->kcmu", table, part, preferred_element_type=F32)
+
+        real = product(cosine, grid[0]) - product(sine_table, grid[1])
+        imag = product(sine_table, grid[0]) + product(cosine, grid[1])
+        both = jnp.stack([real, imag], axis=1).astype(BF16)
+        return [both[k] for k in range(strips)], jnp.zeros((8, 128), F32)
+    block = 4 if chans % 4 == 0 else 1
+    results = pl.pallas_call(
+        functools.partial(pieces_body, strips),
+        grid=(chans // block,),
+        in_specs=[
+            SMEM,
+            pl.BlockSpec(table.shape, lambda i: (0, 0, 0, 0)),
+            pl.BlockSpec((2, block, width, side_len), lambda i: (0, i, 0, 0)),
+            ANY,
+        ],
+        out_specs=[pl.BlockSpec((2, block, rows, width), lambda i: (0, i, 0, 0))] * strips
+        + [pl.BlockSpec((8, 128), lambda i: (0, 0))],
+        out_shape=[jax.ShapeDtypeStruct((2, chans, rows, width), BF16)] * strips
+        + [jax.ShapeDtypeStruct((8, 128), F32)],
+        compiler_params=kernel_params(60),
+        cost_estimate=COST,
+        name="first_pieces",
+    )(strip, table, grid, after)
+    return results[:strips], results[strips]
 
 
 def band_matrix(taps_of, levels, taps, own_rows, reach, first_row, image_rows):
@@ -255,6 +309,68 @@
         cost_estimate=COST,
         name="second_transform",
     )(step_size, half, cosine, sine_table, base, after)
+
+
+def second_pieces_body(strips, strip_ref, step_ref, cosine_ref, sine_ref, base_ref, after_ref, *refs):
+    halves = refs[:strips]
+    moved_ref, pixels_ref = refs[strips:]
+    _, chans, rows, width = halves[0].shape
+    real = jnp.concatenate([half[0].reshape(chans * rows, width) for half in halves], axis=1)
+    imag = jnp.concatenate([half[1].reshape(chans * rows, width) for half in halves], axis=1)
+
+    def ordered(table_ref):
+        parts = [table_ref[pl.ds(pl.multiple_of((strip_ref[0] ^ k) * width, width), width), :] for k in range(strips)]
+        return jnp.concatenate(parts, axis=0)
+
+    dirty = dot_nn(real, ordered(cosine_ref)) - dot_nn(imag, ordered(sine_ref))
+    pieces = []
+    for chan in range(chans):
+        moved = base_ref[chan] + step_ref[chan] * dirty[chan * rows : (chan + 1) * rows]
+        moved_ref[chan] = moved
+        pieces.append(moved)
+    pixels_ref[...] = jnp.swapaxes(jnp.stack(pieces), 0, 1).astype(BF16)
+
+
+def second_pieces(strip, step_size, halves, cosine, sine_table, base, after):
+    strips = len(halves)
+    _, chans, rows, width = halves[0].shape
+    side_len = cosine.shape[0]
+    if width % 128 or rows % 16 or chans % 16:
+        order = strip[0] ^ jnp.arange(strips, dtype=jnp.int32)
+        both = jnp.stack(halves)
+
+        def product(part, table):
+            parts = jnp.take(jnp.asarray(table).reshape(strips, width, side_len), order, axis=0)
+            return jnp.einsum("kcmu,kul->cml", part, parts, preferred_element_type=F32)
+
+        moved = base + step_size[:, None, None] * (product(both[:, 0], cosine) - product(both[:, 1], sine_table))
+        return moved, moved.astype(BF16).transpose(1, 0, 2)
+    block = min(256, side_len)
+    half_spec = pl.BlockSpec(halves[0].shape, lambda i: (0, 0, 0, 0))
+    return pl.pallas_call(
+        functools.partial(second_pieces_body, strips),
+        grid=(side_len // block,),
+        in_specs=[
+            SMEM,
+            SMEM,
+            pl.BlockSpec((side_len, block), lambda i: (0, i)),
+            pl.BlockSpec((side_len, block), lambda i: (0, i)),
+            pl.BlockSpec((chans, rows, block), lambda i: (0, 0, i)),
+            ANY,
+        ]
+        + [half_spec] * strips,
+        out_specs=[
+            pl.BlockSpec((chans, rows, block), lambda i: (0, 0, i)),
+            pl.BlockSpec((rows, chans, block), lambda i: (0, 0, i)),
+        ],
+        out_shape=[
+            jax.ShapeDtypeStruct(base.shape, F32),
+            jax.ShapeDtypeStruct((rows, chans, side_len), BF16),
+        ],
+        compiler_params=kernel_params(60),
+        cost_estimate=COST,
+        name="second_pieces",
+    )(strip, step_size, cosine, sine_table, base, after, *halves)
 
 
 def stacked(group_refs, first, count):
@@ -416,14 +532,18 @@
     return lax.ppermute(value, axis, [(i, i ^ bits) for i in range(count)])
 
 
-def gather_channels(pixels, after=None):
+def gather_channels(pixels, after):
     devices = lax.axis_size("chan")
-    kept = [pixels] + [swap(pixels, "chan", bits) for bits in range(2, devices, 2)]
-    if after is not None:
-        kept = [pixels] + [gate(piece, after) for piece in kept[1:]]
+    kept = [pixels] + [gate(swap(pixels, "chan", bits), after) for bits in range(2, devices, 2)]
     if devices == 1:
         return kept
     return kept + [swap(piece, "chan", 1) for piece in kept]
+
+
+def exchange(pieces):
+    order = [k for k in (1, 2) if k < len(pieces)] + list(range(4, len(pieces))) + [3][: max(0, len(pieces) - 3)]
+    arrived = {k: swap(pieces[k], "strip", k) for k in order}
+    return [pieces[0]] + [arrived[k] for k in range(1, len(pieces))]
 
 
 def local(grid, model_image, step_size, highpass, shrinkage):
@@ -453,6 +573,10 @@
     state = dict(last=strip, gram=jnp.zeros((GRAM_ROWS * size, GRAM_ROWS * size), F32), bases=None)
 
     def first(chunk):
+        if chunk == 0:
+            sent, state["last"] = first_pieces(strip, tables[chunk], grid, strips, state["last"])
+            halves[chunk] = exchange(sent)
+            return
         sent, state["last"] = first_transform(tables[chunk], grid, strips, state["last"])
         if chunk == 1:
             sent = gate(sent, edges)
@@ -470,9 +594,11 @@
         state["last"] = state["bases"][0]
 
     def second(chunk):
-        moved[chunk], pixels[chunk] = second_transform(
-            step_size, halves[chunk], cosine, sine_table, state["bases"][chunk], state["last"]
-        )
+        inputs = (step_size, halves[chunk], cosine, sine_table, state["bases"][chunk], state["last"])
+        if chunk == 0:
+            moved[chunk], pixels[chunk] = second_pieces(strip, *inputs)
+        else:
+            moved[chunk], pixels[chunk] = second_transform(*inputs)
         state["last"] = pixels[chunk]
 
     def gather(chunk):

time: 278 us -> 316 us (1.14)
  waiting for transfers between devices: 120 us -> 156 us
    ppermute x12 -> x19, waiting for transfers between devices: 32.7 us -> 150 us  [swap(): return lax.ppermute(value, axis, [(i, i ^ bits) for i in range(count)])]
    all_to_all x4 -> x3, waiting for transfers between devices: 48.5 us -> 4.82 us  [first(): lax.all_to_all(sent, 'strip', split_axis=0, concat_axis=0, tiled=True)]
    ppermute x1, waiting for transfers between devices: 37.5 us -> 1.56 us  [neighbour_rows(): lax.ppermute(tail.astype(BF16), 'strip', [(i, i + 1) for i in range(ends)])]
    pallas_call x0 -> x2, Pallas kernels: none -> 12.4 us  [the longest x1 6.6 us: first_pieces(): pl.pallas_call(functools.partial(pieces_body, strips), grid=(chans // blo...]
    ppermute x12 -> x19, starting transfers between devices: 6.73 us -> 15.9 us  [swap(): return lax.ppermute(value, axis, [(i, i ^ bits) for i in range(count)])]
    all_to_all x4 -> x3, starting transfers between devices: 25.5 us -> 18.4 us  [first(): lax.all_to_all(sent, 'strip', split_axis=0, concat_axis=0, tiled=True)]
    pallas_call x4 -> x3, Pallas kernels: 33.7 us -> 27.7 us  [first_transform(): pl.pallas_call(first_body, grid=(chans // block,), in_specs=[pl.BlockSpec...]
    pallas_call x4 -> x3, Pallas kernels: 29.2 us -> 23.6 us  [second_transform(): pl.pallas_call(second_body, grid=(side_len // block,), in_specs=[SMEM, pl...]
  transfers between devices with their start and end apart: 18 -> 24, of which waited for: 11 -> 15; matrix products, arithmetic and copies ran while one was open for 2% -> 0% of each run, Pallas kernels for 30% -> 29%
where the time goes in v9:
time: 316 us; the launch traced here: 313 us
  waiting for transfers between devices  156 us (49%)
  Pallas kernels  104 us (33%)
  starting transfers between devices  40.2 us (13%)
  local copies, waits for them, and re-layouts  10.4 us (3%)
    ppermute x19, waiting for transfers between devices, swap(): return lax.ppermute(value, axis, [(i, i ^ bits) for i in range(count)])  150 us
    pallas_call x3, Pallas kernels, first_transform(): pl.pallas_call(first_body, grid=(chans // block,), in_specs=[pl.BlockSpec...  27.7 us
    pallas_call x3, Pallas kernels, second_transform(): pl.pallas_call(second_body, grid=(side_len // block,), in_specs=[SMEM, pl...  23.6 us
    all_to_all x3, starting transfers between devices, first(): lax.all_to_all(sent, 'strip', split_axis=0, concat_axis=0, tiled=True)  18.4 us
    pallas_call x3, Pallas kernels, gram_step(): pl.pallas_call(functools.partial(gram_body, len(pieces)), grid=(rows // b...  16.1 us
    ppermute x19, starting transfers between devices, swap(): return lax.ppermute(value, axis, [(i, i ^ bits) for i in range(count)])  15.9 us
    pallas_call x1, Pallas kernels, polar_step(): pl.pallas_call(functools.partial(polar_body, starts, sizes, groups), in_s...  13.4 us
    pallas_call x1, Pallas kernels, base_step(): pl.pallas_call(functools.partial(base_body, levels, taps, starts, strips)...  11.2 us
  transfers between devices with their start and end apart: 24, of which 15 were waited for; matrix products, arithmetic and copies ran while one was open for 0% of the time, Pallas kernels for 29%

profile of v9, /device:TPU:12, one launch (start us, length us, event | category | flops | bytes accessed | tf_op | source)
XLA Modules:
  0.0 313.3 jit_solution(8388988731009949813)
XLA Ops:
  0.0 1.7 fusion
  1.7 3.4 %collective-permute-start = (bf16[16,12,1024]{2,1,0:T(8,128)(2,1)S(1)}, bf16[16,12,1024]{2,1,0:T(8,128)(2,1)S(1)}, u32[]{:S(2)}, u32[]{:S(2)}) collective-permute-start(bf16[16,12,1024]{2,1,0:T(8,128)(2,1)S(1)} %get-tuple-element.34), channel_id=1, source_target_pairs={{0,4},{4,8},{8,12},{12,16},{16,20},{20,24},{24,28},{1,5},{5,9},{9,... | collective-permute-start | bytes 1179656 | tf_op jit(solution)/shard_map/ppermute | solution.py:525
  5.2 2.4 collective-permute-start.1
  7.6 6.6 %first_pieces.1 = (bf16[2,16,16,128]{3,2,1,0:T(8,128)(2,1)}, bf16[2,16,16,128]{3,2,1,0:T(8,128)(2,1)}, bf16[2,16,16,128]{3,2,1,0:T(8,128)(2,1)}, bf16[2,16,16,12...) custom-call(s32[1]{0:T(128)} %bitcast.strip_ref.after_ref, ...), custom_call_target="tpu_custom_call" | custom-call | bytes 65536 | tf_op jit(solution)/shard_map/first_pieces/pallas_call | solution.py:164
  14.2 12.8 %first_transform.3 = (bf16[8,2,16,64,128]{4,3,2,1,0:T(8,128)(2,1)}, f32[8,128]{1,0:T(8,128)}) custom-call(bf16[1024,1024]{1,0:T(8,128)(2,1)} %constant.21.clone.table_ref, bf16[2,16,128,1024]{3,2,1,0:T(8,128)(2,1)} %grid_ref.7, f32[8,128]{1,0:T(8,128)} %get-tuple-element.36.after_ref), custom_call_target="tpu_custom_call" | custom-call | bytes 65536 | tf_op jit(solution)/shard_map/first_transform/pallas_call | solution.py:110
  27.0 1.6 collective-permute-done
  28.5 1.1 pad_maximum_fusion.edge_ref.after_ref
  29.7 6.3 %all-to-all-start.1 = ((bf16[8,2,16,64,128]{4,3,2,1,0:T(8,128)(2,1)}), bf16[8,2,16,64,128]{4,3,2,1,0:T(8,128)(2,1)}, u32[]{:S(2)}, u32[]{:S(2)}) async-start(bf16[8,2,16,64,128]{4,3,2,1,0:T(8,128)(2,1)} %gate.8), calls=%async_computation.1 | async-start | bytes 8388608 | tf_op jit(solution)/shard_map/all_to_all | solution.py:588
  36.6 2.8 collective-permute-start.4
  39.5 2.4 collective-permute-start.5
  42.4 31.2 %collective-permute-done.2.refs_1_ = bf16[2,16,16,128]{3,2,1,0:T(8,128)(2,1)S(1)} collective-permute-done((bf16[2,16,16,128]{3,2,1,0:T(8,128)(2,1)S(1)}, bf16[2,16,16,128]{3,2,1,0:T(8,128)(2,1)S(1)}, u32[]{:S(2)}, u32[]{:S(2)}) %collective-permute-start.2) | collective-permute-done | bytes 131104 | tf_op jit(solution)/shard_map/ppermute | solution.py:532
  73.6 1.5 collective-permute-start.7
  75.1 34.1 %collective-permute-done.3.refs_2_ = bf16[2,16,16,128]{3,2,1,0:T(8,128)(2,1)S(1)} collective-permute-done((bf16[2,16,16,128]{3,2,1,0:T(8,128)(2,1)S(1)}, bf16[2,16,16,128]{3,2,1,0:T(8,128)(2,1)S(1)}, u32[]{:S(2)}, u32[]{:S(2)}) %collective-permute-start.3) | collective-permute-done | bytes 131104 | tf_op jit(solution)/shard_map/ppermute | solution.py:532
  109.2 1.8 collective-permute-start.8
  111.0 11.2 %base_step.1 = (f32[16,16,1024]{2,1,0:T(8,128)}, f32[16,64,1024]{2,1,0:T(8,128)}, f32[16,32,1024]{2,1,0:T(8,128)}, f32[16,16,1024]{2,1,0:T(8,128)}) custom-call(s32[1]{0:T(128)} %bitcast.strip_ref.after_ref, f32[16]{0:T(128)} %step_ref.9, f32[3,4]{1,0:T(4,128)} %highpass_ref.1, f32[16,128,1024]{2,1,0:T(8,128)} %model_ref.1, ...), custom_call_target="tpu_custom_call" | custom-call | bytes 65536 | tf_op jit(solution)/shard_map/base_step/pallas_call | solution.py:246
  122.3 18.3 %collective-permute-done.5.refs_4_ = bf16[2,16,16,128]{3,2,1,0:T(8,128)(2,1)S(1)} collective-permute-done((bf16[2,16,16,128]{3,2,1,0:T(8,128)(2,1)S(1)}, bf16[2,16,16,128]{3,2,1,0:T(8,128)(2,1)S(1)}, u32[]{:S(2)}, u32[]{:S(2)}) %collective-permute-start.5) | collective-permute-done | bytes 131104 | tf_op jit(solution)/shard_map/ppermute | solution.py:532
  140.6 2.8 collective-permute-done.6.refs_5_
  143.4 6.1 %collective-permute-done.7.refs_6_ = bf16[2,16,16,128]{3,2,1,0:T(8,128)(2,1)S(1)} collective-permute-done((bf16[2,16,16,128]{3,2,1,0:T(8,128)(2,1)S(1)}, bf16[2,16,16,128]{3,2,1,0:T(8,128)(2,1)S(1)}, u32[]{:S(2)}, u32[]{:S(2)}) %collective-permute-start.7) | collective-permute-done | bytes 131104 | tf_op jit(solution)/shard_map/ppermute | solution.py:532
  149.4 0.9 collective-permute-done.8.refs_7_
  151.0 5.8 %second_pieces.1 = (f32[16,16,1024]{2,1,0:T(8,128)}, bf16[16,16,1024]{2,1,0:T(8,128)(2,1)}) custom-call(s32[1]{0:T(128)} %bitcast.strip_ref.after_ref, f32[16]{0:T(128)} %step_ref.9, bf16[1024,1024]{1,0:T(8,128)(2,1)} %constant.22.clone.cosine_ref, bf16[1024,1024]{1,0:T(8,128)(2,1)} %constant.23.clone.sine_ref, ...), custom_call_target="tpu_custom_call" | custom-call | bytes 65536 | tf_op jit(solution)/shard_map/second_pieces/pallas_call | solution.py:350
  156.8 1.5 collective-permute-start.9
  158.3 8.5 %first_transform.4 = (bf16[8,2,16,32,128]{4,3,2,1,0:T(8,128)(2,1)}, f32[8,128]{1,0:T(8,128)}) custom-call(bf16[512,1024]{1,0:T(8,128)(2,1)} %constant.24.clone.table_ref, bf16[2,16,128,1024]{3,2,1,0:T(8,128)(2,1)} %grid_ref.7, bf16[16,16,1024]{2,1,0:T(8,128)(2,1)} %get-tuple-element.47.after_ref.refs_0_.refs_4_), custom_call_target="tpu_custom_call" | custom-call | bytes 65536 | tf_op jit(solution)/shard_map/first_transform/pallas_call | solution.py:110
  166.8 3.0 collective-permute-done.9.value_ref
  170.5 2.1 collective-permute-done.11.refs_3_.refs_7_
  173.5 3.1 gram_step.3.after_ref.before_ref
  176.6 6.1 %all-to-all-start = ((bf16[8,2,16,32,128]{4,3,2,1,0:T(8,128)(2,1)}), bf16[8,2,16,32,128]{4,3,2,1,0:T(8,128)(2,1)}, u32[]{:S(2)}, u32[]{:S(2)}) async-start(bf16[8,2,16,32,128]{4,3,2,1,0:T(8,128)(2,1)} %gate.7), calls=%async_computation | async-start | bytes 4194304 | tf_op jit(solution)/shard_map/all_to_all | solution.py:588
  182.7 10.7 %second_transform.3 = (f32[16,64,1024]{2,1,0:T(8,128)}, bf16[64,16,1024]{2,1,0:T(8,128)(2,1)}) custom-call(f32[16]{0:T(128)} %step_ref.9, bf16[8,2,16,64,128]{4,3,2,1,0:T(8,128)(2,1)} %all-to-all-done.1.half_ref, bf16[1024,1024]{1,0:T(8,128)(2,1)} %constant.22.clone.cosine_ref, bf16[1024,1024]{1,0:T(8,128)(2,1)} %constant.23.clone.sine_ref, ...), custom_call_target="tpu_custom_call" | custom-call | bytes 65536 | tf_op jit(solution)/shard_map/second_transform/pallas_call | solution.py:289
  193.4 1.5 collective-permute-start.12
  194.9 6.5 %first_transform.5 = (bf16[8,2,16,16,128]{4,3,2,1,0:T(8,128)(2,1)}, f32[8,128]{1,0:T(8,128)}) custom-call(bf16[256,1024]{1,0:T(8,128)(2,1)} %constant.25.clone.table_ref, bf16[2,16,128,1024]{3,2,1,0:T(8,128)(2,1)} %grid_ref.7, bf16[64,16,1024]{2,1,0:T(8,128)(2,1)} %get-tuple-element.53.after_ref.refs_0_.refs_8_), custom_call_target="tpu_custom_call" | custom-call | bytes 65536 | tf_op jit(solution)/shard_map/first_transform/pallas_call | solution.py:110
  201.4 39.3 %collective-permute-done.12.value_ref = bf16[64,16,1024]{2,1,0:T(8,128)(2,1)S(1)} collective-permute-done((bf16[64,16,1024]{2,1,0:T(8,128)(2,1)}, bf16[64,16,1024]{2,1,0:T(8,128)(2,1)S(1)}, u32[]{:S(2)}, u32[]{:S(2)}) %collective-permute-start.12) | collective-permute-done | bytes 2097184 | tf_op jit(solution)/shard_map/ppermute | solution.py:532
  240.7 1.4 copy-done
  242.1 6.0 %all-to-all-start.2 = ((bf16[8,2,16,16,128]{4,3,2,1,0:T(8,128)(2,1)}), bf16[8,2,16,16,128]{4,3,2,1,0:T(8,128)(2,1)}, u32[]{:S(2)}, u32[]{:S(2)}) async-start(bf16[8,2,16,16,128]{4,3,2,1,0:T(8,128)(2,1)} %get-tuple-element.56), calls=%async_computation.2 | async-start | bytes 2097152 | tf_op jit(solution)/shard_map/all_to_all | solution.py:588
  248.1 7.3 %second_transform.4 = (f32[16,32,1024]{2,1,0:T(8,128)}, bf16[32,16,1024]{2,1,0:T(8,128)(2,1)}) custom-call(f32[16]{0:T(128)} %step_ref.9, bf16[8,2,16,32,128]{4,3,2,1,0:T(8,128)(2,1)} %all-to-all-done.half_ref, bf16[1024,1024]{1,0:T(8,128)(2,1)} %constant.22.clone.cosine_ref, bf16[1024,1024]{1,0:T(8,128)(2,1)} %constant.23.clone.sine_ref, ...), custom_call_target="tpu_custom_call" | custom-call | bytes 65536 | tf_op jit(solution)/shard_map/second_transform/pallas_call | solution.py:289
  255.4 1.5 collective-permute-start.15
  256.9 1.3 copy-done.2
  258.2 8.3 %gram_step.4.after_ref.before_ref = f32[256,256]{1,0:T(8,128)} custom-call(f32[256,256]{1,0:T(8,128)} %gram_step.3.after_ref.before_ref, bf16[32,16,1024]{2,1,0:T(8,128)(2,1)} %get-tuple-element.55.after_ref.refs_0_.refs_12_, bf16[64,16,1024]{2,1,0:T(8,128)(2,1)} %get-tuple-element.53.after_ref.refs_0_.refs_8_, bf16[64,16,1024]{2,1,0:T(8,128)(2,1)} %gate.9.refs_1_.refs_9_, ...), custom_call_target="tpu_custom_call" | custom-call | bytes 65536 | tf_op jit(solution)/shard_map/gram_step/pallas_call | solution.py:398
  266.5 4.8 %all-to-all-done.2.half_ref = bf16[8,2,16,16,128]{4,3,2,1,0:T(8,128)(2,1)} async-done(((bf16[8,2,16,16,128]{4,3,2,1,0:T(8,128)(2,1)}), bf16[8,2,16,16,128]{4,3,2,1,0:T(8,128)(2,1)}, u32[]{:S(2)}, u32[]{:S(2)}) %all-to-all-start.2) | async-done | bytes 1048608 | tf_op jit(solution)/shard_map/all_to_all | solution.py:588
  271.3 5.7 %second_transform.5 = (f32[16,16,1024]{2,1,0:T(8,128)}, bf16[16,16,1024]{2,1,0:T(8,128)(2,1)}) custom-call(f32[16]{0:T(128)} %step_ref.9, bf16[8,2,16,16,128]{4,3,2,1,0:T(8,128)(2,1)} %all-to-all-done.2.half_ref, bf16[1024,1024]{1,0:T(8,128)(2,1)} %constant.22.clone.cosine_ref, bf16[1024,1024]{1,0:T(8,128)(2,1)} %constant.23.clone.sine_ref, ...), custom_call_target="tpu_custom_call" | custom-call | bytes 65536 | tf_op jit(solution)/shard_map/second_transform/pallas_call | solution.py:289
  277.0 3.6 %collective-permute-done.15.value_ref = bf16[32,16,1024]{2,1,0:T(8,128)(2,1)S(1)} collective-permute-done((bf16[32,16,1024]{2,1,0:T(8,128)(2,1)}, bf16[32,16,1024]{2,1,0:T(8,128)(2,1)S(1)}, u32[]{:S(2)}, u32[]{:S(2)}) %collective-permute-start.15) | collective-permute-done | bytes 1048608 | tf_op jit(solution)/shard_map/ppermute | solution.py:532
  280.6 1.0 copy-done.1
  281.7 1.5 collective-permute-start.18
  283.4 1.1 collective-permute-done.17.refs_3_.refs_15_
  284.5 1.0 copy-done.5
  285.5 4.8 %gram_step.5.after_ref.gram_ref = f32[256,256]{1,0:T(8,128)} custom-call(f32[256,256]{1,0:T(8,128)} %gram_step.4.after_ref.before_ref, bf16[16,16,1024]{2,1,0:T(8,128)(2,1)} %get-tuple-element.58.after_ref.refs_16_, bf16[32,16,1024]{2,1,0:T(8,128)(2,1)} %get-tuple-element.55.after_ref.refs_0_.refs_12_, bf16[32,16,1024]{2,1,0:T(8,128)(2,1)} %gate.10.refs_1_.refs_13_, ...), custom_call_target="tpu_custom_call" | custom-call | bytes 65536 | tf_op jit(solution)/shard_map/gram_step/pallas_call | solution.py:398
  290.3 5.7 %collective-permute-done.18.value_ref = bf16[16,16,1024]{2,1,0:T(8,128)(2,1)S(1)} collective-permute-done((bf16[16,16,1024]{2,1,0:T(8,128)(2,1)S(1)}, bf16[16,16,1024]{2,1,0:T(8,128)(2,1)S(1)}, u32[]{:S(2)}, u32[]{:S(2)}) %collective-permute-start.18) | collective-permute-done | bytes 524320 | tf_op jit(solution)/shard_map/ppermute | solution.py:532
  296.0 0.8 copy-done.8
  297.5 1.4 collective-permute-done.20.refs_19_
  299.7 13.4 %polar_step.1 = f32[16,128,1024]{2,1,0:T(8,128)} custom-call(f32[1]{0:T(128)S(6)} %copy.24.shrink_ref, f32[256,256]{1,0:T(8,128)} %gram_step.5.after_ref.gram_ref, f32[16,16,1024]{2,1,0:T(8,128)} %get-tuple-element.59.refs_0_, f32[16,64,1024]{2,1,0:T(8,128)} %get-tuple-element.60.refs_1_, f32[16,32,1024]{2,1,0:T(8,128)} %get-tuple-element.61.refs_2_, ...), custom_call_target="tpu_custom_call" | custom-call | bytes 65536 | tf_op jit(solution)/shard_map/polar_step/pallas_call | solution.py:504
  (72 shorter events, 4.6 us)
Async XLA Ops:
  1.7 26.8 %collective-permute-start = (bf16[16,12,1024]{2,1,0:T(8,128)(2,1)S(1)}, bf16[16,12,1024]{2,1,0:T(8,128)(2,1)S(1)}, u32[]{:S(2)}, u32[]{:S(2)}) collective-permute-start(bf16[16,12,1024]{2,1,0:T(8,128)(2,1)S(1)} %get-tuple-element.34), channel_id=1, source_target_pairs={{0,4},{4,8},{8,12},{12,16},{16,20},{20,24},{24,28},{1,5},{5,9},{9,... | collective-permute-start | bytes 1179656 | tf_op jit(solution)/shard_map/ppermute | solution.py:525
  5.2 23.4 %collective-permute-start.1 = (bf16[16,12,1024]{2,1,0:T(8,128)(2,1)S(1)}, bf16[16,12,1024]{2,1,0:T(8,128)(2,1)S(1)}, u32[]{:S(2)}, u32[]{:S(2)}) collective-permute-start(bf16[16,12,1024]{2,1,0:T(8,128)(2,1)S(1)} %get-tuple-element.35), channel_id=1, source_target_pairs={{4,0},{8,4},{12,8},{16,12},{20,16},{24,20},{28,24},{5,1},{9,5},{13... | collective-permute-start | bytes 1179656 | tf_op jit(solution)/shard_map/ppermute | solution.py:526
  29.7 6.3 %copy-start.24 = (bf16[2,16,16,128]{3,2,1,0:T(8,128)(2,1)S(1)}, bf16[2,16,16,128]{3,2,1,0:T(8,128)(2,1)}, u32[]{:S(2)}) copy-start(bf16[2,16,16,128]{3,2,1,0:T(8,128)(2,1)} %get-tuple-element.40) | copy-start | bytes 393220
  29.7 6.9 %copy-start.23 = (bf16[2,16,16,128]{3,2,1,0:T(8,128)(2,1)S(1)}, bf16[2,16,16,128]{3,2,1,0:T(8,128)(2,1)}, u32[]{:S(2)}) copy-start(bf16[2,16,16,128]{3,2,1,0:T(8,128)(2,1)} %get-tuple-element.41) | copy-start | bytes 393220
  29.7 7.0 %copy-start.22 = (bf16[2,16,16,128]{3,2,1,0:T(8,128)(2,1)S(1)}, bf16[2,16,16,128]{3,2,1,0:T(8,128)(2,1)}, u32[]{:S(2)}) copy-start(bf16[2,16,16,128]{3,2,1,0:T(8,128)(2,1)} %get-tuple-element.42) | copy-start | bytes 393220
  29.7 9.8 %copy-start.21 = (bf16[2,16,16,128]{3,2,1,0:T(8,128)(2,1)S(1)}, bf16[2,16,16,128]{3,2,1,0:T(8,128)(2,1)}, u32[]{:S(2)}) copy-start(bf16[2,16,16,128]{3,2,1,0:T(8,128)(2,1)} %get-tuple-element.43) | copy-start | bytes 393220
  29.7 12.2 %copy-start.20 = (bf16[2,16,16,128]{3,2,1,0:T(8,128)(2,1)S(1)}, bf16[2,16,16,128]{3,2,1,0:T(8,128)(2,1)}, u32[]{:S(2)}) copy-start(bf16[2,16,16,128]{3,2,1,0:T(8,128)(2,1)} %get-tuple-element.44) | copy-start | bytes 393220
  29.7 43.9 %copy-start.19 = (bf16[2,16,16,128]{3,2,1,0:T(8,128)(2,1)S(1)}, bf16[2,16,16,128]{3,2,1,0:T(8,128)(2,1)}, u32[]{:S(2)}) copy-start(bf16[2,16,16,128]{3,2,1,0:T(8,128)(2,1)} %get-tuple-element.45) | copy-start | bytes 393220
  29.7 79.5 %copy-start.18 = (bf16[2,16,16,128]{3,2,1,0:T(8,128)(2,1)S(1)}, bf16[2,16,16,128]{3,2,1,0:T(8,128)(2,1)}, u32[]{:S(2)}) copy-start(bf16[2,16,16,128]{3,2,1,0:T(8,128)(2,1)} %get-tuple-element.46) | copy-start | bytes 393220
  29.7 146.9 %all-to-all-start.1 = ((bf16[8,2,16,64,128]{4,3,2,1,0:T(8,128)(2,1)}), bf16[8,2,16,64,128]{4,3,2,1,0:T(8,128)(2,1)}, u32[]{:S(2)}, u32[]{:S(2)}) async-start(bf16[8,2,16,64,128]{4,3,2,1,0:T(8,128)(2,1)} %gate.8), calls=%async_computation.1 | async-start | bytes 8388608 | tf_op jit(solution)/shard_map/all_to_all | solution.py:588
  36.0 37.6 %collective-permute-start.2 = (bf16[2,16,16,128]{3,2,1,0:T(8,128)(2,1)S(1)}, bf16[2,16,16,128]{3,2,1,0:T(8,128)(2,1)S(1)}, u32[]{:S(2)}, u32[]{:S(2)}) collective-permute-start(bf16[2,16,16,128]{3,2,1,0:T(8,128)(2,1)S(1)} %copy-done.24), channel_id=1, source_target_pairs={{0,4},{4,0},{8,12},{12,8},{16,20},{20,16},{24,28},{28,24},{1,5},{5... | collective-permute-start | bytes 393224 | tf_op jit(solution)/shard_map/ppermute | solution.py:532
  36.6 72.6 %collective-permute-start.3 = (bf16[2,16,16,128]{3,2,1,0:T(8,128)(2,1)S(1)}, bf16[2,16,16,128]{3,2,1,0:T(8,128)(2,1)S(1)}, u32[]{:S(2)}, u32[]{:S(2)}) collective-permute-start(bf16[2,16,16,128]{3,2,1,0:T(8,128)(2,1)S(1)} %copy-done.23), channel_id=1, source_target_pairs={{0,8},{4,12},{8,0},{12,4},{16,24},{20,28},{24,16},{28,20},{1,9},{5... | collective-permute-start | bytes 393224 | tf_op jit(solution)/shard_map/ppermute | solution.py:532
  36.6 85.6 %collective-permute-start.4 = (bf16[2,16,16,128]{3,2,1,0:T(8,128)(2,1)S(1)}, bf16[2,16,16,128]{3,2,1,0:T(8,128)(2,1)S(1)}, u32[]{:S(2)}, u32[]{:S(2)}) collective-permute-start(bf16[2,16,16,128]{3,2,1,0:T(8,128)(2,1)S(1)} %copy-done.22), channel_id=1, source_target_pairs={{0,12},{4,8},{8,4},{12,0},{16,28},{20,24},{24,20},{28,16},{1,13},{... | collective-permute-start | bytes 393224 | tf_op jit(solution)/shard_map/ppermute | solution.py:532
  39.5 101.0 %collective-permute-start.5 = (bf16[2,16,16,128]{3,2,1,0:T(8,128)(2,1)S(1)}, bf16[2,16,16,128]{3,2,1,0:T(8,128)(2,1)S(1)}, u32[]{:S(2)}, u32[]{:S(2)}) collective-permute-start(bf16[2,16,16,128]{3,2,1,0:T(8,128)(2,1)S(1)} %copy-done.21), channel_id=1, source_target_pairs={{0,16},{4,20},{8,24},{12,28},{16,0},{20,4},{24,8},{28,12},{1,17},{... | collective-permute-start | bytes 393224 | tf_op jit(solution)/shard_map/ppermute | solution.py:532
  41.9 101.5 %collective-permute-start.6 = (bf16[2,16,16,128]{3,2,1,0:T(8,128)(2,1)S(1)}, bf16[2,16,16,128]{3,2,1,0:T(8,128)(2,1)S(1)}, u32[]{:S(2)}, u32[]{:S(2)}) collective-permute-start(bf16[2,16,16,128]{3,2,1,0:T(8,128)(2,1)S(1)} %copy-done.20), channel_id=1, source_target_pairs={{0,20},{4,16},{8,28},{12,24},{16,4},{20,0},{24,12},{28,8},{1,21},{... | collective-permute-start | bytes 393224 | tf_op jit(solution)/shard_map/ppermute | solution.py:532
  73.6 48.6 %copy-start.11 = (bf16[2,16,16,128]{3,2,1,0:T(8,128)(2,1)}, bf16[2,16,16,128]{3,2,1,0:T(8,128)(2,1)S(1)}, u32[]{:S(2)}) copy-start(bf16[2,16,16,128]{3,2,1,0:T(8,128)(2,1)S(1)} %collective-permute-done.2.refs_1_) | copy-start | bytes 393220
  73.6 75.8 %collective-permute-start.7 = (bf16[2,16,16,128]{3,2,1,0:T(8,128)(2,1)S(1)}, bf16[2,16,16,128]{3,2,1,0:T(8,128)(2,1)S(1)}, u32[]{:S(2)}, u32[]{:S(2)}) collective-permute-start(bf16[2,16,16,128]{3,2,1,0:T(8,128)(2,1)S(1)} %copy-done.19), channel_id=1, source_target_pairs={{0,24},{4,28},{8,16},{12,20},{16,8},{20,12},{24,0},{28,4},{1,25},{... | collective-permute-start | bytes 393224 | tf_op jit(solution)/shard_map/ppermute | solution.py:532
  109.2 13.1 %copy-start.12 = (bf16[2,16,16,128]{3,2,1,0:T(8,128)(2,1)}, bf16[2,16,16,128]{3,2,1,0:T(8,128)(2,1)S(1)}, u32[]{:S(2)}) copy-start(bf16[2,16,16,128]{3,2,1,0:T(8,128)(2,1)S(1)} %collective-permute-done.3.refs_2_) | copy-start | bytes 393220
  109.2 41.2 %collective-permute-start.8 = (bf16[2,16,16,128]{3,2,1,0:T(8,128)(2,1)S(1)}, bf16[2,16,16,128]{3,2,1,0:T(8,128)(2,1)S(1)}, u32[]{:S(2)}, u32[]{:S(2)}) collective-permute-start(bf16[2,16,16,128]{3,2,1,0:T(8,128)(2,1)S(1)} %copy-done.18), channel_id=1, source_target_pairs={{0,28},{4,24},{8,20},{12,16},{16,12},{20,8},{24,4},{28,0},{1,29},{... | collective-permute-start | bytes 393224 | tf_op jit(solution)/shard_map/ppermute | solution.py:532
  122.2 28.1 %copy-start.13 = (bf16[2,16,16,128]{3,2,1,0:T(8,128)(2,1)}, bf16[2,16,16,128]{3,2,1,0:T(8,128)(2,1)S(1)}, u32[]{:S(2)}) copy-start(bf16[2,16,16,128]{3,2,1,0:T(8,128)(2,1)S(1)} %collective-permute-done.4.refs_3_) | copy-start | bytes 393220
  140.5 9.8 %copy-start.14 = (bf16[2,16,16,128]{3,2,1,0:T(8,128)(2,1)}, bf16[2,16,16,128]{3,2,1,0:T(8,128)(2,1)S(1)}, u32[]{:S(2)}) copy-start(bf16[2,16,16,128]{3,2,1,0:T(8,128)(2,1)S(1)} %collective-permute-done.5.refs_4_) | copy-start | bytes 393220
  143.4 7.0 %copy-start.15 = (bf16[2,16,16,128]{3,2,1,0:T(8,128)(2,1)}, bf16[2,16,16,128]{3,2,1,0:T(8,128)(2,1)S(1)}, u32[]{:S(2)}) copy-start(bf16[2,16,16,128]{3,2,1,0:T(8,128)(2,1)S(1)} %collective-permute-done.6.refs_5_) | copy-start | bytes 393220
  149.4 1.0 copy-start.16
  156.8 12.9 %collective-permute-start.9 = (bf16[16,16,1024]{2,1,0:T(8,128)(2,1)}, bf16[16,16,1024]{2,1,0:T(8,128)(2,1)S(1)}, u32[]{:S(2)}, u32[]{:S(2)}) collective-permute-start(bf16[16,16,1024]{2,1,0:T(8,128)(2,1)} %get-tuple-element.47.after_ref.refs_0_.refs_4_), channel_id=1, source_target_pairs={{0,2},{1,3},{2,0},{3,1},{4,6},{5,7},{6,4},{7,5},{8,10},{9,11},{10,... | collective-permute-start | bytes 1572872 | tf_op jit(solution)/shard_map/ppermute | solution.py:532
  158.3 12.2 %collective-permute-start.10 = (bf16[16,16,1024]{2,1,0:T(8,128)(2,1)}, bf16[16,16,1024]{2,1,0:T(8,128)(2,1)S(1)}, u32[]{:S(2)}, u32[]{:S(2)}) collective-permute-start(bf16[16,16,1024]{2,1,0:T(8,128)(2,1)} %get-tuple-element.47.after_ref.refs_0_.refs_4_), channel_id=1, source_target_pairs={{0,1},{1,0},{2,3},{3,2},{4,5},{5,4},{6,7},{7,6},{8,9},{9,8},{10,11... | collective-permute-start | bytes 1572872 | tf_op jit(solution)/shard_map/ppermute | solution.py:532
  169.7 0.8 copy-start.4
  170.5 2.1 collective-permute-start.11
  170.5 2.9 copy-start.6
  172.7 0.9 copy-start.7
  176.6 65.5 %all-to-all-start = ((bf16[8,2,16,32,128]{4,3,2,1,0:T(8,128)(2,1)}), bf16[8,2,16,32,128]{4,3,2,1,0:T(8,128)(2,1)}, u32[]{:S(2)}, u32[]{:S(2)}) async-start(bf16[8,2,16,32,128]{4,3,2,1,0:T(8,128)(2,1)} %gate.7), calls=%async_computation | async-start | bytes 4194304 | tf_op jit(solution)/shard_map/all_to_all | solution.py:588
  193.4 47.3 %collective-permute-start.12 = (bf16[64,16,1024]{2,1,0:T(8,128)(2,1)}, bf16[64,16,1024]{2,1,0:T(8,128)(2,1)S(1)}, u32[]{:S(2)}, u32[]{:S(2)}) collective-permute-start(bf16[64,16,1024]{2,1,0:T(8,128)(2,1)} %get-tuple-element.53.after_ref.refs_0_.refs_8_), channel_id=1, source_target_pairs={{0,2},{1,3},{2,0},{3,1},{4,6},{5,7},{6,4},{7,5},{8,10},{9,11},{10,... | collective-permute-start | bytes 6291464 | tf_op jit(solution)/shard_map/ppermute | solution.py:532
  194.9 62.0 %collective-permute-start.13 = (bf16[64,16,1024]{2,1,0:T(8,128)(2,1)}, bf16[64,16,1024]{2,1,0:T(8,128)(2,1)}, u32[]{:S(2)}, u32[]{:S(2)}) collective-permute-start(bf16[64,16,1024]{2,1,0:T(8,128)(2,1)} %get-tuple-element.53.after_ref.refs_0_.refs_8_), channel_id=1, source_target_pairs={{0,1},{1,0},{2,3},{3,2},{4,5},{5,4},{6,7},{7,6},{8,9},{9,8},{10,11... | collective-permute-start | bytes 6291464 | tf_op jit(solution)/shard_map/ppermute | solution.py:532
  240.7 1.4 copy-start
  242.1 14.8 %collective-permute-start.14 = (bf16[64,16,1024]{2,1,0:T(8,128)(2,1)}, bf16[64,16,1024]{2,1,0:T(8,128)(2,1)S(1)}, u32[]{:S(2)}, u32[]{:S(2)}) collective-permute-start(bf16[64,16,1024]{2,1,0:T(8,128)(2,1)} %gate.9.refs_1_.refs_9_), channel_id=1, source_target_pairs={{0,1},{1,0},{2,3},{3,2},{4,5},{5,4},{6,7},{7,6},{8,9},{9,8},{10,11... | collective-permute-start | bytes 6291464 | tf_op jit(solution)/shard_map/ppermute | solution.py:532
  242.1 29.2 %all-to-all-start.2 = ((bf16[8,2,16,16,128]{4,3,2,1,0:T(8,128)(2,1)}), bf16[8,2,16,16,128]{4,3,2,1,0:T(8,128)(2,1)}, u32[]{:S(2)}, u32[]{:S(2)}) async-start(bf16[8,2,16,16,128]{4,3,2,1,0:T(8,128)(2,1)} %get-tuple-element.56), calls=%async_computation.2 | async-start | bytes 2097152 | tf_op jit(solution)/shard_map/all_to_all | solution.py:588
  255.4 25.2 %collective-permute-start.15 = (bf16[32,16,1024]{2,1,0:T(8,128)(2,1)}, bf16[32,16,1024]{2,1,0:T(8,128)(2,1)S(1)}, u32[]{:S(2)}, u32[]{:S(2)}) collective-permute-start(bf16[32,16,1024]{2,1,0:T(8,128)(2,1)} %get-tuple-element.55.after_ref.refs_0_.refs_12_), channel_id=1, source_target_pairs={{0,2},{1,3},{2,0},{3,1},{4,6},{5,7},{6,4},{7,5},{8,10},{9,11},{10,... | collective-permute-start | bytes 3145736 | tf_op jit(solution)/shard_map/ppermute | solution.py:532
  256.9 26.5 %collective-permute-start.16 = (bf16[32,16,1024]{2,1,0:T(8,128)(2,1)}, bf16[32,16,1024]{2,1,0:T(8,128)(2,1)}, u32[]{:S(2)}, u32[]{:S(2)}) collective-permute-start(bf16[32,16,1024]{2,1,0:T(8,128)(2,1)} %get-tuple-element.55.after_ref.refs_0_.refs_12_), channel_id=1, source_target_pairs={{0,1},{1,0},{2,3},{3,2},{4,5},{5,4},{6,7},{7,6},{8,9},{9,8},{10,11... | collective-permute-start | bytes 3145736 | tf_op jit(solution)/shard_map/ppermute | solution.py:532
  256.9 1.3 copy-start.2
  277.0 4.7 %copy-start.3 = (bf16[16,16,1024]{2,1,0:T(8,128)(2,1)S(1)}, bf16[16,16,1024]{2,1,0:T(8,128)(2,1)}, u32[]{:S(2)}) copy-start(bf16[16,16,1024]{2,1,0:T(8,128)(2,1)} %get-tuple-element.58.after_ref.refs_16_) | copy-start | bytes 1572868
  280.6 1.0 copy-start.1
  281.7 2.9 collective-permute-start.17
  281.7 14.3 %collective-permute-start.18 = (bf16[16,16,1024]{2,1,0:T(8,128)(2,1)S(1)}, bf16[16,16,1024]{2,1,0:T(8,128)(2,1)S(1)}, u32[]{:S(2)}, u32[]{:S(2)}) collective-permute-start(bf16[16,16,1024]{2,1,0:T(8,128)(2,1)S(1)} %copy-done.3), channel_id=1, source_target_pairs={{0,2},{1,3},{2,0},{3,1},{4,6},{5,7},{6,4},{7,5},{8,10},{9,11},{10,... | collective-permute-start | bytes 1572872 | tf_op jit(solution)/shard_map/ppermute | solution.py:532
  283.2 14.3 %collective-permute-start.19 = (bf16[16,16,1024]{2,1,0:T(8,128)(2,1)S(1)}, bf16[16,16,1024]{2,1,0:T(8,128)(2,1)S(1)}, u32[]{:S(2)}, u32[]{:S(2)}) collective-permute-start(bf16[16,16,1024]{2,1,0:T(8,128)(2,1)S(1)} %copy-done.3), channel_id=1, source_target_pairs={{0,1},{1,0},{2,3},{3,2},{4,5},{5,4},{6,7},{7,6},{8,9},{9,8},{10,11... | collective-permute-start | bytes 1572872 | tf_op jit(solution)/shard_map/ppermute | solution.py:532
  284.5 1.0 copy-start.5
  296.0 0.8 copy-start.8
  296.8 2.1 collective-permute-start.20
  297.5 1.5 copy-start.9
  298.9 0.8 copy-start.10
  (1 other events, 0.7 us)

commit v10 on v9

--- a/solution.py
+++ b/solution.py
@@ -57,8 +57,8 @@
 
 
 def chunk_rows(own_rows):
-    sizes = [EDGE_ROWS, own_rows // 2, own_rows // 2 - 2 * EDGE_ROWS, EDGE_ROWS]
-    sizes = [size for size in sizes if size > 0]
+    quarter = own_rows // 4
+    sizes = [own_rows - 2 * quarter - EDGE_ROWS, quarter, quarter, EDGE_ROWS]
     return [sum(sizes[:place]) for place in range(len(sizes))], sizes
 
 
@@ -541,7 +541,8 @@
 
 
 def exchange(pieces):
-    order = [k for k in (1, 2) if k < len(pieces)] + list(range(4, len(pieces))) + [3][: max(0, len(pieces) - 3)]
+    half = len(pieces) // 2
+    order = list(range(half, len(pieces))) + list(range(1, half))
     arrived = {k: swap(pieces[k], "strip", k) for k in order}
     return [pieces[0]] + [arrived[k] for k in range(1, len(pieces))]
 
@@ -569,23 +570,15 @@
     moved = {}
     gathered = {}
     pixels = {}
-    done = set()
     state = dict(last=strip, gram=jnp.zeros((GRAM_ROWS * size, GRAM_ROWS * size), F32), bases=None)
 
     def first(chunk):
-        if chunk == 0:
+        if chunk == 1:
             sent, state["last"] = first_pieces(strip, tables[chunk], grid, strips, state["last"])
             halves[chunk] = exchange(sent)
-            return
-        sent, state["last"] = first_transform(tables[chunk], grid, strips, state["last"])
-        if chunk == 1:
-            sent = gate(sent, edges)
-        if chunk == 2:
-            gather(0)
-            gram(0)
-            done.add(0)
-            sent = gate(sent, state["gram"])
-        halves[chunk] = lax.all_to_all(sent, "strip", split_axis=0, concat_axis=0, tiled=True)
+        else:
+            sent, state["last"] = first_transform(tables[chunk], grid, strips, state["last"])
+            halves[chunk] = lax.all_to_all(sent, "strip", split_axis=0, concat_axis=0, tiled=True)
 
     def base():
         state["bases"] = base_step(
@@ -595,7 +588,7 @@
 
     def second(chunk):
         inputs = (step_size, halves[chunk], cosine, sine_table, state["bases"][chunk], state["last"])
-        if chunk == 0:
+        if chunk == 1:
             moved[chunk], pixels[chunk] = second_pieces(strip, *inputs)
         else:
             moved[chunk], pixels[chunk] = second_transform(*inputs)
@@ -612,21 +605,22 @@
         state["last"] = state["gram"]
 
     first(0)
-    if chunks > 1:
-        first(1)
+    first(1)
+    state["last"] = gate(state["last"], edges)
+    first(2)
     base()
-    for chunk in range(chunks):
-        second(chunk)
-        if chunk + 2 < chunks:
-            first(chunk + 2)
-        if chunk == 1:
-            gather(1)
-        if chunk >= 1 and chunk - 1 not in done:
-            if chunk - 1 not in gathered:
-                gather(chunk - 1)
-            gram(chunk - 1)
-    if chunks - 1 not in gathered:
-        gather(chunks - 1)
+    second(1)
+    second(0)
+    gather(1)
+    first(3)
+    gather(0)
+    gram(1)
+    second(2)
+    gram(0)
+    second(3)
+    gather(2)
+    gram(2)
+    gather(3)
     order = range(chunks)
     return polar_step(
         shrinkage, state["gram"], [moved[k] for k in order], [gathered[k] for k in order], starts, sizes

time: 316 us -> 347 us (1.098)
  waiting for transfers between devices: 156 us -> 189 us
    ppermute x1, waiting for transfers between devices: 1.56 us -> 61.6 us  [neighbour_rows(): lax.ppermute(tail.astype(BF16), 'strip', [(i, i + 1) for i in range(ends)])]
    ppermute x19, waiting for transfers between devices: 150 us -> 126 us  [swap(): return lax.ppermute(value, axis, [(i, i ^ bits) for i in range(count)])]
    all_to_all x3, waiting for transfers between devices: 4.82 us -> 0.01 us  [first(): lax.all_to_all(sent, 'strip', split_axis=0, concat_axis=0, tiled=True)]
    unnamed x50 -> x36, local copies, waits for them, and re-layouts: 7.91 us -> 8.23 us
  transfers between devices with their start and end apart: 24 -> 24, of which waited for: 15 -> 14; matrix products, arithmetic and copies ran while one was open for 0% -> 2% of each run, Pallas kernels for 29% -> 23%
where the time goes in v10:
time: 347 us; the launch traced here: 345 us
  waiting for transfers between devices  189 us (54%)
  Pallas kernels  104 us (30%)
  starting transfers between devices  37.4 us (11%)
  local copies, waits for them, and re-layouts  11.7 us (3%)
    ppermute x19, waiting for transfers between devices, swap(): return lax.ppermute(value, axis, [(i, i ^ bits) for i in range(count)])  126 us
    ppermute x1, waiting for transfers between devices, neighbour_rows(): lax.ppermute(tail.astype(BF16), 'strip', [(i, i + 1) for i in range(ends)])  61.6 us
    pallas_call x3, Pallas kernels, first_transform(): pl.pallas_call(first_body, grid=(chans // block,), in_specs=[pl.BlockSpec...  25.3 us
    pallas_call x3, Pallas kernels, second_transform(): pl.pallas_call(second_body, grid=(side_len // block,), in_specs=[SMEM, pl...  21.9 us
    ppermute x19, starting transfers between devices, swap(): return lax.ppermute(value, axis, [(i, i ^ bits) for i in range(count)])  16.5 us
    pallas_call x3, Pallas kernels, gram_step(): pl.pallas_call(functools.partial(gram_body, len(pieces)), grid=(rows // b...  16.1 us
    all_to_all x3, starting transfers between devices, first(): lax.all_to_all(sent, 'strip', split_axis=0, concat_axis=0, tiled=True)  15 us
    pallas_call x1, Pallas kernels, polar_step(): pl.pallas_call(functools.partial(polar_body, starts, sizes, groups), in_s...  13.4 us
  transfers between devices with their start and end apart: 24, of which 14 were waited for; matrix products, arithmetic and copies ran while one was open for 2% of the time, Pallas kernels for 23%

profile of v10, /device:TPU:12, one launch (start us, length us, event | category | flops | bytes accessed | tf_op | source)
XLA Modules:
  0.0 345.3 jit_solution(6005703000288948048)
XLA Ops:
  0.0 10.3 %first_transform.3 = (bf16[8,2,16,48,128]{4,3,2,1,0:T(8,128)(2,1)}, f32[8,128]{1,0:T(8,128)}) custom-call(bf16[768,1024]{1,0:T(8,128)(2,1)} %constant.20.clone.table_ref, bf16[2,16,128,1024]{3,2,1,0:T(8,128)(2,1)} %grid_ref.7, s32[1]{0:T(128)} %bitcast.after_ref.strip_ref), custom_call_target="tpu_custom_call" | custom-call | bytes 65536 | tf_op jit(solution)/shard_map/first_transform/pallas_call | solution.py:110
  10.3 6.2 %all-to-all-start = ((bf16[8,2,16,48,128]{4,3,2,1,0:T(8,128)(2,1)}), bf16[8,2,16,48,128]{4,3,2,1,0:T(8,128)(2,1)S(1)}, u32[]{:S(2)}, u32[]{:S(2)}) async-start(bf16[8,2,16,48,128]{4,3,2,1,0:T(8,128)(2,1)} %get-tuple-element.34), calls=%async_computation | async-start | bytes 6291456 | tf_op jit(solution)/shard_map/all_to_all | solution.py:581
  16.5 2.7 fusion
  19.3 3.4 collective-permute-start
  22.6 2.5 collective-permute-start.1
  25.1 8.5 %first_pieces.1 = (bf16[2,16,32,128]{3,2,1,0:T(8,128)(2,1)}, bf16[2,16,32,128]{3,2,1,0:T(8,128)(2,1)}, bf16[2,16,32,128]{3,2,1,0:T(8,128)(2,1)}, bf16[2,16,32,12...) custom-call(s32[1]{0:T(128)} %bitcast.after_ref.strip_ref, ...), custom_call_target="tpu_custom_call" | custom-call | bytes 65536 | tf_op jit(solution)/shard_map/first_pieces/pallas_call | solution.py:164
  33.7 61.6 %collective-permute-done = bf16[16,12,1024]{2,1,0:T(8,128)(2,1)S(1)} collective-permute-done((bf16[16,12,1024]{2,1,0:T(8,128)(2,1)}, bf16[16,12,1024]{2,1,0:T(8,128)(2,1)S(1)}, u32[]{:S(2)}, u32[]{:S(2)}) %collective-permute-start) | collective-permute-done | bytes 393248 | tf_op jit(solution)/shard_map/ppermute | solution.py:525
  95.3 1.9 collective-permute-done.1
  97.1 2.2 pad_maximum_fusion.after_ref.edge_ref
  99.3 8.5 %first_transform.4 = (bf16[8,2,16,32,128]{4,3,2,1,0:T(8,128)(2,1)}, f32[8,128]{1,0:T(8,128)}) custom-call(bf16[512,1024]{1,0:T(8,128)(2,1)} %constant.22.clone.table_ref, bf16[2,16,128,1024]{3,2,1,0:T(8,128)(2,1)} %grid_ref.7, f32[8,128]{1,0:T(8,128)} %gate.5.after_ref), custom_call_target="tpu_custom_call" | custom-call | bytes 65536 | tf_op jit(solution)/shard_map/first_transform/pallas_call | solution.py:110
  107.8 1.6 copy-done.2
  109.4 4.3 %all-to-all-start.1 = ((bf16[8,2,16,32,128]{4,3,2,1,0:T(8,128)(2,1)}), bf16[8,2,16,32,128]{4,3,2,1,0:T(8,128)(2,1)}, u32[]{:S(2)}, u32[]{:S(2)}) async-start(bf16[8,2,16,32,128]{4,3,2,1,0:T(8,128)(2,1)} %get-tuple-element.53), calls=%async_computation.1 | async-start | bytes 4194304 | tf_op jit(solution)/shard_map/all_to_all | solution.py:581
  114.2 3.1 collective-permute-start.4
  117.3 2.2 collective-permute-start.5
  120.0 17.1 %collective-permute-done.2.refs_1_ = bf16[2,16,32,128]{3,2,1,0:T(8,128)(2,1)S(1)} collective-permute-done((bf16[2,16,32,128]{3,2,1,0:T(8,128)(2,1)}, bf16[2,16,32,128]{3,2,1,0:T(8,128)(2,1)S(1)}, u32[]{:S(2)}, u32[]{:S(2)}) %collective-permute-start.2) | collective-permute-done | bytes 262176 | tf_op jit(solution)/shard_map/ppermute | solution.py:532
  137.1 2.4 collective-permute-start.7
  139.5 16.4 %collective-permute-done.3.refs_2_ = bf16[2,16,32,128]{3,2,1,0:T(8,128)(2,1)S(1)} collective-permute-done((bf16[2,16,32,128]{3,2,1,0:T(8,128)(2,1)}, bf16[2,16,32,128]{3,2,1,0:T(8,128)(2,1)S(1)}, u32[]{:S(2)}, u32[]{:S(2)}) %collective-permute-start.3) | collective-permute-done | bytes 262176 | tf_op jit(solution)/shard_map/ppermute | solution.py:532
  155.9 1.9 collective-permute-start.8
  157.8 11.2 %base_step.1 = (f32[16,48,1024]{2,1,0:T(8,128)}, f32[16,32,1024]{2,1,0:T(8,128)}, f32[16,32,1024]{2,1,0:T(8,128)}, f32[16,16,1024]{2,1,0:T(8,128)}) custom-call(s32[1]{0:T(128)} %bitcast.after_ref.strip_ref, f32[16]{0:T(128)} %step_ref.9, f32[3,4]{1,0:T(4,128)} %highpass_ref.1, f32[16,128,1024]{2,1,0:T(8,128)} %model_ref.1, ...), custom_call_target="tpu_custom_call" | custom-call | bytes 65536 | tf_op jit(solution)/shard_map/base_step/pallas_call | solution.py:246
  169.0 17.9 %collective-permute-done.5.refs_4_ = bf16[2,16,32,128]{3,2,1,0:T(8,128)(2,1)S(1)} collective-permute-done((bf16[2,16,32,128]{3,2,1,0:T(8,128)(2,1)}, bf16[2,16,32,128]{3,2,1,0:T(8,128)(2,1)S(1)}, u32[]{:S(2)}, u32[]{:S(2)}) %collective-permute-start.5) | collective-permute-done | bytes 262176 | tf_op jit(solution)/shard_map/ppermute | solution.py:532
  187.0 5.6 %collective-permute-done.6.refs_5_ = bf16[2,16,32,128]{3,2,1,0:T(8,128)(2,1)S(1)} collective-permute-done((bf16[2,16,32,128]{3,2,1,0:T(8,128)(2,1)}, bf16[2,16,32,128]{3,2,1,0:T(8,128)(2,1)S(1)}, u32[]{:S(2)}, u32[]{:S(2)}) %collective-permute-start.6) | collective-permute-done | bytes 262176 | tf_op jit(solution)/shard_map/ppermute | solution.py:532
  192.6 8.3 %collective-permute-done.7.refs_6_ = bf16[2,16,32,128]{3,2,1,0:T(8,128)(2,1)S(1)} collective-permute-done((bf16[2,16,32,128]{3,2,1,0:T(8,128)(2,1)}, bf16[2,16,32,128]{3,2,1,0:T(8,128)(2,1)S(1)}, u32[]{:S(2)}, u32[]{:S(2)}) %collective-permute-start.7) | collective-permute-done | bytes 262176 | tf_op jit(solution)/shard_map/ppermute | solution.py:532
  200.9 5.5 %collective-permute-done.8.refs_7_ = bf16[2,16,32,128]{3,2,1,0:T(8,128)(2,1)S(1)} collective-permute-done((bf16[2,16,32,128]{3,2,1,0:T(8,128)(2,1)S(1)}, bf16[2,16,32,128]{3,2,1,0:T(8,128)(2,1)S(1)}, u32[]{:S(2)}, u32[]{:S(2)}) %collective-permute-start.8) | collective-permute-done | bytes 262176 | tf_op jit(solution)/shard_map/ppermute | solution.py:532
  207.1 7.3 %second_pieces.1 = (f32[16,32,1024]{2,1,0:T(8,128)}, bf16[32,16,1024]{2,1,0:T(8,128)(2,1)}) custom-call(s32[1]{0:T(128)} %bitcast.after_ref.strip_ref, f32[16]{0:T(128)} %step_ref.9, bf16[1024,1024]{1,0:T(8,128)(2,1)} %constant.23.clone.cosine_ref, bf16[1024,1024]{1,0:T(8,128)(2,1)} %constant.24.clone.sine_ref, f32[16,32,1024]{2,1,0:T(8,128)} %get-tuple-element.41.base_ref, ...), custom_call_target="tpu_custom_call" | custom-call | bytes 65536 | tf_op jit(solution)/shard_map/second_pieces/pallas_call | solution.py:350
  214.4 1.5 collective-permute-start.9
  215.9 9.0 %second_transform.3 = (f32[16,48,1024]{2,1,0:T(8,128)}, bf16[48,16,1024]{2,1,0:T(8,128)(2,1)}) custom-call(f32[16]{0:T(128)} %step_ref.9, bf16[8,2,16,48,128]{4,3,2,1,0:T(8,128)(2,1)} %copy-done.2, bf16[1024,1024]{1,0:T(8,128)(2,1)} %constant.23.clone.cosine_ref, bf16[1024,1024]{1,0:T(8,128)(2,1)} %constant.24.clone.sine_ref, ...), custom_call_target="tpu_custom_call" | custom-call | bytes 65536 | tf_op jit(solution)/shard_map/second_transform/pallas_call | solution.py:289
  225.4 15.3 %collective-permute-done.9.value_ref = bf16[32,16,1024]{2,1,0:T(8,128)(2,1)S(1)} collective-permute-done((bf16[32,16,1024]{2,1,0:T(8,128)(2,1)}, bf16[32,16,1024]{2,1,0:T(8,128)(2,1)S(1)}, u32[]{:S(2)}, u32[]{:S(2)}) %collective-permute-start.9) | collective-permute-done | bytes 1048608 | tf_op jit(solution)/shard_map/ppermute | solution.py:532
  240.7 1.1 copy-done.4
  241.7 6.5 %first_transform.5 = (bf16[8,2,16,16,128]{4,3,2,1,0:T(8,128)(2,1)}, f32[8,128]{1,0:T(8,128)}) custom-call(bf16[256,1024]{1,0:T(8,128)(2,1)} %constant.25.clone.table_ref, bf16[2,16,128,1024]{3,2,1,0:T(8,128)(2,1)} %grid_ref.7, bf16[48,16,1024]{2,1,0:T(8,128)(2,1)} %get-tuple-element.51.after_ref.refs_0_.refs_4_), custom_call_target="tpu_custom_call" | custom-call | bytes 65536 | tf_op jit(solution)/shard_map/first_transform/pallas_call | solution.py:110
  248.2 4.5 %all-to-all-start.2 = ((bf16[8,2,16,16,128]{4,3,2,1,0:T(8,128)(2,1)}), bf16[8,2,16,16,128]{4,3,2,1,0:T(8,128)(2,1)}, u32[]{:S(2)}, u32[]{:S(2)}) async-start(bf16[8,2,16,16,128]{4,3,2,1,0:T(8,128)(2,1)} %get-tuple-element.56), calls=%async_computation.2 | async-start | bytes 2097152 | tf_op jit(solution)/shard_map/all_to_all | solution.py:581
  253.3 19.5 %collective-permute-done.12.value_ref = bf16[48,16,1024]{2,1,0:T(8,128)(2,1)S(1)} collective-permute-done((bf16[48,16,1024]{2,1,0:T(8,128)(2,1)}, bf16[48,16,1024]{2,1,0:T(8,128)(2,1)S(1)}, u32[]{:S(2)}, u32[]{:S(2)}) %collective-permute-start.12) | collective-permute-done | bytes 1572896 | tf_op jit(solution)/shard_map/ppermute | solution.py:532
  272.8 1.1 copy-done.1
  274.7 4.8 %gram_step.3.after_ref.before_ref = f32[256,256]{1,0:T(8,128)} custom-call(f32[256,256]{1,0:T(8,128)} %broadcast_in_dim.3.before_ref, f32[8,128]{1,0:T(8,128)} %get-tuple-element.52.after_ref, bf16[32,16,1024]{2,1,0:T(8,128)(2,1)} %get-tuple-element.50.after_ref.refs_0_.refs_8_, bf16[32,16,1024]{2,1,0:T(8,128)(2,1)} %gate.6.refs_1_.refs_9_, ...), custom_call_target="tpu_custom_call" | custom-call | bytes 65536 | tf_op jit(solution)/shard_map/gram_step/pallas_call | solution.py:398
  279.5 7.3 %second_transform.4 = (f32[16,32,1024]{2,1,0:T(8,128)}, bf16[32,16,1024]{2,1,0:T(8,128)(2,1)}) custom-call(f32[16]{0:T(128)} %step_ref.9, bf16[8,2,16,32,128]{4,3,2,1,0:T(8,128)(2,1)} %all-to-all-done.1.half_ref, bf16[1024,1024]{1,0:T(8,128)(2,1)} %constant.23.clone.cosine_ref, bf16[1024,1024]{1,0:T(8,128)(2,1)} %constant.24.clone.sine_ref, ...), custom_call_target="tpu_custom_call" | custom-call | bytes 65536 | tf_op jit(solution)/shard_map/second_transform/pallas_call | solution.py:289
  286.8 1.5 collective-permute-start.15
  288.5 6.6 %gram_step.4.after_ref.before_ref = f32[256,256]{1,0:T(8,128)} custom-call(f32[256,256]{1,0:T(8,128)} %gram_step.3.after_ref.before_ref, bf16[32,16,1024]{2,1,0:T(8,128)(2,1)} %get-tuple-element.55.after_ref.refs_0_.refs_12_, bf16[48,16,1024]{2,1,0:T(8,128)(2,1)} %get-tuple-element.51.after_ref.refs_0_.refs_4_, bf16[48,16,1024]{2,1,0:T(8,128)(2,1)} %gate.7.refs_1_.refs_5_, ...), custom_call_target="tpu_custom_call" | custom-call | bytes 65536 | tf_op jit(solution)/shard_map/gram_step/pallas_call | solution.py:398
  295.1 5.7 %second_transform.5 = (f32[16,16,1024]{2,1,0:T(8,128)}, bf16[16,16,1024]{2,1,0:T(8,128)(2,1)}) custom-call(f32[16]{0:T(128)} %step_ref.9, bf16[8,2,16,16,128]{4,3,2,1,0:T(8,128)(2,1)} %all-to-all-done.2.half_ref, bf16[1024,1024]{1,0:T(8,128)(2,1)} %constant.23.clone.cosine_ref, bf16[1024,1024]{1,0:T(8,128)(2,1)} %constant.24.clone.sine_ref, ...), custom_call_target="tpu_custom_call" | custom-call | bytes 65536 | tf_op jit(solution)/shard_map/second_transform/pallas_call | solution.py:289
  300.7 11.8 %collective-permute-done.15.value_ref = bf16[32,16,1024]{2,1,0:T(8,128)(2,1)S(1)} collective-permute-done((bf16[32,16,1024]{2,1,0:T(8,128)(2,1)}, bf16[32,16,1024]{2,1,0:T(8,128)(2,1)S(1)}, u32[]{:S(2)}, u32[]{:S(2)}) %collective-permute-start.15) | collective-permute-done | bytes 1048608 | tf_op jit(solution)/shard_map/ppermute | solution.py:532
  312.6 1.0 copy-done.3
  313.6 1.5 collective-permute-start.18
  315.3 1.2 collective-permute-done.17.refs_3_.refs_15_
  316.5 1.0 copy-done.6
  317.5 4.8 %gram_step.5.after_ref.gram_ref = f32[256,256]{1,0:T(8,128)} custom-call(f32[256,256]{1,0:T(8,128)} %gram_step.4.after_ref.before_ref, bf16[16,16,1024]{2,1,0:T(8,128)(2,1)} %get-tuple-element.58.after_ref.refs_16_, bf16[32,16,1024]{2,1,0:T(8,128)(2,1)} %get-tuple-element.55.after_ref.refs_0_.refs_12_, bf16[32,16,1024]{2,1,0:T(8,128)(2,1)} %gate.8.refs_1_.refs_13_, ...), custom_call_target="tpu_custom_call" | custom-call | bytes 65536 | tf_op jit(solution)/shard_map/gram_step/pallas_call | solution.py:398
  322.3 5.7 %collective-permute-done.18.value_ref = bf16[16,16,1024]{2,1,0:T(8,128)(2,1)S(1)} collective-permute-done((bf16[16,16,1024]{2,1,0:T(8,128)(2,1)S(1)}, bf16[16,16,1024]{2,1,0:T(8,128)(2,1)S(1)}, u32[]{:S(2)}, u32[]{:S(2)}) %collective-permute-start.18) | collective-permute-done | bytes 524320 | tf_op jit(solution)/shard_map/ppermute | solution.py:532
  328.0 0.8 copy-done.7
  329.5 1.4 collective-permute-done.20.refs_19_
  330.9 0.8 copy-done.9
  331.7 13.4 %polar_step.1 = f32[16,128,1024]{2,1,0:T(8,128)} custom-call(f32[1]{0:T(128)S(6)} %copy.22.shrink_ref, f32[256,256]{1,0:T(8,128)} %gram_step.5.after_ref.gram_ref, f32[16,48,1024]{2,1,0:T(8,128)} %get-tuple-element.59.refs_0_, f32[16,32,1024]{2,1,0:T(8,128)} %get-tuple-element.60.refs_1_, f32[16,32,1024]{2,1,0:T(8,128)} %get-tuple-element.61.refs_2_, ...), custom_call_target="tpu_custom_call" | custom-call | bytes 65536 | tf_op jit(solution)/shard_map/polar_step/pallas_call | solution.py:504
  (57 shorter events, 4.1 us)
Async XLA Ops:
  10.3 97.5 %all-to-all-start = ((bf16[8,2,16,48,128]{4,3,2,1,0:T(8,128)(2,1)}), bf16[8,2,16,48,128]{4,3,2,1,0:T(8,128)(2,1)S(1)}, u32[]{:S(2)}, u32[]{:S(2)}) async-start(bf16[8,2,16,48,128]{4,3,2,1,0:T(8,128)(2,1)} %get-tuple-element.34), calls=%async_computation | async-start | bytes 6291456 | tf_op jit(solution)/shard_map/all_to_all | solution.py:581
  19.3 76.0 %collective-permute-start = (bf16[16,12,1024]{2,1,0:T(8,128)(2,1)}, bf16[16,12,1024]{2,1,0:T(8,128)(2,1)S(1)}, u32[]{:S(2)}, u32[]{:S(2)}) collective-permute-start(bf16[16,12,1024]{2,1,0:T(8,128)(2,1)} %get-tuple-element.35), channel_id=1, source_target_pairs={{0,4},{4,8},{8,12},{12,16},{16,20},{20,24},{24,28},{1,5},{5,9},{9,... | collective-permute-start | bytes 1179656 | tf_op jit(solution)/shard_map/ppermute | solution.py:525
  22.6 74.5 %collective-permute-start.1 = (bf16[16,12,1024]{2,1,0:T(8,128)(2,1)}, bf16[16,12,1024]{2,1,0:T(8,128)(2,1)}, u32[]{:S(2)}, u32[]{:S(2)}) collective-permute-start(bf16[16,12,1024]{2,1,0:T(8,128)(2,1)} %get-tuple-element.36), channel_id=1, source_target_pairs={{4,0},{8,4},{12,8},{16,12},{20,16},{24,20},{28,24},{5,1},{9,5},{13... | collective-permute-start | bytes 1179656 | tf_op jit(solution)/shard_map/ppermute | solution.py:526
  107.8 1.7 copy-start.2
  107.8 48.1 %copy-start.17 = (bf16[2,16,32,128]{3,2,1,0:T(8,128)(2,1)S(1)}, bf16[2,16,32,128]{3,2,1,0:T(8,128)(2,1)}, u32[]{:S(2)}) copy-start(bf16[2,16,32,128]{3,2,1,0:T(8,128)(2,1)} %get-tuple-element.49) | copy-start | bytes 786436
  109.4 138.8 %all-to-all-start.1 = ((bf16[8,2,16,32,128]{4,3,2,1,0:T(8,128)(2,1)}), bf16[8,2,16,32,128]{4,3,2,1,0:T(8,128)(2,1)}, u32[]{:S(2)}, u32[]{:S(2)}) async-start(bf16[8,2,16,32,128]{4,3,2,1,0:T(8,128)(2,1)} %get-tuple-element.53), calls=%async_computation.1 | async-start | bytes 4194304 | tf_op jit(solution)/shard_map/all_to_all | solution.py:581
  113.7 23.4 %collective-permute-start.2 = (bf16[2,16,32,128]{3,2,1,0:T(8,128)(2,1)}, bf16[2,16,32,128]{3,2,1,0:T(8,128)(2,1)S(1)}, u32[]{:S(2)}, u32[]{:S(2)}) collective-permute-start(bf16[2,16,32,128]{3,2,1,0:T(8,128)(2,1)} %get-tuple-element.43), channel_id=1, source_target_pairs={{0,4},{4,0},{8,12},{12,8},{16,20},{20,16},{24,28},{28,24},{1,5},{5... | collective-permute-start | bytes 786440 | tf_op jit(solution)/shard_map/ppermute | solution.py:532
  114.2 41.7 %collective-permute-start.3 = (bf16[2,16,32,128]{3,2,1,0:T(8,128)(2,1)}, bf16[2,16,32,128]{3,2,1,0:T(8,128)(2,1)S(1)}, u32[]{:S(2)}, u32[]{:S(2)}) collective-permute-start(bf16[2,16,32,128]{3,2,1,0:T(8,128)(2,1)} %get-tuple-element.44), channel_id=1, source_target_pairs={{0,8},{4,12},{8,0},{12,4},{16,24},{20,28},{24,16},{28,20},{1,9},{5... | collective-permute-start | bytes 786440 | tf_op jit(solution)/shard_map/ppermute | solution.py:532
  114.2 54.8 %collective-permute-start.4 = (bf16[2,16,32,128]{3,2,1,0:T(8,128)(2,1)}, bf16[2,16,32,128]{3,2,1,0:T(8,128)(2,1)S(1)}, u32[]{:S(2)}, u32[]{:S(2)}) collective-permute-start(bf16[2,16,32,128]{3,2,1,0:T(8,128)(2,1)} %get-tuple-element.45), channel_id=1, source_target_pairs={{0,12},{4,8},{8,4},{12,0},{16,28},{20,24},{24,20},{28,16},{1,13},{... | collective-permute-start | bytes 786440 | tf_op jit(solution)/shard_map/ppermute | solution.py:532
  117.3 69.7 %collective-permute-start.5 = (bf16[2,16,32,128]{3,2,1,0:T(8,128)(2,1)}, bf16[2,16,32,128]{3,2,1,0:T(8,128)(2,1)S(1)}, u32[]{:S(2)}, u32[]{:S(2)}) collective-permute-start(bf16[2,16,32,128]{3,2,1,0:T(8,128)(2,1)} %get-tuple-element.46), channel_id=1, source_target_pairs={{0,16},{4,20},{8,24},{12,28},{16,0},{20,4},{24,8},{28,12},{1,17},{... | collective-permute-start | bytes 786440 | tf_op jit(solution)/shard_map/ppermute | solution.py:532
  119.5 73.1 %collective-permute-start.6 = (bf16[2,16,32,128]{3,2,1,0:T(8,128)(2,1)}, bf16[2,16,32,128]{3,2,1,0:T(8,128)(2,1)S(1)}, u32[]{:S(2)}, u32[]{:S(2)}) collective-permute-start(bf16[2,16,32,128]{3,2,1,0:T(8,128)(2,1)} %get-tuple-element.47), channel_id=1, source_target_pairs={{0,20},{4,16},{8,28},{12,24},{16,4},{20,0},{24,12},{28,8},{1,21},{... | collective-permute-start | bytes 786440 | tf_op jit(solution)/shard_map/ppermute | solution.py:532
  137.1 31.9 %copy-start.10 = (bf16[2,16,32,128]{3,2,1,0:T(8,128)(2,1)}, bf16[2,16,32,128]{3,2,1,0:T(8,128)(2,1)S(1)}, u32[]{:S(2)}) copy-start(bf16[2,16,32,128]{3,2,1,0:T(8,128)(2,1)S(1)} %collective-permute-done.2.refs_1_) | copy-start | bytes 786436
  137.1 63.8 %collective-permute-start.7 = (bf16[2,16,32,128]{3,2,1,0:T(8,128)(2,1)}, bf16[2,16,32,128]{3,2,1,0:T(8,128)(2,1)S(1)}, u32[]{:S(2)}, u32[]{:S(2)}) collective-permute-start(bf16[2,16,32,128]{3,2,1,0:T(8,128)(2,1)} %get-tuple-element.48), channel_id=1, source_target_pairs={{0,24},{4,28},{8,16},{12,20},{16,8},{20,12},{24,0},{28,4},{1,25},{... | collective-permute-start | bytes 786440 | tf_op jit(solution)/shard_map/ppermute | solution.py:532
  155.9 13.1 %copy-start.11 = (bf16[2,16,32,128]{3,2,1,0:T(8,128)(2,1)}, bf16[2,16,32,128]{3,2,1,0:T(8,128)(2,1)S(1)}, u32[]{:S(2)}) copy-start(bf16[2,16,32,128]{3,2,1,0:T(8,128)(2,1)S(1)} %collective-permute-done.3.refs_2_) | copy-start | bytes 786436
  155.9 50.5 %collective-permute-start.8 = (bf16[2,16,32,128]{3,2,1,0:T(8,128)(2,1)S(1)}, bf16[2,16,32,128]{3,2,1,0:T(8,128)(2,1)S(1)}, u32[]{:S(2)}, u32[]{:S(2)}) collective-permute-start(bf16[2,16,32,128]{3,2,1,0:T(8,128)(2,1)S(1)} %copy-done.17), channel_id=1, source_target_pairs={{0,28},{4,24},{8,20},{12,16},{16,12},{20,8},{24,4},{28,0},{1,29},{... | collective-permute-start | bytes 786440 | tf_op jit(solution)/shard_map/ppermute | solution.py:532
  169.0 37.4 %copy-start.12 = (bf16[2,16,32,128]{3,2,1,0:T(8,128)(2,1)}, bf16[2,16,32,128]{3,2,1,0:T(8,128)(2,1)S(1)}, u32[]{:S(2)}) copy-start(bf16[2,16,32,128]{3,2,1,0:T(8,128)(2,1)S(1)} %collective-permute-done.4.refs_3_) | copy-start | bytes 786436
  187.0 19.5 %copy-start.13 = (bf16[2,16,32,128]{3,2,1,0:T(8,128)(2,1)}, bf16[2,16,32,128]{3,2,1,0:T(8,128)(2,1)S(1)}, u32[]{:S(2)}) copy-start(bf16[2,16,32,128]{3,2,1,0:T(8,128)(2,1)S(1)} %collective-permute-done.5.refs_4_) | copy-start | bytes 786436
  192.6 13.8 %copy-start.14 = (bf16[2,16,32,128]{3,2,1,0:T(8,128)(2,1)}, bf16[2,16,32,128]{3,2,1,0:T(8,128)(2,1)S(1)}, u32[]{:S(2)}) copy-start(bf16[2,16,32,128]{3,2,1,0:T(8,128)(2,1)S(1)} %collective-permute-done.6.refs_5_) | copy-start | bytes 786436
  200.9 5.5 %copy-start.15 = (bf16[2,16,32,128]{3,2,1,0:T(8,128)(2,1)}, bf16[2,16,32,128]{3,2,1,0:T(8,128)(2,1)S(1)}, u32[]{:S(2)}) copy-start(bf16[2,16,32,128]{3,2,1,0:T(8,128)(2,1)S(1)} %collective-permute-done.7.refs_6_) | copy-start | bytes 786436
  206.4 0.7 copy-start.16
  214.4 26.3 %collective-permute-start.9 = (bf16[32,16,1024]{2,1,0:T(8,128)(2,1)}, bf16[32,16,1024]{2,1,0:T(8,128)(2,1)S(1)}, u32[]{:S(2)}, u32[]{:S(2)}) collective-permute-start(bf16[32,16,1024]{2,1,0:T(8,128)(2,1)} %get-tuple-element.50.after_ref.refs_0_.refs_8_), channel_id=1, source_target_pairs={{0,2},{1,3},{2,0},{3,1},{4,6},{5,7},{6,4},{7,5},{8,10},{9,11},{10,... | collective-permute-start | bytes 3145736 | tf_op jit(solution)/shard_map/ppermute | solution.py:532
  224.8 48.0 %collective-permute-start.12 = (bf16[48,16,1024]{2,1,0:T(8,128)(2,1)}, bf16[48,16,1024]{2,1,0:T(8,128)(2,1)S(1)}, u32[]{:S(2)}, u32[]{:S(2)}) collective-permute-start(bf16[48,16,1024]{2,1,0:T(8,128)(2,1)} %get-tuple-element.51.after_ref.refs_0_.refs_4_), channel_id=1, source_target_pairs={{0,2},{1,3},{2,0},{3,1},{4,6},{5,7},{6,4},{7,5},{8,10},{9,11},{10,... | collective-permute-start | bytes 4718600 | tf_op jit(solution)/shard_map/ppermute | solution.py:532
  225.4 48.6 %collective-permute-start.10 = (bf16[32,16,1024]{2,1,0:T(8,128)(2,1)}, bf16[32,16,1024]{2,1,0:T(8,128)(2,1)}, u32[]{:S(2)}, u32[]{:S(2)}) collective-permute-start(bf16[32,16,1024]{2,1,0:T(8,128)(2,1)} %get-tuple-element.50.after_ref.refs_0_.refs_8_), channel_id=1, source_target_pairs={{0,1},{1,0},{2,3},{3,2},{4,5},{5,4},{6,7},{7,6},{8,9},{9,8},{10,11... | collective-permute-start | bytes 3145736 | tf_op jit(solution)/shard_map/ppermute | solution.py:532
  240.7 1.1 copy-start.4
  241.7 32.3 %collective-permute-start.11 = (bf16[32,16,1024]{2,1,0:T(8,128)(2,1)}, bf16[32,16,1024]{2,1,0:T(8,128)(2,1)}, u32[]{:S(2)}, u32[]{:S(2)}) collective-permute-start(bf16[32,16,1024]{2,1,0:T(8,128)(2,1)} %gate.6.refs_1_.refs_9_), channel_id=1, source_target_pairs={{0,1},{1,0},{2,3},{3,2},{4,5},{5,4},{6,7},{7,6},{8,9},{9,8},{10,11... | collective-permute-start | bytes 3145736 | tf_op jit(solution)/shard_map/ppermute | solution.py:532
  248.2 4.5 %copy-start = (bf16[48,16,1024]{2,1,0:T(8,128)(2,1)S(1)}, bf16[48,16,1024]{2,1,0:T(8,128)(2,1)}, u32[]{:S(2)}) copy-start(bf16[48,16,1024]{2,1,0:T(8,128)(2,1)} %get-tuple-element.51.after_ref.refs_0_.refs_4_) | copy-start | bytes 4718596
  248.2 46.8 %all-to-all-start.2 = ((bf16[8,2,16,16,128]{4,3,2,1,0:T(8,128)(2,1)}), bf16[8,2,16,16,128]{4,3,2,1,0:T(8,128)(2,1)}, u32[]{:S(2)}, u32[]{:S(2)}) async-start(bf16[8,2,16,16,128]{4,3,2,1,0:T(8,128)(2,1)} %get-tuple-element.56), calls=%async_computation.2 | async-start | bytes 2097152 | tf_op jit(solution)/shard_map/all_to_all | solution.py:581
  252.8 35.7 %collective-permute-start.13 = (bf16[48,16,1024]{2,1,0:T(8,128)(2,1)S(1)}, bf16[48,16,1024]{2,1,0:T(8,128)(2,1)}, u32[]{:S(2)}, u32[]{:S(2)}) collective-permute-start(bf16[48,16,1024]{2,1,0:T(8,128)(2,1)S(1)} %copy-done), channel_id=1, source_target_pairs={{0,1},{1,0},{2,3},{3,2},{4,5},{5,4},{6,7},{7,6},{8,9},{9,8},{10,11... | collective-permute-start | bytes 4718600 | tf_op jit(solution)/shard_map/ppermute | solution.py:532
  272.8 1.1 copy-start.1
  274.0 14.5 %collective-permute-start.14 = (bf16[48,16,1024]{2,1,0:T(8,128)(2,1)}, bf16[48,16,1024]{2,1,0:T(8,128)(2,1)}, u32[]{:S(2)}, u32[]{:S(2)}) collective-permute-start(bf16[48,16,1024]{2,1,0:T(8,128)(2,1)} %gate.7.refs_1_.refs_5_), channel_id=1, source_target_pairs={{0,1},{1,0},{2,3},{3,2},{4,5},{5,4},{6,7},{7,6},{8,9},{9,8},{10,11... | collective-permute-start | bytes 4718600 | tf_op jit(solution)/shard_map/ppermute | solution.py:532
  286.8 25.8 %collective-permute-start.15 = (bf16[32,16,1024]{2,1,0:T(8,128)(2,1)}, bf16[32,16,1024]{2,1,0:T(8,128)(2,1)S(1)}, u32[]{:S(2)}, u32[]{:S(2)}) collective-permute-start(bf16[32,16,1024]{2,1,0:T(8,128)(2,1)} %get-tuple-element.55.after_ref.refs_0_.refs_12_), channel_id=1, source_target_pairs={{0,2},{1,3},{2,0},{3,1},{4,6},{5,7},{6,4},{7,5},{8,10},{9,11},{10,... | collective-permute-start | bytes 3145736 | tf_op jit(solution)/shard_map/ppermute | solution.py:532
  288.3 27.1 %collective-permute-start.16 = (bf16[32,16,1024]{2,1,0:T(8,128)(2,1)}, bf16[32,16,1024]{2,1,0:T(8,128)(2,1)}, u32[]{:S(2)}, u32[]{:S(2)}) collective-permute-start(bf16[32,16,1024]{2,1,0:T(8,128)(2,1)} %get-tuple-element.55.after_ref.refs_0_.refs_12_), channel_id=1, source_target_pairs={{0,1},{1,0},{2,3},{3,2},{4,5},{5,4},{6,7},{7,6},{8,9},{9,8},{10,11... | collective-permute-start | bytes 3145736 | tf_op jit(solution)/shard_map/ppermute | solution.py:532
  300.7 12.9 %copy-start.5 = (bf16[16,16,1024]{2,1,0:T(8,128)(2,1)S(1)}, bf16[16,16,1024]{2,1,0:T(8,128)(2,1)}, u32[]{:S(2)}) copy-start(bf16[16,16,1024]{2,1,0:T(8,128)(2,1)} %get-tuple-element.58.after_ref.refs_16_) | copy-start | bytes 1572868
  312.6 1.0 copy-start.3
  313.6 2.9 collective-permute-start.17
  313.6 14.3 %collective-permute-start.18 = (bf16[16,16,1024]{2,1,0:T(8,128)(2,1)S(1)}, bf16[16,16,1024]{2,1,0:T(8,128)(2,1)S(1)}, u32[]{:S(2)}, u32[]{:S(2)}) collective-permute-start(bf16[16,16,1024]{2,1,0:T(8,128)(2,1)S(1)} %copy-done.5), channel_id=1, source_target_pairs={{0,2},{1,3},{2,0},{3,1},{4,6},{5,7},{6,4},{7,5},{8,10},{9,11},{10,... | collective-permute-start | bytes 1572872 | tf_op jit(solution)/shard_map/ppermute | solution.py:532
  315.1 14.3 %collective-permute-start.19 = (bf16[16,16,1024]{2,1,0:T(8,128)(2,1)S(1)}, bf16[16,16,1024]{2,1,0:T(8,128)(2,1)S(1)}, u32[]{:S(2)}, u32[]{:S(2)}) collective-permute-start(bf16[16,16,1024]{2,1,0:T(8,128)(2,1)S(1)} %copy-done.5), channel_id=1, source_target_pairs={{0,1},{1,0},{2,3},{3,2},{4,5},{5,4},{6,7},{7,6},{8,9},{9,8},{10,11... | collective-permute-start | bytes 1572872 | tf_op jit(solution)/shard_map/ppermute | solution.py:532
  316.5 1.0 copy-start.6
  328.0 0.8 copy-start.7
  328.8 2.1 collective-permute-start.20
  329.5 1.5 copy-start.8
  330.9 0.8 copy-start.9

commit v11 on v10

--- a/solution.py
+++ b/solution.py
@@ -573,7 +573,7 @@
     state = dict(last=strip, gram=jnp.zeros((GRAM_ROWS * size, GRAM_ROWS * size), F32), bases=None)
 
     def first(chunk):
-        if chunk == 1:
+        if chunk == 2:
             sent, state["last"] = first_pieces(strip, tables[chunk], grid, strips, state["last"])
             halves[chunk] = exchange(sent)
         else:
@@ -588,7 +588,7 @@
 
     def second(chunk):
         inputs = (step_size, halves[chunk], cosine, sine_table, state["bases"][chunk], state["last"])
-        if chunk == 1:
+        if chunk == 2:
             moved[chunk], pixels[chunk] = second_pieces(strip, *inputs)
         else:
             moved[chunk], pixels[chunk] = second_transform(*inputs)
@@ -606,20 +606,19 @@
 
     first(0)
     first(1)
-    state["last"] = gate(state["last"], edges)
     first(2)
     base()
-    second(1)
     second(0)
-    gather(1)
     first(3)
     gather(0)
-    gram(1)
     second(2)
     gram(0)
+    gather(2)
+    second(1)
+    gram(2)
     second(3)
-    gather(2)
-    gram(2)
+    gather(1)
+    gram(1)
     gather(3)
     order = range(chunks)
     return polar_step(

time: 347 us -> 347 us (level)
    all_to_all x3, waiting for transfers between devices: 0.01 us -> 59 us  [first(): lax.all_to_all(sent, 'strip', split_axis=0, concat_axis=0, tiled=True)]
    ppermute x19, waiting for transfers between devices: 126 us -> 91.9 us  [swap(): return lax.ppermute(value, axis, [(i, i ^ bits) for i in range(count)])]
    ppermute x1, waiting for transfers between devices: 61.6 us -> 39.6 us  [neighbour_rows(): lax.ppermute(tail.astype(BF16), 'strip', [(i, i + 1) for i in range(ends)])]
    unnamed x36 -> x28, local copies, waits for them, and re-layouts: 8.23 us -> 7.17 us
  transfers between devices with their start and end apart: 24 -> 24, of which waited for: 14 -> 12; matrix products, arithmetic and copies ran while one was open for 2% -> 1% of each run, Pallas kernels for 23% -> 23%
where the time goes in v11:
time: 347 us; the launch traced here: 345 us
  waiting for transfers between devices  192 us (55%)
  Pallas kernels  104 us (30%)
  starting transfers between devices  37.6 us (11%)
  local copies, waits for them, and re-layouts  9.63 us (3%)
    ppermute x19, waiting for transfers between devices, swap(): return lax.ppermute(value, axis, [(i, i ^ bits) for i in range(count)])  91.9 us
    all_to_all x3, waiting for transfers between devices, first(): lax.all_to_all(sent, 'strip', split_axis=0, concat_axis=0, tiled=True)  59 us
    ppermute x1, waiting for transfers between devices, neighbour_rows(): lax.ppermute(tail.astype(BF16), 'strip', [(i, i + 1) for i in range(ends)])  39.6 us
    pallas_call x3, Pallas kernels, first_transform(): pl.pallas_call(first_body, grid=(chans // block,), in_specs=[pl.BlockSpec...  25.4 us
    pallas_call x3, Pallas kernels, second_transform(): pl.pallas_call(second_body, grid=(side_len // block,), in_specs=[SMEM, pl...  21.9 us
    all_to_all x3, starting transfers between devices, first(): lax.all_to_all(sent, 'strip', split_axis=0, concat_axis=0, tiled=True)  18.1 us
    pallas_call x3, Pallas kernels, gram_step(): pl.pallas_call(functools.partial(gram_body, len(pieces)), grid=(rows // b...  16.2 us
    ppermute x19, starting transfers between devices, swap(): return lax.ppermute(value, axis, [(i, i ^ bits) for i in range(count)])  13.6 us
  transfers between devices with their start and end apart: 24, of which 12 were waited for; matrix products, arithmetic and copies ran while one was open for 1% of the time, Pallas kernels for 23%

profile of v11, /device:TPU:12, one launch (start us, length us, event | category | flops | bytes accessed | tf_op | source)
XLA Modules:
  0.0 345.5 jit_solution(14824188920806070709)
XLA Ops:
  0.0 10.3 %first_transform.3 = (bf16[8,2,16,48,128]{4,3,2,1,0:T(8,128)(2,1)}, f32[8,128]{1,0:T(8,128)}) custom-call(bf16[768,1024]{1,0:T(8,128)(2,1)} %constant.20.clone.table_ref, bf16[2,16,128,1024]{3,2,1,0:T(8,128)(2,1)} %grid_ref.7, s32[1]{0:T(128)} %bitcast.after_ref.strip_ref), custom_call_target="tpu_custom_call" | custom-call | bytes 65536 | tf_op jit(solution)/shard_map/first_transform/pallas_call | solution.py:110
  10.3 6.2 %all-to-all-start = ((bf16[8,2,16,48,128]{4,3,2,1,0:T(8,128)(2,1)}), bf16[8,2,16,48,128]{4,3,2,1,0:T(8,128)(2,1)S(1)}, u32[]{:S(2)}, u32[]{:S(2)}) async-start(bf16[8,2,16,48,128]{4,3,2,1,0:T(8,128)(2,1)} %get-tuple-element.40), calls=%async_computation | async-start | bytes 6291456 | tf_op jit(solution)/shard_map/all_to_all | solution.py:581
  16.5 8.5 %first_transform.4 = (bf16[8,2,16,32,128]{4,3,2,1,0:T(8,128)(2,1)}, f32[8,128]{1,0:T(8,128)}) custom-call(bf16[512,1024]{1,0:T(8,128)(2,1)} %constant.21.clone.table_ref, bf16[2,16,128,1024]{3,2,1,0:T(8,128)(2,1)} %grid_ref.7, f32[8,128]{1,0:T(8,128)} %get-tuple-element.36.after_ref), custom_call_target="tpu_custom_call" | custom-call | bytes 65536 | tf_op jit(solution)/shard_map/first_transform/pallas_call | solution.py:110
  25.0 59.0 %all-to-all-done.half_ref = bf16[8,2,16,48,128]{4,3,2,1,0:T(8,128)(2,1)S(1)} async-done(((bf16[8,2,16,48,128]{4,3,2,1,0:T(8,128)(2,1)}), bf16[8,2,16,48,128]{4,3,2,1,0:T(8,128)(2,1)S(1)}, u32[]{:S(2)}, u32[]{:S(2)}) %all-to-all-start) | async-done | bytes 3145760 | tf_op jit(solution)/shard_map/all_to_all | solution.py:581
  84.0 1.7 copy-done.2
  85.6 7.5 %all-to-all-start.1 = ((bf16[8,2,16,32,128]{4,3,2,1,0:T(8,128)(2,1)}), bf16[8,2,16,32,128]{4,3,2,1,0:T(8,128)(2,1)}, u32[]{:S(2)}, u32[]{:S(2)}) async-start(bf16[8,2,16,32,128]{4,3,2,1,0:T(8,128)(2,1)} %get-tuple-element.53), calls=%async_computation.1 | async-start | bytes 4194304 | tf_op jit(solution)/shard_map/all_to_all | solution.py:581
  93.2 1.7 fusion
  94.9 3.4 collective-permute-start
  98.3 2.5 collective-permute-start.1
  100.8 8.5 %first_pieces.1 = (bf16[2,16,32,128]{3,2,1,0:T(8,128)(2,1)}, bf16[2,16,32,128]{3,2,1,0:T(8,128)(2,1)}, bf16[2,16,32,128]{3,2,1,0:T(8,128)(2,1)}, bf16[2,16,32,12...) custom-call(s32[1]{0:T(128)} %bitcast.after_ref.strip_ref, ...), custom_call_target="tpu_custom_call" | custom-call | bytes 65536 | tf_op jit(solution)/shard_map/first_pieces/pallas_call | solution.py:164
  109.3 39.6 %collective-permute-done = bf16[16,12,1024]{2,1,0:T(8,128)(2,1)S(1)} collective-permute-done((bf16[16,12,1024]{2,1,0:T(8,128)(2,1)S(1)}, bf16[16,12,1024]{2,1,0:T(8,128)(2,1)S(1)}, u32[]{:S(2)}, u32[]{:S(2)}) %collective-permute-start) | collective-permute-done | bytes 393248 | tf_op jit(solution)/shard_map/ppermute | solution.py:525
  148.9 1.9 collective-permute-done.1
  150.8 1.1 pad_maximum_fusion.edge_ref
  151.9 11.2 %base_step.1 = (f32[16,48,1024]{2,1,0:T(8,128)}, f32[16,32,1024]{2,1,0:T(8,128)}, f32[16,32,1024]{2,1,0:T(8,128)}, f32[16,16,1024]{2,1,0:T(8,128)}) custom-call(s32[1]{0:T(128)} %bitcast.after_ref.strip_ref, f32[16]{0:T(128)} %step_ref.9, f32[3,4]{1,0:T(4,128)} %highpass_ref.1, f32[16,128,1024]{2,1,0:T(8,128)} %model_ref.1, ...), custom_call_target="tpu_custom_call" | custom-call | bytes 65536 | tf_op jit(solution)/shard_map/base_step/pallas_call | solution.py:246
  163.1 9.0 %second_transform.3 = (f32[16,48,1024]{2,1,0:T(8,128)}, bf16[48,16,1024]{2,1,0:T(8,128)(2,1)}) custom-call(f32[16]{0:T(128)} %step_ref.9, bf16[8,2,16,48,128]{4,3,2,1,0:T(8,128)(2,1)} %copy-done.2, bf16[1024,1024]{1,0:T(8,128)(2,1)} %constant.23.clone.cosine_ref, bf16[1024,1024]{1,0:T(8,128)(2,1)} %constant.24.clone.sine_ref, ...), custom_call_target="tpu_custom_call" | custom-call | bytes 65536 | tf_op jit(solution)/shard_map/second_transform/pallas_call | solution.py:289
  172.0 1.5 collective-permute-start.9
  173.6 3.5 %collective-permute-start.4 = (bf16[2,16,32,128]{3,2,1,0:T(8,128)(2,1)}, bf16[2,16,32,128]{3,2,1,0:T(8,128)(2,1)}, u32[]{:S(2)}, u32[]{:S(2)}) collective-permute-start(bf16[2,16,32,128]{3,2,1,0:T(8,128)(2,1)} %get-tuple-element.47), channel_id=1, source_target_pairs={{0,12},{4,8},{8,4},{12,0},{16,28},{20,24},{24,20},{28,16},{1,13},{... | collective-permute-start | bytes 786440 | tf_op jit(solution)/shard_map/ppermute | solution.py:532
  177.1 6.6 %first_transform.5 = (bf16[8,2,16,16,128]{4,3,2,1,0:T(8,128)(2,1)}, f32[8,128]{1,0:T(8,128)}) custom-call(bf16[256,1024]{1,0:T(8,128)(2,1)} %constant.25.clone.table_ref, bf16[2,16,128,1024]{3,2,1,0:T(8,128)(2,1)} %grid_ref.7, bf16[48,16,1024]{2,1,0:T(8,128)(2,1)} %get-tuple-element.42.after_ref.refs_0_.refs_4_), custom_call_target="tpu_custom_call" | custom-call | bytes 65536 | tf_op jit(solution)/shard_map/first_transform/pallas_call | solution.py:110
  183.7 23.1 %collective-permute-done.9.value_ref = bf16[48,16,1024]{2,1,0:T(8,128)(2,1)S(1)} collective-permute-done((bf16[48,16,1024]{2,1,0:T(8,128)(2,1)}, bf16[48,16,1024]{2,1,0:T(8,128)(2,1)S(1)}, u32[]{:S(2)}, u32[]{:S(2)}) %collective-permute-start.9) | collective-permute-done | bytes 1572896 | tf_op jit(solution)/shard_map/ppermute | solution.py:532
  206.8 1.2 copy-done.1
  208.2 3.3 collective-permute-start.8
  211.5 20.4 %collective-permute-done.6.refs_5_ = bf16[2,16,32,128]{3,2,1,0:T(8,128)(2,1)S(1)} collective-permute-done((bf16[2,16,32,128]{3,2,1,0:T(8,128)(2,1)}, bf16[2,16,32,128]{3,2,1,0:T(8,128)(2,1)S(1)}, u32[]{:S(2)}, u32[]{:S(2)}) %collective-permute-start.6) | collective-permute-done | bytes 262176 | tf_op jit(solution)/shard_map/ppermute | solution.py:532
  231.9 5.6 %collective-permute-done.7.refs_6_ = bf16[2,16,32,128]{3,2,1,0:T(8,128)(2,1)S(1)} collective-permute-done((bf16[2,16,32,128]{3,2,1,0:T(8,128)(2,1)}, bf16[2,16,32,128]{3,2,1,0:T(8,128)(2,1)S(1)}, u32[]{:S(2)}, u32[]{:S(2)}) %collective-permute-start.7) | collective-permute-done | bytes 262176 | tf_op jit(solution)/shard_map/ppermute | solution.py:532
  237.5 9.0 %collective-permute-done.8.refs_7_ = bf16[2,16,32,128]{3,2,1,0:T(8,128)(2,1)S(1)} collective-permute-done((bf16[2,16,32,128]{3,2,1,0:T(8,128)(2,1)}, bf16[2,16,32,128]{3,2,1,0:T(8,128)(2,1)S(1)}, u32[]{:S(2)}, u32[]{:S(2)}) %collective-permute-start.8) | collective-permute-done | bytes 262176 | tf_op jit(solution)/shard_map/ppermute | solution.py:532
  246.5 0.7 copy-done.13
  247.2 7.2 %second_pieces.1 = (f32[16,32,1024]{2,1,0:T(8,128)}, bf16[32,16,1024]{2,1,0:T(8,128)(2,1)}) custom-call(s32[1]{0:T(128)} %bitcast.after_ref.strip_ref, f32[16]{0:T(128)} %step_ref.9, bf16[1024,1024]{1,0:T(8,128)(2,1)} %constant.23.clone.cosine_ref, bf16[1024,1024]{1,0:T(8,128)(2,1)} %constant.24.clone.sine_ref, f32[16,32,1024]{2,1,0:T(8,128)} %get-tuple-element.39.base_ref, ...), custom_call_target="tpu_custom_call" | custom-call | bytes 65536 | tf_op jit(solution)/shard_map/second_pieces/pallas_call | solution.py:350
  254.5 1.6 collective-permute-start.12
  256.1 4.4 %all-to-all-start.2 = ((bf16[8,2,16,16,128]{4,3,2,1,0:T(8,128)(2,1)}), bf16[8,2,16,16,128]{4,3,2,1,0:T(8,128)(2,1)}, u32[]{:S(2)}, u32[]{:S(2)}) async-start(bf16[8,2,16,16,128]{4,3,2,1,0:T(8,128)(2,1)} %get-tuple-element.56), calls=%async_computation.2 | async-start | bytes 2097152 | tf_op jit(solution)/shard_map/all_to_all | solution.py:581
  260.6 0.7 broadcast_in_dim.3.before_ref
  261.3 6.5 %gram_step.3.after_ref.before_ref = f32[256,256]{1,0:T(8,128)} custom-call(f32[256,256]{1,0:T(8,128)} %broadcast_in_dim.3.before_ref, bf16[32,16,1024]{2,1,0:T(8,128)(2,1)} %get-tuple-element.52.after_ref.refs_0_.refs_12_, bf16[48,16,1024]{2,1,0:T(8,128)(2,1)} %get-tuple-element.42.after_ref.refs_0_.refs_4_, bf16[48,16,1024]{2,1,0:T(8,128)(2,1)} %gate.4.refs_1_.refs_5_, ...), custom_call_target="tpu_custom_call" | custom-call | bytes 65536 | tf_op jit(solution)/shard_map/gram_step/pallas_call | solution.py:398
  267.8 12.0 %collective-permute-done.12.value_ref = bf16[32,16,1024]{2,1,0:T(8,128)(2,1)} collective-permute-done((bf16[32,16,1024]{2,1,0:T(8,128)(2,1)}, bf16[32,16,1024]{2,1,0:T(8,128)(2,1)}, u32[]{:S(2)}, u32[]{:S(2)}) %collective-permute-start.12) | collective-permute-done | bytes 1048608 | tf_op jit(solution)/shard_map/ppermute | solution.py:532
  279.8 7.3 %second_transform.4 = (f32[16,32,1024]{2,1,0:T(8,128)}, bf16[32,16,1024]{2,1,0:T(8,128)(2,1)}) custom-call(f32[16]{0:T(128)} %step_ref.9, bf16[8,2,16,32,128]{4,3,2,1,0:T(8,128)(2,1)} %all-to-all-done.1.half_ref, bf16[1024,1024]{1,0:T(8,128)(2,1)} %constant.23.clone.cosine_ref, bf16[1024,1024]{1,0:T(8,128)(2,1)} %constant.24.clone.sine_ref, ...), custom_call_target="tpu_custom_call" | custom-call | bytes 65536 | tf_op jit(solution)/shard_map/second_transform/pallas_call | solution.py:289
  287.1 1.5 collective-permute-start.15
  288.6 0.2 collective-permute-start.16
  288.8 4.8 %gram_step.4.after_ref.before_ref = f32[256,256]{1,0:T(8,128)} custom-call(f32[256,256]{1,0:T(8,128)} %gram_step.3.after_ref.before_ref, bf16[32,16,1024]{2,1,0:T(8,128)(2,1)} %get-tuple-element.55.after_ref.refs_0_.refs_8_, bf16[32,16,1024]{2,1,0:T(8,128)(2,1)} %get-tuple-element.52.after_ref.refs_0_.refs_12_, bf16[32,16,1024]{2,1,0:T(8,128)(2,1)} %gate.5.refs_1_.refs_13_, ...), custom_call_target="tpu_custom_call" | custom-call | bytes 65536 | tf_op jit(solution)/shard_map/gram_step/pallas_call | solution.py:398
  293.6 5.6 %second_transform.5 = (f32[16,16,1024]{2,1,0:T(8,128)}, bf16[16,16,1024]{2,1,0:T(8,128)(2,1)}) custom-call(f32[16]{0:T(128)} %step_ref.9, bf16[8,2,16,16,128]{4,3,2,1,0:T(8,128)(2,1)} %all-to-all-done.2.half_ref, bf16[1024,1024]{1,0:T(8,128)(2,1)} %constant.23.clone.cosine_ref, bf16[1024,1024]{1,0:T(8,128)(2,1)} %constant.24.clone.sine_ref, ...), custom_call_target="tpu_custom_call" | custom-call | bytes 65536 | tf_op jit(solution)/shard_map/second_transform/pallas_call | solution.py:289
  299.3 13.6 %collective-permute-done.15.value_ref = bf16[32,16,1024]{2,1,0:T(8,128)(2,1)S(1)} collective-permute-done((bf16[32,16,1024]{2,1,0:T(8,128)(2,1)}, bf16[32,16,1024]{2,1,0:T(8,128)(2,1)S(1)}, u32[]{:S(2)}, u32[]{:S(2)}) %collective-permute-start.15) | collective-permute-done | bytes 1048608 | tf_op jit(solution)/shard_map/ppermute | solution.py:532
  312.8 1.0 copy-done.3
  313.8 1.5 collective-permute-start.18
  315.3 0.2 collective-permute-start.19
  315.6 1.1 collective-permute-done.17.refs_3_.refs_11_
  316.7 1.0 copy-done.6
  317.7 4.8 %gram_step.5.after_ref.gram_ref = f32[256,256]{1,0:T(8,128)} custom-call(f32[256,256]{1,0:T(8,128)} %gram_step.4.after_ref.before_ref, bf16[16,16,1024]{2,1,0:T(8,128)(2,1)} %get-tuple-element.58.after_ref.refs_16_, bf16[32,16,1024]{2,1,0:T(8,128)(2,1)} %get-tuple-element.55.after_ref.refs_0_.refs_8_, bf16[32,16,1024]{2,1,0:T(8,128)(2,1)} %gate.6.refs_1_.refs_9_, ...), custom_call_target="tpu_custom_call" | custom-call | bytes 65536 | tf_op jit(solution)/shard_map/gram_step/pallas_call | solution.py:398
  322.5 5.7 %collective-permute-done.18.value_ref = bf16[16,16,1024]{2,1,0:T(8,128)(2,1)S(1)} collective-permute-done((bf16[16,16,1024]{2,1,0:T(8,128)(2,1)S(1)}, bf16[16,16,1024]{2,1,0:T(8,128)(2,1)S(1)}, u32[]{:S(2)}, u32[]{:S(2)}) %collective-permute-start.18) | collective-permute-done | bytes 524320 | tf_op jit(solution)/shard_map/ppermute | solution.py:532
  328.2 0.8 copy-done.7
  329.7 1.4 collective-permute-done.20.refs_19_
  331.1 0.8 copy-done.9
  331.9 13.4 %polar_step.1 = f32[16,128,1024]{2,1,0:T(8,128)} custom-call(f32[1]{0:T(128)S(6)} %copy.20.shrink_ref, f32[256,256]{1,0:T(8,128)} %gram_step.5.after_ref.gram_ref, f32[16,48,1024]{2,1,0:T(8,128)} %get-tuple-element.59.refs_0_, f32[16,32,1024]{2,1,0:T(8,128)} %get-tuple-element.60.refs_1_, f32[16,32,1024]{2,1,0:T(8,128)} %get-tuple-element.61.refs_2_, ...), custom_call_target="tpu_custom_call" | custom-call | bytes 65536 | tf_op jit(solution)/shard_map/polar_step/pallas_call | solution.py:504
  (48 shorter events, 0.3 us)
Async XLA Ops:
  10.3 73.7 %all-to-all-start = ((bf16[8,2,16,48,128]{4,3,2,1,0:T(8,128)(2,1)}), bf16[8,2,16,48,128]{4,3,2,1,0:T(8,128)(2,1)S(1)}, u32[]{:S(2)}, u32[]{:S(2)}) async-start(bf16[8,2,16,48,128]{4,3,2,1,0:T(8,128)(2,1)} %get-tuple-element.40), calls=%async_computation | async-start | bytes 6291456 | tf_op jit(solution)/shard_map/all_to_all | solution.py:581
  84.0 1.7 copy-start.2
  85.6 170.4 %all-to-all-start.1 = ((bf16[8,2,16,32,128]{4,3,2,1,0:T(8,128)(2,1)}), bf16[8,2,16,32,128]{4,3,2,1,0:T(8,128)(2,1)}, u32[]{:S(2)}, u32[]{:S(2)}) async-start(bf16[8,2,16,32,128]{4,3,2,1,0:T(8,128)(2,1)} %get-tuple-element.53), calls=%async_computation.1 | async-start | bytes 4194304 | tf_op jit(solution)/shard_map/all_to_all | solution.py:581
  94.9 54.0 %collective-permute-start = (bf16[16,12,1024]{2,1,0:T(8,128)(2,1)S(1)}, bf16[16,12,1024]{2,1,0:T(8,128)(2,1)S(1)}, u32[]{:S(2)}, u32[]{:S(2)}) collective-permute-start(bf16[16,12,1024]{2,1,0:T(8,128)(2,1)S(1)} %get-tuple-element.34), channel_id=1, source_target_pairs={{0,4},{4,8},{8,12},{12,16},{16,20},{20,24},{24,28},{1,5},{5,9},{9,... | collective-permute-start | bytes 1179656 | tf_op jit(solution)/shard_map/ppermute | solution.py:525
  98.3 52.5 %collective-permute-start.1 = (bf16[16,12,1024]{2,1,0:T(8,128)(2,1)S(1)}, bf16[16,12,1024]{2,1,0:T(8,128)(2,1)S(1)}, u32[]{:S(2)}, u32[]{:S(2)}) collective-permute-start(bf16[16,12,1024]{2,1,0:T(8,128)(2,1)S(1)} %get-tuple-element.35), channel_id=1, source_target_pairs={{4,0},{8,4},{12,8},{16,12},{20,16},{24,20},{28,24},{5,1},{9,5},{13... | collective-permute-start | bytes 1179656 | tf_op jit(solution)/shard_map/ppermute | solution.py:526
  172.0 34.7 %collective-permute-start.9 = (bf16[48,16,1024]{2,1,0:T(8,128)(2,1)}, bf16[48,16,1024]{2,1,0:T(8,128)(2,1)S(1)}, u32[]{:S(2)}, u32[]{:S(2)}) collective-permute-start(bf16[48,16,1024]{2,1,0:T(8,128)(2,1)} %get-tuple-element.42.after_ref.refs_0_.refs_4_), channel_id=1, source_target_pairs={{0,2},{1,3},{2,0},{3,1},{4,6},{5,7},{6,4},{7,5},{8,10},{9,11},{10,... | collective-permute-start | bytes 4718600 | tf_op jit(solution)/shard_map/ppermute | solution.py:532
  173.5 34.4 %collective-permute-start.2 = (bf16[2,16,32,128]{3,2,1,0:T(8,128)(2,1)}, bf16[2,16,32,128]{3,2,1,0:T(8,128)(2,1)S(1)}, u32[]{:S(2)}, u32[]{:S(2)}) collective-permute-start(bf16[2,16,32,128]{3,2,1,0:T(8,128)(2,1)} %get-tuple-element.45), channel_id=1, source_target_pairs={{0,4},{4,0},{8,12},{12,8},{16,20},{20,16},{24,28},{28,24},{1,5},{5... | collective-permute-start | bytes 786440 | tf_op jit(solution)/shard_map/ppermute | solution.py:532
  173.6 34.4 %collective-permute-start.3 = (bf16[2,16,32,128]{3,2,1,0:T(8,128)(2,1)}, bf16[2,16,32,128]{3,2,1,0:T(8,128)(2,1)}, u32[]{:S(2)}, u32[]{:S(2)}) collective-permute-start(bf16[2,16,32,128]{3,2,1,0:T(8,128)(2,1)} %get-tuple-element.46), channel_id=1, source_target_pairs={{0,8},{4,12},{8,0},{12,4},{16,24},{20,28},{24,16},{28,20},{1,9},{5... | collective-permute-start | bytes 786440 | tf_op jit(solution)/shard_map/ppermute | solution.py:532
  173.6 34.5 %collective-permute-start.4 = (bf16[2,16,32,128]{3,2,1,0:T(8,128)(2,1)}, bf16[2,16,32,128]{3,2,1,0:T(8,128)(2,1)}, u32[]{:S(2)}, u32[]{:S(2)}) collective-permute-start(bf16[2,16,32,128]{3,2,1,0:T(8,128)(2,1)} %get-tuple-element.47), channel_id=1, source_target_pairs={{0,12},{4,8},{8,4},{12,0},{16,28},{20,24},{24,20},{28,16},{1,13},{... | collective-permute-start | bytes 786440 | tf_op jit(solution)/shard_map/ppermute | solution.py:532
  177.0 29.8 %copy-start = (bf16[48,16,1024]{2,1,0:T(8,128)(2,1)S(1)}, bf16[48,16,1024]{2,1,0:T(8,128)(2,1)}, u32[]{:S(2)}) copy-start(bf16[48,16,1024]{2,1,0:T(8,128)(2,1)} %get-tuple-element.42.after_ref.refs_0_.refs_4_) | copy-start | bytes 4718596
  177.0 31.1 %collective-permute-start.5 = (bf16[2,16,32,128]{3,2,1,0:T(8,128)(2,1)}, bf16[2,16,32,128]{3,2,1,0:T(8,128)(2,1)}, u32[]{:S(2)}, u32[]{:S(2)}) collective-permute-start(bf16[2,16,32,128]{3,2,1,0:T(8,128)(2,1)} %get-tuple-element.48), channel_id=1, source_target_pairs={{0,16},{4,20},{8,24},{12,28},{16,0},{20,4},{24,8},{28,12},{1,17},{... | collective-permute-start | bytes 786440 | tf_op jit(solution)/shard_map/ppermute | solution.py:532
  206.8 1.2 copy-start.1
  206.8 53.7 %collective-permute-start.10 = (bf16[48,16,1024]{2,1,0:T(8,128)(2,1)S(1)}, bf16[48,16,1024]{2,1,0:T(8,128)(2,1)}, u32[]{:S(2)}, u32[]{:S(2)}) collective-permute-start(bf16[48,16,1024]{2,1,0:T(8,128)(2,1)S(1)} %copy-done), channel_id=1, source_target_pairs={{0,1},{1,0},{2,3},{3,2},{4,5},{5,4},{6,7},{7,6},{8,9},{9,8},{10,11... | collective-permute-start | bytes 4718600 | tf_op jit(solution)/shard_map/ppermute | solution.py:532
  208.0 38.6 %copy-start.10 = (bf16[2,16,32,128]{3,2,1,0:T(8,128)(2,1)}, bf16[2,16,32,128]{3,2,1,0:T(8,128)(2,1)S(1)}, u32[]{:S(2)}) copy-start(bf16[2,16,32,128]{3,2,1,0:T(8,128)(2,1)S(1)} %collective-permute-done.2.refs_1_) | copy-start | bytes 786436
  208.0 52.6 %collective-permute-start.11 = (bf16[48,16,1024]{2,1,0:T(8,128)(2,1)}, bf16[48,16,1024]{2,1,0:T(8,128)(2,1)}, u32[]{:S(2)}, u32[]{:S(2)}) collective-permute-start(bf16[48,16,1024]{2,1,0:T(8,128)(2,1)} %gate.4.refs_1_.refs_5_), channel_id=1, source_target_pairs={{0,1},{1,0},{2,3},{3,2},{4,5},{5,4},{6,7},{7,6},{8,9},{9,8},{10,11... | collective-permute-start | bytes 4718600 | tf_op jit(solution)/shard_map/ppermute | solution.py:532
  208.0 23.9 %collective-permute-start.6 = (bf16[2,16,32,128]{3,2,1,0:T(8,128)(2,1)}, bf16[2,16,32,128]{3,2,1,0:T(8,128)(2,1)S(1)}, u32[]{:S(2)}, u32[]{:S(2)}) collective-permute-start(bf16[2,16,32,128]{3,2,1,0:T(8,128)(2,1)} %get-tuple-element.49), channel_id=1, source_target_pairs={{0,20},{4,16},{8,28},{12,24},{16,4},{20,0},{24,12},{28,8},{1,21},{... | collective-permute-start | bytes 786440 | tf_op jit(solution)/shard_map/ppermute | solution.py:532
  208.1 29.5 %collective-permute-start.7 = (bf16[2,16,32,128]{3,2,1,0:T(8,128)(2,1)}, bf16[2,16,32,128]{3,2,1,0:T(8,128)(2,1)S(1)}, u32[]{:S(2)}, u32[]{:S(2)}) collective-permute-start(bf16[2,16,32,128]{3,2,1,0:T(8,128)(2,1)} %get-tuple-element.50), channel_id=1, source_target_pairs={{0,24},{4,28},{8,16},{12,20},{16,8},{20,12},{24,0},{28,4},{1,25},{... | collective-permute-start | bytes 786440 | tf_op jit(solution)/shard_map/ppermute | solution.py:532
  208.2 38.4 %collective-permute-start.8 = (bf16[2,16,32,128]{3,2,1,0:T(8,128)(2,1)}, bf16[2,16,32,128]{3,2,1,0:T(8,128)(2,1)S(1)}, u32[]{:S(2)}, u32[]{:S(2)}) collective-permute-start(bf16[2,16,32,128]{3,2,1,0:T(8,128)(2,1)} %get-tuple-element.51), channel_id=1, source_target_pairs={{0,28},{4,24},{8,20},{12,16},{16,12},{20,8},{24,4},{28,0},{1,29},{... | collective-permute-start | bytes 786440 | tf_op jit(solution)/shard_map/ppermute | solution.py:532
  231.9 14.6 %copy-start.11 = (bf16[2,16,32,128]{3,2,1,0:T(8,128)(2,1)}, bf16[2,16,32,128]{3,2,1,0:T(8,128)(2,1)S(1)}, u32[]{:S(2)}) copy-start(bf16[2,16,32,128]{3,2,1,0:T(8,128)(2,1)S(1)} %collective-permute-done.6.refs_5_) | copy-start | bytes 786436
  237.5 9.0 %copy-start.12 = (bf16[2,16,32,128]{3,2,1,0:T(8,128)(2,1)}, bf16[2,16,32,128]{3,2,1,0:T(8,128)(2,1)S(1)}, u32[]{:S(2)}) copy-start(bf16[2,16,32,128]{3,2,1,0:T(8,128)(2,1)S(1)} %collective-permute-done.7.refs_6_) | copy-start | bytes 786436
  246.5 0.7 copy-start.13
  254.5 6.0 %copy-start.4 = (bf16[32,16,1024]{2,1,0:T(8,128)(2,1)S(1)}, bf16[32,16,1024]{2,1,0:T(8,128)(2,1)}, u32[]{:S(2)}) copy-start(bf16[32,16,1024]{2,1,0:T(8,128)(2,1)} %get-tuple-element.52.after_ref.refs_0_.refs_12_) | copy-start | bytes 3145732
  254.5 25.3 %collective-permute-start.12 = (bf16[32,16,1024]{2,1,0:T(8,128)(2,1)}, bf16[32,16,1024]{2,1,0:T(8,128)(2,1)}, u32[]{:S(2)}, u32[]{:S(2)}) collective-permute-start(bf16[32,16,1024]{2,1,0:T(8,128)(2,1)} %get-tuple-element.52.after_ref.refs_0_.refs_12_), channel_id=1, source_target_pairs={{0,2},{1,3},{2,0},{3,1},{4,6},{5,7},{6,4},{7,5},{8,10},{9,11},{10,... | collective-permute-start | bytes 3145736 | tf_op jit(solution)/shard_map/ppermute | solution.py:532
  256.1 37.5 %all-to-all-start.2 = ((bf16[8,2,16,16,128]{4,3,2,1,0:T(8,128)(2,1)}), bf16[8,2,16,16,128]{4,3,2,1,0:T(8,128)(2,1)}, u32[]{:S(2)}, u32[]{:S(2)}) async-start(bf16[8,2,16,16,128]{4,3,2,1,0:T(8,128)(2,1)} %get-tuple-element.56), calls=%async_computation.2 | async-start | bytes 2097152 | tf_op jit(solution)/shard_map/all_to_all | solution.py:581
  260.5 28.3 %collective-permute-start.13 = (bf16[32,16,1024]{2,1,0:T(8,128)(2,1)S(1)}, bf16[32,16,1024]{2,1,0:T(8,128)(2,1)}, u32[]{:S(2)}, u32[]{:S(2)}) collective-permute-start(bf16[32,16,1024]{2,1,0:T(8,128)(2,1)S(1)} %copy-done.4), channel_id=1, source_target_pairs={{0,1},{1,0},{2,3},{3,2},{4,5},{5,4},{6,7},{7,6},{8,9},{9,8},{10,11... | collective-permute-start | bytes 3145736 | tf_op jit(solution)/shard_map/ppermute | solution.py:532
  279.8 9.0 %collective-permute-start.14 = (bf16[32,16,1024]{2,1,0:T(8,128)(2,1)}, bf16[32,16,1024]{2,1,0:T(8,128)(2,1)}, u32[]{:S(2)}, u32[]{:S(2)}) collective-permute-start(bf16[32,16,1024]{2,1,0:T(8,128)(2,1)} %gate.5.refs_1_.refs_13_), channel_id=1, source_target_pairs={{0,1},{1,0},{2,3},{3,2},{4,5},{5,4},{6,7},{7,6},{8,9},{9,8},{10,11... | collective-permute-start | bytes 3145736 | tf_op jit(solution)/shard_map/ppermute | solution.py:532
  287.1 25.8 %collective-permute-start.15 = (bf16[32,16,1024]{2,1,0:T(8,128)(2,1)}, bf16[32,16,1024]{2,1,0:T(8,128)(2,1)S(1)}, u32[]{:S(2)}, u32[]{:S(2)}) collective-permute-start(bf16[32,16,1024]{2,1,0:T(8,128)(2,1)} %get-tuple-element.55.after_ref.refs_0_.refs_8_), channel_id=1, source_target_pairs={{0,2},{1,3},{2,0},{3,1},{4,6},{5,7},{6,4},{7,5},{8,10},{9,11},{10,... | collective-permute-start | bytes 3145736 | tf_op jit(solution)/shard_map/ppermute | solution.py:532
  288.6 27.0 %collective-permute-start.16 = (bf16[32,16,1024]{2,1,0:T(8,128)(2,1)}, bf16[32,16,1024]{2,1,0:T(8,128)(2,1)}, u32[]{:S(2)}, u32[]{:S(2)}) collective-permute-start(bf16[32,16,1024]{2,1,0:T(8,128)(2,1)} %get-tuple-element.55.after_ref.refs_0_.refs_8_), channel_id=1, source_target_pairs={{0,1},{1,0},{2,3},{3,2},{4,5},{5,4},{6,7},{7,6},{8,9},{9,8},{10,11... | collective-permute-start | bytes 3145736 | tf_op jit(solution)/shard_map/ppermute | solution.py:532
  299.3 14.6 %copy-start.5 = (bf16[16,16,1024]{2,1,0:T(8,128)(2,1)S(1)}, bf16[16,16,1024]{2,1,0:T(8,128)(2,1)}, u32[]{:S(2)}) copy-start(bf16[16,16,1024]{2,1,0:T(8,128)(2,1)} %get-tuple-element.58.after_ref.refs_16_) | copy-start | bytes 1572868
  312.8 1.0 copy-start.3
  313.8 2.9 collective-permute-start.17
  313.8 14.3 %collective-permute-start.18 = (bf16[16,16,1024]{2,1,0:T(8,128)(2,1)S(1)}, bf16[16,16,1024]{2,1,0:T(8,128)(2,1)S(1)}, u32[]{:S(2)}, u32[]{:S(2)}) collective-permute-start(bf16[16,16,1024]{2,1,0:T(8,128)(2,1)S(1)} %copy-done.5), channel_id=1, source_target_pairs={{0,2},{1,3},{2,0},{3,1},{4,6},{5,7},{6,4},{7,5},{8,10},{9,11},{10,... | collective-permute-start | bytes 1572872 | tf_op jit(solution)/shard_map/ppermute | solution.py:532
  315.3 14.3 %collective-permute-start.19 = (bf16[16,16,1024]{2,1,0:T(8,128)(2,1)S(1)}, bf16[16,16,1024]{2,1,0:T(8,128)(2,1)S(1)}, u32[]{:S(2)}, u32[]{:S(2)}) collective-permute-start(bf16[16,16,1024]{2,1,0:T(8,128)(2,1)S(1)} %copy-done.5), channel_id=1, source_target_pairs={{0,1},{1,0},{2,3},{3,2},{4,5},{5,4},{6,7},{7,6},{8,9},{9,8},{10,11... | collective-permute-start | bytes 1572872 | tf_op jit(solution)/shard_map/ppermute | solution.py:532
  316.7 1.0 copy-start.6
  328.2 0.8 copy-start.7
  329.0 2.1 collective-permute-start.20
  329.7 1.5 copy-start.8
  331.1 0.8 copy-start.9

commit v12 on v10

--- a/solution.py
+++ b/solution.py
@@ -578,6 +578,9 @@
             halves[chunk] = exchange(sent)
         else:
             sent, state["last"] = first_transform(tables[chunk], grid, strips, state["last"])
+            if chunk == 2:
+                for piece in [edges] + halves[1][1:]:
+                    sent = gate(sent, piece)
             halves[chunk] = lax.all_to_all(sent, "strip", split_axis=0, concat_axis=0, tiled=True)
 
     def base():
@@ -606,7 +609,6 @@
 
     first(0)
     first(1)
-    state["last"] = gate(state["last"], edges)
     first(2)
     base()
     second(1)

time: 347 us -> 301 us (0.87)
  waiting for transfers between devices: 189 us -> 134 us
  starting transfers between devices: 37.4 us -> 47.1 us
    ppermute x1, waiting for transfers between devices: 61.6 us -> 3.16 us  [neighbour_rows(): lax.ppermute(tail.astype(BF16), 'strip', [(i, i + 1) for i in range(ends)])]
    ppermute x1, waiting for transfers between devices: 1.87 us -> 24.3 us  [neighbour_rows(): lax.ppermute(head.astype(BF16), 'strip', [(i + 1, i) for i in range(ends)])]
    ppermute x19, waiting for transfers between devices: 126 us -> 106 us  [swap(): return lax.ppermute(value, axis, [(i, i ^ bits) for i in range(count)])]
    ppermute x19, starting transfers between devices: 16.5 us -> 23.2 us  [swap(): return lax.ppermute(value, axis, [(i, i ^ bits) for i in range(count)])]
    unnamed x36 -> x22, local copies, waits for them, and re-layouts: 8.23 us -> 7.45 us
  transfers between devices with their start and end apart: 24 -> 24, of which waited for: 14 -> 12; matrix products, arithmetic and copies ran while one was open for 2% -> 2% of each run, Pallas kernels for 23% -> 27%
where the time goes in v12:
time: 301 us; the launch traced here: 299 us
  waiting for transfers between devices  134 us (45%)
  Pallas kernels  104 us (35%)
  starting transfers between devices  47.1 us (16%)
  local copies, waits for them, and re-layouts  10.9 us (4%)
    ppermute x19, waiting for transfers between devices, swap(): return lax.ppermute(value, axis, [(i, i ^ bits) for i in range(count)])  106 us
    pallas_call x3, Pallas kernels, first_transform(): pl.pallas_call(first_body, grid=(chans // block,), in_specs=[pl.BlockSpec...  25.3 us
    ppermute x1, waiting for transfers between devices, neighbour_rows(): lax.ppermute(head.astype(BF16), 'strip', [(i + 1, i) for i in range(ends)])  24.3 us
    ppermute x19, starting transfers between devices, swap(): return lax.ppermute(value, axis, [(i, i ^ bits) for i in range(count)])  23.2 us
    pallas_call x3, Pallas kernels, second_transform(): pl.pallas_call(second_body, grid=(side_len // block,), in_specs=[SMEM, pl...  21.9 us
    all_to_all x3, starting transfers between devices, first(): lax.all_to_all(sent, 'strip', split_axis=0, concat_axis=0, tiled=True)  18 us
    pallas_call x3, Pallas kernels, gram_step(): pl.pallas_call(functools.partial(gram_body, len(pieces)), grid=(rows // b...  16.1 us
    pallas_call x1, Pallas kernels, polar_step(): pl.pallas_call(functools.partial(polar_body, starts, sizes, groups), in_s...  13.4 us
  transfers between devices with their start and end apart: 24, of which 12 were waited for; matrix products, arithmetic and copies ran while one was open for 2% of the time, Pallas kernels for 27%

profile of v12, /device:TPU:12, one launch (start us, length us, event | category | flops | bytes accessed | tf_op | source)
XLA Modules:
  0.0 298.7 jit_solution(11250219225518482888)
XLA Ops:
  0.0 10.3 %first_transform.3 = (bf16[8,2,16,48,128]{4,3,2,1,0:T(8,128)(2,1)}, f32[8,128]{1,0:T(8,128)}) custom-call(bf16[768,1024]{1,0:T(8,128)(2,1)} %constant.20.clone.table_ref, bf16[2,16,128,1024]{3,2,1,0:T(8,128)(2,1)} %grid_ref.7, s32[1]{0:T(128)} %bitcast.after_ref.strip_ref), custom_call_target="tpu_custom_call" | custom-call | bytes 65536 | tf_op jit(solution)/shard_map/first_transform/pallas_call | solution.py:110
  10.3 6.2 %all-to-all-start = ((bf16[8,2,16,48,128]{4,3,2,1,0:T(8,128)(2,1)}), bf16[8,2,16,48,128]{4,3,2,1,0:T(8,128)(2,1)S(1)}, u32[]{:S(2)}, u32[]{:S(2)}) async-start(bf16[8,2,16,48,128]{4,3,2,1,0:T(8,128)(2,1)} %get-tuple-element.34), calls=%async_computation | async-start | bytes 6291456 | tf_op jit(solution)/shard_map/all_to_all | solution.py:584
  16.5 2.8 fusion
  19.3 3.4 %collective-permute-start = (bf16[16,12,1024]{2,1,0:T(8,128)(2,1)}, bf16[16,12,1024]{2,1,0:T(8,128)(2,1)S(1)}, u32[]{:S(2)}, u32[]{:S(2)}) collective-permute-start(bf16[16,12,1024]{2,1,0:T(8,128)(2,1)} %get-tuple-element.35), channel_id=1, source_target_pairs={{0,4},{4,8},{8,12},{12,16},{16,20},{20,24},{24,28},{1,5},{5,9},{9,... | collective-permute-start | bytes 1179656 | tf_op jit(solution)/shard_map/ppermute | solution.py:525
  22.7 2.5 collective-permute-start.1
  25.1 8.5 %first_pieces.1 = (bf16[2,16,32,128]{3,2,1,0:T(8,128)(2,1)}, bf16[2,16,32,128]{3,2,1,0:T(8,128)(2,1)}, bf16[2,16,32,128]{3,2,1,0:T(8,128)(2,1)}, bf16[2,16,32,12...) custom-call(s32[1]{0:T(128)} %bitcast.after_ref.strip_ref, ...), custom_call_target="tpu_custom_call" | custom-call | bytes 65536 | tf_op jit(solution)/shard_map/first_pieces/pallas_call | solution.py:164
  33.7 1.5 collective-permute-start.2
  35.2 2.0 collective-permute-start.4
  37.2 30.8 %collective-permute-done.2.refs_1_.after_ref = bf16[2,16,32,128]{3,2,1,0:T(8,128)(2,1)S(1)} collective-permute-done((bf16[2,16,32,128]{3,2,1,0:T(8,128)(2,1)}, bf16[2,16,32,128]{3,2,1,0:T(8,128)(2,1)S(1)}, u32[]{:S(2)}, u32[]{:S(2)}) %collective-permute-start.2) | collective-permute-done | bytes 262176 | tf_op jit(solution)/shard_map/ppermute | solution.py:532
  68.0 14.2 %collective-permute-start.5 = (bf16[2,16,32,128]{3,2,1,0:T(8,128)(2,1)}, bf16[2,16,32,128]{3,2,1,0:T(8,128)(2,1)}, u32[]{:S(2)}, u32[]{:S(2)}) collective-permute-start(bf16[2,16,32,128]{3,2,1,0:T(8,128)(2,1)} %get-tuple-element.46), channel_id=1, source_target_pairs={{0,16},{4,20},{8,24},{12,28},{16,0},{20,4},{24,8},{28,12},{1,17},{... | collective-permute-start | bytes 786440 | tf_op jit(solution)/shard_map/ppermute | solution.py:532
  82.2 11.4 %collective-permute-done.3.refs_2_.after_ref = bf16[2,16,32,128]{3,2,1,0:T(8,128)(2,1)} collective-permute-done((bf16[2,16,32,128]{3,2,1,0:T(8,128)(2,1)}, bf16[2,16,32,128]{3,2,1,0:T(8,128)(2,1)}, u32[]{:S(2)}, u32[]{:S(2)}) %collective-permute-start.3) | collective-permute-done | bytes 262176 | tf_op jit(solution)/shard_map/ppermute | solution.py:532
  93.6 3.2 %collective-permute-done = bf16[16,12,1024]{2,1,0:T(8,128)(2,1)S(1)} collective-permute-done((bf16[16,12,1024]{2,1,0:T(8,128)(2,1)}, bf16[16,12,1024]{2,1,0:T(8,128)(2,1)S(1)}, u32[]{:S(2)}, u32[]{:S(2)}) %collective-permute-start) | collective-permute-done | bytes 393248 | tf_op jit(solution)/shard_map/ppermute | solution.py:525
  96.8 24.3 %collective-permute-done.1 = bf16[16,12,1024]{2,1,0:T(8,128)(2,1)} collective-permute-done((bf16[16,12,1024]{2,1,0:T(8,128)(2,1)}, bf16[16,12,1024]{2,1,0:T(8,128)(2,1)}, u32[]{:S(2)}, u32[]{:S(2)}) %collective-permute-start.1) | collective-permute-done | bytes 393248 | tf_op jit(solution)/shard_map/ppermute | solution.py:526
  121.1 8.5 %first_transform.4 = (bf16[8,2,16,32,128]{4,3,2,1,0:T(8,128)(2,1)}, f32[8,128]{1,0:T(8,128)}) custom-call(bf16[512,1024]{1,0:T(8,128)(2,1)} %constant.22.clone.table_ref, bf16[2,16,128,1024]{3,2,1,0:T(8,128)(2,1)} %grid_ref.7, f32[8,128]{1,0:T(8,128)} %get-tuple-element.38.after_ref), custom_call_target="tpu_custom_call" | custom-call | bytes 65536 | tf_op jit(solution)/shard_map/first_transform/pallas_call | solution.py:110
  129.6 2.1 pad_maximum_fusion.edge_ref.after_ref
  131.8 4.3 %collective-permute-done.7.refs_6_.after_ref = bf16[2,16,32,128]{3,2,1,0:T(8,128)(2,1)} collective-permute-done((bf16[2,16,32,128]{3,2,1,0:T(8,128)(2,1)}, bf16[2,16,32,128]{3,2,1,0:T(8,128)(2,1)}, u32[]{:S(2)}, u32[]{:S(2)}) %collective-permute-start.7) | collective-permute-done | bytes 262176 | tf_op jit(solution)/shard_map/ppermute | solution.py:532
  136.1 6.0 %collective-permute-done.8.refs_7_.after_ref = bf16[2,16,32,128]{3,2,1,0:T(8,128)(2,1)} collective-permute-done((bf16[2,16,32,128]{3,2,1,0:T(8,128)(2,1)}, bf16[2,16,32,128]{3,2,1,0:T(8,128)(2,1)}, u32[]{:S(2)}, u32[]{:S(2)}) %collective-permute-start.8) | collective-permute-done | bytes 262176 | tf_op jit(solution)/shard_map/ppermute | solution.py:532
  142.1 1.7 copy-done.2
  143.8 5.6 %all-to-all-start.1 = ((bf16[8,2,16,32,128]{4,3,2,1,0:T(8,128)(2,1)}), bf16[8,2,16,32,128]{4,3,2,1,0:T(8,128)(2,1)}, u32[]{:S(2)}, u32[]{:S(2)}) async-start(bf16[8,2,16,32,128]{4,3,2,1,0:T(8,128)(2,1)} %gate.20), calls=%async_computation.1 | async-start | bytes 4194304 | tf_op jit(solution)/shard_map/all_to_all | solution.py:584
  149.4 11.2 %base_step.1 = (f32[16,48,1024]{2,1,0:T(8,128)}, f32[16,32,1024]{2,1,0:T(8,128)}, f32[16,32,1024]{2,1,0:T(8,128)}, f32[16,16,1024]{2,1,0:T(8,128)}) custom-call(s32[1]{0:T(128)} %bitcast.after_ref.strip_ref, f32[16]{0:T(128)} %step_ref.9, f32[3,4]{1,0:T(4,128)} %highpass_ref.1, f32[16,128,1024]{2,1,0:T(8,128)} %model_ref.1, ...), custom_call_target="tpu_custom_call" | custom-call | bytes 65536 | tf_op jit(solution)/shard_map/base_step/pallas_call | solution.py:246
  160.6 7.2 %second_pieces.1 = (f32[16,32,1024]{2,1,0:T(8,128)}, bf16[32,16,1024]{2,1,0:T(8,128)(2,1)}) custom-call(s32[1]{0:T(128)} %bitcast.after_ref.strip_ref, f32[16]{0:T(128)} %step_ref.9, bf16[1024,1024]{1,0:T(8,128)(2,1)} %constant.23.clone.cosine_ref, bf16[1024,1024]{1,0:T(8,128)(2,1)} %constant.24.clone.sine_ref, f32[16,32,1024]{2,1,0:T(8,128)} %get-tuple-element.41.base_ref, ...), custom_call_target="tpu_custom_call" | custom-call | bytes 65536 | tf_op jit(solution)/shard_map/second_pieces/pallas_call | solution.py:350
  167.8 1.5 collective-permute-start.9
  169.3 9.0 %second_transform.3 = (f32[16,48,1024]{2,1,0:T(8,128)}, bf16[48,16,1024]{2,1,0:T(8,128)(2,1)}) custom-call(f32[16]{0:T(128)} %step_ref.9, bf16[8,2,16,48,128]{4,3,2,1,0:T(8,128)(2,1)} %copy-done.2, bf16[1024,1024]{1,0:T(8,128)(2,1)} %constant.23.clone.cosine_ref, bf16[1024,1024]{1,0:T(8,128)(2,1)} %constant.24.clone.sine_ref, ...), custom_call_target="tpu_custom_call" | custom-call | bytes 65536 | tf_op jit(solution)/shard_map/second_transform/pallas_call | solution.py:289
  178.3 0.5 collective-permute-start.12
  178.9 15.3 %collective-permute-done.9.value_ref = bf16[32,16,1024]{2,1,0:T(8,128)(2,1)S(1)} collective-permute-done((bf16[32,16,1024]{2,1,0:T(8,128)(2,1)}, bf16[32,16,1024]{2,1,0:T(8,128)(2,1)S(1)}, u32[]{:S(2)}, u32[]{:S(2)}) %collective-permute-start.9) | collective-permute-done | bytes 1048608 | tf_op jit(solution)/shard_map/ppermute | solution.py:532
  194.2 1.1 copy-done.4
  195.2 6.5 %first_transform.5 = (bf16[8,2,16,16,128]{4,3,2,1,0:T(8,128)(2,1)}, f32[8,128]{1,0:T(8,128)}) custom-call(bf16[256,1024]{1,0:T(8,128)(2,1)} %constant.25.clone.table_ref, bf16[2,16,128,1024]{3,2,1,0:T(8,128)(2,1)} %grid_ref.7, bf16[48,16,1024]{2,1,0:T(8,128)(2,1)} %get-tuple-element.51.after_ref.refs_0_.refs_4_), custom_call_target="tpu_custom_call" | custom-call | bytes 65536 | tf_op jit(solution)/shard_map/first_transform/pallas_call | solution.py:110
  201.7 6.1 %all-to-all-start.2 = ((bf16[8,2,16,16,128]{4,3,2,1,0:T(8,128)(2,1)}), bf16[8,2,16,16,128]{4,3,2,1,0:T(8,128)(2,1)}, u32[]{:S(2)}, u32[]{:S(2)}) async-start(bf16[8,2,16,16,128]{4,3,2,1,0:T(8,128)(2,1)} %get-tuple-element.56), calls=%async_computation.2 | async-start | bytes 2097152 | tf_op jit(solution)/shard_map/all_to_all | solution.py:584
  207.9 18.4 %collective-permute-done.12.value_ref = bf16[48,16,1024]{2,1,0:T(8,128)(2,1)S(1)} collective-permute-done((bf16[48,16,1024]{2,1,0:T(8,128)(2,1)}, bf16[48,16,1024]{2,1,0:T(8,128)(2,1)S(1)}, u32[]{:S(2)}, u32[]{:S(2)}) %collective-permute-start.12) | collective-permute-done | bytes 1572896 | tf_op jit(solution)/shard_map/ppermute | solution.py:532
  226.3 1.1 copy-done.1
  227.4 0.7 broadcast_in_dim.3.before_ref
  228.2 4.8 %gram_step.3.after_ref.before_ref = f32[256,256]{1,0:T(8,128)} custom-call(f32[256,256]{1,0:T(8,128)} %broadcast_in_dim.3.before_ref, f32[8,128]{1,0:T(8,128)} %get-tuple-element.52.after_ref, bf16[32,16,1024]{2,1,0:T(8,128)(2,1)} %get-tuple-element.50.after_ref.refs_0_.refs_8_, bf16[32,16,1024]{2,1,0:T(8,128)(2,1)} %gate.12.refs_1_.refs_9_, ...), custom_call_target="tpu_custom_call" | custom-call | bytes 65536 | tf_op jit(solution)/shard_map/gram_step/pallas_call | solution.py:398
  233.0 7.3 %second_transform.4 = (f32[16,32,1024]{2,1,0:T(8,128)}, bf16[32,16,1024]{2,1,0:T(8,128)(2,1)}) custom-call(f32[16]{0:T(128)} %step_ref.9, bf16[8,2,16,32,128]{4,3,2,1,0:T(8,128)(2,1)} %all-to-all-done.1.half_ref, bf16[1024,1024]{1,0:T(8,128)(2,1)} %constant.23.clone.cosine_ref, bf16[1024,1024]{1,0:T(8,128)(2,1)} %constant.24.clone.sine_ref, ...), custom_call_target="tpu_custom_call" | custom-call | bytes 65536 | tf_op jit(solution)/shard_map/second_transform/pallas_call | solution.py:289
  240.3 1.5 collective-permute-start.15
  242.0 6.6 %gram_step.4.after_ref.before_ref = f32[256,256]{1,0:T(8,128)} custom-call(f32[256,256]{1,0:T(8,128)} %gram_step.3.after_ref.before_ref, bf16[32,16,1024]{2,1,0:T(8,128)(2,1)} %get-tuple-element.55.after_ref.refs_0_.refs_12_, bf16[48,16,1024]{2,1,0:T(8,128)(2,1)} %get-tuple-element.51.after_ref.refs_0_.refs_4_, bf16[48,16,1024]{2,1,0:T(8,128)(2,1)} %gate.21.refs_1_.refs_5_, ...), custom_call_target="tpu_custom_call" | custom-call | bytes 65536 | tf_op jit(solution)/shard_map/gram_step/pallas_call | solution.py:398
  248.6 5.6 %second_transform.5 = (f32[16,16,1024]{2,1,0:T(8,128)}, bf16[16,16,1024]{2,1,0:T(8,128)(2,1)}) custom-call(f32[16]{0:T(128)} %step_ref.9, bf16[8,2,16,16,128]{4,3,2,1,0:T(8,128)(2,1)} %all-to-all-done.2.half_ref, bf16[1024,1024]{1,0:T(8,128)(2,1)} %constant.23.clone.cosine_ref, bf16[1024,1024]{1,0:T(8,128)(2,1)} %constant.24.clone.sine_ref, ...), custom_call_target="tpu_custom_call" | custom-call | bytes 65536 | tf_op jit(solution)/shard_map/second_transform/pallas_call | solution.py:289
  254.2 11.9 %collective-permute-done.15.value_ref = bf16[32,16,1024]{2,1,0:T(8,128)(2,1)S(1)} collective-permute-done((bf16[32,16,1024]{2,1,0:T(8,128)(2,1)}, bf16[32,16,1024]{2,1,0:T(8,128)(2,1)S(1)}, u32[]{:S(2)}, u32[]{:S(2)}) %collective-permute-start.15) | collective-permute-done | bytes 1048608 | tf_op jit(solution)/shard_map/ppermute | solution.py:532
  266.1 1.0 copy-done.3
  267.1 1.5 collective-permute-start.18
  268.6 0.2 collective-permute-start.19
  268.8 1.1 collective-permute-done.17.refs_3_.refs_15_
  269.9 1.0 copy-done.6
  270.9 4.8 %gram_step.5.after_ref.gram_ref = f32[256,256]{1,0:T(8,128)} custom-call(f32[256,256]{1,0:T(8,128)} %gram_step.4.after_ref.before_ref, bf16[16,16,1024]{2,1,0:T(8,128)(2,1)} %get-tuple-element.58.after_ref.refs_16_, bf16[32,16,1024]{2,1,0:T(8,128)(2,1)} %get-tuple-element.55.after_ref.refs_0_.refs_12_, bf16[32,16,1024]{2,1,0:T(8,128)(2,1)} %gate.22.refs_1_.refs_13_, ...), custom_call_target="tpu_custom_call" | custom-call | bytes 65536 | tf_op jit(solution)/shard_map/gram_step/pallas_call | solution.py:398
  275.7 5.7 %collective-permute-done.18.value_ref = bf16[16,16,1024]{2,1,0:T(8,128)(2,1)S(1)} collective-permute-done((bf16[16,16,1024]{2,1,0:T(8,128)(2,1)S(1)}, bf16[16,16,1024]{2,1,0:T(8,128)(2,1)S(1)}, u32[]{:S(2)}, u32[]{:S(2)}) %collective-permute-start.18) | collective-permute-done | bytes 524320 | tf_op jit(solution)/shard_map/ppermute | solution.py:532
  281.4 0.8 copy-done.7
  282.9 1.4 collective-permute-done.20.refs_19_
  284.3 0.8 copy-done.10
  285.1 13.4 %polar_step.1 = f32[16,128,1024]{2,1,0:T(8,128)} custom-call(f32[1]{0:T(128)S(6)} %copy.36.shrink_ref, f32[256,256]{1,0:T(8,128)} %gram_step.5.after_ref.gram_ref, f32[16,48,1024]{2,1,0:T(8,128)} %get-tuple-element.59.refs_0_, f32[16,32,1024]{2,1,0:T(8,128)} %get-tuple-element.60.refs_1_, f32[16,32,1024]{2,1,0:T(8,128)} %get-tuple-element.61.refs_2_, ...), custom_call_target="tpu_custom_call" | custom-call | bytes 65536 | tf_op jit(solution)/shard_map/polar_step/pallas_call | solution.py:504
  (50 shorter events, 0.3 us)
Async XLA Ops:
  10.3 131.8 %all-to-all-start = ((bf16[8,2,16,48,128]{4,3,2,1,0:T(8,128)(2,1)}), bf16[8,2,16,48,128]{4,3,2,1,0:T(8,128)(2,1)S(1)}, u32[]{:S(2)}, u32[]{:S(2)}) async-start(bf16[8,2,16,48,128]{4,3,2,1,0:T(8,128)(2,1)} %get-tuple-element.34), calls=%async_computation | async-start | bytes 6291456 | tf_op jit(solution)/shard_map/all_to_all | solution.py:584
  19.3 77.5 %collective-permute-start = (bf16[16,12,1024]{2,1,0:T(8,128)(2,1)}, bf16[16,12,1024]{2,1,0:T(8,128)(2,1)S(1)}, u32[]{:S(2)}, u32[]{:S(2)}) collective-permute-start(bf16[16,12,1024]{2,1,0:T(8,128)(2,1)} %get-tuple-element.35), channel_id=1, source_target_pairs={{0,4},{4,8},{8,12},{12,16},{16,20},{20,24},{24,28},{1,5},{5,9},{9,... | collective-permute-start | bytes 1179656 | tf_op jit(solution)/shard_map/ppermute | solution.py:525
  22.7 98.4 %collective-permute-start.1 = (bf16[16,12,1024]{2,1,0:T(8,128)(2,1)}, bf16[16,12,1024]{2,1,0:T(8,128)(2,1)}, u32[]{:S(2)}, u32[]{:S(2)}) collective-permute-start(bf16[16,12,1024]{2,1,0:T(8,128)(2,1)} %get-tuple-element.36), channel_id=1, source_target_pairs={{4,0},{8,4},{12,8},{16,12},{20,16},{24,20},{28,24},{5,1},{9,5},{13... | collective-permute-start | bytes 1179656 | tf_op jit(solution)/shard_map/ppermute | solution.py:526
  33.7 34.3 %collective-permute-start.2 = (bf16[2,16,32,128]{3,2,1,0:T(8,128)(2,1)}, bf16[2,16,32,128]{3,2,1,0:T(8,128)(2,1)S(1)}, u32[]{:S(2)}, u32[]{:S(2)}) collective-permute-start(bf16[2,16,32,128]{3,2,1,0:T(8,128)(2,1)} %get-tuple-element.43), channel_id=1, source_target_pairs={{0,4},{4,0},{8,12},{12,8},{16,20},{20,16},{24,28},{28,24},{1,5},{5... | collective-permute-start | bytes 786440 | tf_op jit(solution)/shard_map/ppermute | solution.py:532
  35.2 58.4 %collective-permute-start.3 = (bf16[2,16,32,128]{3,2,1,0:T(8,128)(2,1)}, bf16[2,16,32,128]{3,2,1,0:T(8,128)(2,1)}, u32[]{:S(2)}, u32[]{:S(2)}) collective-permute-start(bf16[2,16,32,128]{3,2,1,0:T(8,128)(2,1)} %get-tuple-element.44), channel_id=1, source_target_pairs={{0,8},{4,12},{8,0},{12,4},{16,24},{20,28},{24,16},{28,20},{1,9},{5... | collective-permute-start | bytes 786440 | tf_op jit(solution)/shard_map/ppermute | solution.py:532
  35.2 96.5 %collective-permute-start.4 = (bf16[2,16,32,128]{3,2,1,0:T(8,128)(2,1)}, bf16[2,16,32,128]{3,2,1,0:T(8,128)(2,1)}, u32[]{:S(2)}, u32[]{:S(2)}) collective-permute-start(bf16[2,16,32,128]{3,2,1,0:T(8,128)(2,1)} %get-tuple-element.45), channel_id=1, source_target_pairs={{0,12},{4,8},{8,4},{12,0},{16,28},{20,24},{24,20},{28,16},{1,13},{... | collective-permute-start | bytes 786440 | tf_op jit(solution)/shard_map/ppermute | solution.py:532
  68.0 61.6 %copy-start.8 = (bf16[2,16,32,128]{3,2,1,0:T(8,128)(2,1)}, bf16[2,16,32,128]{3,2,1,0:T(8,128)(2,1)S(1)}, u32[]{:S(2)}) copy-start(bf16[2,16,32,128]{3,2,1,0:T(8,128)(2,1)S(1)} %collective-permute-done.2.refs_1_.after_ref) | copy-start | bytes 786436
  68.0 63.7 %collective-permute-start.5 = (bf16[2,16,32,128]{3,2,1,0:T(8,128)(2,1)}, bf16[2,16,32,128]{3,2,1,0:T(8,128)(2,1)}, u32[]{:S(2)}, u32[]{:S(2)}) collective-permute-start(bf16[2,16,32,128]{3,2,1,0:T(8,128)(2,1)} %get-tuple-element.46), channel_id=1, source_target_pairs={{0,16},{4,20},{8,24},{12,28},{16,0},{20,4},{24,8},{28,12},{1,17},{... | collective-permute-start | bytes 786440 | tf_op jit(solution)/shard_map/ppermute | solution.py:532
  93.6 38.1 %collective-permute-start.6 = (bf16[2,16,32,128]{3,2,1,0:T(8,128)(2,1)}, bf16[2,16,32,128]{3,2,1,0:T(8,128)(2,1)}, u32[]{:S(2)}, u32[]{:S(2)}) collective-permute-start(bf16[2,16,32,128]{3,2,1,0:T(8,128)(2,1)} %get-tuple-element.47), channel_id=1, source_target_pairs={{0,20},{4,16},{8,28},{12,24},{16,4},{20,0},{24,12},{28,8},{1,21},{... | collective-permute-start | bytes 786440 | tf_op jit(solution)/shard_map/ppermute | solution.py:532
  96.8 39.3 %collective-permute-start.7 = (bf16[2,16,32,128]{3,2,1,0:T(8,128)(2,1)}, bf16[2,16,32,128]{3,2,1,0:T(8,128)(2,1)}, u32[]{:S(2)}, u32[]{:S(2)}) collective-permute-start(bf16[2,16,32,128]{3,2,1,0:T(8,128)(2,1)} %get-tuple-element.48), channel_id=1, source_target_pairs={{0,24},{4,28},{8,16},{12,20},{16,8},{20,12},{24,0},{28,4},{1,25},{... | collective-permute-start | bytes 786440 | tf_op jit(solution)/shard_map/ppermute | solution.py:532
  121.1 21.0 %collective-permute-start.8 = (bf16[2,16,32,128]{3,2,1,0:T(8,128)(2,1)}, bf16[2,16,32,128]{3,2,1,0:T(8,128)(2,1)}, u32[]{:S(2)}, u32[]{:S(2)}) collective-permute-start(bf16[2,16,32,128]{3,2,1,0:T(8,128)(2,1)} %get-tuple-element.49), channel_id=1, source_target_pairs={{0,28},{4,24},{8,20},{12,16},{16,12},{20,8},{24,4},{28,0},{1,29},{... | collective-permute-start | bytes 786440 | tf_op jit(solution)/shard_map/ppermute | solution.py:532
  142.1 1.7 copy-start.2
  143.8 57.9 %all-to-all-start.1 = ((bf16[8,2,16,32,128]{4,3,2,1,0:T(8,128)(2,1)}), bf16[8,2,16,32,128]{4,3,2,1,0:T(8,128)(2,1)}, u32[]{:S(2)}, u32[]{:S(2)}) async-start(bf16[8,2,16,32,128]{4,3,2,1,0:T(8,128)(2,1)} %gate.20), calls=%async_computation.1 | async-start | bytes 4194304 | tf_op jit(solution)/shard_map/all_to_all | solution.py:584
  167.8 26.3 %collective-permute-start.9 = (bf16[32,16,1024]{2,1,0:T(8,128)(2,1)}, bf16[32,16,1024]{2,1,0:T(8,128)(2,1)S(1)}, u32[]{:S(2)}, u32[]{:S(2)}) collective-permute-start(bf16[32,16,1024]{2,1,0:T(8,128)(2,1)} %get-tuple-element.50.after_ref.refs_0_.refs_8_), channel_id=1, source_target_pairs={{0,2},{1,3},{2,0},{3,1},{4,6},{5,7},{6,4},{7,5},{8,10},{9,11},{10,... | collective-permute-start | bytes 3145736 | tf_op jit(solution)/shard_map/ppermute | solution.py:532
  178.3 48.0 %collective-permute-start.12 = (bf16[48,16,1024]{2,1,0:T(8,128)(2,1)}, bf16[48,16,1024]{2,1,0:T(8,128)(2,1)S(1)}, u32[]{:S(2)}, u32[]{:S(2)}) collective-permute-start(bf16[48,16,1024]{2,1,0:T(8,128)(2,1)} %get-tuple-element.51.after_ref.refs_0_.refs_4_), channel_id=1, source_target_pairs={{0,2},{1,3},{2,0},{3,1},{4,6},{5,7},{6,4},{7,5},{8,10},{9,11},{10,... | collective-permute-start | bytes 4718600 | tf_op jit(solution)/shard_map/ppermute | solution.py:532
  178.9 48.6 %collective-permute-start.10 = (bf16[32,16,1024]{2,1,0:T(8,128)(2,1)}, bf16[32,16,1024]{2,1,0:T(8,128)(2,1)}, u32[]{:S(2)}, u32[]{:S(2)}) collective-permute-start(bf16[32,16,1024]{2,1,0:T(8,128)(2,1)} %get-tuple-element.50.after_ref.refs_0_.refs_8_), channel_id=1, source_target_pairs={{0,1},{1,0},{2,3},{3,2},{4,5},{5,4},{6,7},{7,6},{8,9},{9,8},{10,11... | collective-permute-start | bytes 3145736 | tf_op jit(solution)/shard_map/ppermute | solution.py:532
  194.2 1.1 copy-start.4
  195.2 32.2 %collective-permute-start.11 = (bf16[32,16,1024]{2,1,0:T(8,128)(2,1)}, bf16[32,16,1024]{2,1,0:T(8,128)(2,1)}, u32[]{:S(2)}, u32[]{:S(2)}) collective-permute-start(bf16[32,16,1024]{2,1,0:T(8,128)(2,1)} %gate.12.refs_1_.refs_9_), channel_id=1, source_target_pairs={{0,1},{1,0},{2,3},{3,2},{4,5},{5,4},{6,7},{7,6},{8,9},{9,8},{10,11... | collective-permute-start | bytes 3145736 | tf_op jit(solution)/shard_map/ppermute | solution.py:532
  201.7 6.1 %copy-start = (bf16[48,16,1024]{2,1,0:T(8,128)(2,1)S(1)}, bf16[48,16,1024]{2,1,0:T(8,128)(2,1)}, u32[]{:S(2)}) copy-start(bf16[48,16,1024]{2,1,0:T(8,128)(2,1)} %get-tuple-element.51.after_ref.refs_0_.refs_4_) | copy-start | bytes 4718596
  201.7 46.8 %all-to-all-start.2 = ((bf16[8,2,16,16,128]{4,3,2,1,0:T(8,128)(2,1)}), bf16[8,2,16,16,128]{4,3,2,1,0:T(8,128)(2,1)}, u32[]{:S(2)}, u32[]{:S(2)}) async-start(bf16[8,2,16,16,128]{4,3,2,1,0:T(8,128)(2,1)} %get-tuple-element.56), calls=%async_computation.2 | async-start | bytes 2097152 | tf_op jit(solution)/shard_map/all_to_all | solution.py:584
  207.9 34.1 %collective-permute-start.13 = (bf16[48,16,1024]{2,1,0:T(8,128)(2,1)S(1)}, bf16[48,16,1024]{2,1,0:T(8,128)(2,1)}, u32[]{:S(2)}, u32[]{:S(2)}) collective-permute-start(bf16[48,16,1024]{2,1,0:T(8,128)(2,1)S(1)} %copy-done), channel_id=1, source_target_pairs={{0,1},{1,0},{2,3},{3,2},{4,5},{5,4},{6,7},{7,6},{8,9},{9,8},{10,11... | collective-permute-start | bytes 4718600 | tf_op jit(solution)/shard_map/ppermute | solution.py:532
  226.3 1.1 copy-start.1
  227.4 14.6 %collective-permute-start.14 = (bf16[48,16,1024]{2,1,0:T(8,128)(2,1)}, bf16[48,16,1024]{2,1,0:T(8,128)(2,1)}, u32[]{:S(2)}, u32[]{:S(2)}) collective-permute-start(bf16[48,16,1024]{2,1,0:T(8,128)(2,1)} %gate.21.refs_1_.refs_5_), channel_id=1, source_target_pairs={{0,1},{1,0},{2,3},{3,2},{4,5},{5,4},{6,7},{7,6},{8,9},{9,8},{10,11... | collective-permute-start | bytes 4718600 | tf_op jit(solution)/shard_map/ppermute | solution.py:532
  240.3 25.8 %collective-permute-start.15 = (bf16[32,16,1024]{2,1,0:T(8,128)(2,1)}, bf16[32,16,1024]{2,1,0:T(8,128)(2,1)S(1)}, u32[]{:S(2)}, u32[]{:S(2)}) collective-permute-start(bf16[32,16,1024]{2,1,0:T(8,128)(2,1)} %get-tuple-element.55.after_ref.refs_0_.refs_12_), channel_id=1, source_target_pairs={{0,2},{1,3},{2,0},{3,1},{4,6},{5,7},{6,4},{7,5},{8,10},{9,11},{10,... | collective-permute-start | bytes 3145736 | tf_op jit(solution)/shard_map/ppermute | solution.py:532
  241.8 27.0 %collective-permute-start.16 = (bf16[32,16,1024]{2,1,0:T(8,128)(2,1)}, bf16[32,16,1024]{2,1,0:T(8,128)(2,1)}, u32[]{:S(2)}, u32[]{:S(2)}) collective-permute-start(bf16[32,16,1024]{2,1,0:T(8,128)(2,1)} %get-tuple-element.55.after_ref.refs_0_.refs_12_), channel_id=1, source_target_pairs={{0,1},{1,0},{2,3},{3,2},{4,5},{5,4},{6,7},{7,6},{8,9},{9,8},{10,11... | collective-permute-start | bytes 3145736 | tf_op jit(solution)/shard_map/ppermute | solution.py:532
  254.2 12.9 %copy-start.5 = (bf16[16,16,1024]{2,1,0:T(8,128)(2,1)S(1)}, bf16[16,16,1024]{2,1,0:T(8,128)(2,1)}, u32[]{:S(2)}) copy-start(bf16[16,16,1024]{2,1,0:T(8,128)(2,1)} %get-tuple-element.58.after_ref.refs_16_) | copy-start | bytes 1572868
  266.1 1.0 copy-start.3
  267.1 2.9 collective-permute-start.17
  267.1 14.3 %collective-permute-start.18 = (bf16[16,16,1024]{2,1,0:T(8,128)(2,1)S(1)}, bf16[16,16,1024]{2,1,0:T(8,128)(2,1)S(1)}, u32[]{:S(2)}, u32[]{:S(2)}) collective-permute-start(bf16[16,16,1024]{2,1,0:T(8,128)(2,1)S(1)} %copy-done.5), channel_id=1, source_target_pairs={{0,2},{1,3},{2,0},{3,1},{4,6},{5,7},{6,4},{7,5},{8,10},{9,11},{10,... | collective-permute-start | bytes 1572872 | tf_op jit(solution)/shard_map/ppermute | solution.py:532
  268.6 14.3 %collective-permute-start.19 = (bf16[16,16,1024]{2,1,0:T(8,128)(2,1)S(1)}, bf16[16,16,1024]{2,1,0:T(8,128)(2,1)S(1)}, u32[]{:S(2)}, u32[]{:S(2)}) collective-permute-start(bf16[16,16,1024]{2,1,0:T(8,128)(2,1)S(1)} %copy-done.5), channel_id=1, source_target_pairs={{0,1},{1,0},{2,3},{3,2},{4,5},{5,4},{6,7},{7,6},{8,9},{9,8},{10,11... | collective-permute-start | bytes 1572872 | tf_op jit(solution)/shard_map/ppermute | solution.py:532
  269.9 1.0 copy-start.6
  281.4 0.8 copy-start.7
  282.2 2.1 collective-permute-start.20
  282.9 1.5 copy-start.9
  284.3 0.8 copy-start.10

commit v13 on v8

--- a/solution.py
+++ b/solution.py
@@ -74,6 +74,7 @@
         out_specs=ANY,
         out_shape=jax.ShapeDtypeStruct(value.shape, value.dtype),
         input_output_aliases={0: 0},
+        compiler_params=kernel_params(63),
         cost_estimate=COST,
         name="gate",
     )(value, after)
@@ -107,7 +108,7 @@
         total = total + jnp.einsum("mv,cuv->mcu", turned, grid[1], preferred_element_type=F32)
         total = total.astype(BF16).reshape(2, strips, rows, chans, width)
         return total.transpose(1, 0, 3, 2, 4), jnp.zeros((8, 128), F32)
-    block = 4 if chans % 4 == 0 else 1
+    block = 2 if chans % 2 == 0 else 1
     return pl.pallas_call(
         first_body,
         grid=(chans // block,),
@@ -121,7 +122,7 @@
             pl.BlockSpec((8, 128), lambda i: (0, 0)),
         ],
         out_shape=[jax.ShapeDtypeStruct(shape, BF16), jax.ShapeDtypeStruct((8, 128), F32)],
-        compiler_params=kernel_params(60),
+        compiler_params=kernel_params(63),
         cost_estimate=COST,
         name="first_transform",
     )(table, grid, after)
@@ -203,7 +204,7 @@
         out_specs=[pl.BlockSpec((block, part, side_len), lambda i: (i, 0, 0)) for part in sizes],
         out_shape=[jax.ShapeDtypeStruct((chans, part, side_len), F32) for part in sizes],
         scratch_shapes=[pltpu.VMEM((rows, wide), BF16), pltpu.VMEM((rows, wide), BF16)],
-        compiler_params=kernel_params(60),
+        compiler_params=kernel_params(63),
         cost_estimate=COST,
         name="base_step",
     )(strip, step_size, highpass, model_image, edges, after)
@@ -251,7 +252,7 @@
             jax.ShapeDtypeStruct(base.shape, F32),
             jax.ShapeDtypeStruct((rows, chans, side_len), BF16),
         ],
-        compiler_params=kernel_params(60),
+        compiler_params=kernel_params(63),
         cost_estimate=COST,
         name="second_transform",
     )(step_size, half, cosine, sine_table, base, after)
@@ -285,7 +286,7 @@
         in_specs=[pl.BlockSpec(before.shape, lambda i: (0, 0)), ANY] + [spec] * len(pieces),
         out_specs=pl.BlockSpec(before.shape, lambda i: (0, 0)),
         out_shape=jax.ShapeDtypeStruct(before.shape, F32),
-        compiler_params=kernel_params(60),
+        compiler_params=kernel_params(63),
         cost_estimate=COST,
         name="gram_step",
     )(before, after, *pieces)
@@ -317,6 +318,7 @@
     blocks = [
         (chunk, row) for chunk in [chunks - 1] + list(range(chunks - 1)) for row in range(0, sizes[chunk], EDGE_ROWS)
     ]
+    far = 1 if groups > 1 else 0
     pixel_copies = []
     moved_copies = []
     for place, (chunk, row) in enumerate(blocks):
@@ -326,7 +328,7 @@
             pltpu.make_async_copy(
                 pixels_hbm[chunk * groups + group].at[part], pixels[chunk].at[group, part], pixel_sems.at[place, group]
             )
-            for group in range(groups)
+            for group in range(0 if chunk == chunks - 1 else far, groups)
         ]
         pixel_copies.append(copies)
         moved_copies.append(
@@ -349,15 +351,23 @@
     inverse, frob_norm = newton_schulz(gram)
     factor = shrink_ref[0] * jnp.sqrt(all_rows * side_len / frob_norm)
     select = (iota((own, size), 0) == iota((own, size), 1)).astype(F32)
-    weights = dot_nt(select, inverse, HIGHEST) * factor
+    weights = (dot_nt(select, inverse, HIGHEST) * factor).astype(BF16)
     spread = POLAR_ROWS * own
-    wide = POLAR_ROWS * size
     repeat = (iota((spread, own), 0) // POLAR_ROWS == iota((spread, own), 1)).astype(BF16)
-    weights = dot_nn(repeat, weights.astype(BF16)).astype(BF16)
-    repeat = (iota((size, wide), 1) % size == iota((size, wide), 0)).astype(BF16)
-    weights = dot_nn(weights, repeat)
-    keep = iota((spread, wide), 0) % POLAR_ROWS == iota((spread, wide), 1) // size
-    weights = jnp.where(keep, weights, 0.0).astype(BF16)
+    weights = dot_nn(repeat, weights).astype(BF16)
+
+    def widened(count, first, channel_of, pixel_row_of):
+        columns = iota((size, count), 1)
+        chosen = dot_nn(weights, (iota((size, count), 0) == first + channel_of(columns)).astype(BF16))
+        columns = iota((spread, count), 1)
+        keep = iota((spread, count), 0) % POLAR_ROWS == pixel_row_of(columns)
+        return jnp.where(keep, chosen, 0.0).astype(BF16)
+
+    others = size - far * own
+    far_weights = widened(POLAR_ROWS * others, far * own, lambda c: c % others, lambda c: c // others)
+    if far:
+        own_weights = widened(spread, 0, lambda c: c // POLAR_ROWS, lambda c: c % POLAR_ROWS)
+        far_weights = jnp.concatenate([own_weights, far_weights], axis=1)
 
     out_copies = []
     for place, (chunk, row) in enumerate(blocks):
@@ -366,10 +376,13 @@
                 copy.wait()
         moved_copies[place].wait()
         for first in range(row, row + EDGE_ROWS, POLAR_ROWS):
-            data = stacked([pixels[chunk].at[group] for group in range(groups)], first, POLAR_ROWS)
-            polar = dot_nn(weights, data).reshape(own, POLAR_ROWS, side_len)
             into = starts[chunk] + first
-            moved[:, into : into + POLAR_ROWS] -= polar
+            rows = moved[:, into : into + POLAR_ROWS]
+            data = stacked([pixels[chunk].at[group] for group in range(far, groups)], first, POLAR_ROWS)
+            if far:
+                data = jnp.concatenate([rows.reshape(spread, side_len).astype(BF16), data], axis=0)
+            polar = dot_nn(far_weights, data).reshape(own, POLAR_ROWS, side_len)
+            moved[:, into : into + POLAR_ROWS] = rows - polar
         part = pl.ds(starts[chunk] + row, EDGE_ROWS)
         copy = pltpu.make_async_copy(moved.at[:, part], out_hbm.at[:, part], out_sems.at[place])
         copy.start()
@@ -397,7 +410,7 @@
             pltpu.SemaphoreType.DMA((blocks,)),
         ]
         + [pltpu.VMEM((groups,) + pieces[0].shape, BF16) for pieces in gathered],
-        compiler_params=kernel_params(60),
+        compiler_params=kernel_params(63),
         cost_estimate=COST,
         name="polar_step",
     )(shrinkage, gram, *moved, *flat)
@@ -408,7 +421,7 @@
     head, tail = lax.optimization_barrier((model_image[:, :reach], model_image[:, model_image.shape[1] - reach :]))
     before = lax.ppermute(tail.astype(BF16), "strip", [(i, i + 1) for i in range(ends)])
     after = lax.ppermute(head.astype(BF16), "strip", [(i + 1, i) for i in range(ends)])
-    return jnp.concatenate([before, after], axis=1)
+    return before, after
 
 
 def swap(value, axis, bits):
@@ -443,7 +456,8 @@
 
     levels, taps = highpass.shape
     reach = (taps - 1) * 2 ** (levels - 1)
-    edges = neighbour_rows(model_image, reach)
+    sides = neighbour_rows(model_image, reach)
+    edges = jnp.concatenate(sides, axis=1)
 
     halves = {}
     moved = {}
@@ -454,8 +468,10 @@
 
     def first(chunk):
         sent, state["last"] = first_transform(tables[chunk], grid, strips, state["last"])
-        if chunk == 1:
-            sent = gate(sent, edges)
+        if chunk == 0:
+            for side in sides:
+                sent = gate(sent, side)
+                state["last"] = gate(state["last"], side)
         if chunk == 2:
             gather(0)
             gram(0)

time: 278 us -> 280 us (level)
  local copies, waits for them, and re-layouts: 11 us -> 4.23 us
  Pallas kernels: 104 us -> 109 us
  starting transfers between devices: 38.1 us -> 41 us
    all_to_all x4, waiting for transfers between devices: 48.5 us -> 78.6 us  [first(): lax.all_to_all(sent, 'strip', split_axis=0, concat_axis=0, tiled=True)]
    ppermute x1, waiting for transfers between devices: 37.5 us -> 10.9 us  [neighbour_rows(): lax.ppermute(tail.astype(BF16), 'strip', [(i, i + 1) for i in range(ends)])]
    pallas_call x4, Pallas kernels: 33.7 us -> 41.1 us  [first_transform(): pl.pallas_call(first_body, grid=(chans // block,), in_specs=[pl.BlockSpec...]
    unnamed x20 -> x6, local copies, waits for them, and re-layouts: 7.77 us -> 0.79 us
    all_to_all x4, starting transfers between devices: 25.5 us -> 28.5 us  [first(): lax.all_to_all(sent, 'strip', split_axis=0, concat_axis=0, tiled=True)]
  transfers between devices with their start and end apart: 18 -> 18, of which waited for: 11 -> 11; matrix products, arithmetic and copies ran while one was open for 2% -> 1% of each run, Pallas kernels for 30% -> 35%
where the time goes in v13:
time: 280 us; the launch traced here: 277 us
  waiting for transfers between devices  120 us (43%)
  Pallas kernels  109 us (39%)
  starting transfers between devices  41 us (15%)
  local copies, waits for them, and re-layouts  4.23 us (2%)
    all_to_all x4, waiting for transfers between devices, first(): lax.all_to_all(sent, 'strip', split_axis=0, concat_axis=0, tiled=True)  78.6 us
    pallas_call x4, Pallas kernels, first_transform(): pl.pallas_call(first_body, grid=(chans // block,), in_specs=[pl.BlockSpec...  41.1 us
    ppermute x12, waiting for transfers between devices, swap(): return lax.ppermute(value, axis, [(i, i ^ bits) for i in range(count)])  30.4 us
    pallas_call x4, Pallas kernels, second_transform(): pl.pallas_call(second_body, grid=(side_len // block,), in_specs=[SMEM, pl...  29.2 us
    all_to_all x4, starting transfers between devices, first(): lax.all_to_all(sent, 'strip', split_axis=0, concat_axis=0, tiled=True)  28.5 us
    pallas_call x3, Pallas kernels, gram_step(): pl.pallas_call(functools.partial(gram_body, len(pieces)), grid=(rows // b...  16.1 us
    pallas_call x1, Pallas kernels, polar_step(): pl.pallas_call(functools.partial(polar_body, starts, sizes, groups), in_s...  11.3 us
    pallas_call x1, Pallas kernels, base_step(): pl.pallas_call(functools.partial(base_body, levels, taps, starts, strips)...  11.2 us
  transfers between devices with their start and end apart: 18, of which 11 were waited for; matrix products, arithmetic and copies ran while one was open for 1% of the time, Pallas kernels for 35%

profile of v13, /device:TPU:12, one launch (start us, length us, event | category | flops | bytes accessed | tf_op | source)
XLA Modules:
  0.0 277.1 jit_solution(14379115170145649285)
XLA Ops:
  0.0 2.7 fusion
  2.7 3.4 %collective-permute-start = (bf16[16,12,1024]{2,1,0:T(8,128)(2,1)}, bf16[16,12,1024]{2,1,0:T(8,128)(2,1)S(1)}, u32[]{:S(2)}, u32[]{:S(2)}) collective-permute-start(bf16[16,12,1024]{2,1,0:T(8,128)(2,1)} %get-tuple-element.28), channel_id=1, source_target_pairs={{0,4},{4,8},{8,12},{12,16},{16,20},{20,24},{24,28},{1,5},{5,9},{9,... | collective-permute-start | bytes 1179656 | tf_op jit(solution)/shard_map/ppermute | solution.py:422
  6.1 2.4 collective-permute-start.1
  8.6 10.3 %first_transform.4 = (bf16[8,2,16,32,128]{4,3,2,1,0:T(8,128)(2,1)}, f32[8,128]{1,0:T(8,128)}) custom-call(bf16[512,1024]{1,0:T(8,128)(2,1)} %constant.20.clone.table_ref, bf16[2,16,128,1024]{3,2,1,0:T(8,128)(2,1)} %grid_ref.7, s32[1]{0:T(128)} %bitcast.after_ref.strip_ref), custom_call_target="tpu_custom_call" | custom-call | bytes 65536 | tf_op jit(solution)/shard_map/first_transform/pallas_call | solution.py:112
  18.9 10.9 %collective-permute-done.after_ref = bf16[16,12,1024]{2,1,0:T(8,128)(2,1)S(1)} collective-permute-done((bf16[16,12,1024]{2,1,0:T(8,128)(2,1)}, bf16[16,12,1024]{2,1,0:T(8,128)(2,1)S(1)}, u32[]{:S(2)}, u32[]{:S(2)}) %collective-permute-start) | collective-permute-done | bytes 393248 | tf_op jit(solution)/shard_map/ppermute | solution.py:422
  29.7 0.8 copy-done.1
  30.5 5.5 %all-to-all-start = ((bf16[8,2,16,32,128]{4,3,2,1,0:T(8,128)(2,1)}), bf16[8,2,16,32,128]{4,3,2,1,0:T(8,128)(2,1)}, u32[]{:S(2)}, u32[]{:S(2)}) async-start(bf16[8,2,16,32,128]{4,3,2,1,0:T(8,128)(2,1)} %gate.10), calls=%async_computation | async-start | bytes 4194304 | tf_op jit(solution)/shard_map/all_to_all | solution.py:480
  36.0 11.9 %first_transform.5 = (bf16[8,2,16,48,128]{4,3,2,1,0:T(8,128)(2,1)}, f32[8,128]{1,0:T(8,128)}) custom-call(bf16[768,1024]{1,0:T(8,128)(2,1)} %constant.21.clone.table_ref, bf16[2,16,128,1024]{3,2,1,0:T(8,128)(2,1)} %grid_ref.7, f32[8,128]{1,0:T(8,128)} %gate.12.after_ref), custom_call_target="tpu_custom_call" | custom-call | bytes 65536 | tf_op jit(solution)/shard_map/first_transform/pallas_call | solution.py:112
  47.9 33.2 %all-to-all-done.half_ref = bf16[8,2,16,32,128]{4,3,2,1,0:T(8,128)(2,1)} async-done(((bf16[8,2,16,32,128]{4,3,2,1,0:T(8,128)(2,1)}), bf16[8,2,16,32,128]{4,3,2,1,0:T(8,128)(2,1)}, u32[]{:S(2)}, u32[]{:S(2)}) %all-to-all-start) | async-done | bytes 2097184 | tf_op jit(solution)/shard_map/all_to_all | solution.py:480
  81.1 7.9 %all-to-all-start.2 = ((bf16[8,2,16,48,128]{4,3,2,1,0:T(8,128)(2,1)}), bf16[8,2,16,48,128]{4,3,2,1,0:T(8,128)(2,1)}, u32[]{:S(2)}, u32[]{:S(2)}) async-start(bf16[8,2,16,48,128]{4,3,2,1,0:T(8,128)(2,1)} %get-tuple-element.37), calls=%async_computation.2 | async-start | bytes 6291456 | tf_op jit(solution)/shard_map/all_to_all | solution.py:480
  89.0 2.2 pad_maximum_fusion.edge_ref
  91.2 11.2 %base_step.1 = (f32[16,32,1024]{2,1,0:T(8,128)}, f32[16,48,1024]{2,1,0:T(8,128)}, f32[16,32,1024]{2,1,0:T(8,128)}, f32[16,16,1024]{2,1,0:T(8,128)}) custom-call(s32[1]{0:T(128)} %bitcast.after_ref.strip_ref, f32[16]{0:T(128)} %step_ref.9, f32[3,4]{1,0:T(4,128)} %highpass_ref.1, f32[16,128,1024]{2,1,0:T(8,128)} %model_ref.1, ...), custom_call_target="tpu_custom_call" | custom-call | bytes 65536 | tf_op jit(solution)/shard_map/base_step/pallas_call | solution.py:193
  102.3 7.3 %second_transform.4 = (f32[16,32,1024]{2,1,0:T(8,128)}, bf16[32,16,1024]{2,1,0:T(8,128)(2,1)}) custom-call(f32[16]{0:T(128)} %step_ref.9, bf16[8,2,16,32,128]{4,3,2,1,0:T(8,128)(2,1)} %all-to-all-done.half_ref, bf16[1024,1024]{1,0:T(8,128)(2,1)} %constant.22.clone.cosine_ref, bf16[1024,1024]{1,0:T(8,128)(2,1)} %constant.23.clone.sine_ref, ...), custom_call_target="tpu_custom_call" | custom-call | bytes 65536 | tf_op jit(solution)/shard_map/second_transform/pallas_call | solution.py:236
  109.6 1.5 collective-permute-start.2
  111.1 10.3 %first_transform.6 = (bf16[8,2,16,32,128]{4,3,2,1,0:T(8,128)(2,1)}, f32[8,128]{1,0:T(8,128)}) custom-call(bf16[512,1024]{1,0:T(8,128)(2,1)} %constant.24.clone.table_ref, bf16[2,16,128,1024]{3,2,1,0:T(8,128)(2,1)} %grid_ref.7, bf16[32,16,1024]{2,1,0:T(8,128)(2,1)} %get-tuple-element.33.after_ref.refs_0_.refs_4_), custom_call_target="tpu_custom_call" | custom-call | bytes 65536 | tf_op jit(solution)/shard_map/first_transform/pallas_call | solution.py:112
  121.4 12.3 %collective-permute-done.2.value_ref = bf16[32,16,1024]{2,1,0:T(8,128)(2,1)} collective-permute-done((bf16[32,16,1024]{2,1,0:T(8,128)(2,1)}, bf16[32,16,1024]{2,1,0:T(8,128)(2,1)}, u32[]{:S(2)}, u32[]{:S(2)}) %collective-permute-start.2) | collective-permute-done | bytes 1048608 | tf_op jit(solution)/shard_map/ppermute | solution.py:429
  133.8 0.0 collective-permute-start.4
  133.8 0.0 collective-permute-done.3.refs_2_.refs_6_
  133.8 3.0 %collective-permute-done.4.refs_3_.refs_7_ = bf16[32,16,1024]{2,1,0:T(8,128)(2,1)} collective-permute-done((bf16[32,16,1024]{2,1,0:T(8,128)(2,1)}, bf16[32,16,1024]{2,1,0:T(8,128)(2,1)}, u32[]{:S(2)}, u32[]{:S(2)}) %collective-permute-start.4) | collective-permute-done | bytes 1048608 | tf_op jit(solution)/shard_map/ppermute | solution.py:429
  136.8 0.7 broadcast_in_dim.3.before_ref
  137.5 4.8 %gram_step.3.after_ref.before_ref = f32[256,256]{1,0:T(8,128)} custom-call(f32[256,256]{1,0:T(8,128)} %broadcast_in_dim.3.before_ref, f32[8,128]{1,0:T(8,128)} %get-tuple-element.34.after_ref, bf16[32,16,1024]{2,1,0:T(8,128)(2,1)} %get-tuple-element.33.after_ref.refs_0_.refs_4_, bf16[32,16,1024]{2,1,0:T(8,128)(2,1)} %gate.13.refs_1_.refs_5_, ...), custom_call_target="tpu_custom_call" | custom-call | bytes 65536 | tf_op jit(solution)/shard_map/gram_step/pallas_call | solution.py:283
  142.2 13.7 %all-to-all-done.2.half_ref = bf16[8,2,16,48,128]{4,3,2,1,0:T(8,128)(2,1)} async-done(((bf16[8,2,16,48,128]{4,3,2,1,0:T(8,128)(2,1)}), bf16[8,2,16,48,128]{4,3,2,1,0:T(8,128)(2,1)}, u32[]{:S(2)}, u32[]{:S(2)}) %all-to-all-start.2) | async-done | bytes 3145760 | tf_op jit(solution)/shard_map/all_to_all | solution.py:480
  155.9 7.6 %all-to-all-start.1 = ((bf16[8,2,16,32,128]{4,3,2,1,0:T(8,128)(2,1)}), bf16[8,2,16,32,128]{4,3,2,1,0:T(8,128)(2,1)}, u32[]{:S(2)}, u32[]{:S(2)}) async-start(bf16[8,2,16,32,128]{4,3,2,1,0:T(8,128)(2,1)} %gate.14), calls=%async_computation.1 | async-start | bytes 4194304 | tf_op jit(solution)/shard_map/all_to_all | solution.py:480
  163.5 9.0 %second_transform.5 = (f32[16,48,1024]{2,1,0:T(8,128)}, bf16[48,16,1024]{2,1,0:T(8,128)(2,1)}) custom-call(f32[16]{0:T(128)} %step_ref.9, bf16[8,2,16,48,128]{4,3,2,1,0:T(8,128)(2,1)} %all-to-all-done.2.half_ref, bf16[1024,1024]{1,0:T(8,128)(2,1)} %constant.22.clone.cosine_ref, bf16[1024,1024]{1,0:T(8,128)(2,1)} %constant.23.clone.sine_ref, ...), custom_call_target="tpu_custom_call" | custom-call | bytes 65536 | tf_op jit(solution)/shard_map/second_transform/pallas_call | solution.py:236
  172.5 1.5 collective-permute-start.5
  174.0 8.6 %first_transform.7 = (bf16[8,2,16,16,128]{4,3,2,1,0:T(8,128)(2,1)}, f32[8,128]{1,0:T(8,128)}) custom-call(bf16[256,1024]{1,0:T(8,128)(2,1)} %constant.25.clone.table_ref, bf16[2,16,128,1024]{3,2,1,0:T(8,128)(2,1)} %grid_ref.7, bf16[48,16,1024]{2,1,0:T(8,128)(2,1)} %get-tuple-element.39.after_ref.refs_0_.refs_8_), custom_call_target="tpu_custom_call" | custom-call | bytes 65536 | tf_op jit(solution)/shard_map/first_transform/pallas_call | solution.py:112
  182.6 25.5 %all-to-all-done.1.half_ref = bf16[8,2,16,32,128]{4,3,2,1,0:T(8,128)(2,1)} async-done(((bf16[8,2,16,32,128]{4,3,2,1,0:T(8,128)(2,1)}), bf16[8,2,16,32,128]{4,3,2,1,0:T(8,128)(2,1)}, u32[]{:S(2)}, u32[]{:S(2)}) %all-to-all-start.1) | async-done | bytes 2097184 | tf_op jit(solution)/shard_map/all_to_all | solution.py:480
  208.1 7.5 %all-to-all-start.3 = ((bf16[8,2,16,16,128]{4,3,2,1,0:T(8,128)(2,1)}), bf16[8,2,16,16,128]{4,3,2,1,0:T(8,128)(2,1)}, u32[]{:S(2)}, u32[]{:S(2)}) async-start(bf16[8,2,16,16,128]{4,3,2,1,0:T(8,128)(2,1)} %get-tuple-element.42), calls=%async_computation.3 | async-start | bytes 2097152 | tf_op jit(solution)/shard_map/all_to_all | solution.py:480
  215.6 0.0 collective-permute-done.5.value_ref
  215.6 0.5 collective-permute-start.7
  216.1 7.3 %second_transform.6 = (f32[16,32,1024]{2,1,0:T(8,128)}, bf16[32,16,1024]{2,1,0:T(8,128)(2,1)}) custom-call(f32[16]{0:T(128)} %step_ref.9, bf16[8,2,16,32,128]{4,3,2,1,0:T(8,128)(2,1)} %all-to-all-done.1.half_ref, bf16[1024,1024]{1,0:T(8,128)(2,1)} %constant.22.clone.cosine_ref, bf16[1024,1024]{1,0:T(8,128)(2,1)} %constant.23.clone.sine_ref, ...), custom_call_target="tpu_custom_call" | custom-call | bytes 65536 | tf_op jit(solution)/shard_map/second_transform/pallas_call | solution.py:236
  223.4 1.5 collective-permute-start.8
  224.9 0.0 collective-permute-start.9
  224.9 0.0 collective-permute-done.6.refs_2_.refs_10_
  224.9 0.0 collective-permute-done.7.refs_3_.refs_11_
  224.9 6.5 %gram_step.4.after_ref.before_ref = f32[256,256]{1,0:T(8,128)} custom-call(f32[256,256]{1,0:T(8,128)} %gram_step.3.after_ref.before_ref, bf16[32,16,1024]{2,1,0:T(8,128)(2,1)} %get-tuple-element.41.after_ref.refs_0_.refs_12_, bf16[48,16,1024]{2,1,0:T(8,128)(2,1)} %get-tuple-element.39.after_ref.refs_0_.refs_8_, bf16[48,16,1024]{2,1,0:T(8,128)(2,1)} %gate.15.refs_1_.refs_9_, ...), custom_call_target="tpu_custom_call" | custom-call | bytes 65536 | tf_op jit(solution)/shard_map/gram_step/pallas_call | solution.py:283
  231.5 6.3 %all-to-all-done.3.half_ref = bf16[8,2,16,16,128]{4,3,2,1,0:T(8,128)(2,1)} async-done(((bf16[8,2,16,16,128]{4,3,2,1,0:T(8,128)(2,1)}), bf16[8,2,16,16,128]{4,3,2,1,0:T(8,128)(2,1)}, u32[]{:S(2)}, u32[]{:S(2)}) %all-to-all-start.3) | async-done | bytes 1048608 | tf_op jit(solution)/shard_map/all_to_all | solution.py:480
  237.7 5.6 %second_transform.7 = (f32[16,16,1024]{2,1,0:T(8,128)}, bf16[16,16,1024]{2,1,0:T(8,128)(2,1)}) custom-call(f32[16]{0:T(128)} %step_ref.9, bf16[8,2,16,16,128]{4,3,2,1,0:T(8,128)(2,1)} %all-to-all-done.3.half_ref, bf16[1024,1024]{1,0:T(8,128)(2,1)} %constant.22.clone.cosine_ref, bf16[1024,1024]{1,0:T(8,128)(2,1)} %constant.23.clone.sine_ref, ...), custom_call_target="tpu_custom_call" | custom-call | bytes 65536 | tf_op jit(solution)/shard_map/second_transform/pallas_call | solution.py:236
  243.3 5.5 %collective-permute-done.8.value_ref = bf16[32,16,1024]{2,1,0:T(8,128)(2,1)} collective-permute-done((bf16[32,16,1024]{2,1,0:T(8,128)(2,1)}, bf16[32,16,1024]{2,1,0:T(8,128)(2,1)}, u32[]{:S(2)}, u32[]{:S(2)}) %collective-permute-start.8) | collective-permute-done | bytes 1048608 | tf_op jit(solution)/shard_map/ppermute | solution.py:429
  248.9 0.0 collective-permute-start.10
  248.9 1.5 collective-permute-start.11
  250.4 0.2 collective-permute-start.12
  250.6 0.0 collective-permute-done.9.refs_2_.refs_14_
  250.6 1.3 collective-permute-done.10.refs_3_.refs_15_
  251.9 4.8 %gram_step.5.after_ref.gram_ref = f32[256,256]{1,0:T(8,128)} custom-call(f32[256,256]{1,0:T(8,128)} %gram_step.4.after_ref.before_ref, bf16[16,16,1024]{2,1,0:T(8,128)(2,1)} %get-tuple-element.44.after_ref.refs_16_, bf16[32,16,1024]{2,1,0:T(8,128)(2,1)} %get-tuple-element.41.after_ref.refs_0_.refs_12_, bf16[32,16,1024]{2,1,0:T(8,128)(2,1)} %gate.16.refs_1_.refs_13_, ...), custom_call_target="tpu_custom_call" | custom-call | bytes 65536 | tf_op jit(solution)/shard_map/gram_step/pallas_call | solution.py:283
  256.7 6.6 %collective-permute-done.11.value_ref = bf16[16,16,1024]{2,1,0:T(8,128)(2,1)} collective-permute-done((bf16[16,16,1024]{2,1,0:T(8,128)(2,1)S(1)}, bf16[16,16,1024]{2,1,0:T(8,128)(2,1)}, u32[]{:S(2)}, u32[]{:S(2)}) %collective-permute-start.11) | collective-permute-done | bytes 524320 | tf_op jit(solution)/shard_map/ppermute | solution.py:429
  264.0 1.6 collective-permute-done.13.refs_19_
  265.6 11.3 %polar_step.1 = f32[16,128,1024]{2,1,0:T(8,128)} custom-call(f32[1]{0:T(128)S(6)} %copy.30.shrink_ref, f32[256,256]{1,0:T(8,128)} %gram_step.5.after_ref.gram_ref, f32[16,32,1024]{2,1,0:T(8,128)} %get-tuple-element.45.refs_0_, f32[16,48,1024]{2,1,0:T(8,128)} %get-tuple-element.46.refs_1_, f32[16,32,1024]{2,1,0:T(8,128)} %get-tuple-element.47.refs_2_, ...), custom_call_target="tpu_custom_call" | custom-call | bytes 65536 | tf_op jit(solution)/shard_map/polar_step/pallas_call | solution.py:401
  (19 shorter events, 0.0 us)
Async XLA Ops:
  2.7 27.0 %collective-permute-start = (bf16[16,12,1024]{2,1,0:T(8,128)(2,1)}, bf16[16,12,1024]{2,1,0:T(8,128)(2,1)S(1)}, u32[]{:S(2)}, u32[]{:S(2)}) collective-permute-start(bf16[16,12,1024]{2,1,0:T(8,128)(2,1)} %get-tuple-element.28), channel_id=1, source_target_pairs={{0,4},{4,8},{8,12},{12,16},{16,20},{20,24},{24,28},{1,5},{5,9},{9,... | collective-permute-start | bytes 1179656 | tf_op jit(solution)/shard_map/ppermute | solution.py:422
  6.1 24.4 %collective-permute-start.1 = (bf16[16,12,1024]{2,1,0:T(8,128)(2,1)}, bf16[16,12,1024]{2,1,0:T(8,128)(2,1)}, u32[]{:S(2)}, u32[]{:S(2)}) collective-permute-start(bf16[16,12,1024]{2,1,0:T(8,128)(2,1)} %get-tuple-element.29), channel_id=1, source_target_pairs={{4,0},{8,4},{12,8},{16,12},{20,16},{24,20},{28,24},{5,1},{9,5},{13... | collective-permute-start | bytes 1179656 | tf_op jit(solution)/shard_map/ppermute | solution.py:423
  29.7 0.8 copy-start.1
  30.5 50.6 %all-to-all-start = ((bf16[8,2,16,32,128]{4,3,2,1,0:T(8,128)(2,1)}), bf16[8,2,16,32,128]{4,3,2,1,0:T(8,128)(2,1)}, u32[]{:S(2)}, u32[]{:S(2)}) async-start(bf16[8,2,16,32,128]{4,3,2,1,0:T(8,128)(2,1)} %gate.10), calls=%async_computation | async-start | bytes 4194304 | tf_op jit(solution)/shard_map/all_to_all | solution.py:480
  81.1 7.9 %copy-start.2 = (bf16[16,12,1024]{2,1,0:T(8,128)(2,1)S(1)}, bf16[16,12,1024]{2,1,0:T(8,128)(2,1)}, u32[]{:S(2)}) copy-start(bf16[16,12,1024]{2,1,0:T(8,128)(2,1)} %copy-done.1) | copy-start | bytes 1179652
  81.1 74.8 %all-to-all-start.2 = ((bf16[8,2,16,48,128]{4,3,2,1,0:T(8,128)(2,1)}), bf16[8,2,16,48,128]{4,3,2,1,0:T(8,128)(2,1)}, u32[]{:S(2)}, u32[]{:S(2)}) async-start(bf16[8,2,16,48,128]{4,3,2,1,0:T(8,128)(2,1)} %get-tuple-element.37), calls=%async_computation.2 | async-start | bytes 6291456 | tf_op jit(solution)/shard_map/all_to_all | solution.py:480
  109.6 24.1 %collective-permute-start.2 = (bf16[32,16,1024]{2,1,0:T(8,128)(2,1)}, bf16[32,16,1024]{2,1,0:T(8,128)(2,1)}, u32[]{:S(2)}, u32[]{:S(2)}) collective-permute-start(bf16[32,16,1024]{2,1,0:T(8,128)(2,1)} %get-tuple-element.33.after_ref.refs_0_.refs_4_), channel_id=1, source_target_pairs={{0,2},{1,3},{2,0},{3,1},{4,6},{5,7},{6,4},{7,5},{8,10},{9,11},{10,... | collective-permute-start | bytes 3145736 | tf_op jit(solution)/shard_map/ppermute | solution.py:429
  111.1 22.6 %collective-permute-start.3 = (bf16[32,16,1024]{2,1,0:T(8,128)(2,1)}, bf16[32,16,1024]{2,1,0:T(8,128)(2,1)}, u32[]{:S(2)}, u32[]{:S(2)}) collective-permute-start(bf16[32,16,1024]{2,1,0:T(8,128)(2,1)} %get-tuple-element.33.after_ref.refs_0_.refs_4_), channel_id=1, source_target_pairs={{0,1},{1,0},{2,3},{3,2},{4,5},{5,4},{6,7},{7,6},{8,9},{9,8},{10,11... | collective-permute-start | bytes 3145736 | tf_op jit(solution)/shard_map/ppermute | solution.py:429
  133.8 3.0 %collective-permute-start.4 = (bf16[32,16,1024]{2,1,0:T(8,128)(2,1)}, bf16[32,16,1024]{2,1,0:T(8,128)(2,1)}, u32[]{:S(2)}, u32[]{:S(2)}) collective-permute-start(bf16[32,16,1024]{2,1,0:T(8,128)(2,1)} %gate.13.refs_1_.refs_5_), channel_id=1, source_target_pairs={{0,1},{1,0},{2,3},{3,2},{4,5},{5,4},{6,7},{7,6},{8,9},{9,8},{10,11... | collective-permute-start | bytes 3145736 | tf_op jit(solution)/shard_map/ppermute | solution.py:429
  155.9 52.2 %all-to-all-start.1 = ((bf16[8,2,16,32,128]{4,3,2,1,0:T(8,128)(2,1)}), bf16[8,2,16,32,128]{4,3,2,1,0:T(8,128)(2,1)}, u32[]{:S(2)}, u32[]{:S(2)}) async-start(bf16[8,2,16,32,128]{4,3,2,1,0:T(8,128)(2,1)} %gate.14), calls=%async_computation.1 | async-start | bytes 4194304 | tf_op jit(solution)/shard_map/all_to_all | solution.py:480
  172.5 43.1 %collective-permute-start.5 = (bf16[48,16,1024]{2,1,0:T(8,128)(2,1)}, bf16[48,16,1024]{2,1,0:T(8,128)(2,1)}, u32[]{:S(2)}, u32[]{:S(2)}) collective-permute-start(bf16[48,16,1024]{2,1,0:T(8,128)(2,1)} %get-tuple-element.39.after_ref.refs_0_.refs_8_), channel_id=1, source_target_pairs={{0,2},{1,3},{2,0},{3,1},{4,6},{5,7},{6,4},{7,5},{8,10},{9,11},{10,... | collective-permute-start | bytes 4718600 | tf_op jit(solution)/shard_map/ppermute | solution.py:429
  208.1 29.6 %all-to-all-start.3 = ((bf16[8,2,16,16,128]{4,3,2,1,0:T(8,128)(2,1)}), bf16[8,2,16,16,128]{4,3,2,1,0:T(8,128)(2,1)}, u32[]{:S(2)}, u32[]{:S(2)}) async-start(bf16[8,2,16,16,128]{4,3,2,1,0:T(8,128)(2,1)} %get-tuple-element.42), calls=%async_computation.3 | async-start | bytes 2097152 | tf_op jit(solution)/shard_map/all_to_all | solution.py:480
  215.6 9.3 %collective-permute-start.6 = (bf16[48,16,1024]{2,1,0:T(8,128)(2,1)}, bf16[48,16,1024]{2,1,0:T(8,128)(2,1)}, u32[]{:S(2)}, u32[]{:S(2)}) collective-permute-start(bf16[48,16,1024]{2,1,0:T(8,128)(2,1)} %get-tuple-element.39.after_ref.refs_0_.refs_8_), channel_id=1, source_target_pairs={{0,1},{1,0},{2,3},{3,2},{4,5},{5,4},{6,7},{7,6},{8,9},{9,8},{10,11... | collective-permute-start | bytes 4718600 | tf_op jit(solution)/shard_map/ppermute | solution.py:429
  215.6 9.3 %collective-permute-start.7 = (bf16[48,16,1024]{2,1,0:T(8,128)(2,1)}, bf16[48,16,1024]{2,1,0:T(8,128)(2,1)}, u32[]{:S(2)}, u32[]{:S(2)}) collective-permute-start(bf16[48,16,1024]{2,1,0:T(8,128)(2,1)} %gate.15.refs_1_.refs_9_), channel_id=1, source_target_pairs={{0,1},{1,0},{2,3},{3,2},{4,5},{5,4},{6,7},{7,6},{8,9},{9,8},{10,11... | collective-permute-start | bytes 4718600 | tf_op jit(solution)/shard_map/ppermute | solution.py:429
  223.4 25.5 %collective-permute-start.8 = (bf16[32,16,1024]{2,1,0:T(8,128)(2,1)}, bf16[32,16,1024]{2,1,0:T(8,128)(2,1)}, u32[]{:S(2)}, u32[]{:S(2)}) collective-permute-start(bf16[32,16,1024]{2,1,0:T(8,128)(2,1)} %get-tuple-element.41.after_ref.refs_0_.refs_12_), channel_id=1, source_target_pairs={{0,2},{1,3},{2,0},{3,1},{4,6},{5,7},{6,4},{7,5},{8,10},{9,11},{10,... | collective-permute-start | bytes 3145736 | tf_op jit(solution)/shard_map/ppermute | solution.py:429
  224.9 25.7 %collective-permute-start.9 = (bf16[32,16,1024]{2,1,0:T(8,128)(2,1)}, bf16[32,16,1024]{2,1,0:T(8,128)(2,1)}, u32[]{:S(2)}, u32[]{:S(2)}) collective-permute-start(bf16[32,16,1024]{2,1,0:T(8,128)(2,1)} %get-tuple-element.41.after_ref.refs_0_.refs_12_), channel_id=1, source_target_pairs={{0,1},{1,0},{2,3},{3,2},{4,5},{5,4},{6,7},{7,6},{8,9},{9,8},{10,11... | collective-permute-start | bytes 3145736 | tf_op jit(solution)/shard_map/ppermute | solution.py:429
  243.3 5.5 %copy-start = (bf16[16,16,1024]{2,1,0:T(8,128)(2,1)S(1)}, bf16[16,16,1024]{2,1,0:T(8,128)(2,1)}, u32[]{:S(2)}) copy-start(bf16[16,16,1024]{2,1,0:T(8,128)(2,1)} %get-tuple-element.44.after_ref.refs_16_) | copy-start | bytes 1572868
  248.9 3.0 %collective-permute-start.10 = (bf16[32,16,1024]{2,1,0:T(8,128)(2,1)}, bf16[32,16,1024]{2,1,0:T(8,128)(2,1)}, u32[]{:S(2)}, u32[]{:S(2)}) collective-permute-start(bf16[32,16,1024]{2,1,0:T(8,128)(2,1)} %gate.16.refs_1_.refs_13_), channel_id=1, source_target_pairs={{0,1},{1,0},{2,3},{3,2},{4,5},{5,4},{6,7},{7,6},{8,9},{9,8},{10,11... | collective-permute-start | bytes 3145736 | tf_op jit(solution)/shard_map/ppermute | solution.py:429
  248.9 14.4 %collective-permute-start.11 = (bf16[16,16,1024]{2,1,0:T(8,128)(2,1)S(1)}, bf16[16,16,1024]{2,1,0:T(8,128)(2,1)}, u32[]{:S(2)}, u32[]{:S(2)}) collective-permute-start(bf16[16,16,1024]{2,1,0:T(8,128)(2,1)S(1)} %copy-done), channel_id=1, source_target_pairs={{0,2},{1,3},{2,0},{3,1},{4,6},{5,7},{6,4},{7,5},{8,10},{9,11},{10,... | collective-permute-start | bytes 1572872 | tf_op jit(solution)/shard_map/ppermute | solution.py:429
  250.4 13.6 %collective-permute-start.12 = (bf16[16,16,1024]{2,1,0:T(8,128)(2,1)S(1)}, bf16[16,16,1024]{2,1,0:T(8,128)(2,1)}, u32[]{:S(2)}, u32[]{:S(2)}) collective-permute-start(bf16[16,16,1024]{2,1,0:T(8,128)(2,1)S(1)} %copy-done), channel_id=1, source_target_pairs={{0,1},{1,0},{2,3},{3,2},{4,5},{5,4},{6,7},{7,6},{8,9},{9,8},{10,11... | collective-permute-start | bytes 1572872 | tf_op jit(solution)/shard_map/ppermute | solution.py:429
  263.3 2.3 collective-permute-start.13

commit v14 on v13

--- a/solution.py
+++ b/solution.py
@@ -108,7 +108,7 @@
         total = total + jnp.einsum("mv,cuv->mcu", turned, grid[1], preferred_element_type=F32)
         total = total.astype(BF16).reshape(2, strips, rows, chans, width)
         return total.transpose(1, 0, 3, 2, 4), jnp.zeros((8, 128), F32)
-    block = 2 if chans % 2 == 0 else 1
+    block = 4 if chans % 4 == 0 else 1
     return pl.pallas_call(
         first_body,
         grid=(chans // block,),
@@ -468,10 +468,9 @@
 
     def first(chunk):
         sent, state["last"] = first_transform(tables[chunk], grid, strips, state["last"])
-        if chunk == 0:
+        if chunk == 1:
             for side in sides:
                 sent = gate(sent, side)
-                state["last"] = gate(state["last"], side)
         if chunk == 2:
             gather(0)
             gram(0)

time: 280 us -> 271 us (0.968)
  Pallas kernels: 109 us -> 102 us
    all_to_all x4, waiting for transfers between devices: 78.6 us -> 47.8 us  [first(): lax.all_to_all(sent, 'strip', split_axis=0, concat_axis=0, tiled=True)]
    ppermute x1, waiting for transfers between devices: 10.9 us -> 37.3 us  [neighbour_rows(): lax.ppermute(tail.astype(BF16), 'strip', [(i, i + 1) for i in range(ends)])]
    pallas_call x4, Pallas kernels: 41.1 us -> 33.8 us  [first_transform(): pl.pallas_call(first_body, grid=(chans // block,), in_specs=[pl.BlockSpec...]
  transfers between devices with their start and end apart: 18 -> 18, of which waited for: 11 -> 11; matrix products, arithmetic and copies ran while one was open for 1% -> 2% of each run, Pallas kernels for 35% -> 31%
where the time goes in v14:
time: 271 us; the launch traced here: 268 us
  waiting for transfers between devices  119 us (44%)
  Pallas kernels  102 us (38%)
  starting transfers between devices  40 us (15%)
  local copies, waits for them, and re-layouts  4.32 us (2%)
    all_to_all x4, waiting for transfers between devices, first(): lax.all_to_all(sent, 'strip', split_axis=0, concat_axis=0, tiled=True)  47.8 us
    ppermute x1, waiting for transfers between devices, neighbour_rows(): lax.ppermute(tail.astype(BF16), 'strip', [(i, i + 1) for i in range(ends)])  37.3 us
    pallas_call x4, Pallas kernels, first_transform(): pl.pallas_call(first_body, grid=(chans // block,), in_specs=[pl.BlockSpec...  33.8 us
    ppermute x12, waiting for transfers between devices, swap(): return lax.ppermute(value, axis, [(i, i ^ bits) for i in range(count)])  32.9 us
    pallas_call x4, Pallas kernels, second_transform(): pl.pallas_call(second_body, grid=(side_len // block,), in_specs=[SMEM, pl...  29.2 us
    all_to_all x4, starting transfers between devices, first(): lax.all_to_all(sent, 'strip', split_axis=0, concat_axis=0, tiled=True)  27.5 us
    pallas_call x3, Pallas kernels, gram_step(): pl.pallas_call(functools.partial(gram_body, len(pieces)), grid=(rows // b...  16.1 us
    pallas_call x1, Pallas kernels, polar_step(): pl.pallas_call(functools.partial(polar_body, starts, sizes, groups), in_s...  11.3 us
  transfers between devices with their start and end apart: 18, of which 11 were waited for; matrix products, arithmetic and copies ran while one was open for 2% of the time, Pallas kernels for 31%

profile of v14, /device:TPU:12, one launch (start us, length us, event | category | flops | bytes accessed | tf_op | source)
XLA Modules:
  0.0 268.0 jit_solution(4881688250447080447)
XLA Ops:
  0.0 8.5 %first_transform.4 = (bf16[8,2,16,32,128]{4,3,2,1,0:T(8,128)(2,1)}, f32[8,128]{1,0:T(8,128)}) custom-call(bf16[512,1024]{1,0:T(8,128)(2,1)} %constant.20.clone.table_ref, bf16[2,16,128,1024]{3,2,1,0:T(8,128)(2,1)} %grid_ref.7, s32[1]{0:T(128)} %bitcast.after_ref.strip_ref), custom_call_target="tpu_custom_call" | custom-call | bytes 65536 | tf_op jit(solution)/shard_map/first_transform/pallas_call | solution.py:112
  8.5 6.2 %all-to-all-start = ((bf16[8,2,16,32,128]{4,3,2,1,0:T(8,128)(2,1)}), bf16[8,2,16,32,128]{4,3,2,1,0:T(8,128)(2,1)}, u32[]{:S(2)}, u32[]{:S(2)}) async-start(bf16[8,2,16,32,128]{4,3,2,1,0:T(8,128)(2,1)} %get-tuple-element.27), calls=%async_computation | async-start | bytes 4194304 | tf_op jit(solution)/shard_map/all_to_all | solution.py:479
  14.7 2.8 %fusion = (bf16[16,12,1024]{2,1,0:T(8,128)(2,1)}, bf16[16,12,1024]{2,1,0:T(8,128)(2,1)}) fusion(f32[16,128,1024]{2,1,0:T(8,128)} %model_ref.1), kind=kLoop, calls=%fused_computation.1 | loop fusion | bytes 1572864 | tf_op jit(solution)/shard_map/slice | solution.py:421
  17.5 3.4 %collective-permute-start = (bf16[16,12,1024]{2,1,0:T(8,128)(2,1)}, bf16[16,12,1024]{2,1,0:T(8,128)(2,1)S(1)}, u32[]{:S(2)}, u32[]{:S(2)}) collective-permute-start(bf16[16,12,1024]{2,1,0:T(8,128)(2,1)} %get-tuple-element.28), channel_id=1, source_target_pairs={{0,4},{4,8},{8,12},{12,16},{16,20},{20,24},{24,28},{1,5},{5,9},{9,... | collective-permute-start | bytes 1179656 | tf_op jit(solution)/shard_map/ppermute | solution.py:422
  20.9 2.5 collective-permute-start.1
  23.4 10.3 %first_transform.5 = (bf16[8,2,16,48,128]{4,3,2,1,0:T(8,128)(2,1)}, f32[8,128]{1,0:T(8,128)}) custom-call(bf16[768,1024]{1,0:T(8,128)(2,1)} %constant.21.clone.table_ref, bf16[2,16,128,1024]{3,2,1,0:T(8,128)(2,1)} %grid_ref.7, f32[8,128]{1,0:T(8,128)} %get-tuple-element.30.after_ref), custom_call_target="tpu_custom_call" | custom-call | bytes 65536 | tf_op jit(solution)/shard_map/first_transform/pallas_call | solution.py:112
  33.7 37.3 %collective-permute-done.after_ref = bf16[16,12,1024]{2,1,0:T(8,128)(2,1)S(1)} collective-permute-done((bf16[16,12,1024]{2,1,0:T(8,128)(2,1)}, bf16[16,12,1024]{2,1,0:T(8,128)(2,1)S(1)}, u32[]{:S(2)}, u32[]{:S(2)}) %collective-permute-start) | collective-permute-done | bytes 393248 | tf_op jit(solution)/shard_map/ppermute | solution.py:422
  70.9 0.8 copy-done.1
  71.7 1.1 collective-permute-done.1.after_ref
  72.8 0.0 all-to-all-done.half_ref
  72.8 5.1 %all-to-all-start.2 = ((bf16[8,2,16,48,128]{4,3,2,1,0:T(8,128)(2,1)}), bf16[8,2,16,48,128]{4,3,2,1,0:T(8,128)(2,1)}, u32[]{:S(2)}, u32[]{:S(2)}) async-start(bf16[8,2,16,48,128]{4,3,2,1,0:T(8,128)(2,1)} %gate.10), calls=%async_computation.2 | async-start | bytes 6291456 | tf_op jit(solution)/shard_map/all_to_all | solution.py:479
  77.9 2.2 pad_maximum_fusion.edge_ref
  80.1 11.2 %base_step.1 = (f32[16,32,1024]{2,1,0:T(8,128)}, f32[16,48,1024]{2,1,0:T(8,128)}, f32[16,32,1024]{2,1,0:T(8,128)}, f32[16,16,1024]{2,1,0:T(8,128)}) custom-call(s32[1]{0:T(128)} %bitcast.after_ref.strip_ref, f32[16]{0:T(128)} %step_ref.9, f32[3,4]{1,0:T(4,128)} %highpass_ref.1, f32[16,128,1024]{2,1,0:T(8,128)} %model_ref.1, ...), custom_call_target="tpu_custom_call" | custom-call | bytes 65536 | tf_op jit(solution)/shard_map/base_step/pallas_call | solution.py:193
  91.2 7.3 %second_transform.4 = (f32[16,32,1024]{2,1,0:T(8,128)}, bf16[32,16,1024]{2,1,0:T(8,128)(2,1)}) custom-call(f32[16]{0:T(128)} %step_ref.9, bf16[8,2,16,32,128]{4,3,2,1,0:T(8,128)(2,1)} %all-to-all-done.half_ref, bf16[1024,1024]{1,0:T(8,128)(2,1)} %constant.22.clone.cosine_ref, bf16[1024,1024]{1,0:T(8,128)(2,1)} %constant.23.clone.sine_ref, ...), custom_call_target="tpu_custom_call" | custom-call | bytes 65536 | tf_op jit(solution)/shard_map/second_transform/pallas_call | solution.py:236
  98.5 1.5 collective-permute-start.2
  100.0 0.0 collective-permute-start.3
  100.0 8.5 %first_transform.6 = (bf16[8,2,16,32,128]{4,3,2,1,0:T(8,128)(2,1)}, f32[8,128]{1,0:T(8,128)}) custom-call(bf16[512,1024]{1,0:T(8,128)(2,1)} %constant.24.clone.table_ref, bf16[2,16,128,1024]{3,2,1,0:T(8,128)(2,1)} %grid_ref.7, bf16[32,16,1024]{2,1,0:T(8,128)(2,1)} %get-tuple-element.33.after_ref.refs_0_.refs_4_), custom_call_target="tpu_custom_call" | custom-call | bytes 65536 | tf_op jit(solution)/shard_map/first_transform/pallas_call | solution.py:112
  108.5 14.8 %collective-permute-done.2.value_ref = bf16[32,16,1024]{2,1,0:T(8,128)(2,1)} collective-permute-done((bf16[32,16,1024]{2,1,0:T(8,128)(2,1)}, bf16[32,16,1024]{2,1,0:T(8,128)(2,1)}, u32[]{:S(2)}, u32[]{:S(2)}) %collective-permute-start.2) | collective-permute-done | bytes 1048608 | tf_op jit(solution)/shard_map/ppermute | solution.py:429
  123.4 0.0 collective-permute-start.4
  123.4 0.0 collective-permute-done.3.refs_2_.refs_6_
  123.4 3.0 %collective-permute-done.4.refs_3_.refs_7_ = bf16[32,16,1024]{2,1,0:T(8,128)(2,1)} collective-permute-done((bf16[32,16,1024]{2,1,0:T(8,128)(2,1)}, bf16[32,16,1024]{2,1,0:T(8,128)(2,1)}, u32[]{:S(2)}, u32[]{:S(2)}) %collective-permute-start.4) | collective-permute-done | bytes 1048608 | tf_op jit(solution)/shard_map/ppermute | solution.py:429
  126.4 0.7 broadcast_in_dim.3.before_ref
  127.1 4.8 %gram_step.3.after_ref.before_ref = f32[256,256]{1,0:T(8,128)} custom-call(f32[256,256]{1,0:T(8,128)} %broadcast_in_dim.3.before_ref, f32[8,128]{1,0:T(8,128)} %get-tuple-element.34.after_ref, bf16[32,16,1024]{2,1,0:T(8,128)(2,1)} %get-tuple-element.33.after_ref.refs_0_.refs_4_, bf16[32,16,1024]{2,1,0:T(8,128)(2,1)} %gate.7.refs_1_.refs_5_, ...), custom_call_target="tpu_custom_call" | custom-call | bytes 65536 | tf_op jit(solution)/shard_map/gram_step/pallas_call | solution.py:283
  131.9 13.7 %all-to-all-done.2.half_ref = bf16[8,2,16,48,128]{4,3,2,1,0:T(8,128)(2,1)} async-done(((bf16[8,2,16,48,128]{4,3,2,1,0:T(8,128)(2,1)}), bf16[8,2,16,48,128]{4,3,2,1,0:T(8,128)(2,1)}, u32[]{:S(2)}, u32[]{:S(2)}) %all-to-all-start.2) | async-done | bytes 3145760 | tf_op jit(solution)/shard_map/all_to_all | solution.py:479
  145.5 8.6 %all-to-all-start.1 = ((bf16[8,2,16,32,128]{4,3,2,1,0:T(8,128)(2,1)}), bf16[8,2,16,32,128]{4,3,2,1,0:T(8,128)(2,1)}, u32[]{:S(2)}, u32[]{:S(2)}) async-start(bf16[8,2,16,32,128]{4,3,2,1,0:T(8,128)(2,1)} %gate.8), calls=%async_computation.1 | async-start | bytes 4194304 | tf_op jit(solution)/shard_map/all_to_all | solution.py:479
  154.1 9.0 %second_transform.5 = (f32[16,48,1024]{2,1,0:T(8,128)}, bf16[48,16,1024]{2,1,0:T(8,128)(2,1)}) custom-call(f32[16]{0:T(128)} %step_ref.9, bf16[8,2,16,48,128]{4,3,2,1,0:T(8,128)(2,1)} %all-to-all-done.2.half_ref, bf16[1024,1024]{1,0:T(8,128)(2,1)} %constant.22.clone.cosine_ref, bf16[1024,1024]{1,0:T(8,128)(2,1)} %constant.23.clone.sine_ref, ...), custom_call_target="tpu_custom_call" | custom-call | bytes 65536 | tf_op jit(solution)/shard_map/second_transform/pallas_call | solution.py:236
  163.1 1.5 collective-permute-start.5
  164.6 6.5 %first_transform.7 = (bf16[8,2,16,16,128]{4,3,2,1,0:T(8,128)(2,1)}, f32[8,128]{1,0:T(8,128)}) custom-call(bf16[256,1024]{1,0:T(8,128)(2,1)} %constant.25.clone.table_ref, bf16[2,16,128,1024]{3,2,1,0:T(8,128)(2,1)} %grid_ref.7, bf16[48,16,1024]{2,1,0:T(8,128)(2,1)} %get-tuple-element.39.after_ref.refs_0_.refs_8_), custom_call_target="tpu_custom_call" | custom-call | bytes 65536 | tf_op jit(solution)/shard_map/first_transform/pallas_call | solution.py:112
  171.1 27.9 %all-to-all-done.1.half_ref = bf16[8,2,16,32,128]{4,3,2,1,0:T(8,128)(2,1)} async-done(((bf16[8,2,16,32,128]{4,3,2,1,0:T(8,128)(2,1)}), bf16[8,2,16,32,128]{4,3,2,1,0:T(8,128)(2,1)}, u32[]{:S(2)}, u32[]{:S(2)}) %all-to-all-start.1) | async-done | bytes 2097184 | tf_op jit(solution)/shard_map/all_to_all | solution.py:479
  199.0 7.5 %all-to-all-start.3 = ((bf16[8,2,16,16,128]{4,3,2,1,0:T(8,128)(2,1)}), bf16[8,2,16,16,128]{4,3,2,1,0:T(8,128)(2,1)}, u32[]{:S(2)}, u32[]{:S(2)}) async-start(bf16[8,2,16,16,128]{4,3,2,1,0:T(8,128)(2,1)} %get-tuple-element.42), calls=%async_computation.3 | async-start | bytes 2097152 | tf_op jit(solution)/shard_map/all_to_all | solution.py:479
  206.6 0.0 collective-permute-start.6
  206.6 0.0 collective-permute-done.5.value_ref
  206.6 0.5 collective-permute-start.7
  207.1 7.3 %second_transform.6 = (f32[16,32,1024]{2,1,0:T(8,128)}, bf16[32,16,1024]{2,1,0:T(8,128)(2,1)}) custom-call(f32[16]{0:T(128)} %step_ref.9, bf16[8,2,16,32,128]{4,3,2,1,0:T(8,128)(2,1)} %all-to-all-done.1.half_ref, bf16[1024,1024]{1,0:T(8,128)(2,1)} %constant.22.clone.cosine_ref, bf16[1024,1024]{1,0:T(8,128)(2,1)} %constant.23.clone.sine_ref, ...), custom_call_target="tpu_custom_call" | custom-call | bytes 65536 | tf_op jit(solution)/shard_map/second_transform/pallas_call | solution.py:236
  214.4 1.5 collective-permute-start.8
  215.9 6.5 %gram_step.4.after_ref.before_ref = f32[256,256]{1,0:T(8,128)} custom-call(f32[256,256]{1,0:T(8,128)} %gram_step.3.after_ref.before_ref, bf16[32,16,1024]{2,1,0:T(8,128)(2,1)} %get-tuple-element.41.after_ref.refs_0_.refs_12_, bf16[48,16,1024]{2,1,0:T(8,128)(2,1)} %get-tuple-element.39.after_ref.refs_0_.refs_8_, bf16[48,16,1024]{2,1,0:T(8,128)(2,1)} %gate.11.refs_1_.refs_9_, ...), custom_call_target="tpu_custom_call" | custom-call | bytes 65536 | tf_op jit(solution)/shard_map/gram_step/pallas_call | solution.py:283
  222.4 6.2 %all-to-all-done.3.half_ref = bf16[8,2,16,16,128]{4,3,2,1,0:T(8,128)(2,1)} async-done(((bf16[8,2,16,16,128]{4,3,2,1,0:T(8,128)(2,1)}), bf16[8,2,16,16,128]{4,3,2,1,0:T(8,128)(2,1)}, u32[]{:S(2)}, u32[]{:S(2)}) %all-to-all-start.3) | async-done | bytes 1048608 | tf_op jit(solution)/shard_map/all_to_all | solution.py:479
  228.7 5.6 %second_transform.7 = (f32[16,16,1024]{2,1,0:T(8,128)}, bf16[16,16,1024]{2,1,0:T(8,128)(2,1)}) custom-call(f32[16]{0:T(128)} %step_ref.9, bf16[8,2,16,16,128]{4,3,2,1,0:T(8,128)(2,1)} %all-to-all-done.3.half_ref, bf16[1024,1024]{1,0:T(8,128)(2,1)} %constant.22.clone.cosine_ref, bf16[1024,1024]{1,0:T(8,128)(2,1)} %constant.23.clone.sine_ref, ...), custom_call_target="tpu_custom_call" | custom-call | bytes 65536 | tf_op jit(solution)/shard_map/second_transform/pallas_call | solution.py:236
  234.3 5.5 %collective-permute-done.8.value_ref = bf16[32,16,1024]{2,1,0:T(8,128)(2,1)} collective-permute-done((bf16[32,16,1024]{2,1,0:T(8,128)(2,1)}, bf16[32,16,1024]{2,1,0:T(8,128)(2,1)}, u32[]{:S(2)}, u32[]{:S(2)}) %collective-permute-start.8) | collective-permute-done | bytes 1048608 | tf_op jit(solution)/shard_map/ppermute | solution.py:429
  239.8 0.0 collective-permute-start.10
  239.8 1.5 collective-permute-start.11
  241.3 0.2 collective-permute-start.12
  241.6 0.0 collective-permute-done.9.refs_2_.refs_14_
  241.6 1.3 collective-permute-done.10.refs_3_.refs_15_
  242.8 4.8 %gram_step.5.after_ref.gram_ref = f32[256,256]{1,0:T(8,128)} custom-call(f32[256,256]{1,0:T(8,128)} %gram_step.4.after_ref.before_ref, bf16[16,16,1024]{2,1,0:T(8,128)(2,1)} %get-tuple-element.44.after_ref.refs_16_, bf16[32,16,1024]{2,1,0:T(8,128)(2,1)} %get-tuple-element.41.after_ref.refs_0_.refs_12_, bf16[32,16,1024]{2,1,0:T(8,128)(2,1)} %gate.12.refs_1_.refs_13_, ...), custom_call_target="tpu_custom_call" | custom-call | bytes 65536 | tf_op jit(solution)/shard_map/gram_step/pallas_call | solution.py:283
  247.6 6.6 %collective-permute-done.11.value_ref = bf16[16,16,1024]{2,1,0:T(8,128)(2,1)} collective-permute-done((bf16[16,16,1024]{2,1,0:T(8,128)(2,1)S(1)}, bf16[16,16,1024]{2,1,0:T(8,128)(2,1)}, u32[]{:S(2)}, u32[]{:S(2)}) %collective-permute-start.11) | collective-permute-done | bytes 524320 | tf_op jit(solution)/shard_map/ppermute | solution.py:429
  254.9 1.6 collective-permute-done.13.refs_19_
  256.5 11.3 %polar_step.1 = f32[16,128,1024]{2,1,0:T(8,128)} custom-call(f32[1]{0:T(128)S(6)} %copy.26.shrink_ref, f32[256,256]{1,0:T(8,128)} %gram_step.5.after_ref.gram_ref, f32[16,32,1024]{2,1,0:T(8,128)} %get-tuple-element.45.refs_0_, f32[16,48,1024]{2,1,0:T(8,128)} %get-tuple-element.46.refs_1_, f32[16,32,1024]{2,1,0:T(8,128)} %get-tuple-element.47.refs_2_, ...), custom_call_target="tpu_custom_call" | custom-call | bytes 65536 | tf_op jit(solution)/shard_map/polar_step/pallas_call | solution.py:401
  (17 shorter events, 0.0 us)
Async XLA Ops:
  8.5 64.4 %all-to-all-start = ((bf16[8,2,16,32,128]{4,3,2,1,0:T(8,128)(2,1)}), bf16[8,2,16,32,128]{4,3,2,1,0:T(8,128)(2,1)}, u32[]{:S(2)}, u32[]{:S(2)}) async-start(bf16[8,2,16,32,128]{4,3,2,1,0:T(8,128)(2,1)} %get-tuple-element.27), calls=%async_computation | async-start | bytes 4194304 | tf_op jit(solution)/shard_map/all_to_all | solution.py:479
  17.5 53.4 %collective-permute-start = (bf16[16,12,1024]{2,1,0:T(8,128)(2,1)}, bf16[16,12,1024]{2,1,0:T(8,128)(2,1)S(1)}, u32[]{:S(2)}, u32[]{:S(2)}) collective-permute-start(bf16[16,12,1024]{2,1,0:T(8,128)(2,1)} %get-tuple-element.28), channel_id=1, source_target_pairs={{0,4},{4,8},{8,12},{12,16},{16,20},{20,24},{24,28},{1,5},{5,9},{9,... | collective-permute-start | bytes 1179656 | tf_op jit(solution)/shard_map/ppermute | solution.py:422
  20.9 51.9 %collective-permute-start.1 = (bf16[16,12,1024]{2,1,0:T(8,128)(2,1)}, bf16[16,12,1024]{2,1,0:T(8,128)(2,1)}, u32[]{:S(2)}, u32[]{:S(2)}) collective-permute-start(bf16[16,12,1024]{2,1,0:T(8,128)(2,1)} %get-tuple-element.29), channel_id=1, source_target_pairs={{4,0},{8,4},{12,8},{16,12},{20,16},{24,20},{28,24},{5,1},{9,5},{13... | collective-permute-start | bytes 1179656 | tf_op jit(solution)/shard_map/ppermute | solution.py:423
  70.9 0.8 copy-start.1
  72.8 5.1 %copy-start.2 = (bf16[16,12,1024]{2,1,0:T(8,128)(2,1)S(1)}, bf16[16,12,1024]{2,1,0:T(8,128)(2,1)}, u32[]{:S(2)}) copy-start(bf16[16,12,1024]{2,1,0:T(8,128)(2,1)} %copy-done.1) | copy-start | bytes 1179652
  72.8 72.7 %all-to-all-start.2 = ((bf16[8,2,16,48,128]{4,3,2,1,0:T(8,128)(2,1)}), bf16[8,2,16,48,128]{4,3,2,1,0:T(8,128)(2,1)}, u32[]{:S(2)}, u32[]{:S(2)}) async-start(bf16[8,2,16,48,128]{4,3,2,1,0:T(8,128)(2,1)} %gate.10), calls=%async_computation.2 | async-start | bytes 6291456 | tf_op jit(solution)/shard_map/all_to_all | solution.py:479
  98.5 24.8 %collective-permute-start.2 = (bf16[32,16,1024]{2,1,0:T(8,128)(2,1)}, bf16[32,16,1024]{2,1,0:T(8,128)(2,1)}, u32[]{:S(2)}, u32[]{:S(2)}) collective-permute-start(bf16[32,16,1024]{2,1,0:T(8,128)(2,1)} %get-tuple-element.33.after_ref.refs_0_.refs_4_), channel_id=1, source_target_pairs={{0,2},{1,3},{2,0},{3,1},{4,6},{5,7},{6,4},{7,5},{8,10},{9,11},{10,... | collective-permute-start | bytes 3145736 | tf_op jit(solution)/shard_map/ppermute | solution.py:429
  100.0 23.4 %collective-permute-start.3 = (bf16[32,16,1024]{2,1,0:T(8,128)(2,1)}, bf16[32,16,1024]{2,1,0:T(8,128)(2,1)}, u32[]{:S(2)}, u32[]{:S(2)}) collective-permute-start(bf16[32,16,1024]{2,1,0:T(8,128)(2,1)} %get-tuple-element.33.after_ref.refs_0_.refs_4_), channel_id=1, source_target_pairs={{0,1},{1,0},{2,3},{3,2},{4,5},{5,4},{6,7},{7,6},{8,9},{9,8},{10,11... | collective-permute-start | bytes 3145736 | tf_op jit(solution)/shard_map/ppermute | solution.py:429
  123.4 3.0 %collective-permute-start.4 = (bf16[32,16,1024]{2,1,0:T(8,128)(2,1)}, bf16[32,16,1024]{2,1,0:T(8,128)(2,1)}, u32[]{:S(2)}, u32[]{:S(2)}) collective-permute-start(bf16[32,16,1024]{2,1,0:T(8,128)(2,1)} %gate.7.refs_1_.refs_5_), channel_id=1, source_target_pairs={{0,1},{1,0},{2,3},{3,2},{4,5},{5,4},{6,7},{7,6},{8,9},{9,8},{10,11... | collective-permute-start | bytes 3145736 | tf_op jit(solution)/shard_map/ppermute | solution.py:429
  145.5 53.5 %all-to-all-start.1 = ((bf16[8,2,16,32,128]{4,3,2,1,0:T(8,128)(2,1)}), bf16[8,2,16,32,128]{4,3,2,1,0:T(8,128)(2,1)}, u32[]{:S(2)}, u32[]{:S(2)}) async-start(bf16[8,2,16,32,128]{4,3,2,1,0:T(8,128)(2,1)} %gate.8), calls=%async_computation.1 | async-start | bytes 4194304 | tf_op jit(solution)/shard_map/all_to_all | solution.py:479
  163.1 43.5 %collective-permute-start.5 = (bf16[48,16,1024]{2,1,0:T(8,128)(2,1)}, bf16[48,16,1024]{2,1,0:T(8,128)(2,1)}, u32[]{:S(2)}, u32[]{:S(2)}) collective-permute-start(bf16[48,16,1024]{2,1,0:T(8,128)(2,1)} %get-tuple-element.39.after_ref.refs_0_.refs_8_), channel_id=1, source_target_pairs={{0,2},{1,3},{2,0},{3,1},{4,6},{5,7},{6,4},{7,5},{8,10},{9,11},{10,... | collective-permute-start | bytes 4718600 | tf_op jit(solution)/shard_map/ppermute | solution.py:429
  199.0 29.6 %all-to-all-start.3 = ((bf16[8,2,16,16,128]{4,3,2,1,0:T(8,128)(2,1)}), bf16[8,2,16,16,128]{4,3,2,1,0:T(8,128)(2,1)}, u32[]{:S(2)}, u32[]{:S(2)}) async-start(bf16[8,2,16,16,128]{4,3,2,1,0:T(8,128)(2,1)} %get-tuple-element.42), calls=%async_computation.3 | async-start | bytes 2097152 | tf_op jit(solution)/shard_map/all_to_all | solution.py:479
  206.6 9.3 %collective-permute-start.6 = (bf16[48,16,1024]{2,1,0:T(8,128)(2,1)}, bf16[48,16,1024]{2,1,0:T(8,128)(2,1)}, u32[]{:S(2)}, u32[]{:S(2)}) collective-permute-start(bf16[48,16,1024]{2,1,0:T(8,128)(2,1)} %get-tuple-element.39.after_ref.refs_0_.refs_8_), channel_id=1, source_target_pairs={{0,1},{1,0},{2,3},{3,2},{4,5},{5,4},{6,7},{7,6},{8,9},{9,8},{10,11... | collective-permute-start | bytes 4718600 | tf_op jit(solution)/shard_map/ppermute | solution.py:429
  206.6 9.3 %collective-permute-start.7 = (bf16[48,16,1024]{2,1,0:T(8,128)(2,1)}, bf16[48,16,1024]{2,1,0:T(8,128)(2,1)}, u32[]{:S(2)}, u32[]{:S(2)}) collective-permute-start(bf16[48,16,1024]{2,1,0:T(8,128)(2,1)} %gate.11.refs_1_.refs_9_), channel_id=1, source_target_pairs={{0,1},{1,0},{2,3},{3,2},{4,5},{5,4},{6,7},{7,6},{8,9},{9,8},{10,11... | collective-permute-start | bytes 4718600 | tf_op jit(solution)/shard_map/ppermute | solution.py:429
  214.4 25.5 %collective-permute-start.8 = (bf16[32,16,1024]{2,1,0:T(8,128)(2,1)}, bf16[32,16,1024]{2,1,0:T(8,128)(2,1)}, u32[]{:S(2)}, u32[]{:S(2)}) collective-permute-start(bf16[32,16,1024]{2,1,0:T(8,128)(2,1)} %get-tuple-element.41.after_ref.refs_0_.refs_12_), channel_id=1, source_target_pairs={{0,2},{1,3},{2,0},{3,1},{4,6},{5,7},{6,4},{7,5},{8,10},{9,11},{10,... | collective-permute-start | bytes 3145736 | tf_op jit(solution)/shard_map/ppermute | solution.py:429
  215.9 25.7 %collective-permute-start.9 = (bf16[32,16,1024]{2,1,0:T(8,128)(2,1)}, bf16[32,16,1024]{2,1,0:T(8,128)(2,1)}, u32[]{:S(2)}, u32[]{:S(2)}) collective-permute-start(bf16[32,16,1024]{2,1,0:T(8,128)(2,1)} %get-tuple-element.41.after_ref.refs_0_.refs_12_), channel_id=1, source_target_pairs={{0,1},{1,0},{2,3},{3,2},{4,5},{5,4},{6,7},{7,6},{8,9},{9,8},{10,11... | collective-permute-start | bytes 3145736 | tf_op jit(solution)/shard_map/ppermute | solution.py:429
  234.3 5.5 %copy-start = (bf16[16,16,1024]{2,1,0:T(8,128)(2,1)S(1)}, bf16[16,16,1024]{2,1,0:T(8,128)(2,1)}, u32[]{:S(2)}) copy-start(bf16[16,16,1024]{2,1,0:T(8,128)(2,1)} %get-tuple-element.44.after_ref.refs_16_) | copy-start | bytes 1572868
  239.8 3.0 %collective-permute-start.10 = (bf16[32,16,1024]{2,1,0:T(8,128)(2,1)}, bf16[32,16,1024]{2,1,0:T(8,128)(2,1)}, u32[]{:S(2)}, u32[]{:S(2)}) collective-permute-start(bf16[32,16,1024]{2,1,0:T(8,128)(2,1)} %gate.12.refs_1_.refs_13_), channel_id=1, source_target_pairs={{0,1},{1,0},{2,3},{3,2},{4,5},{5,4},{6,7},{7,6},{8,9},{9,8},{10,11... | collective-permute-start | bytes 3145736 | tf_op jit(solution)/shard_map/ppermute | solution.py:429
  239.8 14.4 %collective-permute-start.11 = (bf16[16,16,1024]{2,1,0:T(8,128)(2,1)S(1)}, bf16[16,16,1024]{2,1,0:T(8,128)(2,1)}, u32[]{:S(2)}, u32[]{:S(2)}) collective-permute-start(bf16[16,16,1024]{2,1,0:T(8,128)(2,1)S(1)} %copy-done), channel_id=1, source_target_pairs={{0,2},{1,3},{2,0},{3,1},{4,6},{5,7},{6,4},{7,5},{8,10},{9,11},{10,... | collective-permute-start | bytes 1572872 | tf_op jit(solution)/shard_map/ppermute | solution.py:429
  241.3 13.6 %collective-permute-start.12 = (bf16[16,16,1024]{2,1,0:T(8,128)(2,1)S(1)}, bf16[16,16,1024]{2,1,0:T(8,128)(2,1)}, u32[]{:S(2)}, u32[]{:S(2)}) collective-permute-start(bf16[16,16,1024]{2,1,0:T(8,128)(2,1)S(1)} %copy-done), channel_id=1, source_target_pairs={{0,1},{1,0},{2,3},{3,2},{4,5},{5,4},{6,7},{7,6},{8,9},{9,8},{10,11... | collective-permute-start | bytes 1572872 | tf_op jit(solution)/shard_map/ppermute | solution.py:429
  254.3 2.3 collective-permute-start.13

commit v15 on v14

--- a/solution.py
+++ b/solution.py
@@ -56,11 +56,16 @@
     return cosine, sine_table
 
 
-def chunk_rows(own_rows):
-    quarter = own_rows // 4
-    sizes = [quarter, own_rows - 2 * quarter - EDGE_ROWS, quarter, EDGE_ROWS]
-    sizes = [size for size in sizes if size > 0]
-    return [sum(sizes[:place]) for place in range(len(sizes))], sizes
+def chunk_blocks(own_rows, reach):
+    blocks = list(range(0, own_rows, EDGE_ROWS))
+    near = [row for row in blocks if row < reach or row + EDGE_ROWS > own_rows - reach]
+    inner = [row for row in blocks if row not in near]
+    quarter = len(blocks) // 4
+    sizes = [quarter, len(blocks) - 2 * quarter - 1, quarter, 1]
+    ahead = sizes[0] + sizes[1]
+    order = inner[:ahead] + near + inner[ahead:]
+    chunks = [order[sum(sizes[:place]) : sum(sizes[: place + 1])] for place in range(len(sizes))]
+    return chunks, [any(row in near for row in chunk) for chunk in chunks]
 
 
 def gate_body(value_ref, after_ref, out_ref):
@@ -148,11 +153,10 @@
     return total
 
 
-def base_body(levels, taps, starts, strips, strip_ref, step_ref, highpass_ref, model_ref, edge_ref, after_ref, *refs):
+def base_body(levels, taps, blocks, strips, reach, with_edges, strip_ref, step_ref, highpass_ref, model_ref, *refs):
     high, low = refs[-2:]
-    out_refs = refs[:-2]
-    block, own_rows, side_len = model_ref.shape
-    reach = edge_ref.shape[1] // 2
+    out_refs = refs[2:-2] if with_edges else refs[1:-2]
+    count, own_rows, side_len = model_ref.shape
 
     @pl.when(pl.program_id(0) == 0)
     def _():
@@ -169,45 +173,43 @@
         high[...] = top
         low[...] = (band - top.astype(F32)).astype(BF16)
 
-    first = pl.program_id(0) * block
-    for chan in range(block):
+    wide = own_rows + 2 * reach if with_edges else own_rows
+    first = pl.program_id(0) * count
+    for chan in range(count):
         model = model_ref[chan]
         top = model.astype(BF16)
         rest = (model - top.astype(F32)).astype(BF16)
-        edge = edge_ref[chan].astype(F32)
-        whole = jnp.concatenate([top.astype(F32), edge], axis=0).astype(BF16)
-        gradient = dot_nn(high[...], whole)
-        gradient = gradient + dot_nn(low[...], whole)
+        whole = top
+        if with_edges:
+            whole = jnp.concatenate([top.astype(F32), refs[0][chan].astype(F32)], axis=0).astype(BF16)
+        gradient = dot_nn(high[:, :wide], whole)
+        gradient = gradient + dot_nn(low[:, :wide], whole)
         gradient = gradient + dot_nn(high[:, :own_rows], rest)
         base = model - step_ref[first + chan] * gradient
-        for start, out_ref in zip(starts, out_refs):
-            out_ref[chan] = base[start : start + out_ref.shape[1]]
-
-
-def base_step(strip, strips, step_size, highpass, model_image, edges, starts, sizes, after):
+        for rows, out_ref in zip(blocks, out_refs):
+            for place, row in enumerate(rows):
+                out_ref[chan, place * EDGE_ROWS : (place + 1) * EDGE_ROWS] = base[row : row + EDGE_ROWS]
+
+
+def base_step(strip, strips, step_size, highpass, model_image, edges, reach, blocks, after):
     chans, rows, side_len = model_image.shape
     levels, taps = highpass.shape
-    reach = edges.shape[1] // 2
-    block = 2 if chans % 2 == 0 else 1
+    count = 2 if chans % 2 == 0 else 1
     wide = rows + 2 * reach
+    sizes = [len(chunk) * EDGE_ROWS for chunk in blocks]
+    with_edges = edges is not None
+    edge_specs = [pl.BlockSpec((count, 2 * reach, side_len), lambda i: (i, 0, 0))] if with_edges else []
     return pl.pallas_call(
-        functools.partial(base_body, levels, taps, starts, strips),
-        grid=(chans // block,),
-        in_specs=[
-            SMEM,
-            SMEM,
-            SMEM,
-            pl.BlockSpec((block, rows, side_len), lambda i: (i, 0, 0)),
-            pl.BlockSpec((block, 2 * reach, side_len), lambda i: (i, 0, 0)),
-            ANY,
-        ],
-        out_specs=[pl.BlockSpec((block, part, side_len), lambda i: (i, 0, 0)) for part in sizes],
+        functools.partial(base_body, levels, taps, blocks, strips, reach, with_edges),
+        grid=(chans // count,),
+        in_specs=[SMEM, SMEM, SMEM, pl.BlockSpec((count, rows, side_len), lambda i: (i, 0, 0))] + edge_specs + [ANY],
+        out_specs=[pl.BlockSpec((count, part, side_len), lambda i: (i, 0, 0)) for part in sizes],
         out_shape=[jax.ShapeDtypeStruct((chans, part, side_len), F32) for part in sizes],
         scratch_shapes=[pltpu.VMEM((rows, wide), BF16), pltpu.VMEM((rows, wide), BF16)],
         compiler_params=kernel_params(63),
         cost_estimate=COST,
         name="base_step",
-    )(strip, step_size, highpass, model_image, edges, after)
+    )(strip, step_size, highpass, model_image, *([edges] if with_edges else []), after)
 
 
 def second_body(step_ref, half_ref, cosine_ref, sine_ref, base_ref, after_ref, moved_ref, pixels_ref):
@@ -306,8 +308,9 @@
     return inverse, frob_norm
 
 
-def polar_body(starts, sizes, groups, shrink_ref, gram_ref, *refs):
-    chunks = len(sizes)
+def polar_body(block_rows, groups, shrink_ref, gram_ref, *refs):
+    chunks = len(block_rows)
+    sizes = [len(rows) * EDGE_ROWS for rows in block_rows]
     moved_hbm = refs[:chunks]
     pixels_hbm = refs[chunks : chunks * (groups + 1)]
     out_hbm, moved, pixel_sems, moved_sems, out_sems = refs[chunks * (groups + 1) : chunks * (groups + 1) + 5]
@@ -323,7 +326,7 @@
     moved_copies = []
     for place, (chunk, row) in enumerate(blocks):
         part = pl.ds(row, EDGE_ROWS)
-        into = pl.ds(starts[chunk] + row, EDGE_ROWS)
+        into = pl.ds(block_rows[chunk][row // EDGE_ROWS], EDGE_ROWS)
         copies = [
             pltpu.make_async_copy(
                 pixels_hbm[chunk * groups + group].at[part], pixels[chunk].at[group, part], pixel_sems.at[place, group]
@@ -376,14 +379,14 @@
                 copy.wait()
         moved_copies[place].wait()
         for first in range(row, row + EDGE_ROWS, POLAR_ROWS):
-            into = starts[chunk] + first
+            into = block_rows[chunk][row // EDGE_ROWS] + first - row
             rows = moved[:, into : into + POLAR_ROWS]
             data = stacked([pixels[chunk].at[group] for group in range(far, groups)], first, POLAR_ROWS)
             if far:
                 data = jnp.concatenate([rows.reshape(spread, side_len).astype(BF16), data], axis=0)
             polar = dot_nn(far_weights, data).reshape(own, POLAR_ROWS, side_len)
             moved[:, into : into + POLAR_ROWS] = rows - polar
-        part = pl.ds(starts[chunk] + row, EDGE_ROWS)
+        part = pl.ds(block_rows[chunk][row // EDGE_ROWS], EDGE_ROWS)
         copy = pltpu.make_async_copy(moved.at[:, part], out_hbm.at[:, part], out_sems.at[place])
         copy.start()
         out_copies.append(copy)
@@ -391,15 +394,15 @@
         copy.wait()
 
 
-def polar_step(shrinkage, gram, moved, gathered, starts, sizes):
+def polar_step(shrinkage, gram, moved, gathered, block_rows):
     chunks = len(gathered)
     groups = len(gathered[0])
     chans, _, side_len = moved[0].shape
-    shape = (chans, sum(sizes), side_len)
-    blocks = sum(sizes) // EDGE_ROWS
+    blocks = sum(len(rows) for rows in block_rows)
+    shape = (chans, blocks * EDGE_ROWS, side_len)
     flat = [piece for pieces in gathered for piece in pieces]
     return pl.pallas_call(
-        functools.partial(polar_body, starts, sizes, groups),
+        functools.partial(polar_body, block_rows, groups),
         in_specs=[SMEM, pl.BlockSpec(memory_space=pltpu.VMEM)] + [ANY] * (chunks + len(flat)),
         out_specs=ANY,
         out_shape=jax.ShapeDtypeStruct(shape, F32),
@@ -443,19 +446,19 @@
     chans, own_rows, side_len = model_image.shape
     strips = lax.axis_size("strip")
     size = chans * lax.axis_size("chan")
-    starts, sizes = chunk_rows(own_rows)
-    chunks = len(sizes)
+    levels, taps = highpass.shape
+    reach = (taps - 1) * 2 ** (levels - 1)
+    blocks, near = chunk_blocks(own_rows, reach)
+    chunks = len(blocks)
     strip = lax.axis_index("strip").astype(jnp.int32).reshape(1)
 
     cosine, sine_table = make_tables(side_len)
     split = np.stack([cosine.reshape(strips, own_rows, side_len), sine_table.reshape(strips, own_rows, side_len)])
     tables = [
-        np.ascontiguousarray(split[:, :, start : start + rows]).reshape(2 * strips * rows, side_len)
-        for start, rows in zip(starts, sizes)
+        np.concatenate([split[:, :, row : row + EDGE_ROWS] for row in rows], axis=2).reshape(-1, side_len)
+        for rows in blocks
     ]
 
-    levels, taps = highpass.shape
-    reach = (taps - 1) * 2 ** (levels - 1)
     sides = neighbour_rows(model_image, reach)
     edges = jnp.concatenate(sides, axis=1)
 
@@ -464,25 +467,33 @@
     gathered = {}
     pixels = {}
     done = set()
-    state = dict(last=strip, gram=jnp.zeros((GRAM_ROWS * size, GRAM_ROWS * size), F32), bases=None)
+    state = dict(last=strip, gram=jnp.zeros((GRAM_ROWS * size, GRAM_ROWS * size), F32), bases={})
 
     def first(chunk):
         sent, state["last"] = first_transform(tables[chunk], grid, strips, state["last"])
-        if chunk == 1:
-            for side in sides:
-                sent = gate(sent, side)
         if chunk == 2:
             gather(0)
             gram(0)
             done.add(0)
-            sent = gate(sent, state["gram"])
+            for value in [state["gram"]] + list(sides):
+                sent = gate(sent, value)
         halves[chunk] = lax.all_to_all(sent, "strip", split_axis=0, concat_axis=0, tiled=True)
 
-    def base():
-        state["bases"] = base_step(
-            strip, strips, step_size, highpass, model_image, edges, starts, sizes, state["last"]
+    def base(with_edges):
+        wanted = [chunk for chunk in range(chunks) if near[chunk] == with_edges]
+        results = base_step(
+            strip,
+            strips,
+            step_size,
+            highpass,
+            model_image,
+            edges if with_edges else None,
+            reach,
+            [blocks[chunk] for chunk in wanted],
+            state["last"],
         )
-        state["last"] = state["bases"][0]
+        state["bases"].update(zip(wanted, results))
+        state["last"] = results[0]
 
     def second(chunk):
         moved[chunk], pixels[chunk] = second_transform(
@@ -503,12 +514,13 @@
     first(0)
     if chunks > 1:
         first(1)
-    base()
+    base(False)
     for chunk in range(chunks):
         second(chunk)
         if chunk + 2 < chunks:
             first(chunk + 2)
         if chunk == 1:
+            base(True)
             gather(1)
         if chunk >= 1 and chunk - 1 not in done:
             if chunk - 1 not in gathered:
@@ -518,7 +530,7 @@
         gather(chunks - 1)
     order = range(chunks)
     return polar_step(
-        shrinkage, state["gram"], [moved[k] for k in order], [gathered[k] for k in order], starts, sizes
+        shrinkage, state["gram"], [moved[k] for k in order], [gathered[k] for k in order], blocks
     )
 
 

time: 271 us -> 283 us (1.044)
  Pallas kernels: 102 us -> 110 us
    all_to_all x4, waiting for transfers between devices: 47.8 us -> 62.6 us  [first(): lax.all_to_all(sent, 'strip', split_axis=0, concat_axis=0, tiled=True)]
    ppermute x1, waiting for transfers between devices: 37.3 us -> 22.5 us  [neighbour_rows(): lax.ppermute(tail.astype(BF16), 'strip', [(i, i + 1) for i in range(ends)])]
    pallas_call x2 -> x3, Pallas kernels: 22.5 us -> 31.2 us  [the longest x2 19.9 us: base_step(): pl.pallas_call(functools.partial(base_body, levels, taps, blocks, strips,...]
  transfers between devices with their start and end apart: 18 -> 18, of which waited for: 11 -> 9; matrix products, arithmetic and copies ran while one was open for 2% -> 2% of each run, Pallas kernels for 31% -> 32%
where the time goes in v15:
time: 283 us; the launch traced here: 280 us
  waiting for transfers between devices  121 us (43%)
  Pallas kernels  110 us (39%)
  starting transfers between devices  41.2 us (15%)
  local copies, waits for them, and re-layouts  4.29 us (2%)
    all_to_all x4, waiting for transfers between devices, first(): lax.all_to_all(sent, 'strip', split_axis=0, concat_axis=0, tiled=True)  62.6 us
    ppermute x12, waiting for transfers between devices, swap(): return lax.ppermute(value, axis, [(i, i ^ bits) for i in range(count)])  35.2 us
    pallas_call x4, Pallas kernels, first_transform(): pl.pallas_call(first_body, grid=(chans // block,), in_specs=[pl.BlockSpec...  33.9 us
    pallas_call x4, Pallas kernels, second_transform(): pl.pallas_call(second_body, grid=(side_len // block,), in_specs=[SMEM, pl...  29.3 us
    all_to_all x4, starting transfers between devices, first(): lax.all_to_all(sent, 'strip', split_axis=0, concat_axis=0, tiled=True)  28.6 us
    ppermute x1, waiting for transfers between devices, neighbour_rows(): lax.ppermute(tail.astype(BF16), 'strip', [(i, i + 1) for i in range(ends)])  22.5 us
    pallas_call x2, Pallas kernels, base_step(): pl.pallas_call(functools.partial(base_body, levels, taps, blocks, strips,...  19.9 us
    pallas_call x3, Pallas kernels, gram_step(): pl.pallas_call(functools.partial(gram_body, len(pieces)), grid=(rows // b...  16.1 us
  transfers between devices with their start and end apart: 18, of which 9 were waited for; matrix products, arithmetic and copies ran while one was open for 2% of the time, Pallas kernels for 32%

profile of v15, /device:TPU:12, one launch (start us, length us, event | category | flops | bytes accessed | tf_op | source)
XLA Modules:
  0.0 280.3 jit_solution(3609115421378010878)
XLA Ops:
  0.0 8.5 %first_transform.4 = (bf16[8,2,16,32,128]{4,3,2,1,0:T(8,128)(2,1)}, f32[8,128]{1,0:T(8,128)}) custom-call(bf16[512,1024]{1,0:T(8,128)(2,1)} %constant.20.clone.table_ref, bf16[2,16,128,1024]{3,2,1,0:T(8,128)(2,1)} %grid_ref.7, s32[1]{0:T(128)} %bitcast.after_ref.strip_ref), custom_call_target="tpu_custom_call" | custom-call | bytes 65536 | tf_op jit(solution)/shard_map/first_transform/pallas_call | solution.py:117
  8.5 6.2 %all-to-all-start = ((bf16[8,2,16,32,128]{4,3,2,1,0:T(8,128)(2,1)}), bf16[8,2,16,32,128]{4,3,2,1,0:T(8,128)(2,1)}, u32[]{:S(2)}, u32[]{:S(2)}) async-start(bf16[8,2,16,32,128]{4,3,2,1,0:T(8,128)(2,1)} %get-tuple-element.26), calls=%async_computation | async-start | bytes 4194304 | tf_op jit(solution)/shard_map/all_to_all | solution.py:480
  14.7 10.3 %first_transform.5 = (bf16[8,2,16,48,128]{4,3,2,1,0:T(8,128)(2,1)}, f32[8,128]{1,0:T(8,128)}) custom-call(bf16[768,1024]{1,0:T(8,128)(2,1)} %constant.21.clone.table_ref, bf16[2,16,128,1024]{3,2,1,0:T(8,128)(2,1)} %grid_ref.7, f32[8,128]{1,0:T(8,128)} %get-tuple-element.27.after_ref), custom_call_target="tpu_custom_call" | custom-call | bytes 65536 | tf_op jit(solution)/shard_map/first_transform/pallas_call | solution.py:117
  25.0 34.6 %all-to-all-done.half_ref = bf16[8,2,16,32,128]{4,3,2,1,0:T(8,128)(2,1)} async-done(((bf16[8,2,16,32,128]{4,3,2,1,0:T(8,128)(2,1)}), bf16[8,2,16,32,128]{4,3,2,1,0:T(8,128)(2,1)}, u32[]{:S(2)}, u32[]{:S(2)}) %all-to-all-start) | async-done | bytes 2097184 | tf_op jit(solution)/shard_map/all_to_all | solution.py:480
  59.7 7.7 %all-to-all-start.2 = ((bf16[8,2,16,48,128]{4,3,2,1,0:T(8,128)(2,1)}), bf16[8,2,16,48,128]{4,3,2,1,0:T(8,128)(2,1)}, u32[]{:S(2)}, u32[]{:S(2)}) async-start(bf16[8,2,16,48,128]{4,3,2,1,0:T(8,128)(2,1)} %get-tuple-element.35), calls=%async_computation.2 | async-start | bytes 6291456 | tf_op jit(solution)/shard_map/all_to_all | solution.py:480
  67.4 10.2 %base_step.2 = (f32[16,32,1024]{2,1,0:T(8,128)}, f32[16,48,1024]{2,1,0:T(8,128)}, f32[16,16,1024]{2,1,0:T(8,128)}) custom-call(s32[1]{0:T(128)} %bitcast.after_ref.strip_ref, f32[16]{0:T(128)} %step_ref.11, f32[3,4]{1,0:T(4,128)} %highpass_ref.3, f32[16,128,1024]{2,1,0:T(8,128)} %model_ref.3, f32[8,128]{1,0:T(8,128)} %get-tuple-element.28.refs_0_), custom_call_target="tpu_custom_call" | custom-call | bytes 65536 | tf_op jit(solution)/shard_map/base_step/pallas_call | solution.py:202
  77.6 7.3 %second_transform.4 = (f32[16,32,1024]{2,1,0:T(8,128)}, bf16[32,16,1024]{2,1,0:T(8,128)(2,1)}) custom-call(f32[16]{0:T(128)} %step_ref.11, bf16[8,2,16,32,128]{4,3,2,1,0:T(8,128)(2,1)} %all-to-all-done.half_ref, bf16[1024,1024]{1,0:T(8,128)(2,1)} %constant.22.clone.cosine_ref, bf16[1024,1024]{1,0:T(8,128)(2,1)} %constant.23.clone.sine_ref, ...), custom_call_target="tpu_custom_call" | custom-call | bytes 65536 | tf_op jit(solution)/shard_map/second_transform/pallas_call | solution.py:238
  84.9 1.5 collective-permute-start
  86.4 0.0 collective-permute-start.1
  86.4 8.6 %first_transform.6 = (bf16[8,2,16,32,128]{4,3,2,1,0:T(8,128)(2,1)}, f32[8,128]{1,0:T(8,128)}) custom-call(bf16[512,1024]{1,0:T(8,128)(2,1)} %constant.24.clone.table_ref, bf16[2,16,128,1024]{3,2,1,0:T(8,128)(2,1)} %grid_ref.7, bf16[32,16,1024]{2,1,0:T(8,128)(2,1)} %get-tuple-element.30.after_ref.refs_0_.refs_4_), custom_call_target="tpu_custom_call" | custom-call | bytes 65536 | tf_op jit(solution)/shard_map/first_transform/pallas_call | solution.py:117
  95.0 14.1 %collective-permute-done.value_ref = bf16[32,16,1024]{2,1,0:T(8,128)(2,1)} collective-permute-done((bf16[32,16,1024]{2,1,0:T(8,128)(2,1)}, bf16[32,16,1024]{2,1,0:T(8,128)(2,1)}, u32[]{:S(2)}, u32[]{:S(2)}) %collective-permute-start) | collective-permute-done | bytes 1048608 | tf_op jit(solution)/shard_map/ppermute | solution.py:432
  109.0 0.0 collective-permute-start.2
  109.0 2.7 fusion
  111.8 3.4 %collective-permute-start.3 = (bf16[16,12,1024]{2,1,0:T(8,128)(2,1)}, bf16[16,12,1024]{2,1,0:T(8,128)(2,1)S(1)}, u32[]{:S(2)}, u32[]{:S(2)}) collective-permute-start(bf16[16,12,1024]{2,1,0:T(8,128)(2,1)} %get-tuple-element.33), channel_id=1, source_target_pairs={{0,4},{4,8},{8,12},{12,16},{16,20},{20,24},{24,28},{1,5},{5,9},{9,... | collective-permute-start | bytes 1179656 | tf_op jit(solution)/shard_map/ppermute | solution.py:425
  115.2 2.5 collective-permute-start.4
  117.6 0.0 collective-permute-done.1.refs_2_.refs_6_
  117.6 0.0 collective-permute-done.2.refs_3_.refs_7_
  117.7 0.7 broadcast_in_dim.3.before_ref
  118.4 4.8 %gram_step.3.after_ref.before_ref = f32[256,256]{1,0:T(8,128)} custom-call(f32[256,256]{1,0:T(8,128)} %broadcast_in_dim.3.before_ref, f32[8,128]{1,0:T(8,128)} %get-tuple-element.31.after_ref, bf16[32,16,1024]{2,1,0:T(8,128)(2,1)} %get-tuple-element.30.after_ref.refs_0_.refs_4_, bf16[32,16,1024]{2,1,0:T(8,128)(2,1)} %gate.7.refs_1_.refs_5_, ...), custom_call_target="tpu_custom_call" | custom-call | bytes 65536 | tf_op jit(solution)/shard_map/gram_step/pallas_call | solution.py:285
  123.1 22.5 %collective-permute-done.3.after_ref = bf16[16,12,1024]{2,1,0:T(8,128)(2,1)S(1)} collective-permute-done((bf16[16,12,1024]{2,1,0:T(8,128)(2,1)}, bf16[16,12,1024]{2,1,0:T(8,128)(2,1)S(1)}, u32[]{:S(2)}, u32[]{:S(2)}) %collective-permute-start.3) | collective-permute-done | bytes 393248 | tf_op jit(solution)/shard_map/ppermute | solution.py:425
  145.7 0.8 copy-done.1
  146.5 1.0 collective-permute-done.4.after_ref
  147.5 6.2 %all-to-all-start.1 = ((bf16[8,2,16,32,128]{4,3,2,1,0:T(8,128)(2,1)}), bf16[8,2,16,32,128]{4,3,2,1,0:T(8,128)(2,1)}, u32[]{:S(2)}, u32[]{:S(2)}) async-start(bf16[8,2,16,32,128]{4,3,2,1,0:T(8,128)(2,1)} %gate.10), calls=%async_computation.1 | async-start | bytes 4194304 | tf_op jit(solution)/shard_map/all_to_all | solution.py:480
  153.6 8.9 %second_transform.5 = (f32[16,48,1024]{2,1,0:T(8,128)}, bf16[48,16,1024]{2,1,0:T(8,128)(2,1)}) custom-call(f32[16]{0:T(128)} %step_ref.11, bf16[8,2,16,48,128]{4,3,2,1,0:T(8,128)(2,1)} %all-to-all-done.2.half_ref, bf16[1024,1024]{1,0:T(8,128)(2,1)} %constant.22.clone.cosine_ref, bf16[1024,1024]{1,0:T(8,128)(2,1)} %constant.23.clone.sine_ref, ...), custom_call_target="tpu_custom_call" | custom-call | bytes 65536 | tf_op jit(solution)/shard_map/second_transform/pallas_call | solution.py:238
  162.6 1.5 collective-permute-start.5
  164.1 6.5 %first_transform.7 = (bf16[8,2,16,16,128]{4,3,2,1,0:T(8,128)(2,1)}, f32[8,128]{1,0:T(8,128)}) custom-call(bf16[256,1024]{1,0:T(8,128)(2,1)} %constant.25.clone.table_ref, bf16[2,16,128,1024]{3,2,1,0:T(8,128)(2,1)} %grid_ref.7, bf16[48,16,1024]{2,1,0:T(8,128)(2,1)} %get-tuple-element.37.after_ref.refs_0_.refs_8_), custom_call_target="tpu_custom_call" | custom-call | bytes 65536 | tf_op jit(solution)/shard_map/first_transform/pallas_call | solution.py:117
  170.6 27.9 %all-to-all-done.1.half_ref = bf16[8,2,16,32,128]{4,3,2,1,0:T(8,128)(2,1)} async-done(((bf16[8,2,16,32,128]{4,3,2,1,0:T(8,128)(2,1)}), bf16[8,2,16,32,128]{4,3,2,1,0:T(8,128)(2,1)}, u32[]{:S(2)}, u32[]{:S(2)}) %all-to-all-start.1) | async-done | bytes 2097184 | tf_op jit(solution)/shard_map/all_to_all | solution.py:480
  198.6 8.4 %all-to-all-start.3 = ((bf16[8,2,16,16,128]{4,3,2,1,0:T(8,128)(2,1)}), bf16[8,2,16,16,128]{4,3,2,1,0:T(8,128)(2,1)}, u32[]{:S(2)}, u32[]{:S(2)}) async-start(bf16[8,2,16,16,128]{4,3,2,1,0:T(8,128)(2,1)} %get-tuple-element.40), calls=%async_computation.3 | async-start | bytes 2097152 | tf_op jit(solution)/shard_map/all_to_all | solution.py:480
  207.0 2.2 pad_maximum_fusion.refs_0_
  209.2 9.7 %base_step.3.base_ref.after_ref = f32[16,32,1024]{2,1,0:T(8,128)} custom-call(s32[1]{0:T(128)} %bitcast.after_ref.strip_ref, f32[16]{0:T(128)} %step_ref.11, f32[3,4]{1,0:T(4,128)} %highpass_ref.3, f32[16,128,1024]{2,1,0:T(8,128)} %model_ref.3, bf16[16,24,1024]{2,1,0:T(8,128)(2,1)} %pad_maximum_fusion.refs_0_, f32[8,128]{1,0:T(8,128)} %get-tuple-element.38.refs_1_), custom_call_target="tpu_custom_call" | custom-call | bytes 65536 | tf_op jit(solution)/shard_map/base_step/pallas_call | solution.py:202
  218.8 0.0 collective-permute-done.5.value_ref
  218.8 0.6 collective-permute-start.7
  219.4 7.3 %second_transform.6 = (f32[16,32,1024]{2,1,0:T(8,128)}, bf16[32,16,1024]{2,1,0:T(8,128)(2,1)}) custom-call(f32[16]{0:T(128)} %step_ref.11, bf16[8,2,16,32,128]{4,3,2,1,0:T(8,128)(2,1)} %all-to-all-done.1.half_ref, bf16[1024,1024]{1,0:T(8,128)(2,1)} %constant.22.clone.cosine_ref, bf16[1024,1024]{1,0:T(8,128)(2,1)} %constant.23.clone.sine_ref, ...), custom_call_target="tpu_custom_call" | custom-call | bytes 65536 | tf_op jit(solution)/shard_map/second_transform/pallas_call | solution.py:238
  226.7 1.5 collective-permute-start.8
  228.2 0.0 collective-permute-start.9
  228.2 0.0 collective-permute-done.6.refs_2_.refs_10_
  228.2 6.5 %gram_step.4.after_ref.before_ref = f32[256,256]{1,0:T(8,128)} custom-call(f32[256,256]{1,0:T(8,128)} %gram_step.3.after_ref.before_ref, bf16[32,16,1024]{2,1,0:T(8,128)(2,1)} %get-tuple-element.39.after_ref.refs_0_.refs_12_, bf16[48,16,1024]{2,1,0:T(8,128)(2,1)} %get-tuple-element.37.after_ref.refs_0_.refs_8_, bf16[48,16,1024]{2,1,0:T(8,128)(2,1)} %gate.11.refs_1_.refs_9_, ...), custom_call_target="tpu_custom_call" | custom-call | bytes 65536 | tf_op jit(solution)/shard_map/gram_step/pallas_call | solution.py:285
  234.7 5.7 %second_transform.7 = (f32[16,16,1024]{2,1,0:T(8,128)}, bf16[16,16,1024]{2,1,0:T(8,128)(2,1)}) custom-call(f32[16]{0:T(128)} %step_ref.11, bf16[8,2,16,16,128]{4,3,2,1,0:T(8,128)(2,1)} %all-to-all-done.3.half_ref, bf16[1024,1024]{1,0:T(8,128)(2,1)} %constant.22.clone.cosine_ref, bf16[1024,1024]{1,0:T(8,128)(2,1)} %constant.23.clone.sine_ref, ...), custom_call_target="tpu_custom_call" | custom-call | bytes 65536 | tf_op jit(solution)/shard_map/second_transform/pallas_call | solution.py:238
  240.5 11.6 %collective-permute-done.8.value_ref = bf16[32,16,1024]{2,1,0:T(8,128)(2,1)} collective-permute-done((bf16[32,16,1024]{2,1,0:T(8,128)(2,1)}, bf16[32,16,1024]{2,1,0:T(8,128)(2,1)}, u32[]{:S(2)}, u32[]{:S(2)}) %collective-permute-start.8) | collective-permute-done | bytes 1048608 | tf_op jit(solution)/shard_map/ppermute | solution.py:432
  252.1 0.0 collective-permute-start.10
  252.1 1.5 collective-permute-start.11
  253.6 0.2 collective-permute-start.12
  253.8 0.0 collective-permute-done.9.refs_2_.refs_14_
  253.8 1.3 collective-permute-done.10.refs_3_.refs_15_
  255.1 4.8 %gram_step.5.after_ref.gram_ref = f32[256,256]{1,0:T(8,128)} custom-call(f32[256,256]{1,0:T(8,128)} %gram_step.4.after_ref.before_ref, bf16[16,16,1024]{2,1,0:T(8,128)(2,1)} %get-tuple-element.42.after_ref.refs_16_, bf16[32,16,1024]{2,1,0:T(8,128)(2,1)} %get-tuple-element.39.after_ref.refs_0_.refs_12_, bf16[32,16,1024]{2,1,0:T(8,128)(2,1)} %gate.12.refs_1_.refs_13_, ...), custom_call_target="tpu_custom_call" | custom-call | bytes 65536 | tf_op jit(solution)/shard_map/gram_step/pallas_call | solution.py:285
  259.9 6.6 %collective-permute-done.11.value_ref = bf16[16,16,1024]{2,1,0:T(8,128)(2,1)} collective-permute-done((bf16[16,16,1024]{2,1,0:T(8,128)(2,1)S(1)}, bf16[16,16,1024]{2,1,0:T(8,128)(2,1)}, u32[]{:S(2)}, u32[]{:S(2)}) %collective-permute-start.11) | collective-permute-done | bytes 524320 | tf_op jit(solution)/shard_map/ppermute | solution.py:432
  267.2 1.6 collective-permute-done.13.refs_19_
  268.8 11.3 %polar_step.1 = f32[16,128,1024]{2,1,0:T(8,128)} custom-call(f32[1]{0:T(128)S(6)} %copy.26.shrink_ref, f32[256,256]{1,0:T(8,128)} %gram_step.5.after_ref.gram_ref, f32[16,32,1024]{2,1,0:T(8,128)} %get-tuple-element.43.refs_0_, f32[16,48,1024]{2,1,0:T(8,128)} %get-tuple-element.44.refs_1_, f32[16,32,1024]{2,1,0:T(8,128)} %get-tuple-element.45.refs_2_, ...), custom_call_target="tpu_custom_call" | custom-call | bytes 65536 | tf_op jit(solution)/shard_map/polar_step/pallas_call | solution.py:404
  (18 shorter events, 0.0 us)
Async XLA Ops:
  8.5 51.2 %all-to-all-start = ((bf16[8,2,16,32,128]{4,3,2,1,0:T(8,128)(2,1)}), bf16[8,2,16,32,128]{4,3,2,1,0:T(8,128)(2,1)}, u32[]{:S(2)}, u32[]{:S(2)}) async-start(bf16[8,2,16,32,128]{4,3,2,1,0:T(8,128)(2,1)} %get-tuple-element.26), calls=%async_computation | async-start | bytes 4194304 | tf_op jit(solution)/shard_map/all_to_all | solution.py:480
  59.7 87.8 %all-to-all-start.2 = ((bf16[8,2,16,48,128]{4,3,2,1,0:T(8,128)(2,1)}), bf16[8,2,16,48,128]{4,3,2,1,0:T(8,128)(2,1)}, u32[]{:S(2)}, u32[]{:S(2)}) async-start(bf16[8,2,16,48,128]{4,3,2,1,0:T(8,128)(2,1)} %get-tuple-element.35), calls=%async_computation.2 | async-start | bytes 6291456 | tf_op jit(solution)/shard_map/all_to_all | solution.py:480
  84.9 24.1 %collective-permute-start = (bf16[32,16,1024]{2,1,0:T(8,128)(2,1)}, bf16[32,16,1024]{2,1,0:T(8,128)(2,1)}, u32[]{:S(2)}, u32[]{:S(2)}) collective-permute-start(bf16[32,16,1024]{2,1,0:T(8,128)(2,1)} %get-tuple-element.30.after_ref.refs_0_.refs_4_), channel_id=1, source_target_pairs={{0,2},{1,3},{2,0},{3,1},{4,6},{5,7},{6,4},{7,5},{8,10},{9,11},{10,... | collective-permute-start | bytes 3145736 | tf_op jit(solution)/shard_map/ppermute | solution.py:432
  86.4 31.2 %collective-permute-start.1 = (bf16[32,16,1024]{2,1,0:T(8,128)(2,1)}, bf16[32,16,1024]{2,1,0:T(8,128)(2,1)}, u32[]{:S(2)}, u32[]{:S(2)}) collective-permute-start(bf16[32,16,1024]{2,1,0:T(8,128)(2,1)} %get-tuple-element.30.after_ref.refs_0_.refs_4_), channel_id=1, source_target_pairs={{0,1},{1,0},{2,3},{3,2},{4,5},{5,4},{6,7},{7,6},{8,9},{9,8},{10,11... | collective-permute-start | bytes 3145736 | tf_op jit(solution)/shard_map/ppermute | solution.py:432
  109.0 8.6 %collective-permute-start.2 = (bf16[32,16,1024]{2,1,0:T(8,128)(2,1)}, bf16[32,16,1024]{2,1,0:T(8,128)(2,1)}, u32[]{:S(2)}, u32[]{:S(2)}) collective-permute-start(bf16[32,16,1024]{2,1,0:T(8,128)(2,1)} %gate.7.refs_1_.refs_5_), channel_id=1, source_target_pairs={{0,1},{1,0},{2,3},{3,2},{4,5},{5,4},{6,7},{7,6},{8,9},{9,8},{10,11... | collective-permute-start | bytes 3145736 | tf_op jit(solution)/shard_map/ppermute | solution.py:432
  111.8 33.9 %collective-permute-start.3 = (bf16[16,12,1024]{2,1,0:T(8,128)(2,1)}, bf16[16,12,1024]{2,1,0:T(8,128)(2,1)S(1)}, u32[]{:S(2)}, u32[]{:S(2)}) collective-permute-start(bf16[16,12,1024]{2,1,0:T(8,128)(2,1)} %get-tuple-element.33), channel_id=1, source_target_pairs={{0,4},{4,8},{8,12},{12,16},{16,20},{20,24},{24,28},{1,5},{5,9},{9,... | collective-permute-start | bytes 1179656 | tf_op jit(solution)/shard_map/ppermute | solution.py:425
  115.2 32.3 %collective-permute-start.4 = (bf16[16,12,1024]{2,1,0:T(8,128)(2,1)}, bf16[16,12,1024]{2,1,0:T(8,128)(2,1)}, u32[]{:S(2)}, u32[]{:S(2)}) collective-permute-start(bf16[16,12,1024]{2,1,0:T(8,128)(2,1)} %get-tuple-element.34), channel_id=1, source_target_pairs={{4,0},{8,4},{12,8},{16,12},{20,16},{24,20},{28,24},{5,1},{9,5},{13... | collective-permute-start | bytes 1179656 | tf_op jit(solution)/shard_map/ppermute | solution.py:426
  145.7 0.8 copy-start.1
  147.5 51.1 %all-to-all-start.1 = ((bf16[8,2,16,32,128]{4,3,2,1,0:T(8,128)(2,1)}), bf16[8,2,16,32,128]{4,3,2,1,0:T(8,128)(2,1)}, u32[]{:S(2)}, u32[]{:S(2)}) async-start(bf16[8,2,16,32,128]{4,3,2,1,0:T(8,128)(2,1)} %gate.10), calls=%async_computation.1 | async-start | bytes 4194304 | tf_op jit(solution)/shard_map/all_to_all | solution.py:480
  162.6 56.3 %collective-permute-start.5 = (bf16[48,16,1024]{2,1,0:T(8,128)(2,1)}, bf16[48,16,1024]{2,1,0:T(8,128)(2,1)}, u32[]{:S(2)}, u32[]{:S(2)}) collective-permute-start(bf16[48,16,1024]{2,1,0:T(8,128)(2,1)} %get-tuple-element.37.after_ref.refs_0_.refs_8_), channel_id=1, source_target_pairs={{0,2},{1,3},{2,0},{3,1},{4,6},{5,7},{6,4},{7,5},{8,10},{9,11},{10,... | collective-permute-start | bytes 4718600 | tf_op jit(solution)/shard_map/ppermute | solution.py:432
  170.6 36.4 %copy-start.2 = (bf16[16,12,1024]{2,1,0:T(8,128)(2,1)S(1)}, bf16[16,12,1024]{2,1,0:T(8,128)(2,1)}, u32[]{:S(2)}) copy-start(bf16[16,12,1024]{2,1,0:T(8,128)(2,1)} %copy-done.1) | copy-start | bytes 1179652
  198.6 36.2 %all-to-all-start.3 = ((bf16[8,2,16,16,128]{4,3,2,1,0:T(8,128)(2,1)}), bf16[8,2,16,16,128]{4,3,2,1,0:T(8,128)(2,1)}, u32[]{:S(2)}, u32[]{:S(2)}) async-start(bf16[8,2,16,16,128]{4,3,2,1,0:T(8,128)(2,1)} %get-tuple-element.40), calls=%async_computation.3 | async-start | bytes 2097152 | tf_op jit(solution)/shard_map/all_to_all | solution.py:480
  209.2 19.0 %collective-permute-start.6 = (bf16[48,16,1024]{2,1,0:T(8,128)(2,1)}, bf16[48,16,1024]{2,1,0:T(8,128)(2,1)}, u32[]{:S(2)}, u32[]{:S(2)}) collective-permute-start(bf16[48,16,1024]{2,1,0:T(8,128)(2,1)} %get-tuple-element.37.after_ref.refs_0_.refs_8_), channel_id=1, source_target_pairs={{0,1},{1,0},{2,3},{3,2},{4,5},{5,4},{6,7},{7,6},{8,9},{9,8},{10,11... | collective-permute-start | bytes 4718600 | tf_op jit(solution)/shard_map/ppermute | solution.py:432
  218.8 9.3 %collective-permute-start.7 = (bf16[48,16,1024]{2,1,0:T(8,128)(2,1)}, bf16[48,16,1024]{2,1,0:T(8,128)(2,1)}, u32[]{:S(2)}, u32[]{:S(2)}) collective-permute-start(bf16[48,16,1024]{2,1,0:T(8,128)(2,1)} %gate.11.refs_1_.refs_9_), channel_id=1, source_target_pairs={{0,1},{1,0},{2,3},{3,2},{4,5},{5,4},{6,7},{7,6},{8,9},{9,8},{10,11... | collective-permute-start | bytes 4718600 | tf_op jit(solution)/shard_map/ppermute | solution.py:432
  226.7 25.4 %collective-permute-start.8 = (bf16[32,16,1024]{2,1,0:T(8,128)(2,1)}, bf16[32,16,1024]{2,1,0:T(8,128)(2,1)}, u32[]{:S(2)}, u32[]{:S(2)}) collective-permute-start(bf16[32,16,1024]{2,1,0:T(8,128)(2,1)} %get-tuple-element.39.after_ref.refs_0_.refs_12_), channel_id=1, source_target_pairs={{0,2},{1,3},{2,0},{3,1},{4,6},{5,7},{6,4},{7,5},{8,10},{9,11},{10,... | collective-permute-start | bytes 3145736 | tf_op jit(solution)/shard_map/ppermute | solution.py:432
  228.2 25.7 %collective-permute-start.9 = (bf16[32,16,1024]{2,1,0:T(8,128)(2,1)}, bf16[32,16,1024]{2,1,0:T(8,128)(2,1)}, u32[]{:S(2)}, u32[]{:S(2)}) collective-permute-start(bf16[32,16,1024]{2,1,0:T(8,128)(2,1)} %get-tuple-element.39.after_ref.refs_0_.refs_12_), channel_id=1, source_target_pairs={{0,1},{1,0},{2,3},{3,2},{4,5},{5,4},{6,7},{7,6},{8,9},{9,8},{10,11... | collective-permute-start | bytes 3145736 | tf_op jit(solution)/shard_map/ppermute | solution.py:432
  240.5 11.6 %copy-start = (bf16[16,16,1024]{2,1,0:T(8,128)(2,1)S(1)}, bf16[16,16,1024]{2,1,0:T(8,128)(2,1)}, u32[]{:S(2)}) copy-start(bf16[16,16,1024]{2,1,0:T(8,128)(2,1)} %get-tuple-element.42.after_ref.refs_16_) | copy-start | bytes 1572868
  252.1 3.0 %collective-permute-start.10 = (bf16[32,16,1024]{2,1,0:T(8,128)(2,1)}, bf16[32,16,1024]{2,1,0:T(8,128)(2,1)}, u32[]{:S(2)}, u32[]{:S(2)}) collective-permute-start(bf16[32,16,1024]{2,1,0:T(8,128)(2,1)} %gate.12.refs_1_.refs_13_), channel_id=1, source_target_pairs={{0,1},{1,0},{2,3},{3,2},{4,5},{5,4},{6,7},{7,6},{8,9},{9,8},{10,11... | collective-permute-start | bytes 3145736 | tf_op jit(solution)/shard_map/ppermute | solution.py:432
  252.1 14.4 %collective-permute-start.11 = (bf16[16,16,1024]{2,1,0:T(8,128)(2,1)S(1)}, bf16[16,16,1024]{2,1,0:T(8,128)(2,1)}, u32[]{:S(2)}, u32[]{:S(2)}) collective-permute-start(bf16[16,16,1024]{2,1,0:T(8,128)(2,1)S(1)} %copy-done), channel_id=1, source_target_pairs={{0,2},{1,3},{2,0},{3,1},{4,6},{5,7},{6,4},{7,5},{8,10},{9,11},{10,... | collective-permute-start | bytes 1572872 | tf_op jit(solution)/shard_map/ppermute | solution.py:432
  253.6 13.6 %collective-permute-start.12 = (bf16[16,16,1024]{2,1,0:T(8,128)(2,1)S(1)}, bf16[16,16,1024]{2,1,0:T(8,128)(2,1)}, u32[]{:S(2)}, u32[]{:S(2)}) collective-permute-start(bf16[16,16,1024]{2,1,0:T(8,128)(2,1)S(1)} %copy-done), channel_id=1, source_target_pairs={{0,1},{1,0},{2,3},{3,2},{4,5},{5,4},{6,7},{7,6},{8,9},{9,8},{10,11... | collective-permute-start | bytes 1572872 | tf_op jit(solution)/shard_map/ppermute | solution.py:432
  266.6 2.3 collective-permute-start.13

commit v16 on v15

--- a/solution.py
+++ b/solution.py
@@ -432,11 +432,11 @@
     return lax.ppermute(value, axis, [(i, i ^ bits) for i in range(count)])
 
 
-def gather_channels(pixels, after=None):
+def gather_channels(pixels, after):
     devices = lax.axis_size("chan")
     kept = [pixels] + [swap(pixels, "chan", bits) for bits in range(2, devices, 2)]
-    if after is not None:
-        kept = [pixels] + [gate(piece, after) for piece in kept[1:]]
+    for value in after:
+        kept = [pixels] + [gate(piece, value) for piece in kept[1:]]
     if devices == 1:
         return kept
     return kept + [swap(piece, "chan", 1) for piece in kept]
@@ -471,12 +471,17 @@
 
     def first(chunk):
         sent, state["last"] = first_transform(tables[chunk], grid, strips, state["last"])
+        if chunk == 1:
+            base(False)
+            sent = gate(sent, state["last"])
         if chunk == 2:
             gather(0)
             gram(0)
             done.add(0)
-            for value in [state["gram"]] + list(sides):
-                sent = gate(sent, value)
+            sent = gate(sent, state["last"])
+        if chunk == 3:
+            base(True)
+            sent = gate(sent, state["last"])
         halves[chunk] = lax.all_to_all(sent, "strip", split_axis=0, concat_axis=0, tiled=True)
 
     def base(with_edges):
@@ -502,7 +507,7 @@
         state["last"] = pixels[chunk]
 
     def gather(chunk):
-        pieces = gather_channels(pixels[chunk], state["last"])
+        pieces = gather_channels(pixels[chunk], [state["last"]] + (list(sides) if chunk == 0 else []))
         if chans % 16:
             pieces = [jnp.concatenate(pieces, axis=1)]
         gathered[chunk] = pieces
@@ -512,15 +517,12 @@
         state["last"] = state["gram"]
 
     first(0)
-    if chunks > 1:
-        first(1)
-    base(False)
+    first(1)
     for chunk in range(chunks):
         second(chunk)
         if chunk + 2 < chunks:
             first(chunk + 2)
         if chunk == 1:
-            base(True)
             gather(1)
         if chunk >= 1 and chunk - 1 not in done:
             if chunk - 1 not in gathered:

time: 283 us -> 279 us (0.986)
  waiting for transfers between devices: 121 us -> 118 us
    ppermute x1, waiting for transfers between devices: 22.5 us -> 46.8 us  [neighbour_rows(): lax.ppermute(tail.astype(BF16), 'strip', [(i, i + 1) for i in range(ends)])]
    all_to_all x4, waiting for transfers between devices: 62.6 us -> 47.5 us  [first(): lax.all_to_all(sent, 'strip', split_axis=0, concat_axis=0, tiled=True)]
    ppermute x12, waiting for transfers between devices: 35.2 us -> 22.9 us  [swap(): return lax.ppermute(value, axis, [(i, i ^ bits) for i in range(count)])]
  transfers between devices with their start and end apart: 18 -> 18, of which waited for: 9 -> 11; matrix products, arithmetic and copies ran while one was open for 2% -> 2% of each run, Pallas kernels for 32% -> 33%
where the time goes in v16:
time: 279 us; the launch traced here: 276 us
  waiting for transfers between devices  118 us (42%)
  Pallas kernels  111 us (40%)
  starting transfers between devices  39.9 us (14%)
  local copies, waits for them, and re-layouts  4.25 us (2%)
    all_to_all x4, waiting for transfers between devices, first(): lax.all_to_all(sent, 'strip', split_axis=0, concat_axis=0, tiled=True)  47.5 us
    ppermute x1, waiting for transfers between devices, neighbour_rows(): lax.ppermute(tail.astype(BF16), 'strip', [(i, i + 1) for i in range(ends)])  46.8 us
    pallas_call x4, Pallas kernels, first_transform(): pl.pallas_call(first_body, grid=(chans // block,), in_specs=[pl.BlockSpec...  33.9 us
    pallas_call x4, Pallas kernels, second_transform(): pl.pallas_call(second_body, grid=(side_len // block,), in_specs=[SMEM, pl...  29.3 us
    all_to_all x4, starting transfers between devices, first(): lax.all_to_all(sent, 'strip', split_axis=0, concat_axis=0, tiled=True)  27.3 us
    ppermute x12, waiting for transfers between devices, swap(): return lax.ppermute(value, axis, [(i, i ^ bits) for i in range(count)])  22.9 us
    pallas_call x2, Pallas kernels, base_step(): pl.pallas_call(functools.partial(base_body, levels, taps, blocks, strips,...  19.9 us
    pallas_call x3, Pallas kernels, gram_step(): pl.pallas_call(functools.partial(gram_body, len(pieces)), grid=(rows // b...  16.1 us
  transfers between devices with their start and end apart: 18, of which 11 were waited for; matrix products, arithmetic and copies ran while one was open for 2% of the time, Pallas kernels for 33%

profile of v16, /device:TPU:12, one launch (start us, length us, event | category | flops | bytes accessed | tf_op | source)
XLA Modules:
  0.0 276.1 jit_solution(14288198844825993626)
XLA Ops:
  0.0 8.5 %first_transform.4 = (bf16[8,2,16,32,128]{4,3,2,1,0:T(8,128)(2,1)}, f32[8,128]{1,0:T(8,128)}) custom-call(bf16[512,1024]{1,0:T(8,128)(2,1)} %constant.20.clone.table_ref, bf16[2,16,128,1024]{3,2,1,0:T(8,128)(2,1)} %grid_ref.7, s32[1]{0:T(128)} %bitcast.after_ref.strip_ref), custom_call_target="tpu_custom_call" | custom-call | bytes 65536 | tf_op jit(solution)/shard_map/first_transform/pallas_call | solution.py:117
  8.5 6.2 %all-to-all-start = ((bf16[8,2,16,32,128]{4,3,2,1,0:T(8,128)(2,1)}), bf16[8,2,16,32,128]{4,3,2,1,0:T(8,128)(2,1)}, u32[]{:S(2)}, u32[]{:S(2)}) async-start(bf16[8,2,16,32,128]{4,3,2,1,0:T(8,128)(2,1)} %get-tuple-element.26), calls=%async_computation | async-start | bytes 4194304 | tf_op jit(solution)/shard_map/all_to_all | solution.py:485
  14.7 10.3 %first_transform.5 = (bf16[8,2,16,48,128]{4,3,2,1,0:T(8,128)(2,1)}, f32[8,128]{1,0:T(8,128)}) custom-call(bf16[768,1024]{1,0:T(8,128)(2,1)} %constant.21.clone.table_ref, bf16[2,16,128,1024]{3,2,1,0:T(8,128)(2,1)} %grid_ref.7, f32[8,128]{1,0:T(8,128)} %get-tuple-element.27.after_ref), custom_call_target="tpu_custom_call" | custom-call | bytes 65536 | tf_op jit(solution)/shard_map/first_transform/pallas_call | solution.py:117
  25.0 10.2 %base_step.2 = (f32[16,32,1024]{2,1,0:T(8,128)}, f32[16,48,1024]{2,1,0:T(8,128)}, f32[16,16,1024]{2,1,0:T(8,128)}) custom-call(s32[1]{0:T(128)} %bitcast.after_ref.strip_ref, f32[16]{0:T(128)} %step_ref.11, f32[3,4]{1,0:T(4,128)} %highpass_ref.3, f32[16,128,1024]{2,1,0:T(8,128)} %model_ref.3, f32[8,128]{1,0:T(8,128)} %get-tuple-element.28.refs_0_), custom_call_target="tpu_custom_call" | custom-call | bytes 65536 | tf_op jit(solution)/shard_map/base_step/pallas_call | solution.py:202
  35.3 24.4 %all-to-all-done.half_ref = bf16[8,2,16,32,128]{4,3,2,1,0:T(8,128)(2,1)} async-done(((bf16[8,2,16,32,128]{4,3,2,1,0:T(8,128)(2,1)}), bf16[8,2,16,32,128]{4,3,2,1,0:T(8,128)(2,1)}, u32[]{:S(2)}, u32[]{:S(2)}) %all-to-all-start) | async-done | bytes 2097184 | tf_op jit(solution)/shard_map/all_to_all | solution.py:485
  59.7 7.7 %all-to-all-start.2 = ((bf16[8,2,16,48,128]{4,3,2,1,0:T(8,128)(2,1)}), bf16[8,2,16,48,128]{4,3,2,1,0:T(8,128)(2,1)}, u32[]{:S(2)}, u32[]{:S(2)}) async-start(bf16[8,2,16,48,128]{4,3,2,1,0:T(8,128)(2,1)} %gate.13), calls=%async_computation.2 | async-start | bytes 6291456 | tf_op jit(solution)/shard_map/all_to_all | solution.py:485
  67.4 7.3 %second_transform.4 = (f32[16,32,1024]{2,1,0:T(8,128)}, bf16[32,16,1024]{2,1,0:T(8,128)(2,1)}) custom-call(f32[16]{0:T(128)} %step_ref.11, bf16[8,2,16,32,128]{4,3,2,1,0:T(8,128)(2,1)} %all-to-all-done.half_ref, bf16[1024,1024]{1,0:T(8,128)(2,1)} %constant.22.clone.cosine_ref, bf16[1024,1024]{1,0:T(8,128)(2,1)} %constant.23.clone.sine_ref, ...), custom_call_target="tpu_custom_call" | custom-call | bytes 65536 | tf_op jit(solution)/shard_map/second_transform/pallas_call | solution.py:238
  74.7 1.5 collective-permute-start
  76.2 2.7 fusion
  78.9 3.4 %collective-permute-start.1 = (bf16[16,12,1024]{2,1,0:T(8,128)(2,1)}, bf16[16,12,1024]{2,1,0:T(8,128)(2,1)S(1)}, u32[]{:S(2)}, u32[]{:S(2)}) collective-permute-start(bf16[16,12,1024]{2,1,0:T(8,128)(2,1)} %get-tuple-element.32), channel_id=1, source_target_pairs={{0,4},{4,8},{8,12},{12,16},{16,20},{20,24},{24,28},{1,5},{5,9},{9,... | collective-permute-start | bytes 1179656 | tf_op jit(solution)/shard_map/ppermute | solution.py:425
  82.3 2.5 collective-permute-start.2
  84.8 0.1 collective-permute-start.3
  84.9 8.6 %first_transform.6 = (bf16[8,2,16,32,128]{4,3,2,1,0:T(8,128)(2,1)}, f32[8,128]{1,0:T(8,128)}) custom-call(bf16[512,1024]{1,0:T(8,128)(2,1)} %constant.24.clone.table_ref, bf16[2,16,128,1024]{3,2,1,0:T(8,128)(2,1)} %grid_ref.7, bf16[32,16,1024]{2,1,0:T(8,128)(2,1)} %get-tuple-element.30.after_ref.refs_0_.refs_4_), custom_call_target="tpu_custom_call" | custom-call | bytes 65536 | tf_op jit(solution)/shard_map/first_transform/pallas_call | solution.py:117
  93.4 5.4 %collective-permute-done.value_ref = bf16[32,16,1024]{2,1,0:T(8,128)(2,1)} collective-permute-done((bf16[32,16,1024]{2,1,0:T(8,128)(2,1)}, bf16[32,16,1024]{2,1,0:T(8,128)(2,1)}, u32[]{:S(2)}, u32[]{:S(2)}) %collective-permute-start) | collective-permute-done | bytes 1048608 | tf_op jit(solution)/shard_map/ppermute | solution.py:432
  98.8 46.8 %collective-permute-done.1.after_ref = bf16[16,12,1024]{2,1,0:T(8,128)(2,1)S(1)} collective-permute-done((bf16[16,12,1024]{2,1,0:T(8,128)(2,1)}, bf16[16,12,1024]{2,1,0:T(8,128)(2,1)S(1)}, u32[]{:S(2)}, u32[]{:S(2)}) %collective-permute-start.1) | collective-permute-done | bytes 393248 | tf_op jit(solution)/shard_map/ppermute | solution.py:425
  145.6 0.8 copy-done.1
  146.4 1.1 collective-permute-done.2.after_ref
  147.5 0.0 collective-permute-start.4
  147.5 0.0 collective-permute-done.3.refs_2_.refs_6_
  147.5 3.0 %collective-permute-done.4.refs_3_.refs_7_ = bf16[32,16,1024]{2,1,0:T(8,128)(2,1)} collective-permute-done((bf16[32,16,1024]{2,1,0:T(8,128)(2,1)}, bf16[32,16,1024]{2,1,0:T(8,128)(2,1)}, u32[]{:S(2)}, u32[]{:S(2)}) %collective-permute-start.4) | collective-permute-done | bytes 1048608 | tf_op jit(solution)/shard_map/ppermute | solution.py:432
  150.5 0.7 broadcast_in_dim.3.before_ref
  151.2 4.8 %gram_step.3.after_ref.before_ref = f32[256,256]{1,0:T(8,128)} custom-call(f32[256,256]{1,0:T(8,128)} %broadcast_in_dim.3.before_ref, f32[8,128]{1,0:T(8,128)} %get-tuple-element.31.after_ref, bf16[32,16,1024]{2,1,0:T(8,128)(2,1)} %get-tuple-element.30.after_ref.refs_0_.refs_4_, bf16[32,16,1024]{2,1,0:T(8,128)(2,1)} %gate.11.refs_1_.refs_5_, ...), custom_call_target="tpu_custom_call" | custom-call | bytes 65536 | tf_op jit(solution)/shard_map/gram_step/pallas_call | solution.py:285
  156.0 0.0 all-to-all-done.2.half_ref
  156.0 4.9 %all-to-all-start.1 = ((bf16[8,2,16,32,128]{4,3,2,1,0:T(8,128)(2,1)}), bf16[8,2,16,32,128]{4,3,2,1,0:T(8,128)(2,1)}, u32[]{:S(2)}, u32[]{:S(2)}) async-start(bf16[8,2,16,32,128]{4,3,2,1,0:T(8,128)(2,1)} %gate.12), calls=%async_computation.1 | async-start | bytes 4194304 | tf_op jit(solution)/shard_map/all_to_all | solution.py:485
  160.9 9.0 %second_transform.5 = (f32[16,48,1024]{2,1,0:T(8,128)}, bf16[48,16,1024]{2,1,0:T(8,128)(2,1)}) custom-call(f32[16]{0:T(128)} %step_ref.11, bf16[8,2,16,48,128]{4,3,2,1,0:T(8,128)(2,1)} %all-to-all-done.2.half_ref, bf16[1024,1024]{1,0:T(8,128)(2,1)} %constant.22.clone.cosine_ref, bf16[1024,1024]{1,0:T(8,128)(2,1)} %constant.23.clone.sine_ref, ...), custom_call_target="tpu_custom_call" | custom-call | bytes 65536 | tf_op jit(solution)/shard_map/second_transform/pallas_call | solution.py:238
  169.9 1.5 collective-permute-start.5
  171.4 2.2 pad_maximum_fusion.refs_0_
  173.6 6.5 %first_transform.7 = (bf16[8,2,16,16,128]{4,3,2,1,0:T(8,128)(2,1)}, f32[8,128]{1,0:T(8,128)}) custom-call(bf16[256,1024]{1,0:T(8,128)(2,1)} %constant.25.clone.table_ref, bf16[2,16,128,1024]{3,2,1,0:T(8,128)(2,1)} %grid_ref.7, bf16[48,16,1024]{2,1,0:T(8,128)(2,1)} %get-tuple-element.37.after_ref.refs_0_.refs_8_), custom_call_target="tpu_custom_call" | custom-call | bytes 65536 | tf_op jit(solution)/shard_map/first_transform/pallas_call | solution.py:117
  180.1 9.7 %base_step.3.base_ref.after_ref = f32[16,32,1024]{2,1,0:T(8,128)} custom-call(s32[1]{0:T(128)} %bitcast.after_ref.strip_ref, f32[16]{0:T(128)} %step_ref.11, f32[3,4]{1,0:T(4,128)} %highpass_ref.3, f32[16,128,1024]{2,1,0:T(8,128)} %model_ref.3, bf16[16,24,1024]{2,1,0:T(8,128)(2,1)} %pad_maximum_fusion.refs_0_, f32[8,128]{1,0:T(8,128)} %get-tuple-element.38.refs_1_), custom_call_target="tpu_custom_call" | custom-call | bytes 65536 | tf_op jit(solution)/shard_map/base_step/pallas_call | solution.py:202
  189.8 16.4 %all-to-all-done.1.half_ref = bf16[8,2,16,32,128]{4,3,2,1,0:T(8,128)(2,1)} async-done(((bf16[8,2,16,32,128]{4,3,2,1,0:T(8,128)(2,1)}), bf16[8,2,16,32,128]{4,3,2,1,0:T(8,128)(2,1)}, u32[]{:S(2)}, u32[]{:S(2)}) %all-to-all-start.1) | async-done | bytes 2097184 | tf_op jit(solution)/shard_map/all_to_all | solution.py:485
  206.2 8.4 %all-to-all-start.3 = ((bf16[8,2,16,16,128]{4,3,2,1,0:T(8,128)(2,1)}), bf16[8,2,16,16,128]{4,3,2,1,0:T(8,128)(2,1)}, u32[]{:S(2)}, u32[]{:S(2)}) async-start(bf16[8,2,16,16,128]{4,3,2,1,0:T(8,128)(2,1)} %gate.15), calls=%async_computation.3 | async-start | bytes 2097152 | tf_op jit(solution)/shard_map/all_to_all | solution.py:485
  214.6 0.0 collective-permute-start.6
  214.6 0.0 collective-permute-done.5.value_ref
  214.6 0.5 collective-permute-start.7
  215.1 7.3 %second_transform.6 = (f32[16,32,1024]{2,1,0:T(8,128)}, bf16[32,16,1024]{2,1,0:T(8,128)(2,1)}) custom-call(f32[16]{0:T(128)} %step_ref.11, bf16[8,2,16,32,128]{4,3,2,1,0:T(8,128)(2,1)} %all-to-all-done.1.half_ref, bf16[1024,1024]{1,0:T(8,128)(2,1)} %constant.22.clone.cosine_ref, bf16[1024,1024]{1,0:T(8,128)(2,1)} %constant.23.clone.sine_ref, ...), custom_call_target="tpu_custom_call" | custom-call | bytes 65536 | tf_op jit(solution)/shard_map/second_transform/pallas_call | solution.py:238
  222.4 1.5 collective-permute-start.8
  223.9 0.0 collective-permute-start.9
  223.9 6.5 %gram_step.4.after_ref.before_ref = f32[256,256]{1,0:T(8,128)} custom-call(f32[256,256]{1,0:T(8,128)} %gram_step.3.after_ref.before_ref, bf16[32,16,1024]{2,1,0:T(8,128)(2,1)} %get-tuple-element.39.after_ref.refs_0_.refs_12_, bf16[48,16,1024]{2,1,0:T(8,128)(2,1)} %get-tuple-element.37.after_ref.refs_0_.refs_8_, bf16[48,16,1024]{2,1,0:T(8,128)(2,1)} %gate.14.refs_1_.refs_9_, ...), custom_call_target="tpu_custom_call" | custom-call | bytes 65536 | tf_op jit(solution)/shard_map/gram_step/pallas_call | solution.py:285
  230.5 6.7 %all-to-all-done.3.half_ref = bf16[8,2,16,16,128]{4,3,2,1,0:T(8,128)(2,1)} async-done(((bf16[8,2,16,16,128]{4,3,2,1,0:T(8,128)(2,1)}), bf16[8,2,16,16,128]{4,3,2,1,0:T(8,128)(2,1)}, u32[]{:S(2)}, u32[]{:S(2)}) %all-to-all-start.3) | async-done | bytes 1048608 | tf_op jit(solution)/shard_map/all_to_all | solution.py:485
  237.2 5.7 %second_transform.7 = (f32[16,16,1024]{2,1,0:T(8,128)}, bf16[16,16,1024]{2,1,0:T(8,128)(2,1)}) custom-call(f32[16]{0:T(128)} %step_ref.11, bf16[8,2,16,16,128]{4,3,2,1,0:T(8,128)(2,1)} %all-to-all-done.3.half_ref, bf16[1024,1024]{1,0:T(8,128)(2,1)} %constant.22.clone.cosine_ref, bf16[1024,1024]{1,0:T(8,128)(2,1)} %constant.23.clone.sine_ref, ...), custom_call_target="tpu_custom_call" | custom-call | bytes 65536 | tf_op jit(solution)/shard_map/second_transform/pallas_call | solution.py:238
  242.9 5.0 %collective-permute-done.8.value_ref = bf16[32,16,1024]{2,1,0:T(8,128)(2,1)} collective-permute-done((bf16[32,16,1024]{2,1,0:T(8,128)(2,1)}, bf16[32,16,1024]{2,1,0:T(8,128)(2,1)}, u32[]{:S(2)}, u32[]{:S(2)}) %collective-permute-start.8) | collective-permute-done | bytes 1048608 | tf_op jit(solution)/shard_map/ppermute | solution.py:432
  247.9 1.5 collective-permute-start.11
  249.4 0.2 collective-permute-start.12
  249.6 1.3 collective-permute-done.10.refs_3_.refs_15_
  250.9 4.8 %gram_step.5.after_ref.gram_ref = f32[256,256]{1,0:T(8,128)} custom-call(f32[256,256]{1,0:T(8,128)} %gram_step.4.after_ref.before_ref, bf16[16,16,1024]{2,1,0:T(8,128)(2,1)} %get-tuple-element.42.after_ref.refs_16_, bf16[32,16,1024]{2,1,0:T(8,128)(2,1)} %get-tuple-element.39.after_ref.refs_0_.refs_12_, bf16[32,16,1024]{2,1,0:T(8,128)(2,1)} %gate.16.refs_1_.refs_13_, ...), custom_call_target="tpu_custom_call" | custom-call | bytes 65536 | tf_op jit(solution)/shard_map/gram_step/pallas_call | solution.py:285
  255.7 6.6 %collective-permute-done.11.value_ref = bf16[16,16,1024]{2,1,0:T(8,128)(2,1)} collective-permute-done((bf16[16,16,1024]{2,1,0:T(8,128)(2,1)S(1)}, bf16[16,16,1024]{2,1,0:T(8,128)(2,1)}, u32[]{:S(2)}, u32[]{:S(2)}) %collective-permute-start.11) | collective-permute-done | bytes 524320 | tf_op jit(solution)/shard_map/ppermute | solution.py:432
  263.0 1.6 collective-permute-done.13.refs_19_
  264.6 11.3 %polar_step.1 = f32[16,128,1024]{2,1,0:T(8,128)} custom-call(f32[1]{0:T(128)S(6)} %copy.30.shrink_ref, f32[256,256]{1,0:T(8,128)} %gram_step.5.after_ref.gram_ref, f32[16,32,1024]{2,1,0:T(8,128)} %get-tuple-element.43.refs_0_, f32[16,48,1024]{2,1,0:T(8,128)} %get-tuple-element.44.refs_1_, f32[16,32,1024]{2,1,0:T(8,128)} %get-tuple-element.45.refs_2_, ...), custom_call_target="tpu_custom_call" | custom-call | bytes 65536 | tf_op jit(solution)/shard_map/polar_step/pallas_call | solution.py:404
  (20 shorter events, 0.0 us)
Async XLA Ops:
  8.5 51.2 %all-to-all-start = ((bf16[8,2,16,32,128]{4,3,2,1,0:T(8,128)(2,1)}), bf16[8,2,16,32,128]{4,3,2,1,0:T(8,128)(2,1)}, u32[]{:S(2)}, u32[]{:S(2)}) async-start(bf16[8,2,16,32,128]{4,3,2,1,0:T(8,128)(2,1)} %get-tuple-element.26), calls=%async_computation | async-start | bytes 4194304 | tf_op jit(solution)/shard_map/all_to_all | solution.py:485
  59.7 96.3 %all-to-all-start.2 = ((bf16[8,2,16,48,128]{4,3,2,1,0:T(8,128)(2,1)}), bf16[8,2,16,48,128]{4,3,2,1,0:T(8,128)(2,1)}, u32[]{:S(2)}, u32[]{:S(2)}) async-start(bf16[8,2,16,48,128]{4,3,2,1,0:T(8,128)(2,1)} %gate.13), calls=%async_computation.2 | async-start | bytes 6291456 | tf_op jit(solution)/shard_map/all_to_all | solution.py:485
  74.7 24.1 %collective-permute-start = (bf16[32,16,1024]{2,1,0:T(8,128)(2,1)}, bf16[32,16,1024]{2,1,0:T(8,128)(2,1)}, u32[]{:S(2)}, u32[]{:S(2)}) collective-permute-start(bf16[32,16,1024]{2,1,0:T(8,128)(2,1)} %get-tuple-element.30.after_ref.refs_0_.refs_4_), channel_id=1, source_target_pairs={{0,2},{1,3},{2,0},{3,1},{4,6},{5,7},{6,4},{7,5},{8,10},{9,11},{10,... | collective-permute-start | bytes 3145736 | tf_op jit(solution)/shard_map/ppermute | solution.py:432
  78.9 66.7 %collective-permute-start.1 = (bf16[16,12,1024]{2,1,0:T(8,128)(2,1)}, bf16[16,12,1024]{2,1,0:T(8,128)(2,1)S(1)}, u32[]{:S(2)}, u32[]{:S(2)}) collective-permute-start(bf16[16,12,1024]{2,1,0:T(8,128)(2,1)} %get-tuple-element.32), channel_id=1, source_target_pairs={{0,4},{4,8},{8,12},{12,16},{16,20},{20,24},{24,28},{1,5},{5,9},{9,... | collective-permute-start | bytes 1179656 | tf_op jit(solution)/shard_map/ppermute | solution.py:425
  82.3 65.2 %collective-permute-start.2 = (bf16[16,12,1024]{2,1,0:T(8,128)(2,1)}, bf16[16,12,1024]{2,1,0:T(8,128)(2,1)}, u32[]{:S(2)}, u32[]{:S(2)}) collective-permute-start(bf16[16,12,1024]{2,1,0:T(8,128)(2,1)} %get-tuple-element.33), channel_id=1, source_target_pairs={{4,0},{8,4},{12,8},{16,12},{20,16},{24,20},{28,24},{5,1},{9,5},{13... | collective-permute-start | bytes 1179656 | tf_op jit(solution)/shard_map/ppermute | solution.py:426
  84.8 62.7 %collective-permute-start.3 = (bf16[32,16,1024]{2,1,0:T(8,128)(2,1)}, bf16[32,16,1024]{2,1,0:T(8,128)(2,1)}, u32[]{:S(2)}, u32[]{:S(2)}) collective-permute-start(bf16[32,16,1024]{2,1,0:T(8,128)(2,1)} %get-tuple-element.30.after_ref.refs_0_.refs_4_), channel_id=1, source_target_pairs={{0,1},{1,0},{2,3},{3,2},{4,5},{5,4},{6,7},{7,6},{8,9},{9,8},{10,11... | collective-permute-start | bytes 3145736 | tf_op jit(solution)/shard_map/ppermute | solution.py:432
  145.6 0.8 copy-start.1
  147.5 3.0 %collective-permute-start.4 = (bf16[32,16,1024]{2,1,0:T(8,128)(2,1)}, bf16[32,16,1024]{2,1,0:T(8,128)(2,1)}, u32[]{:S(2)}, u32[]{:S(2)}) collective-permute-start(bf16[32,16,1024]{2,1,0:T(8,128)(2,1)} %gate.11.refs_1_.refs_5_), channel_id=1, source_target_pairs={{0,1},{1,0},{2,3},{3,2},{4,5},{5,4},{6,7},{7,6},{8,9},{9,8},{10,11... | collective-permute-start | bytes 3145736 | tf_op jit(solution)/shard_map/ppermute | solution.py:432
  156.0 50.2 %all-to-all-start.1 = ((bf16[8,2,16,32,128]{4,3,2,1,0:T(8,128)(2,1)}), bf16[8,2,16,32,128]{4,3,2,1,0:T(8,128)(2,1)}, u32[]{:S(2)}, u32[]{:S(2)}) async-start(bf16[8,2,16,32,128]{4,3,2,1,0:T(8,128)(2,1)} %gate.12), calls=%async_computation.1 | async-start | bytes 4194304 | tf_op jit(solution)/shard_map/all_to_all | solution.py:485
  160.9 10.5 %copy-start.2 = (bf16[16,12,1024]{2,1,0:T(8,128)(2,1)S(1)}, bf16[16,12,1024]{2,1,0:T(8,128)(2,1)}, u32[]{:S(2)}) copy-start(bf16[16,12,1024]{2,1,0:T(8,128)(2,1)} %copy-done.1) | copy-start | bytes 1179652
  169.9 44.7 %collective-permute-start.5 = (bf16[48,16,1024]{2,1,0:T(8,128)(2,1)}, bf16[48,16,1024]{2,1,0:T(8,128)(2,1)}, u32[]{:S(2)}, u32[]{:S(2)}) collective-permute-start(bf16[48,16,1024]{2,1,0:T(8,128)(2,1)} %get-tuple-element.37.after_ref.refs_0_.refs_8_), channel_id=1, source_target_pairs={{0,2},{1,3},{2,0},{3,1},{4,6},{5,7},{6,4},{7,5},{8,10},{9,11},{10,... | collective-permute-start | bytes 4718600 | tf_op jit(solution)/shard_map/ppermute | solution.py:432
  206.2 31.0 %all-to-all-start.3 = ((bf16[8,2,16,16,128]{4,3,2,1,0:T(8,128)(2,1)}), bf16[8,2,16,16,128]{4,3,2,1,0:T(8,128)(2,1)}, u32[]{:S(2)}, u32[]{:S(2)}) async-start(bf16[8,2,16,16,128]{4,3,2,1,0:T(8,128)(2,1)} %gate.15), calls=%async_computation.3 | async-start | bytes 2097152 | tf_op jit(solution)/shard_map/all_to_all | solution.py:485
  214.6 9.3 %collective-permute-start.6 = (bf16[48,16,1024]{2,1,0:T(8,128)(2,1)}, bf16[48,16,1024]{2,1,0:T(8,128)(2,1)}, u32[]{:S(2)}, u32[]{:S(2)}) collective-permute-start(bf16[48,16,1024]{2,1,0:T(8,128)(2,1)} %get-tuple-element.37.after_ref.refs_0_.refs_8_), channel_id=1, source_target_pairs={{0,1},{1,0},{2,3},{3,2},{4,5},{5,4},{6,7},{7,6},{8,9},{9,8},{10,11... | collective-permute-start | bytes 4718600 | tf_op jit(solution)/shard_map/ppermute | solution.py:432
  214.6 9.3 %collective-permute-start.7 = (bf16[48,16,1024]{2,1,0:T(8,128)(2,1)}, bf16[48,16,1024]{2,1,0:T(8,128)(2,1)}, u32[]{:S(2)}, u32[]{:S(2)}) collective-permute-start(bf16[48,16,1024]{2,1,0:T(8,128)(2,1)} %gate.14.refs_1_.refs_9_), channel_id=1, source_target_pairs={{0,1},{1,0},{2,3},{3,2},{4,5},{5,4},{6,7},{7,6},{8,9},{9,8},{10,11... | collective-permute-start | bytes 4718600 | tf_op jit(solution)/shard_map/ppermute | solution.py:432
  222.4 25.5 %collective-permute-start.8 = (bf16[32,16,1024]{2,1,0:T(8,128)(2,1)}, bf16[32,16,1024]{2,1,0:T(8,128)(2,1)}, u32[]{:S(2)}, u32[]{:S(2)}) collective-permute-start(bf16[32,16,1024]{2,1,0:T(8,128)(2,1)} %get-tuple-element.39.after_ref.refs_0_.refs_12_), channel_id=1, source_target_pairs={{0,2},{1,3},{2,0},{3,1},{4,6},{5,7},{6,4},{7,5},{8,10},{9,11},{10,... | collective-permute-start | bytes 3145736 | tf_op jit(solution)/shard_map/ppermute | solution.py:432
  223.9 25.7 %collective-permute-start.9 = (bf16[32,16,1024]{2,1,0:T(8,128)(2,1)}, bf16[32,16,1024]{2,1,0:T(8,128)(2,1)}, u32[]{:S(2)}, u32[]{:S(2)}) collective-permute-start(bf16[32,16,1024]{2,1,0:T(8,128)(2,1)} %get-tuple-element.39.after_ref.refs_0_.refs_12_), channel_id=1, source_target_pairs={{0,1},{1,0},{2,3},{3,2},{4,5},{5,4},{6,7},{7,6},{8,9},{9,8},{10,11... | collective-permute-start | bytes 3145736 | tf_op jit(solution)/shard_map/ppermute | solution.py:432
  242.9 5.0 %copy-start = (bf16[16,16,1024]{2,1,0:T(8,128)(2,1)S(1)}, bf16[16,16,1024]{2,1,0:T(8,128)(2,1)}, u32[]{:S(2)}) copy-start(bf16[16,16,1024]{2,1,0:T(8,128)(2,1)} %get-tuple-element.42.after_ref.refs_16_) | copy-start | bytes 1572868
  247.9 3.0 %collective-permute-start.10 = (bf16[32,16,1024]{2,1,0:T(8,128)(2,1)}, bf16[32,16,1024]{2,1,0:T(8,128)(2,1)}, u32[]{:S(2)}, u32[]{:S(2)}) collective-permute-start(bf16[32,16,1024]{2,1,0:T(8,128)(2,1)} %gate.16.refs_1_.refs_13_), channel_id=1, source_target_pairs={{0,1},{1,0},{2,3},{3,2},{4,5},{5,4},{6,7},{7,6},{8,9},{9,8},{10,11... | collective-permute-start | bytes 3145736 | tf_op jit(solution)/shard_map/ppermute | solution.py:432
  247.9 14.4 %collective-permute-start.11 = (bf16[16,16,1024]{2,1,0:T(8,128)(2,1)S(1)}, bf16[16,16,1024]{2,1,0:T(8,128)(2,1)}, u32[]{:S(2)}, u32[]{:S(2)}) collective-permute-start(bf16[16,16,1024]{2,1,0:T(8,128)(2,1)S(1)} %copy-done), channel_id=1, source_target_pairs={{0,2},{1,3},{2,0},{3,1},{4,6},{5,7},{6,4},{7,5},{8,10},{9,11},{10,... | collective-permute-start | bytes 1572872 | tf_op jit(solution)/shard_map/ppermute | solution.py:432
  249.4 13.6 %collective-permute-start.12 = (bf16[16,16,1024]{2,1,0:T(8,128)(2,1)S(1)}, bf16[16,16,1024]{2,1,0:T(8,128)(2,1)}, u32[]{:S(2)}, u32[]{:S(2)}) collective-permute-start(bf16[16,16,1024]{2,1,0:T(8,128)(2,1)S(1)} %copy-done), channel_id=1, source_target_pairs={{0,1},{1,0},{2,3},{3,2},{4,5},{5,4},{6,7},{7,6},{8,9},{9,8},{10,11... | collective-permute-start | bytes 1572872 | tf_op jit(solution)/shard_map/ppermute | solution.py:432
  262.3 2.3 collective-permute-start.13

commit v17 on v14

--- a/solution.py
+++ b/solution.py
@@ -416,12 +416,17 @@
     )(shrinkage, gram, *moved, *flat)
 
 
-def neighbour_rows(model_image, reach):
-    ends = lax.axis_size("strip") - 1
-    head, tail = lax.optimization_barrier((model_image[:, :reach], model_image[:, model_image.shape[1] - reach :]))
-    before = lax.ppermute(tail.astype(BF16), "strip", [(i, i + 1) for i in range(ends)])
-    after = lax.ppermute(head.astype(BF16), "strip", [(i + 1, i) for i in range(ends)])
-    return before, after
+def neighbour_rows(strip, model_image, reach):
+    count = lax.axis_size("strip")
+    head, tail = model_image[:, :reach], model_image[:, model_image.shape[1] - reach :]
+    odd = strip[0] % 2 == 1
+    outer, inner = lax.optimization_barrier((jnp.where(odd, tail, head), jnp.where(odd, head, tail)))
+
+    def exchanged(rows, firsts):
+        pairs = [(i, i + 1) for i in firsts if i + 1 < count]
+        return lax.ppermute(rows.astype(BF16), "strip", pairs + [(j, i) for i, j in pairs])
+
+    return exchanged(outer, range(1, count, 2)), exchanged(inner, range(0, count, 2))
 
 
 def swap(value, axis, bits):
@@ -456,8 +461,9 @@
 
     levels, taps = highpass.shape
     reach = (taps - 1) * 2 ** (levels - 1)
-    sides = neighbour_rows(model_image, reach)
-    edges = jnp.concatenate(sides, axis=1)
+    outer, inner = neighbour_rows(strip, model_image, reach)
+    odd = strip[0] % 2 == 1
+    edges = jnp.concatenate([jnp.where(odd, inner, outer), jnp.where(odd, outer, inner)], axis=1)
 
     halves = {}
     moved = {}
@@ -468,9 +474,11 @@
 
     def first(chunk):
         sent, state["last"] = first_transform(tables[chunk], grid, strips, state["last"])
+        if chunk == 0:
+            sent = gate(sent, outer)
+            state["last"] = gate(state["last"], outer)
         if chunk == 1:
-            for side in sides:
-                sent = gate(sent, side)
+            sent = gate(sent, inner)
         if chunk == 2:
             gather(0)
             gram(0)

time: 271 us -> 268 us (0.989)
    ppermute x2, waiting for transfers between devices: 38.3 us -> 27.6 us  [exchanged(): lax.ppermute(rows.astype(BF16), 'strip', pairs + [(j, i) for i, j in pairs])]
    all_to_all x4, waiting for transfers between devices: 47.8 us -> 58.1 us  [first(): lax.all_to_all(sent, 'strip', split_axis=0, concat_axis=0, tiled=True)]
    slice x1 -> x0, local copies, waits for them, and re-layouts: 2.81 us -> none  [neighbour_rows(): model_image[:, model_image.shape[1] - reach:]]
    select_n x0 -> x2, other arithmetic: none -> 2.72 us  [the longest x1 2.65 us: neighbour_rows(): jnp.where(odd, head, tail)]
  transfers between devices with their start and end apart: 18 -> 18, of which waited for: 11 -> 12; matrix products, arithmetic and copies ran while one was open for 2% -> 1% of each run, Pallas kernels for 31% -> 34%
where the time goes in v17:
time: 268 us; the launch traced here: 265 us
  waiting for transfers between devices  118 us (44%)
  Pallas kernels  102 us (38%)
  starting transfers between devices  38.8 us (14%)
  other arithmetic  3.84 us (1%)
    all_to_all x4, waiting for transfers between devices, first(): lax.all_to_all(sent, 'strip', split_axis=0, concat_axis=0, tiled=True)  58.1 us
    pallas_call x4, Pallas kernels, first_transform(): pl.pallas_call(first_body, grid=(chans // block,), in_specs=[pl.BlockSpec...  33.7 us
    ppermute x12, waiting for transfers between devices, swap(): return lax.ppermute(value, axis, [(i, i ^ bits) for i in range(count)])  32.2 us
    pallas_call x4, Pallas kernels, second_transform(): pl.pallas_call(second_body, grid=(side_len // block,), in_specs=[SMEM, pl...  29.3 us
    all_to_all x4, starting transfers between devices, first(): lax.all_to_all(sent, 'strip', split_axis=0, concat_axis=0, tiled=True)  28.1 us
    ppermute x2, waiting for transfers between devices, exchanged(): lax.ppermute(rows.astype(BF16), 'strip', pairs + [(j, i) for i, j in pairs])  27.6 us
    pallas_call x3, Pallas kernels, gram_step(): pl.pallas_call(functools.partial(gram_body, len(pieces)), grid=(rows // b...  16.1 us
    pallas_call x1, Pallas kernels, polar_step(): pl.pallas_call(functools.partial(polar_body, starts, sizes, groups), in_s...  11.3 us
  transfers between devices with their start and end apart: 18, of which 12 were waited for; matrix products, arithmetic and copies ran while one was open for 1% of the time, Pallas kernels for 34%

profile of v17, /device:TPU:12, one launch (start us, length us, event | category | flops | bytes accessed | tf_op | source)
XLA Modules:
  0.0 265.3 jit_solution(8785530433493836194)
XLA Ops:
  0.0 2.6 slice_select_fusion
  2.6 3.4 %collective-permute-start = (bf16[16,12,1024]{2,1,0:T(8,128)(2,1)}, bf16[16,12,1024]{2,1,0:T(8,128)(2,1)S(1)}, u32[]{:S(2)}, u32[]{:S(2)}) collective-permute-start(bf16[16,12,1024]{2,1,0:T(8,128)(2,1)} %get-tuple-element.28), channel_id=1, source_target_pairs={{4,8},{12,16},{20,24},{8,4},{16,12},{24,20},{5,9},{13,17},{21,25},... | collective-permute-start | bytes 1179656 | tf_op jit(solution)/shard_map/ppermute | solution.py:427
  6.1 8.5 %first_transform.4 = (bf16[8,2,16,32,128]{4,3,2,1,0:T(8,128)(2,1)}, f32[8,128]{1,0:T(8,128)}) custom-call(bf16[512,1024]{1,0:T(8,128)(2,1)} %constant.36.clone.table_ref, bf16[2,16,128,1024]{3,2,1,0:T(8,128)(2,1)} %grid_ref.7, s32[1]{0:T(128)} %bitcast.after_ref.strip_ref), custom_call_target="tpu_custom_call" | custom-call | bytes 65536 | tf_op jit(solution)/shard_map/first_transform/pallas_call | solution.py:112
  14.6 4.7 %collective-permute-done.after_ref = bf16[16,12,1024]{2,1,0:T(8,128)(2,1)S(1)} collective-permute-done((bf16[16,12,1024]{2,1,0:T(8,128)(2,1)}, bf16[16,12,1024]{2,1,0:T(8,128)(2,1)S(1)}, u32[]{:S(2)}, u32[]{:S(2)}) %collective-permute-start) | collective-permute-done | bytes 393248 | tf_op jit(solution)/shard_map/ppermute | solution.py:427
  19.3 0.8 copy-done.1
  20.1 5.3 %all-to-all-start = ((bf16[8,2,16,32,128]{4,3,2,1,0:T(8,128)(2,1)}), bf16[8,2,16,32,128]{4,3,2,1,0:T(8,128)(2,1)}, u32[]{:S(2)}, u32[]{:S(2)}) async-start(bf16[8,2,16,32,128]{4,3,2,1,0:T(8,128)(2,1)} %gate.8), calls=%async_computation | async-start | bytes 4194304 | tf_op jit(solution)/shard_map/all_to_all | solution.py:487
  25.4 0.6 collective-permute-start.1
  25.9 10.3 %first_transform.5 = (bf16[8,2,16,48,128]{4,3,2,1,0:T(8,128)(2,1)}, f32[8,128]{1,0:T(8,128)}) custom-call(bf16[768,1024]{1,0:T(8,128)(2,1)} %constant.37.clone.table_ref, bf16[2,16,128,1024]{3,2,1,0:T(8,128)(2,1)} %grid_ref.7, f32[8,128]{1,0:T(8,128)} %gate.9.after_ref), custom_call_target="tpu_custom_call" | custom-call | bytes 65536 | tf_op jit(solution)/shard_map/first_transform/pallas_call | solution.py:112
  36.2 22.9 %collective-permute-done.1.after_ref = bf16[16,12,1024]{2,1,0:T(8,128)(2,1)S(1)} collective-permute-done((bf16[16,12,1024]{2,1,0:T(8,128)(2,1)}, bf16[16,12,1024]{2,1,0:T(8,128)(2,1)S(1)}, u32[]{:S(2)}, u32[]{:S(2)}) %collective-permute-start.1) | collective-permute-done | bytes 393248 | tf_op jit(solution)/shard_map/ppermute | solution.py:427
  59.1 0.8 copy-done.3
  59.9 9.6 %all-to-all-done.half_ref = bf16[8,2,16,32,128]{4,3,2,1,0:T(8,128)(2,1)} async-done(((bf16[8,2,16,32,128]{4,3,2,1,0:T(8,128)(2,1)}), bf16[8,2,16,32,128]{4,3,2,1,0:T(8,128)(2,1)}, u32[]{:S(2)}, u32[]{:S(2)}) %all-to-all-start) | async-done | bytes 2097184 | tf_op jit(solution)/shard_map/all_to_all | solution.py:487
  69.5 7.7 %all-to-all-start.2 = ((bf16[8,2,16,48,128]{4,3,2,1,0:T(8,128)(2,1)}), bf16[8,2,16,48,128]{4,3,2,1,0:T(8,128)(2,1)}, u32[]{:S(2)}, u32[]{:S(2)}) async-start(bf16[8,2,16,48,128]{4,3,2,1,0:T(8,128)(2,1)} %gate.12), calls=%async_computation.2 | async-start | bytes 6291456 | tf_op jit(solution)/shard_map/all_to_all | solution.py:487
  77.2 0.1 broadcast_select_fusion.1
  77.3 1.1 pad_maximum_fusion.edge_ref
  78.4 11.1 %base_step.1 = (f32[16,32,1024]{2,1,0:T(8,128)}, f32[16,48,1024]{2,1,0:T(8,128)}, f32[16,32,1024]{2,1,0:T(8,128)}, f32[16,16,1024]{2,1,0:T(8,128)}) custom-call(s32[1]{0:T(128)} %bitcast.after_ref.strip_ref, f32[16]{0:T(128)} %step_ref.9, f32[3,4]{1,0:T(4,128)} %highpass_ref.1, f32[16,128,1024]{2,1,0:T(8,128)} %model_ref.1, ...), custom_call_target="tpu_custom_call" | custom-call | bytes 65536 | tf_op jit(solution)/shard_map/base_step/pallas_call | solution.py:193
  89.6 7.3 %second_transform.4 = (f32[16,32,1024]{2,1,0:T(8,128)}, bf16[32,16,1024]{2,1,0:T(8,128)(2,1)}) custom-call(f32[16]{0:T(128)} %step_ref.9, bf16[8,2,16,32,128]{4,3,2,1,0:T(8,128)(2,1)} %all-to-all-done.half_ref, bf16[1024,1024]{1,0:T(8,128)(2,1)} %constant.38.clone.cosine_ref, bf16[1024,1024]{1,0:T(8,128)(2,1)} %constant.39.clone.sine_ref, ...), custom_call_target="tpu_custom_call" | custom-call | bytes 65536 | tf_op jit(solution)/shard_map/second_transform/pallas_call | solution.py:236
  96.9 1.5 collective-permute-start.2
  98.4 0.0 collective-permute-start.3
  98.4 8.4 %first_transform.6 = (bf16[8,2,16,32,128]{4,3,2,1,0:T(8,128)(2,1)}, f32[8,128]{1,0:T(8,128)}) custom-call(bf16[512,1024]{1,0:T(8,128)(2,1)} %constant.40.clone.table_ref, bf16[2,16,128,1024]{3,2,1,0:T(8,128)(2,1)} %grid_ref.7, bf16[32,16,1024]{2,1,0:T(8,128)(2,1)} %get-tuple-element.33.after_ref.refs_0_.refs_4_), custom_call_target="tpu_custom_call" | custom-call | bytes 65536 | tf_op jit(solution)/shard_map/first_transform/pallas_call | solution.py:112
  106.8 14.2 %collective-permute-done.2.value_ref = bf16[32,16,1024]{2,1,0:T(8,128)(2,1)} collective-permute-done((bf16[32,16,1024]{2,1,0:T(8,128)(2,1)}, bf16[32,16,1024]{2,1,0:T(8,128)(2,1)}, u32[]{:S(2)}, u32[]{:S(2)}) %collective-permute-start.2) | collective-permute-done | bytes 1048608 | tf_op jit(solution)/shard_map/ppermute | solution.py:434
  121.0 3.0 %collective-permute-done.4.refs_3_.refs_7_ = bf16[32,16,1024]{2,1,0:T(8,128)(2,1)} collective-permute-done((bf16[32,16,1024]{2,1,0:T(8,128)(2,1)}, bf16[32,16,1024]{2,1,0:T(8,128)(2,1)}, u32[]{:S(2)}, u32[]{:S(2)}) %collective-permute-start.4) | collective-permute-done | bytes 1048608 | tf_op jit(solution)/shard_map/ppermute | solution.py:434
  124.0 0.7 broadcast_in_dim.3.before_ref
  124.8 4.8 %gram_step.3.after_ref.before_ref = f32[256,256]{1,0:T(8,128)} custom-call(f32[256,256]{1,0:T(8,128)} %broadcast_in_dim.3.before_ref, f32[8,128]{1,0:T(8,128)} %get-tuple-element.34.after_ref, bf16[32,16,1024]{2,1,0:T(8,128)(2,1)} %get-tuple-element.33.after_ref.refs_0_.refs_4_, bf16[32,16,1024]{2,1,0:T(8,128)(2,1)} %gate.10.refs_1_.refs_5_, ...), custom_call_target="tpu_custom_call" | custom-call | bytes 65536 | tf_op jit(solution)/shard_map/gram_step/pallas_call | solution.py:283
  129.5 14.6 %all-to-all-done.2.half_ref = bf16[8,2,16,48,128]{4,3,2,1,0:T(8,128)(2,1)} async-done(((bf16[8,2,16,48,128]{4,3,2,1,0:T(8,128)(2,1)}), bf16[8,2,16,48,128]{4,3,2,1,0:T(8,128)(2,1)}, u32[]{:S(2)}, u32[]{:S(2)}) %all-to-all-start.2) | async-done | bytes 3145760 | tf_op jit(solution)/shard_map/all_to_all | solution.py:487
  144.2 7.6 %all-to-all-start.1 = ((bf16[8,2,16,32,128]{4,3,2,1,0:T(8,128)(2,1)}), bf16[8,2,16,32,128]{4,3,2,1,0:T(8,128)(2,1)}, u32[]{:S(2)}, u32[]{:S(2)}) async-start(bf16[8,2,16,32,128]{4,3,2,1,0:T(8,128)(2,1)} %gate.11), calls=%async_computation.1 | async-start | bytes 4194304 | tf_op jit(solution)/shard_map/all_to_all | solution.py:487
  151.8 9.0 %second_transform.5 = (f32[16,48,1024]{2,1,0:T(8,128)}, bf16[48,16,1024]{2,1,0:T(8,128)(2,1)}) custom-call(f32[16]{0:T(128)} %step_ref.9, bf16[8,2,16,48,128]{4,3,2,1,0:T(8,128)(2,1)} %all-to-all-done.2.half_ref, bf16[1024,1024]{1,0:T(8,128)(2,1)} %constant.38.clone.cosine_ref, bf16[1024,1024]{1,0:T(8,128)(2,1)} %constant.39.clone.sine_ref, ...), custom_call_target="tpu_custom_call" | custom-call | bytes 65536 | tf_op jit(solution)/shard_map/second_transform/pallas_call | solution.py:236
  160.8 1.5 collective-permute-start.5
  162.3 6.5 %first_transform.7 = (bf16[8,2,16,16,128]{4,3,2,1,0:T(8,128)(2,1)}, f32[8,128]{1,0:T(8,128)}) custom-call(bf16[256,1024]{1,0:T(8,128)(2,1)} %constant.41.clone.table_ref, bf16[2,16,128,1024]{3,2,1,0:T(8,128)(2,1)} %grid_ref.7, bf16[48,16,1024]{2,1,0:T(8,128)(2,1)} %get-tuple-element.39.after_ref.refs_0_.refs_8_), custom_call_target="tpu_custom_call" | custom-call | bytes 65536 | tf_op jit(solution)/shard_map/first_transform/pallas_call | solution.py:112
  168.8 27.5 %all-to-all-done.1.half_ref = bf16[8,2,16,32,128]{4,3,2,1,0:T(8,128)(2,1)} async-done(((bf16[8,2,16,32,128]{4,3,2,1,0:T(8,128)(2,1)}), bf16[8,2,16,32,128]{4,3,2,1,0:T(8,128)(2,1)}, u32[]{:S(2)}, u32[]{:S(2)}) %all-to-all-start.1) | async-done | bytes 2097184 | tf_op jit(solution)/shard_map/all_to_all | solution.py:487
  196.3 7.5 %all-to-all-start.3 = ((bf16[8,2,16,16,128]{4,3,2,1,0:T(8,128)(2,1)}), bf16[8,2,16,16,128]{4,3,2,1,0:T(8,128)(2,1)}, u32[]{:S(2)}, u32[]{:S(2)}) async-start(bf16[8,2,16,16,128]{4,3,2,1,0:T(8,128)(2,1)} %get-tuple-element.42), calls=%async_computation.3 | async-start | bytes 2097152 | tf_op jit(solution)/shard_map/all_to_all | solution.py:487
  203.8 0.0 collective-permute-start.6
  203.8 0.0 collective-permute-done.5.value_ref
  203.9 0.5 collective-permute-start.7
  204.3 7.3 %second_transform.6 = (f32[16,32,1024]{2,1,0:T(8,128)}, bf16[32,16,1024]{2,1,0:T(8,128)(2,1)}) custom-call(f32[16]{0:T(128)} %step_ref.9, bf16[8,2,16,32,128]{4,3,2,1,0:T(8,128)(2,1)} %all-to-all-done.1.half_ref, bf16[1024,1024]{1,0:T(8,128)(2,1)} %constant.38.clone.cosine_ref, bf16[1024,1024]{1,0:T(8,128)(2,1)} %constant.39.clone.sine_ref, ...), custom_call_target="tpu_custom_call" | custom-call | bytes 65536 | tf_op jit(solution)/shard_map/second_transform/pallas_call | solution.py:236
  211.6 1.5 collective-permute-start.8
  213.1 0.0 collective-permute-start.9
  213.1 6.5 %gram_step.4.after_ref.before_ref = f32[256,256]{1,0:T(8,128)} custom-call(f32[256,256]{1,0:T(8,128)} %gram_step.3.after_ref.before_ref, bf16[32,16,1024]{2,1,0:T(8,128)(2,1)} %get-tuple-element.41.after_ref.refs_0_.refs_12_, bf16[48,16,1024]{2,1,0:T(8,128)(2,1)} %get-tuple-element.39.after_ref.refs_0_.refs_8_, bf16[48,16,1024]{2,1,0:T(8,128)(2,1)} %gate.13.refs_1_.refs_9_, ...), custom_call_target="tpu_custom_call" | custom-call | bytes 65536 | tf_op jit(solution)/shard_map/gram_step/pallas_call | solution.py:283
  219.7 6.3 %all-to-all-done.3.half_ref = bf16[8,2,16,16,128]{4,3,2,1,0:T(8,128)(2,1)} async-done(((bf16[8,2,16,16,128]{4,3,2,1,0:T(8,128)(2,1)}), bf16[8,2,16,16,128]{4,3,2,1,0:T(8,128)(2,1)}, u32[]{:S(2)}, u32[]{:S(2)}) %all-to-all-start.3) | async-done | bytes 1048608 | tf_op jit(solution)/shard_map/all_to_all | solution.py:487
  226.0 5.7 %second_transform.7 = (f32[16,16,1024]{2,1,0:T(8,128)}, bf16[16,16,1024]{2,1,0:T(8,128)(2,1)}) custom-call(f32[16]{0:T(128)} %step_ref.9, bf16[8,2,16,16,128]{4,3,2,1,0:T(8,128)(2,1)} %all-to-all-done.3.half_ref, bf16[1024,1024]{1,0:T(8,128)(2,1)} %constant.38.clone.cosine_ref, bf16[1024,1024]{1,0:T(8,128)(2,1)} %constant.39.clone.sine_ref, ...), custom_call_target="tpu_custom_call" | custom-call | bytes 65536 | tf_op jit(solution)/shard_map/second_transform/pallas_call | solution.py:236
  231.7 5.4 %collective-permute-done.8.value_ref = bf16[32,16,1024]{2,1,0:T(8,128)(2,1)} collective-permute-done((bf16[32,16,1024]{2,1,0:T(8,128)(2,1)}, bf16[32,16,1024]{2,1,0:T(8,128)(2,1)}, u32[]{:S(2)}, u32[]{:S(2)}) %collective-permute-start.8) | collective-permute-done | bytes 1048608 | tf_op jit(solution)/shard_map/ppermute | solution.py:434
  237.1 0.0 collective-permute-start.10
  237.1 1.5 collective-permute-start.11
  238.6 0.2 collective-permute-start.12
  238.8 1.3 collective-permute-done.10.refs_3_.refs_15_
  240.1 4.8 %gram_step.5.after_ref.gram_ref = f32[256,256]{1,0:T(8,128)} custom-call(f32[256,256]{1,0:T(8,128)} %gram_step.4.after_ref.before_ref, bf16[16,16,1024]{2,1,0:T(8,128)(2,1)} %get-tuple-element.44.after_ref.refs_16_, bf16[32,16,1024]{2,1,0:T(8,128)(2,1)} %get-tuple-element.41.after_ref.refs_0_.refs_12_, bf16[32,16,1024]{2,1,0:T(8,128)(2,1)} %gate.14.refs_1_.refs_13_, ...), custom_call_target="tpu_custom_call" | custom-call | bytes 65536 | tf_op jit(solution)/shard_map/gram_step/pallas_call | solution.py:283
  244.9 6.7 %collective-permute-done.11.value_ref = bf16[16,16,1024]{2,1,0:T(8,128)(2,1)} collective-permute-done((bf16[16,16,1024]{2,1,0:T(8,128)(2,1)S(1)}, bf16[16,16,1024]{2,1,0:T(8,128)(2,1)}, u32[]{:S(2)}, u32[]{:S(2)}) %collective-permute-start.11) | collective-permute-done | bytes 524320 | tf_op jit(solution)/shard_map/ppermute | solution.py:434
  252.2 1.6 collective-permute-done.13.refs_19_
  253.8 11.3 %polar_step.1 = f32[16,128,1024]{2,1,0:T(8,128)} custom-call(f32[1]{0:T(128)S(6)} %copy.28.shrink_ref, f32[256,256]{1,0:T(8,128)} %gram_step.5.after_ref.gram_ref, f32[16,32,1024]{2,1,0:T(8,128)} %get-tuple-element.45.refs_0_, f32[16,48,1024]{2,1,0:T(8,128)} %get-tuple-element.46.refs_1_, f32[16,32,1024]{2,1,0:T(8,128)} %get-tuple-element.47.refs_2_, ...), custom_call_target="tpu_custom_call" | custom-call | bytes 65536 | tf_op jit(solution)/shard_map/polar_step/pallas_call | solution.py:401
  (23 shorter events, 0.0 us)
Async XLA Ops:
  2.6 16.7 %collective-permute-start = (bf16[16,12,1024]{2,1,0:T(8,128)(2,1)}, bf16[16,12,1024]{2,1,0:T(8,128)(2,1)S(1)}, u32[]{:S(2)}, u32[]{:S(2)}) collective-permute-start(bf16[16,12,1024]{2,1,0:T(8,128)(2,1)} %get-tuple-element.28), channel_id=1, source_target_pairs={{4,8},{12,16},{20,24},{8,4},{16,12},{24,20},{5,9},{13,17},{21,25},... | collective-permute-start | bytes 1179656 | tf_op jit(solution)/shard_map/ppermute | solution.py:427
  19.3 0.8 copy-start.1
  20.1 49.4 %all-to-all-start = ((bf16[8,2,16,32,128]{4,3,2,1,0:T(8,128)(2,1)}), bf16[8,2,16,32,128]{4,3,2,1,0:T(8,128)(2,1)}, u32[]{:S(2)}, u32[]{:S(2)}) async-start(bf16[8,2,16,32,128]{4,3,2,1,0:T(8,128)(2,1)} %gate.8), calls=%async_computation | async-start | bytes 4194304 | tf_op jit(solution)/shard_map/all_to_all | solution.py:487
  25.4 33.7 %collective-permute-start.1 = (bf16[16,12,1024]{2,1,0:T(8,128)(2,1)}, bf16[16,12,1024]{2,1,0:T(8,128)(2,1)S(1)}, u32[]{:S(2)}, u32[]{:S(2)}) collective-permute-start(bf16[16,12,1024]{2,1,0:T(8,128)(2,1)} %get-tuple-element.29), channel_id=1, source_target_pairs={{0,4},{8,12},{16,20},{24,28},{4,0},{12,8},{20,16},{28,24},{1,5},{9... | collective-permute-start | bytes 1179656 | tf_op jit(solution)/shard_map/ppermute | solution.py:427
  59.1 0.8 copy-start.3
  59.9 17.3 %copy-start.2 = (bf16[16,12,1024]{2,1,0:T(8,128)(2,1)S(1)}, bf16[16,12,1024]{2,1,0:T(8,128)(2,1)}, u32[]{:S(2)}) copy-start(bf16[16,12,1024]{2,1,0:T(8,128)(2,1)} %copy-done.1) | copy-start | bytes 1179652
  59.9 17.3 %copy-start.4 = (bf16[16,12,1024]{2,1,0:T(8,128)(2,1)S(1)}, bf16[16,12,1024]{2,1,0:T(8,128)(2,1)}, u32[]{:S(2)}) copy-start(bf16[16,12,1024]{2,1,0:T(8,128)(2,1)} %copy-done.3) | copy-start | bytes 1179652
  69.5 74.6 %all-to-all-start.2 = ((bf16[8,2,16,48,128]{4,3,2,1,0:T(8,128)(2,1)}), bf16[8,2,16,48,128]{4,3,2,1,0:T(8,128)(2,1)}, u32[]{:S(2)}, u32[]{:S(2)}) async-start(bf16[8,2,16,48,128]{4,3,2,1,0:T(8,128)(2,1)} %gate.12), calls=%async_computation.2 | async-start | bytes 6291456 | tf_op jit(solution)/shard_map/all_to_all | solution.py:487
  96.9 24.2 %collective-permute-start.2 = (bf16[32,16,1024]{2,1,0:T(8,128)(2,1)}, bf16[32,16,1024]{2,1,0:T(8,128)(2,1)}, u32[]{:S(2)}, u32[]{:S(2)}) collective-permute-start(bf16[32,16,1024]{2,1,0:T(8,128)(2,1)} %get-tuple-element.33.after_ref.refs_0_.refs_4_), channel_id=1, source_target_pairs={{0,2},{1,3},{2,0},{3,1},{4,6},{5,7},{6,4},{7,5},{8,10},{9,11},{10,... | collective-permute-start | bytes 3145736 | tf_op jit(solution)/shard_map/ppermute | solution.py:434
  98.4 22.7 %collective-permute-start.3 = (bf16[32,16,1024]{2,1,0:T(8,128)(2,1)}, bf16[32,16,1024]{2,1,0:T(8,128)(2,1)}, u32[]{:S(2)}, u32[]{:S(2)}) collective-permute-start(bf16[32,16,1024]{2,1,0:T(8,128)(2,1)} %get-tuple-element.33.after_ref.refs_0_.refs_4_), channel_id=1, source_target_pairs={{0,1},{1,0},{2,3},{3,2},{4,5},{5,4},{6,7},{7,6},{8,9},{9,8},{10,11... | collective-permute-start | bytes 3145736 | tf_op jit(solution)/shard_map/ppermute | solution.py:434
  121.0 3.0 %collective-permute-start.4 = (bf16[32,16,1024]{2,1,0:T(8,128)(2,1)}, bf16[32,16,1024]{2,1,0:T(8,128)(2,1)}, u32[]{:S(2)}, u32[]{:S(2)}) collective-permute-start(bf16[32,16,1024]{2,1,0:T(8,128)(2,1)} %gate.10.refs_1_.refs_5_), channel_id=1, source_target_pairs={{0,1},{1,0},{2,3},{3,2},{4,5},{5,4},{6,7},{7,6},{8,9},{9,8},{10,11... | collective-permute-start | bytes 3145736 | tf_op jit(solution)/shard_map/ppermute | solution.py:434
  144.2 52.2 %all-to-all-start.1 = ((bf16[8,2,16,32,128]{4,3,2,1,0:T(8,128)(2,1)}), bf16[8,2,16,32,128]{4,3,2,1,0:T(8,128)(2,1)}, u32[]{:S(2)}, u32[]{:S(2)}) async-start(bf16[8,2,16,32,128]{4,3,2,1,0:T(8,128)(2,1)} %gate.11), calls=%async_computation.1 | async-start | bytes 4194304 | tf_op jit(solution)/shard_map/all_to_all | solution.py:487
  160.8 43.0 %collective-permute-start.5 = (bf16[48,16,1024]{2,1,0:T(8,128)(2,1)}, bf16[48,16,1024]{2,1,0:T(8,128)(2,1)}, u32[]{:S(2)}, u32[]{:S(2)}) collective-permute-start(bf16[48,16,1024]{2,1,0:T(8,128)(2,1)} %get-tuple-element.39.after_ref.refs_0_.refs_8_), channel_id=1, source_target_pairs={{0,2},{1,3},{2,0},{3,1},{4,6},{5,7},{6,4},{7,5},{8,10},{9,11},{10,... | collective-permute-start | bytes 4718600 | tf_op jit(solution)/shard_map/ppermute | solution.py:434
  196.3 29.6 %all-to-all-start.3 = ((bf16[8,2,16,16,128]{4,3,2,1,0:T(8,128)(2,1)}), bf16[8,2,16,16,128]{4,3,2,1,0:T(8,128)(2,1)}, u32[]{:S(2)}, u32[]{:S(2)}) async-start(bf16[8,2,16,16,128]{4,3,2,1,0:T(8,128)(2,1)} %get-tuple-element.42), calls=%async_computation.3 | async-start | bytes 2097152 | tf_op jit(solution)/shard_map/all_to_all | solution.py:487
  203.8 9.3 %collective-permute-start.6 = (bf16[48,16,1024]{2,1,0:T(8,128)(2,1)}, bf16[48,16,1024]{2,1,0:T(8,128)(2,1)}, u32[]{:S(2)}, u32[]{:S(2)}) collective-permute-start(bf16[48,16,1024]{2,1,0:T(8,128)(2,1)} %get-tuple-element.39.after_ref.refs_0_.refs_8_), channel_id=1, source_target_pairs={{0,1},{1,0},{2,3},{3,2},{4,5},{5,4},{6,7},{7,6},{8,9},{9,8},{10,11... | collective-permute-start | bytes 4718600 | tf_op jit(solution)/shard_map/ppermute | solution.py:434
  203.9 9.3 %collective-permute-start.7 = (bf16[48,16,1024]{2,1,0:T(8,128)(2,1)}, bf16[48,16,1024]{2,1,0:T(8,128)(2,1)}, u32[]{:S(2)}, u32[]{:S(2)}) collective-permute-start(bf16[48,16,1024]{2,1,0:T(8,128)(2,1)} %gate.13.refs_1_.refs_9_), channel_id=1, source_target_pairs={{0,1},{1,0},{2,3},{3,2},{4,5},{5,4},{6,7},{7,6},{8,9},{9,8},{10,11... | collective-permute-start | bytes 4718600 | tf_op jit(solution)/shard_map/ppermute | solution.py:434
  211.6 25.5 %collective-permute-start.8 = (bf16[32,16,1024]{2,1,0:T(8,128)(2,1)}, bf16[32,16,1024]{2,1,0:T(8,128)(2,1)}, u32[]{:S(2)}, u32[]{:S(2)}) collective-permute-start(bf16[32,16,1024]{2,1,0:T(8,128)(2,1)} %get-tuple-element.41.after_ref.refs_0_.refs_12_), channel_id=1, source_target_pairs={{0,2},{1,3},{2,0},{3,1},{4,6},{5,7},{6,4},{7,5},{8,10},{9,11},{10,... | collective-permute-start | bytes 3145736 | tf_op jit(solution)/shard_map/ppermute | solution.py:434
  213.1 25.7 %collective-permute-start.9 = (bf16[32,16,1024]{2,1,0:T(8,128)(2,1)}, bf16[32,16,1024]{2,1,0:T(8,128)(2,1)}, u32[]{:S(2)}, u32[]{:S(2)}) collective-permute-start(bf16[32,16,1024]{2,1,0:T(8,128)(2,1)} %get-tuple-element.41.after_ref.refs_0_.refs_12_), channel_id=1, source_target_pairs={{0,1},{1,0},{2,3},{3,2},{4,5},{5,4},{6,7},{7,6},{8,9},{9,8},{10,11... | collective-permute-start | bytes 3145736 | tf_op jit(solution)/shard_map/ppermute | solution.py:434
  231.7 5.5 %copy-start = (bf16[16,16,1024]{2,1,0:T(8,128)(2,1)S(1)}, bf16[16,16,1024]{2,1,0:T(8,128)(2,1)}, u32[]{:S(2)}) copy-start(bf16[16,16,1024]{2,1,0:T(8,128)(2,1)} %get-tuple-element.44.after_ref.refs_16_) | copy-start | bytes 1572868
  237.1 3.0 %collective-permute-start.10 = (bf16[32,16,1024]{2,1,0:T(8,128)(2,1)}, bf16[32,16,1024]{2,1,0:T(8,128)(2,1)}, u32[]{:S(2)}, u32[]{:S(2)}) collective-permute-start(bf16[32,16,1024]{2,1,0:T(8,128)(2,1)} %gate.14.refs_1_.refs_13_), channel_id=1, source_target_pairs={{0,1},{1,0},{2,3},{3,2},{4,5},{5,4},{6,7},{7,6},{8,9},{9,8},{10,11... | collective-permute-start | bytes 3145736 | tf_op jit(solution)/shard_map/ppermute | solution.py:434
  237.1 14.4 %collective-permute-start.11 = (bf16[16,16,1024]{2,1,0:T(8,128)(2,1)S(1)}, bf16[16,16,1024]{2,1,0:T(8,128)(2,1)}, u32[]{:S(2)}, u32[]{:S(2)}) collective-permute-start(bf16[16,16,1024]{2,1,0:T(8,128)(2,1)S(1)} %copy-done), channel_id=1, source_target_pairs={{0,2},{1,3},{2,0},{3,1},{4,6},{5,7},{6,4},{7,5},{8,10},{9,11},{10,... | collective-permute-start | bytes 1572872 | tf_op jit(solution)/shard_map/ppermute | solution.py:434
  238.6 13.6 %collective-permute-start.12 = (bf16[16,16,1024]{2,1,0:T(8,128)(2,1)S(1)}, bf16[16,16,1024]{2,1,0:T(8,128)(2,1)}, u32[]{:S(2)}, u32[]{:S(2)}) collective-permute-start(bf16[16,16,1024]{2,1,0:T(8,128)(2,1)S(1)} %copy-done), channel_id=1, source_target_pairs={{0,1},{1,0},{2,3},{3,2},{4,5},{5,4},{6,7},{7,6},{8,9},{9,8},{10,11... | collective-permute-start | bytes 1572872 | tf_op jit(solution)/shard_map/ppermute | solution.py:434
  251.6 2.3 collective-permute-start.13

commit v18 on v17

--- a/solution.py
+++ b/solution.py
@@ -292,6 +292,13 @@
     )(before, after, *pieces)
 
 
+def product(a, b):
+    a_high, b_high = a.astype(BF16), b.astype(BF16)
+    a_low, b_low = (a - a_high.astype(F32)).astype(BF16), (b - b_high.astype(F32)).astype(BF16)
+    left = jnp.concatenate([a_high, a_high, a_low], axis=1)
+    return dot_nn(left, jnp.concatenate([b_high, b_low, b_high], axis=0))
+
+
 def newton_schulz(gram):
     size = gram.shape[0]
     frob_norm = jnp.sqrt(jnp.sum(gram * gram))
@@ -300,9 +307,9 @@
     middle = 0.5 * (3.0 * identity - current)
     inverse = middle
     for iteration in range(1, NS_ITERS):
-        current = dot_nn(current, middle, HIGHEST)
-        middle = 0.5 * (3.0 * identity - dot_nn(inverse, current, HIGHEST))
-        inverse = dot_nn(middle, inverse, HIGHEST)
+        current = product(current, middle)
+        middle = 0.5 * (3.0 * identity - product(inverse, current))
+        inverse = product(middle, inverse)
     return inverse, frob_norm
 
 

time: 268 us -> 268 us (level)
  no operation moved by 1% of the time
where the time goes in v18:
time: 268 us; the launch traced here: 265 us
  waiting for transfers between devices  118 us (44%)
  Pallas kernels  102 us (38%)
  starting transfers between devices  38.8 us (14%)
  other arithmetic  3.84 us (1%)
    all_to_all x4, waiting for transfers between devices, first(): lax.all_to_all(sent, 'strip', split_axis=0, concat_axis=0, tiled=True)  58.1 us
    pallas_call x4, Pallas kernels, first_transform(): pl.pallas_call(first_body, grid=(chans // block,), in_specs=[pl.BlockSpec...  33.7 us
    ppermute x12, waiting for transfers between devices, swap(): return lax.ppermute(value, axis, [(i, i ^ bits) for i in range(count)])  32.2 us
    pallas_call x4, Pallas kernels, second_transform(): pl.pallas_call(second_body, grid=(side_len // block,), in_specs=[SMEM, pl...  29.3 us
    all_to_all x4, starting transfers between devices, first(): lax.all_to_all(sent, 'strip', split_axis=0, concat_axis=0, tiled=True)  28.1 us
    ppermute x2, waiting for transfers between devices, exchanged(): lax.ppermute(rows.astype(BF16), 'strip', pairs + [(j, i) for i, j in pairs])  27.6 us
    pallas_call x3, Pallas kernels, gram_step(): pl.pallas_call(functools.partial(gram_body, len(pieces)), grid=(rows // b...  16.1 us
    pallas_call x1, Pallas kernels, polar_step(): pl.pallas_call(functools.partial(polar_body, starts, sizes, groups), in_s...  11.5 us
  transfers between devices with their start and end apart: 18, of which 12 were waited for; matrix products, arithmetic and copies ran while one was open for 1% of the time, Pallas kernels for 34%

profile of v18, /device:TPU:12, one launch (start us, length us, event | category | flops | bytes accessed | tf_op | source)
XLA Modules:
  0.0 265.4 jit_solution(16430445890347807277)
XLA Ops:
  0.0 2.6 slice_select_fusion
  2.6 3.4 %collective-permute-start = (bf16[16,12,1024]{2,1,0:T(8,128)(2,1)}, bf16[16,12,1024]{2,1,0:T(8,128)(2,1)S(1)}, u32[]{:S(2)}, u32[]{:S(2)}) collective-permute-start(bf16[16,12,1024]{2,1,0:T(8,128)(2,1)} %get-tuple-element.28), channel_id=1, source_target_pairs={{4,8},{12,16},{20,24},{8,4},{16,12},{24,20},{5,9},{13,17},{21,25},... | collective-permute-start | bytes 1179656 | tf_op jit(solution)/shard_map/ppermute | solution.py:434
  6.1 8.5 %first_transform.4 = (bf16[8,2,16,32,128]{4,3,2,1,0:T(8,128)(2,1)}, f32[8,128]{1,0:T(8,128)}) custom-call(bf16[512,1024]{1,0:T(8,128)(2,1)} %constant.36.clone.table_ref, bf16[2,16,128,1024]{3,2,1,0:T(8,128)(2,1)} %grid_ref.7, s32[1]{0:T(128)} %bitcast.after_ref.strip_ref), custom_call_target="tpu_custom_call" | custom-call | bytes 65536 | tf_op jit(solution)/shard_map/first_transform/pallas_call | solution.py:112
  14.6 4.7 %collective-permute-done.after_ref = bf16[16,12,1024]{2,1,0:T(8,128)(2,1)S(1)} collective-permute-done((bf16[16,12,1024]{2,1,0:T(8,128)(2,1)}, bf16[16,12,1024]{2,1,0:T(8,128)(2,1)S(1)}, u32[]{:S(2)}, u32[]{:S(2)}) %collective-permute-start) | collective-permute-done | bytes 393248 | tf_op jit(solution)/shard_map/ppermute | solution.py:434
  19.3 0.8 copy-done.1
  20.1 5.3 %all-to-all-start = ((bf16[8,2,16,32,128]{4,3,2,1,0:T(8,128)(2,1)}), bf16[8,2,16,32,128]{4,3,2,1,0:T(8,128)(2,1)}, u32[]{:S(2)}, u32[]{:S(2)}) async-start(bf16[8,2,16,32,128]{4,3,2,1,0:T(8,128)(2,1)} %gate.8), calls=%async_computation | async-start | bytes 4194304 | tf_op jit(solution)/shard_map/all_to_all | solution.py:494
  25.4 0.6 collective-permute-start.1
  25.9 10.3 %first_transform.5 = (bf16[8,2,16,48,128]{4,3,2,1,0:T(8,128)(2,1)}, f32[8,128]{1,0:T(8,128)}) custom-call(bf16[768,1024]{1,0:T(8,128)(2,1)} %constant.37.clone.table_ref, bf16[2,16,128,1024]{3,2,1,0:T(8,128)(2,1)} %grid_ref.7, f32[8,128]{1,0:T(8,128)} %gate.9.after_ref), custom_call_target="tpu_custom_call" | custom-call | bytes 65536 | tf_op jit(solution)/shard_map/first_transform/pallas_call | solution.py:112
  36.2 22.9 %collective-permute-done.1.after_ref = bf16[16,12,1024]{2,1,0:T(8,128)(2,1)S(1)} collective-permute-done((bf16[16,12,1024]{2,1,0:T(8,128)(2,1)}, bf16[16,12,1024]{2,1,0:T(8,128)(2,1)S(1)}, u32[]{:S(2)}, u32[]{:S(2)}) %collective-permute-start.1) | collective-permute-done | bytes 393248 | tf_op jit(solution)/shard_map/ppermute | solution.py:434
  59.1 0.8 copy-done.3
  59.9 9.6 %all-to-all-done.half_ref = bf16[8,2,16,32,128]{4,3,2,1,0:T(8,128)(2,1)} async-done(((bf16[8,2,16,32,128]{4,3,2,1,0:T(8,128)(2,1)}), bf16[8,2,16,32,128]{4,3,2,1,0:T(8,128)(2,1)}, u32[]{:S(2)}, u32[]{:S(2)}) %all-to-all-start) | async-done | bytes 2097184 | tf_op jit(solution)/shard_map/all_to_all | solution.py:494
  69.5 7.7 %all-to-all-start.2 = ((bf16[8,2,16,48,128]{4,3,2,1,0:T(8,128)(2,1)}), bf16[8,2,16,48,128]{4,3,2,1,0:T(8,128)(2,1)}, u32[]{:S(2)}, u32[]{:S(2)}) async-start(bf16[8,2,16,48,128]{4,3,2,1,0:T(8,128)(2,1)} %gate.12), calls=%async_computation.2 | async-start | bytes 6291456 | tf_op jit(solution)/shard_map/all_to_all | solution.py:494
  77.2 0.1 broadcast_select_fusion.1
  77.3 1.1 pad_maximum_fusion.edge_ref
  78.4 11.1 %base_step.1 = (f32[16,32,1024]{2,1,0:T(8,128)}, f32[16,48,1024]{2,1,0:T(8,128)}, f32[16,32,1024]{2,1,0:T(8,128)}, f32[16,16,1024]{2,1,0:T(8,128)}) custom-call(s32[1]{0:T(128)} %bitcast.after_ref.strip_ref, f32[16]{0:T(128)} %step_ref.9, f32[3,4]{1,0:T(4,128)} %highpass_ref.1, f32[16,128,1024]{2,1,0:T(8,128)} %model_ref.1, ...), custom_call_target="tpu_custom_call" | custom-call | bytes 65536 | tf_op jit(solution)/shard_map/base_step/pallas_call | solution.py:193
  89.6 7.3 %second_transform.4 = (f32[16,32,1024]{2,1,0:T(8,128)}, bf16[32,16,1024]{2,1,0:T(8,128)(2,1)}) custom-call(f32[16]{0:T(128)} %step_ref.9, bf16[8,2,16,32,128]{4,3,2,1,0:T(8,128)(2,1)} %all-to-all-done.half_ref, bf16[1024,1024]{1,0:T(8,128)(2,1)} %constant.38.clone.cosine_ref, bf16[1024,1024]{1,0:T(8,128)(2,1)} %constant.39.clone.sine_ref, ...), custom_call_target="tpu_custom_call" | custom-call | bytes 65536 | tf_op jit(solution)/shard_map/second_transform/pallas_call | solution.py:236
  96.9 1.5 collective-permute-start.2
  98.4 0.0 collective-permute-start.3
  98.4 8.4 %first_transform.6 = (bf16[8,2,16,32,128]{4,3,2,1,0:T(8,128)(2,1)}, f32[8,128]{1,0:T(8,128)}) custom-call(bf16[512,1024]{1,0:T(8,128)(2,1)} %constant.40.clone.table_ref, bf16[2,16,128,1024]{3,2,1,0:T(8,128)(2,1)} %grid_ref.7, bf16[32,16,1024]{2,1,0:T(8,128)(2,1)} %get-tuple-element.33.after_ref.refs_0_.refs_4_), custom_call_target="tpu_custom_call" | custom-call | bytes 65536 | tf_op jit(solution)/shard_map/first_transform/pallas_call | solution.py:112
  106.8 14.2 %collective-permute-done.2.value_ref = bf16[32,16,1024]{2,1,0:T(8,128)(2,1)} collective-permute-done((bf16[32,16,1024]{2,1,0:T(8,128)(2,1)}, bf16[32,16,1024]{2,1,0:T(8,128)(2,1)}, u32[]{:S(2)}, u32[]{:S(2)}) %collective-permute-start.2) | collective-permute-done | bytes 1048608 | tf_op jit(solution)/shard_map/ppermute | solution.py:441
  121.0 3.0 %collective-permute-done.4.refs_3_.refs_7_ = bf16[32,16,1024]{2,1,0:T(8,128)(2,1)} collective-permute-done((bf16[32,16,1024]{2,1,0:T(8,128)(2,1)}, bf16[32,16,1024]{2,1,0:T(8,128)(2,1)}, u32[]{:S(2)}, u32[]{:S(2)}) %collective-permute-start.4) | collective-permute-done | bytes 1048608 | tf_op jit(solution)/shard_map/ppermute | solution.py:441
  124.0 0.7 broadcast_in_dim.3.before_ref
  124.8 4.8 %gram_step.3.after_ref.before_ref = f32[256,256]{1,0:T(8,128)} custom-call(f32[256,256]{1,0:T(8,128)} %broadcast_in_dim.3.before_ref, f32[8,128]{1,0:T(8,128)} %get-tuple-element.34.after_ref, bf16[32,16,1024]{2,1,0:T(8,128)(2,1)} %get-tuple-element.33.after_ref.refs_0_.refs_4_, bf16[32,16,1024]{2,1,0:T(8,128)(2,1)} %gate.10.refs_1_.refs_5_, ...), custom_call_target="tpu_custom_call" | custom-call | bytes 65536 | tf_op jit(solution)/shard_map/gram_step/pallas_call | solution.py:283
  129.5 14.6 %all-to-all-done.2.half_ref = bf16[8,2,16,48,128]{4,3,2,1,0:T(8,128)(2,1)} async-done(((bf16[8,2,16,48,128]{4,3,2,1,0:T(8,128)(2,1)}), bf16[8,2,16,48,128]{4,3,2,1,0:T(8,128)(2,1)}, u32[]{:S(2)}, u32[]{:S(2)}) %all-to-all-start.2) | async-done | bytes 3145760 | tf_op jit(solution)/shard_map/all_to_all | solution.py:494
  144.2 7.6 %all-to-all-start.1 = ((bf16[8,2,16,32,128]{4,3,2,1,0:T(8,128)(2,1)}), bf16[8,2,16,32,128]{4,3,2,1,0:T(8,128)(2,1)}, u32[]{:S(2)}, u32[]{:S(2)}) async-start(bf16[8,2,16,32,128]{4,3,2,1,0:T(8,128)(2,1)} %gate.11), calls=%async_computation.1 | async-start | bytes 4194304 | tf_op jit(solution)/shard_map/all_to_all | solution.py:494
  151.8 9.0 %second_transform.5 = (f32[16,48,1024]{2,1,0:T(8,128)}, bf16[48,16,1024]{2,1,0:T(8,128)(2,1)}) custom-call(f32[16]{0:T(128)} %step_ref.9, bf16[8,2,16,48,128]{4,3,2,1,0:T(8,128)(2,1)} %all-to-all-done.2.half_ref, bf16[1024,1024]{1,0:T(8,128)(2,1)} %constant.38.clone.cosine_ref, bf16[1024,1024]{1,0:T(8,128)(2,1)} %constant.39.clone.sine_ref, ...), custom_call_target="tpu_custom_call" | custom-call | bytes 65536 | tf_op jit(solution)/shard_map/second_transform/pallas_call | solution.py:236
  160.8 1.5 collective-permute-start.5
  162.3 6.5 %first_transform.7 = (bf16[8,2,16,16,128]{4,3,2,1,0:T(8,128)(2,1)}, f32[8,128]{1,0:T(8,128)}) custom-call(bf16[256,1024]{1,0:T(8,128)(2,1)} %constant.41.clone.table_ref, bf16[2,16,128,1024]{3,2,1,0:T(8,128)(2,1)} %grid_ref.7, bf16[48,16,1024]{2,1,0:T(8,128)(2,1)} %get-tuple-element.39.after_ref.refs_0_.refs_8_), custom_call_target="tpu_custom_call" | custom-call | bytes 65536 | tf_op jit(solution)/shard_map/first_transform/pallas_call | solution.py:112
  168.8 27.5 %all-to-all-done.1.half_ref = bf16[8,2,16,32,128]{4,3,2,1,0:T(8,128)(2,1)} async-done(((bf16[8,2,16,32,128]{4,3,2,1,0:T(8,128)(2,1)}), bf16[8,2,16,32,128]{4,3,2,1,0:T(8,128)(2,1)}, u32[]{:S(2)}, u32[]{:S(2)}) %all-to-all-start.1) | async-done | bytes 2097184 | tf_op jit(solution)/shard_map/all_to_all | solution.py:494
  196.3 7.5 %all-to-all-start.3 = ((bf16[8,2,16,16,128]{4,3,2,1,0:T(8,128)(2,1)}), bf16[8,2,16,16,128]{4,3,2,1,0:T(8,128)(2,1)}, u32[]{:S(2)}, u32[]{:S(2)}) async-start(bf16[8,2,16,16,128]{4,3,2,1,0:T(8,128)(2,1)} %get-tuple-element.42), calls=%async_computation.3 | async-start | bytes 2097152 | tf_op jit(solution)/shard_map/all_to_all | solution.py:494
  203.8 0.0 collective-permute-start.6
  203.8 0.0 collective-permute-done.5.value_ref
  203.9 0.5 collective-permute-start.7
  204.3 7.3 %second_transform.6 = (f32[16,32,1024]{2,1,0:T(8,128)}, bf16[32,16,1024]{2,1,0:T(8,128)(2,1)}) custom-call(f32[16]{0:T(128)} %step_ref.9, bf16[8,2,16,32,128]{4,3,2,1,0:T(8,128)(2,1)} %all-to-all-done.1.half_ref, bf16[1024,1024]{1,0:T(8,128)(2,1)} %constant.38.clone.cosine_ref, bf16[1024,1024]{1,0:T(8,128)(2,1)} %constant.39.clone.sine_ref, ...), custom_call_target="tpu_custom_call" | custom-call | bytes 65536 | tf_op jit(solution)/shard_map/second_transform/pallas_call | solution.py:236
  211.6 1.5 collective-permute-start.8
  213.1 0.0 collective-permute-start.9
  213.1 0.0 collective-permute-done.6.refs_2_.refs_10_
  213.1 6.5 %gram_step.4.after_ref.before_ref = f32[256,256]{1,0:T(8,128)} custom-call(f32[256,256]{1,0:T(8,128)} %gram_step.3.after_ref.before_ref, bf16[32,16,1024]{2,1,0:T(8,128)(2,1)} %get-tuple-element.41.after_ref.refs_0_.refs_12_, bf16[48,16,1024]{2,1,0:T(8,128)(2,1)} %get-tuple-element.39.after_ref.refs_0_.refs_8_, bf16[48,16,1024]{2,1,0:T(8,128)(2,1)} %gate.13.refs_1_.refs_9_, ...), custom_call_target="tpu_custom_call" | custom-call | bytes 65536 | tf_op jit(solution)/shard_map/gram_step/pallas_call | solution.py:283
  219.7 6.3 %all-to-all-done.3.half_ref = bf16[8,2,16,16,128]{4,3,2,1,0:T(8,128)(2,1)} async-done(((bf16[8,2,16,16,128]{4,3,2,1,0:T(8,128)(2,1)}), bf16[8,2,16,16,128]{4,3,2,1,0:T(8,128)(2,1)}, u32[]{:S(2)}, u32[]{:S(2)}) %all-to-all-start.3) | async-done | bytes 1048608 | tf_op jit(solution)/shard_map/all_to_all | solution.py:494
  226.0 5.7 %second_transform.7 = (f32[16,16,1024]{2,1,0:T(8,128)}, bf16[16,16,1024]{2,1,0:T(8,128)(2,1)}) custom-call(f32[16]{0:T(128)} %step_ref.9, bf16[8,2,16,16,128]{4,3,2,1,0:T(8,128)(2,1)} %all-to-all-done.3.half_ref, bf16[1024,1024]{1,0:T(8,128)(2,1)} %constant.38.clone.cosine_ref, bf16[1024,1024]{1,0:T(8,128)(2,1)} %constant.39.clone.sine_ref, ...), custom_call_target="tpu_custom_call" | custom-call | bytes 65536 | tf_op jit(solution)/shard_map/second_transform/pallas_call | solution.py:236
  231.7 5.4 %collective-permute-done.8.value_ref = bf16[32,16,1024]{2,1,0:T(8,128)(2,1)} collective-permute-done((bf16[32,16,1024]{2,1,0:T(8,128)(2,1)}, bf16[32,16,1024]{2,1,0:T(8,128)(2,1)}, u32[]{:S(2)}, u32[]{:S(2)}) %collective-permute-start.8) | collective-permute-done | bytes 1048608 | tf_op jit(solution)/shard_map/ppermute | solution.py:441
  237.1 1.5 collective-permute-start.11
  238.6 0.2 collective-permute-start.12
  238.8 1.3 collective-permute-done.10.refs_3_.refs_15_
  240.1 4.8 %gram_step.5.after_ref.gram_ref = f32[256,256]{1,0:T(8,128)} custom-call(f32[256,256]{1,0:T(8,128)} %gram_step.4.after_ref.before_ref, bf16[16,16,1024]{2,1,0:T(8,128)(2,1)} %get-tuple-element.44.after_ref.refs_16_, bf16[32,16,1024]{2,1,0:T(8,128)(2,1)} %get-tuple-element.41.after_ref.refs_0_.refs_12_, bf16[32,16,1024]{2,1,0:T(8,128)(2,1)} %gate.14.refs_1_.refs_13_, ...), custom_call_target="tpu_custom_call" | custom-call | bytes 65536 | tf_op jit(solution)/shard_map/gram_step/pallas_call | solution.py:283
  244.9 6.7 %collective-permute-done.11.value_ref = bf16[16,16,1024]{2,1,0:T(8,128)(2,1)} collective-permute-done((bf16[16,16,1024]{2,1,0:T(8,128)(2,1)S(1)}, bf16[16,16,1024]{2,1,0:T(8,128)(2,1)}, u32[]{:S(2)}, u32[]{:S(2)}) %collective-permute-start.11) | collective-permute-done | bytes 524320 | tf_op jit(solution)/shard_map/ppermute | solution.py:441
  252.2 1.6 collective-permute-done.13.refs_19_
  253.8 11.5 %polar_step.1 = f32[16,128,1024]{2,1,0:T(8,128)} custom-call(f32[1]{0:T(128)S(6)} %copy.28.shrink_ref, f32[256,256]{1,0:T(8,128)} %gram_step.5.after_ref.gram_ref, f32[16,32,1024]{2,1,0:T(8,128)} %get-tuple-element.45.refs_0_, f32[16,48,1024]{2,1,0:T(8,128)} %get-tuple-element.46.refs_1_, f32[16,32,1024]{2,1,0:T(8,128)} %get-tuple-element.47.refs_2_, ...), custom_call_target="tpu_custom_call" | custom-call | bytes 65536 | tf_op jit(solution)/shard_map/polar_step/pallas_call | solution.py:408
  (23 shorter events, 0.0 us)
Async XLA Ops:
  2.6 16.7 %collective-permute-start = (bf16[16,12,1024]{2,1,0:T(8,128)(2,1)}, bf16[16,12,1024]{2,1,0:T(8,128)(2,1)S(1)}, u32[]{:S(2)}, u32[]{:S(2)}) collective-permute-start(bf16[16,12,1024]{2,1,0:T(8,128)(2,1)} %get-tuple-element.28), channel_id=1, source_target_pairs={{4,8},{12,16},{20,24},{8,4},{16,12},{24,20},{5,9},{13,17},{21,25},... | collective-permute-start | bytes 1179656 | tf_op jit(solution)/shard_map/ppermute | solution.py:434
  19.3 0.8 copy-start.1
  20.1 49.4 %all-to-all-start = ((bf16[8,2,16,32,128]{4,3,2,1,0:T(8,128)(2,1)}), bf16[8,2,16,32,128]{4,3,2,1,0:T(8,128)(2,1)}, u32[]{:S(2)}, u32[]{:S(2)}) async-start(bf16[8,2,16,32,128]{4,3,2,1,0:T(8,128)(2,1)} %gate.8), calls=%async_computation | async-start | bytes 4194304 | tf_op jit(solution)/shard_map/all_to_all | solution.py:494
  25.4 33.7 %collective-permute-start.1 = (bf16[16,12,1024]{2,1,0:T(8,128)(2,1)}, bf16[16,12,1024]{2,1,0:T(8,128)(2,1)S(1)}, u32[]{:S(2)}, u32[]{:S(2)}) collective-permute-start(bf16[16,12,1024]{2,1,0:T(8,128)(2,1)} %get-tuple-element.29), channel_id=1, source_target_pairs={{0,4},{8,12},{16,20},{24,28},{4,0},{12,8},{20,16},{28,24},{1,5},{9... | collective-permute-start | bytes 1179656 | tf_op jit(solution)/shard_map/ppermute | solution.py:434
  59.1 0.8 copy-start.3
  59.9 17.3 %copy-start.2 = (bf16[16,12,1024]{2,1,0:T(8,128)(2,1)S(1)}, bf16[16,12,1024]{2,1,0:T(8,128)(2,1)}, u32[]{:S(2)}) copy-start(bf16[16,12,1024]{2,1,0:T(8,128)(2,1)} %copy-done.1) | copy-start | bytes 1179652
  59.9 17.3 %copy-start.4 = (bf16[16,12,1024]{2,1,0:T(8,128)(2,1)S(1)}, bf16[16,12,1024]{2,1,0:T(8,128)(2,1)}, u32[]{:S(2)}) copy-start(bf16[16,12,1024]{2,1,0:T(8,128)(2,1)} %copy-done.3) | copy-start | bytes 1179652
  69.5 74.6 %all-to-all-start.2 = ((bf16[8,2,16,48,128]{4,3,2,1,0:T(8,128)(2,1)}), bf16[8,2,16,48,128]{4,3,2,1,0:T(8,128)(2,1)}, u32[]{:S(2)}, u32[]{:S(2)}) async-start(bf16[8,2,16,48,128]{4,3,2,1,0:T(8,128)(2,1)} %gate.12), calls=%async_computation.2 | async-start | bytes 6291456 | tf_op jit(solution)/shard_map/all_to_all | solution.py:494
  96.9 24.2 %collective-permute-start.2 = (bf16[32,16,1024]{2,1,0:T(8,128)(2,1)}, bf16[32,16,1024]{2,1,0:T(8,128)(2,1)}, u32[]{:S(2)}, u32[]{:S(2)}) collective-permute-start(bf16[32,16,1024]{2,1,0:T(8,128)(2,1)} %get-tuple-element.33.after_ref.refs_0_.refs_4_), channel_id=1, source_target_pairs={{0,2},{1,3},{2,0},{3,1},{4,6},{5,7},{6,4},{7,5},{8,10},{9,11},{10,... | collective-permute-start | bytes 3145736 | tf_op jit(solution)/shard_map/ppermute | solution.py:441
  98.4 22.7 %collective-permute-start.3 = (bf16[32,16,1024]{2,1,0:T(8,128)(2,1)}, bf16[32,16,1024]{2,1,0:T(8,128)(2,1)}, u32[]{:S(2)}, u32[]{:S(2)}) collective-permute-start(bf16[32,16,1024]{2,1,0:T(8,128)(2,1)} %get-tuple-element.33.after_ref.refs_0_.refs_4_), channel_id=1, source_target_pairs={{0,1},{1,0},{2,3},{3,2},{4,5},{5,4},{6,7},{7,6},{8,9},{9,8},{10,11... | collective-permute-start | bytes 3145736 | tf_op jit(solution)/shard_map/ppermute | solution.py:441
  121.0 3.0 %collective-permute-start.4 = (bf16[32,16,1024]{2,1,0:T(8,128)(2,1)}, bf16[32,16,1024]{2,1,0:T(8,128)(2,1)}, u32[]{:S(2)}, u32[]{:S(2)}) collective-permute-start(bf16[32,16,1024]{2,1,0:T(8,128)(2,1)} %gate.10.refs_1_.refs_5_), channel_id=1, source_target_pairs={{0,1},{1,0},{2,3},{3,2},{4,5},{5,4},{6,7},{7,6},{8,9},{9,8},{10,11... | collective-permute-start | bytes 3145736 | tf_op jit(solution)/shard_map/ppermute | solution.py:441
  144.2 52.2 %all-to-all-start.1 = ((bf16[8,2,16,32,128]{4,3,2,1,0:T(8,128)(2,1)}), bf16[8,2,16,32,128]{4,3,2,1,0:T(8,128)(2,1)}, u32[]{:S(2)}, u32[]{:S(2)}) async-start(bf16[8,2,16,32,128]{4,3,2,1,0:T(8,128)(2,1)} %gate.11), calls=%async_computation.1 | async-start | bytes 4194304 | tf_op jit(solution)/shard_map/all_to_all | solution.py:494
  160.8 43.0 %collective-permute-start.5 = (bf16[48,16,1024]{2,1,0:T(8,128)(2,1)}, bf16[48,16,1024]{2,1,0:T(8,128)(2,1)}, u32[]{:S(2)}, u32[]{:S(2)}) collective-permute-start(bf16[48,16,1024]{2,1,0:T(8,128)(2,1)} %get-tuple-element.39.after_ref.refs_0_.refs_8_), channel_id=1, source_target_pairs={{0,2},{1,3},{2,0},{3,1},{4,6},{5,7},{6,4},{7,5},{8,10},{9,11},{10,... | collective-permute-start | bytes 4718600 | tf_op jit(solution)/shard_map/ppermute | solution.py:441
  196.3 29.6 %all-to-all-start.3 = ((bf16[8,2,16,16,128]{4,3,2,1,0:T(8,128)(2,1)}), bf16[8,2,16,16,128]{4,3,2,1,0:T(8,128)(2,1)}, u32[]{:S(2)}, u32[]{:S(2)}) async-start(bf16[8,2,16,16,128]{4,3,2,1,0:T(8,128)(2,1)} %get-tuple-element.42), calls=%async_computation.3 | async-start | bytes 2097152 | tf_op jit(solution)/shard_map/all_to_all | solution.py:494
  203.8 9.3 %collective-permute-start.6 = (bf16[48,16,1024]{2,1,0:T(8,128)(2,1)}, bf16[48,16,1024]{2,1,0:T(8,128)(2,1)}, u32[]{:S(2)}, u32[]{:S(2)}) collective-permute-start(bf16[48,16,1024]{2,1,0:T(8,128)(2,1)} %get-tuple-element.39.after_ref.refs_0_.refs_8_), channel_id=1, source_target_pairs={{0,1},{1,0},{2,3},{3,2},{4,5},{5,4},{6,7},{7,6},{8,9},{9,8},{10,11... | collective-permute-start | bytes 4718600 | tf_op jit(solution)/shard_map/ppermute | solution.py:441
  203.9 9.3 %collective-permute-start.7 = (bf16[48,16,1024]{2,1,0:T(8,128)(2,1)}, bf16[48,16,1024]{2,1,0:T(8,128)(2,1)}, u32[]{:S(2)}, u32[]{:S(2)}) collective-permute-start(bf16[48,16,1024]{2,1,0:T(8,128)(2,1)} %gate.13.refs_1_.refs_9_), channel_id=1, source_target_pairs={{0,1},{1,0},{2,3},{3,2},{4,5},{5,4},{6,7},{7,6},{8,9},{9,8},{10,11... | collective-permute-start | bytes 4718600 | tf_op jit(solution)/shard_map/ppermute | solution.py:441
  211.6 25.5 %collective-permute-start.8 = (bf16[32,16,1024]{2,1,0:T(8,128)(2,1)}, bf16[32,16,1024]{2,1,0:T(8,128)(2,1)}, u32[]{:S(2)}, u32[]{:S(2)}) collective-permute-start(bf16[32,16,1024]{2,1,0:T(8,128)(2,1)} %get-tuple-element.41.after_ref.refs_0_.refs_12_), channel_id=1, source_target_pairs={{0,2},{1,3},{2,0},{3,1},{4,6},{5,7},{6,4},{7,5},{8,10},{9,11},{10,... | collective-permute-start | bytes 3145736 | tf_op jit(solution)/shard_map/ppermute | solution.py:441
  213.1 25.7 %collective-permute-start.9 = (bf16[32,16,1024]{2,1,0:T(8,128)(2,1)}, bf16[32,16,1024]{2,1,0:T(8,128)(2,1)}, u32[]{:S(2)}, u32[]{:S(2)}) collective-permute-start(bf16[32,16,1024]{2,1,0:T(8,128)(2,1)} %get-tuple-element.41.after_ref.refs_0_.refs_12_), channel_id=1, source_target_pairs={{0,1},{1,0},{2,3},{3,2},{4,5},{5,4},{6,7},{7,6},{8,9},{9,8},{10,11... | collective-permute-start | bytes 3145736 | tf_op jit(solution)/shard_map/ppermute | solution.py:441
  231.7 5.5 %copy-start = (bf16[16,16,1024]{2,1,0:T(8,128)(2,1)S(1)}, bf16[16,16,1024]{2,1,0:T(8,128)(2,1)}, u32[]{:S(2)}) copy-start(bf16[16,16,1024]{2,1,0:T(8,128)(2,1)} %get-tuple-element.44.after_ref.refs_16_) | copy-start | bytes 1572868
  237.1 3.0 %collective-permute-start.10 = (bf16[32,16,1024]{2,1,0:T(8,128)(2,1)}, bf16[32,16,1024]{2,1,0:T(8,128)(2,1)}, u32[]{:S(2)}, u32[]{:S(2)}) collective-permute-start(bf16[32,16,1024]{2,1,0:T(8,128)(2,1)} %gate.14.refs_1_.refs_13_), channel_id=1, source_target_pairs={{0,1},{1,0},{2,3},{3,2},{4,5},{5,4},{6,7},{7,6},{8,9},{9,8},{10,11... | collective-permute-start | bytes 3145736 | tf_op jit(solution)/shard_map/ppermute | solution.py:441
  237.1 14.4 %collective-permute-start.11 = (bf16[16,16,1024]{2,1,0:T(8,128)(2,1)S(1)}, bf16[16,16,1024]{2,1,0:T(8,128)(2,1)}, u32[]{:S(2)}, u32[]{:S(2)}) collective-permute-start(bf16[16,16,1024]{2,1,0:T(8,128)(2,1)S(1)} %copy-done), channel_id=1, source_target_pairs={{0,2},{1,3},{2,0},{3,1},{4,6},{5,7},{6,4},{7,5},{8,10},{9,11},{10,... | collective-permute-start | bytes 1572872 | tf_op jit(solution)/shard_map/ppermute | solution.py:441
  238.6 13.6 %collective-permute-start.12 = (bf16[16,16,1024]{2,1,0:T(8,128)(2,1)S(1)}, bf16[16,16,1024]{2,1,0:T(8,128)(2,1)}, u32[]{:S(2)}, u32[]{:S(2)}) collective-permute-start(bf16[16,16,1024]{2,1,0:T(8,128)(2,1)S(1)} %copy-done), channel_id=1, source_target_pairs={{0,1},{1,0},{2,3},{3,2},{4,5},{5,4},{6,7},{7,6},{8,9},{9,8},{10,11... | collective-permute-start | bytes 1572872 | tf_op jit(solution)/shard_map/ppermute | solution.py:441
  251.6 2.3 collective-permute-start.13

commit v19 on v17

--- a/solution.py
+++ b/solution.py
@@ -58,8 +58,7 @@
 
 def chunk_rows(own_rows):
     quarter = own_rows // 4
-    sizes = [quarter, own_rows - 2 * quarter - EDGE_ROWS, quarter, EDGE_ROWS]
-    sizes = [size for size in sizes if size > 0]
+    sizes = [own_rows - quarter - EDGE_ROWS, quarter, EDGE_ROWS]
     return [sum(sizes[:place]) for place in range(len(sizes))], sizes
 
 
@@ -469,7 +468,6 @@
     moved = {}
     gathered = {}
     pixels = {}
-    done = set()
     state = dict(last=strip, gram=jnp.zeros((GRAM_ROWS * size, GRAM_ROWS * size), F32), bases=None)
 
     def first(chunk):
@@ -479,11 +477,8 @@
             state["last"] = gate(state["last"], outer)
         if chunk == 1:
             sent = gate(sent, inner)
-        if chunk == 2:
-            gather(0)
-            gram(0)
-            done.add(0)
-            sent = gate(sent, state["gram"])
+            base()
+            sent = gate(sent, state["last"])
         halves[chunk] = lax.all_to_all(sent, "strip", split_axis=0, concat_axis=0, tiled=True)
 
     def base():
@@ -509,21 +504,16 @@
         state["last"] = state["gram"]
 
     first(0)
-    if chunks > 1:
-        first(1)
-    base()
-    for chunk in range(chunks):
-        second(chunk)
-        if chunk + 2 < chunks:
-            first(chunk + 2)
-        if chunk == 1:
-            gather(1)
-        if chunk >= 1 and chunk - 1 not in done:
-            if chunk - 1 not in gathered:
-                gather(chunk - 1)
-            gram(chunk - 1)
-    if chunks - 1 not in gathered:
-        gather(chunks - 1)
+    first(1)
+    first(2)
+    second(0)
+    second(1)
+    gather(0)
+    second(2)
+    gather(1)
+    gram(0)
+    gram(1)
+    gather(2)
     order = range(chunks)
     return polar_step(
         shrinkage, state["gram"], [moved[k] for k in order], [gathered[k] for k in order], starts, sizes

time: 268 us -> 284 us (1.060)
  waiting for transfers between devices: 118 us -> 151 us
  starting transfers between devices: 38.8 us -> 29.6 us
  Pallas kernels: 102 us -> 93.2 us
    ppermute x2, waiting for transfers between devices: 27.6 us -> 45 us  [exchanged(): lax.ppermute(rows.astype(BF16), 'strip', pairs + [(j, i) for i, j in pairs])]
    all_to_all x4 -> x3, waiting for transfers between devices: 58.1 us -> 68.7 us  [first(): lax.all_to_all(sent, 'strip', split_axis=0, concat_axis=0, tiled=True)]
    all_to_all x4 -> x3, starting transfers between devices: 28.1 us -> 20.3 us  [first(): lax.all_to_all(sent, 'strip', split_axis=0, concat_axis=0, tiled=True)]
    ppermute x12 -> x9, waiting for transfers between devices: 32.2 us -> 37.3 us  [swap(): return lax.ppermute(value, axis, [(i, i ^ bits) for i in range(count)])]
    pallas_call x4 -> x3, Pallas kernels: 29.3 us -> 25.5 us  [second_transform(): pl.pallas_call(second_body, grid=(side_len // block,), in_specs=[SMEM, pl...]
    pallas_call x4 -> x3, Pallas kernels: 33.7 us -> 30.2 us  [first_transform(): pl.pallas_call(first_body, grid=(chans // block,), in_specs=[pl.BlockSpec...]
    ppermute x12 -> x9, starting transfers between devices: 6.7 us -> 5.3 us  [swap(): return lax.ppermute(value, axis, [(i, i ^ bits) for i in range(count)])]
    pallas_call x3 -> x2, Pallas kernels: 16.1 us -> 14.9 us  [gram_step(): pl.pallas_call(functools.partial(gram_body, len(pieces)), grid=(rows // b...]
  transfers between devices with their start and end apart: 18 -> 14, of which waited for: 12 -> 6; matrix products, arithmetic and copies ran while one was open for 1% -> 1% of each run, Pallas kernels for 34% -> 29%
where the time goes in v19:
time: 284 us; the launch traced here: 281 us
  waiting for transfers between devices  151 us (53%)
  Pallas kernels  93.2 us (33%)
  starting transfers between devices  29.6 us (10%)
  other arithmetic  4.92 us (2%)
    all_to_all x3, waiting for transfers between devices, first(): lax.all_to_all(sent, 'strip', split_axis=0, concat_axis=0, tiled=True)  68.7 us
    ppermute x2, waiting for transfers between devices, exchanged(): lax.ppermute(rows.astype(BF16), 'strip', pairs + [(j, i) for i, j in pairs])  45 us
    ppermute x9, waiting for transfers between devices, swap(): return lax.ppermute(value, axis, [(i, i ^ bits) for i in range(count)])  37.3 us
    pallas_call x3, Pallas kernels, first_transform(): pl.pallas_call(first_body, grid=(chans // block,), in_specs=[pl.BlockSpec...  30.2 us
    pallas_call x3, Pallas kernels, second_transform(): pl.pallas_call(second_body, grid=(side_len // block,), in_specs=[SMEM, pl...  25.5 us
    all_to_all x3, starting transfers between devices, first(): lax.all_to_all(sent, 'strip', split_axis=0, concat_axis=0, tiled=True)  20.3 us
    pallas_call x2, Pallas kernels, gram_step(): pl.pallas_call(functools.partial(gram_body, len(pieces)), grid=(rows // b...  14.9 us
    pallas_call x1, Pallas kernels, polar_step(): pl.pallas_call(functools.partial(polar_body, starts, sizes, groups), in_s...  11.3 us
  transfers between devices with their start and end apart: 14, of which 6 were waited for; matrix products, arithmetic and copies ran while one was open for 1% of the time, Pallas kernels for 29%

profile of v19, /device:TPU:12, one launch (start us, length us, event | category | flops | bytes accessed | tf_op | source)
XLA Modules:
  0.0 281.0 jit_solution(9743535041618246037)
XLA Ops:
  0.0 2.7 slice_select_fusion
  2.7 3.4 %collective-permute-start.1 = (bf16[16,12,1024]{2,1,0:T(8,128)(2,1)}, bf16[16,12,1024]{2,1,0:T(8,128)(2,1)S(1)}, u32[]{:S(2)}, u32[]{:S(2)}) collective-permute-start(bf16[16,12,1024]{2,1,0:T(8,128)(2,1)} %get-tuple-element.23), channel_id=1, source_target_pairs={{4,8},{12,16},{20,24},{8,4},{16,12},{24,20},{5,9},{13,17},{21,25},... | collective-permute-start | bytes 1179656 | tf_op jit(solution)/shard_map/ppermute | solution.py:426
  6.1 15.2 %first_transform.3 = (bf16[8,2,16,80,128]{4,3,2,1,0:T(8,128)(2,1)}, f32[8,128]{1,0:T(8,128)}) custom-call(bf16[1280,1024]{1,0:T(8,128)(2,1)} %constant.34.clone.table_ref, bf16[2,16,128,1024]{3,2,1,0:T(8,128)(2,1)} %grid_ref.5, s32[1]{0:T(128)} %bitcast.after_ref.strip_ref), custom_call_target="tpu_custom_call" | custom-call | bytes 65536 | tf_op jit(solution)/shard_map/first_transform/pallas_call | solution.py:111
  21.3 0.0 collective-permute-done.1.after_ref
  21.3 0.0 copy-start.1
  21.3 0.8 copy-done.1
  22.1 5.2 %all-to-all-start.2 = ((bf16[8,2,16,80,128]{4,3,2,1,0:T(8,128)(2,1)}), bf16[8,2,16,80,128]{4,3,2,1,0:T(8,128)(2,1)}, u32[]{:S(2)}, u32[]{:S(2)}) async-start(bf16[8,2,16,80,128]{4,3,2,1,0:T(8,128)(2,1)} %gate.10), calls=%async_computation.2 | async-start | bytes 10485760 | tf_op jit(solution)/shard_map/all_to_all | solution.py:482
  27.4 0.6 collective-permute-start
  27.9 0.0 copy-start.2
  27.9 8.5 %first_transform.4 = (bf16[8,2,16,32,128]{4,3,2,1,0:T(8,128)(2,1)}, f32[8,128]{1,0:T(8,128)}) custom-call(bf16[512,1024]{1,0:T(8,128)(2,1)} %constant.35.clone.table_ref, bf16[2,16,128,1024]{3,2,1,0:T(8,128)(2,1)} %grid_ref.5, f32[8,128]{1,0:T(8,128)} %gate.7.after_ref), custom_call_target="tpu_custom_call" | custom-call | bytes 65536 | tf_op jit(solution)/shard_map/first_transform/pallas_call | solution.py:111
  36.5 45.0 %collective-permute-done.after_ref = bf16[16,12,1024]{2,1,0:T(8,128)(2,1)} collective-permute-done((bf16[16,12,1024]{2,1,0:T(8,128)(2,1)}, bf16[16,12,1024]{2,1,0:T(8,128)(2,1)}, u32[]{:S(2)}, u32[]{:S(2)}) %collective-permute-start) | collective-permute-done | bytes 393248 | tf_op jit(solution)/shard_map/ppermute | solution.py:426
  81.4 0.0 copy-done.2
  81.4 1.1 broadcast_select_fusion.1
  82.6 1.1 pad_maximum_fusion.edge_ref
  83.7 11.2 %base_step.1 = (f32[16,80,1024]{2,1,0:T(8,128)}, f32[16,32,1024]{2,1,0:T(8,128)}, f32[16,16,1024]{2,1,0:T(8,128)}) custom-call(s32[1]{0:T(128)} %bitcast.after_ref.strip_ref, f32[16]{0:T(128)} %step_ref.7, f32[3,4]{1,0:T(4,128)} %highpass_ref.1, f32[16,128,1024]{2,1,0:T(8,128)} %model_ref.1, bf16[16,24,1024]{2,1,0:T(8,128)(2,1)} %pad_maximum_fusion.edge_ref, ...), custom_call_target="tpu_custom_call" | custom-call | bytes 65536 | tf_op jit(solution)/shard_map/base_step/pallas_call | solution.py:192
  94.9 44.6 %all-to-all-done.2.half_ref = bf16[8,2,16,80,128]{4,3,2,1,0:T(8,128)(2,1)} async-done(((bf16[8,2,16,80,128]{4,3,2,1,0:T(8,128)(2,1)}), bf16[8,2,16,80,128]{4,3,2,1,0:T(8,128)(2,1)}, u32[]{:S(2)}, u32[]{:S(2)}) %all-to-all-start.2) | async-done | bytes 5242912 | tf_op jit(solution)/shard_map/all_to_all | solution.py:482
  139.4 7.6 %all-to-all-start.1 = ((bf16[8,2,16,32,128]{4,3,2,1,0:T(8,128)(2,1)}), bf16[8,2,16,32,128]{4,3,2,1,0:T(8,128)(2,1)}, u32[]{:S(2)}, u32[]{:S(2)}) async-start(bf16[8,2,16,32,128]{4,3,2,1,0:T(8,128)(2,1)} %gate.9), calls=%async_computation.1 | async-start | bytes 4194304 | tf_op jit(solution)/shard_map/all_to_all | solution.py:482
  147.0 6.5 %first_transform.5 = (bf16[8,2,16,16,128]{4,3,2,1,0:T(8,128)(2,1)}, f32[8,128]{1,0:T(8,128)}) custom-call(bf16[256,1024]{1,0:T(8,128)(2,1)} %constant.36.clone.table_ref, bf16[2,16,128,1024]{3,2,1,0:T(8,128)(2,1)} %grid_ref.5, f32[16,80,1024]{2,1,0:T(8,128)} %get-tuple-element.26.after_ref.base_ref), custom_call_target="tpu_custom_call" | custom-call | bytes 65536 | tf_op jit(solution)/shard_map/first_transform/pallas_call | solution.py:111
  153.5 12.5 %second_transform.3 = (f32[16,80,1024]{2,1,0:T(8,128)}, bf16[80,16,1024]{2,1,0:T(8,128)(2,1)}) custom-call(f32[16]{0:T(128)} %step_ref.7, bf16[8,2,16,80,128]{4,3,2,1,0:T(8,128)(2,1)} %all-to-all-done.2.half_ref, bf16[1024,1024]{1,0:T(8,128)(2,1)} %constant.37.clone.cosine_ref, bf16[1024,1024]{1,0:T(8,128)(2,1)} %constant.38.clone.sine_ref, ...), custom_call_target="tpu_custom_call" | custom-call | bytes 65536 | tf_op jit(solution)/shard_map/second_transform/pallas_call | solution.py:235
  166.0 1.5 collective-permute-start.2
  167.5 24.1 %all-to-all-done.1.half_ref = bf16[8,2,16,32,128]{4,3,2,1,0:T(8,128)(2,1)} async-done(((bf16[8,2,16,32,128]{4,3,2,1,0:T(8,128)(2,1)}), bf16[8,2,16,32,128]{4,3,2,1,0:T(8,128)(2,1)}, u32[]{:S(2)}, u32[]{:S(2)}) %all-to-all-start.1) | async-done | bytes 2097184 | tf_op jit(solution)/shard_map/all_to_all | solution.py:482
  191.6 7.5 %all-to-all-start = ((bf16[8,2,16,16,128]{4,3,2,1,0:T(8,128)(2,1)}), bf16[8,2,16,16,128]{4,3,2,1,0:T(8,128)(2,1)}, u32[]{:S(2)}, u32[]{:S(2)}) async-start(bf16[8,2,16,16,128]{4,3,2,1,0:T(8,128)(2,1)} %get-tuple-element.27), calls=%async_computation | async-start | bytes 2097152 | tf_op jit(solution)/shard_map/all_to_all | solution.py:482
  199.1 0.0 collective-permute-start.3
  199.1 7.3 %second_transform.4 = (f32[16,32,1024]{2,1,0:T(8,128)}, bf16[32,16,1024]{2,1,0:T(8,128)(2,1)}) custom-call(f32[16]{0:T(128)} %step_ref.7, bf16[8,2,16,32,128]{4,3,2,1,0:T(8,128)(2,1)} %all-to-all-done.1.half_ref, bf16[1024,1024]{1,0:T(8,128)(2,1)} %constant.37.clone.cosine_ref, bf16[1024,1024]{1,0:T(8,128)(2,1)} %constant.38.clone.sine_ref, ...), custom_call_target="tpu_custom_call" | custom-call | bytes 65536 | tf_op jit(solution)/shard_map/second_transform/pallas_call | solution.py:235
  206.4 17.5 %collective-permute-done.2.value_ref = bf16[80,16,1024]{2,1,0:T(8,128)(2,1)} collective-permute-done((bf16[80,16,1024]{2,1,0:T(8,128)(2,1)}, bf16[80,16,1024]{2,1,0:T(8,128)(2,1)}, u32[]{:S(2)}, u32[]{:S(2)}) %collective-permute-start.2) | collective-permute-done | bytes 2621472 | tf_op jit(solution)/shard_map/ppermute | solution.py:433
  224.0 0.0 collective-permute-start.4
  224.0 1.5 collective-permute-start.5
  225.5 0.2 collective-permute-start.6
  225.7 0.0 all-to-all-done.half_ref
  225.7 5.8 %second_transform.5 = (f32[16,16,1024]{2,1,0:T(8,128)}, bf16[16,16,1024]{2,1,0:T(8,128)(2,1)}) custom-call(f32[16]{0:T(128)} %step_ref.7, bf16[8,2,16,16,128]{4,3,2,1,0:T(8,128)(2,1)} %all-to-all-done.half_ref, bf16[1024,1024]{1,0:T(8,128)(2,1)} %constant.37.clone.cosine_ref, bf16[1024,1024]{1,0:T(8,128)(2,1)} %constant.38.clone.sine_ref, ...), custom_call_target="tpu_custom_call" | custom-call | bytes 65536 | tf_op jit(solution)/shard_map/second_transform/pallas_call | solution.py:235
  231.5 0.0 copy-start
  231.5 18.4 %collective-permute-done.5.value_ref = bf16[32,16,1024]{2,1,0:T(8,128)(2,1)} collective-permute-done((bf16[32,16,1024]{2,1,0:T(8,128)(2,1)}, bf16[32,16,1024]{2,1,0:T(8,128)(2,1)}, u32[]{:S(2)}, u32[]{:S(2)}) %collective-permute-start.5) | collective-permute-done | bytes 1048608 | tf_op jit(solution)/shard_map/ppermute | solution.py:433
  249.9 0.0 collective-permute-start.7
  249.9 0.0 copy-done
  249.9 1.5 collective-permute-start.8
  251.4 0.0 collective-permute-done.3.refs_2_.refs_5_
  251.4 0.2 collective-permute-start.9
  251.6 0.0 collective-permute-done.4.refs_3_.refs_6_
  251.6 0.7 broadcast_in_dim.3.before_ref
  252.3 10.0 %gram_step.2.before_ref.after_ref = f32[256,256]{1,0:T(8,128)} custom-call(f32[256,256]{1,0:T(8,128)} %broadcast_in_dim.3.before_ref, bf16[16,16,1024]{2,1,0:T(8,128)(2,1)} %get-tuple-element.35.after_ref.refs_11_, bf16[80,16,1024]{2,1,0:T(8,128)(2,1)} %get-tuple-element.33.after_ref.refs_0_.refs_3_, bf16[80,16,1024]{2,1,0:T(8,128)(2,1)} %gate.11.refs_1_.refs_4_, ...), custom_call_target="tpu_custom_call" | custom-call | bytes 65536 | tf_op jit(solution)/shard_map/gram_step/pallas_call | solution.py:282
  262.3 0.0 collective-permute-done.6.refs_2_.refs_9_
  262.4 0.0 collective-permute-done.7.refs_3_.refs_10_
  262.4 4.8 %gram_step.3.after_ref.gram_ref = f32[256,256]{1,0:T(8,128)} custom-call(f32[256,256]{1,0:T(8,128)} %gram_step.2.before_ref.after_ref, f32[256,256]{1,0:T(8,128)} %gram_step.2.before_ref.after_ref, bf16[32,16,1024]{2,1,0:T(8,128)(2,1)} %get-tuple-element.34.after_ref.refs_0_.refs_7_, bf16[32,16,1024]{2,1,0:T(8,128)(2,1)} %gate.12.refs_1_.refs_8_, ...), custom_call_target="tpu_custom_call" | custom-call | bytes 65536 | tf_op jit(solution)/shard_map/gram_step/pallas_call | solution.py:282
  267.2 0.0 collective-permute-done.8.value_ref
  267.2 0.3 collective-permute-start.10
  268.2 0.0 collective-permute-done.9.refs_13_
  268.2 1.3 collective-permute-done.10.refs_14_
  269.5 11.3 %polar_step.1 = f32[16,128,1024]{2,1,0:T(8,128)} custom-call(f32[1]{0:T(128)S(6)} %copy.25.shrink_ref, f32[256,256]{1,0:T(8,128)} %gram_step.3.after_ref.gram_ref, f32[16,80,1024]{2,1,0:T(8,128)} %get-tuple-element.36.refs_0_, f32[16,32,1024]{2,1,0:T(8,128)} %get-tuple-element.37.refs_1_, f32[16,16,1024]{2,1,0:T(8,128)} %get-tuple-element.38.refs_2_, ...), custom_call_target="tpu_custom_call" | custom-call | bytes 65536 | tf_op jit(solution)/shard_map/polar_step/pallas_call | solution.py:400
  (7 shorter events, 0.0 us)
Async XLA Ops:
  2.7 18.6 %collective-permute-start.1 = (bf16[16,12,1024]{2,1,0:T(8,128)(2,1)}, bf16[16,12,1024]{2,1,0:T(8,128)(2,1)S(1)}, u32[]{:S(2)}, u32[]{:S(2)}) collective-permute-start(bf16[16,12,1024]{2,1,0:T(8,128)(2,1)} %get-tuple-element.23), channel_id=1, source_target_pairs={{4,8},{12,16},{20,24},{8,4},{16,12},{24,20},{5,9},{13,17},{21,25},... | collective-permute-start | bytes 1179656 | tf_op jit(solution)/shard_map/ppermute | solution.py:426
  21.3 0.8 copy-start.1
  22.1 117.3 %all-to-all-start.2 = ((bf16[8,2,16,80,128]{4,3,2,1,0:T(8,128)(2,1)}), bf16[8,2,16,80,128]{4,3,2,1,0:T(8,128)(2,1)}, u32[]{:S(2)}, u32[]{:S(2)}) async-start(bf16[8,2,16,80,128]{4,3,2,1,0:T(8,128)(2,1)} %gate.10), calls=%async_computation.2 | async-start | bytes 10485760 | tf_op jit(solution)/shard_map/all_to_all | solution.py:482
  27.4 54.1 %collective-permute-start = (bf16[16,12,1024]{2,1,0:T(8,128)(2,1)}, bf16[16,12,1024]{2,1,0:T(8,128)(2,1)}, u32[]{:S(2)}, u32[]{:S(2)}) collective-permute-start(bf16[16,12,1024]{2,1,0:T(8,128)(2,1)} %get-tuple-element.22), channel_id=1, source_target_pairs={{0,4},{8,12},{16,20},{24,28},{4,0},{12,8},{20,16},{28,24},{1,5},{9... | collective-permute-start | bytes 1179656 | tf_op jit(solution)/shard_map/ppermute | solution.py:426
  27.9 53.5 %copy-start.2 = (bf16[16,12,1024]{2,1,0:T(8,128)(2,1)S(1)}, bf16[16,12,1024]{2,1,0:T(8,128)(2,1)}, u32[]{:S(2)}) copy-start(bf16[16,12,1024]{2,1,0:T(8,128)(2,1)} %copy-done.1) | copy-start | bytes 1179652
  139.4 52.2 %all-to-all-start.1 = ((bf16[8,2,16,32,128]{4,3,2,1,0:T(8,128)(2,1)}), bf16[8,2,16,32,128]{4,3,2,1,0:T(8,128)(2,1)}, u32[]{:S(2)}, u32[]{:S(2)}) async-start(bf16[8,2,16,32,128]{4,3,2,1,0:T(8,128)(2,1)} %gate.9), calls=%async_computation.1 | async-start | bytes 4194304 | tf_op jit(solution)/shard_map/all_to_all | solution.py:482
  166.0 58.0 %collective-permute-start.2 = (bf16[80,16,1024]{2,1,0:T(8,128)(2,1)}, bf16[80,16,1024]{2,1,0:T(8,128)(2,1)}, u32[]{:S(2)}, u32[]{:S(2)}) collective-permute-start(bf16[80,16,1024]{2,1,0:T(8,128)(2,1)} %get-tuple-element.33.after_ref.refs_0_.refs_3_), channel_id=1, source_target_pairs={{0,2},{1,3},{2,0},{3,1},{4,6},{5,7},{6,4},{7,5},{8,10},{9,11},{10,... | collective-permute-start | bytes 7864328 | tf_op jit(solution)/shard_map/ppermute | solution.py:433
  191.6 34.1 %all-to-all-start = ((bf16[8,2,16,16,128]{4,3,2,1,0:T(8,128)(2,1)}), bf16[8,2,16,16,128]{4,3,2,1,0:T(8,128)(2,1)}, u32[]{:S(2)}, u32[]{:S(2)}) async-start(bf16[8,2,16,16,128]{4,3,2,1,0:T(8,128)(2,1)} %get-tuple-element.27), calls=%async_computation | async-start | bytes 2097152 | tf_op jit(solution)/shard_map/all_to_all | solution.py:482
  199.1 52.2 %collective-permute-start.3 = (bf16[80,16,1024]{2,1,0:T(8,128)(2,1)}, bf16[80,16,1024]{2,1,0:T(8,128)(2,1)}, u32[]{:S(2)}, u32[]{:S(2)}) collective-permute-start(bf16[80,16,1024]{2,1,0:T(8,128)(2,1)} %get-tuple-element.33.after_ref.refs_0_.refs_3_), channel_id=1, source_target_pairs={{0,1},{1,0},{2,3},{3,2},{4,5},{5,4},{6,7},{7,6},{8,9},{9,8},{10,11... | collective-permute-start | bytes 7864328 | tf_op jit(solution)/shard_map/ppermute | solution.py:433
  224.0 27.6 %collective-permute-start.4 = (bf16[80,16,1024]{2,1,0:T(8,128)(2,1)}, bf16[80,16,1024]{2,1,0:T(8,128)(2,1)}, u32[]{:S(2)}, u32[]{:S(2)}) collective-permute-start(bf16[80,16,1024]{2,1,0:T(8,128)(2,1)} %gate.11.refs_1_.refs_4_), channel_id=1, source_target_pairs={{0,1},{1,0},{2,3},{3,2},{4,5},{5,4},{6,7},{7,6},{8,9},{9,8},{10,11... | collective-permute-start | bytes 7864328 | tf_op jit(solution)/shard_map/ppermute | solution.py:433
  224.0 25.9 %collective-permute-start.5 = (bf16[32,16,1024]{2,1,0:T(8,128)(2,1)}, bf16[32,16,1024]{2,1,0:T(8,128)(2,1)}, u32[]{:S(2)}, u32[]{:S(2)}) collective-permute-start(bf16[32,16,1024]{2,1,0:T(8,128)(2,1)} %get-tuple-element.34.after_ref.refs_0_.refs_7_), channel_id=1, source_target_pairs={{0,2},{1,3},{2,0},{3,1},{4,6},{5,7},{6,4},{7,5},{8,10},{9,11},{10,... | collective-permute-start | bytes 3145736 | tf_op jit(solution)/shard_map/ppermute | solution.py:433
  225.5 36.9 %collective-permute-start.6 = (bf16[32,16,1024]{2,1,0:T(8,128)(2,1)}, bf16[32,16,1024]{2,1,0:T(8,128)(2,1)}, u32[]{:S(2)}, u32[]{:S(2)}) collective-permute-start(bf16[32,16,1024]{2,1,0:T(8,128)(2,1)} %get-tuple-element.34.after_ref.refs_0_.refs_7_), channel_id=1, source_target_pairs={{0,1},{1,0},{2,3},{3,2},{4,5},{5,4},{6,7},{7,6},{8,9},{9,8},{10,11... | collective-permute-start | bytes 3145736 | tf_op jit(solution)/shard_map/ppermute | solution.py:433
  231.5 18.4 %copy-start = (bf16[16,16,1024]{2,1,0:T(8,128)(2,1)S(1)}, bf16[16,16,1024]{2,1,0:T(8,128)(2,1)}, u32[]{:S(2)}) copy-start(bf16[16,16,1024]{2,1,0:T(8,128)(2,1)} %get-tuple-element.35.after_ref.refs_11_) | copy-start | bytes 1572868
  249.9 12.5 %collective-permute-start.7 = (bf16[32,16,1024]{2,1,0:T(8,128)(2,1)}, bf16[32,16,1024]{2,1,0:T(8,128)(2,1)}, u32[]{:S(2)}, u32[]{:S(2)}) collective-permute-start(bf16[32,16,1024]{2,1,0:T(8,128)(2,1)} %gate.12.refs_1_.refs_8_), channel_id=1, source_target_pairs={{0,1},{1,0},{2,3},{3,2},{4,5},{5,4},{6,7},{7,6},{8,9},{9,8},{10,11... | collective-permute-start | bytes 3145736 | tf_op jit(solution)/shard_map/ppermute | solution.py:433
  249.9 17.3 %collective-permute-start.8 = (bf16[16,16,1024]{2,1,0:T(8,128)(2,1)S(1)}, bf16[16,16,1024]{2,1,0:T(8,128)(2,1)}, u32[]{:S(2)}, u32[]{:S(2)}) collective-permute-start(bf16[16,16,1024]{2,1,0:T(8,128)(2,1)S(1)} %copy-done), channel_id=1, source_target_pairs={{0,2},{1,3},{2,0},{3,1},{4,6},{5,7},{6,4},{7,5},{8,10},{9,11},{10,... | collective-permute-start | bytes 1572872 | tf_op jit(solution)/shard_map/ppermute | solution.py:433
  251.4 16.8 %collective-permute-start.9 = (bf16[16,16,1024]{2,1,0:T(8,128)(2,1)S(1)}, bf16[16,16,1024]{2,1,0:T(8,128)(2,1)}, u32[]{:S(2)}, u32[]{:S(2)}) collective-permute-start(bf16[16,16,1024]{2,1,0:T(8,128)(2,1)S(1)} %copy-done), channel_id=1, source_target_pairs={{0,1},{1,0},{2,3},{3,2},{4,5},{5,4},{6,7},{7,6},{8,9},{9,8},{10,11... | collective-permute-start | bytes 1572872 | tf_op jit(solution)/shard_map/ppermute | solution.py:433
  267.2 2.3 collective-permute-start.10

commit v20 on v17

--- a/solution.py
+++ b/solution.py
@@ -232,7 +232,7 @@
         dirty = dirty - jnp.einsum("scmu,sul->cml", half[:, 1], sine_table.reshape(split), preferred_element_type=F32)
         moved = base + step_size[:, None, None] * dirty
         return moved, moved.astype(BF16).transpose(1, 0, 2)
-    block = min(256, side_len)
+    block = min(512, side_len)
     return pl.pallas_call(
         second_body,
         grid=(side_len // block,),

time: 268 us -> 268 us (level)
  no operation moved by 1% of the time
where the time goes in v20:
time: 268 us; the launch traced here: 265 us
  waiting for transfers between devices  119 us (44%)
  Pallas kernels  101 us (38%)
  starting transfers between devices  38.8 us (14%)
  other arithmetic  3.84 us (1%)
    all_to_all x4, waiting for transfers between devices, first(): lax.all_to_all(sent, 'strip', split_axis=0, concat_axis=0, tiled=True)  58.4 us
    pallas_call x4, Pallas kernels, first_transform(): pl.pallas_call(first_body, grid=(chans // block,), in_specs=[pl.BlockSpec...  33.7 us
    ppermute x12, waiting for transfers between devices, swap(): return lax.ppermute(value, axis, [(i, i ^ bits) for i in range(count)])  32.7 us
    pallas_call x4, Pallas kernels, second_transform(): pl.pallas_call(second_body, grid=(side_len // block,), in_specs=[SMEM, pl...  28.2 us
    all_to_all x4, starting transfers between devices, first(): lax.all_to_all(sent, 'strip', split_axis=0, concat_axis=0, tiled=True)  28.1 us
    ppermute x2, waiting for transfers between devices, exchanged(): lax.ppermute(rows.astype(BF16), 'strip', pairs + [(j, i) for i, j in pairs])  27.6 us
    pallas_call x3, Pallas kernels, gram_step(): pl.pallas_call(functools.partial(gram_body, len(pieces)), grid=(rows // b...  16.1 us
    pallas_call x1, Pallas kernels, polar_step(): pl.pallas_call(functools.partial(polar_body, starts, sizes, groups), in_s...  11.3 us
  transfers between devices with their start and end apart: 18, of which 12 were waited for; matrix products, arithmetic and copies ran while one was open for 1% of the time, Pallas kernels for 34%

profile of v20, /device:TPU:12, one launch (start us, length us, event | category | flops | bytes accessed | tf_op | source)
XLA Modules:
  0.0 265.1 jit_solution(7013847810750498348)
XLA Ops:
  0.0 2.6 slice_select_fusion
  2.6 3.4 %collective-permute-start = (bf16[16,12,1024]{2,1,0:T(8,128)(2,1)}, bf16[16,12,1024]{2,1,0:T(8,128)(2,1)S(1)}, u32[]{:S(2)}, u32[]{:S(2)}) collective-permute-start(bf16[16,12,1024]{2,1,0:T(8,128)(2,1)} %get-tuple-element.28), channel_id=1, source_target_pairs={{4,8},{12,16},{20,24},{8,4},{16,12},{24,20},{5,9},{13,17},{21,25},... | collective-permute-start | bytes 1179656 | tf_op jit(solution)/shard_map/ppermute | solution.py:427
  6.1 8.5 %first_transform.4 = (bf16[8,2,16,32,128]{4,3,2,1,0:T(8,128)(2,1)}, f32[8,128]{1,0:T(8,128)}) custom-call(bf16[512,1024]{1,0:T(8,128)(2,1)} %constant.36.clone.table_ref, bf16[2,16,128,1024]{3,2,1,0:T(8,128)(2,1)} %grid_ref.7, s32[1]{0:T(128)} %bitcast.after_ref.strip_ref), custom_call_target="tpu_custom_call" | custom-call | bytes 65536 | tf_op jit(solution)/shard_map/first_transform/pallas_call | solution.py:112
  14.6 4.7 %collective-permute-done.after_ref = bf16[16,12,1024]{2,1,0:T(8,128)(2,1)S(1)} collective-permute-done((bf16[16,12,1024]{2,1,0:T(8,128)(2,1)}, bf16[16,12,1024]{2,1,0:T(8,128)(2,1)S(1)}, u32[]{:S(2)}, u32[]{:S(2)}) %collective-permute-start) | collective-permute-done | bytes 393248 | tf_op jit(solution)/shard_map/ppermute | solution.py:427
  19.3 0.8 copy-done.1
  20.1 5.3 %all-to-all-start = ((bf16[8,2,16,32,128]{4,3,2,1,0:T(8,128)(2,1)}), bf16[8,2,16,32,128]{4,3,2,1,0:T(8,128)(2,1)}, u32[]{:S(2)}, u32[]{:S(2)}) async-start(bf16[8,2,16,32,128]{4,3,2,1,0:T(8,128)(2,1)} %gate.8), calls=%async_computation | async-start | bytes 4194304 | tf_op jit(solution)/shard_map/all_to_all | solution.py:487
  25.4 0.6 collective-permute-start.1
  25.9 10.3 %first_transform.5 = (bf16[8,2,16,48,128]{4,3,2,1,0:T(8,128)(2,1)}, f32[8,128]{1,0:T(8,128)}) custom-call(bf16[768,1024]{1,0:T(8,128)(2,1)} %constant.37.clone.table_ref, bf16[2,16,128,1024]{3,2,1,0:T(8,128)(2,1)} %grid_ref.7, f32[8,128]{1,0:T(8,128)} %gate.9.after_ref), custom_call_target="tpu_custom_call" | custom-call | bytes 65536 | tf_op jit(solution)/shard_map/first_transform/pallas_call | solution.py:112
  36.2 22.9 %collective-permute-done.1.after_ref = bf16[16,12,1024]{2,1,0:T(8,128)(2,1)S(1)} collective-permute-done((bf16[16,12,1024]{2,1,0:T(8,128)(2,1)}, bf16[16,12,1024]{2,1,0:T(8,128)(2,1)S(1)}, u32[]{:S(2)}, u32[]{:S(2)}) %collective-permute-start.1) | collective-permute-done | bytes 393248 | tf_op jit(solution)/shard_map/ppermute | solution.py:427
  59.1 0.8 copy-done.3
  59.9 9.6 %all-to-all-done.half_ref = bf16[8,2,16,32,128]{4,3,2,1,0:T(8,128)(2,1)} async-done(((bf16[8,2,16,32,128]{4,3,2,1,0:T(8,128)(2,1)}), bf16[8,2,16,32,128]{4,3,2,1,0:T(8,128)(2,1)}, u32[]{:S(2)}, u32[]{:S(2)}) %all-to-all-start) | async-done | bytes 2097184 | tf_op jit(solution)/shard_map/all_to_all | solution.py:487
  69.5 7.7 %all-to-all-start.2 = ((bf16[8,2,16,48,128]{4,3,2,1,0:T(8,128)(2,1)}), bf16[8,2,16,48,128]{4,3,2,1,0:T(8,128)(2,1)}, u32[]{:S(2)}, u32[]{:S(2)}) async-start(bf16[8,2,16,48,128]{4,3,2,1,0:T(8,128)(2,1)} %gate.12), calls=%async_computation.2 | async-start | bytes 6291456 | tf_op jit(solution)/shard_map/all_to_all | solution.py:487
  77.2 0.1 broadcast_select_fusion.1
  77.3 1.1 pad_maximum_fusion.edge_ref
  78.4 11.1 %base_step.1 = (f32[16,32,1024]{2,1,0:T(8,128)}, f32[16,48,1024]{2,1,0:T(8,128)}, f32[16,32,1024]{2,1,0:T(8,128)}, f32[16,16,1024]{2,1,0:T(8,128)}) custom-call(s32[1]{0:T(128)} %bitcast.after_ref.strip_ref, f32[16]{0:T(128)} %step_ref.9, f32[3,4]{1,0:T(4,128)} %highpass_ref.1, f32[16,128,1024]{2,1,0:T(8,128)} %model_ref.1, ...), custom_call_target="tpu_custom_call" | custom-call | bytes 65536 | tf_op jit(solution)/shard_map/base_step/pallas_call | solution.py:193
  89.6 7.1 %second_transform.4 = (f32[16,32,1024]{2,1,0:T(8,128)}, bf16[32,16,1024]{2,1,0:T(8,128)(2,1)}) custom-call(f32[16]{0:T(128)} %step_ref.9, bf16[8,2,16,32,128]{4,3,2,1,0:T(8,128)(2,1)} %all-to-all-done.half_ref, bf16[1024,1024]{1,0:T(8,128)(2,1)} %constant.38.clone.cosine_ref, bf16[1024,1024]{1,0:T(8,128)(2,1)} %constant.39.clone.sine_ref, ...), custom_call_target="tpu_custom_call" | custom-call | bytes 65536 | tf_op jit(solution)/shard_map/second_transform/pallas_call | solution.py:236
  96.6 1.5 collective-permute-start.2
  98.1 8.4 %first_transform.6 = (bf16[8,2,16,32,128]{4,3,2,1,0:T(8,128)(2,1)}, f32[8,128]{1,0:T(8,128)}) custom-call(bf16[512,1024]{1,0:T(8,128)(2,1)} %constant.40.clone.table_ref, bf16[2,16,128,1024]{3,2,1,0:T(8,128)(2,1)} %grid_ref.7, bf16[32,16,1024]{2,1,0:T(8,128)(2,1)} %get-tuple-element.33.after_ref.refs_0_.refs_4_), custom_call_target="tpu_custom_call" | custom-call | bytes 65536 | tf_op jit(solution)/shard_map/first_transform/pallas_call | solution.py:112
  106.5 14.2 %collective-permute-done.2.value_ref = bf16[32,16,1024]{2,1,0:T(8,128)(2,1)} collective-permute-done((bf16[32,16,1024]{2,1,0:T(8,128)(2,1)}, bf16[32,16,1024]{2,1,0:T(8,128)(2,1)}, u32[]{:S(2)}, u32[]{:S(2)}) %collective-permute-start.2) | collective-permute-done | bytes 1048608 | tf_op jit(solution)/shard_map/ppermute | solution.py:434
  120.8 0.0 collective-permute-start.4
  120.8 0.0 collective-permute-done.3.refs_2_.refs_6_
  120.8 3.0 %collective-permute-done.4.refs_3_.refs_7_ = bf16[32,16,1024]{2,1,0:T(8,128)(2,1)} collective-permute-done((bf16[32,16,1024]{2,1,0:T(8,128)(2,1)}, bf16[32,16,1024]{2,1,0:T(8,128)(2,1)}, u32[]{:S(2)}, u32[]{:S(2)}) %collective-permute-start.4) | collective-permute-done | bytes 1048608 | tf_op jit(solution)/shard_map/ppermute | solution.py:434
  123.8 0.7 broadcast_in_dim.3.before_ref
  124.5 4.8 %gram_step.3.after_ref.before_ref = f32[256,256]{1,0:T(8,128)} custom-call(f32[256,256]{1,0:T(8,128)} %broadcast_in_dim.3.before_ref, f32[8,128]{1,0:T(8,128)} %get-tuple-element.34.after_ref, bf16[32,16,1024]{2,1,0:T(8,128)(2,1)} %get-tuple-element.33.after_ref.refs_0_.refs_4_, bf16[32,16,1024]{2,1,0:T(8,128)(2,1)} %gate.10.refs_1_.refs_5_, ...), custom_call_target="tpu_custom_call" | custom-call | bytes 65536 | tf_op jit(solution)/shard_map/gram_step/pallas_call | solution.py:283
  129.3 14.9 %all-to-all-done.2.half_ref = bf16[8,2,16,48,128]{4,3,2,1,0:T(8,128)(2,1)} async-done(((bf16[8,2,16,48,128]{4,3,2,1,0:T(8,128)(2,1)}), bf16[8,2,16,48,128]{4,3,2,1,0:T(8,128)(2,1)}, u32[]{:S(2)}, u32[]{:S(2)}) %all-to-all-start.2) | async-done | bytes 3145760 | tf_op jit(solution)/shard_map/all_to_all | solution.py:487
  144.2 7.6 %all-to-all-start.1 = ((bf16[8,2,16,32,128]{4,3,2,1,0:T(8,128)(2,1)}), bf16[8,2,16,32,128]{4,3,2,1,0:T(8,128)(2,1)}, u32[]{:S(2)}, u32[]{:S(2)}) async-start(bf16[8,2,16,32,128]{4,3,2,1,0:T(8,128)(2,1)} %gate.11), calls=%async_computation.1 | async-start | bytes 4194304 | tf_op jit(solution)/shard_map/all_to_all | solution.py:487
  151.8 9.1 %second_transform.5 = (f32[16,48,1024]{2,1,0:T(8,128)}, bf16[48,16,1024]{2,1,0:T(8,128)(2,1)}) custom-call(f32[16]{0:T(128)} %step_ref.9, bf16[8,2,16,48,128]{4,3,2,1,0:T(8,128)(2,1)} %all-to-all-done.2.half_ref, bf16[1024,1024]{1,0:T(8,128)(2,1)} %constant.38.clone.cosine_ref, bf16[1024,1024]{1,0:T(8,128)(2,1)} %constant.39.clone.sine_ref, ...), custom_call_target="tpu_custom_call" | custom-call | bytes 65536 | tf_op jit(solution)/shard_map/second_transform/pallas_call | solution.py:236
  160.9 1.5 collective-permute-start.5
  162.4 6.5 %first_transform.7 = (bf16[8,2,16,16,128]{4,3,2,1,0:T(8,128)(2,1)}, f32[8,128]{1,0:T(8,128)}) custom-call(bf16[256,1024]{1,0:T(8,128)(2,1)} %constant.41.clone.table_ref, bf16[2,16,128,1024]{3,2,1,0:T(8,128)(2,1)} %grid_ref.7, bf16[48,16,1024]{2,1,0:T(8,128)(2,1)} %get-tuple-element.39.after_ref.refs_0_.refs_8_), custom_call_target="tpu_custom_call" | custom-call | bytes 65536 | tf_op jit(solution)/shard_map/first_transform/pallas_call | solution.py:112
  168.9 27.4 %all-to-all-done.1.half_ref = bf16[8,2,16,32,128]{4,3,2,1,0:T(8,128)(2,1)} async-done(((bf16[8,2,16,32,128]{4,3,2,1,0:T(8,128)(2,1)}), bf16[8,2,16,32,128]{4,3,2,1,0:T(8,128)(2,1)}, u32[]{:S(2)}, u32[]{:S(2)}) %all-to-all-start.1) | async-done | bytes 2097184 | tf_op jit(solution)/shard_map/all_to_all | solution.py:487
  196.3 7.5 %all-to-all-start.3 = ((bf16[8,2,16,16,128]{4,3,2,1,0:T(8,128)(2,1)}), bf16[8,2,16,16,128]{4,3,2,1,0:T(8,128)(2,1)}, u32[]{:S(2)}, u32[]{:S(2)}) async-start(bf16[8,2,16,16,128]{4,3,2,1,0:T(8,128)(2,1)} %get-tuple-element.42), calls=%async_computation.3 | async-start | bytes 2097152 | tf_op jit(solution)/shard_map/all_to_all | solution.py:487
  203.8 0.0 collective-permute-start.6
  203.8 0.0 collective-permute-done.5.value_ref
  203.9 0.5 collective-permute-start.7
  204.3 7.1 %second_transform.6 = (f32[16,32,1024]{2,1,0:T(8,128)}, bf16[32,16,1024]{2,1,0:T(8,128)(2,1)}) custom-call(f32[16]{0:T(128)} %step_ref.9, bf16[8,2,16,32,128]{4,3,2,1,0:T(8,128)(2,1)} %all-to-all-done.1.half_ref, bf16[1024,1024]{1,0:T(8,128)(2,1)} %constant.38.clone.cosine_ref, bf16[1024,1024]{1,0:T(8,128)(2,1)} %constant.39.clone.sine_ref, ...), custom_call_target="tpu_custom_call" | custom-call | bytes 65536 | tf_op jit(solution)/shard_map/second_transform/pallas_call | solution.py:236
  211.4 1.5 collective-permute-start.8
  212.9 0.0 collective-permute-start.9
  212.9 6.5 %gram_step.4.after_ref.before_ref = f32[256,256]{1,0:T(8,128)} custom-call(f32[256,256]{1,0:T(8,128)} %gram_step.3.after_ref.before_ref, bf16[32,16,1024]{2,1,0:T(8,128)(2,1)} %get-tuple-element.41.after_ref.refs_0_.refs_12_, bf16[48,16,1024]{2,1,0:T(8,128)(2,1)} %get-tuple-element.39.after_ref.refs_0_.refs_8_, bf16[48,16,1024]{2,1,0:T(8,128)(2,1)} %gate.13.refs_1_.refs_9_, ...), custom_call_target="tpu_custom_call" | custom-call | bytes 65536 | tf_op jit(solution)/shard_map/gram_step/pallas_call | solution.py:283
  219.5 6.5 %all-to-all-done.3.half_ref = bf16[8,2,16,16,128]{4,3,2,1,0:T(8,128)(2,1)} async-done(((bf16[8,2,16,16,128]{4,3,2,1,0:T(8,128)(2,1)}), bf16[8,2,16,16,128]{4,3,2,1,0:T(8,128)(2,1)}, u32[]{:S(2)}, u32[]{:S(2)}) %all-to-all-start.3) | async-done | bytes 1048608 | tf_op jit(solution)/shard_map/all_to_all | solution.py:487
  226.0 5.0 %second_transform.7 = (f32[16,16,1024]{2,1,0:T(8,128)}, bf16[16,16,1024]{2,1,0:T(8,128)(2,1)}) custom-call(f32[16]{0:T(128)} %step_ref.9, bf16[8,2,16,16,128]{4,3,2,1,0:T(8,128)(2,1)} %all-to-all-done.3.half_ref, bf16[1024,1024]{1,0:T(8,128)(2,1)} %constant.38.clone.cosine_ref, bf16[1024,1024]{1,0:T(8,128)(2,1)} %constant.39.clone.sine_ref, ...), custom_call_target="tpu_custom_call" | custom-call | bytes 65536 | tf_op jit(solution)/shard_map/second_transform/pallas_call | solution.py:236
  230.9 6.0 %collective-permute-done.8.value_ref = bf16[32,16,1024]{2,1,0:T(8,128)(2,1)} collective-permute-done((bf16[32,16,1024]{2,1,0:T(8,128)(2,1)}, bf16[32,16,1024]{2,1,0:T(8,128)(2,1)}, u32[]{:S(2)}, u32[]{:S(2)}) %collective-permute-start.8) | collective-permute-done | bytes 1048608 | tf_op jit(solution)/shard_map/ppermute | solution.py:434
  236.9 1.5 collective-permute-start.11
  238.4 0.2 collective-permute-start.12
  238.6 1.3 collective-permute-done.10.refs_3_.refs_15_
  239.9 4.8 %gram_step.5.after_ref.gram_ref = f32[256,256]{1,0:T(8,128)} custom-call(f32[256,256]{1,0:T(8,128)} %gram_step.4.after_ref.before_ref, bf16[16,16,1024]{2,1,0:T(8,128)(2,1)} %get-tuple-element.44.after_ref.refs_16_, bf16[32,16,1024]{2,1,0:T(8,128)(2,1)} %get-tuple-element.41.after_ref.refs_0_.refs_12_, bf16[32,16,1024]{2,1,0:T(8,128)(2,1)} %gate.14.refs_1_.refs_13_, ...), custom_call_target="tpu_custom_call" | custom-call | bytes 65536 | tf_op jit(solution)/shard_map/gram_step/pallas_call | solution.py:283
  244.7 6.7 %collective-permute-done.11.value_ref = bf16[16,16,1024]{2,1,0:T(8,128)(2,1)} collective-permute-done((bf16[16,16,1024]{2,1,0:T(8,128)(2,1)S(1)}, bf16[16,16,1024]{2,1,0:T(8,128)(2,1)}, u32[]{:S(2)}, u32[]{:S(2)}) %collective-permute-start.11) | collective-permute-done | bytes 524320 | tf_op jit(solution)/shard_map/ppermute | solution.py:434
  252.0 1.6 collective-permute-done.13.refs_19_
  253.6 11.3 %polar_step.1 = f32[16,128,1024]{2,1,0:T(8,128)} custom-call(f32[1]{0:T(128)S(6)} %copy.28.shrink_ref, f32[256,256]{1,0:T(8,128)} %gram_step.5.after_ref.gram_ref, f32[16,32,1024]{2,1,0:T(8,128)} %get-tuple-element.45.refs_0_, f32[16,48,1024]{2,1,0:T(8,128)} %get-tuple-element.46.refs_1_, f32[16,32,1024]{2,1,0:T(8,128)} %get-tuple-element.47.refs_2_, ...), custom_call_target="tpu_custom_call" | custom-call | bytes 65536 | tf_op jit(solution)/shard_map/polar_step/pallas_call | solution.py:401
  (23 shorter events, 0.0 us)
Async XLA Ops:
  2.6 16.7 %collective-permute-start = (bf16[16,12,1024]{2,1,0:T(8,128)(2,1)}, bf16[16,12,1024]{2,1,0:T(8,128)(2,1)S(1)}, u32[]{:S(2)}, u32[]{:S(2)}) collective-permute-start(bf16[16,12,1024]{2,1,0:T(8,128)(2,1)} %get-tuple-element.28), channel_id=1, source_target_pairs={{4,8},{12,16},{20,24},{8,4},{16,12},{24,20},{5,9},{13,17},{21,25},... | collective-permute-start | bytes 1179656 | tf_op jit(solution)/shard_map/ppermute | solution.py:427
  19.3 0.8 copy-start.1
  20.1 49.4 %all-to-all-start = ((bf16[8,2,16,32,128]{4,3,2,1,0:T(8,128)(2,1)}), bf16[8,2,16,32,128]{4,3,2,1,0:T(8,128)(2,1)}, u32[]{:S(2)}, u32[]{:S(2)}) async-start(bf16[8,2,16,32,128]{4,3,2,1,0:T(8,128)(2,1)} %gate.8), calls=%async_computation | async-start | bytes 4194304 | tf_op jit(solution)/shard_map/all_to_all | solution.py:487
  25.4 33.7 %collective-permute-start.1 = (bf16[16,12,1024]{2,1,0:T(8,128)(2,1)}, bf16[16,12,1024]{2,1,0:T(8,128)(2,1)S(1)}, u32[]{:S(2)}, u32[]{:S(2)}) collective-permute-start(bf16[16,12,1024]{2,1,0:T(8,128)(2,1)} %get-tuple-element.29), channel_id=1, source_target_pairs={{0,4},{8,12},{16,20},{24,28},{4,0},{12,8},{20,16},{28,24},{1,5},{9... | collective-permute-start | bytes 1179656 | tf_op jit(solution)/shard_map/ppermute | solution.py:427
  59.1 0.8 copy-start.3
  59.9 17.3 %copy-start.2 = (bf16[16,12,1024]{2,1,0:T(8,128)(2,1)S(1)}, bf16[16,12,1024]{2,1,0:T(8,128)(2,1)}, u32[]{:S(2)}) copy-start(bf16[16,12,1024]{2,1,0:T(8,128)(2,1)} %copy-done.1) | copy-start | bytes 1179652
  59.9 17.3 %copy-start.4 = (bf16[16,12,1024]{2,1,0:T(8,128)(2,1)S(1)}, bf16[16,12,1024]{2,1,0:T(8,128)(2,1)}, u32[]{:S(2)}) copy-start(bf16[16,12,1024]{2,1,0:T(8,128)(2,1)} %copy-done.3) | copy-start | bytes 1179652
  69.5 74.6 %all-to-all-start.2 = ((bf16[8,2,16,48,128]{4,3,2,1,0:T(8,128)(2,1)}), bf16[8,2,16,48,128]{4,3,2,1,0:T(8,128)(2,1)}, u32[]{:S(2)}, u32[]{:S(2)}) async-start(bf16[8,2,16,48,128]{4,3,2,1,0:T(8,128)(2,1)} %gate.12), calls=%async_computation.2 | async-start | bytes 6291456 | tf_op jit(solution)/shard_map/all_to_all | solution.py:487
  96.6 24.2 %collective-permute-start.2 = (bf16[32,16,1024]{2,1,0:T(8,128)(2,1)}, bf16[32,16,1024]{2,1,0:T(8,128)(2,1)}, u32[]{:S(2)}, u32[]{:S(2)}) collective-permute-start(bf16[32,16,1024]{2,1,0:T(8,128)(2,1)} %get-tuple-element.33.after_ref.refs_0_.refs_4_), channel_id=1, source_target_pairs={{0,2},{1,3},{2,0},{3,1},{4,6},{5,7},{6,4},{7,5},{8,10},{9,11},{10,... | collective-permute-start | bytes 3145736 | tf_op jit(solution)/shard_map/ppermute | solution.py:434
  98.1 22.7 %collective-permute-start.3 = (bf16[32,16,1024]{2,1,0:T(8,128)(2,1)}, bf16[32,16,1024]{2,1,0:T(8,128)(2,1)}, u32[]{:S(2)}, u32[]{:S(2)}) collective-permute-start(bf16[32,16,1024]{2,1,0:T(8,128)(2,1)} %get-tuple-element.33.after_ref.refs_0_.refs_4_), channel_id=1, source_target_pairs={{0,1},{1,0},{2,3},{3,2},{4,5},{5,4},{6,7},{7,6},{8,9},{9,8},{10,11... | collective-permute-start | bytes 3145736 | tf_op jit(solution)/shard_map/ppermute | solution.py:434
  120.8 3.0 %collective-permute-start.4 = (bf16[32,16,1024]{2,1,0:T(8,128)(2,1)}, bf16[32,16,1024]{2,1,0:T(8,128)(2,1)}, u32[]{:S(2)}, u32[]{:S(2)}) collective-permute-start(bf16[32,16,1024]{2,1,0:T(8,128)(2,1)} %gate.10.refs_1_.refs_5_), channel_id=1, source_target_pairs={{0,1},{1,0},{2,3},{3,2},{4,5},{5,4},{6,7},{7,6},{8,9},{9,8},{10,11... | collective-permute-start | bytes 3145736 | tf_op jit(solution)/shard_map/ppermute | solution.py:434
  144.2 52.2 %all-to-all-start.1 = ((bf16[8,2,16,32,128]{4,3,2,1,0:T(8,128)(2,1)}), bf16[8,2,16,32,128]{4,3,2,1,0:T(8,128)(2,1)}, u32[]{:S(2)}, u32[]{:S(2)}) async-start(bf16[8,2,16,32,128]{4,3,2,1,0:T(8,128)(2,1)} %gate.11), calls=%async_computation.1 | async-start | bytes 4194304 | tf_op jit(solution)/shard_map/all_to_all | solution.py:487
  160.9 42.9 %collective-permute-start.5 = (bf16[48,16,1024]{2,1,0:T(8,128)(2,1)}, bf16[48,16,1024]{2,1,0:T(8,128)(2,1)}, u32[]{:S(2)}, u32[]{:S(2)}) collective-permute-start(bf16[48,16,1024]{2,1,0:T(8,128)(2,1)} %get-tuple-element.39.after_ref.refs_0_.refs_8_), channel_id=1, source_target_pairs={{0,2},{1,3},{2,0},{3,1},{4,6},{5,7},{6,4},{7,5},{8,10},{9,11},{10,... | collective-permute-start | bytes 4718600 | tf_op jit(solution)/shard_map/ppermute | solution.py:434
  196.3 29.6 %all-to-all-start.3 = ((bf16[8,2,16,16,128]{4,3,2,1,0:T(8,128)(2,1)}), bf16[8,2,16,16,128]{4,3,2,1,0:T(8,128)(2,1)}, u32[]{:S(2)}, u32[]{:S(2)}) async-start(bf16[8,2,16,16,128]{4,3,2,1,0:T(8,128)(2,1)} %get-tuple-element.42), calls=%async_computation.3 | async-start | bytes 2097152 | tf_op jit(solution)/shard_map/all_to_all | solution.py:487
  203.8 9.1 %collective-permute-start.6 = (bf16[48,16,1024]{2,1,0:T(8,128)(2,1)}, bf16[48,16,1024]{2,1,0:T(8,128)(2,1)}, u32[]{:S(2)}, u32[]{:S(2)}) collective-permute-start(bf16[48,16,1024]{2,1,0:T(8,128)(2,1)} %get-tuple-element.39.after_ref.refs_0_.refs_8_), channel_id=1, source_target_pairs={{0,1},{1,0},{2,3},{3,2},{4,5},{5,4},{6,7},{7,6},{8,9},{9,8},{10,11... | collective-permute-start | bytes 4718600 | tf_op jit(solution)/shard_map/ppermute | solution.py:434
  203.9 9.1 %collective-permute-start.7 = (bf16[48,16,1024]{2,1,0:T(8,128)(2,1)}, bf16[48,16,1024]{2,1,0:T(8,128)(2,1)}, u32[]{:S(2)}, u32[]{:S(2)}) collective-permute-start(bf16[48,16,1024]{2,1,0:T(8,128)(2,1)} %gate.13.refs_1_.refs_9_), channel_id=1, source_target_pairs={{0,1},{1,0},{2,3},{3,2},{4,5},{5,4},{6,7},{7,6},{8,9},{9,8},{10,11... | collective-permute-start | bytes 4718600 | tf_op jit(solution)/shard_map/ppermute | solution.py:434
  211.4 25.5 %collective-permute-start.8 = (bf16[32,16,1024]{2,1,0:T(8,128)(2,1)}, bf16[32,16,1024]{2,1,0:T(8,128)(2,1)}, u32[]{:S(2)}, u32[]{:S(2)}) collective-permute-start(bf16[32,16,1024]{2,1,0:T(8,128)(2,1)} %get-tuple-element.41.after_ref.refs_0_.refs_12_), channel_id=1, source_target_pairs={{0,2},{1,3},{2,0},{3,1},{4,6},{5,7},{6,4},{7,5},{8,10},{9,11},{10,... | collective-permute-start | bytes 3145736 | tf_op jit(solution)/shard_map/ppermute | solution.py:434
  212.9 25.7 %collective-permute-start.9 = (bf16[32,16,1024]{2,1,0:T(8,128)(2,1)}, bf16[32,16,1024]{2,1,0:T(8,128)(2,1)}, u32[]{:S(2)}, u32[]{:S(2)}) collective-permute-start(bf16[32,16,1024]{2,1,0:T(8,128)(2,1)} %get-tuple-element.41.after_ref.refs_0_.refs_12_), channel_id=1, source_target_pairs={{0,1},{1,0},{2,3},{3,2},{4,5},{5,4},{6,7},{7,6},{8,9},{9,8},{10,11... | collective-permute-start | bytes 3145736 | tf_op jit(solution)/shard_map/ppermute | solution.py:434
  230.9 6.0 %copy-start = (bf16[16,16,1024]{2,1,0:T(8,128)(2,1)S(1)}, bf16[16,16,1024]{2,1,0:T(8,128)(2,1)}, u32[]{:S(2)}) copy-start(bf16[16,16,1024]{2,1,0:T(8,128)(2,1)} %get-tuple-element.44.after_ref.refs_16_) | copy-start | bytes 1572868
  236.9 3.0 %collective-permute-start.10 = (bf16[32,16,1024]{2,1,0:T(8,128)(2,1)}, bf16[32,16,1024]{2,1,0:T(8,128)(2,1)}, u32[]{:S(2)}, u32[]{:S(2)}) collective-permute-start(bf16[32,16,1024]{2,1,0:T(8,128)(2,1)} %gate.14.refs_1_.refs_13_), channel_id=1, source_target_pairs={{0,1},{1,0},{2,3},{3,2},{4,5},{5,4},{6,7},{7,6},{8,9},{9,8},{10,11... | collective-permute-start | bytes 3145736 | tf_op jit(solution)/shard_map/ppermute | solution.py:434
  236.9 14.4 %collective-permute-start.11 = (bf16[16,16,1024]{2,1,0:T(8,128)(2,1)S(1)}, bf16[16,16,1024]{2,1,0:T(8,128)(2,1)}, u32[]{:S(2)}, u32[]{:S(2)}) collective-permute-start(bf16[16,16,1024]{2,1,0:T(8,128)(2,1)S(1)} %copy-done), channel_id=1, source_target_pairs={{0,2},{1,3},{2,0},{3,1},{4,6},{5,7},{6,4},{7,5},{8,10},{9,11},{10,... | collective-permute-start | bytes 1572872 | tf_op jit(solution)/shard_map/ppermute | solution.py:434
  238.4 13.6 %collective-permute-start.12 = (bf16[16,16,1024]{2,1,0:T(8,128)(2,1)S(1)}, bf16[16,16,1024]{2,1,0:T(8,128)(2,1)}, u32[]{:S(2)}, u32[]{:S(2)}) collective-permute-start(bf16[16,16,1024]{2,1,0:T(8,128)(2,1)S(1)} %copy-done), channel_id=1, source_target_pairs={{0,1},{1,0},{2,3},{3,2},{4,5},{5,4},{6,7},{7,6},{8,9},{9,8},{10,11... | collective-permute-start | bytes 1572872 | tf_op jit(solution)/shard_map/ppermute | solution.py:434
  251.3 2.3 collective-permute-start.13

commit v21 on v20

--- a/solution.py
+++ b/solution.py
@@ -57,8 +57,8 @@
 
 
 def chunk_rows(own_rows):
-    quarter = own_rows // 4
-    sizes = [quarter, own_rows - 2 * quarter - EDGE_ROWS, quarter, EDGE_ROWS]
+    large = own_rows // 2 - EDGE_ROWS
+    sizes = [large, large, EDGE_ROWS, EDGE_ROWS]
     sizes = [size for size in sizes if size > 0]
     return [sum(sizes[:place]) for place in range(len(sizes))], sizes
 

time: 268 us -> 271 us (1.011)
    all_to_all x4, waiting for transfers between devices: 58.4 us -> 27.5 us  [first(): lax.all_to_all(sent, 'strip', split_axis=0, concat_axis=0, tiled=True)]
    ppermute x12, waiting for transfers between devices: 32.7 us -> 58.5 us  [swap(): return lax.ppermute(value, axis, [(i, i ^ bits) for i in range(count)])]
    ppermute x2, waiting for transfers between devices: 27.6 us -> 35.4 us  [exchanged(): lax.ppermute(rows.astype(BF16), 'strip', pairs + [(j, i) for i, j in pairs])]
  transfers between devices with their start and end apart: 18 -> 18, of which waited for: 12 -> 11; matrix products, arithmetic and copies ran while one was open for 1% -> 1% of each run, Pallas kernels for 34% -> 33%
where the time goes in v21:
time: 271 us; the launch traced here: 269 us
  waiting for transfers between devices  121 us (45%)
  Pallas kernels  100 us (37%)
  starting transfers between devices  37.8 us (14%)
  local copies, waits for them, and re-layouts  4.76 us (2%)
  other arithmetic  3.84 us (1%)
    ppermute x12, waiting for transfers between devices, swap(): return lax.ppermute(value, axis, [(i, i ^ bits) for i in range(count)])  58.5 us
    ppermute x2, waiting for transfers between devices, exchanged(): lax.ppermute(rows.astype(BF16), 'strip', pairs + [(j, i) for i, j in pairs])  35.4 us
    pallas_call x4, Pallas kernels, first_transform(): pl.pallas_call(first_body, grid=(chans // block,), in_specs=[pl.BlockSpec...  33.7 us
    pallas_call x4, Pallas kernels, second_transform(): pl.pallas_call(second_body, grid=(side_len // block,), in_specs=[SMEM, pl...  28 us
    all_to_all x4, waiting for transfers between devices, first(): lax.all_to_all(sent, 'strip', split_axis=0, concat_axis=0, tiled=True)  27.5 us
    all_to_all x4, starting transfers between devices, first(): lax.all_to_all(sent, 'strip', split_axis=0, concat_axis=0, tiled=True)  27.3 us
    pallas_call x3, Pallas kernels, gram_step(): pl.pallas_call(functools.partial(gram_body, len(pieces)), grid=(rows // b...  16.1 us
    pallas_call x1, Pallas kernels, polar_step(): pl.pallas_call(functools.partial(polar_body, starts, sizes, groups), in_s...  11.3 us
  transfers between devices with their start and end apart: 18, of which 11 were waited for; matrix products, arithmetic and copies ran while one was open for 1% of the time, Pallas kernels for 33%

profile of v21, /device:TPU:12, one launch (start us, length us, event | category | flops | bytes accessed | tf_op | source)
XLA Modules:
  0.0 268.8 jit_solution(4818770798551972788)
XLA Ops:
  0.0 2.6 slice_select_fusion
  2.6 3.4 %collective-permute-start = (bf16[16,12,1024]{2,1,0:T(8,128)(2,1)}, bf16[16,12,1024]{2,1,0:T(8,128)(2,1)S(1)}, u32[]{:S(2)}, u32[]{:S(2)}) collective-permute-start(bf16[16,12,1024]{2,1,0:T(8,128)(2,1)} %get-tuple-element.28), channel_id=1, source_target_pairs={{4,8},{12,16},{20,24},{8,4},{16,12},{24,20},{5,9},{13,17},{21,25},... | collective-permute-start | bytes 1179656 | tf_op jit(solution)/shard_map/ppermute | solution.py:427
  6.1 10.3 %first_transform.4 = (bf16[8,2,16,48,128]{4,3,2,1,0:T(8,128)(2,1)}, f32[8,128]{1,0:T(8,128)}) custom-call(bf16[768,1024]{1,0:T(8,128)(2,1)} %constant.36.clone.table_ref, bf16[2,16,128,1024]{3,2,1,0:T(8,128)(2,1)} %grid_ref.7, s32[1]{0:T(128)} %bitcast.after_ref.strip_ref), custom_call_target="tpu_custom_call" | custom-call | bytes 65536 | tf_op jit(solution)/shard_map/first_transform/pallas_call | solution.py:112
  16.4 2.9 %collective-permute-done.after_ref = bf16[16,12,1024]{2,1,0:T(8,128)(2,1)S(1)} collective-permute-done((bf16[16,12,1024]{2,1,0:T(8,128)(2,1)}, bf16[16,12,1024]{2,1,0:T(8,128)(2,1)S(1)}, u32[]{:S(2)}, u32[]{:S(2)}) %collective-permute-start) | collective-permute-done | bytes 393248 | tf_op jit(solution)/shard_map/ppermute | solution.py:427
  19.3 0.8 copy-done.1
  20.1 5.3 %all-to-all-start = ((bf16[8,2,16,48,128]{4,3,2,1,0:T(8,128)(2,1)}), bf16[8,2,16,48,128]{4,3,2,1,0:T(8,128)(2,1)}, u32[]{:S(2)}, u32[]{:S(2)}) async-start(bf16[8,2,16,48,128]{4,3,2,1,0:T(8,128)(2,1)} %gate.8), calls=%async_computation | async-start | bytes 6291456 | tf_op jit(solution)/shard_map/all_to_all | solution.py:487
  25.4 0.6 collective-permute-start.1
  25.9 10.3 %first_transform.5 = (bf16[8,2,16,48,128]{4,3,2,1,0:T(8,128)(2,1)}, f32[8,128]{1,0:T(8,128)}) custom-call(bf16[768,1024]{1,0:T(8,128)(2,1)} %constant.37.clone.table_ref, bf16[2,16,128,1024]{3,2,1,0:T(8,128)(2,1)} %grid_ref.7, f32[8,128]{1,0:T(8,128)} %gate.9.after_ref), custom_call_target="tpu_custom_call" | custom-call | bytes 65536 | tf_op jit(solution)/shard_map/first_transform/pallas_call | solution.py:112
  36.3 32.5 %collective-permute-done.1.after_ref = bf16[16,12,1024]{2,1,0:T(8,128)(2,1)S(1)} collective-permute-done((bf16[16,12,1024]{2,1,0:T(8,128)(2,1)}, bf16[16,12,1024]{2,1,0:T(8,128)(2,1)S(1)}, u32[]{:S(2)}, u32[]{:S(2)}) %collective-permute-start.1) | collective-permute-done | bytes 393248 | tf_op jit(solution)/shard_map/ppermute | solution.py:427
  68.8 0.8 copy-done.4
  69.6 22.4 %all-to-all-done.half_ref = bf16[8,2,16,48,128]{4,3,2,1,0:T(8,128)(2,1)} async-done(((bf16[8,2,16,48,128]{4,3,2,1,0:T(8,128)(2,1)}), bf16[8,2,16,48,128]{4,3,2,1,0:T(8,128)(2,1)}, u32[]{:S(2)}, u32[]{:S(2)}) %all-to-all-start) | async-done | bytes 3145760 | tf_op jit(solution)/shard_map/all_to_all | solution.py:487
  92.0 7.7 %all-to-all-start.2 = ((bf16[8,2,16,48,128]{4,3,2,1,0:T(8,128)(2,1)}), bf16[8,2,16,48,128]{4,3,2,1,0:T(8,128)(2,1)}, u32[]{:S(2)}, u32[]{:S(2)}) async-start(bf16[8,2,16,48,128]{4,3,2,1,0:T(8,128)(2,1)} %gate.12), calls=%async_computation.2 | async-start | bytes 6291456 | tf_op jit(solution)/shard_map/all_to_all | solution.py:487
  99.7 0.1 broadcast_select_fusion.1
  99.7 1.1 pad_maximum_fusion.edge_ref
  100.9 11.2 %base_step.1 = (f32[16,48,1024]{2,1,0:T(8,128)}, f32[16,48,1024]{2,1,0:T(8,128)}, f32[16,16,1024]{2,1,0:T(8,128)}, f32[16,16,1024]{2,1,0:T(8,128)}) custom-call(s32[1]{0:T(128)} %bitcast.after_ref.strip_ref, f32[16]{0:T(128)} %step_ref.9, f32[3,4]{1,0:T(4,128)} %highpass_ref.1, f32[16,128,1024]{2,1,0:T(8,128)} %model_ref.1, ...), custom_call_target="tpu_custom_call" | custom-call | bytes 65536 | tf_op jit(solution)/shard_map/base_step/pallas_call | solution.py:193
  112.0 9.0 %second_transform.4 = (f32[16,48,1024]{2,1,0:T(8,128)}, bf16[48,16,1024]{2,1,0:T(8,128)(2,1)}) custom-call(f32[16]{0:T(128)} %step_ref.9, bf16[8,2,16,48,128]{4,3,2,1,0:T(8,128)(2,1)} %all-to-all-done.half_ref, bf16[1024,1024]{1,0:T(8,128)(2,1)} %constant.38.clone.cosine_ref, bf16[1024,1024]{1,0:T(8,128)(2,1)} %constant.39.clone.sine_ref, ...), custom_call_target="tpu_custom_call" | custom-call | bytes 65536 | tf_op jit(solution)/shard_map/second_transform/pallas_call | solution.py:236
  121.1 1.5 collective-permute-start.2
  122.6 6.5 %first_transform.6 = (bf16[8,2,16,16,128]{4,3,2,1,0:T(8,128)(2,1)}, f32[8,128]{1,0:T(8,128)}) custom-call(bf16[256,1024]{1,0:T(8,128)(2,1)} %constant.40.clone.table_ref, bf16[2,16,128,1024]{3,2,1,0:T(8,128)(2,1)} %grid_ref.7, bf16[48,16,1024]{2,1,0:T(8,128)(2,1)} %get-tuple-element.33.after_ref.refs_0_.refs_4_), custom_call_target="tpu_custom_call" | custom-call | bytes 65536 | tf_op jit(solution)/shard_map/first_transform/pallas_call | solution.py:112
  129.1 27.4 %collective-permute-done.2.value_ref = bf16[48,16,1024]{2,1,0:T(8,128)(2,1)} collective-permute-done((bf16[48,16,1024]{2,1,0:T(8,128)(2,1)}, bf16[48,16,1024]{2,1,0:T(8,128)(2,1)}, u32[]{:S(2)}, u32[]{:S(2)}) %collective-permute-start.2) | collective-permute-done | bytes 1572896 | tf_op jit(solution)/shard_map/ppermute | solution.py:434
  156.5 3.7 %collective-permute-done.4.refs_3_.refs_7_ = bf16[48,16,1024]{2,1,0:T(8,128)(2,1)} collective-permute-done((bf16[48,16,1024]{2,1,0:T(8,128)(2,1)}, bf16[48,16,1024]{2,1,0:T(8,128)(2,1)}, u32[]{:S(2)}, u32[]{:S(2)}) %collective-permute-start.4) | collective-permute-done | bytes 1572896 | tf_op jit(solution)/shard_map/ppermute | solution.py:434
  160.2 0.7 broadcast_in_dim.3.before_ref
  161.0 6.5 %gram_step.3.after_ref.before_ref = f32[256,256]{1,0:T(8,128)} custom-call(f32[256,256]{1,0:T(8,128)} %broadcast_in_dim.3.before_ref, f32[8,128]{1,0:T(8,128)} %get-tuple-element.34.after_ref, bf16[48,16,1024]{2,1,0:T(8,128)(2,1)} %get-tuple-element.33.after_ref.refs_0_.refs_4_, bf16[48,16,1024]{2,1,0:T(8,128)(2,1)} %gate.10.refs_1_.refs_5_, ...), custom_call_target="tpu_custom_call" | custom-call | bytes 65536 | tf_op jit(solution)/shard_map/gram_step/pallas_call | solution.py:283
  167.5 6.7 %all-to-all-start.1 = ((bf16[8,2,16,16,128]{4,3,2,1,0:T(8,128)(2,1)}), bf16[8,2,16,16,128]{4,3,2,1,0:T(8,128)(2,1)}, u32[]{:S(2)}, u32[]{:S(2)}) async-start(bf16[8,2,16,16,128]{4,3,2,1,0:T(8,128)(2,1)} %gate.11), calls=%async_computation.1 | async-start | bytes 2097152 | tf_op jit(solution)/shard_map/all_to_all | solution.py:487
  174.1 9.0 %second_transform.5 = (f32[16,48,1024]{2,1,0:T(8,128)}, bf16[48,16,1024]{2,1,0:T(8,128)(2,1)}) custom-call(f32[16]{0:T(128)} %step_ref.9, bf16[8,2,16,48,128]{4,3,2,1,0:T(8,128)(2,1)} %all-to-all-done.2.half_ref, bf16[1024,1024]{1,0:T(8,128)(2,1)} %constant.38.clone.cosine_ref, bf16[1024,1024]{1,0:T(8,128)(2,1)} %constant.39.clone.sine_ref, ...), custom_call_target="tpu_custom_call" | custom-call | bytes 65536 | tf_op jit(solution)/shard_map/second_transform/pallas_call | solution.py:236
  183.2 1.5 collective-permute-start.5
  184.7 6.5 %first_transform.7 = (bf16[8,2,16,16,128]{4,3,2,1,0:T(8,128)(2,1)}, f32[8,128]{1,0:T(8,128)}) custom-call(bf16[256,1024]{1,0:T(8,128)(2,1)} %constant.41.clone.table_ref, bf16[2,16,128,1024]{3,2,1,0:T(8,128)(2,1)} %grid_ref.7, bf16[48,16,1024]{2,1,0:T(8,128)(2,1)} %get-tuple-element.39.after_ref.refs_0_.refs_8_), custom_call_target="tpu_custom_call" | custom-call | bytes 65536 | tf_op jit(solution)/shard_map/first_transform/pallas_call | solution.py:112
  191.2 5.1 %all-to-all-done.1.half_ref = bf16[8,2,16,16,128]{4,3,2,1,0:T(8,128)(2,1)} async-done(((bf16[8,2,16,16,128]{4,3,2,1,0:T(8,128)(2,1)}), bf16[8,2,16,16,128]{4,3,2,1,0:T(8,128)(2,1)}, u32[]{:S(2)}, u32[]{:S(2)}) %all-to-all-start.1) | async-done | bytes 1048608 | tf_op jit(solution)/shard_map/all_to_all | solution.py:487
  196.3 7.7 %all-to-all-start.3 = ((bf16[8,2,16,16,128]{4,3,2,1,0:T(8,128)(2,1)}), bf16[8,2,16,16,128]{4,3,2,1,0:T(8,128)(2,1)}, u32[]{:S(2)}, u32[]{:S(2)}) async-start(bf16[8,2,16,16,128]{4,3,2,1,0:T(8,128)(2,1)} %get-tuple-element.42), calls=%async_computation.3 | async-start | bytes 2097152 | tf_op jit(solution)/shard_map/all_to_all | solution.py:487
  204.0 0.0 collective-permute-start.6
  204.0 14.7 %collective-permute-done.5.value_ref = bf16[48,16,1024]{2,1,0:T(8,128)(2,1)} collective-permute-done((bf16[48,16,1024]{2,1,0:T(8,128)(2,1)}, bf16[48,16,1024]{2,1,0:T(8,128)(2,1)}, u32[]{:S(2)}, u32[]{:S(2)}) %collective-permute-start.5) | collective-permute-done | bytes 1572896 | tf_op jit(solution)/shard_map/ppermute | solution.py:434
  218.7 0.0 collective-permute-start.7
  218.7 5.0 %second_transform.6 = (f32[16,16,1024]{2,1,0:T(8,128)}, bf16[16,16,1024]{2,1,0:T(8,128)(2,1)}) custom-call(f32[16]{0:T(128)} %step_ref.9, bf16[8,2,16,16,128]{4,3,2,1,0:T(8,128)(2,1)} %all-to-all-done.1.half_ref, bf16[1024,1024]{1,0:T(8,128)(2,1)} %constant.38.clone.cosine_ref, bf16[1024,1024]{1,0:T(8,128)(2,1)} %constant.39.clone.sine_ref, ...), custom_call_target="tpu_custom_call" | custom-call | bytes 65536 | tf_op jit(solution)/shard_map/second_transform/pallas_call | solution.py:236
  223.7 1.5 collective-permute-start.8
  225.2 0.2 collective-permute-start.9
  225.4 0.0 collective-permute-done.6.refs_2_.refs_10_
  225.4 6.5 %gram_step.4.after_ref.before_ref = f32[256,256]{1,0:T(8,128)} custom-call(f32[256,256]{1,0:T(8,128)} %gram_step.3.after_ref.before_ref, bf16[16,16,1024]{2,1,0:T(8,128)(2,1)} %get-tuple-element.41.after_ref.refs_0_.refs_12_, bf16[48,16,1024]{2,1,0:T(8,128)(2,1)} %get-tuple-element.39.after_ref.refs_0_.refs_8_, bf16[48,16,1024]{2,1,0:T(8,128)(2,1)} %gate.13.refs_1_.refs_9_, ...), custom_call_target="tpu_custom_call" | custom-call | bytes 65536 | tf_op jit(solution)/shard_map/gram_step/pallas_call | solution.py:283
  232.0 4.9 %second_transform.7 = (f32[16,16,1024]{2,1,0:T(8,128)}, bf16[16,16,1024]{2,1,0:T(8,128)(2,1)}) custom-call(f32[16]{0:T(128)} %step_ref.9, bf16[8,2,16,16,128]{4,3,2,1,0:T(8,128)(2,1)} %all-to-all-done.3.half_ref, bf16[1024,1024]{1,0:T(8,128)(2,1)} %constant.38.clone.cosine_ref, bf16[1024,1024]{1,0:T(8,128)(2,1)} %constant.39.clone.sine_ref, ...), custom_call_target="tpu_custom_call" | custom-call | bytes 65536 | tf_op jit(solution)/shard_map/second_transform/pallas_call | solution.py:236
  236.9 1.4 collective-permute-done.8.value_ref
  238.2 0.8 copy-done
  239.1 1.5 collective-permute-start.11
  240.6 0.2 collective-permute-start.12
  240.8 0.5 collective-permute-done.10.refs_3_.refs_15_
  241.3 3.1 %gram_step.5.after_ref.gram_ref = f32[256,256]{1,0:T(8,128)} custom-call(f32[256,256]{1,0:T(8,128)} %gram_step.4.after_ref.before_ref, bf16[16,16,1024]{2,1,0:T(8,128)(2,1)} %get-tuple-element.44.after_ref.refs_16_, bf16[16,16,1024]{2,1,0:T(8,128)(2,1)} %get-tuple-element.41.after_ref.refs_0_.refs_12_, bf16[16,16,1024]{2,1,0:T(8,128)(2,1)} %gate.14.refs_1_.refs_13_, ...), custom_call_target="tpu_custom_call" | custom-call | bytes 65536 | tf_op jit(solution)/shard_map/gram_step/pallas_call | solution.py:283
  244.4 9.2 %collective-permute-done.11.value_ref = bf16[16,16,1024]{2,1,0:T(8,128)(2,1)S(1)} collective-permute-done((bf16[16,16,1024]{2,1,0:T(8,128)(2,1)}, bf16[16,16,1024]{2,1,0:T(8,128)(2,1)S(1)}, u32[]{:S(2)}, u32[]{:S(2)}) %collective-permute-start.11) | collective-permute-done | bytes 524320 | tf_op jit(solution)/shard_map/ppermute | solution.py:434
  253.6 0.8 copy-done.3
  255.1 1.5 collective-permute-done.13.refs_19_
  256.6 0.8 copy-done.6
  257.4 11.3 %polar_step.1 = f32[16,128,1024]{2,1,0:T(8,128)} custom-call(f32[1]{0:T(128)S(6)} %copy.28.shrink_ref, f32[256,256]{1,0:T(8,128)} %gram_step.5.after_ref.gram_ref, f32[16,48,1024]{2,1,0:T(8,128)} %get-tuple-element.45.refs_0_, f32[16,48,1024]{2,1,0:T(8,128)} %get-tuple-element.46.refs_1_, f32[16,16,1024]{2,1,0:T(8,128)} %get-tuple-element.47.refs_2_, ...), custom_call_target="tpu_custom_call" | custom-call | bytes 65536 | tf_op jit(solution)/shard_map/polar_step/pallas_call | solution.py:401
  (27 shorter events, 0.0 us)
Async XLA Ops:
  2.6 16.7 %collective-permute-start = (bf16[16,12,1024]{2,1,0:T(8,128)(2,1)}, bf16[16,12,1024]{2,1,0:T(8,128)(2,1)S(1)}, u32[]{:S(2)}, u32[]{:S(2)}) collective-permute-start(bf16[16,12,1024]{2,1,0:T(8,128)(2,1)} %get-tuple-element.28), channel_id=1, source_target_pairs={{4,8},{12,16},{20,24},{8,4},{16,12},{24,20},{5,9},{13,17},{21,25},... | collective-permute-start | bytes 1179656 | tf_op jit(solution)/shard_map/ppermute | solution.py:427
  19.3 0.8 copy-start.1
  20.1 71.9 %all-to-all-start = ((bf16[8,2,16,48,128]{4,3,2,1,0:T(8,128)(2,1)}), bf16[8,2,16,48,128]{4,3,2,1,0:T(8,128)(2,1)}, u32[]{:S(2)}, u32[]{:S(2)}) async-start(bf16[8,2,16,48,128]{4,3,2,1,0:T(8,128)(2,1)} %gate.8), calls=%async_computation | async-start | bytes 6291456 | tf_op jit(solution)/shard_map/all_to_all | solution.py:487
  25.4 43.4 %collective-permute-start.1 = (bf16[16,12,1024]{2,1,0:T(8,128)(2,1)}, bf16[16,12,1024]{2,1,0:T(8,128)(2,1)S(1)}, u32[]{:S(2)}, u32[]{:S(2)}) collective-permute-start(bf16[16,12,1024]{2,1,0:T(8,128)(2,1)} %get-tuple-element.29), channel_id=1, source_target_pairs={{0,4},{8,12},{16,20},{24,28},{4,0},{12,8},{20,16},{28,24},{1,5},{9... | collective-permute-start | bytes 1179656 | tf_op jit(solution)/shard_map/ppermute | solution.py:427
  68.8 0.8 copy-start.4
  69.6 30.0 %copy-start.2 = (bf16[16,12,1024]{2,1,0:T(8,128)(2,1)S(1)}, bf16[16,12,1024]{2,1,0:T(8,128)(2,1)}, u32[]{:S(2)}) copy-start(bf16[16,12,1024]{2,1,0:T(8,128)(2,1)} %copy-done.1) | copy-start | bytes 1179652
  69.6 30.0 %copy-start.5 = (bf16[16,12,1024]{2,1,0:T(8,128)(2,1)S(1)}, bf16[16,12,1024]{2,1,0:T(8,128)(2,1)}, u32[]{:S(2)}) copy-start(bf16[16,12,1024]{2,1,0:T(8,128)(2,1)} %copy-done.4) | copy-start | bytes 1179652
  92.0 75.5 %all-to-all-start.2 = ((bf16[8,2,16,48,128]{4,3,2,1,0:T(8,128)(2,1)}), bf16[8,2,16,48,128]{4,3,2,1,0:T(8,128)(2,1)}, u32[]{:S(2)}, u32[]{:S(2)}) async-start(bf16[8,2,16,48,128]{4,3,2,1,0:T(8,128)(2,1)} %gate.12), calls=%async_computation.2 | async-start | bytes 6291456 | tf_op jit(solution)/shard_map/all_to_all | solution.py:487
  121.1 35.4 %collective-permute-start.2 = (bf16[48,16,1024]{2,1,0:T(8,128)(2,1)}, bf16[48,16,1024]{2,1,0:T(8,128)(2,1)}, u32[]{:S(2)}, u32[]{:S(2)}) collective-permute-start(bf16[48,16,1024]{2,1,0:T(8,128)(2,1)} %get-tuple-element.33.after_ref.refs_0_.refs_4_), channel_id=1, source_target_pairs={{0,2},{1,3},{2,0},{3,1},{4,6},{5,7},{6,4},{7,5},{8,10},{9,11},{10,... | collective-permute-start | bytes 4718600 | tf_op jit(solution)/shard_map/ppermute | solution.py:434
  122.6 33.9 %collective-permute-start.3 = (bf16[48,16,1024]{2,1,0:T(8,128)(2,1)}, bf16[48,16,1024]{2,1,0:T(8,128)(2,1)}, u32[]{:S(2)}, u32[]{:S(2)}) collective-permute-start(bf16[48,16,1024]{2,1,0:T(8,128)(2,1)} %get-tuple-element.33.after_ref.refs_0_.refs_4_), channel_id=1, source_target_pairs={{0,1},{1,0},{2,3},{3,2},{4,5},{5,4},{6,7},{7,6},{8,9},{9,8},{10,11... | collective-permute-start | bytes 4718600 | tf_op jit(solution)/shard_map/ppermute | solution.py:434
  156.5 3.8 %collective-permute-start.4 = (bf16[48,16,1024]{2,1,0:T(8,128)(2,1)}, bf16[48,16,1024]{2,1,0:T(8,128)(2,1)}, u32[]{:S(2)}, u32[]{:S(2)}) collective-permute-start(bf16[48,16,1024]{2,1,0:T(8,128)(2,1)} %gate.10.refs_1_.refs_5_), channel_id=1, source_target_pairs={{0,1},{1,0},{2,3},{3,2},{4,5},{5,4},{6,7},{7,6},{8,9},{9,8},{10,11... | collective-permute-start | bytes 4718600 | tf_op jit(solution)/shard_map/ppermute | solution.py:434
  167.5 28.8 %all-to-all-start.1 = ((bf16[8,2,16,16,128]{4,3,2,1,0:T(8,128)(2,1)}), bf16[8,2,16,16,128]{4,3,2,1,0:T(8,128)(2,1)}, u32[]{:S(2)}, u32[]{:S(2)}) async-start(bf16[8,2,16,16,128]{4,3,2,1,0:T(8,128)(2,1)} %gate.11), calls=%async_computation.1 | async-start | bytes 2097152 | tf_op jit(solution)/shard_map/all_to_all | solution.py:487
  183.2 35.6 %collective-permute-start.5 = (bf16[48,16,1024]{2,1,0:T(8,128)(2,1)}, bf16[48,16,1024]{2,1,0:T(8,128)(2,1)}, u32[]{:S(2)}, u32[]{:S(2)}) collective-permute-start(bf16[48,16,1024]{2,1,0:T(8,128)(2,1)} %get-tuple-element.39.after_ref.refs_0_.refs_8_), channel_id=1, source_target_pairs={{0,2},{1,3},{2,0},{3,1},{4,6},{5,7},{6,4},{7,5},{8,10},{9,11},{10,... | collective-permute-start | bytes 4718600 | tf_op jit(solution)/shard_map/ppermute | solution.py:434
  196.3 35.7 %all-to-all-start.3 = ((bf16[8,2,16,16,128]{4,3,2,1,0:T(8,128)(2,1)}), bf16[8,2,16,16,128]{4,3,2,1,0:T(8,128)(2,1)}, u32[]{:S(2)}, u32[]{:S(2)}) async-start(bf16[8,2,16,16,128]{4,3,2,1,0:T(8,128)(2,1)} %get-tuple-element.42), calls=%async_computation.3 | async-start | bytes 2097152 | tf_op jit(solution)/shard_map/all_to_all | solution.py:487
  204.0 21.4 %collective-permute-start.6 = (bf16[48,16,1024]{2,1,0:T(8,128)(2,1)}, bf16[48,16,1024]{2,1,0:T(8,128)(2,1)}, u32[]{:S(2)}, u32[]{:S(2)}) collective-permute-start(bf16[48,16,1024]{2,1,0:T(8,128)(2,1)} %get-tuple-element.39.after_ref.refs_0_.refs_8_), channel_id=1, source_target_pairs={{0,1},{1,0},{2,3},{3,2},{4,5},{5,4},{6,7},{7,6},{8,9},{9,8},{10,11... | collective-permute-start | bytes 4718600 | tf_op jit(solution)/shard_map/ppermute | solution.py:434
  218.7 6.7 %collective-permute-start.7 = (bf16[48,16,1024]{2,1,0:T(8,128)(2,1)}, bf16[48,16,1024]{2,1,0:T(8,128)(2,1)}, u32[]{:S(2)}, u32[]{:S(2)}) collective-permute-start(bf16[48,16,1024]{2,1,0:T(8,128)(2,1)} %gate.13.refs_1_.refs_9_), channel_id=1, source_target_pairs={{0,1},{1,0},{2,3},{3,2},{4,5},{5,4},{6,7},{7,6},{8,9},{9,8},{10,11... | collective-permute-start | bytes 4718600 | tf_op jit(solution)/shard_map/ppermute | solution.py:434
  223.7 14.5 %collective-permute-start.8 = (bf16[16,16,1024]{2,1,0:T(8,128)(2,1)}, bf16[16,16,1024]{2,1,0:T(8,128)(2,1)S(1)}, u32[]{:S(2)}, u32[]{:S(2)}) collective-permute-start(bf16[16,16,1024]{2,1,0:T(8,128)(2,1)} %get-tuple-element.41.after_ref.refs_0_.refs_12_), channel_id=1, source_target_pairs={{0,2},{1,3},{2,0},{3,1},{4,6},{5,7},{6,4},{7,5},{8,10},{9,11},{10,... | collective-permute-start | bytes 1572872 | tf_op jit(solution)/shard_map/ppermute | solution.py:434
  225.2 15.6 %collective-permute-start.9 = (bf16[16,16,1024]{2,1,0:T(8,128)(2,1)}, bf16[16,16,1024]{2,1,0:T(8,128)(2,1)}, u32[]{:S(2)}, u32[]{:S(2)}) collective-permute-start(bf16[16,16,1024]{2,1,0:T(8,128)(2,1)} %get-tuple-element.41.after_ref.refs_0_.refs_12_), channel_id=1, source_target_pairs={{0,1},{1,0},{2,3},{3,2},{4,5},{5,4},{6,7},{7,6},{8,9},{9,8},{10,11... | collective-permute-start | bytes 1572872 | tf_op jit(solution)/shard_map/ppermute | solution.py:434
  238.2 0.8 copy-start
  239.1 2.3 collective-permute-start.10
  239.1 14.5 %collective-permute-start.11 = (bf16[16,16,1024]{2,1,0:T(8,128)(2,1)}, bf16[16,16,1024]{2,1,0:T(8,128)(2,1)S(1)}, u32[]{:S(2)}, u32[]{:S(2)}) collective-permute-start(bf16[16,16,1024]{2,1,0:T(8,128)(2,1)} %get-tuple-element.44.after_ref.refs_16_), channel_id=1, source_target_pairs={{0,2},{1,3},{2,0},{3,1},{4,6},{5,7},{6,4},{7,5},{8,10},{9,11},{10,... | collective-permute-start | bytes 1572872 | tf_op jit(solution)/shard_map/ppermute | solution.py:434
  240.6 14.6 %collective-permute-start.12 = (bf16[16,16,1024]{2,1,0:T(8,128)(2,1)}, bf16[16,16,1024]{2,1,0:T(8,128)(2,1)}, u32[]{:S(2)}, u32[]{:S(2)}) collective-permute-start(bf16[16,16,1024]{2,1,0:T(8,128)(2,1)} %get-tuple-element.44.after_ref.refs_16_), channel_id=1, source_target_pairs={{0,1},{1,0},{2,3},{3,2},{4,5},{5,4},{6,7},{7,6},{8,9},{9,8},{10,11... | collective-permute-start | bytes 1572872 | tf_op jit(solution)/shard_map/ppermute | solution.py:434
  253.6 0.8 copy-start.3
  254.4 2.1 collective-permute-start.13
  256.6 0.8 copy-start.6
